TPU v7x, 32 devices: a whole 2x2x4 slice. The times are simulated.
32 devices in a mesh: ep: 16 (over z, y, x), et: 2 (over core).
Axes of the slice: x: 2, y: 2, z: 4, core: 2. Of those that a mesh axis runs over, the one named last changes fastest.
Arguments:
- tokens: bfloat16 [2048, 3584], P('ep', 'et'), may hold values from -6 to 6
- slot_ids: int32 [2048, 8], P('ep'), may hold values from 0 to 15, all different within a row; in each aligned block of 128 rows (0 to 127, 128 to 255, ...) at most 80 rows name the same one
- gate_weights: float32 [2048, 8], P('ep'), may hold values from 0.1 to 1
- old_expert: int32 [16], replicated, may hold values from 0 to 13, as said below
- new_expert: int32 [16], replicated, may hold values from 0 to 13, as said below
- gate_proj: bfloat16 [16, 3584, 1024], P(None, 'ep', 'et'), may hold values from -0.09375 to 0.09375
- up_proj: bfloat16 [16, 3584, 1024], P(None, 'ep', 'et'), may hold values from -0.09375 to 0.09375
- down_proj: bfloat16 [16, 3584, 1024], P(None, 'ep', 'et'), may hold values from -0.1875 to 0.1875
Outputs:
- layer_out: bfloat16 [2048, 3584], P('ep', 'et')
Inputs may be any that keep to these rules, and one draw needn't show every extreme that they name: `slot_ids`: each row names 8 different slots. The rows of one index of ep name no slot more than 80 times, and in every draw some slot exactly 80 times on some index. `old_expert`: names every expert 0 to 13 once or twice; 2 of them twice. `new_expert`: names every expert 0 to 13 once or twice; 2 of them twice.
All inputs are finite; a program needn't handle non-finite values.
Results may differ from a plain program's by a relative error of at most 0.015.
Values may be sent and summed in bfloat16 or wider, within the bound.
No kernel may reach another device: no remote copies, remote signals or barrier semaphores. Data moves between devices by JAX's collectives and lax.ppermute only.
A program may use at most 128 MiB of HBM per device.

v0:
```python
import jax
import jax.numpy as jnp
from jax import lax
from jax.sharding import PartitionSpec as P


def gather_rows(source_rows, row_table, slot_total, capacity):
    padded = jnp.concatenate(
        [source_rows, jnp.zeros((1, source_rows.shape[1]), source_rows.dtype)], axis=0
    )
    return jnp.take(padded, row_table, axis=0).reshape(slot_total, capacity, source_rows.shape[1])


def combine_rows(returned, target, gate_flat, tok_rows, top_count):
    flat_rows = returned.reshape(-1, returned.shape[-1])
    picked = jnp.take(flat_rows, target, axis=0).astype(jnp.float32)
    scaled = picked * gate_flat[:, None]
    return jnp.sum(scaled.reshape(tok_rows, top_count, -1), axis=1)


def per_device(
    tokens, slot_ids, gate_weights, old_expert, new_expert, gate_proj, up_proj, down_proj
):
    slot_total = lax.axis_size("ep")
    tok_rows = tokens.shape[0]
    top_count = slot_ids.shape[1]
    capacity = min(tok_rows, (tok_rows * top_count * 5 + 4 * slot_total - 1) // (4 * slot_total))
    slot_index = jnp.arange(slot_total, dtype=jnp.int32)
    holders = new_expert[:, None] == old_expert[None, :]
    source = jnp.min(jnp.where(holders, slot_index[None, :], slot_total), axis=1)
    chosen_slabs = (
        jnp.take(gate_proj, source, axis=0),
        jnp.take(up_proj, source, axis=0),
        jnp.take(down_proj, source, axis=0),
    )
    moved = (
        lax.all_to_all(chosen_slabs[0], "ep", split_axis=0, concat_axis=0, tiled=True),
        lax.all_to_all(chosen_slabs[1], "ep", split_axis=0, concat_axis=0, tiled=True),
        lax.all_to_all(chosen_slabs[2], "ep", split_axis=0, concat_axis=0, tiled=True),
    )
    gate_slab, up_slab, down_slab = (
        moved_slab.reshape(-1, moved_slab.shape[-1]) for moved_slab in moved
    )
    flat_slot = slot_ids.reshape(-1)
    onehot = (flat_slot[:, None] == slot_index[None, :]).astype(jnp.int32)
    before = jnp.cumsum(onehot, axis=0) - onehot
    position = jnp.sum(before * onehot, axis=1)
    target = flat_slot * capacity + position
    pair_row = jnp.arange(flat_slot.shape[0], dtype=jnp.int32) // top_count
    row_table = jnp.full((slot_total * capacity,), tok_rows, jnp.int32).at[target].set(pair_row)
    full_rows = lax.all_gather(tokens, "et", axis=1, tiled=True)
    arrived = lax.all_to_all(
        gather_rows(full_rows, row_table, slot_total, capacity),
        "ep",
        split_axis=0,
        concat_axis=0,
        tiled=True,
    )
    rows_in = arrived.reshape(-1, arrived.shape[-1])
    gate_part = jnp.dot(rows_in, gate_slab, preferred_element_type=jnp.float32)
    up_part = jnp.dot(rows_in, up_slab, preferred_element_type=jnp.float32)
    hidden = (jax.nn.silu(gate_part) * up_part).astype(jnp.bfloat16)
    partial_value = lax.dot_general(
        hidden, down_slab, (((1,), (1,)), ((), ())), preferred_element_type=jnp.float32
    )
    gate_flat = gate_weights.reshape(-1)
    expert_out = lax.psum_scatter(
        partial_value.astype(jnp.bfloat16), "et", scatter_dimension=1, tiled=True
    ).astype(jnp.float32)
    returned = lax.all_to_all(
        expert_out.reshape(slot_total, capacity, -1).astype(jnp.bfloat16),
        "ep",
        split_axis=0,
        concat_axis=0,
        tiled=True,
    ).astype(jnp.float32)
    layer_out = combine_rows(returned, target, gate_flat, tok_rows, top_count)
    return layer_out.astype(jnp.bfloat16)


def solution(mesh):
    placed = (
        P("ep", "et"),
        P("ep", None),
        P("ep", None),
        P(),
        P(),
        P(None, "ep", "et"),
        P(None, "ep", "et"),
        P(None, "ep", "et"),
    )
    return jax.shard_map(
        per_device, mesh=mesh, in_specs=placed, out_specs=P("ep", "et"), check_vma=False
    )
```

profile of v0, /device:TPU:14, one launch (start us, length us, event | category | flops | bytes accessed | tf_op | source)
XLA Modules:
  0.0 669.6 jit_solution(10445348588057418489)
XLA Ops:
  6.5 0.9 select_reduce_fusion
  7.4 4.6 gather_fusion.2
  12.0 4.6 gather_fusion.3
  16.7 4.6 gather_fusion.4
  21.3 6.6 broadcast_select_fusion.1
  27.9 87.5 %all_to_all.25 = bf16[16,224,512]{2,1,0:T(8,128)(2,1)} all-to-all(bf16[16,224,512]{2,1,0:T(8,128)(2,1)S(1)} %get-tuple-element.8), channel_id=1, replica_groups=mesh['ep'=16,'et'=2] {'ep'}, dimensions={0} | all-to-all | bytes 7340032 | tf_op jit(solution)/shard_map/all_to_all | solution.py:37
  115.4 0.0 copy-start.1
  115.4 0.0 copy-start
  115.4 6.6 all-to-all-start.2
  122.0 0.0 copy-done.1
  122.0 0.1 copy.25
  122.1 0.1 eq.39
  122.2 0.1 reshape.107
  122.3 4.5 reduce-window.6
  126.8 0.1 slice.18
  126.9 0.1 copy.27
  127.1 0.1 copy.28
  127.1 0.1 copy.31
  127.2 0.1 mul.41
  127.4 0.1 broadcast_add_fusion
  127.5 4.3 scatter_custom_fusion
  131.8 0.1 broadcast_in_dim.56
  131.9 0.0 copy-done
  131.9 2.5 all_gather.3
  134.4 0.1 concatenate.3
  134.5 7.9 %gather_fusion = bf16[1280,3584]{1,0:T(8,128)(2,1)} fusion(bf16[129,3584]{1,0:T(8,128)(2,1)S(1)} %concatenate.3, s32[2048]{0:T(1024)S(1)} %pad_clamp_fusion), kind=kCustom, calls=%fused_computation.3 | custom fusion | bytes 18355200 | tf_op jit(solution)/shard_map/jit(_take)/gather | solution.py:11
  142.4 8.0 %broadcast_select_fusion = bf16[16,80,3584]{2,1,0:T(8,128)(2,1)} fusion(bf16[16,80,3584]{2,1,0:T(8,128)(2,1)} %bitcast.49, pred[16,80]{1,0:T(8,128)(4,1)S(1)} %broadcast_in_dim.56), kind=kLoop, calls=%fused_computation.7 | loop fusion | flops 4587520 | bytes 18351360 | tf_op jit(solution)/shard_map/jit(_take)/select_n | solution.py:11
  150.5 52.0 %all-to-all-done.2 = bf16[16,224,512]{2,1,0:T(8,128)(2,1)} async-done(((bf16[16,224,512]{2,1,0:T(8,128)(2,1)}), bf16[16,224,512]{2,1,0:T(8,128)(2,1)}, u32[]{:S(2)}, u32[]{:S(2)}) %all-to-all-start.2) | async-done | bytes 3670048 | tf_op jit(solution)/shard_map/all_to_all | solution.py:38
  202.4 203.4 %all_to_all.26 = bf16[16,80,3584]{2,1,0:T(8,128)(2,1)} all-to-all(bf16[16,80,3584]{2,1,0:T(8,128)(2,1)} %broadcast_select_fusion), channel_id=1, replica_groups=mesh['ep'=16,'et'=2] {'ep'}, dimensions={0} | all-to-all | bytes 18350080 | tf_op jit(solution)/shard_map/all_to_all | solution.py:52
  405.8 7.0 %all-to-all-start.3 = ((bf16[16,224,512]{2,1,0:T(8,128)(2,1)}), bf16[16,224,512]{2,1,0:T(8,128)(2,1)}, u32[]{:S(2)}, u32[]{:S(2)}) async-start(bf16[16,224,512]{2,1,0:T(8,128)(2,1)} %get-tuple-element.6), calls=%async_computation.3 | async-start | bytes 7340032 | tf_op jit(solution)/shard_map/all_to_all | solution.py:39
  412.8 0.2 reduce-scatter.2.cloned.1.call-start
  413.0 11.0 %fusion.12 = f32[1280,512]{1,0:T(8,128)} fusion(bf16[1280,3584]{1,0:T(8,128)(2,1)} %bitcast.50, bf16[3584,512]{1,0:T(8,128)(2,1)} %bitcast.53), kind=kOutput, calls=%fused_computation.46 | convolution fusion | flops 4697620480 | bytes 15466496 | tf_op jit(solution)/shard_map/dot_general | solution.py:60
  424.1 69.1 %all-to-all-done.3 = bf16[16,224,512]{2,1,0:T(8,128)(2,1)} async-done(((bf16[16,224,512]{2,1,0:T(8,128)(2,1)}), bf16[16,224,512]{2,1,0:T(8,128)(2,1)}, u32[]{:S(2)}, u32[]{:S(2)}) %all-to-all-start.3) | async-done | bytes 3670048 | tf_op jit(solution)/shard_map/all_to_all | solution.py:39
  493.2 16.9 %convolution_convert_fusion = bf16[1280,3584]{1,0:T(8,128)(2,1)} fusion(bf16[3584,512]{1,0:T(8,128)(2,1)} %bitcast.8, bf16[1280,3584]{1,0:T(8,128)(2,1)} %bitcast.51, bf16[3584,512]{1,0:T(8,128)(2,1)} %bitcast.7, f32[1280,512]{1,0:T(8,128)} %fusion.12), kind=kOutput, calls=%fused_computation.6 | convolution fusion | flops 9403760640 | bytes 28311552 | tf_op jit(solution)/shard_map/dot_general | solution.py:63
  510.1 0.0 reduce-scatter.2.cloned.1.call-update
  510.1 17.1 %reduce-scatter.2.cloned.1.call-done = bf16[1280,1792]{1,0:T(8,128)(2,1)} async-done(((bf16[1280,3584]{1,0:T(8,128)(2,1)}), bf16[1280,1792]{1,0:T(8,128)(2,1)}) %reduce-scatter.2.cloned.1.call-update) | async-done | bytes 4587536 | tf_op jit(solution)/shard_map/reduce_scatter | solution.py:67
  527.2 0.0 copy-start.2
  527.2 7.1 %all-to-all-start.4 = ((bf16[16,80,1792]{2,1,0:T(8,128)(2,1)}), bf16[16,80,1792]{2,1,0:T(8,128)(2,1)}, u32[]{:S(2)}, u32[]{:S(2)}) async-start(bf16[16,80,1792]{2,1,0:T(8,128)(2,1)} %bitcast.52), calls=%async_computation.5 | async-start | bytes 9175040 | tf_op jit(solution)/shard_map/all_to_all | solution.py:70
  534.3 0.1 reduce_sum.23
  534.5 0.1 copy.30
  534.6 0.0 copy-done.2
  534.6 0.1 copy.32
  534.7 103.8 %all-to-all-done.4 = bf16[16,80,1792]{2,1,0:T(8,128)(2,1)} async-done(((bf16[16,80,1792]{2,1,0:T(8,128)(2,1)}), bf16[16,80,1792]{2,1,0:T(8,128)(2,1)}, u32[]{:S(2)}, u32[]{:S(2)}) %all-to-all-start.4) | async-done | bytes 4587552 | tf_op jit(solution)/shard_map/all_to_all | solution.py:70
  638.5 6.5 bitcast_convert_fusion
  645.0 11.9 %gather_fusion.1 = f32[1024,1792]{1,0:T(8,128)} fusion(f32[1280,1792]{1,0:T(8,128)} %bitcast_convert_fusion, s32[1024]{0:T(1024)S(1)} %broadcast_clamp_fusion), kind=kCustom, calls=%fused_computation.4 | custom fusion | bytes 14684160 | tf_op jit(solution)/shard_map/jit(_take)/gather | solution.py:16
  656.9 5.9 fusion.1
  (16 shorter events, 0.2 us)
Async XLA Ops:
  115.4 6.6 copy-start.1
  115.4 16.6 %copy-start = (bf16[128,1792]{1,0:T(8,128)(2,1)S(1)}, bf16[128,1792]{1,0:T(8,128)(2,1)}, u32[]{:S(2)}) copy-start(bf16[128,1792]{1,0:T(8,128)(2,1)} %param.10) | copy-start | bytes 1376260
  115.4 87.1 %all-to-all-start.2 = ((bf16[16,224,512]{2,1,0:T(8,128)(2,1)}), bf16[16,224,512]{2,1,0:T(8,128)(2,1)}, u32[]{:S(2)}, u32[]{:S(2)}) async-start(bf16[16,224,512]{2,1,0:T(8,128)(2,1)} %get-tuple-element.7), calls=%async_computation.2 | async-start | bytes 7340032 | tf_op jit(solution)/shard_map/all_to_all | solution.py:38
  405.8 87.4 %all-to-all-start.3 = ((bf16[16,224,512]{2,1,0:T(8,128)(2,1)}), bf16[16,224,512]{2,1,0:T(8,128)(2,1)}, u32[]{:S(2)}, u32[]{:S(2)}) async-start(bf16[16,224,512]{2,1,0:T(8,128)(2,1)} %get-tuple-element.6), calls=%async_computation.3 | async-start | bytes 7340032 | tf_op jit(solution)/shard_map/all_to_all | solution.py:39
  412.8 114.4 %reduce-scatter.2.cloned.1.call-start = ((), (), s32[]{:S(2)}) async-start(), calls=%async_computation.6 | async-start | bytes 13762560 | tf_op jit(solution)/shard_map/reduce_scatter | solution.py:67
  527.2 7.4 %copy-start.2 = (f32[128,8]{0,1:T(8,128)S(1)}, f32[128,8]{0,1:T(8,128)}, u32[]{:S(2)}) copy-start(f32[128,8]{0,1:T(8,128)} %param.12) | copy-start | bytes 12292
  527.2 111.3 %all-to-all-start.4 = ((bf16[16,80,1792]{2,1,0:T(8,128)(2,1)}), bf16[16,80,1792]{2,1,0:T(8,128)(2,1)}, u32[]{:S(2)}, u32[]{:S(2)}) async-start(bf16[16,80,1792]{2,1,0:T(8,128)(2,1)} %bitcast.52), calls=%async_computation.5 | async-start | bytes 9175040 | tf_op jit(solution)/shard_map/all_to_all | solution.py:70
Sparse Core Ops, SparseCore 0:
  510.2 16.9 reduce-scatter.1
where the time goes:
time: 670 us
  blocking collectives  293 us (44%)
  waiting for transfers between devices  242 us (36%)
  local copies, waits for them, and re-layouts  39.3 us (6%)
  other arithmetic  32.7 us (5%)
  matrix products  27.9 us (4%)
  starting transfers between devices  21 us (3%)
  between operations  13.5 us (2%)
    all_to_all x1, blocking collectives, per_device(): lax.all_to_all(gather_rows(full_rows, row_table, slot_total, capacity), '...  203 us
    all_to_all x1, waiting for transfers between devices, per_device(): lax.all_to_all(expert_out.reshape(slot_total, capacity, -1).astype(jnp.bf...  104 us
    all_to_all x1, blocking collectives, per_device(): lax.all_to_all(chosen_slabs[0], 'ep', split_axis=0, concat_axis=0, tiled=...  87.5 us
    all_to_all x1, waiting for transfers between devices, per_device(): lax.all_to_all(chosen_slabs[2], 'ep', split_axis=0, concat_axis=0, tiled=...  69.1 us
    all_to_all x1, waiting for transfers between devices, per_device(): lax.all_to_all(chosen_slabs[1], 'ep', split_axis=0, concat_axis=0, tiled=...  52 us
    reduce_scatter x1, waiting for transfers between devices, per_device(): lax.psum_scatter(partial_value.astype(jnp.bfloat16), 'et', scatter_dimens...  17.1 us
    dot_general x1, matrix products, per_device(): lax.dot_general(hidden, down_slab, (((1,), (1,)), ((), ())), preferred_el...  16.9 us
  transfers between devices with their start and end apart: 4, of which 4 were waited for; matrix products, arithmetic and copies ran while one was open for 6% of the time, Pallas kernels for 0%

commit v1 on v0

v1 whole, which is shorter than its diff:
```python
import functools

import jax
import jax.numpy as jnp
from jax import lax
from jax.experimental import pallas as pl
from jax.experimental.layout import Layout, with_layout_constraint
from jax.experimental.pallas import tpu as pltpu
from jax.sharding import PartitionSpec as P

LANES = 128
HALF = 64
MIB = 1 << 20


def distinct_sources(old_expert, new_expert):
    slots = old_expert.shape[0]
    index = jnp.arange(slots, dtype=jnp.int32)
    holders = new_expert[:, None] == old_expert[None, :]
    source = jnp.min(jnp.where(holders, index[None, :], slots), axis=1)
    used = jnp.any(source[:, None] == index[None, :], axis=0)
    earlier = (index[None, :] < index[:, None]) & used[None, :]
    place = jnp.sum(earlier.astype(jnp.int32), axis=1)
    count = slots - slots // 8
    wanted = jnp.arange(count, dtype=jnp.int32)
    listing = jnp.sum(
        jnp.where(used[None, :] & (place[None, :] == wanted[:, None]), index[None, :], 0), axis=1
    )
    slot_place = jnp.sum(jnp.where(source[:, None] == index[None, :], place[None, :], 0), axis=1)
    return source, listing, slot_place


def units_of(dest):
    if dest % 2 == 0:
        start = 7 * dest // 2
        return start, start + 3, 0
    start = (7 * dest + 1) // 2
    return start, start - 1, 1


def pack_rows(slab_of, out_ref, base, dest, lo, rows, per_slab):
    first, half, side = units_of(dest)
    for number in range(3):
        unit = first + number
        ref, slab = slab_of(unit // per_slab)
        lane = (unit % per_slab) * LANES
        out_ref[dest, base + number * rows : base + (number + 1) * rows, :] = ref[
            slab, lo : lo + rows, lane : lane + LANES
        ]
    ref, slab = slab_of(half // per_slab)
    lane = (half % per_slab) * LANES
    mid = rows // 2
    top = ref[slab, lo : lo + mid, lane : lane + LANES].astype(jnp.float32)
    low = ref[slab, lo + mid : lo + rows, lane : lane + LANES].astype(jnp.float32)
    left = lax.broadcasted_iota(jnp.int32, (mid, LANES), 1) < HALF
    if side == 0:
        both = jnp.where(left, top, pltpu.roll(low, HALF, 1))
    else:
        both = jnp.where(left, pltpu.roll(top, HALF, 1), low)
    out_ref[dest, base + 3 * rows : base + 3 * rows + mid, :] = both.astype(out_ref.dtype)


def pack_pair_kernel(list_ref, gate_ref, up_ref, out_ref):
    slots, depth, width = gate_ref.shape
    size = depth * 7 // 2
    for dest in range(out_ref.shape[0]):
        for number, ref in enumerate((gate_ref, up_ref)):
            pack_rows(
                lambda place, ref=ref: (ref, list_ref[place]),
                out_ref, number * size, dest, 0, depth, width // LANES,
            )


def pack_down_kernel(parts, list_ref, down_ref, *out_refs):
    slots, depth, width = down_ref.shape
    for dest in range(out_refs[0].shape[0]):
        lo = 0
        for rows, out_ref in zip(parts, out_refs):
            pack_rows(
                lambda place: (down_ref, list_ref[place]),
                out_ref, 0, dest, lo, rows, width // LANES,
            )
            lo += rows


def whole(*shape):
    return pl.BlockSpec(shape, lambda *_: (0,) * len(shape))


def pack_pair(listing, gate_proj, up_proj, dests):
    slots, depth, width = gate_proj.shape
    shape = (dests, depth * 7, LANES)
    return pl.pallas_call(
        pack_pair_kernel,
        out_shape=jax.ShapeDtypeStruct(shape, gate_proj.dtype),
        in_specs=[pl.BlockSpec(memory_space=pltpu.SMEM)]
        + [pl.BlockSpec(memory_space=pltpu.VMEM)] * 2,
        out_specs=pl.BlockSpec(memory_space=pltpu.VMEM),
        compiler_params=pltpu.CompilerParams(vmem_limit_bytes=32 * MIB),
        name="pack_gate_up",
    )(listing, gate_proj, up_proj)


def pack_down(listing, down_proj, dests, parts):
    return pl.pallas_call(
        functools.partial(pack_down_kernel, parts),
        out_shape=[
            jax.ShapeDtypeStruct((dests, rows * 7 // 2, LANES), down_proj.dtype) for rows in parts
        ],
        in_specs=[
            pl.BlockSpec(memory_space=pltpu.SMEM),
            pl.BlockSpec(memory_space=pltpu.VMEM),
        ],
        out_specs=[pl.BlockSpec(memory_space=pltpu.VMEM)] * len(parts),
        compiler_params=pltpu.CompilerParams(vmem_limit_bytes=32 * MIB),
        name="pack_down",
    )(listing, down_proj)


def unpack_rows(in_ref, at, base, rows, out_ref, out_row, out_lane):
    for number in range(3):
        out_ref[out_row : out_row + rows, out_lane + number * LANES : out_lane + (number + 1) * LANES] = (
            in_ref[at, base + number * rows : base + (number + 1) * rows, :]
        )
    mid = rows // 2
    both = in_ref[at, base + 3 * rows : base + 3 * rows + mid, :]
    lanes = slice(out_lane + 3 * LANES, out_lane + 4 * LANES)
    out_ref[out_row : out_row + mid, lanes] = both
    out_ref[out_row + mid : out_row + rows, lanes] = pltpu.roll(
        both.astype(jnp.float32), HALF, 1
    ).astype(out_ref.dtype)


def hidden_kernel(core_ref, own_ref, other_ref, share_ref, packed_ref, out_ref, gate_w, up_w):
    sources, packed_rows, _ = packed_ref.shape
    depth = packed_rows // 7
    size = packed_rows // 2
    group = sources // 2

    @pl.when(pl.program_id(0) == 0)
    def _():
        for at in range(sources):
            place = (core_ref[0] + at // group) % 2 * group + at % group
            unpack_rows(packed_ref, place, 0, depth, gate_w, at * depth, 0)
            unpack_rows(packed_ref, place, size, depth, up_w, at * depth, 0)

    own, other = own_ref[...], other_ref[...]
    mid = own.shape[1]

    def product(w_ref):
        return jnp.dot(own, w_ref[:mid, :], preferred_element_type=jnp.float32) + jnp.dot(
            other, w_ref[mid:, :], preferred_element_type=jnp.float32
        )

    gate = product(gate_w)
    value = gate / (1.0 + jnp.exp(-gate)) * product(up_w)
    left = lax.broadcasted_iota(jnp.int32, (own.shape[0], LANES), 1) < HALF
    for number in range(4):
        lanes = slice(number * LANES, (number + 1) * LANES)
        part = value[:, lanes] * share_ref[:, number : number + 1]
        if number == 3:
            part = jnp.where(left, part, 0.0)
        out_ref[:, lanes] = part.astype(out_ref.dtype)


def hidden_units(core, own, other, share, packed):
    total, model = own.shape
    tile = 256
    wide = 4 * LANES
    return pl.pallas_call(
        hidden_kernel,
        grid=(total // tile,),
        out_shape=jax.ShapeDtypeStruct((total, wide), own.dtype),
        in_specs=[
            pl.BlockSpec(memory_space=pltpu.SMEM),
            pl.BlockSpec((tile, model), lambda i: (i, 0)),
            pl.BlockSpec((tile, model), lambda i: (i, 0)),
            pl.BlockSpec((tile, 4), lambda i: (i, 0)),
            whole(*packed.shape),
        ],
        out_specs=pl.BlockSpec((tile, wide), lambda i: (i, 0)),
        scratch_shapes=[pltpu.VMEM((2 * model, wide), own.dtype)] * 2,
        compiler_params=pltpu.CompilerParams(vmem_limit_bytes=40 * MIB),
        cost_estimate=pl.CostEstimate(
            flops=8 * total * model * wide, bytes_accessed=24 * MIB, transcendentals=total * wide
        ),
        name="hidden",
    )(core.reshape(1), own, other, share, packed)


def down_kernel(rows, side, own_h, other_h, own_ref, other_ref, out_a, out_b, own_w, other_w):
    for in_ref, w_ref in ((own_ref, own_w), (other_ref, other_w)):
        for at in range(in_ref.shape[0]):
            unpack_rows(in_ref, at, 0, rows, w_ref, at * rows, 0)
    half = own_w.shape[0] // 2
    quarter = own_h.shape[0] // 4

    def product(at, size, span):
        tokens = slice(at * quarter, (at + size) * quarter)
        dims = (((1,), (1,)), ((), ()))
        return lax.dot_general(
            own_h[tokens, :], own_w[span, :], dims, preferred_element_type=jnp.float32
        ) + lax.dot_general(
            other_h[tokens, :], other_w[span, :], dims, preferred_element_type=jnp.float32
        )

    out_a[...] = product(2 * side, 2, slice(0, half)).astype(out_a.dtype)
    for first in range(2):
        out_b[first * quarter : (first + 1) * quarter, :] = product(
            2 * first + side, 1, slice(half, 2 * half)
        ).astype(out_b.dtype)


def down_product(own_h, other_h, own, other, rows, side, dtype, name):
    sources = own.shape[0]
    total, wide = own_h.shape
    tokens = total // 2
    features = sources * rows // 2
    vmem = pl.BlockSpec(memory_space=pltpu.VMEM)
    return pl.pallas_call(
        functools.partial(down_kernel, rows, side),
        out_shape=[jax.ShapeDtypeStruct((tokens, features), dtype)] * 2,
        in_specs=[vmem] * 4,
        out_specs=[vmem] * 2,
        scratch_shapes=[pltpu.VMEM((sources * rows, wide), own.dtype)] * 2,
        compiler_params=pltpu.CompilerParams(vmem_limit_bytes=40 * MIB),
        cost_estimate=pl.CostEstimate(
            flops=8 * tokens * wide * features, bytes_accessed=8 * MIB, transcendentals=0
        ),
        name=name,
    )(own_h, other_h, own, other)


def swap(value, bit):
    size = lax.axis_size("ep")
    return lax.ppermute(value, "ep", [(i, i ^ (1 << bit)) for i in range(size)])


def gather_bits(value, bits, order, have=()):
    have = list(have)
    for bit in order:
        axis = sum(1 for b in have if b < bit)
        value = jnp.stack([value, swap(value, bit)], axis=axis)
        have.append(bit)
    return value


def take_half(value, axis, number):
    return lax.index_in_dim(value, number, axis, keepdims=False)


def sum_stages(keep, arrived, order, left):
    left = list(left)
    for bit in order:
        axis = left.index(bit)
        total = keep + arrived.astype(jnp.float32)
        arrived = swap(take_half(total, axis, 1).astype(jnp.bfloat16), bit)
        keep = take_half(total, axis, 0)
        left.remove(bit)
    return keep, arrived


def share_of_slots(slot_ids, gate_weights, slots):
    index = jnp.arange(slots, dtype=jnp.int32)
    picked = slot_ids.T[None, :, :] == index[:, None, None]
    return jnp.sum(jnp.where(picked, gate_weights.T[None, :, :], 0.0), axis=1)


def packed_layer(
    tokens, slot_ids, gate_weights, old_expert, new_expert, gate_proj, up_proj, down_proj
):
    devices = lax.axis_size("ep")
    bits = devices.bit_length() - 1
    slots, depth, width = gate_proj.shape
    me = lax.axis_index("ep")
    core = lax.axis_index("et")
    other_core = [(0, 1), (1, 0)]
    _, listing, slot_place = distinct_sources(old_expert, new_expert)

    places = []
    for dest in range(devices):
        first, half, _ = units_of(dest)
        places.append([unit // (width // LANES) for unit in (first, first + 1, first + 2, half)])
    places = jnp.asarray(places, jnp.int32)
    share = share_of_slots(slot_ids, gate_weights, slots)
    belongs = slot_place[None, None, :, None] == places[:, :, None, None]
    unit_share = jnp.sum(jnp.where(belongs, share[None, None], 0.0), axis=2)
    unit_share = lax.all_to_all(unit_share, "ep", 0, 0, tiled=True)
    unit_share = jnp.take(unit_share, me ^ jnp.arange(devices), axis=0, mode="clip")
    unit_share = unit_share.reshape((2,) * bits + unit_share.shape[1:])
    unit_share = unit_share.transpose(tuple(range(bits - 1, -1, -1)) + (bits + 1, bits))
    unit_share = unit_share.reshape(-1, 4)

    parts = (96, 64, 64)
    down_packed = pack_down(listing, down_proj, devices, parts)

    packed, tokens_in = lax.optimization_barrier(
        (pack_pair(listing, gate_proj, up_proj, devices), tokens)
    )
    moved = lax.all_to_all(packed, "ep", 0, 0, tiled=True)
    late = list(range(bits - 1, 1, -1))
    rows = gather_bits(tokens_in, bits, late)
    mid = tokens.shape[1] // 2
    rows = jnp.concatenate(
        [
            gather_bits(rows[..., :mid], bits, (1, 0), late),
            gather_bits(rows[..., mid:], bits, (0, 1), late),
        ],
        axis=-1,
    ).reshape(-1, tokens.shape[1])
    rows_other = lax.ppermute(rows, "et", other_core)

    def hidden_of(moved):
        hidden = hidden_units(core, rows, rows_other, unit_share, moved)
        return hidden, lax.ppermute(hidden, "et", other_core)

    group = devices // 2
    tie = lax.optimization_barrier
    row_major = Layout(major_to_minor=(0, 1))

    def move_down(packed, after):
        packed, after = tie((packed, after))
        return lax.all_to_all(packed, "ep", 0, 0, tiled=True), after

    def products(down, rows_in):
        own = lax.dynamic_slice_in_dim(down, core * group, group, 0)
        other = lax.dynamic_slice_in_dim(down, (1 - core) * group, group, 0)
        other = lax.ppermute(other, "et", other_core)
        args = (hidden, hidden_other, own, other)
        sent = down_product(*args, rows_in, 1, jnp.bfloat16, "down_send")
        sent, args = tie((sent, args))
        arrived = [swap(value, bit) for bit, value in enumerate(sent)]
        return down_product(*args, rows_in, 0, jnp.float32, "down_keep"), arrived

    def stages(kept, arrived, rows_in, count, done=0):
        out = [], []
        for bit in (0, 1):
            left = [b for b in range(bits) if b != bit]
            order = ([1 - bit] + left[1:])[done : done + count]
            left = [b for b in left if b not in ([1 - bit] + left[1:])[:done]]
            shape = (2,) * len(left) + tokens.shape[:1] + (group // 2 * rows_in,)
            keep, come = sum_stages(
                kept[bit].reshape(shape), arrived[bit].reshape(shape), order, left
            )
            out[0].append(keep)
            out[1].append(come)
        return out

    def finish(kept, arrived, rows_in):
        sums = []
        for keep, come in zip(kept, arrived):
            total = (keep + come.astype(jnp.float32)).astype(jnp.bfloat16)
            total = with_layout_constraint(total, row_major)
            sums.append(total.reshape(total.shape[0], group // 2, rows_in))
        return jnp.concatenate(sums, axis=1)

    down0, moved = move_down(down_packed[0], moved)
    hidden, hidden_other = hidden_of(moved)
    down1, (down0, hidden, hidden_other) = move_down(
        down_packed[1], (down0, hidden, hidden_other)
    )
    kept0, arrived0 = products(down0, parts[0])
    down2, (down1, kept0) = move_down(down_packed[2], (down1, kept0))
    kept0, arrived0 = stages(kept0, arrived0, parts[0], 1)
    kept1, arrived1 = products(down1, parts[1])
    down2, kept0, kept1 = tie((down2, kept0, kept1))
    kept2, arrived2 = products(down2, parts[2])
    kept0, arrived0 = stages(kept0, arrived0, parts[0], bits - 2, 1)
    kept1, arrived1 = stages(kept1, arrived1, parts[1], bits - 1)
    kept2, arrived2 = stages(kept2, arrived2, parts[2], bits - 1)
    done = [
        finish(kept0, arrived0, parts[0]),
        finish(kept1, arrived1, parts[1]),
        finish(kept2, arrived2, parts[2]),
    ]
    return jnp.concatenate(done, axis=2).reshape(tokens.shape)


def plain_layer(
    tokens, slot_ids, gate_weights, old_expert, new_expert, gate_proj, up_proj, down_proj
):
    devices = lax.axis_size("ep")
    bits = devices.bit_length() - 1
    slots = gate_proj.shape[0]
    me = lax.axis_index("ep")
    source, _, _ = distinct_sources(old_expert, new_expert)

    def move(weights):
        chosen = jnp.take(weights, source, axis=0, mode="clip")
        return lax.all_to_all(chosen, "ep", 0, 0, tiled=True)

    gate_slab = move(gate_proj).reshape(-1, gate_proj.shape[-1])
    up_slab = move(up_proj).reshape(-1, up_proj.shape[-1])
    down = move(down_proj)
    order = range(bits - 1, -1, -1)
    rows = gather_bits(tokens, bits, order).reshape(-1, tokens.shape[1])
    rows = lax.all_gather(rows, "et", axis=1, tiled=True)
    share = gather_bits(share_of_slots(slot_ids, gate_weights, slots), bits, order)
    share = lax.dynamic_index_in_dim(share, me, bits, keepdims=False).reshape(-1, 1)
    gate_part = jnp.dot(rows, gate_slab, preferred_element_type=jnp.float32)
    up_part = jnp.dot(rows, up_slab, preferred_element_type=jnp.float32)
    hidden = (jax.nn.silu(gate_part) * up_part * share).astype(jnp.bfloat16)
    hidden = lax.all_gather(hidden, "et", axis=1, tiled=True)
    down = lax.all_to_all(down, "et", 0, 2, tiled=True)
    value = lax.dot_general(
        hidden,
        down.reshape(-1, down.shape[-1]),
        (((1,), (1,)), ((), ())),
        preferred_element_type=jnp.float32,
    )
    value = value.reshape((2,) * bits + (-1,) + value.shape[1:])
    arrived = swap(take_half(value, 0, 1).astype(jnp.bfloat16), 0)
    left = list(range(1, bits))
    keep, arrived = sum_stages(take_half(value, 0, 0), arrived, left, left)
    return (keep + arrived.astype(jnp.float32)).astype(jnp.bfloat16)


def per_device(tokens, slot_ids, gate_weights, old_expert, new_expert, gate_proj, up_proj, down_proj):
    slots, depth, width = gate_proj.shape
    count = slots - slots // 8
    devices = lax.axis_size("ep")
    fits = (
        lax.axis_size("et") == 2
        and depth == 224
        and width % LANES == 0
        and count * width == devices * 7 * HALF
        and devices % 8 == 0
    )
    layer = packed_layer if fits else plain_layer
    return layer(
        tokens, slot_ids, gate_weights, old_expert, new_expert, gate_proj, up_proj, down_proj
    )


def solution(mesh):
    placed = (
        P("ep", "et"),
        P("ep", None),
        P("ep", None),
        P(),
        P(),
        P(None, "ep", "et"),
        P(None, "ep", "et"),
        P(None, "ep", "et"),
    )
    return jax.shard_map(
        per_device, mesh=mesh, in_specs=placed, out_specs=P("ep", "et"), check_vma=False
    )
```

time: 670 us -> 421 us (0.63)
  blocking collectives: 293 us -> 22.7 us
  starting transfers between devices: 21 us -> 70.5 us
  Pallas kernels: 0 us -> 37.9 us
  matrix products: 27.9 us -> 0 us
  waiting for transfers between devices: 242 us -> 223 us
  other arithmetic: 32.7 us -> 17.7 us
  between operations: 13.5 us -> 0.63 us
    all_to_all x2 -> x1, blocking collectives: 291 us -> 22.7 us  [packed_layer(): unit_share = lax.all_to_all(unit_share, 'ep', 0, 0, tiled=True)]
    all_to_all x3 -> x4, waiting for transfers between devices: 225 us -> 15.4 us  [the longest x3 15.4 us: move_down(): return (lax.all_to_all(packed, 'ep', 0, 0, tiled=True), after)]
    ppermute x0 -> x35, waiting for transfers between devices: none -> 208 us  [the longest x30 200 us: swap(): return lax.ppermute(value, 'ep', [(i, i ^ 1 << bit) for i in range(size)])]
    pallas_call x0 -> x9, Pallas kernels: none -> 37.9 us  [the longest x1 21.4 us: hidden_units(): pl.pallas_call(hidden_kernel, grid=(total // tile,), out_shape=jax.ShapeD...]
    gather x5 -> x2, local copies, waits for them, and re-layouts: 33.7 us -> 0.59 us  [packed_layer(): jnp.take(unit_share, me ^ jnp.arange(devices), axis=0, mode='clip')]
    ppermute x0 -> x35, starting transfers between devices: none -> 31.3 us  [the longest x30 31.1 us: swap(): return lax.ppermute(value, 'ep', [(i, i ^ 1 << bit) for i in range(size)])]
    dot_general x2 -> x0, matrix products: 27.9 us -> none  [the longest x1 16.9 us: per_device(): lax.dot_general(hidden, down_slab, (((1,), (1,)), ((), ())), preferred_el...]
    unnamed x8 -> x62, local copies, waits for them, and re-layouts: 0.21 us -> 20.9 us
  transfers between devices with their start and end apart: 4 -> 39, of which waited for: 4 -> 22; matrix products, arithmetic and copies ran while one was open for 6% -> 9% of each run, Pallas kernels for 0% -> 9%
where the time goes in v1:
time: 421 us; the launch traced here: 417 us
  waiting for transfers between devices  223 us (53%)
  starting transfers between devices  70.5 us (17%)
  local copies, waits for them, and re-layouts  44.1 us (10%)
  Pallas kernels  37.9 us (9%)
  blocking collectives  22.7 us (5%)
  other arithmetic  17.7 us (4%)
    ppermute x30, waiting for transfers between devices, swap(): return lax.ppermute(value, 'ep', [(i, i ^ 1 << bit) for i in range(size)])  200 us
    all_to_all x3, starting transfers between devices, move_down(): return (lax.all_to_all(packed, 'ep', 0, 0, tiled=True), after)  31.5 us
    ppermute x30, starting transfers between devices, swap(): return lax.ppermute(value, 'ep', [(i, i ^ 1 << bit) for i in range(size)])  31.1 us
    all_to_all x1, blocking collectives, packed_layer(): unit_share = lax.all_to_all(unit_share, 'ep', 0, 0, tiled=True)  22.7 us
    pallas_call x1, Pallas kernels, hidden_units(): pl.pallas_call(hidden_kernel, grid=(total // tile,), out_shape=jax.ShapeD...  21.4 us
    unnamed x62, local copies, waits for them, and re-layouts  20.9 us
    all_to_all x3, waiting for transfers between devices, move_down(): return (lax.all_to_all(packed, 'ep', 0, 0, tiled=True), after)  15.4 us
    pallas_call x6, Pallas kernels, down_product(): pl.pallas_call(functools.partial(down_kernel, rows, side), out_shape=[jax...  12.2 us
  transfers between devices with their start and end apart: 39, of which 22 were waited for; matrix products, arithmetic and copies ran while one was open for 9% of the time, Pallas kernels for 9%

profile of v1, /device:TPU:14, one launch (start us, length us, event | category | flops | bytes accessed | tf_op | source)
XLA Modules:
  0.0 416.6 jit_solution(2740640689327479168)
XLA Ops:
  1.2 2.0 copy-done.7
  3.2 2.0 copy-done.8
  5.3 1.8 pack_gate_up.1
  7.1 2.7 copy-done.5
  9.8 2.6 collective-permute-start
  12.7 19.2 %collective-permute-done = bf16[128,1792]{1,0:T(8,128)(2,1)S(1)} collective-permute-done((bf16[128,1792]{1,0:T(8,128)(2,1)S(1)}, bf16[128,1792]{1,0:T(8,128)(2,1)S(1)}, u32[]{:S(2)}, u32[]{:S(2)}) %collective-permute-start) | collective-permute-done | bytes 458784 | tf_op jit(solution)/shard_map/ppermute | solution.py:236
  32.0 1.4 collective-permute-start.1
  33.7 22.7 %all_to_all.25 = f32[16,4,128]{2,1,0:T(4,128)S(1)} all-to-all(f32[16,4,128]{2,1,0:T(4,128)S(1)} %select_reduce_fusion), channel_id=1, replica_groups=mesh['ep'=16,'et'=2] {'ep'}, dimensions={0} | all-to-all | bytes 65536 | tf_op jit(solution)/shard_map/all_to_all | solution.py:288
  56.4 7.6 %all-to-all-start = ((bf16[16,1568,128]{2,1,0:T(8,128)(2,1)}), bf16[16,1568,128]{2,1,0:T(8,128)(2,1)}, u32[]{:S(2)}, u32[]{:S(2)}) async-start(bf16[16,1568,128]{2,1,0:T(8,128)(2,1)} %copy-done.5), calls=%async_computation | async-start | bytes 12845056 | tf_op jit(solution)/shard_map/all_to_all | solution.py:300
  65.4 40.0 %collective-permute-done.4 = bf16[2,2,128,896]{3,2,1,0:T(8,128)(2,1)S(1)} collective-permute-done((bf16[2,2,128,896]{3,2,1,0:T(8,128)(2,1)S(1)}, bf16[2,2,128,896]{3,2,1,0:T(8,128)(2,1)S(1)}, u32[]{:S(2)}, u32[]{:S(2)}) %collective-permute-start.4) | collective-permute-done | bytes 917536 | tf_op jit(solution)/shard_map/ppermute | solution.py:236
  106.0 17.8 %collective-permute-done.2 = bf16[2,2,128,896]{3,2,1,0:T(8,128)(2,1)S(1)} collective-permute-done((bf16[2,2,128,896]{3,2,1,0:T(8,128)(2,1)S(1)}, bf16[2,2,128,896]{3,2,1,0:T(8,128)(2,1)S(1)}, u32[]{:S(2)}, u32[]{:S(2)}) %collective-permute-start.2) | collective-permute-done | bytes 917536 | tf_op jit(solution)/shard_map/ppermute | solution.py:236
  124.2 59.5 %collective-permute-done.5 = bf16[2,2,2,128,896]{4,3,2,1,0:T(8,128)(2,1)S(1)} collective-permute-done((bf16[2,2,2,128,896]{4,3,2,1,0:T(8,128)(2,1)S(1)}, bf16[2,2,2,128,896]{4,3,2,1,0:T(8,128)(2,1)S(1)}, u32[]{:S(2)}, u32[]{:S(2)}) %collective-permute-start.5) | collective-permute-done | bytes 1835040 | tf_op jit(solution)/shard_map/ppermute | solution.py:236
  183.6 20.4 %collective-permute-done.3 = bf16[2,2,2,128,896]{4,3,2,1,0:T(8,128)(2,1)S(1)} collective-permute-done((bf16[2,2,2,128,896]{4,3,2,1,0:T(8,128)(2,1)S(1)}, bf16[2,2,2,128,896]{4,3,2,1,0:T(8,128)(2,1)S(1)}, u32[]{:S(2)}, u32[]{:S(2)}) %collective-permute-start.3) | collective-permute-done | bytes 1835040 | tf_op jit(solution)/shard_map/ppermute | solution.py:236
  204.7 3.6 copy.34
  208.3 2.0 copy-done.6
  210.3 2.5 pack_down.1
  214.7 20.1 %all-to-all-start.1 = ((bf16[16,336,128]{2,1,0:T(8,128)(2,1)}), bf16[16,336,128]{2,1,0:T(8,128)(2,1)}, u32[]{:S(2)}, u32[]{:S(2)}) async-start(bf16[16,336,128]{2,1,0:T(8,128)(2,1)} %get-tuple-element.59), calls=%async_computation.1 | async-start | bytes 2752512 | tf_op jit(solution)/shard_map/all_to_all | solution.py:323
  234.9 21.4 %hidden.1.own_h = bf16[2048,512]{1,0:T(8,128)(2,1)S(1)} custom-call(s32[1]{0:T(128)} %bitcast.core_ref, bf16[2048,1792]{1,0:T(8,128)(2,1)} %bitcast.132, bf16[2048,1792]{1,0:T(8,128)(2,1)} %collective-permute-done.6.other_ref, f32[2048,4]{1,0:T(8,128)S(1)} %bitcast.130, bf16[16,1568,128]{2,1,0:T(8,128)(2,1)} %all-to-all-done.packed_ref), custom_call_target="tpu_custom_call" | custom-call | flops 15032385536 | bytes 25165824 | tf_op jit(solution)/shard_map/hidden/pallas_call | solution.py:170
  256.3 4.1 collective-permute-done.7.other_h
  260.5 1.3 copy-done
  261.8 6.3 %all-to-all-done.1 = bf16[16,336,128]{2,1,0:T(8,128)(2,1)} async-done(((bf16[16,336,128]{2,1,0:T(8,128)(2,1)}), bf16[16,336,128]{2,1,0:T(8,128)(2,1)}, u32[]{:S(2)}, u32[]{:S(2)}) %all-to-all-start.1) | async-done | bytes 1376288 | tf_op jit(solution)/shard_map/all_to_all | solution.py:323
  268.1 5.4 %all-to-all-start.3 = ((bf16[16,224,128]{2,1,0:T(8,128)(2,1)}), bf16[16,224,128]{2,1,0:T(8,128)(2,1)}, u32[]{:S(2)}, u32[]{:S(2)}) async-start(bf16[16,224,128]{2,1,0:T(8,128)(2,1)} %copy-done.14), calls=%async_computation.3 | async-start | bytes 1835008 | tf_op jit(solution)/shard_map/all_to_all | solution.py:323
  273.5 1.5 constant_dynamic-slice_fusion.2
  275.1 2.1 collective-permute-done.8.other_ref
  277.3 2.5 down_send.3
  280.7 2.5 down_keep.3
  285.5 9.1 %all-to-all-done.3 = bf16[16,224,128]{2,1,0:T(8,128)(2,1)} async-done(((bf16[16,224,128]{2,1,0:T(8,128)(2,1)}), bf16[16,224,128]{2,1,0:T(8,128)(2,1)}, u32[]{:S(2)}, u32[]{:S(2)}) %all-to-all-start.3) | async-done | bytes 917536 | tf_op jit(solution)/shard_map/all_to_all | solution.py:323
  294.7 6.0 %all-to-all-start.4 = ((bf16[16,224,128]{2,1,0:T(8,128)(2,1)}), bf16[16,224,128]{2,1,0:T(8,128)(2,1)}, u32[]{:S(2)}, u32[]{:S(2)}) async-start(bf16[16,224,128]{2,1,0:T(8,128)(2,1)} %get-tuple-element.74), calls=%async_computation.4 | async-start | bytes 1835008 | tf_op jit(solution)/shard_map/all_to_all | solution.py:323
  303.1 1.8 collective-permute-done.11.other_ref
  304.9 1.6 copy-done.2
  306.5 2.4 down_send.4
  308.8 1.5 collective-permute-start.22
  310.3 1.5 collective-permute-start.18
  311.8 16.7 %collective-permute-done.10 = bf16[1024,384]{1,0:T(8,128)(2,1)S(1)} collective-permute-done((bf16[1024,384]{1,0:T(8,128)(2,1)}, bf16[1024,384]{1,0:T(8,128)(2,1)S(1)}, u32[]{:S(2)}, u32[]{:S(2)}) %collective-permute-start.10) | collective-permute-done | bytes 786464 | tf_op jit(solution)/shard_map/ppermute | solution.py:236
  332.7 1.5 collective-permute-start.15
  334.8 1.4 down_keep.4
  337.2 2.7 collective-permute-done.22
  339.8 1.5 convert_add_fusion.4
  341.3 1.5 convert_add_fusion.5
  342.9 2.4 constant_dynamic-slice_fusion.4
  346.1 1.8 collective-permute-start.19
  350.2 2.1 collective-permute-start.13
  352.3 4.6 %collective-permute-done.16 = bf16[2,128,384]{2,1,0:T(8,128)(2,1)S(1)} collective-permute-done((bf16[2,128,384]{2,1,0:T(8,128)(2,1)S(1)}, bf16[2,128,384]{2,1,0:T(8,128)(2,1)S(1)}, u32[]{:S(2)}, u32[]{:S(2)}) %collective-permute-start.16) | collective-permute-done | bytes 196640 | tf_op jit(solution)/shard_map/ppermute | solution.py:236
  356.9 1.3 collective-permute-start.17
  358.2 2.8 collective-permute-done.13
  368.2 1.6 copy.38
  369.8 1.6 fusion.12
  371.4 1.7 copy.37
  374.0 1.7 collective-permute-start.25
  377.5 1.3 collective-permute-start.21
  378.8 1.6 copy-done.3
  380.3 2.2 down_send.5
  385.1 1.6 copy.40
  386.7 1.5 fusion.24
  388.2 1.6 copy.39
  389.8 1.6 copy-done.4
  391.4 1.4 down_keep.5
  392.8 1.6 collective-permute-done.31
  395.6 1.7 collective-permute-start.32
  398.9 3.1 collective-permute-done.32
  402.4 2.5 collective-permute-done.28
  405.4 1.9 collective-permute-done.33
  408.6 1.5 collective-permute-done.29
  412.8 2.6 collective-permute-done.30
  (165 shorter events, 42.3 us)
Async XLA Ops:
  1.2 2.0 copy-start.7
  3.2 2.0 copy-start.8
  5.3 4.5 %copy-start.23 = (bf16[128,1792]{1,0:T(8,128)(2,1)S(1)}, bf16[128,1792]{1,0:T(8,128)(2,1)}, u32[]{:S(2)}) copy-start(bf16[128,1792]{1,0:T(8,128)(2,1)} %param.9) | copy-start | bytes 1376260
  5.3 7.3 %copy-start.29 = (f32[128,8]{0,1:T(8,128)S(1)}, f32[128,8]{0,1:T(8,128)}, u32[]{:S(2)}) copy-start(f32[128,8]{0,1:T(8,128)} %param.11) | copy-start | bytes 12292
  5.3 7.3 %copy-start.30 = (s32[128,8]{0,1:T(8,128)S(1)}, s32[128,8]{0,1:T(8,128)}, u32[]{:S(2)}) copy-start(s32[128,8]{0,1:T(8,128)} %param.10) | copy-start | bytes 12292
  5.3 7.3 %copy-start.28 = (s32[16,4]{1,0:T(8,128)S(1)}, s32[16,4]{1,0:T(8,128)}, u32[]{:S(2)}) copy-start(s32[16,4]{1,0:T(8,128)} %constant.24.clone) | copy-start | bytes 772
  7.1 2.7 copy-start.5
  9.8 22.1 %collective-permute-start = (bf16[128,1792]{1,0:T(8,128)(2,1)S(1)}, bf16[128,1792]{1,0:T(8,128)(2,1)S(1)}, u32[]{:S(2)}, u32[]{:S(2)}) collective-permute-start(bf16[128,1792]{1,0:T(8,128)(2,1)S(1)} %copy-done.23), channel_id=1, source_target_pairs={{0,16},{2,18},{4,20},{6,22},{8,24},{10,26},{12,28},{14,30},{16,0},... | collective-permute-start | bytes 1376264 | tf_op jit(solution)/shard_map/ppermute | solution.py:236
  32.0 32.0 %collective-permute-start.1 = (bf16[2,128,1792]{2,1,0:T(8,128)(2,1)S(1)}, bf16[2,128,1792]{2,1,0:T(8,128)(2,1)S(1)}, u32[]{:S(2)}, u32[]{:S(2)}) collective-permute-start(bf16[2,128,1792]{2,1,0:T(8,128)(2,1)S(1)} %get-tuple-element.118), channel_id=1, source_target_pairs={{0,8},{2,10},{4,12},{6,14},{8,0},{10,2},{12,4},{14,6},{16,24},{18,... | collective-permute-start | bytes 2752520 | tf_op jit(solution)/shard_map/ppermute | solution.py:236
  56.4 158.3 %all-to-all-start = ((bf16[16,1568,128]{2,1,0:T(8,128)(2,1)}), bf16[16,1568,128]{2,1,0:T(8,128)(2,1)}, u32[]{:S(2)}, u32[]{:S(2)}) async-start(bf16[16,1568,128]{2,1,0:T(8,128)(2,1)} %copy-done.5), calls=%async_computation | async-start | bytes 12845056 | tf_op jit(solution)/shard_map/all_to_all | solution.py:300
  64.3 41.2 %collective-permute-start.4 = (bf16[2,2,128,896]{3,2,1,0:T(8,128)(2,1)S(1)}, bf16[2,2,128,896]{3,2,1,0:T(8,128)(2,1)S(1)}, u32[]{:S(2)}, u32[]{:S(2)}) collective-permute-start(bf16[2,2,128,896]{3,2,1,0:T(8,128)(2,1)S(1)} %get-tuple-element.108), channel_id=1, source_target_pairs={{0,2},{2,0},{4,6},{6,4},{8,10},{10,8},{12,14},{14,12},{16,18},{18,... | collective-permute-start | bytes 2752520 | tf_op jit(solution)/shard_map/ppermute | solution.py:236
  64.9 58.9 %collective-permute-start.2 = (bf16[2,2,128,896]{3,2,1,0:T(8,128)(2,1)S(1)}, bf16[2,2,128,896]{3,2,1,0:T(8,128)(2,1)S(1)}, u32[]{:S(2)}, u32[]{:S(2)}) collective-permute-start(bf16[2,2,128,896]{3,2,1,0:T(8,128)(2,1)S(1)} %get-tuple-element.107), channel_id=1, source_target_pairs={{0,4},{2,6},{4,0},{6,2},{8,12},{10,14},{12,8},{14,10},{16,20},{18,... | collective-permute-start | bytes 2752520 | tf_op jit(solution)/shard_map/ppermute | solution.py:236
  105.8 77.9 %collective-permute-start.5 = (bf16[2,2,2,128,896]{4,3,2,1,0:T(8,128)(2,1)S(1)}, bf16[2,2,2,128,896]{4,3,2,1,0:T(8,128)(2,1)S(1)}, u32[]{:S(2)}, u32[]{:S(2)}) collective-permute-start(bf16[2,2,2,128,896]{4,3,2,1,0:T(8,128)(2,1)S(1)} %get-tuple-element.110), channel_id=1, source_target_pairs={{0,4},{2,6},{4,0},{6,2},{8,12},{10,14},{12,8},{14,10},{16,20},{18,... | collective-permute-start | bytes 5505032 | tf_op jit(solution)/shard_map/ppermute | solution.py:236
  124.1 80.0 %collective-permute-start.3 = (bf16[2,2,2,128,896]{4,3,2,1,0:T(8,128)(2,1)S(1)}, bf16[2,2,2,128,896]{4,3,2,1,0:T(8,128)(2,1)S(1)}, u32[]{:S(2)}, u32[]{:S(2)}) collective-permute-start(bf16[2,2,2,128,896]{4,3,2,1,0:T(8,128)(2,1)S(1)} %get-tuple-element.106), channel_id=1, source_target_pairs={{0,2},{2,0},{4,6},{6,4},{8,10},{10,8},{12,14},{14,12},{16,18},{18,... | collective-permute-start | bytes 5505032 | tf_op jit(solution)/shard_map/ppermute | solution.py:236
  208.3 26.6 %collective-permute-start.6 = (bf16[2048,1792]{1,0:T(8,128)(2,1)}, bf16[2048,1792]{1,0:T(8,128)(2,1)}, u32[]{:S(2)}, u32[]{:S(2)}) collective-permute-start(bf16[2048,1792]{1,0:T(8,128)(2,1)} %bitcast.131), channel_id=1, source_target_pairs={{0,1},{1,0},{2,3},{3,2},{4,5},{5,4},{6,7},{7,6},{8,9},{9,8},{10,11... | collective-permute-start | bytes 22020104 | tf_op jit(solution)/shard_map/ppermute | solution.py:311
  208.3 2.0 copy-start.6
  214.7 53.3 %all-to-all-start.1 = ((bf16[16,336,128]{2,1,0:T(8,128)(2,1)}), bf16[16,336,128]{2,1,0:T(8,128)(2,1)}, u32[]{:S(2)}, u32[]{:S(2)}) async-start(bf16[16,336,128]{2,1,0:T(8,128)(2,1)} %get-tuple-element.59), calls=%async_computation.1 | async-start | bytes 2752512 | tf_op jit(solution)/shard_map/all_to_all | solution.py:323
  256.2 4.2 %collective-permute-start.7 = (bf16[2048,512]{1,0:T(8,128)(2,1)S(1)}, bf16[2048,512]{1,0:T(8,128)(2,1)S(1)}, u32[]{:S(2)}, u32[]{:S(2)}) collective-permute-start(bf16[2048,512]{1,0:T(8,128)(2,1)S(1)} %hidden.1.own_h), channel_id=1, source_target_pairs={{0,1},{1,0},{2,3},{3,2},{4,5},{5,4},{6,7},{7,6},{8,9},{9,8},{10,11... | collective-permute-start | bytes 6291464 | tf_op jit(solution)/shard_map/ppermute | solution.py:315
  268.1 26.6 %all-to-all-start.3 = ((bf16[16,224,128]{2,1,0:T(8,128)(2,1)}), bf16[16,224,128]{2,1,0:T(8,128)(2,1)}, u32[]{:S(2)}, u32[]{:S(2)}) async-start(bf16[16,224,128]{2,1,0:T(8,128)(2,1)} %copy-done.14), calls=%async_computation.3 | async-start | bytes 1835008 | tf_op jit(solution)/shard_map/all_to_all | solution.py:323
  273.5 3.8 copy-start.1
  275.1 2.2 collective-permute-start.8
  294.7 42.5 %all-to-all-start.4 = ((bf16[16,224,128]{2,1,0:T(8,128)(2,1)}), bf16[16,224,128]{2,1,0:T(8,128)(2,1)}, u32[]{:S(2)}, u32[]{:S(2)}) async-start(bf16[16,224,128]{2,1,0:T(8,128)(2,1)} %get-tuple-element.74), calls=%async_computation.4 | async-start | bytes 1835008 | tf_op jit(solution)/shard_map/all_to_all | solution.py:323
  300.6 27.8 %collective-permute-start.10 = (bf16[1024,384]{1,0:T(8,128)(2,1)}, bf16[1024,384]{1,0:T(8,128)(2,1)S(1)}, u32[]{:S(2)}, u32[]{:S(2)}) collective-permute-start(bf16[1024,384]{1,0:T(8,128)(2,1)} %copy-done.15), channel_id=1, source_target_pairs={{0,4},{2,6},{4,0},{6,2},{8,12},{10,14},{12,8},{14,10},{16,20},{18,... | collective-permute-start | bytes 2359304 | tf_op jit(solution)/shard_map/ppermute | solution.py:236
  301.2 28.5 %collective-permute-start.9 = (bf16[1024,384]{1,0:T(8,128)(2,1)S(1)}, bf16[1024,384]{1,0:T(8,128)(2,1)S(1)}, u32[]{:S(2)}, u32[]{:S(2)}) collective-permute-start(bf16[1024,384]{1,0:T(8,128)(2,1)S(1)} %get-tuple-element.76), channel_id=1, source_target_pairs={{0,2},{2,0},{4,6},{6,4},{8,10},{10,8},{12,14},{14,12},{16,18},{18,... | collective-permute-start | bytes 2359304 | tf_op jit(solution)/shard_map/ppermute | solution.py:236
  303.0 1.9 collective-permute-start.11
  304.9 1.6 copy-start.2
  306.5 23.2 %copy-start.10 = (f32[1024,384]{1,0:T(8,128)S(1)}, f32[1024,384]{1,0:T(8,128)}, u32[]{:S(2)}) copy-start(f32[1024,384]{1,0:T(8,128)} %copy-done.9) | copy-start | bytes 4718596
  306.5 23.2 %copy-start.12 = (f32[1024,384]{1,0:T(8,128)S(1)}, f32[1024,384]{1,0:T(8,128)}, u32[]{:S(2)}) copy-start(f32[1024,384]{1,0:T(8,128)} %copy-done.11) | copy-start | bytes 4718596
  308.8 31.0 %collective-permute-start.22 = (bf16[1024,256]{1,0:T(8,128)(2,1)}, bf16[1024,256]{1,0:T(8,128)(2,1)}, u32[]{:S(2)}, u32[]{:S(2)}) collective-permute-start(bf16[1024,256]{1,0:T(8,128)(2,1)} %get-tuple-element.93), channel_id=1, source_target_pairs={{0,4},{2,6},{4,0},{6,2},{8,12},{10,14},{12,8},{14,10},{16,20},{18,... | collective-permute-start | bytes 1572872 | tf_op jit(solution)/shard_map/ppermute | solution.py:236
  310.3 31.0 %collective-permute-start.18 = (bf16[1024,256]{1,0:T(8,128)(2,1)}, bf16[1024,256]{1,0:T(8,128)(2,1)}, u32[]{:S(2)}, u32[]{:S(2)}) collective-permute-start(bf16[1024,256]{1,0:T(8,128)(2,1)} %get-tuple-element.91), channel_id=1, source_target_pairs={{0,2},{2,0},{4,6},{6,4},{8,10},{10,8},{12,14},{14,12},{16,18},{18,... | collective-permute-start | bytes 1572872 | tf_op jit(solution)/shard_map/ppermute | solution.py:236
  332.7 15.2 %collective-permute-start.15 = (bf16[2,2,128,384]{3,2,1,0:T(8,128)(2,1)}, bf16[2,2,128,384]{3,2,1,0:T(8,128)(2,1)}, u32[]{:S(2)}, u32[]{:S(2)}) collective-permute-start(bf16[2,2,128,384]{3,2,1,0:T(8,128)(2,1)} %bitcast.29), channel_id=1, source_target_pairs={{0,2},{2,0},{4,6},{6,4},{8,10},{10,8},{12,14},{14,12},{16,18},{18,... | collective-permute-start | bytes 1179656 | tf_op jit(solution)/shard_map/ppermute | solution.py:236
  334.3 14.9 %collective-permute-start.12 = (bf16[2,2,128,384]{3,2,1,0:T(8,128)(2,1)S(1)}, bf16[2,2,128,384]{3,2,1,0:T(8,128)(2,1)}, u32[]{:S(2)}, u32[]{:S(2)}) collective-permute-start(bf16[2,2,128,384]{3,2,1,0:T(8,128)(2,1)S(1)} %bitcast.149), channel_id=1, source_target_pairs={{0,4},{2,6},{4,0},{6,2},{8,12},{10,14},{12,8},{14,10},{16,20},{18,... | collective-permute-start | bytes 1179656 | tf_op jit(solution)/shard_map/ppermute | solution.py:236
  342.8 6.2 %copy-start.17 = (f32[1024,256]{1,0:T(8,128)}, f32[1024,256]{1,0:T(8,128)S(1)}, u32[]{:S(2)}) copy-start(f32[1024,256]{1,0:T(8,128)S(1)} %convert_add_fusion.5) | copy-start | bytes 3145732
  342.8 5.1 %copy-start.19 = (f32[512,384]{1,0:T(8,128)S(1)}, f32[512,384]{1,0:T(8,128)}, u32[]{:S(2)}) copy-start(f32[512,384]{1,0:T(8,128)} %slice.187) | copy-start | bytes 2359300
  342.9 6.2 %copy-start.18 = (f32[512,384]{1,0:T(8,128)S(1)}, f32[512,384]{1,0:T(8,128)}, u32[]{:S(2)}) copy-start(f32[512,384]{1,0:T(8,128)} %slice.186) | copy-start | bytes 2359300
  345.3 33.4 %collective-permute-start.26 = (bf16[8,224,128]{2,1,0:T(8,128)(2,1)}, bf16[8,224,128]{2,1,0:T(8,128)(2,1)S(1)}, u32[]{:S(2)}, u32[]{:S(2)}) collective-permute-start(bf16[8,224,128]{2,1,0:T(8,128)(2,1)} %get-tuple-element.113), channel_id=1, source_target_pairs={{0,1},{1,0},{2,3},{3,2},{4,5},{5,4},{6,7},{7,6},{8,9},{9,8},{10,11... | collective-permute-start | bytes 1376264 | tf_op jit(solution)/shard_map/ppermute | solution.py:328
  345.3 17.8 %collective-permute-start.23 = (bf16[2,2,128,256]{3,2,1,0:T(8,128)(2,1)S(1)}, bf16[2,2,128,256]{3,2,1,0:T(8,128)(2,1)S(1)}, u32[]{:S(2)}, u32[]{:S(2)}) collective-permute-start(bf16[2,2,128,256]{3,2,1,0:T(8,128)(2,1)S(1)} %bitcast.157), channel_id=1, source_target_pairs={{0,2},{2,0},{4,6},{6,4},{8,10},{10,8},{12,14},{14,12},{16,18},{18,... | collective-permute-start | bytes 786440 | tf_op jit(solution)/shard_map/ppermute | solution.py:236
  346.1 18.8 %collective-permute-start.19 = (bf16[2,2,128,256]{3,2,1,0:T(8,128)(2,1)S(1)}, bf16[2,2,128,256]{3,2,1,0:T(8,128)(2,1)S(1)}, u32[]{:S(2)}, u32[]{:S(2)}) collective-permute-start(bf16[2,2,128,256]{3,2,1,0:T(8,128)(2,1)S(1)} %bitcast.156), channel_id=1, source_target_pairs={{0,4},{2,6},{4,0},{6,2},{8,12},{10,14},{12,8},{14,10},{16,20},{18,... | collective-permute-start | bytes 786440 | tf_op jit(solution)/shard_map/ppermute | solution.py:236
  349.0 7.8 %collective-permute-start.16 = (bf16[2,128,384]{2,1,0:T(8,128)(2,1)S(1)}, bf16[2,128,384]{2,1,0:T(8,128)(2,1)S(1)}, u32[]{:S(2)}, u32[]{:S(2)}) collective-permute-start(bf16[2,128,384]{2,1,0:T(8,128)(2,1)S(1)} %fusion.8), channel_id=1, source_target_pairs={{0,8},{2,10},{4,12},{6,14},{8,0},{10,2},{12,4},{14,6},{16,24},{18,... | collective-permute-start | bytes 589832 | tf_op jit(solution)/shard_map/ppermute | solution.py:236
  350.2 13.0 %slice-start = ((f32[1024,256]{1,0:T(8,128)}), f32[512,256]{1,0:T(8,128)S(1)}, s32[]{:S(2)}) async-start(f32[1024,256]{1,0:T(8,128)} %copy-done.16), calls=%async_computation.5 | async-start | bytes 1048576 | tf_op jit(solution)/shard_map/slice | solution.py:249
  350.2 14.7 %slice-start.1 = ((f32[1024,256]{1,0:T(8,128)}), f32[512,256]{1,0:T(8,128)S(1)}, s32[]{:S(2)}) async-start(f32[1024,256]{1,0:T(8,128)} %copy-done.17), calls=%async_computation.6 | async-start | bytes 1048576 | tf_op jit(solution)/shard_map/slice | solution.py:249
  350.2 10.8 %collective-permute-start.13 = (bf16[2,128,384]{2,1,0:T(8,128)(2,1)S(1)}, bf16[2,128,384]{2,1,0:T(8,128)(2,1)S(1)}, u32[]{:S(2)}, u32[]{:S(2)}) collective-permute-start(bf16[2,128,384]{2,1,0:T(8,128)(2,1)S(1)} %fusion.7), channel_id=1, source_target_pairs={{0,8},{2,10},{4,12},{6,14},{8,0},{10,2},{12,4},{14,6},{16,24},{18,... | collective-permute-start | bytes 589832 | tf_op jit(solution)/shard_map/ppermute | solution.py:236
  356.9 10.5 %collective-permute-start.17 = (bf16[128,384]{1,0:T(8,128)(2,1)S(1)}, bf16[128,384]{1,0:T(8,128)(2,1)S(1)}, u32[]{:S(2)}, u32[]{:S(2)}) collective-permute-start(bf16[128,384]{1,0:T(8,128)(2,1)S(1)} %fusion.26), channel_id=1, source_target_pairs={{0,16},{2,18},{4,20},{6,22},{8,24},{10,26},{12,28},{14,30},{16,0},... | collective-permute-start | bytes 294920 | tf_op jit(solution)/shard_map/ppermute | solution.py:236
  361.1 5.4 %copy-start.21 = (f32[2,128,384]{2,1,0:T(8,128)}, f32[2,128,384]{2,1,0:T(8,128)S(1)}, u32[]{:S(2)}) copy-start(f32[2,128,384]{2,1,0:T(8,128)S(1)} %fusion.2) | copy-start | bytes 1179652
  361.9 7.9 %collective-permute-start.14 = (bf16[128,384]{1,0:T(8,128)(2,1)}, bf16[128,384]{1,0:T(8,128)(2,1)}, u32[]{:S(2)}, u32[]{:S(2)}) collective-permute-start(bf16[128,384]{1,0:T(8,128)(2,1)} %fusion.25), channel_id=1, source_target_pairs={{0,16},{2,18},{4,20},{6,22},{8,24},{10,26},{12,28},{14,30},{16,0},... | collective-permute-start | bytes 294920 | tf_op jit(solution)/shard_map/ppermute | solution.py:236
  363.9 9.2 %collective-permute-start.24 = (bf16[2,128,256]{2,1,0:T(8,128)(2,1)}, bf16[2,128,256]{2,1,0:T(8,128)(2,1)}, u32[]{:S(2)}, u32[]{:S(2)}) collective-permute-start(bf16[2,128,256]{2,1,0:T(8,128)(2,1)} %fusion.14), channel_id=1, source_target_pairs={{0,8},{2,10},{4,12},{6,14},{8,0},{10,2},{12,4},{14,6},{16,24},{18,... | collective-permute-start | bytes 393224 | tf_op jit(solution)/shard_map/ppermute | solution.py:236
  366.5 9.3 %collective-permute-start.20 = (bf16[2,128,256]{2,1,0:T(8,128)(2,1)}, bf16[2,128,256]{2,1,0:T(8,128)(2,1)}, u32[]{:S(2)}, u32[]{:S(2)}) collective-permute-start(bf16[2,128,256]{2,1,0:T(8,128)(2,1)} %fusion.13), channel_id=1, source_target_pairs={{0,8},{2,10},{4,12},{6,14},{8,0},{10,2},{12,4},{14,6},{16,24},{18,... | collective-permute-start | bytes 393224 | tf_op jit(solution)/shard_map/ppermute | solution.py:236
  374.0 10.4 %collective-permute-start.25 = (bf16[128,256]{1,0:T(8,128)(2,1)S(1)}, bf16[128,256]{1,0:T(8,128)(2,1)S(1)}, u32[]{:S(2)}, u32[]{:S(2)}) collective-permute-start(bf16[128,256]{1,0:T(8,128)(2,1)S(1)} %fusion.28), channel_id=1, source_target_pairs={{0,16},{2,18},{4,20},{6,22},{8,24},{10,26},{12,28},{14,30},{16,0},... | collective-permute-start | bytes 196616 | tf_op jit(solution)/shard_map/ppermute | solution.py:236
  376.8 5.7 %copy-start.22 = (f32[2,128,256]{2,1,0:T(8,128)}, f32[2,128,256]{2,1,0:T(8,128)S(1)}, u32[]{:S(2)}) copy-start(f32[2,128,256]{2,1,0:T(8,128)S(1)} %fusion.6) | copy-start | bytes 786436
  377.5 9.2 %collective-permute-start.21 = (bf16[128,256]{1,0:T(8,128)(2,1)}, bf16[128,256]{1,0:T(8,128)(2,1)}, u32[]{:S(2)}, u32[]{:S(2)}) collective-permute-start(bf16[128,256]{1,0:T(8,128)(2,1)} %fusion.27), channel_id=1, source_target_pairs={{0,16},{2,18},{4,20},{6,22},{8,24},{10,26},{12,28},{14,30},{16,0},... | collective-permute-start | bytes 196616 | tf_op jit(solution)/shard_map/ppermute | solution.py:236
  378.7 1.6 copy-start.3
  382.5 11.8 %collective-permute-start.31 = (bf16[1024,256]{1,0:T(8,128)(2,1)}, bf16[1024,256]{1,0:T(8,128)(2,1)}, u32[]{:S(2)}, u32[]{:S(2)}) collective-permute-start(bf16[1024,256]{1,0:T(8,128)(2,1)} %get-tuple-element.104), channel_id=1, source_target_pairs={{0,4},{2,6},{4,0},{6,2},{8,12},{10,14},{12,8},{14,10},{16,20},{18,... | collective-permute-start | bytes 1572872 | tf_op jit(solution)/shard_map/ppermute | solution.py:236
  383.6 13.7 %collective-permute-start.27 = (bf16[1024,256]{1,0:T(8,128)(2,1)S(1)}, bf16[1024,256]{1,0:T(8,128)(2,1)}, u32[]{:S(2)}, u32[]{:S(2)}) collective-permute-start(bf16[1024,256]{1,0:T(8,128)(2,1)S(1)} %get-tuple-element.102), channel_id=1, source_target_pairs={{0,2},{2,0},{4,6},{6,4},{8,10},{10,8},{12,14},{14,12},{16,18},{18,... | collective-permute-start | bytes 1572872 | tf_op jit(solution)/shard_map/ppermute | solution.py:236
  389.8 1.6 copy-start.4
  395.6 6.4 %collective-permute-start.32 = (bf16[2,2,128,256]{3,2,1,0:T(8,128)(2,1)S(1)}, bf16[2,2,128,256]{3,2,1,0:T(8,128)(2,1)S(1)}, u32[]{:S(2)}, u32[]{:S(2)}) collective-permute-start(bf16[2,2,128,256]{3,2,1,0:T(8,128)(2,1)S(1)} %bitcast.158), channel_id=1, source_target_pairs={{0,2},{2,0},{4,6},{6,4},{8,10},{10,8},{12,14},{14,12},{16,18},{18,... | collective-permute-start | bytes 786440 | tf_op jit(solution)/shard_map/ppermute | solution.py:236
  398.5 6.4 %collective-permute-start.28 = (bf16[2,2,128,256]{3,2,1,0:T(8,128)(2,1)S(1)}, bf16[2,2,128,256]{3,2,1,0:T(8,128)(2,1)S(1)}, u32[]{:S(2)}, u32[]{:S(2)}) collective-permute-start(bf16[2,2,128,256]{3,2,1,0:T(8,128)(2,1)S(1)} %bitcast.159), channel_id=1, source_target_pairs={{0,4},{2,6},{4,0},{6,2},{8,12},{10,14},{12,8},{14,10},{16,20},{18,... | collective-permute-start | bytes 786440 | tf_op jit(solution)/shard_map/ppermute | solution.py:236
  402.1 5.2 %collective-permute-start.33 = (bf16[2,128,256]{2,1,0:T(8,128)(2,1)S(1)}, bf16[2,128,256]{2,1,0:T(8,128)(2,1)S(1)}, u32[]{:S(2)}, u32[]{:S(2)}) collective-permute-start(bf16[2,128,256]{2,1,0:T(8,128)(2,1)S(1)} %fusion.16), channel_id=1, source_target_pairs={{0,8},{2,10},{4,12},{6,14},{8,0},{10,2},{12,4},{14,6},{16,24},{18,... | collective-permute-start | bytes 393224 | tf_op jit(solution)/shard_map/ppermute | solution.py:236
  405.0 10.6 %copy-start.24 = (bf16[128,384]{0,1:T(8,128)(2,1)S(1)}, bf16[128,384]{0,1:T(8,128)(2,1)}, u32[]{:S(2)}) copy-start(bf16[128,384]{0,1:T(8,128)(2,1)} %copy.38) | copy-start | bytes 294916
  405.0 10.6 %copy-start.25 = (bf16[128,384]{0,1:T(8,128)(2,1)S(1)}, bf16[128,384]{0,1:T(8,128)(2,1)}, u32[]{:S(2)}) copy-start(bf16[128,384]{0,1:T(8,128)(2,1)} %copy.37) | copy-start | bytes 294916
  405.0 10.6 %copy-start.26 = (bf16[128,256]{0,1:T(8,128)(2,1)S(1)}, bf16[128,256]{0,1:T(8,128)(2,1)}, u32[]{:S(2)}) copy-start(bf16[128,256]{0,1:T(8,128)(2,1)} %copy.40) | copy-start | bytes 196612
  405.0 10.6 %copy-start.27 = (bf16[128,256]{0,1:T(8,128)(2,1)S(1)}, bf16[128,256]{0,1:T(8,128)(2,1)}, u32[]{:S(2)}) copy-start(bf16[128,256]{0,1:T(8,128)(2,1)} %copy.39) | copy-start | bytes 196612
  405.1 5.0 %collective-permute-start.29 = (bf16[2,128,256]{2,1,0:T(8,128)(2,1)S(1)}, bf16[2,128,256]{2,1,0:T(8,128)(2,1)S(1)}, u32[]{:S(2)}, u32[]{:S(2)}) collective-permute-start(bf16[2,128,256]{2,1,0:T(8,128)(2,1)S(1)} %fusion.15), channel_id=1, source_target_pairs={{0,8},{2,10},{4,12},{6,14},{8,0},{10,2},{12,4},{14,6},{16,24},{18,... | collective-permute-start | bytes 393224 | tf_op jit(solution)/shard_map/ppermute | solution.py:236
  407.3 5.3 %collective-permute-start.34 = (bf16[128,256]{1,0:T(8,128)(2,1)S(1)}, bf16[128,256]{1,0:T(8,128)(2,1)S(1)}, u32[]{:S(2)}, u32[]{:S(2)}) collective-permute-start(bf16[128,256]{1,0:T(8,128)(2,1)S(1)} %fusion.30), channel_id=1, source_target_pairs={{0,16},{2,18},{4,20},{6,22},{8,24},{10,26},{12,28},{14,30},{16,0},... | collective-permute-start | bytes 196616 | tf_op jit(solution)/shard_map/ppermute | solution.py:236
  410.1 5.2 %collective-permute-start.30 = (bf16[128,256]{1,0:T(8,128)(2,1)S(1)}, bf16[128,256]{1,0:T(8,128)(2,1)S(1)}, u32[]{:S(2)}, u32[]{:S(2)}) collective-permute-start(bf16[128,256]{1,0:T(8,128)(2,1)S(1)} %fusion.29), channel_id=1, source_target_pairs={{0,16},{2,18},{4,20},{6,22},{8,24},{10,26},{12,28},{14,30},{16,0},... | collective-permute-start | bytes 196616 | tf_op jit(solution)/shard_map/ppermute | solution.py:236
  (8 other events, 8.8 us)

commit v2 on v1

v2 whole, which is shorter than its diff:
```python
import functools

import jax
import jax.numpy as jnp
from jax import lax
from jax.experimental import pallas as pl
from jax.experimental.pallas import tpu as pltpu
from jax.sharding import PartitionSpec as P

LANES = 128
HALF = 64
MIB = 1 << 20


def distinct_sources(old_expert, new_expert):
    slots = old_expert.shape[0]
    index = jnp.arange(slots, dtype=jnp.int32)
    holders = new_expert[:, None] == old_expert[None, :]
    source = jnp.min(jnp.where(holders, index[None, :], slots), axis=1)
    used = jnp.any(source[:, None] == index[None, :], axis=0)
    earlier = (index[None, :] < index[:, None]) & used[None, :]
    place = jnp.sum(earlier.astype(jnp.int32), axis=1)
    count = slots - slots // 8
    wanted = jnp.arange(count, dtype=jnp.int32)
    listing = jnp.sum(
        jnp.where(used[None, :] & (place[None, :] == wanted[:, None]), index[None, :], 0), axis=1
    )
    slot_place = jnp.sum(jnp.where(source[:, None] == index[None, :], place[None, :], 0), axis=1)
    return source, listing, slot_place


def units_of(dest):
    if dest % 2 == 0:
        start = 7 * dest // 2
        return start, start + 3, 0
    start = (7 * dest + 1) // 2
    return start, start - 1, 1


def pack_rows(slab_of, out_ref, base, dest, lo, rows, per_slab):
    first, half, side = units_of(dest)
    for number in range(3):
        unit = first + number
        ref, slab = slab_of(unit // per_slab)
        lane = (unit % per_slab) * LANES
        out_ref[dest, base + number * rows : base + (number + 1) * rows, :] = ref[
            slab, lo : lo + rows, lane : lane + LANES
        ]
    ref, slab = slab_of(half // per_slab)
    lane = (half % per_slab) * LANES
    mid = rows // 2
    top = ref[slab, lo : lo + mid, lane : lane + LANES].astype(jnp.float32)
    low = ref[slab, lo + mid : lo + rows, lane : lane + LANES].astype(jnp.float32)
    left = lax.broadcasted_iota(jnp.int32, (mid, LANES), 1) < HALF
    if side == 0:
        both = jnp.where(left, top, pltpu.roll(low, HALF, 1))
    else:
        both = jnp.where(left, pltpu.roll(top, HALF, 1), low)
    out_ref[dest, base + 3 * rows : base + 3 * rows + mid, :] = both.astype(out_ref.dtype)


def pack_gate_kernel(list_ref, gate_ref, share_ref, out_ref):
    slots, depth, width = gate_ref.shape
    size = depth * 7 // 2
    row = lax.broadcasted_iota(jnp.int32, share_ref.shape[1:], 0) // 4
    for dest in range(out_ref.shape[0]):
        pack_rows(
            lambda place: (gate_ref, list_ref[place]),
            out_ref, 0, dest, 0, depth, width // LANES,
        )
        value = share_ref[dest]
        high = value.astype(out_ref.dtype)
        rest = value - high.astype(jnp.float32)
        middle = rest.astype(out_ref.dtype)
        low = (rest - middle.astype(jnp.float32)).astype(out_ref.dtype)
        terms = jnp.where(
            row == 0,
            high.astype(jnp.float32),
            jnp.where(
                row == 1,
                middle.astype(jnp.float32),
                jnp.where(row == 2, low.astype(jnp.float32), 0.0),
            ),
        )
        out_ref[dest, size:, :] = terms.astype(out_ref.dtype)


def pack_kernel(parts, list_ref, in_ref, *out_refs):
    slots, depth, width = in_ref.shape
    for dest in range(out_refs[0].shape[0]):
        lo = 0
        for rows, out_ref in zip(parts, out_refs):
            pack_rows(
                lambda place: (in_ref, list_ref[place]),
                out_ref, 0, dest, lo, rows, width // LANES,
            )
            lo += rows


def vmem():
    return pl.BlockSpec(memory_space=pltpu.VMEM)


def smem():
    return pl.BlockSpec(memory_space=pltpu.SMEM)


def pack_gate(listing, gate_proj, share, dests):
    slots, depth, width = gate_proj.shape
    shape = (dests, depth * 7 // 2 + share.shape[1], LANES)
    return pl.pallas_call(
        pack_gate_kernel,
        out_shape=jax.ShapeDtypeStruct(shape, gate_proj.dtype),
        in_specs=[smem(), vmem(), vmem()],
        out_specs=vmem(),
        compiler_params=pltpu.CompilerParams(vmem_limit_bytes=32 * MIB),
        name="pack_gate",
    )(listing, gate_proj, share)


def pack(listing, weights, dests, parts, name):
    return pl.pallas_call(
        functools.partial(pack_kernel, parts),
        out_shape=[
            jax.ShapeDtypeStruct((dests, rows * 7 // 2, LANES), weights.dtype) for rows in parts
        ],
        in_specs=[smem(), vmem()],
        out_specs=[vmem()] * len(parts),
        compiler_params=pltpu.CompilerParams(vmem_limit_bytes=32 * MIB),
        name=name,
    )(listing, weights)


def unpack_rows(in_ref, at, base, rows, out_ref, out_row, out_lane):
    for number in range(3):
        out_ref[out_row : out_row + rows, out_lane + number * LANES : out_lane + (number + 1) * LANES] = (
            in_ref[at, base + number * rows : base + (number + 1) * rows, :]
        )
    mid = rows // 2
    both = in_ref[at, base + 3 * rows : base + 3 * rows + mid, :]
    lanes = slice(out_lane + 3 * LANES, out_lane + 4 * LANES)
    out_ref[out_row : out_row + mid, lanes] = both
    out_ref[out_row + mid : out_row + rows, lanes] = pltpu.roll(
        both.astype(jnp.float32), HALF, 1
    ).astype(out_ref.dtype)


def hidden_kernel(at_ref, *refs):
    pieces, (gate_ref, up_ref, out_ref, gate_w, up_w, rows) = refs[:8], refs[8:]
    sources, packed_rows, _ = up_ref.shape
    depth = packed_rows * 2 // 7
    group = sources // 2
    tile = pl.program_id(0)
    x, y, zl = tile // 4, tile // 2 % 2, tile % 2
    me, core = at_ref[0], at_ref[1]

    @pl.when(tile == 0)
    def _():
        for at in range(sources):
            place = (core + at // group) % 2 * group + at % group
            unpack_rows(gate_ref, place, 0, depth, gate_w, at * depth, 0)
            unpack_rows(up_ref, place, 0, depth, up_w, at * depth, 0)

    mid = pieces[0].shape[1]
    for number in range(4):
        lanes = slice(number * mid, (number + 1) * mid)
        coordinate = (x, y)[number % 2]
        for value in range(2):

            @pl.when(coordinate == value)
            def _():
                rows[:, lanes] = pieces[2 * number + value][...]

    gate = jnp.dot(rows[...], gate_w[...], preferred_element_type=jnp.float32)
    up = jnp.dot(rows[...], up_w[...], preferred_element_type=jnp.float32)
    value = gate / (1.0 + jnp.exp(-gate)) * up

    wide = gate.shape[1]
    term = lax.broadcasted_iota(jnp.int32, (16, wide), 0)
    lane = lax.broadcasted_iota(jnp.int32, (16, wide), 1)
    chosen = (term % 4 == lane // LANES) & (term < 12) & (lane < wide - HALF)
    chosen = jnp.where(chosen, 1.0, 0.0).astype(jnp.bfloat16)
    block = rows.shape[0] // 2
    for zh in range(2):
        source = me ^ (x + 2 * y + 4 * zl + 8 * zh)
        weight = lax.dot_general(
            gate_ref[source, packed_rows:, :],
            chosen,
            (((0,), (0,)), ((), ())),
            preferred_element_type=jnp.float32,
        )
        span = slice(zh * block, (zh + 1) * block)
        out_ref[span, :] = (value[span, :] * weight).astype(out_ref.dtype)


def hidden_units(at, pieces, gate, up):
    total = 2 * pieces[0].shape[0]
    mid = pieces[0].shape[1]
    tile = total // 8
    wide = 4 * LANES
    model = 4 * mid
    by_x = [lambda i: (jnp.minimum(i, 3), 0), lambda i: (jnp.maximum(i - 4, 0), 0)]
    by_y = [
        lambda i: (i // 4 * 2 + jnp.where(i // 2 % 2 == 0, i % 2, 1), 0),
        lambda i: (i // 4 * 2 + jnp.where(i // 2 % 2 == 1, i % 2, 0), 0),
    ]
    maps = (by_x + by_y) * 2
    return pl.pallas_call(
        hidden_kernel,
        grid=(8,),
        out_shape=jax.ShapeDtypeStruct((total, wide), up.dtype),
        in_specs=[smem()]
        + [pl.BlockSpec((tile, mid), where) for where in maps]
        + [vmem(), vmem()],
        out_specs=pl.BlockSpec((tile, wide), lambda i: (i, 0)),
        scratch_shapes=[pltpu.VMEM((model, wide), up.dtype)] * 2
        + [pltpu.VMEM((tile, model), up.dtype)],
        compiler_params=pltpu.CompilerParams(vmem_limit_bytes=40 * MIB),
        cost_estimate=pl.CostEstimate(
            flops=4 * total * model * wide, bytes_accessed=24 * MIB, transcendentals=total * wide
        ),
        name="hidden",
    )(at, *pieces, gate, up)


def down_kernel(rows, side, own_h, other_h, own_ref, other_ref, out_a, out_b, own_w, other_w):
    for in_ref, w_ref in ((own_ref, own_w), (other_ref, other_w)):
        for at in range(in_ref.shape[0]):
            unpack_rows(in_ref, at, 0, rows, w_ref, at * rows, 0)
    half = own_w.shape[0] // 2
    quarter = own_h.shape[0] // 4

    def product(at, size, span):
        tokens = slice(at * quarter, (at + size) * quarter)
        dims = (((1,), (1,)), ((), ()))
        return lax.dot_general(
            own_h[tokens, :], own_w[span, :], dims, preferred_element_type=jnp.float32
        ) + lax.dot_general(
            other_h[tokens, :], other_w[span, :], dims, preferred_element_type=jnp.float32
        )

    out_a[...] = product(2 * side, 2, slice(0, half)).astype(out_a.dtype)
    for first in range(2):
        out_b[first * quarter : (first + 1) * quarter, :] = product(
            2 * first + side, 1, slice(half, 2 * half)
        ).astype(out_b.dtype)


def down_product(own_h, other_h, own, other, rows, side, dtype, name):
    sources = own.shape[0]
    total, wide = own_h.shape
    tokens = total // 2
    features = sources * rows // 2
    return pl.pallas_call(
        functools.partial(down_kernel, rows, side),
        out_shape=[jax.ShapeDtypeStruct((tokens, features), dtype)] * 2,
        in_specs=[vmem()] * 4,
        out_specs=[vmem()] * 2,
        scratch_shapes=[pltpu.VMEM((sources * rows, wide), own.dtype)] * 2,
        compiler_params=pltpu.CompilerParams(vmem_limit_bytes=40 * MIB),
        cost_estimate=pl.CostEstimate(
            flops=8 * tokens * wide * features, bytes_accessed=8 * MIB, transcendentals=0
        ),
        name=name,
    )(own_h, other_h, own, other)


def halve_kernel(joined, *refs):
    count = (len(refs) - 2 * (1 if joined else 0)) // 2 if joined else len(refs) // 4
    out_refs = refs[2 * count :]
    lane = 0
    for number in range(count):
        keep_ref, come_ref = refs[2 * number : 2 * number + 2]
        half = keep_ref.shape[0] // 2
        total = keep_ref[...] + come_ref[...].astype(jnp.float32)
        if joined:
            send_ref, left_ref = out_refs
            lanes = slice(lane, lane + keep_ref.shape[1])
            lane += keep_ref.shape[1]
        else:
            send_ref, left_ref = out_refs[2 * number : 2 * number + 2]
            lanes = slice(0, keep_ref.shape[1])
        send_ref[:, lanes] = total[half:, :].astype(send_ref.dtype)
        left_ref[:, lanes] = total[:half, :]


def halve(pairs, joined):
    sizes = [(keep.shape[0] // 2, keep.shape[1]) for keep, _ in pairs]
    if joined:
        sizes = [(sizes[0][0], sum(width for _, width in sizes))]
    shapes = []
    for size in sizes:
        shapes += [jax.ShapeDtypeStruct(size, jnp.bfloat16), jax.ShapeDtypeStruct(size, jnp.float32)]
    out = pl.pallas_call(
        functools.partial(halve_kernel, joined),
        out_shape=shapes,
        in_specs=[vmem()] * (2 * len(pairs)),
        out_specs=[vmem()] * len(shapes),
        compiler_params=pltpu.CompilerParams(vmem_limit_bytes=40 * MIB),
        cost_estimate=pl.CostEstimate(
            flops=sum(keep.size for keep, _ in pairs), bytes_accessed=4 * MIB, transcendentals=0
        ),
        name="sum_stage",
    )(*[value for pair in pairs for value in pair])
    return [(out[2 * n], out[2 * n + 1]) for n in range(len(out) // 2)]


def swap(value, bit):
    size = lax.axis_size("ep")
    return lax.ppermute(value, "ep", [(i, i ^ (1 << bit)) for i in range(size)])


def gather_bits(value, bits, order, have=()):
    have = list(have)
    for bit in order:
        axis = sum(1 for b in have if b < bit)
        value = jnp.stack([value, swap(value, bit)], axis=axis)
        have.append(bit)
    return value


def take_half(value, axis, number):
    return lax.index_in_dim(value, number, axis, keepdims=False)


def sum_stages(keep, arrived, order, left):
    left = list(left)
    for bit in order:
        axis = left.index(bit)
        total = keep + arrived.astype(jnp.float32)
        arrived = swap(take_half(total, axis, 1).astype(jnp.bfloat16), bit)
        keep = take_half(total, axis, 0)
        left.remove(bit)
    return keep, arrived


def share_of_slots(slot_ids, gate_weights, slots):
    index = jnp.arange(slots, dtype=jnp.int32)
    picked = slot_ids.T[None, :, :] == index[:, None, None]
    return jnp.sum(jnp.where(picked, gate_weights.T[None, :, :], 0.0), axis=1)


def packed_layer(
    tokens, slot_ids, gate_weights, old_expert, new_expert, gate_proj, up_proj, down_proj
):
    devices = lax.axis_size("ep")
    slots, depth, width = gate_proj.shape
    block = tokens.shape[0]
    me = lax.axis_index("ep")
    core = lax.axis_index("et")
    group = devices // 2
    tie = lax.optimization_barrier
    _, listing, slot_place = distinct_sources(old_expert, new_expert)

    def exchange(value):
        return lax.ppermute(value, "et", [(0, 1), (1, 0)])

    def move(packed):
        return lax.all_to_all(packed, "ep", 0, 0, tiled=True)

    places = []
    for dest in range(devices):
        first, half, _ = units_of(dest)
        places.append([unit // (width // LANES) for unit in (first, first + 1, first + 2, half)] * 4)
    places = jnp.asarray(places, jnp.int32)
    share = share_of_slots(slot_ids, gate_weights, slots)
    belongs = slot_place[None, None, :, None] == places[:, :, None, None]
    share = jnp.sum(jnp.where(belongs, share[None, None], 0.0), axis=2)

    gate = move(pack_gate(listing, gate_proj, share, devices))
    mid = tokens.shape[1] // 2
    rows = jnp.concatenate([tokens, swap(tokens, 3)], axis=0)
    rows = jnp.concatenate([rows, swap(rows, 2)], axis=0)
    first, second = rows[:, :mid], rows[:, mid:]
    first = jnp.concatenate([first, swap(first, 1)], axis=0)
    second = jnp.concatenate([second, swap(second, 0)], axis=0)
    (up_packed,) = pack(listing, up_proj, devices, (depth,), "pack_up")
    gate, first, second, up_packed = tie((gate, first, second, up_packed))

    up = move(up_packed)
    pieces = [first, swap(first, 0), second, swap(second, 1)]
    others = [exchange(first), None, exchange(second), None]
    parts = (128, 64, 32)
    down_packed = pack(listing, down_proj, devices, parts, "pack_down")
    up, pieces, others[0], others[2], down_packed = tie(
        (up, pieces, others[0], others[2], down_packed)
    )

    down0 = move(down_packed[0])
    others[1], others[3] = exchange(pieces[1]), exchange(pieces[3])
    at = jnp.stack([me, core]).astype(jnp.int32)
    hidden = hidden_units(at, pieces + others, gate, up)
    hidden_other = exchange(hidden)
    down0, hidden, hidden_other, packed = tie((down0, hidden, hidden_other, down_packed[1]))

    def products(down, rows_in):
        own = lax.dynamic_slice_in_dim(down, core * group, group, 0)
        other = exchange(lax.dynamic_slice_in_dim(down, (1 - core) * group, group, 0))
        args = (hidden, hidden_other, own, other)
        sent = down_product(*args, rows_in, 1, jnp.bfloat16, "down_send")
        sent, args = tie((sent, args))
        come = [swap(value, bit) for bit, value in enumerate(sent)]
        return list(zip(down_product(*args, rows_in, 0, jnp.float32, "down_keep"), come))

    def cross(pairs):
        (send_a, keep_a), (send_b, keep_b) = halve(pairs, False)
        return [(keep_a, swap(send_a, 1)), (keep_b, swap(send_b, 0))]

    def along(pairs, bit):
        ((send, keep),) = halve(pairs, True)
        return [(keep, swap(send, bit))]

    def finish(pairs):
        ((keep, come),) = pairs
        return (keep + come.astype(jnp.float32)).astype(jnp.bfloat16)

    down1 = move(packed)
    sums0 = products(down0, parts[0])
    down1, sums0, packed = tie((down1, sums0, down_packed[2]))
    down2 = move(packed)
    sums0 = cross(sums0)
    sums1 = products(down1, parts[1])
    down2, sums0, sums1 = tie((down2, sums0, sums1))
    sums2 = products(down2, parts[2])
    sums1 = cross(sums1)
    sums01 = along(sums0 + sums1, 2)
    sums2 = cross(sums2)
    sums01 = along(sums01, 3)
    sums2 = along(along(sums2, 2), 3)

    out01, out2 = finish(sums01), finish(sums2)
    out = []
    lane = 0
    for rows_in in parts[:2]:
        wide = group * rows_in
        out.append(out01[:, lane : lane + wide].reshape(block, group, rows_in))
        lane += wide
    out.append(out2.reshape(block, group, parts[2]))
    return jnp.concatenate(out, axis=2).reshape(tokens.shape)


def plain_layer(
    tokens, slot_ids, gate_weights, old_expert, new_expert, gate_proj, up_proj, down_proj
):
    devices = lax.axis_size("ep")
    bits = devices.bit_length() - 1
    slots = gate_proj.shape[0]
    me = lax.axis_index("ep")
    source, _, _ = distinct_sources(old_expert, new_expert)

    def move(weights):
        chosen = jnp.take(weights, source, axis=0, mode="clip")
        return lax.all_to_all(chosen, "ep", 0, 0, tiled=True)

    gate_slab = move(gate_proj).reshape(-1, gate_proj.shape[-1])
    up_slab = move(up_proj).reshape(-1, up_proj.shape[-1])
    down = move(down_proj)
    order = range(bits - 1, -1, -1)
    rows = gather_bits(tokens, bits, order).reshape(-1, tokens.shape[1])
    rows = lax.all_gather(rows, "et", axis=1, tiled=True)
    share = gather_bits(share_of_slots(slot_ids, gate_weights, slots), bits, order)
    share = lax.dynamic_index_in_dim(share, me, bits, keepdims=False).reshape(-1, 1)
    gate_part = jnp.dot(rows, gate_slab, preferred_element_type=jnp.float32)
    up_part = jnp.dot(rows, up_slab, preferred_element_type=jnp.float32)
    hidden = (jax.nn.silu(gate_part) * up_part * share).astype(jnp.bfloat16)
    hidden = lax.all_gather(hidden, "et", axis=1, tiled=True)
    down = lax.all_to_all(down, "et", 0, 2, tiled=True)
    value = lax.dot_general(
        hidden,
        down.reshape(-1, down.shape[-1]),
        (((1,), (1,)), ((), ())),
        preferred_element_type=jnp.float32,
    )
    value = value.reshape((2,) * bits + (-1,) + value.shape[1:])
    arrived = swap(take_half(value, 0, 1).astype(jnp.bfloat16), 0)
    left = list(range(1, bits))
    keep, arrived = sum_stages(take_half(value, 0, 0), arrived, left, left)
    return (keep + arrived.astype(jnp.float32)).astype(jnp.bfloat16)


def per_device(tokens, slot_ids, gate_weights, old_expert, new_expert, gate_proj, up_proj, down_proj):
    slots, depth, width = gate_proj.shape
    count = slots - slots // 8
    devices = lax.axis_size("ep")
    fits = (
        lax.axis_size("et") == 2
        and depth == 224
        and width % LANES == 0
        and count * width == devices * 7 * HALF
        and devices == 16
        and tokens.shape[0] == LANES
    )
    layer = packed_layer if fits else plain_layer
    return layer(
        tokens, slot_ids, gate_weights, old_expert, new_expert, gate_proj, up_proj, down_proj
    )


def solution(mesh):
    placed = (
        P("ep", "et"),
        P("ep", None),
        P("ep", None),
        P(),
        P(),
        P(None, "ep", "et"),
        P(None, "ep", "et"),
        P(None, "ep", "et"),
    )
    return jax.shard_map(
        per_device, mesh=mesh, in_specs=placed, out_specs=P("ep", "et"), check_vma=False
    )
```

time: 421 us -> 439 us (1.043)
  waiting for transfers between devices: 223 us -> 272 us
  blocking collectives: 22.7 us -> 0 us
  Pallas kernels: 37.9 us -> 50.6 us
  other arithmetic: 17.7 us -> 5.57 us
  starting transfers between devices: 70.5 us -> 59.5 us
    ppermute x30 -> x22, waiting for transfers between devices: 200 us -> 253 us  [swap(): return lax.ppermute(value, 'ep', [(i, i ^ 1 << bit) for i in range(size)])]
    all_to_all x1 -> x0, blocking collectives: 22.7 us -> none  [packed_layer(): unit_share = lax.all_to_all(unit_share, 'ep', 0, 0, tiled=True)]
    unnamed x62 -> x76, local copies, waits for them, and re-layouts: 20.9 us -> 38.2 us
    pallas_call x3 -> x11, Pallas kernels: 25.6 us -> 35.7 us  [the longest x1 24.2 us: hidden_units(): pl.pallas_call(hidden_kernel, grid=(8,), out_shape=jax.ShapeDtypeStruct((...]
    add x17 -> x0, other arithmetic: 9.94 us -> none  [sum_stages(): total = keep + arrived.astype(jnp.float32)]
    another operation x6 -> x0, local copies, waits for them, and re-layouts: 6.65 us -> none  [finish(): total = with_layout_constraint(total, row_major)]
    ppermute x5 -> x8, waiting for transfers between devices: 8.09 us -> 1.49 us  [exchange(): return lax.ppermute(value, 'et', [(0, 1), (1, 0)])]
    all_to_all x4 -> x5, starting transfers between devices: 39.2 us -> 33.2 us  [move(): return lax.all_to_all(packed, 'ep', 0, 0, tiled=True)]
  transfers between devices with their start and end apart: 39 -> 35, of which waited for: 22 -> 20; matrix products, arithmetic and copies ran while one was open for 9% -> 1% of each run, Pallas kernels for 9% -> 11%
where the time goes in v2:
time: 439 us; the launch traced here: 434 us
  waiting for transfers between devices  272 us (62%)
  starting transfers between devices  59.5 us (14%)
  Pallas kernels  50.6 us (12%)
  local copies, waits for them, and re-layouts  45.8 us (10%)
  other arithmetic  5.57 us (1%)
    ppermute x22, waiting for transfers between devices, swap(): return lax.ppermute(value, 'ep', [(i, i ^ 1 << bit) for i in range(size)])  253 us
    unnamed x76, local copies, waits for them, and re-layouts  38.2 us
    all_to_all x5, starting transfers between devices, move(): return lax.all_to_all(packed, 'ep', 0, 0, tiled=True)  33.2 us
    ppermute x22, starting transfers between devices, swap(): return lax.ppermute(value, 'ep', [(i, i ^ 1 << bit) for i in range(size)])  25.2 us
    pallas_call x1, Pallas kernels, hidden_units(): pl.pallas_call(hidden_kernel, grid=(8,), out_shape=jax.ShapeDtypeStruct((...  24.2 us
    all_to_all x5, waiting for transfers between devices, move(): return lax.all_to_all(packed, 'ep', 0, 0, tiled=True)  18.3 us
    pallas_call x6, Pallas kernels, down_product(): pl.pallas_call(functools.partial(down_kernel, rows, side), out_shape=[jax...  14.9 us
  transfers between devices with their start and end apart: 35, of which 20 were waited for; matrix products, arithmetic and copies ran while one was open for 1% of the time, Pallas kernels for 11%

profile of v2, /device:TPU:14, one launch (start us, length us, event | category | flops | bytes accessed | tf_op | source)
XLA Modules:
  0.0 434.1 jit_solution(8578907299633627523)
XLA Ops:
  3.8 2.0 copy-done.5
  5.9 2.9 pack_gate.1
  8.7 7.3 %all-to-all-start = ((bf16[16,800,128]{2,1,0:T(8,128)(2,1)}), bf16[16,800,128]{2,1,0:T(8,128)(2,1)}, u32[]{:S(2)}, u32[]{:S(2)}) async-start(bf16[16,800,128]{2,1,0:T(8,128)(2,1)} %pack_gate.1), calls=%async_computation | async-start | bytes 6553600 | tf_op jit(solution)/shard_map/all_to_all | solution.py:359
  16.0 2.4 collective-permute-start
  18.5 88.7 %collective-permute-done = bf16[128,1792]{1,0:T(8,128)(2,1)S(1)} collective-permute-done((bf16[128,1792]{1,0:T(8,128)(2,1)S(1)}, bf16[128,1792]{1,0:T(8,128)(2,1)S(1)}, u32[]{:S(2)}, u32[]{:S(2)}) %collective-permute-start) | collective-permute-done | bytes 458784 | tf_op jit(solution)/shard_map/ppermute | solution.py:310
  107.2 2.2 collective-permute-start.1
  109.5 19.5 %collective-permute-done.1 = bf16[256,1792]{1,0:T(8,128)(2,1)S(1)} collective-permute-done((bf16[256,1792]{1,0:T(8,128)(2,1)S(1)}, bf16[256,1792]{1,0:T(8,128)(2,1)S(1)}, u32[]{:S(2)}, u32[]{:S(2)}) %collective-permute-start.1) | collective-permute-done | bytes 917536 | tf_op jit(solution)/shard_map/ppermute | solution.py:310
  129.2 1.6 collective-permute-start.3
  131.1 2.8 pack_up.1
  133.9 16.0 %collective-permute-done.3 = bf16[512,896]{1,0:T(8,128)(2,1)S(1)} collective-permute-done((bf16[512,896]{1,0:T(8,128)(2,1)S(1)}, bf16[512,896]{1,0:T(8,128)(2,1)S(1)}, u32[]{:S(2)}, u32[]{:S(2)}) %collective-permute-start.3) | collective-permute-done | bytes 917536 | tf_op jit(solution)/shard_map/ppermute | solution.py:310
  151.2 1.4 pad_maximum_fusion.refs_0_
  152.6 6.0 %all-to-all-start.1 = ((bf16[16,784,128]{2,1,0:T(8,128)(2,1)}), bf16[16,784,128]{2,1,0:T(8,128)(2,1)}, u32[]{:S(2)}, u32[]{:S(2)}) async-start(bf16[16,784,128]{2,1,0:T(8,128)(2,1)} %pack_up.1), calls=%async_computation.1 | async-start | bytes 6422528 | tf_op jit(solution)/shard_map/all_to_all | solution.py:359
  160.2 2.0 copy-done.7
  162.3 2.2 pack_down.1
  164.4 1.3 copy-done.12
  165.7 65.0 %collective-permute-done.4.refs_1_ = bf16[1024,896]{1,0:T(8,128)(2,1)S(1)} collective-permute-done((bf16[1024,896]{1,0:T(8,128)(2,1)}, bf16[1024,896]{1,0:T(8,128)(2,1)S(1)}, u32[]{:S(2)}, u32[]{:S(2)}) %collective-permute-start.4) | collective-permute-done | bytes 1835040 | tf_op jit(solution)/shard_map/ppermute | solution.py:310
  230.7 1.3 copy-done.28
  231.9 1.3 copy-done.30
  233.2 1.3 copy-done.32
  234.5 1.3 copy-done.34
  236.4 7.1 %all-to-all-start.2 = ((bf16[16,448,128]{2,1,0:T(8,128)(2,1)}), bf16[16,448,128]{2,1,0:T(8,128)(2,1)}, u32[]{:S(2)}, u32[]{:S(2)}) async-start(bf16[16,448,128]{2,1,0:T(8,128)(2,1)} %copy-done.12), calls=%async_computation.2 | async-start | bytes 3670016 | tf_op jit(solution)/shard_map/all_to_all | solution.py:359
  243.6 1.5 copy-done.13
  245.1 1.5 copy-done.29
  246.6 1.5 copy-done.31
  248.1 1.5 copy-done.33
  249.6 1.5 copy-done.35
  251.1 24.2 %hidden.1.own_h = bf16[2048,512]{1,0:T(8,128)(2,1)} custom-call(s32[2]{0:T(128)S(1)} %pad_add_fusion.at_ref, bf16[1024,896]{1,0:T(8,128)(2,1)S(1)} %copy-done.13, bf16[1024,896]{1,0:T(8,128)(2,1)S(1)} %copy-done.29, bf16[1024,896]{1,0:T(8,128)(2,1)S(1)} %pad_maximum_fusion.1.refs_2_, bf16[1024,896]{1,0:T(8,128)(2,1)S(1)} %copy-done.31, ...), custom_call_target="tpu_custom_call" | custom-call | flops 15032385536 | bytes 25165824 | tf_op jit(solution)/shard_map/hidden/pallas_call | solution.py:208
  275.2 10.8 %all-to-all-done.2 = bf16[16,448,128]{2,1,0:T(8,128)(2,1)} async-done(((bf16[16,448,128]{2,1,0:T(8,128)(2,1)}), bf16[16,448,128]{2,1,0:T(8,128)(2,1)}, u32[]{:S(2)}, u32[]{:S(2)}) %all-to-all-start.2) | async-done | bytes 1835040 | tf_op jit(solution)/shard_map/all_to_all | solution.py:359
  286.1 1.3 copy-done.1
  287.4 2.7 constant_dynamic-slice_fusion.4
  290.1 5.3 %all-to-all-start.3 = ((bf16[16,224,128]{2,1,0:T(8,128)(2,1)}), bf16[16,224,128]{2,1,0:T(8,128)(2,1)}, u32[]{:S(2)}, u32[]{:S(2)}) async-start(bf16[16,224,128]{2,1,0:T(8,128)(2,1)} %get-tuple-element.107), calls=%async_computation.3 | async-start | bytes 1835008 | tf_op jit(solution)/shard_map/all_to_all | solution.py:359
  295.4 1.6 copy-done.2
  296.9 4.9 %down_send.3 = (bf16[1024,512]{1,0:T(8,128)(2,1)}, bf16[1024,512]{1,0:T(8,128)(2,1)}) custom-call(bf16[2048,512]{1,0:T(8,128)(2,1)S(1)} %copy-done, bf16[2048,512]{1,0:T(8,128)(2,1)S(1)} %copy-done.2, bf16[8,448,128]{2,1,0:T(8,128)(2,1)S(1)} %get-tuple-element.115.own_ref, bf16[8,448,128]{2,1,0:T(8,128)(2,1)} %collective-permute-done.11.other_ref), custom_call_target="tpu_custom_call" | custom-call | flops 2147483648 | bytes 8388608 | tf_op jit(solution)/shard_map/down_send/pallas_call | solution.py:254
  304.1 3.7 down_keep.3
  307.8 1.3 copy-done.8
  309.1 1.4 copy-done.10
  310.5 7.4 %all-to-all-done.3 = bf16[16,224,128]{2,1,0:T(8,128)(2,1)} async-done(((bf16[16,224,128]{2,1,0:T(8,128)(2,1)}), bf16[16,224,128]{2,1,0:T(8,128)(2,1)}, u32[]{:S(2)}, u32[]{:S(2)}) %all-to-all-start.3) | async-done | bytes 917536 | tf_op jit(solution)/shard_map/all_to_all | solution.py:359
  317.9 14.9 %collective-permute-done.12.refs_1_ = bf16[1024,512]{1,0:T(8,128)(2,1)S(1)} collective-permute-done((bf16[1024,512]{1,0:T(8,128)(2,1)}, bf16[1024,512]{1,0:T(8,128)(2,1)S(1)}, u32[]{:S(2)}, u32[]{:S(2)}) %collective-permute-start.12) | collective-permute-done | bytes 1048608 | tf_op jit(solution)/shard_map/ppermute | solution.py:310
  333.8 2.0 constant_dynamic-slice_fusion.2
  335.9 7.5 %all-to-all-start.4 = ((bf16[16,112,128]{2,1,0:T(8,128)(2,1)}), bf16[16,112,128]{2,1,0:T(8,128)(2,1)}, u32[]{:S(2)}, u32[]{:S(2)}) async-start(bf16[16,112,128]{2,1,0:T(8,128)(2,1)} %get-tuple-element.122), calls=%async_computation.4 | async-start | bytes 917504 | tf_op jit(solution)/shard_map/all_to_all | solution.py:359
  343.4 1.6 copy-done.9
  345.0 1.6 copy-done.11
  347.8 1.7 sum_stage.7
  350.7 2.4 down_send.4
  353.1 1.5 collective-permute-start.17
  354.6 1.5 collective-permute-start.18
  356.1 1.4 down_keep.4
  359.4 6.2 %collective-permute-done.14.refs_1_ = bf16[512,512]{1,0:T(8,128)(2,1)S(1)} collective-permute-done((bf16[512,512]{1,0:T(8,128)(2,1)S(1)}, bf16[512,512]{1,0:T(8,128)(2,1)S(1)}, u32[]{:S(2)}, u32[]{:S(2)}) %collective-permute-start.14) | collective-permute-done | bytes 524320 | tf_op jit(solution)/shard_map/ppermute | solution.py:310
  366.9 9.6 %collective-permute-done.17.refs_1_ = bf16[1024,256]{1,0:T(8,128)(2,1)} collective-permute-done((bf16[1024,256]{1,0:T(8,128)(2,1)}, bf16[1024,256]{1,0:T(8,128)(2,1)}, u32[]{:S(2)}, u32[]{:S(2)}) %collective-permute-start.17) | collective-permute-done | bytes 524320 | tf_op jit(solution)/shard_map/ppermute | solution.py:310
  376.5 1.2 copy-done.15
  379.0 1.4 sum_stage.8
  380.4 1.4 collective-permute-start.19
  382.8 5.1 %collective-permute-done.19.refs_5_ = bf16[512,256]{1,0:T(8,128)(2,1)S(1)} collective-permute-done((bf16[512,256]{1,0:T(8,128)(2,1)S(1)}, bf16[512,256]{1,0:T(8,128)(2,1)S(1)}, u32[]{:S(2)}, u32[]{:S(2)}) %collective-permute-start.19) | collective-permute-done | bytes 262176 | tf_op jit(solution)/shard_map/ppermute | solution.py:310
  391.9 1.3 constant_dynamic-slice_fusion
  393.2 1.5 collective-permute-done.23.other_ref
  394.7 1.3 down_send.5
  397.9 1.3 down_keep.5
  399.2 5.2 %collective-permute-done.24.refs_1_ = bf16[1024,128]{1,0:T(8,128)(2,1)S(1)} collective-permute-done((bf16[1024,128]{1,0:T(8,128)(2,1)S(1)}, bf16[1024,128]{1,0:T(8,128)(2,1)S(1)}, u32[]{:S(2)}, u32[]{:S(2)}) %collective-permute-start.24) | collective-permute-done | bytes 262176 | tf_op jit(solution)/shard_map/ppermute | solution.py:310
  407.0 3.4 collective-permute-done.26.refs_1_
  411.1 1.7 collective-permute-start.28
  412.9 2.2 collective-permute-start.22
  415.2 2.3 collective-permute-done.28.refs_1_
  417.5 2.7 collective-permute-start.29
  420.2 12.3 %collective-permute-done.29 = bf16[128,256]{1,0:T(8,128)(2,1)S(1)} collective-permute-done((bf16[128,256]{1,0:T(8,128)(2,1)S(1)}, bf16[128,256]{1,0:T(8,128)(2,1)S(1)}, u32[]{:S(2)}, u32[]{:S(2)}) %collective-permute-start.29) | collective-permute-done | bytes 65568 | tf_op jit(solution)/shard_map/ppermute | solution.py:310
  (125 shorter events, 30.1 us)
Async XLA Ops:
  3.8 2.0 copy-start.5
  8.7 7.3 %copy-start.36 = (bf16[128,1792]{1,0:T(8,128)(2,1)S(1)}, bf16[128,1792]{1,0:T(8,128)(2,1)}, u32[]{:S(2)}) copy-start(bf16[128,1792]{1,0:T(8,128)(2,1)} %param.9) | copy-start | bytes 1376260
  8.7 143.9 %all-to-all-start = ((bf16[16,800,128]{2,1,0:T(8,128)(2,1)}), bf16[16,800,128]{2,1,0:T(8,128)(2,1)}, u32[]{:S(2)}, u32[]{:S(2)}) async-start(bf16[16,800,128]{2,1,0:T(8,128)(2,1)} %pack_gate.1), calls=%async_computation | async-start | bytes 6553600 | tf_op jit(solution)/shard_map/all_to_all | solution.py:359
  16.0 91.2 %collective-permute-start = (bf16[128,1792]{1,0:T(8,128)(2,1)S(1)}, bf16[128,1792]{1,0:T(8,128)(2,1)S(1)}, u32[]{:S(2)}, u32[]{:S(2)}) collective-permute-start(bf16[128,1792]{1,0:T(8,128)(2,1)S(1)} %copy-done.36), channel_id=1, source_target_pairs={{0,16},{2,18},{4,20},{6,22},{8,24},{10,26},{12,28},{14,30},{16,0},... | collective-permute-start | bytes 1376264 | tf_op jit(solution)/shard_map/ppermute | solution.py:310
  107.2 21.8 %collective-permute-start.1 = (bf16[256,1792]{1,0:T(8,128)(2,1)S(1)}, bf16[256,1792]{1,0:T(8,128)(2,1)S(1)}, u32[]{:S(2)}, u32[]{:S(2)}) collective-permute-start(bf16[256,1792]{1,0:T(8,128)(2,1)S(1)} %pad_maximum_fusion.2), channel_id=1, source_target_pairs={{0,8},{2,10},{4,12},{6,14},{8,0},{10,2},{12,4},{14,6},{16,24},{18,... | collective-permute-start | bytes 2752520 | tf_op jit(solution)/shard_map/ppermute | solution.py:310
  129.1 2.0 copy-start.6
  129.2 20.7 %collective-permute-start.3 = (bf16[512,896]{1,0:T(8,128)(2,1)S(1)}, bf16[512,896]{1,0:T(8,128)(2,1)S(1)}, u32[]{:S(2)}, u32[]{:S(2)}) collective-permute-start(bf16[512,896]{1,0:T(8,128)(2,1)S(1)} %get-tuple-element.179), channel_id=1, source_target_pairs={{0,2},{2,0},{4,6},{6,4},{8,10},{10,8},{12,14},{14,12},{16,18},{18,... | collective-permute-start | bytes 2752520 | tf_op jit(solution)/shard_map/ppermute | solution.py:310
  130.9 20.4 %collective-permute-start.2 = (bf16[512,896]{1,0:T(8,128)(2,1)S(1)}, bf16[512,896]{1,0:T(8,128)(2,1)S(1)}, u32[]{:S(2)}, u32[]{:S(2)}) collective-permute-start(bf16[512,896]{1,0:T(8,128)(2,1)S(1)} %get-tuple-element.180), channel_id=1, source_target_pairs={{0,4},{2,6},{4,0},{6,2},{8,12},{10,14},{12,8},{14,10},{16,20},{18,... | collective-permute-start | bytes 2752520 | tf_op jit(solution)/shard_map/ppermute | solution.py:310
  152.6 83.2 %all-to-all-start.1 = ((bf16[16,784,128]{2,1,0:T(8,128)(2,1)}), bf16[16,784,128]{2,1,0:T(8,128)(2,1)}, u32[]{:S(2)}, u32[]{:S(2)}) async-start(bf16[16,784,128]{2,1,0:T(8,128)(2,1)} %pack_up.1), calls=%async_computation.1 | async-start | bytes 6422528 | tf_op jit(solution)/shard_map/all_to_all | solution.py:359
  158.6 72.0 %collective-permute-start.4 = (bf16[1024,896]{1,0:T(8,128)(2,1)}, bf16[1024,896]{1,0:T(8,128)(2,1)S(1)}, u32[]{:S(2)}, u32[]{:S(2)}) collective-permute-start(bf16[1024,896]{1,0:T(8,128)(2,1)} %pad_maximum_fusion.refs_0_), channel_id=1, source_target_pairs={{0,2},{2,0},{4,6},{6,4},{8,10},{10,8},{12,14},{14,12},{16,18},{18,... | collective-permute-start | bytes 5505032 | tf_op jit(solution)/shard_map/ppermute | solution.py:310
  159.2 71.5 %collective-permute-start.5 = (bf16[1024,896]{1,0:T(8,128)(2,1)S(1)}, bf16[1024,896]{1,0:T(8,128)(2,1)S(1)}, u32[]{:S(2)}, u32[]{:S(2)}) collective-permute-start(bf16[1024,896]{1,0:T(8,128)(2,1)S(1)} %pad_maximum_fusion.1.refs_2_), channel_id=1, source_target_pairs={{0,4},{2,6},{4,0},{6,2},{8,12},{10,14},{12,8},{14,10},{16,20},{18,... | collective-permute-start | bytes 5505032 | tf_op jit(solution)/shard_map/ppermute | solution.py:310
  159.7 72.2 %collective-permute-start.6 = (bf16[1024,896]{1,0:T(8,128)(2,1)}, bf16[1024,896]{1,0:T(8,128)(2,1)S(1)}, u32[]{:S(2)}, u32[]{:S(2)}) collective-permute-start(bf16[1024,896]{1,0:T(8,128)(2,1)} %pad_maximum_fusion.refs_0_), channel_id=1, source_target_pairs={{0,1},{1,0},{2,3},{3,2},{4,5},{5,4},{6,7},{7,6},{8,9},{9,8},{10,11... | collective-permute-start | bytes 5505032 | tf_op jit(solution)/shard_map/ppermute | solution.py:356
  159.7 74.8 %collective-permute-start.7 = (bf16[1024,896]{1,0:T(8,128)(2,1)S(1)}, bf16[1024,896]{1,0:T(8,128)(2,1)S(1)}, u32[]{:S(2)}, u32[]{:S(2)}) collective-permute-start(bf16[1024,896]{1,0:T(8,128)(2,1)S(1)} %pad_maximum_fusion.1.refs_2_), channel_id=1, source_target_pairs={{0,1},{1,0},{2,3},{3,2},{4,5},{5,4},{6,7},{7,6},{8,9},{9,8},{10,11... | collective-permute-start | bytes 5505032 | tf_op jit(solution)/shard_map/ppermute | solution.py:356
  160.2 2.0 copy-start.7
  164.4 1.3 copy-start.12
  230.7 1.3 copy-start.28
  231.9 1.3 copy-start.30
  233.2 1.3 copy-start.32
  234.5 1.3 copy-start.34
  235.8 7.7 %collective-permute-start.8 = (bf16[1024,896]{1,0:T(8,128)(2,1)}, bf16[1024,896]{1,0:T(8,128)(2,1)}, u32[]{:S(2)}, u32[]{:S(2)}) collective-permute-start(bf16[1024,896]{1,0:T(8,128)(2,1)} %copy-done.28), channel_id=1, source_target_pairs={{0,1},{1,0},{2,3},{3,2},{4,5},{5,4},{6,7},{7,6},{8,9},{9,8},{10,11... | collective-permute-start | bytes 5505032 | tf_op jit(solution)/shard_map/ppermute | solution.py:356
  235.8 7.7 %collective-permute-start.9 = (bf16[1024,896]{1,0:T(8,128)(2,1)}, bf16[1024,896]{1,0:T(8,128)(2,1)}, u32[]{:S(2)}, u32[]{:S(2)}) collective-permute-start(bf16[1024,896]{1,0:T(8,128)(2,1)} %copy-done.30), channel_id=1, source_target_pairs={{0,1},{1,0},{2,3},{3,2},{4,5},{5,4},{6,7},{7,6},{8,9},{9,8},{10,11... | collective-permute-start | bytes 5505032 | tf_op jit(solution)/shard_map/ppermute | solution.py:356
  236.4 49.7 %all-to-all-start.2 = ((bf16[16,448,128]{2,1,0:T(8,128)(2,1)}), bf16[16,448,128]{2,1,0:T(8,128)(2,1)}, u32[]{:S(2)}, u32[]{:S(2)}) async-start(bf16[16,448,128]{2,1,0:T(8,128)(2,1)} %copy-done.12), calls=%async_computation.2 | async-start | bytes 3670016 | tf_op jit(solution)/shard_map/all_to_all | solution.py:359
  243.6 1.5 copy-start.13
  245.1 1.5 copy-start.29
  246.6 1.5 copy-start.31
  248.1 1.5 copy-start.33
  249.6 1.5 copy-start.35
  275.2 10.8 %collective-permute-start.10 = (bf16[2048,512]{1,0:T(8,128)(2,1)}, bf16[2048,512]{1,0:T(8,128)(2,1)S(1)}, u32[]{:S(2)}, u32[]{:S(2)}) collective-permute-start(bf16[2048,512]{1,0:T(8,128)(2,1)} %hidden.1.own_h), channel_id=1, source_target_pairs={{0,1},{1,0},{2,3},{3,2},{4,5},{5,4},{6,7},{7,6},{8,9},{9,8},{10,11... | collective-permute-start | bytes 6291464 | tf_op jit(solution)/shard_map/ppermute | solution.py:356
  286.1 1.3 copy-start.1
  287.4 7.9 %copy-start = (bf16[2048,512]{1,0:T(8,128)(2,1)S(1)}, bf16[2048,512]{1,0:T(8,128)(2,1)}, u32[]{:S(2)}) copy-start(bf16[2048,512]{1,0:T(8,128)(2,1)} %hidden.1.own_h) | copy-start | bytes 6291460
  290.1 11.7 %copy-start.24 = (bf16[8,448,128]{2,1,0:T(8,128)(2,1)}, bf16[8,448,128]{2,1,0:T(8,128)(2,1)S(1)}, u32[]{:S(2)}) copy-start(bf16[8,448,128]{2,1,0:T(8,128)(2,1)S(1)} %get-tuple-element.115.own_ref) | copy-start | bytes 2752516
  290.1 5.3 %collective-permute-start.11 = (bf16[8,448,128]{2,1,0:T(8,128)(2,1)}, bf16[8,448,128]{2,1,0:T(8,128)(2,1)}, u32[]{:S(2)}, u32[]{:S(2)}) collective-permute-start(bf16[8,448,128]{2,1,0:T(8,128)(2,1)} %get-tuple-element.177), channel_id=1, source_target_pairs={{0,1},{1,0},{2,3},{3,2},{4,5},{5,4},{6,7},{7,6},{8,9},{9,8},{10,11... | collective-permute-start | bytes 2752520 | tf_op jit(solution)/shard_map/ppermute | solution.py:356
  290.1 27.9 %all-to-all-start.3 = ((bf16[16,224,128]{2,1,0:T(8,128)(2,1)}), bf16[16,224,128]{2,1,0:T(8,128)(2,1)}, u32[]{:S(2)}, u32[]{:S(2)}) async-start(bf16[16,224,128]{2,1,0:T(8,128)(2,1)} %get-tuple-element.107), calls=%async_computation.3 | async-start | bytes 1835008 | tf_op jit(solution)/shard_map/all_to_all | solution.py:359
  295.3 1.6 copy-start.2
  301.8 31.1 %collective-permute-start.12 = (bf16[1024,512]{1,0:T(8,128)(2,1)}, bf16[1024,512]{1,0:T(8,128)(2,1)S(1)}, u32[]{:S(2)}, u32[]{:S(2)}) collective-permute-start(bf16[1024,512]{1,0:T(8,128)(2,1)} %get-tuple-element.118), channel_id=1, source_target_pairs={{0,2},{2,0},{4,6},{6,4},{8,10},{10,8},{12,14},{14,12},{16,18},{18,... | collective-permute-start | bytes 3145736 | tf_op jit(solution)/shard_map/ppermute | solution.py:310
  302.4 31.5 %collective-permute-start.13 = (bf16[1024,512]{1,0:T(8,128)(2,1)}, bf16[1024,512]{1,0:T(8,128)(2,1)}, u32[]{:S(2)}, u32[]{:S(2)}) collective-permute-start(bf16[1024,512]{1,0:T(8,128)(2,1)} %get-tuple-element.120), channel_id=1, source_target_pairs={{0,4},{2,6},{4,0},{6,2},{8,12},{10,14},{12,8},{14,10},{16,20},{18,... | collective-permute-start | bytes 3145736 | tf_op jit(solution)/shard_map/ppermute | solution.py:310
  307.8 1.3 copy-start.8
  309.1 1.4 copy-start.10
  335.9 14.9 %collective-permute-start.16 = (bf16[8,224,128]{2,1,0:T(8,128)(2,1)}, bf16[8,224,128]{2,1,0:T(8,128)(2,1)S(1)}, u32[]{:S(2)}, u32[]{:S(2)}) collective-permute-start(bf16[8,224,128]{2,1,0:T(8,128)(2,1)} %get-tuple-element.181), channel_id=1, source_target_pairs={{0,1},{1,0},{2,3},{3,2},{4,5},{5,4},{6,7},{7,6},{8,9},{9,8},{10,11... | collective-permute-start | bytes 1376264 | tf_op jit(solution)/shard_map/ppermute | solution.py:356
  335.9 31.0 %all-to-all-start.4 = ((bf16[16,112,128]{2,1,0:T(8,128)(2,1)}), bf16[16,112,128]{2,1,0:T(8,128)(2,1)}, u32[]{:S(2)}, u32[]{:S(2)}) async-start(bf16[16,112,128]{2,1,0:T(8,128)(2,1)} %get-tuple-element.122), calls=%async_computation.4 | async-start | bytes 917504 | tf_op jit(solution)/shard_map/all_to_all | solution.py:359
  343.4 1.6 copy-start.9
  345.0 1.6 copy-start.11
  347.8 2.9 copy-start.3
  349.5 3.6 copy-start.18
  349.5 3.6 copy-start.20
  349.5 16.1 %collective-permute-start.14 = (bf16[512,512]{1,0:T(8,128)(2,1)S(1)}, bf16[512,512]{1,0:T(8,128)(2,1)S(1)}, u32[]{:S(2)}, u32[]{:S(2)}) collective-permute-start(bf16[512,512]{1,0:T(8,128)(2,1)S(1)} %get-tuple-element.128), channel_id=1, source_target_pairs={{0,4},{2,6},{4,0},{6,2},{8,12},{10,14},{12,8},{14,10},{16,20},{18,... | collective-permute-start | bytes 1572872 | tf_op jit(solution)/shard_map/ppermute | solution.py:310
  350.2 15.9 %collective-permute-start.15 = (bf16[512,512]{1,0:T(8,128)(2,1)S(1)}, bf16[512,512]{1,0:T(8,128)(2,1)S(1)}, u32[]{:S(2)}, u32[]{:S(2)}) collective-permute-start(bf16[512,512]{1,0:T(8,128)(2,1)S(1)} %get-tuple-element.130), channel_id=1, source_target_pairs={{0,2},{2,0},{4,6},{6,4},{8,10},{10,8},{12,14},{14,12},{16,18},{18,... | collective-permute-start | bytes 1572872 | tf_op jit(solution)/shard_map/ppermute | solution.py:310
  353.1 23.4 %collective-permute-start.17 = (bf16[1024,256]{1,0:T(8,128)(2,1)}, bf16[1024,256]{1,0:T(8,128)(2,1)}, u32[]{:S(2)}, u32[]{:S(2)}) collective-permute-start(bf16[1024,256]{1,0:T(8,128)(2,1)} %get-tuple-element.139), channel_id=1, source_target_pairs={{0,2},{2,0},{4,6},{6,4},{8,10},{10,8},{12,14},{14,12},{16,18},{18,... | collective-permute-start | bytes 1572872 | tf_op jit(solution)/shard_map/ppermute | solution.py:310
  354.6 22.0 %collective-permute-start.18 = (bf16[1024,256]{1,0:T(8,128)(2,1)}, bf16[1024,256]{1,0:T(8,128)(2,1)}, u32[]{:S(2)}, u32[]{:S(2)}) collective-permute-start(bf16[1024,256]{1,0:T(8,128)(2,1)} %get-tuple-element.141), channel_id=1, source_target_pairs={{0,4},{2,6},{4,0},{6,2},{8,12},{10,14},{12,8},{14,10},{16,20},{18,... | collective-permute-start | bytes 1572872 | tf_op jit(solution)/shard_map/ppermute | solution.py:310
  376.5 1.2 copy-start.15
  379.0 10.1 %copy-start.27 = (bf16[512,512]{1,0:T(8,128)(2,1)S(1)}, bf16[512,512]{1,0:T(8,128)(2,1)}, u32[]{:S(2)}) copy-start(bf16[512,512]{1,0:T(8,128)(2,1)} %copy-done.26) | copy-start | bytes 1572868
  380.4 7.5 %collective-permute-start.19 = (bf16[512,256]{1,0:T(8,128)(2,1)S(1)}, bf16[512,256]{1,0:T(8,128)(2,1)S(1)}, u32[]{:S(2)}, u32[]{:S(2)}) collective-permute-start(bf16[512,256]{1,0:T(8,128)(2,1)S(1)} %get-tuple-element.151), channel_id=1, source_target_pairs={{0,4},{2,6},{4,0},{6,2},{8,12},{10,14},{12,8},{14,10},{16,20},{18,... | collective-permute-start | bytes 786440 | tf_op jit(solution)/shard_map/ppermute | solution.py:310
  381.8 7.3 %collective-permute-start.20 = (bf16[512,256]{1,0:T(8,128)(2,1)S(1)}, bf16[512,256]{1,0:T(8,128)(2,1)S(1)}, u32[]{:S(2)}, u32[]{:S(2)}) collective-permute-start(bf16[512,256]{1,0:T(8,128)(2,1)S(1)} %get-tuple-element.153), channel_id=1, source_target_pairs={{0,2},{2,0},{4,6},{6,4},{8,10},{10,8},{12,14},{14,12},{16,18},{18,... | collective-permute-start | bytes 786440 | tf_op jit(solution)/shard_map/ppermute | solution.py:310
  389.1 1.2 copy-start.19
  391.6 3.1 copy-start.4
  391.8 21.0 %collective-permute-start.21 = (bf16[256,1536]{1,0:T(8,128)(2,1)S(1)}, bf16[256,1536]{1,0:T(8,128)(2,1)S(1)}, u32[]{:S(2)}, u32[]{:S(2)}) collective-permute-start(bf16[256,1536]{1,0:T(8,128)(2,1)S(1)} %get-tuple-element.155), channel_id=1, source_target_pairs={{0,8},{2,10},{4,12},{6,14},{8,0},{10,2},{12,4},{14,6},{16,24},{18,... | collective-permute-start | bytes 2359304 | tf_op jit(solution)/shard_map/ppermute | solution.py:310
  393.2 1.6 collective-permute-start.23
  396.0 8.4 %collective-permute-start.24 = (bf16[1024,128]{1,0:T(8,128)(2,1)S(1)}, bf16[1024,128]{1,0:T(8,128)(2,1)S(1)}, u32[]{:S(2)}, u32[]{:S(2)}) collective-permute-start(bf16[1024,128]{1,0:T(8,128)(2,1)S(1)} %get-tuple-element.166), channel_id=1, source_target_pairs={{0,2},{2,0},{4,6},{6,4},{8,10},{10,8},{12,14},{14,12},{16,18},{18,... | collective-permute-start | bytes 786440 | tf_op jit(solution)/shard_map/ppermute | solution.py:310
  397.2 8.1 %collective-permute-start.25 = (bf16[1024,128]{1,0:T(8,128)(2,1)S(1)}, bf16[1024,128]{1,0:T(8,128)(2,1)S(1)}, u32[]{:S(2)}, u32[]{:S(2)}) collective-permute-start(bf16[1024,128]{1,0:T(8,128)(2,1)S(1)} %get-tuple-element.168), channel_id=1, source_target_pairs={{0,4},{2,6},{4,0},{6,2},{8,12},{10,14},{12,8},{14,10},{16,20},{18,... | collective-permute-start | bytes 786440 | tf_op jit(solution)/shard_map/ppermute | solution.py:310
  405.4 5.0 %collective-permute-start.26 = (bf16[512,128]{1,0:T(8,128)(2,1)S(1)}, bf16[512,128]{1,0:T(8,128)(2,1)S(1)}, u32[]{:S(2)}, u32[]{:S(2)}) collective-permute-start(bf16[512,128]{1,0:T(8,128)(2,1)S(1)} %get-tuple-element.170), channel_id=1, source_target_pairs={{0,4},{2,6},{4,0},{6,2},{8,12},{10,14},{12,8},{14,10},{16,20},{18,... | collective-permute-start | bytes 393224 | tf_op jit(solution)/shard_map/ppermute | solution.py:310
  406.1 5.0 %collective-permute-start.27 = (bf16[512,128]{1,0:T(8,128)(2,1)S(1)}, bf16[512,128]{1,0:T(8,128)(2,1)S(1)}, u32[]{:S(2)}, u32[]{:S(2)}) collective-permute-start(bf16[512,128]{1,0:T(8,128)(2,1)S(1)} %get-tuple-element.172), channel_id=1, source_target_pairs={{0,2},{2,0},{4,6},{6,4},{8,10},{10,8},{12,14},{14,12},{16,18},{18,... | collective-permute-start | bytes 393224 | tf_op jit(solution)/shard_map/ppermute | solution.py:310
  411.1 6.3 %collective-permute-start.28 = (bf16[256,256]{1,0:T(8,128)(2,1)S(1)}, bf16[256,256]{1,0:T(8,128)(2,1)S(1)}, u32[]{:S(2)}, u32[]{:S(2)}) collective-permute-start(bf16[256,256]{1,0:T(8,128)(2,1)S(1)} %get-tuple-element.174), channel_id=1, source_target_pairs={{0,8},{2,10},{4,12},{6,14},{8,0},{10,2},{12,4},{14,6},{16,24},{18,... | collective-permute-start | bytes 393224 | tf_op jit(solution)/shard_map/ppermute | solution.py:310
  412.9 19.7 %collective-permute-start.22 = (bf16[128,1536]{1,0:T(8,128)(2,1)S(1)}, bf16[128,1536]{1,0:T(8,128)(2,1)S(1)}, u32[]{:S(2)}, u32[]{:S(2)}) collective-permute-start(bf16[128,1536]{1,0:T(8,128)(2,1)S(1)} %get-tuple-element.157), channel_id=1, source_target_pairs={{0,16},{2,18},{4,20},{6,22},{8,24},{10,26},{12,28},{14,30},{16,0},... | collective-permute-start | bytes 1179656 | tf_op jit(solution)/shard_map/ppermute | solution.py:310
  417.5 15.0 %collective-permute-start.29 = (bf16[128,256]{1,0:T(8,128)(2,1)S(1)}, bf16[128,256]{1,0:T(8,128)(2,1)S(1)}, u32[]{:S(2)}, u32[]{:S(2)}) collective-permute-start(bf16[128,256]{1,0:T(8,128)(2,1)S(1)} %get-tuple-element.176), channel_id=1, source_target_pairs={{0,16},{2,18},{4,20},{6,22},{8,24},{10,26},{12,28},{14,30},{16,0},... | collective-permute-start | bytes 196616 | tf_op jit(solution)/shard_map/ppermute | solution.py:310
  (8 other events, 8.6 us)

commit v3 on v2

--- a/solution.py
+++ b/solution.py
@@ -215,7 +215,7 @@
         out_specs=pl.BlockSpec((tile, wide), lambda i: (i, 0)),
         scratch_shapes=[pltpu.VMEM((model, wide), up.dtype)] * 2
         + [pltpu.VMEM((tile, model), up.dtype)],
-        compiler_params=pltpu.CompilerParams(vmem_limit_bytes=40 * MIB),
+        compiler_params=pltpu.CompilerParams(vmem_limit_bytes=56 * MIB),
         cost_estimate=pl.CostEstimate(
             flops=4 * total * model * wide, bytes_accessed=24 * MIB, transcendentals=total * wide
         ),
@@ -223,76 +223,99 @@
     )(at, *pieces, gate, up)
 
 
-def down_kernel(rows, side, own_h, other_h, own_ref, other_ref, out_a, out_b, own_w, other_w):
+ORDERS = ((0, 1, 2), (1, 2, 0), (2, 0, 1))
+
+
+def group_spans(features):
+    tiles = features // LANES
+    cuts = [0, -(-tiles // 3), -(-tiles // 3) + -(-(tiles - -(-tiles // 3)) // 2), tiles]
+    return [slice(lo * LANES, hi * LANES) for lo, hi in zip(cuts, cuts[1:])]
+
+
+def stage_axis(number, stage):
+    order = ORDERS[number]
+    return sum(1 for bit in order[stage:] if bit < order[stage])
+
+
+def half_spans(rows, axis, side):
+    size = rows >> (axis + 1)
+    return [slice((2 * at + side) * size, (2 * at + side + 1) * size) for at in range(1 << axis)]
+
+
+def down_kernel(rows, side, own_h, other_h, own_ref, other_ref, *refs):
+    out_refs, (own_w, other_w) = refs[:-2], refs[-2:]
     for in_ref, w_ref in ((own_ref, own_w), (other_ref, other_w)):
         for at in range(in_ref.shape[0]):
             unpack_rows(in_ref, at, 0, rows, w_ref, at * rows, 0)
-    half = own_w.shape[0] // 2
-    quarter = own_h.shape[0] // 4
-
-    def product(at, size, span):
-        tokens = slice(at * quarter, (at + size) * quarter)
-        dims = (((1,), (1,)), ((), ()))
-        return lax.dot_general(
-            own_h[tokens, :], own_w[span, :], dims, preferred_element_type=jnp.float32
-        ) + lax.dot_general(
-            other_h[tokens, :], other_w[span, :], dims, preferred_element_type=jnp.float32
-        )
-
-    out_a[...] = product(2 * side, 2, slice(0, half)).astype(out_a.dtype)
-    for first in range(2):
-        out_b[first * quarter : (first + 1) * quarter, :] = product(
-            2 * first + side, 1, slice(half, 2 * half)
-        ).astype(out_b.dtype)
+    dims = (((1,), (1,)), ((), ()))
+    for number, span in enumerate(group_spans(own_w.shape[0])):
+        done = 0
+        for tokens in half_spans(own_h.shape[0], stage_axis(number, 0), side):
+            value = lax.dot_general(
+                own_h[tokens, :], own_w[span, :], dims, preferred_element_type=jnp.float32
+            ) + lax.dot_general(
+                other_h[tokens, :], other_w[span, :], dims, preferred_element_type=jnp.float32
+            )
+            size = tokens.stop - tokens.start
+            out_refs[number][done : done + size, :] = value.astype(out_refs[number].dtype)
+            done += size
 
 
 def down_product(own_h, other_h, own, other, rows, side, dtype, name):
     sources = own.shape[0]
     total, wide = own_h.shape
     tokens = total // 2
-    features = sources * rows // 2
+    features = sources * rows
+    shapes = [
+        jax.ShapeDtypeStruct((tokens, span.stop - span.start), dtype)
+        for span in group_spans(features)
+    ]
     return pl.pallas_call(
         functools.partial(down_kernel, rows, side),
-        out_shape=[jax.ShapeDtypeStruct((tokens, features), dtype)] * 2,
+        out_shape=shapes,
         in_specs=[vmem()] * 4,
-        out_specs=[vmem()] * 2,
-        scratch_shapes=[pltpu.VMEM((sources * rows, wide), own.dtype)] * 2,
+        out_specs=[vmem()] * len(shapes),
+        scratch_shapes=[pltpu.VMEM((features, wide), own.dtype)] * 2,
         compiler_params=pltpu.CompilerParams(vmem_limit_bytes=40 * MIB),
         cost_estimate=pl.CostEstimate(
-            flops=8 * tokens * wide * features, bytes_accessed=8 * MIB, transcendentals=0
+            flops=4 * tokens * wide * features, bytes_accessed=8 * MIB, transcendentals=0
         ),
         name=name,
     )(own_h, other_h, own, other)
 
 
-def halve_kernel(joined, *refs):
-    count = (len(refs) - 2 * (1 if joined else 0)) // 2 if joined else len(refs) // 4
+def halve_kernel(axes, *refs):
+    count = len(refs) // 4 if axes else 3
     out_refs = refs[2 * count :]
     lane = 0
     for number in range(count):
         keep_ref, come_ref = refs[2 * number : 2 * number + 2]
-        half = keep_ref.shape[0] // 2
-        total = keep_ref[...] + come_ref[...].astype(jnp.float32)
-        if joined:
+        if axes:
+            send_ref, left_ref = out_refs[2 * number : 2 * number + 2]
+            lanes = slice(0, keep_ref.shape[1])
+        else:
             send_ref, left_ref = out_refs
             lanes = slice(lane, lane + keep_ref.shape[1])
-            lane += keep_ref.shape[1]
-        else:
-            send_ref, left_ref = out_refs[2 * number : 2 * number + 2]
-            lanes = slice(0, keep_ref.shape[1])
-        send_ref[:, lanes] = total[half:, :].astype(send_ref.dtype)
-        left_ref[:, lanes] = total[:half, :]
-
-
-def halve(pairs, joined):
+            lane = lanes.stop
+        axis = axes[number] if axes else 0
+        for side, out_ref in enumerate((left_ref, send_ref)):
+            done = 0
+            for rows in half_spans(keep_ref.shape[0], axis, side):
+                size = rows.stop - rows.start
+                total = keep_ref[rows, :] + come_ref[rows, :].astype(jnp.float32)
+                out_ref[done : done + size, lanes] = total.astype(out_ref.dtype)
+                done += size
+
+
+def halve(pairs, axes):
     sizes = [(keep.shape[0] // 2, keep.shape[1]) for keep, _ in pairs]
-    if joined:
+    if not axes:
         sizes = [(sizes[0][0], sum(width for _, width in sizes))]
     shapes = []
     for size in sizes:
         shapes += [jax.ShapeDtypeStruct(size, jnp.bfloat16), jax.ShapeDtypeStruct(size, jnp.float32)]
     out = pl.pallas_call(
-        functools.partial(halve_kernel, joined),
+        functools.partial(halve_kernel, axes),
         out_shape=shapes,
         in_specs=[vmem()] * (2 * len(pairs)),
         out_specs=[vmem()] * len(shapes),
@@ -367,20 +390,23 @@
     belongs = slot_place[None, None, :, None] == places[:, :, None, None]
     share = jnp.sum(jnp.where(belongs, share[None, None], 0.0), axis=2)
 
-    gate = move(pack_gate(listing, gate_proj, share, devices))
+    far = swap(tokens, 3)
+    gate_packed, far = tie((pack_gate(listing, gate_proj, share, devices), far))
+    (up_packed,) = pack(listing, up_proj, devices, (depth,), "pack_up")
+
+    gate = move(gate_packed)
     mid = tokens.shape[1] // 2
-    rows = jnp.concatenate([tokens, swap(tokens, 3)], axis=0)
+    rows = jnp.concatenate([tokens, far], axis=0)
     rows = jnp.concatenate([rows, swap(rows, 2)], axis=0)
     first, second = rows[:, :mid], rows[:, mid:]
     first = jnp.concatenate([first, swap(first, 1)], axis=0)
     second = jnp.concatenate([second, swap(second, 0)], axis=0)
-    (up_packed,) = pack(listing, up_proj, devices, (depth,), "pack_up")
     gate, first, second, up_packed = tie((gate, first, second, up_packed))
 
     up = move(up_packed)
     pieces = [first, swap(first, 0), second, swap(second, 1)]
     others = [exchange(first), None, exchange(second), None]
-    parts = (128, 64, 32)
+    parts = (128, 96)
     down_packed = pack(listing, down_proj, devices, parts, "pack_down")
     up, pieces, others[0], others[2], down_packed = tie(
         (up, pieces, others[0], others[2], down_packed)
@@ -399,43 +425,31 @@
         args = (hidden, hidden_other, own, other)
         sent = down_product(*args, rows_in, 1, jnp.bfloat16, "down_send")
         sent, args = tie((sent, args))
-        come = [swap(value, bit) for bit, value in enumerate(sent)]
-        return list(zip(down_product(*args, rows_in, 0, jnp.float32, "down_keep"), come))
-
-    def cross(pairs):
-        (send_a, keep_a), (send_b, keep_b) = halve(pairs, False)
-        return [(keep_a, swap(send_a, 1)), (keep_b, swap(send_b, 0))]
-
-    def along(pairs, bit):
-        ((send, keep),) = halve(pairs, True)
-        return [(keep, swap(send, bit))]
-
-    def finish(pairs):
-        ((keep, come),) = pairs
+        come = [swap(value, order[0]) for value, order in zip(sent, ORDERS)]
+        return down_product(*args, rows_in, 0, jnp.float32, "down_keep"), come
+
+    def stage(kept, come, number):
+        axes = tuple(stage_axis(at, number) for at in range(3))
+        out = halve(list(zip(kept, come)), axes)
+        come = [swap(send, order[number]) for (send, _), order in zip(out, ORDERS)]
+        return [keep for _, keep in out], come
+
+    def last_stage(kept, come):
+        ((send, keep),) = halve(list(zip(kept, come)), None)
+        come = swap(send, 3)
         return (keep + come.astype(jnp.float32)).astype(jnp.bfloat16)
 
     down1 = move(packed)
-    sums0 = products(down0, parts[0])
-    down1, sums0, packed = tie((down1, sums0, down_packed[2]))
-    down2 = move(packed)
-    sums0 = cross(sums0)
-    sums1 = products(down1, parts[1])
-    down2, sums0, sums1 = tie((down2, sums0, sums1))
-    sums2 = products(down2, parts[2])
-    sums1 = cross(sums1)
-    sums01 = along(sums0 + sums1, 2)
-    sums2 = cross(sums2)
-    sums01 = along(sums01, 3)
-    sums2 = along(along(sums2, 2), 3)
-
-    out01, out2 = finish(sums01), finish(sums2)
+    kept0, come0 = products(down0, parts[0])
+    down1, kept0 = tie((down1, kept0))
+    kept1, come1 = products(down1, parts[1])
+    kept0, come0 = stage(kept0, come0, 1)
+    kept1, come1 = stage(kept1, come1, 1)
+    kept0, come0 = stage(kept0, come0, 2)
+    kept1, come1 = stage(kept1, come1, 2)
     out = []
-    lane = 0
-    for rows_in in parts[:2]:
-        wide = group * rows_in
-        out.append(out01[:, lane : lane + wide].reshape(block, group, rows_in))
-        lane += wide
-    out.append(out2.reshape(block, group, parts[2]))
+    for rows_in, total in zip(parts, (last_stage(kept0, come0), last_stage(kept1, come1))):
+        out.append(total.reshape(block, group, rows_in))
     return jnp.concatenate(out, axis=2).reshape(tokens.shape)
 
 

time: 439 us -> 376 us (0.86)
  local copies, waits for them, and re-layouts: 45.8 us -> 16.8 us
  waiting for transfers between devices: 272 us -> 247 us
  starting transfers between devices: 59.5 us -> 51 us
    ppermute x22 -> x26, waiting for transfers between devices: 253 us -> 212 us  [swap(): return lax.ppermute(value, 'ep', [(i, i ^ 1 << bit) for i in range(size)])]
    unnamed x76 -> x32, local copies, waits for them, and re-layouts: 38.2 us -> 12 us
    all_to_all x5 -> x4, waiting for transfers between devices: 18.3 us -> 33.2 us  [move(): return lax.all_to_all(packed, 'ep', 0, 0, tiled=True)]
    all_to_all x5 -> x4, starting transfers between devices: 33.2 us -> 26.5 us  [move(): return lax.all_to_all(packed, 'ep', 0, 0, tiled=True)]
    pallas_call x13 -> x10, Pallas kernels: 18.5 us -> 12.9 us  [the longest x4 10.5 us: down_product(): pl.pallas_call(functools.partial(down_kernel, rows, side), out_shape=shap...]
    ppermute x22 -> x26, starting transfers between devices: 25.2 us -> 23.4 us  [swap(): return lax.ppermute(value, 'ep', [(i, i ^ 1 << bit) for i in range(size)])]
  transfers between devices with their start and end apart: 35 -> 37, of which waited for: 20 -> 20; matrix products, arithmetic and copies ran while one was open for 1% -> 4% of each run, Pallas kernels for 11% -> 13%
where the time goes in v3:
time: 376 us; the launch traced here: 371 us
  waiting for transfers between devices  247 us (66%)
  starting transfers between devices  51 us (14%)
  Pallas kernels  46.5 us (12%)
  local copies, waits for them, and re-layouts  16.8 us (4%)
  other arithmetic  8.64 us (2%)
    ppermute x26, waiting for transfers between devices, swap(): return lax.ppermute(value, 'ep', [(i, i ^ 1 << bit) for i in range(size)])  212 us
    all_to_all x4, waiting for transfers between devices, move(): return lax.all_to_all(packed, 'ep', 0, 0, tiled=True)  33.2 us
    all_to_all x4, starting transfers between devices, move(): return lax.all_to_all(packed, 'ep', 0, 0, tiled=True)  26.5 us
    pallas_call x1, Pallas kernels, hidden_units(): pl.pallas_call(hidden_kernel, grid=(8,), out_shape=jax.ShapeDtypeStruct((...  25.2 us
    ppermute x26, starting transfers between devices, swap(): return lax.ppermute(value, 'ep', [(i, i ^ 1 << bit) for i in range(size)])  23.4 us
    unnamed x32, local copies, waits for them, and re-layouts  12 us
    pallas_call x4, Pallas kernels, down_product(): pl.pallas_call(functools.partial(down_kernel, rows, side), out_shape=shap...  10.5 us
  transfers between devices with their start and end apart: 37, of which 20 were waited for; matrix products, arithmetic and copies ran while one was open for 4% of the time, Pallas kernels for 13%

profile of v3, /device:TPU:14, one launch (start us, length us, event | category | flops | bytes accessed | tf_op | source)
XLA Modules:
  0.0 370.5 jit_solution(11081740069486030759)
XLA Ops:
  0.0 2.6 collective-permute-start
  2.6 0.9 select_reduce_fusion.4
  3.8 0.7 select_reduce_fusion.1
  4.7 0.8 broadcast_compare_fusion
  5.5 0.9 select_reduce_fusion.share_ref
  6.4 2.0 copy-done
  8.5 2.8 pack_gate.1
  11.3 11.1 %collective-permute-done = bf16[128,1792]{1,0:T(8,128)(2,1)} collective-permute-done((bf16[128,1792]{1,0:T(8,128)(2,1)}, bf16[128,1792]{1,0:T(8,128)(2,1)}, u32[]{:S(2)}, u32[]{:S(2)}) %collective-permute-start) | collective-permute-done | bytes 458784 | tf_op jit(solution)/shard_map/ppermute | solution.py:333
  22.4 7.9 %all-to-all-start = ((bf16[16,800,128]{2,1,0:T(8,128)(2,1)}), bf16[16,800,128]{2,1,0:T(8,128)(2,1)S(1)}, u32[]{:S(2)}, u32[]{:S(2)}) async-start(bf16[16,800,128]{2,1,0:T(8,128)(2,1)} %pack_gate.1), calls=%async_computation | async-start | bytes 6553600 | tf_op jit(solution)/shard_map/all_to_all | solution.py:382
  30.3 1.3 pad_maximum_fusion.2
  31.6 0.6 collective-permute-start.1
  32.3 1.1 constant_dynamic-update-slice_fusion.1
  33.3 73.0 %collective-permute-done.1 = bf16[256,1792]{1,0:T(8,128)(2,1)S(1)} collective-permute-done((bf16[256,1792]{1,0:T(8,128)(2,1)S(1)}, bf16[256,1792]{1,0:T(8,128)(2,1)S(1)}, u32[]{:S(2)}, u32[]{:S(2)}) %collective-permute-start.1) | collective-permute-done | bytes 917536 | tf_op jit(solution)/shard_map/ppermute | solution.py:333
  106.8 1.7 copy-done.1
  108.5 2.9 pack_up.1
  111.4 16.4 %collective-permute-done.3 = bf16[512,896]{1,0:T(8,128)(2,1)S(1)} collective-permute-done((bf16[512,896]{1,0:T(8,128)(2,1)S(1)}, bf16[512,896]{1,0:T(8,128)(2,1)S(1)}, u32[]{:S(2)}, u32[]{:S(2)}) %collective-permute-start.3) | collective-permute-done | bytes 917536 | tf_op jit(solution)/shard_map/ppermute | solution.py:333
  127.8 1.5 pad_maximum_fusion.1.refs_2_
  129.3 1.4 pad_maximum_fusion.refs_0_
  130.6 1.7 copy-done.12
  132.3 6.2 %all-to-all-start.1 = ((bf16[16,784,128]{2,1,0:T(8,128)(2,1)}), bf16[16,784,128]{2,1,0:T(8,128)(2,1)}, u32[]{:S(2)}, u32[]{:S(2)}) async-start(bf16[16,784,128]{2,1,0:T(8,128)(2,1)} %pack_up.1), calls=%async_computation.1 | async-start | bytes 6422528 | tf_op jit(solution)/shard_map/all_to_all | solution.py:382
  140.2 2.0 copy-done.2
  142.2 2.6 pack_down.1
  144.8 66.6 %collective-permute-done.4.refs_1_ = bf16[1024,896]{1,0:T(8,128)(2,1)S(1)} collective-permute-done((bf16[1024,896]{1,0:T(8,128)(2,1)}, bf16[1024,896]{1,0:T(8,128)(2,1)S(1)}, u32[]{:S(2)}, u32[]{:S(2)}) %collective-permute-start.4) | collective-permute-done | bytes 1835040 | tf_op jit(solution)/shard_map/ppermute | solution.py:333
  212.7 7.1 %all-to-all-start.2 = ((bf16[16,448,128]{2,1,0:T(8,128)(2,1)}), bf16[16,448,128]{2,1,0:T(8,128)(2,1)}, u32[]{:S(2)}, u32[]{:S(2)}) async-start(bf16[16,448,128]{2,1,0:T(8,128)(2,1)} %get-tuple-element.91), calls=%async_computation.2 | async-start | bytes 3670016 | tf_op jit(solution)/shard_map/all_to_all | solution.py:382
  219.8 25.2 %hidden.1.own_h = bf16[2048,512]{1,0:T(8,128)(2,1)} custom-call(s32[2]{0:T(128)} %pad_add_fusion.at_ref, bf16[1024,896]{1,0:T(8,128)(2,1)} %pad_maximum_fusion.refs_0_, bf16[1024,896]{1,0:T(8,128)(2,1)} %copy-done.14, bf16[1024,896]{1,0:T(8,128)(2,1)} %pad_maximum_fusion.1.refs_2_, bf16[1024,896]{1,0:T(8,128)(2,1)} %collective-permute-done.5.refs_3_, ...), custom_call_target="tpu_custom_call" | custom-call | flops 15032385536 | bytes 25165824 | tf_op jit(solution)/shard_map/hidden/pallas_call | solution.py:208
  245.1 17.3 %all-to-all-done.2 = bf16[16,448,128]{2,1,0:T(8,128)(2,1)} async-done(((bf16[16,448,128]{2,1,0:T(8,128)(2,1)}), bf16[16,448,128]{2,1,0:T(8,128)(2,1)}, u32[]{:S(2)}, u32[]{:S(2)}) %all-to-all-start.2) | async-done | bytes 1835040 | tf_op jit(solution)/shard_map/all_to_all | solution.py:382
  262.3 5.2 %all-to-all-start.3 = ((bf16[16,336,128]{2,1,0:T(8,128)(2,1)}), bf16[16,336,128]{2,1,0:T(8,128)(2,1)}, u32[]{:S(2)}, u32[]{:S(2)}) async-start(bf16[16,336,128]{2,1,0:T(8,128)(2,1)} %get-tuple-element.101), calls=%async_computation.3 | async-start | bytes 2752512 | tf_op jit(solution)/shard_map/all_to_all | solution.py:382
  267.6 1.7 constant_dynamic-slice_fusion.2
  269.4 2.5 collective-permute-done.11.other_ref
  271.9 3.7 down_send.2
  275.6 0.8 copy-done.10
  277.5 1.6 copy-done.8
  279.1 3.0 down_keep.2
  282.1 1.0 copy-done.3
  283.1 16.0 %all-to-all-done.3 = bf16[16,336,128]{2,1,0:T(8,128)(2,1)} async-done(((bf16[16,336,128]{2,1,0:T(8,128)(2,1)}), bf16[16,336,128]{2,1,0:T(8,128)(2,1)}, u32[]{:S(2)}, u32[]{:S(2)}) %all-to-all-start.3) | async-done | bytes 1376288 | tf_op jit(solution)/shard_map/all_to_all | solution.py:382
  299.1 1.5 constant_dynamic-slice_fusion
  300.8 14.3 %collective-permute-done.14.refs_5_ = bf16[1024,256]{1,0:T(8,128)(2,1)S(1)} collective-permute-done((bf16[1024,256]{1,0:T(8,128)(2,1)S(1)}, bf16[1024,256]{1,0:T(8,128)(2,1)S(1)}, u32[]{:S(2)}, u32[]{:S(2)}) %collective-permute-start.14) | collective-permute-done | bytes 524320 | tf_op jit(solution)/shard_map/ppermute | solution.py:333
  315.0 1.7 sum_stage.6
  316.7 1.5 collective-permute-start.17
  318.3 1.9 down_send.3
  320.2 0.7 collective-permute-start.23
  320.8 0.7 collective-permute-start.15
  321.7 1.4 collective-permute-start.24
  323.1 2.9 collective-permute-done.17.refs_5_
  326.3 6.6 %collective-permute-done.15.refs_1_ = bf16[512,384]{1,0:T(8,128)(2,1)S(1)} collective-permute-done((bf16[512,384]{1,0:T(8,128)(2,1)S(1)}, bf16[512,384]{1,0:T(8,128)(2,1)S(1)}, u32[]{:S(2)}, u32[]{:S(2)}) %collective-permute-start.15) | collective-permute-done | bytes 393248 | tf_op jit(solution)/shard_map/ppermute | solution.py:333
  332.9 0.7 collective-permute-done.16.refs_3_
  334.0 1.4 collective-permute-start.19
  335.5 1.8 collective-permute-done.23.refs_1_
  337.3 0.6 collective-permute-start.20
  337.9 1.9 down_keep.3
  339.8 4.0 %collective-permute-done.24.refs_3_ = bf16[1024,256]{1,0:T(8,128)(2,1)S(1)} collective-permute-done((bf16[1024,256]{1,0:T(8,128)(2,1)S(1)}, bf16[1024,256]{1,0:T(8,128)(2,1)S(1)}, u32[]{:S(2)}, u32[]{:S(2)}) %collective-permute-start.24) | collective-permute-done | bytes 524320 | tf_op jit(solution)/shard_map/ppermute | solution.py:333
  343.8 1.0 collective-permute-done.25.refs_5_
  345.0 1.4 collective-permute-start.26
  346.7 1.4 collective-permute-start.28
  348.2 0.8 collective-permute-done.18.refs_1_
  349.1 3.3 collective-permute-start.21
  352.4 3.1 collective-permute-done.27.refs_3_
  355.8 1.7 collective-permute-start.30
  357.5 1.4 collective-permute-start.31
  358.9 1.9 collective-permute-done.29.refs_1_
  360.8 1.7 collective-permute-done.31.refs_5_
  362.6 0.8 collective-permute-start.32
  363.6 5.7 %collective-permute-done.32 = bf16[128,768]{1,0:T(8,128)(2,1)S(1)} collective-permute-done((bf16[128,768]{1,0:T(8,128)(2,1)S(1)}, bf16[128,768]{1,0:T(8,128)(2,1)S(1)}, u32[]{:S(2)}, u32[]{:S(2)}) %collective-permute-start.32) | collective-permute-done | bytes 196640 | tf_op jit(solution)/shard_map/ppermute | solution.py:333
  369.5 1.0 copy.15
  (78 shorter events, 7.6 us)
Async XLA Ops:
  0.0 22.4 %collective-permute-start = (bf16[128,1792]{1,0:T(8,128)(2,1)}, bf16[128,1792]{1,0:T(8,128)(2,1)}, u32[]{:S(2)}, u32[]{:S(2)}) collective-permute-start(bf16[128,1792]{1,0:T(8,128)(2,1)} %param.9), channel_id=1, source_target_pairs={{0,16},{2,18},{4,20},{6,22},{8,24},{10,26},{12,28},{14,30},{16,0},... | collective-permute-start | bytes 1376264 | tf_op jit(solution)/shard_map/ppermute | solution.py:333
  6.4 2.0 copy-start
  22.4 108.2 %all-to-all-start = ((bf16[16,800,128]{2,1,0:T(8,128)(2,1)}), bf16[16,800,128]{2,1,0:T(8,128)(2,1)S(1)}, u32[]{:S(2)}, u32[]{:S(2)}) async-start(bf16[16,800,128]{2,1,0:T(8,128)(2,1)} %pack_gate.1), calls=%async_computation | async-start | bytes 6553600 | tf_op jit(solution)/shard_map/all_to_all | solution.py:382
  30.3 1.9 copy-start.13
  31.6 74.8 %collective-permute-start.1 = (bf16[256,1792]{1,0:T(8,128)(2,1)S(1)}, bf16[256,1792]{1,0:T(8,128)(2,1)S(1)}, u32[]{:S(2)}, u32[]{:S(2)}) collective-permute-start(bf16[256,1792]{1,0:T(8,128)(2,1)S(1)} %pad_maximum_fusion.2), channel_id=1, source_target_pairs={{0,8},{2,10},{4,12},{6,14},{8,0},{10,2},{12,4},{14,6},{16,24},{18,... | collective-permute-start | bytes 2752520 | tf_op jit(solution)/shard_map/ppermute | solution.py:333
  106.4 2.0 copy-start.1
  106.6 21.2 %collective-permute-start.3 = (bf16[512,896]{1,0:T(8,128)(2,1)S(1)}, bf16[512,896]{1,0:T(8,128)(2,1)S(1)}, u32[]{:S(2)}, u32[]{:S(2)}) collective-permute-start(bf16[512,896]{1,0:T(8,128)(2,1)S(1)} %get-tuple-element.165), channel_id=1, source_target_pairs={{0,2},{2,0},{4,6},{6,4},{8,10},{10,8},{12,14},{14,12},{16,18},{18,... | collective-permute-start | bytes 2752520 | tf_op jit(solution)/shard_map/ppermute | solution.py:333
  106.7 22.6 %collective-permute-start.2 = (bf16[512,896]{1,0:T(8,128)(2,1)S(1)}, bf16[512,896]{1,0:T(8,128)(2,1)S(1)}, u32[]{:S(2)}, u32[]{:S(2)}) collective-permute-start(bf16[512,896]{1,0:T(8,128)(2,1)S(1)} %get-tuple-element.166), channel_id=1, source_target_pairs={{0,4},{2,6},{4,0},{6,2},{8,12},{10,14},{12,8},{14,10},{16,20},{18,... | collective-permute-start | bytes 2752520 | tf_op jit(solution)/shard_map/ppermute | solution.py:333
  130.6 1.7 copy-start.12
  132.3 79.2 %all-to-all-start.1 = ((bf16[16,784,128]{2,1,0:T(8,128)(2,1)}), bf16[16,784,128]{2,1,0:T(8,128)(2,1)}, u32[]{:S(2)}, u32[]{:S(2)}) async-start(bf16[16,784,128]{2,1,0:T(8,128)(2,1)} %pack_up.1), calls=%async_computation.1 | async-start | bytes 6422528 | tf_op jit(solution)/shard_map/all_to_all | solution.py:382
  138.5 72.9 %collective-permute-start.4 = (bf16[1024,896]{1,0:T(8,128)(2,1)}, bf16[1024,896]{1,0:T(8,128)(2,1)S(1)}, u32[]{:S(2)}, u32[]{:S(2)}) collective-permute-start(bf16[1024,896]{1,0:T(8,128)(2,1)} %pad_maximum_fusion.refs_0_), channel_id=1, source_target_pairs={{0,2},{2,0},{4,6},{6,4},{8,10},{10,8},{12,14},{14,12},{16,18},{18,... | collective-permute-start | bytes 5505032 | tf_op jit(solution)/shard_map/ppermute | solution.py:333
  139.1 72.4 %collective-permute-start.5 = (bf16[1024,896]{1,0:T(8,128)(2,1)}, bf16[1024,896]{1,0:T(8,128)(2,1)}, u32[]{:S(2)}, u32[]{:S(2)}) collective-permute-start(bf16[1024,896]{1,0:T(8,128)(2,1)} %pad_maximum_fusion.1.refs_2_), channel_id=1, source_target_pairs={{0,4},{2,6},{4,0},{6,2},{8,12},{10,14},{12,8},{14,10},{16,20},{18,... | collective-permute-start | bytes 5505032 | tf_op jit(solution)/shard_map/ppermute | solution.py:333
  139.7 71.8 %collective-permute-start.6 = (bf16[1024,896]{1,0:T(8,128)(2,1)}, bf16[1024,896]{1,0:T(8,128)(2,1)}, u32[]{:S(2)}, u32[]{:S(2)}) collective-permute-start(bf16[1024,896]{1,0:T(8,128)(2,1)} %pad_maximum_fusion.refs_0_), channel_id=1, source_target_pairs={{0,1},{1,0},{2,3},{3,2},{4,5},{5,4},{6,7},{7,6},{8,9},{9,8},{10,11... | collective-permute-start | bytes 5505032 | tf_op jit(solution)/shard_map/ppermute | solution.py:379
  139.7 71.8 %collective-permute-start.7 = (bf16[1024,896]{1,0:T(8,128)(2,1)}, bf16[1024,896]{1,0:T(8,128)(2,1)}, u32[]{:S(2)}, u32[]{:S(2)}) collective-permute-start(bf16[1024,896]{1,0:T(8,128)(2,1)} %pad_maximum_fusion.1.refs_2_), channel_id=1, source_target_pairs={{0,1},{1,0},{2,3},{3,2},{4,5},{5,4},{6,7},{7,6},{8,9},{9,8},{10,11... | collective-permute-start | bytes 5505032 | tf_op jit(solution)/shard_map/ppermute | solution.py:379
  140.2 2.0 copy-start.2
  211.4 1.3 copy-start.14
  211.5 8.3 %collective-permute-start.8 = (bf16[1024,896]{1,0:T(8,128)(2,1)S(1)}, bf16[1024,896]{1,0:T(8,128)(2,1)}, u32[]{:S(2)}, u32[]{:S(2)}) collective-permute-start(bf16[1024,896]{1,0:T(8,128)(2,1)S(1)} %collective-permute-done.4.refs_1_), channel_id=1, source_target_pairs={{0,1},{1,0},{2,3},{3,2},{4,5},{5,4},{6,7},{7,6},{8,9},{9,8},{10,11... | collective-permute-start | bytes 5505032 | tf_op jit(solution)/shard_map/ppermute | solution.py:379
  211.6 8.2 %collective-permute-start.9 = (bf16[1024,896]{1,0:T(8,128)(2,1)}, bf16[1024,896]{1,0:T(8,128)(2,1)}, u32[]{:S(2)}, u32[]{:S(2)}) collective-permute-start(bf16[1024,896]{1,0:T(8,128)(2,1)} %collective-permute-done.5.refs_3_), channel_id=1, source_target_pairs={{0,1},{1,0},{2,3},{3,2},{4,5},{5,4},{6,7},{7,6},{8,9},{9,8},{10,11... | collective-permute-start | bytes 5505032 | tf_op jit(solution)/shard_map/ppermute | solution.py:379
  212.7 49.6 %all-to-all-start.2 = ((bf16[16,448,128]{2,1,0:T(8,128)(2,1)}), bf16[16,448,128]{2,1,0:T(8,128)(2,1)}, u32[]{:S(2)}, u32[]{:S(2)}) async-start(bf16[16,448,128]{2,1,0:T(8,128)(2,1)} %get-tuple-element.91), calls=%async_computation.2 | async-start | bytes 3670016 | tf_op jit(solution)/shard_map/all_to_all | solution.py:382
  245.1 17.3 %collective-permute-start.10 = (bf16[2048,512]{1,0:T(8,128)(2,1)}, bf16[2048,512]{1,0:T(8,128)(2,1)S(1)}, u32[]{:S(2)}, u32[]{:S(2)}) collective-permute-start(bf16[2048,512]{1,0:T(8,128)(2,1)} %hidden.1.own_h), channel_id=1, source_target_pairs={{0,1},{1,0},{2,3},{3,2},{4,5},{5,4},{6,7},{7,6},{8,9},{9,8},{10,11... | collective-permute-start | bytes 6291464 | tf_op jit(solution)/shard_map/ppermute | solution.py:379
  262.3 9.5 %copy-start.7 = (bf16[2048,512]{1,0:T(8,128)(2,1)}, bf16[2048,512]{1,0:T(8,128)(2,1)S(1)}, u32[]{:S(2)}) copy-start(bf16[2048,512]{1,0:T(8,128)(2,1)S(1)} %collective-permute-done.10.other_h) | copy-start | bytes 6291460
  262.3 36.7 %all-to-all-start.3 = ((bf16[16,336,128]{2,1,0:T(8,128)(2,1)}), bf16[16,336,128]{2,1,0:T(8,128)(2,1)}, u32[]{:S(2)}, u32[]{:S(2)}) async-start(bf16[16,336,128]{2,1,0:T(8,128)(2,1)} %get-tuple-element.101), calls=%async_computation.3 | async-start | bytes 2752512 | tf_op jit(solution)/shard_map/all_to_all | solution.py:382
  267.6 4.3 %copy-start.5 = (bf16[2048,512]{1,0:T(8,128)(2,1)S(1)}, bf16[2048,512]{1,0:T(8,128)(2,1)}, u32[]{:S(2)}) copy-start(bf16[2048,512]{1,0:T(8,128)(2,1)} %hidden.1.own_h) | copy-start | bytes 6291460
  269.3 2.5 collective-permute-start.11
  275.6 0.8 copy-start.10
  276.3 38.7 %collective-permute-start.12 = (bf16[1024,384]{1,0:T(8,128)(2,1)}, bf16[1024,384]{1,0:T(8,128)(2,1)}, u32[]{:S(2)}, u32[]{:S(2)}) collective-permute-start(bf16[1024,384]{1,0:T(8,128)(2,1)} %get-tuple-element.116), channel_id=1, source_target_pairs={{0,2},{2,0},{4,6},{6,4},{8,10},{10,8},{12,14},{14,12},{16,18},{18,... | collective-permute-start | bytes 2359304 | tf_op jit(solution)/shard_map/ppermute | solution.py:333
  276.9 38.1 %collective-permute-start.13 = (bf16[1024,384]{1,0:T(8,128)(2,1)}, bf16[1024,384]{1,0:T(8,128)(2,1)}, u32[]{:S(2)}, u32[]{:S(2)}) collective-permute-start(bf16[1024,384]{1,0:T(8,128)(2,1)} %get-tuple-element.118), channel_id=1, source_target_pairs={{0,4},{2,6},{4,0},{6,2},{8,12},{10,14},{12,8},{14,10},{16,20},{18,... | collective-permute-start | bytes 2359304 | tf_op jit(solution)/shard_map/ppermute | solution.py:333
  277.5 1.6 copy-start.8
  282.1 1.0 copy-start.3
  299.0 1.6 copy-start.11
  299.0 16.0 %copy-start.4 = (f32[1024,256]{1,0:T(8,128)S(1)}, f32[1024,256]{1,0:T(8,128)}, u32[]{:S(2)}) copy-start(f32[1024,256]{1,0:T(8,128)} %copy-done.3) | copy-start | bytes 3145732
  300.6 17.7 %copy-start.6 = (bf16[2048,512]{1,0:T(8,128)(2,1)S(1)}, bf16[2048,512]{1,0:T(8,128)(2,1)}, u32[]{:S(2)}) copy-start(bf16[2048,512]{1,0:T(8,128)(2,1)} %hidden.1.own_h) | copy-start | bytes 6291460
  300.6 17.7 %copy-start.9 = (bf16[2048,512]{1,0:T(8,128)(2,1)S(1)}, bf16[2048,512]{1,0:T(8,128)(2,1)}, u32[]{:S(2)}) copy-start(bf16[2048,512]{1,0:T(8,128)(2,1)} %copy-done.7) | copy-start | bytes 6291460
  300.6 17.7 %collective-permute-start.22 = (bf16[8,336,128]{2,1,0:T(8,128)(2,1)S(1)}, bf16[8,336,128]{2,1,0:T(8,128)(2,1)S(1)}, u32[]{:S(2)}, u32[]{:S(2)}) collective-permute-start(bf16[8,336,128]{2,1,0:T(8,128)(2,1)S(1)} %get-tuple-element.167), channel_id=1, source_target_pairs={{0,1},{1,0},{2,3},{3,2},{4,5},{5,4},{6,7},{7,6},{8,9},{9,8},{10,11... | collective-permute-start | bytes 2064392 | tf_op jit(solution)/shard_map/ppermute | solution.py:379
  300.7 14.3 %collective-permute-start.14 = (bf16[1024,256]{1,0:T(8,128)(2,1)S(1)}, bf16[1024,256]{1,0:T(8,128)(2,1)S(1)}, u32[]{:S(2)}, u32[]{:S(2)}) collective-permute-start(bf16[1024,256]{1,0:T(8,128)(2,1)S(1)} %copy-done.11), channel_id=1, source_target_pairs={{0,8},{2,10},{4,12},{6,14},{8,0},{10,2},{12,4},{14,6},{16,24},{18,... | collective-permute-start | bytes 1572872 | tf_op jit(solution)/shard_map/ppermute | solution.py:333
  316.7 9.3 %collective-permute-start.17 = (bf16[512,256]{1,0:T(8,128)(2,1)S(1)}, bf16[512,256]{1,0:T(8,128)(2,1)S(1)}, u32[]{:S(2)}, u32[]{:S(2)}) collective-permute-start(bf16[512,256]{1,0:T(8,128)(2,1)S(1)} %get-tuple-element.126), channel_id=1, source_target_pairs={{0,2},{2,0},{4,6},{6,4},{8,10},{10,8},{12,14},{14,12},{16,18},{18,... | collective-permute-start | bytes 786440 | tf_op jit(solution)/shard_map/ppermute | solution.py:333
  320.2 17.1 %collective-permute-start.23 = (bf16[1024,256]{1,0:T(8,128)(2,1)S(1)}, bf16[1024,256]{1,0:T(8,128)(2,1)S(1)}, u32[]{:S(2)}, u32[]{:S(2)}) collective-permute-start(bf16[1024,256]{1,0:T(8,128)(2,1)S(1)} %get-tuple-element.144), channel_id=1, source_target_pairs={{0,2},{2,0},{4,6},{6,4},{8,10},{10,8},{12,14},{14,12},{16,18},{18,... | collective-permute-start | bytes 1572872 | tf_op jit(solution)/shard_map/ppermute | solution.py:333
  320.8 12.1 %collective-permute-start.15 = (bf16[512,384]{1,0:T(8,128)(2,1)S(1)}, bf16[512,384]{1,0:T(8,128)(2,1)S(1)}, u32[]{:S(2)}, u32[]{:S(2)}) collective-permute-start(bf16[512,384]{1,0:T(8,128)(2,1)S(1)} %get-tuple-element.122), channel_id=1, source_target_pairs={{0,4},{2,6},{4,0},{6,2},{8,12},{10,14},{12,8},{14,10},{16,20},{18,... | collective-permute-start | bytes 1179656 | tf_op jit(solution)/shard_map/ppermute | solution.py:333
  321.5 12.1 %collective-permute-start.16 = (bf16[512,384]{1,0:T(8,128)(2,1)S(1)}, bf16[512,384]{1,0:T(8,128)(2,1)S(1)}, u32[]{:S(2)}, u32[]{:S(2)}) collective-permute-start(bf16[512,384]{1,0:T(8,128)(2,1)S(1)} %get-tuple-element.124), channel_id=1, source_target_pairs={{0,8},{2,10},{4,12},{6,14},{8,0},{10,2},{12,4},{14,6},{16,24},{18,... | collective-permute-start | bytes 1179656 | tf_op jit(solution)/shard_map/ppermute | solution.py:333
  321.7 22.0 %collective-permute-start.24 = (bf16[1024,256]{1,0:T(8,128)(2,1)S(1)}, bf16[1024,256]{1,0:T(8,128)(2,1)S(1)}, u32[]{:S(2)}, u32[]{:S(2)}) collective-permute-start(bf16[1024,256]{1,0:T(8,128)(2,1)S(1)} %get-tuple-element.146), channel_id=1, source_target_pairs={{0,4},{2,6},{4,0},{6,2},{8,12},{10,14},{12,8},{14,10},{16,20},{18,... | collective-permute-start | bytes 1572872 | tf_op jit(solution)/shard_map/ppermute | solution.py:333
  326.0 18.8 %collective-permute-start.25 = (bf16[1024,256]{1,0:T(8,128)(2,1)S(1)}, bf16[1024,256]{1,0:T(8,128)(2,1)S(1)}, u32[]{:S(2)}, u32[]{:S(2)}) collective-permute-start(bf16[1024,256]{1,0:T(8,128)(2,1)S(1)} %get-tuple-element.148), channel_id=1, source_target_pairs={{0,8},{2,10},{4,12},{6,14},{8,0},{10,2},{12,4},{14,6},{16,24},{18,... | collective-permute-start | bytes 1572872 | tf_op jit(solution)/shard_map/ppermute | solution.py:333
  333.7 15.3 %collective-permute-start.18 = (bf16[256,384]{1,0:T(8,128)(2,1)S(1)}, bf16[256,384]{1,0:T(8,128)(2,1)S(1)}, u32[]{:S(2)}, u32[]{:S(2)}) collective-permute-start(bf16[256,384]{1,0:T(8,128)(2,1)S(1)} %get-tuple-element.128), channel_id=1, source_target_pairs={{0,8},{2,10},{4,12},{6,14},{8,0},{10,2},{12,4},{14,6},{16,24},{18,... | collective-permute-start | bytes 589832 | tf_op jit(solution)/shard_map/ppermute | solution.py:333
  334.0 15.0 %collective-permute-start.19 = (bf16[256,384]{1,0:T(8,128)(2,1)S(1)}, bf16[256,384]{1,0:T(8,128)(2,1)S(1)}, u32[]{:S(2)}, u32[]{:S(2)}) collective-permute-start(bf16[256,384]{1,0:T(8,128)(2,1)S(1)} %get-tuple-element.130), channel_id=1, source_target_pairs={{0,2},{2,0},{4,6},{6,4},{8,10},{10,8},{12,14},{14,12},{16,18},{18,... | collective-permute-start | bytes 589832 | tf_op jit(solution)/shard_map/ppermute | solution.py:333
  337.3 9.5 %collective-permute-start.20 = (bf16[256,256]{1,0:T(8,128)(2,1)S(1)}, bf16[256,256]{1,0:T(8,128)(2,1)S(1)}, u32[]{:S(2)}, u32[]{:S(2)}) collective-permute-start(bf16[256,256]{1,0:T(8,128)(2,1)S(1)} %get-tuple-element.132), channel_id=1, source_target_pairs={{0,4},{2,6},{4,0},{6,2},{8,12},{10,14},{12,8},{14,10},{16,20},{18,... | collective-permute-start | bytes 393224 | tf_op jit(solution)/shard_map/ppermute | solution.py:333
  345.0 7.4 %collective-permute-start.26 = (bf16[512,256]{1,0:T(8,128)(2,1)S(1)}, bf16[512,256]{1,0:T(8,128)(2,1)S(1)}, u32[]{:S(2)}, u32[]{:S(2)}) collective-permute-start(bf16[512,256]{1,0:T(8,128)(2,1)S(1)} %get-tuple-element.150), channel_id=1, source_target_pairs={{0,4},{2,6},{4,0},{6,2},{8,12},{10,14},{12,8},{14,10},{16,20},{18,... | collective-permute-start | bytes 786440 | tf_op jit(solution)/shard_map/ppermute | solution.py:333
  346.5 9.0 %collective-permute-start.27 = (bf16[512,256]{1,0:T(8,128)(2,1)S(1)}, bf16[512,256]{1,0:T(8,128)(2,1)S(1)}, u32[]{:S(2)}, u32[]{:S(2)}) collective-permute-start(bf16[512,256]{1,0:T(8,128)(2,1)S(1)} %get-tuple-element.152), channel_id=1, source_target_pairs={{0,8},{2,10},{4,12},{6,14},{8,0},{10,2},{12,4},{14,6},{16,24},{18,... | collective-permute-start | bytes 786440 | tf_op jit(solution)/shard_map/ppermute | solution.py:333
  346.7 8.8 %collective-permute-start.28 = (bf16[512,256]{1,0:T(8,128)(2,1)S(1)}, bf16[512,256]{1,0:T(8,128)(2,1)S(1)}, u32[]{:S(2)}, u32[]{:S(2)}) collective-permute-start(bf16[512,256]{1,0:T(8,128)(2,1)S(1)} %get-tuple-element.154), channel_id=1, source_target_pairs={{0,2},{2,0},{4,6},{6,4},{8,10},{10,8},{12,14},{14,12},{16,18},{18,... | collective-permute-start | bytes 786440 | tf_op jit(solution)/shard_map/ppermute | solution.py:333
  349.1 14.3 %collective-permute-start.21 = (bf16[128,1024]{1,0:T(8,128)(2,1)S(1)}, bf16[128,1024]{1,0:T(8,128)(2,1)S(1)}, u32[]{:S(2)}, u32[]{:S(2)}) collective-permute-start(bf16[128,1024]{1,0:T(8,128)(2,1)S(1)} %get-tuple-element.134), channel_id=1, source_target_pairs={{0,16},{2,18},{4,20},{6,22},{8,24},{10,26},{12,28},{14,30},{16,0},... | collective-permute-start | bytes 786440 | tf_op jit(solution)/shard_map/ppermute | solution.py:333
  355.6 5.2 %collective-permute-start.29 = (bf16[256,256]{1,0:T(8,128)(2,1)S(1)}, bf16[256,256]{1,0:T(8,128)(2,1)S(1)}, u32[]{:S(2)}, u32[]{:S(2)}) collective-permute-start(bf16[256,256]{1,0:T(8,128)(2,1)S(1)} %get-tuple-element.156), channel_id=1, source_target_pairs={{0,8},{2,10},{4,12},{6,14},{8,0},{10,2},{12,4},{14,6},{16,24},{18,... | collective-permute-start | bytes 393224 | tf_op jit(solution)/shard_map/ppermute | solution.py:333
  355.8 5.0 %collective-permute-start.30 = (bf16[256,256]{1,0:T(8,128)(2,1)S(1)}, bf16[256,256]{1,0:T(8,128)(2,1)S(1)}, u32[]{:S(2)}, u32[]{:S(2)}) collective-permute-start(bf16[256,256]{1,0:T(8,128)(2,1)S(1)} %get-tuple-element.158), channel_id=1, source_target_pairs={{0,2},{2,0},{4,6},{6,4},{8,10},{10,8},{12,14},{14,12},{16,18},{18,... | collective-permute-start | bytes 393224 | tf_op jit(solution)/shard_map/ppermute | solution.py:333
  357.5 5.0 %collective-permute-start.31 = (bf16[256,256]{1,0:T(8,128)(2,1)S(1)}, bf16[256,256]{1,0:T(8,128)(2,1)S(1)}, u32[]{:S(2)}, u32[]{:S(2)}) collective-permute-start(bf16[256,256]{1,0:T(8,128)(2,1)S(1)} %get-tuple-element.160), channel_id=1, source_target_pairs={{0,4},{2,6},{4,0},{6,2},{8,12},{10,14},{12,8},{14,10},{16,20},{18,... | collective-permute-start | bytes 393224 | tf_op jit(solution)/shard_map/ppermute | solution.py:333
  362.6 6.7 %collective-permute-start.32 = (bf16[128,768]{1,0:T(8,128)(2,1)S(1)}, bf16[128,768]{1,0:T(8,128)(2,1)S(1)}, u32[]{:S(2)}, u32[]{:S(2)}) collective-permute-start(bf16[128,768]{1,0:T(8,128)(2,1)S(1)} %get-tuple-element.162), channel_id=1, source_target_pairs={{0,16},{2,18},{4,20},{6,22},{8,24},{10,26},{12,28},{14,30},{16,0},... | collective-permute-start | bytes 589832 | tf_op jit(solution)/shard_map/ppermute | solution.py:333

commit v4 on v3

--- a/solution.py
+++ b/solution.py
@@ -59,15 +59,16 @@
     out_ref[dest, base + 3 * rows : base + 3 * rows + mid, :] = both.astype(out_ref.dtype)
 
 
-def pack_gate_kernel(list_ref, gate_ref, share_ref, out_ref):
+def pack_pair_kernel(list_ref, gate_ref, up_ref, share_ref, out_ref):
     slots, depth, width = gate_ref.shape
     size = depth * 7 // 2
     row = lax.broadcasted_iota(jnp.int32, share_ref.shape[1:], 0) // 4
     for dest in range(out_ref.shape[0]):
-        pack_rows(
-            lambda place: (gate_ref, list_ref[place]),
-            out_ref, 0, dest, 0, depth, width // LANES,
-        )
+        for number, in_ref in enumerate((gate_ref, up_ref)):
+            pack_rows(
+                lambda place, in_ref=in_ref: (in_ref, list_ref[place]),
+                out_ref, number * size, dest, 0, depth, width // LANES,
+            )
         value = share_ref[dest]
         high = value.astype(out_ref.dtype)
         rest = value - high.astype(jnp.float32)
@@ -82,7 +83,7 @@
                 jnp.where(row == 2, low.astype(jnp.float32), 0.0),
             ),
         )
-        out_ref[dest, size:, :] = terms.astype(out_ref.dtype)
+        out_ref[dest, 2 * size :, :] = terms.astype(out_ref.dtype)
 
 
 def pack_kernel(parts, list_ref, in_ref, *out_refs):
@@ -105,17 +106,17 @@
     return pl.BlockSpec(memory_space=pltpu.SMEM)
 
 
-def pack_gate(listing, gate_proj, share, dests):
+def pack_pair(listing, gate_proj, up_proj, share, dests):
     slots, depth, width = gate_proj.shape
-    shape = (dests, depth * 7 // 2 + share.shape[1], LANES)
+    shape = (dests, depth * 7 + share.shape[1], LANES)
     return pl.pallas_call(
-        pack_gate_kernel,
+        pack_pair_kernel,
         out_shape=jax.ShapeDtypeStruct(shape, gate_proj.dtype),
-        in_specs=[smem(), vmem(), vmem()],
+        in_specs=[smem(), vmem(), vmem(), vmem()],
         out_specs=vmem(),
-        compiler_params=pltpu.CompilerParams(vmem_limit_bytes=32 * MIB),
-        name="pack_gate",
-    )(listing, gate_proj, share)
+        compiler_params=pltpu.CompilerParams(vmem_limit_bytes=40 * MIB),
+        name="pack_gate_up",
+    )(listing, gate_proj, up_proj, share)
 
 
 def pack(listing, weights, dests, parts, name):
@@ -146,9 +147,10 @@
 
 
 def hidden_kernel(at_ref, *refs):
-    pieces, (gate_ref, up_ref, out_ref, gate_w, up_w, rows) = refs[:8], refs[8:]
-    sources, packed_rows, _ = up_ref.shape
-    depth = packed_rows * 2 // 7
+    pieces, (packed_ref, out_ref, gate_w, up_w, rows) = refs[:8], refs[8:]
+    sources = packed_ref.shape[0]
+    depth = gate_w.shape[0] // sources
+    size = depth * 7 // 2
     group = sources // 2
     tile = pl.program_id(0)
     x, y, zl = tile // 4, tile // 2 % 2, tile % 2
@@ -158,8 +160,8 @@
     def _():
         for at in range(sources):
             place = (core + at // group) % 2 * group + at % group
-            unpack_rows(gate_ref, place, 0, depth, gate_w, at * depth, 0)
-            unpack_rows(up_ref, place, 0, depth, up_w, at * depth, 0)
+            unpack_rows(packed_ref, place, 0, depth, gate_w, at * depth, 0)
+            unpack_rows(packed_ref, place, size, depth, up_w, at * depth, 0)
 
     mid = pieces[0].shape[1]
     for number in range(4):
@@ -184,7 +186,7 @@
     for zh in range(2):
         source = me ^ (x + 2 * y + 4 * zl + 8 * zh)
         weight = lax.dot_general(
-            gate_ref[source, packed_rows:, :],
+            packed_ref[source, 2 * size :, :],
             chosen,
             (((0,), (0,)), ((), ())),
             preferred_element_type=jnp.float32,
@@ -193,7 +195,7 @@
         out_ref[span, :] = (value[span, :] * weight).astype(out_ref.dtype)
 
 
-def hidden_units(at, pieces, gate, up):
+def hidden_units(at, pieces, packed):
     total = 2 * pieces[0].shape[0]
     mid = pieces[0].shape[1]
     tile = total // 8
@@ -208,32 +210,32 @@
     return pl.pallas_call(
         hidden_kernel,
         grid=(8,),
-        out_shape=jax.ShapeDtypeStruct((total, wide), up.dtype),
+        out_shape=jax.ShapeDtypeStruct((total, wide), packed.dtype),
         in_specs=[smem()]
         + [pl.BlockSpec((tile, mid), where) for where in maps]
-        + [vmem(), vmem()],
+        + [vmem()],
         out_specs=pl.BlockSpec((tile, wide), lambda i: (i, 0)),
-        scratch_shapes=[pltpu.VMEM((model, wide), up.dtype)] * 2
-        + [pltpu.VMEM((tile, model), up.dtype)],
+        scratch_shapes=[pltpu.VMEM((model, wide), packed.dtype)] * 2
+        + [pltpu.VMEM((tile, model), packed.dtype)],
         compiler_params=pltpu.CompilerParams(vmem_limit_bytes=56 * MIB),
         cost_estimate=pl.CostEstimate(
             flops=4 * total * model * wide, bytes_accessed=24 * MIB, transcendentals=total * wide
         ),
         name="hidden",
-    )(at, *pieces, gate, up)
-
-
-ORDERS = ((0, 1, 2), (1, 2, 0), (2, 0, 1))
-
-
-def group_spans(features):
+    )(at, *pieces, packed)
+
+
+HALVES = ((0, 1, 2), (1, 0, 2))
+THIRDS = ((0, 1, 2), (1, 2, 0), (2, 0, 1))
+
+
+def group_spans(features, count):
     tiles = features // LANES
-    cuts = [0, -(-tiles // 3), -(-tiles // 3) + -(-(tiles - -(-tiles // 3)) // 2), tiles]
-    return [slice(lo * LANES, hi * LANES) for lo, hi in zip(cuts, cuts[1:])]
-
-
-def stage_axis(number, stage):
-    order = ORDERS[number]
+    cuts = [-(-tiles * at // count) * LANES for at in range(count + 1)]
+    return [slice(lo, hi) for lo, hi in zip(cuts, cuts[1:])]
+
+
+def stage_axis(order, stage):
     return sum(1 for bit in order[stage:] if bit < order[stage])
 
 
@@ -242,15 +244,15 @@
     return [slice((2 * at + side) * size, (2 * at + side + 1) * size) for at in range(1 << axis)]
 
 
-def down_kernel(rows, side, own_h, other_h, own_ref, other_ref, *refs):
+def down_kernel(rows, side, orders, own_h, other_h, own_ref, other_ref, *refs):
     out_refs, (own_w, other_w) = refs[:-2], refs[-2:]
     for in_ref, w_ref in ((own_ref, own_w), (other_ref, other_w)):
         for at in range(in_ref.shape[0]):
             unpack_rows(in_ref, at, 0, rows, w_ref, at * rows, 0)
     dims = (((1,), (1,)), ((), ()))
-    for number, span in enumerate(group_spans(own_w.shape[0])):
+    for number, span in enumerate(group_spans(own_w.shape[0], len(orders))):
         done = 0
-        for tokens in half_spans(own_h.shape[0], stage_axis(number, 0), side):
+        for tokens in half_spans(own_h.shape[0], stage_axis(orders[number], 0), side):
             value = lax.dot_general(
                 own_h[tokens, :], own_w[span, :], dims, preferred_element_type=jnp.float32
             ) + lax.dot_general(
@@ -261,17 +263,17 @@
             done += size
 
 
-def down_product(own_h, other_h, own, other, rows, side, dtype, name):
+def down_product(own_h, other_h, own, other, rows, side, orders, dtype, name):
     sources = own.shape[0]
     total, wide = own_h.shape
     tokens = total // 2
     features = sources * rows
     shapes = [
         jax.ShapeDtypeStruct((tokens, span.stop - span.start), dtype)
-        for span in group_spans(features)
+        for span in group_spans(features, len(orders))
     ]
     return pl.pallas_call(
-        functools.partial(down_kernel, rows, side),
+        functools.partial(down_kernel, rows, side, orders),
         out_shape=shapes,
         in_specs=[vmem()] * 4,
         out_specs=[vmem()] * len(shapes),
@@ -285,7 +287,7 @@
 
 
 def halve_kernel(axes, *refs):
-    count = len(refs) // 4 if axes else 3
+    count = len(refs) // 4 if axes else len(refs) // 2 - 1
     out_refs = refs[2 * count :]
     lane = 0
     for number in range(count):
@@ -390,48 +392,42 @@
     belongs = slot_place[None, None, :, None] == places[:, :, None, None]
     share = jnp.sum(jnp.where(belongs, share[None, None], 0.0), axis=2)
 
-    far = swap(tokens, 3)
-    gate_packed, far = tie((pack_gate(listing, gate_proj, share, devices), far))
-    (up_packed,) = pack(listing, up_proj, devices, (depth,), "pack_up")
-
-    gate = move(gate_packed)
+    near, far = swap(tokens, 2), swap(tokens, 3)
+    corner = swap(far, 2)
+    packed = pack_pair(listing, gate_proj, up_proj, share, devices)
+    packed, near, far, corner = tie((packed, near, far, corner))
+
+    moved = move(packed)
     mid = tokens.shape[1] // 2
-    rows = jnp.concatenate([tokens, far], axis=0)
-    rows = jnp.concatenate([rows, swap(rows, 2)], axis=0)
+    rows = jnp.concatenate([tokens, far, near, corner], axis=0)
     first, second = rows[:, :mid], rows[:, mid:]
     first = jnp.concatenate([first, swap(first, 1)], axis=0)
     second = jnp.concatenate([second, swap(second, 0)], axis=0)
-    gate, first, second, up_packed = tie((gate, first, second, up_packed))
-
-    up = move(up_packed)
     pieces = [first, swap(first, 0), second, swap(second, 1)]
-    others = [exchange(first), None, exchange(second), None]
+    others = [exchange(piece) for piece in pieces]
     parts = (128, 96)
     down_packed = pack(listing, down_proj, devices, parts, "pack_down")
-    up, pieces, others[0], others[2], down_packed = tie(
-        (up, pieces, others[0], others[2], down_packed)
-    )
+    moved, down_packed = tie((moved, down_packed))
 
     down0 = move(down_packed[0])
-    others[1], others[3] = exchange(pieces[1]), exchange(pieces[3])
     at = jnp.stack([me, core]).astype(jnp.int32)
-    hidden = hidden_units(at, pieces + others, gate, up)
+    hidden = hidden_units(at, pieces + others, moved)
     hidden_other = exchange(hidden)
     down0, hidden, hidden_other, packed = tie((down0, hidden, hidden_other, down_packed[1]))
 
-    def products(down, rows_in):
+    def products(down, rows_in, orders):
         own = lax.dynamic_slice_in_dim(down, core * group, group, 0)
         other = exchange(lax.dynamic_slice_in_dim(down, (1 - core) * group, group, 0))
         args = (hidden, hidden_other, own, other)
-        sent = down_product(*args, rows_in, 1, jnp.bfloat16, "down_send")
+        sent = down_product(*args, rows_in, 1, orders, jnp.bfloat16, "down_send")
         sent, args = tie((sent, args))
-        come = [swap(value, order[0]) for value, order in zip(sent, ORDERS)]
-        return down_product(*args, rows_in, 0, jnp.float32, "down_keep"), come
-
-    def stage(kept, come, number):
-        axes = tuple(stage_axis(at, number) for at in range(3))
+        come = [swap(value, order[0]) for value, order in zip(sent, orders)]
+        return down_product(*args, rows_in, 0, orders, jnp.float32, "down_keep"), come
+
+    def stage(kept, come, number, orders):
+        axes = tuple(stage_axis(order, number) for order in orders)
         out = halve(list(zip(kept, come)), axes)
-        come = [swap(send, order[number]) for (send, _), order in zip(out, ORDERS)]
+        come = [swap(send, order[number]) for (send, _), order in zip(out, orders)]
         return [keep for _, keep in out], come
 
     def last_stage(kept, come):
@@ -440,13 +436,13 @@
         return (keep + come.astype(jnp.float32)).astype(jnp.bfloat16)
 
     down1 = move(packed)
-    kept0, come0 = products(down0, parts[0])
+    kept0, come0 = products(down0, parts[0], HALVES)
     down1, kept0 = tie((down1, kept0))
-    kept1, come1 = products(down1, parts[1])
-    kept0, come0 = stage(kept0, come0, 1)
-    kept1, come1 = stage(kept1, come1, 1)
-    kept0, come0 = stage(kept0, come0, 2)
-    kept1, come1 = stage(kept1, come1, 2)
+    kept1, come1 = products(down1, parts[1], THIRDS)
+    kept0, come0 = stage(kept0, come0, 1, HALVES)
+    kept1, come1 = stage(kept1, come1, 1, THIRDS)
+    kept0, come0 = stage(kept0, come0, 2, HALVES)
+    kept1, come1 = stage(kept1, come1, 2, THIRDS)
     out = []
     for rows_in, total in zip(parts, (last_stage(kept0, come0), last_stage(kept1, come1))):
         out.append(total.reshape(block, group, rows_in))

time: 376 us -> 357 us (0.949)
  waiting for transfers between devices: 247 us -> 221 us
  starting transfers between devices: 51 us -> 66.5 us
  Pallas kernels: 46.5 us -> 41.9 us
    ppermute x26 -> x24, waiting for transfers between devices: 212 us -> 171 us  [swap(): return lax.ppermute(value, 'ep', [(i, i ^ 1 << bit) for i in range(size)])]
    all_to_all x4 -> x3, waiting for transfers between devices: 33.2 us -> 42.7 us  [move(): return lax.all_to_all(packed, 'ep', 0, 0, tiled=True)]
    all_to_all x4 -> x3, starting transfers between devices: 26.5 us -> 35.4 us  [move(): return lax.all_to_all(packed, 'ep', 0, 0, tiled=True)]
    ppermute x26 -> x24, starting transfers between devices: 23.4 us -> 30.5 us  [swap(): return lax.ppermute(value, 'ep', [(i, i ^ 1 << bit) for i in range(size)])]
    ppermute x7, waiting for transfers between devices: 2.48 us -> 6.83 us  [exchange(): return lax.ppermute(value, 'et', [(0, 1), (1, 0)])]
    unnamed x32 -> x29, local copies, waits for them, and re-layouts: 12 us -> 11.9 us
  transfers between devices with their start and end apart: 37 -> 34, of which waited for: 20 -> 19; matrix products, arithmetic and copies ran while one was open for 4% -> 3% of each run, Pallas kernels for 13% -> 12%
where the time goes in v4:
time: 357 us; the launch traced here: 353 us
  waiting for transfers between devices  221 us (62%)
  starting transfers between devices  66.5 us (19%)
  Pallas kernels  41.9 us (12%)
  local copies, waits for them, and re-layouts  16.7 us (5%)
  other arithmetic  6.16 us (2%)
    ppermute x24, waiting for transfers between devices, swap(): return lax.ppermute(value, 'ep', [(i, i ^ 1 << bit) for i in range(size)])  171 us
    all_to_all x3, waiting for transfers between devices, move(): return lax.all_to_all(packed, 'ep', 0, 0, tiled=True)  42.7 us
    all_to_all x3, starting transfers between devices, move(): return lax.all_to_all(packed, 'ep', 0, 0, tiled=True)  35.4 us
    ppermute x24, starting transfers between devices, swap(): return lax.ppermute(value, 'ep', [(i, i ^ 1 << bit) for i in range(size)])  30.5 us
    pallas_call x1, Pallas kernels, hidden_units(): pl.pallas_call(hidden_kernel, grid=(8,), out_shape=jax.ShapeDtypeStruct((...  25.2 us
    unnamed x29, local copies, waits for them, and re-layouts  11.9 us
    pallas_call x4, Pallas kernels, down_product(): pl.pallas_call(functools.partial(down_kernel, rows, side, orders), out_sh...  10 us
  transfers between devices with their start and end apart: 34, of which 19 were waited for; matrix products, arithmetic and copies ran while one was open for 3% of the time, Pallas kernels for 12%

profile of v4, /device:TPU:14, one launch (start us, length us, event | category | flops | bytes accessed | tf_op | source)
XLA Modules:
  0.0 352.6 jit_solution(16422685327870986109)
XLA Ops:
  0.5 2.6 collective-permute-start.1
  3.0 0.9 select_reduce_fusion.4
  4.3 0.7 select_reduce_fusion.1
  5.0 18.4 %collective-permute-done.1 = bf16[128,1792]{1,0:T(8,128)(2,1)S(1)} collective-permute-done((bf16[128,1792]{1,0:T(8,128)(2,1)}, bf16[128,1792]{1,0:T(8,128)(2,1)S(1)}, u32[]{:S(2)}, u32[]{:S(2)}) %collective-permute-start.1) | collective-permute-done | bytes 458784 | tf_op jit(solution)/shard_map/ppermute | solution.py:335
  23.4 1.6 collective-permute-start.2
  25.1 0.8 broadcast_compare_fusion
  25.9 0.9 select_reduce_fusion.share_ref
  26.9 2.0 copy-done.2
  28.9 2.0 copy-done.3
  30.9 1.8 pack_gate_up.1
  32.8 2.7 copy-done
  35.5 6.3 %all-to-all-start = ((bf16[16,1584,128]{2,1,0:T(8,128)(2,1)}), bf16[16,1584,128]{2,1,0:T(8,128)(2,1)}, u32[]{:S(2)}, u32[]{:S(2)}) async-start(bf16[16,1584,128]{2,1,0:T(8,128)(2,1)} %copy-done), calls=%async_computation | async-start | bytes 12976128 | tf_op jit(solution)/shard_map/all_to_all | solution.py:384
  42.2 0.6 collective-permute-start.3
  42.8 0.6 collective-permute-start.5
  43.4 51.7 %collective-permute-done.3 = bf16[512,896]{1,0:T(8,128)(2,1)S(1)} collective-permute-done((bf16[512,896]{1,0:T(8,128)(2,1)S(1)}, bf16[512,896]{1,0:T(8,128)(2,1)S(1)}, u32[]{:S(2)}, u32[]{:S(2)}) %collective-permute-start.3) | collective-permute-done | bytes 917536 | tf_op jit(solution)/shard_map/ppermute | solution.py:335
  95.6 1.4 pad_maximum_fusion.1.refs_2_
  97.0 2.5 collective-permute-start.6
  100.0 58.5 %collective-permute-done.4.refs_1_ = bf16[1024,896]{1,0:T(8,128)(2,1)} collective-permute-done((bf16[1024,896]{1,0:T(8,128)(2,1)S(1)}, bf16[1024,896]{1,0:T(8,128)(2,1)}, u32[]{:S(2)}, u32[]{:S(2)}) %collective-permute-start.4) | collective-permute-done | bytes 1835040 | tf_op jit(solution)/shard_map/ppermute | solution.py:335
  158.5 5.5 %collective-permute-done.6.refs_3_ = bf16[1024,896]{1,0:T(8,128)(2,1)} collective-permute-done((bf16[1024,896]{1,0:T(8,128)(2,1)}, bf16[1024,896]{1,0:T(8,128)(2,1)}, u32[]{:S(2)}, u32[]{:S(2)}) %collective-permute-start.6) | collective-permute-done | bytes 1835040 | tf_op jit(solution)/shard_map/ppermute | solution.py:335
  164.0 2.0 copy-done.1
  166.1 2.6 pack_down.1
  168.7 0.6 pad_add_fusion.at_ref
  169.4 12.8 %all-to-all-done.refs_8_ = bf16[16,1584,128]{2,1,0:T(8,128)(2,1)} async-done(((bf16[16,1584,128]{2,1,0:T(8,128)(2,1)}), bf16[16,1584,128]{2,1,0:T(8,128)(2,1)}, u32[]{:S(2)}, u32[]{:S(2)}) %all-to-all-start) | async-done | bytes 6488096 | tf_op jit(solution)/shard_map/all_to_all | solution.py:384
  182.2 23.8 %all-to-all-start.1 = ((bf16[16,448,128]{2,1,0:T(8,128)(2,1)}), bf16[16,448,128]{2,1,0:T(8,128)(2,1)}, u32[]{:S(2)}, u32[]{:S(2)}) async-start(bf16[16,448,128]{2,1,0:T(8,128)(2,1)} %get-tuple-element.71), calls=%async_computation.1 | async-start | bytes 3670016 | tf_op jit(solution)/shard_map/all_to_all | solution.py:384
  206.0 25.2 %hidden.1.own_h = bf16[2048,512]{1,0:T(8,128)(2,1)} custom-call(s32[2]{0:T(128)} %pad_add_fusion.at_ref, bf16[1024,896]{1,0:T(8,128)(2,1)} %copy-done.11, bf16[1024,896]{1,0:T(8,128)(2,1)} %collective-permute-done.4.refs_1_, bf16[1024,896]{1,0:T(8,128)(2,1)} %pad_maximum_fusion.1.refs_2_, bf16[1024,896]{1,0:T(8,128)(2,1)} %collective-permute-done.6.refs_3_, ...), custom_call_target="tpu_custom_call" | custom-call | flops 15032385536 | bytes 25165824 | tf_op jit(solution)/shard_map/hidden/pallas_call | solution.py:210
  231.3 4.4 %collective-permute-done.11.other_h = bf16[2048,512]{1,0:T(8,128)(2,1)S(1)} collective-permute-done((bf16[2048,512]{1,0:T(8,128)(2,1)}, bf16[2048,512]{1,0:T(8,128)(2,1)S(1)}, u32[]{:S(2)}, u32[]{:S(2)}) %collective-permute-start.11) | collective-permute-done | bytes 2097184 | tf_op jit(solution)/shard_map/ppermute | solution.py:381
  235.6 12.9 %all-to-all-done.1 = bf16[16,448,128]{2,1,0:T(8,128)(2,1)} async-done(((bf16[16,448,128]{2,1,0:T(8,128)(2,1)}), bf16[16,448,128]{2,1,0:T(8,128)(2,1)}, u32[]{:S(2)}, u32[]{:S(2)}) %all-to-all-start.1) | async-done | bytes 1835040 | tf_op jit(solution)/shard_map/all_to_all | solution.py:384
  248.5 5.2 %all-to-all-start.2 = ((bf16[16,336,128]{2,1,0:T(8,128)(2,1)}), bf16[16,336,128]{2,1,0:T(8,128)(2,1)}, u32[]{:S(2)}, u32[]{:S(2)}) async-start(bf16[16,336,128]{2,1,0:T(8,128)(2,1)} %get-tuple-element.77), calls=%async_computation.2 | async-start | bytes 2752512 | tf_op jit(solution)/shard_map/all_to_all | solution.py:384
  253.8 1.7 constant_dynamic-slice_fusion.2
  255.6 2.5 collective-permute-done.12.other_ref
  258.1 3.7 %down_send.2 = (bf16[1024,512]{1,0:T(8,128)(2,1)}, bf16[1024,512]{1,0:T(8,128)(2,1)}) custom-call(bf16[2048,512]{1,0:T(8,128)(2,1)S(1)} %copy-done.6, bf16[2048,512]{1,0:T(8,128)(2,1)S(1)} %collective-permute-done.11.other_h, bf16[8,448,128]{2,1,0:T(8,128)(2,1)S(1)} %get-tuple-element.85.own_ref, bf16[8,448,128]{2,1,0:T(8,128)(2,1)S(1)} %collective-permute-done.12.other_ref), custom_call_target="tpu_custom_call" | custom-call | flops 2147483648 | bytes 8388608 | tf_op jit(solution)/shard_map/down_send/pallas_call | solution.py:275
  261.7 0.6 collective-permute-start.13
  262.3 0.6 collective-permute-start.14
  262.8 1.6 copy-done.9
  264.4 2.5 down_keep.2
  267.0 1.3 copy-done.4
  268.3 17.0 %all-to-all-done.2 = bf16[16,336,128]{2,1,0:T(8,128)(2,1)} async-done(((bf16[16,336,128]{2,1,0:T(8,128)(2,1)}), bf16[16,336,128]{2,1,0:T(8,128)(2,1)}, u32[]{:S(2)}, u32[]{:S(2)}) %all-to-all-start.2) | async-done | bytes 1376288 | tf_op jit(solution)/shard_map/all_to_all | solution.py:384
  285.3 1.5 constant_dynamic-slice_fusion
  287.0 9.4 %collective-permute-done.13.refs_1_ = bf16[1024,512]{1,0:T(8,128)(2,1)S(1)} collective-permute-done((bf16[1024,512]{1,0:T(8,128)(2,1)}, bf16[1024,512]{1,0:T(8,128)(2,1)S(1)}, u32[]{:S(2)}, u32[]{:S(2)}) %collective-permute-start.13) | collective-permute-done | bytes 1048608 | tf_op jit(solution)/shard_map/ppermute | solution.py:335
  296.4 1.6 sum_stage.6
  297.9 1.4 collective-permute-start.15
  299.4 1.0 collective-permute-start.16
  300.4 1.9 down_send.3
  302.3 1.1 collective-permute-start.21
  303.4 0.7 collective-permute-start.22
  304.0 0.8 collective-permute-start.23
  304.9 8.0 %collective-permute-done.15.refs_1_ = bf16[512,512]{1,0:T(8,128)(2,1)S(1)} collective-permute-done((bf16[512,512]{1,0:T(8,128)(2,1)S(1)}, bf16[512,512]{1,0:T(8,128)(2,1)S(1)}, u32[]{:S(2)}, u32[]{:S(2)}) %collective-permute-start.15) | collective-permute-done | bytes 524320 | tf_op jit(solution)/shard_map/ppermute | solution.py:335
  312.9 1.4 collective-permute-done.16.refs_3_
  314.4 1.0 collective-permute-start.17
  315.4 1.1 collective-permute-start.18
  316.5 1.9 down_keep.3
  318.4 5.5 %collective-permute-done.21.refs_1_ = bf16[1024,256]{1,0:T(8,128)(2,1)S(1)} collective-permute-done((bf16[1024,256]{1,0:T(8,128)(2,1)S(1)}, bf16[1024,256]{1,0:T(8,128)(2,1)S(1)}, u32[]{:S(2)}, u32[]{:S(2)}) %collective-permute-start.21) | collective-permute-done | bytes 524320 | tf_op jit(solution)/shard_map/ppermute | solution.py:335
  324.6 1.2 collective-permute-start.25
  325.7 0.5 collective-permute-start.26
  326.3 2.9 collective-permute-done.18.refs_3_
  329.2 5.2 %collective-permute-start.19 = (bf16[128,1024]{1,0:T(8,128)(2,1)S(1)}, bf16[128,1024]{1,0:T(8,128)(2,1)S(1)}, u32[]{:S(2)}, u32[]{:S(2)}) collective-permute-start(bf16[128,1024]{1,0:T(8,128)(2,1)S(1)} %get-tuple-element.102), channel_id=1, source_target_pairs={{0,16},{2,18},{4,20},{6,22},{8,24},{10,26},{12,28},{14,30},{16,0},... | collective-permute-start | bytes 786440 | tf_op jit(solution)/shard_map/ppermute | solution.py:335
  334.4 0.9 collective-permute-done.25.refs_3_
  335.5 2.7 collective-permute-start.27
  338.4 0.7 collective-permute-start.29
  339.1 2.6 collective-permute-done.27.refs_1_
  341.7 1.4 collective-permute-done.28.refs_3_
  343.5 2.6 collective-permute-start.30
  346.3 5.1 %collective-permute-done.30 = bf16[128,768]{1,0:T(8,128)(2,1)S(1)} collective-permute-done((bf16[128,768]{1,0:T(8,128)(2,1)S(1)}, bf16[128,768]{1,0:T(8,128)(2,1)S(1)}, u32[]{:S(2)}, u32[]{:S(2)}) %collective-permute-start.30) | collective-permute-done | bytes 196640 | tf_op jit(solution)/shard_map/ppermute | solution.py:335
  351.6 1.0 copy.15
  (67 shorter events, 4.6 us)
Async XLA Ops:
  0.0 35.5 %collective-permute-start = (bf16[128,1792]{1,0:T(8,128)(2,1)}, bf16[128,1792]{1,0:T(8,128)(2,1)S(1)}, u32[]{:S(2)}, u32[]{:S(2)}) collective-permute-start(bf16[128,1792]{1,0:T(8,128)(2,1)} %param.9), channel_id=1, source_target_pairs={{0,8},{2,10},{4,12},{6,14},{8,0},{10,2},{12,4},{14,6},{16,24},{18,... | collective-permute-start | bytes 1376264 | tf_op jit(solution)/shard_map/ppermute | solution.py:335
  0.5 23.0 %collective-permute-start.1 = (bf16[128,1792]{1,0:T(8,128)(2,1)}, bf16[128,1792]{1,0:T(8,128)(2,1)S(1)}, u32[]{:S(2)}, u32[]{:S(2)}) collective-permute-start(bf16[128,1792]{1,0:T(8,128)(2,1)} %param.9), channel_id=1, source_target_pairs={{0,16},{2,18},{4,20},{6,22},{8,24},{10,26},{12,28},{14,30},{16,0},... | collective-permute-start | bytes 1376264 | tf_op jit(solution)/shard_map/ppermute | solution.py:335
  23.4 12.1 %collective-permute-start.2 = (bf16[128,1792]{1,0:T(8,128)(2,1)S(1)}, bf16[128,1792]{1,0:T(8,128)(2,1)S(1)}, u32[]{:S(2)}, u32[]{:S(2)}) collective-permute-start(bf16[128,1792]{1,0:T(8,128)(2,1)S(1)} %collective-permute-done.1), channel_id=1, source_target_pairs={{0,8},{2,10},{4,12},{6,14},{8,0},{10,2},{12,4},{14,6},{16,24},{18,... | collective-permute-start | bytes 1376264 | tf_op jit(solution)/shard_map/ppermute | solution.py:335
  26.9 2.0 copy-start.2
  28.9 2.0 copy-start.3
  32.7 2.8 copy-start
  35.5 6.4 %copy-start.12 = (bf16[128,1792]{1,0:T(8,128)(2,1)S(1)}, bf16[128,1792]{1,0:T(8,128)(2,1)}, u32[]{:S(2)}) copy-start(bf16[128,1792]{1,0:T(8,128)(2,1)} %param.9) | copy-start | bytes 1376260
  35.5 146.7 %all-to-all-start = ((bf16[16,1584,128]{2,1,0:T(8,128)(2,1)}), bf16[16,1584,128]{2,1,0:T(8,128)(2,1)}, u32[]{:S(2)}, u32[]{:S(2)}) async-start(bf16[16,1584,128]{2,1,0:T(8,128)(2,1)} %copy-done), calls=%async_computation | async-start | bytes 12976128 | tf_op jit(solution)/shard_map/all_to_all | solution.py:384
  42.2 52.8 %collective-permute-start.3 = (bf16[512,896]{1,0:T(8,128)(2,1)S(1)}, bf16[512,896]{1,0:T(8,128)(2,1)S(1)}, u32[]{:S(2)}, u32[]{:S(2)}) collective-permute-start(bf16[512,896]{1,0:T(8,128)(2,1)S(1)} %get-tuple-element.134), channel_id=1, source_target_pairs={{0,4},{2,6},{4,0},{6,2},{8,12},{10,14},{12,8},{14,10},{16,20},{18,... | collective-permute-start | bytes 2752520 | tf_op jit(solution)/shard_map/ppermute | solution.py:335
  42.8 52.8 %collective-permute-start.5 = (bf16[512,896]{1,0:T(8,128)(2,1)S(1)}, bf16[512,896]{1,0:T(8,128)(2,1)S(1)}, u32[]{:S(2)}, u32[]{:S(2)}) collective-permute-start(bf16[512,896]{1,0:T(8,128)(2,1)S(1)} %get-tuple-element.133), channel_id=1, source_target_pairs={{0,2},{2,0},{4,6},{6,4},{8,10},{10,8},{12,14},{14,12},{16,18},{18,... | collective-permute-start | bytes 2752520 | tf_op jit(solution)/shard_map/ppermute | solution.py:335
  95.2 4.3 %copy-start.11 = (bf16[1024,896]{1,0:T(8,128)(2,1)}, bf16[1024,896]{1,0:T(8,128)(2,1)S(1)}, u32[]{:S(2)}) copy-start(bf16[1024,896]{1,0:T(8,128)(2,1)S(1)} %pad_maximum_fusion.refs_0_) | copy-start | bytes 5505028
  95.2 63.3 %collective-permute-start.4 = (bf16[1024,896]{1,0:T(8,128)(2,1)S(1)}, bf16[1024,896]{1,0:T(8,128)(2,1)}, u32[]{:S(2)}, u32[]{:S(2)}) collective-permute-start(bf16[1024,896]{1,0:T(8,128)(2,1)S(1)} %pad_maximum_fusion.refs_0_), channel_id=1, source_target_pairs={{0,2},{2,0},{4,6},{6,4},{8,10},{10,8},{12,14},{14,12},{16,18},{18,... | collective-permute-start | bytes 5505032 | tf_op jit(solution)/shard_map/ppermute | solution.py:335
  97.0 67.0 %collective-permute-start.6 = (bf16[1024,896]{1,0:T(8,128)(2,1)}, bf16[1024,896]{1,0:T(8,128)(2,1)}, u32[]{:S(2)}, u32[]{:S(2)}) collective-permute-start(bf16[1024,896]{1,0:T(8,128)(2,1)} %pad_maximum_fusion.1.refs_2_), channel_id=1, source_target_pairs={{0,4},{2,6},{4,0},{6,2},{8,12},{10,14},{12,8},{14,10},{16,20},{18,... | collective-permute-start | bytes 5505032 | tf_op jit(solution)/shard_map/ppermute | solution.py:335
  99.5 106.5 %collective-permute-start.7 = (bf16[1024,896]{1,0:T(8,128)(2,1)S(1)}, bf16[1024,896]{1,0:T(8,128)(2,1)}, u32[]{:S(2)}, u32[]{:S(2)}) collective-permute-start(bf16[1024,896]{1,0:T(8,128)(2,1)S(1)} %pad_maximum_fusion.refs_0_), channel_id=1, source_target_pairs={{0,1},{1,0},{2,3},{3,2},{4,5},{5,4},{6,7},{7,6},{8,9},{9,8},{10,11... | collective-permute-start | bytes 5505032 | tf_op jit(solution)/shard_map/ppermute | solution.py:381
  99.5 106.5 %collective-permute-start.9 = (bf16[1024,896]{1,0:T(8,128)(2,1)}, bf16[1024,896]{1,0:T(8,128)(2,1)}, u32[]{:S(2)}, u32[]{:S(2)}) collective-permute-start(bf16[1024,896]{1,0:T(8,128)(2,1)} %pad_maximum_fusion.1.refs_2_), channel_id=1, source_target_pairs={{0,1},{1,0},{2,3},{3,2},{4,5},{5,4},{6,7},{7,6},{8,9},{9,8},{10,11... | collective-permute-start | bytes 5505032 | tf_op jit(solution)/shard_map/ppermute | solution.py:381
  158.5 47.5 %collective-permute-start.8 = (bf16[1024,896]{1,0:T(8,128)(2,1)}, bf16[1024,896]{1,0:T(8,128)(2,1)}, u32[]{:S(2)}, u32[]{:S(2)}) collective-permute-start(bf16[1024,896]{1,0:T(8,128)(2,1)} %collective-permute-done.4.refs_1_), channel_id=1, source_target_pairs={{0,1},{1,0},{2,3},{3,2},{4,5},{5,4},{6,7},{7,6},{8,9},{9,8},{10,11... | collective-permute-start | bytes 5505032 | tf_op jit(solution)/shard_map/ppermute | solution.py:381
  164.0 42.0 %collective-permute-start.10 = (bf16[1024,896]{1,0:T(8,128)(2,1)}, bf16[1024,896]{1,0:T(8,128)(2,1)}, u32[]{:S(2)}, u32[]{:S(2)}) collective-permute-start(bf16[1024,896]{1,0:T(8,128)(2,1)} %collective-permute-done.6.refs_3_), channel_id=1, source_target_pairs={{0,1},{1,0},{2,3},{3,2},{4,5},{5,4},{6,7},{7,6},{8,9},{9,8},{10,11... | collective-permute-start | bytes 5505032 | tf_op jit(solution)/shard_map/ppermute | solution.py:381
  164.0 2.0 copy-start.1
  182.2 66.3 %all-to-all-start.1 = ((bf16[16,448,128]{2,1,0:T(8,128)(2,1)}), bf16[16,448,128]{2,1,0:T(8,128)(2,1)}, u32[]{:S(2)}, u32[]{:S(2)}) async-start(bf16[16,448,128]{2,1,0:T(8,128)(2,1)} %get-tuple-element.71), calls=%async_computation.1 | async-start | bytes 3670016 | tf_op jit(solution)/shard_map/all_to_all | solution.py:384
  231.3 4.4 %collective-permute-start.11 = (bf16[2048,512]{1,0:T(8,128)(2,1)}, bf16[2048,512]{1,0:T(8,128)(2,1)S(1)}, u32[]{:S(2)}, u32[]{:S(2)}) collective-permute-start(bf16[2048,512]{1,0:T(8,128)(2,1)} %hidden.1.own_h), channel_id=1, source_target_pairs={{0,1},{1,0},{2,3},{3,2},{4,5},{5,4},{6,7},{7,6},{8,9},{9,8},{10,11... | collective-permute-start | bytes 6291464 | tf_op jit(solution)/shard_map/ppermute | solution.py:381
  235.6 22.4 %copy-start.8 = (bf16[2048,512]{1,0:T(8,128)(2,1)}, bf16[2048,512]{1,0:T(8,128)(2,1)S(1)}, u32[]{:S(2)}) copy-start(bf16[2048,512]{1,0:T(8,128)(2,1)S(1)} %collective-permute-done.11.other_h) | copy-start | bytes 6291460
  248.5 36.8 %all-to-all-start.2 = ((bf16[16,336,128]{2,1,0:T(8,128)(2,1)}), bf16[16,336,128]{2,1,0:T(8,128)(2,1)}, u32[]{:S(2)}, u32[]{:S(2)}) async-start(bf16[16,336,128]{2,1,0:T(8,128)(2,1)} %get-tuple-element.77), calls=%async_computation.2 | async-start | bytes 2752512 | tf_op jit(solution)/shard_map/all_to_all | solution.py:384
  253.8 4.3 %copy-start.6 = (bf16[2048,512]{1,0:T(8,128)(2,1)S(1)}, bf16[2048,512]{1,0:T(8,128)(2,1)}, u32[]{:S(2)}) copy-start(bf16[2048,512]{1,0:T(8,128)(2,1)} %hidden.1.own_h) | copy-start | bytes 6291460
  255.5 2.5 collective-permute-start.12
  261.7 34.6 %collective-permute-start.13 = (bf16[1024,512]{1,0:T(8,128)(2,1)}, bf16[1024,512]{1,0:T(8,128)(2,1)S(1)}, u32[]{:S(2)}, u32[]{:S(2)}) collective-permute-start(bf16[1024,512]{1,0:T(8,128)(2,1)} %get-tuple-element.90), channel_id=1, source_target_pairs={{0,2},{2,0},{4,6},{6,4},{8,10},{10,8},{12,14},{14,12},{16,18},{18,... | collective-permute-start | bytes 3145736 | tf_op jit(solution)/shard_map/ppermute | solution.py:335
  262.3 34.1 %collective-permute-start.14 = (bf16[1024,512]{1,0:T(8,128)(2,1)}, bf16[1024,512]{1,0:T(8,128)(2,1)}, u32[]{:S(2)}, u32[]{:S(2)}) collective-permute-start(bf16[1024,512]{1,0:T(8,128)(2,1)} %get-tuple-element.92), channel_id=1, source_target_pairs={{0,4},{2,6},{4,0},{6,2},{8,12},{10,14},{12,8},{14,10},{16,20},{18,... | collective-permute-start | bytes 3145736 | tf_op jit(solution)/shard_map/ppermute | solution.py:335
  262.8 1.6 copy-start.9
  267.0 1.3 copy-start.4
  285.3 11.1 %copy-start.5 = (f32[1024,512]{1,0:T(8,128)S(1)}, f32[1024,512]{1,0:T(8,128)}, u32[]{:S(2)}) copy-start(f32[1024,512]{1,0:T(8,128)} %copy-done.4) | copy-start | bytes 6291460
  286.9 13.5 %copy-start.7 = (bf16[2048,512]{1,0:T(8,128)(2,1)S(1)}, bf16[2048,512]{1,0:T(8,128)(2,1)}, u32[]{:S(2)}) copy-start(bf16[2048,512]{1,0:T(8,128)(2,1)} %hidden.1.own_h) | copy-start | bytes 6291460
  286.9 13.5 %copy-start.10 = (bf16[2048,512]{1,0:T(8,128)(2,1)S(1)}, bf16[2048,512]{1,0:T(8,128)(2,1)}, u32[]{:S(2)}) copy-start(bf16[2048,512]{1,0:T(8,128)(2,1)} %copy-done.8) | copy-start | bytes 6291460
  286.9 13.5 %collective-permute-start.20 = (bf16[8,336,128]{2,1,0:T(8,128)(2,1)S(1)}, bf16[8,336,128]{2,1,0:T(8,128)(2,1)S(1)}, u32[]{:S(2)}, u32[]{:S(2)}) collective-permute-start(bf16[8,336,128]{2,1,0:T(8,128)(2,1)S(1)} %get-tuple-element.135), channel_id=1, source_target_pairs={{0,1},{1,0},{2,3},{3,2},{4,5},{5,4},{6,7},{7,6},{8,9},{9,8},{10,11... | collective-permute-start | bytes 2064392 | tf_op jit(solution)/shard_map/ppermute | solution.py:381
  297.9 14.9 %collective-permute-start.15 = (bf16[512,512]{1,0:T(8,128)(2,1)S(1)}, bf16[512,512]{1,0:T(8,128)(2,1)S(1)}, u32[]{:S(2)}, u32[]{:S(2)}) collective-permute-start(bf16[512,512]{1,0:T(8,128)(2,1)S(1)} %get-tuple-element.94), channel_id=1, source_target_pairs={{0,4},{2,6},{4,0},{6,2},{8,12},{10,14},{12,8},{14,10},{16,20},{18,... | collective-permute-start | bytes 1572872 | tf_op jit(solution)/shard_map/ppermute | solution.py:335
  299.4 14.9 %collective-permute-start.16 = (bf16[512,512]{1,0:T(8,128)(2,1)S(1)}, bf16[512,512]{1,0:T(8,128)(2,1)S(1)}, u32[]{:S(2)}, u32[]{:S(2)}) collective-permute-start(bf16[512,512]{1,0:T(8,128)(2,1)S(1)} %get-tuple-element.96), channel_id=1, source_target_pairs={{0,2},{2,0},{4,6},{6,4},{8,10},{10,8},{12,14},{14,12},{16,18},{18,... | collective-permute-start | bytes 1572872 | tf_op jit(solution)/shard_map/ppermute | solution.py:335
  302.3 21.6 %collective-permute-start.21 = (bf16[1024,256]{1,0:T(8,128)(2,1)S(1)}, bf16[1024,256]{1,0:T(8,128)(2,1)S(1)}, u32[]{:S(2)}, u32[]{:S(2)}) collective-permute-start(bf16[1024,256]{1,0:T(8,128)(2,1)S(1)} %get-tuple-element.112), channel_id=1, source_target_pairs={{0,2},{2,0},{4,6},{6,4},{8,10},{10,8},{12,14},{14,12},{16,18},{18,... | collective-permute-start | bytes 1572872 | tf_op jit(solution)/shard_map/ppermute | solution.py:335
  303.4 20.5 %collective-permute-start.22 = (bf16[1024,256]{1,0:T(8,128)(2,1)S(1)}, bf16[1024,256]{1,0:T(8,128)(2,1)S(1)}, u32[]{:S(2)}, u32[]{:S(2)}) collective-permute-start(bf16[1024,256]{1,0:T(8,128)(2,1)S(1)} %get-tuple-element.114), channel_id=1, source_target_pairs={{0,4},{2,6},{4,0},{6,2},{8,12},{10,14},{12,8},{14,10},{16,20},{18,... | collective-permute-start | bytes 1572872 | tf_op jit(solution)/shard_map/ppermute | solution.py:335
  304.0 19.8 %collective-permute-start.23 = (bf16[1024,256]{1,0:T(8,128)(2,1)S(1)}, bf16[1024,256]{1,0:T(8,128)(2,1)S(1)}, u32[]{:S(2)}, u32[]{:S(2)}) collective-permute-start(bf16[1024,256]{1,0:T(8,128)(2,1)S(1)} %get-tuple-element.116), channel_id=1, source_target_pairs={{0,8},{2,10},{4,12},{6,14},{8,0},{10,2},{12,4},{14,6},{16,24},{18,... | collective-permute-start | bytes 1572872 | tf_op jit(solution)/shard_map/ppermute | solution.py:335
  314.4 11.9 %collective-permute-start.17 = (bf16[256,512]{1,0:T(8,128)(2,1)S(1)}, bf16[256,512]{1,0:T(8,128)(2,1)S(1)}, u32[]{:S(2)}, u32[]{:S(2)}) collective-permute-start(bf16[256,512]{1,0:T(8,128)(2,1)S(1)} %get-tuple-element.98), channel_id=1, source_target_pairs={{0,8},{2,10},{4,12},{6,14},{8,0},{10,2},{12,4},{14,6},{16,24},{18,... | collective-permute-start | bytes 786440 | tf_op jit(solution)/shard_map/ppermute | solution.py:335
  315.4 13.7 %collective-permute-start.18 = (bf16[256,512]{1,0:T(8,128)(2,1)S(1)}, bf16[256,512]{1,0:T(8,128)(2,1)S(1)}, u32[]{:S(2)}, u32[]{:S(2)}) collective-permute-start(bf16[256,512]{1,0:T(8,128)(2,1)S(1)} %get-tuple-element.100), channel_id=1, source_target_pairs={{0,8},{2,10},{4,12},{6,14},{8,0},{10,2},{12,4},{14,6},{16,24},{18,... | collective-permute-start | bytes 786440 | tf_op jit(solution)/shard_map/ppermute | solution.py:335
  324.1 10.3 %collective-permute-start.24 = (bf16[512,256]{1,0:T(8,128)(2,1)S(1)}, bf16[512,256]{1,0:T(8,128)(2,1)S(1)}, u32[]{:S(2)}, u32[]{:S(2)}) collective-permute-start(bf16[512,256]{1,0:T(8,128)(2,1)S(1)} %get-tuple-element.118), channel_id=1, source_target_pairs={{0,4},{2,6},{4,0},{6,2},{8,12},{10,14},{12,8},{14,10},{16,20},{18,... | collective-permute-start | bytes 786440 | tf_op jit(solution)/shard_map/ppermute | solution.py:335
  324.6 10.8 %collective-permute-start.25 = (bf16[512,256]{1,0:T(8,128)(2,1)S(1)}, bf16[512,256]{1,0:T(8,128)(2,1)S(1)}, u32[]{:S(2)}, u32[]{:S(2)}) collective-permute-start(bf16[512,256]{1,0:T(8,128)(2,1)S(1)} %get-tuple-element.120), channel_id=1, source_target_pairs={{0,8},{2,10},{4,12},{6,14},{8,0},{10,2},{12,4},{14,6},{16,24},{18,... | collective-permute-start | bytes 786440 | tf_op jit(solution)/shard_map/ppermute | solution.py:335
  325.7 9.6 %collective-permute-start.26 = (bf16[512,256]{1,0:T(8,128)(2,1)S(1)}, bf16[512,256]{1,0:T(8,128)(2,1)S(1)}, u32[]{:S(2)}, u32[]{:S(2)}) collective-permute-start(bf16[512,256]{1,0:T(8,128)(2,1)S(1)} %get-tuple-element.122), channel_id=1, source_target_pairs={{0,2},{2,0},{4,6},{6,4},{8,10},{10,8},{12,14},{14,12},{16,18},{18,... | collective-permute-start | bytes 786440 | tf_op jit(solution)/shard_map/ppermute | solution.py:335
  329.2 16.8 %collective-permute-start.19 = (bf16[128,1024]{1,0:T(8,128)(2,1)S(1)}, bf16[128,1024]{1,0:T(8,128)(2,1)S(1)}, u32[]{:S(2)}, u32[]{:S(2)}) collective-permute-start(bf16[128,1024]{1,0:T(8,128)(2,1)S(1)} %get-tuple-element.102), channel_id=1, source_target_pairs={{0,16},{2,18},{4,20},{6,22},{8,24},{10,26},{12,28},{14,30},{16,0},... | collective-permute-start | bytes 786440 | tf_op jit(solution)/shard_map/ppermute | solution.py:335
  335.5 6.2 %collective-permute-start.27 = (bf16[256,256]{1,0:T(8,128)(2,1)S(1)}, bf16[256,256]{1,0:T(8,128)(2,1)S(1)}, u32[]{:S(2)}, u32[]{:S(2)}) collective-permute-start(bf16[256,256]{1,0:T(8,128)(2,1)S(1)} %get-tuple-element.124), channel_id=1, source_target_pairs={{0,8},{2,10},{4,12},{6,14},{8,0},{10,2},{12,4},{14,6},{16,24},{18,... | collective-permute-start | bytes 393224 | tf_op jit(solution)/shard_map/ppermute | solution.py:335
  338.2 5.0 %collective-permute-start.28 = (bf16[256,256]{1,0:T(8,128)(2,1)S(1)}, bf16[256,256]{1,0:T(8,128)(2,1)S(1)}, u32[]{:S(2)}, u32[]{:S(2)}) collective-permute-start(bf16[256,256]{1,0:T(8,128)(2,1)S(1)} %get-tuple-element.126), channel_id=1, source_target_pairs={{0,2},{2,0},{4,6},{6,4},{8,10},{10,8},{12,14},{14,12},{16,18},{18,... | collective-permute-start | bytes 393224 | tf_op jit(solution)/shard_map/ppermute | solution.py:335
  338.4 5.0 %collective-permute-start.29 = (bf16[256,256]{1,0:T(8,128)(2,1)S(1)}, bf16[256,256]{1,0:T(8,128)(2,1)S(1)}, u32[]{:S(2)}, u32[]{:S(2)}) collective-permute-start(bf16[256,256]{1,0:T(8,128)(2,1)S(1)} %get-tuple-element.128), channel_id=1, source_target_pairs={{0,4},{2,6},{4,0},{6,2},{8,12},{10,14},{12,8},{14,10},{16,20},{18,... | collective-permute-start | bytes 393224 | tf_op jit(solution)/shard_map/ppermute | solution.py:335
  343.5 7.9 %collective-permute-start.30 = (bf16[128,768]{1,0:T(8,128)(2,1)S(1)}, bf16[128,768]{1,0:T(8,128)(2,1)S(1)}, u32[]{:S(2)}, u32[]{:S(2)}) collective-permute-start(bf16[128,768]{1,0:T(8,128)(2,1)S(1)} %get-tuple-element.130), channel_id=1, source_target_pairs={{0,16},{2,18},{4,20},{6,22},{8,24},{10,26},{12,28},{14,30},{16,0},... | collective-permute-start | bytes 589832 | tf_op jit(solution)/shard_map/ppermute | solution.py:335

commit v5 on v4

--- a/solution.py
+++ b/solution.py
@@ -59,7 +59,7 @@
     out_ref[dest, base + 3 * rows : base + 3 * rows + mid, :] = both.astype(out_ref.dtype)
 
 
-def pack_pair_kernel(list_ref, gate_ref, up_ref, share_ref, out_ref):
+def pack_first_kernel(rows, list_ref, gate_ref, up_ref, down_ref, share_ref, out_ref):
     slots, depth, width = gate_ref.shape
     size = depth * 7 // 2
     row = lax.broadcasted_iota(jnp.int32, share_ref.shape[1:], 0) // 4
@@ -69,6 +69,10 @@
                 lambda place, in_ref=in_ref: (in_ref, list_ref[place]),
                 out_ref, number * size, dest, 0, depth, width // LANES,
             )
+        pack_rows(
+            lambda place: (down_ref, list_ref[place]),
+            out_ref, 2 * size, dest, 0, rows, width // LANES,
+        )
         value = share_ref[dest]
         high = value.astype(out_ref.dtype)
         rest = value - high.astype(jnp.float32)
@@ -83,19 +87,16 @@
                 jnp.where(row == 2, low.astype(jnp.float32), 0.0),
             ),
         )
-        out_ref[dest, 2 * size :, :] = terms.astype(out_ref.dtype)
-
-
-def pack_kernel(parts, list_ref, in_ref, *out_refs):
-    slots, depth, width = in_ref.shape
-    for dest in range(out_refs[0].shape[0]):
-        lo = 0
-        for rows, out_ref in zip(parts, out_refs):
-            pack_rows(
-                lambda place: (in_ref, list_ref[place]),
-                out_ref, 0, dest, lo, rows, width // LANES,
-            )
-            lo += rows
+        out_ref[dest, 2 * size + rows * 7 // 2 :, :] = terms.astype(out_ref.dtype)
+
+
+def pack_rest_kernel(rows, list_ref, down_ref, out_ref):
+    slots, depth, width = down_ref.shape
+    for dest in range(out_ref.shape[0]):
+        pack_rows(
+            lambda place: (down_ref, list_ref[place]),
+            out_ref, 0, dest, rows, depth - rows, width // LANES,
+        )
 
 
 def vmem():
@@ -106,30 +107,30 @@
     return pl.BlockSpec(memory_space=pltpu.SMEM)
 
 
-def pack_pair(listing, gate_proj, up_proj, share, dests):
+def pack_first(listing, gate_proj, up_proj, down_proj, rows, share, dests):
     slots, depth, width = gate_proj.shape
-    shape = (dests, depth * 7 + share.shape[1], LANES)
+    shape = (dests, depth * 7 + rows * 7 // 2 + share.shape[1], LANES)
     return pl.pallas_call(
-        pack_pair_kernel,
+        functools.partial(pack_first_kernel, rows),
         out_shape=jax.ShapeDtypeStruct(shape, gate_proj.dtype),
-        in_specs=[smem(), vmem(), vmem(), vmem()],
+        in_specs=[smem(), vmem(), vmem(), vmem(), vmem()],
         out_specs=vmem(),
         compiler_params=pltpu.CompilerParams(vmem_limit_bytes=40 * MIB),
-        name="pack_gate_up",
-    )(listing, gate_proj, up_proj, share)
-
-
-def pack(listing, weights, dests, parts, name):
+        name="pack_first",
+    )(listing, gate_proj, up_proj, down_proj, share)
+
+
+def pack_rest(listing, down_proj, rows, dests):
+    slots, depth, width = down_proj.shape
+    shape = (dests, (depth - rows) * 7 // 2, LANES)
     return pl.pallas_call(
-        functools.partial(pack_kernel, parts),
-        out_shape=[
-            jax.ShapeDtypeStruct((dests, rows * 7 // 2, LANES), weights.dtype) for rows in parts
-        ],
+        functools.partial(pack_rest_kernel, rows),
+        out_shape=jax.ShapeDtypeStruct(shape, down_proj.dtype),
         in_specs=[smem(), vmem()],
-        out_specs=[vmem()] * len(parts),
+        out_specs=vmem(),
         compiler_params=pltpu.CompilerParams(vmem_limit_bytes=32 * MIB),
-        name=name,
-    )(listing, weights)
+        name="pack_rest",
+    )(listing, down_proj)
 
 
 def unpack_rows(in_ref, at, base, rows, out_ref, out_row, out_lane):
@@ -186,7 +187,7 @@
     for zh in range(2):
         source = me ^ (x + 2 * y + 4 * zl + 8 * zh)
         weight = lax.dot_general(
-            packed_ref[source, 2 * size :, :],
+            packed_ref[source, packed_ref.shape[1] - 16 :, :],
             chosen,
             (((0,), (0,)), ((), ())),
             preferred_element_type=jnp.float32,
@@ -225,7 +226,6 @@
     )(at, *pieces, packed)
 
 
-HALVES = ((0, 1, 2), (1, 0, 2))
 THIRDS = ((0, 1, 2), (1, 2, 0), (2, 0, 1))
 
 
@@ -394,7 +394,8 @@
 
     near, far = swap(tokens, 2), swap(tokens, 3)
     corner = swap(far, 2)
-    packed = pack_pair(listing, gate_proj, up_proj, share, devices)
+    parts = (128, 96)
+    packed = pack_first(listing, gate_proj, up_proj, down_proj, parts[0], share, devices)
     packed, near, far, corner = tie((packed, near, far, corner))
 
     moved = move(packed)
@@ -405,15 +406,14 @@
     second = jnp.concatenate([second, swap(second, 0)], axis=0)
     pieces = [first, swap(first, 0), second, swap(second, 1)]
     others = [exchange(piece) for piece in pieces]
-    parts = (128, 96)
-    down_packed = pack(listing, down_proj, devices, parts, "pack_down")
-    moved, down_packed = tie((moved, down_packed))
-
-    down0 = move(down_packed[0])
+    rest = pack_rest(listing, down_proj, parts[0], devices)
+    moved, rest = tie((moved, rest))
+
+    down1 = move(rest)
     at = jnp.stack([me, core]).astype(jnp.int32)
     hidden = hidden_units(at, pieces + others, moved)
     hidden_other = exchange(hidden)
-    down0, hidden, hidden_other, packed = tie((down0, hidden, hidden_other, down_packed[1]))
+    down0 = moved[:, depth * 7 : depth * 7 + parts[0] * 7 // 2]
 
     def products(down, rows_in, orders):
         own = lax.dynamic_slice_in_dim(down, core * group, group, 0)
@@ -422,7 +422,8 @@
         sent = down_product(*args, rows_in, 1, orders, jnp.bfloat16, "down_send")
         sent, args = tie((sent, args))
         come = [swap(value, order[0]) for value, order in zip(sent, orders)]
-        return down_product(*args, rows_in, 0, orders, jnp.float32, "down_keep"), come
+        kept = down_product(*args, rows_in, 0, orders, jnp.float32, "down_keep")
+        return kept, come, sent
 
     def stage(kept, come, number, orders):
         axes = tuple(stage_axis(order, number) for order in orders)
@@ -435,13 +436,13 @@
         come = swap(send, 3)
         return (keep + come.astype(jnp.float32)).astype(jnp.bfloat16)
 
-    down1 = move(packed)
-    kept0, come0 = products(down0, parts[0], HALVES)
+    kept0, come0, _ = products(down0, parts[0], THIRDS)
     down1, kept0 = tie((down1, kept0))
-    kept1, come1 = products(down1, parts[1], THIRDS)
-    kept0, come0 = stage(kept0, come0, 1, HALVES)
+    kept1, come1, sent1 = products(down1, parts[1], THIRDS)
+    kept0, _ = tie((kept0, sent1))
+    kept0, come0 = stage(kept0, come0, 1, THIRDS)
     kept1, come1 = stage(kept1, come1, 1, THIRDS)
-    kept0, come0 = stage(kept0, come0, 2, HALVES)
+    kept0, come0 = stage(kept0, come0, 2, THIRDS)
     kept1, come1 = stage(kept1, come1, 2, THIRDS)
     out = []
     for rows_in, total in zip(parts, (last_stage(kept0, come0), last_stage(kept1, come1))):

time: 357 us -> 359 us (level)
  starting transfers between devices: 66.5 us -> 49.5 us
  waiting for transfers between devices: 221 us -> 235 us
    ppermute x24 -> x27, waiting for transfers between devices: 171 us -> 198 us  [swap(): return lax.ppermute(value, 'ep', [(i, i ^ 1 << bit) for i in range(size)])]
    all_to_all x3 -> x2, starting transfers between devices: 35.4 us -> 17.5 us  [move(): return lax.all_to_all(packed, 'ep', 0, 0, tiled=True)]
    all_to_all x3 -> x2, waiting for transfers between devices: 42.7 us -> 33.9 us  [move(): return lax.all_to_all(packed, 'ep', 0, 0, tiled=True)]
    unnamed x29 -> x39, local copies, waits for them, and re-layouts: 11.9 us -> 15 us
    ppermute x24 -> x27, starting transfers between devices: 30.5 us -> 30.2 us  [swap(): return lax.ppermute(value, 'ep', [(i, i ^ 1 << bit) for i in range(size)])]
  transfers between devices with their start and end apart: 34 -> 36, of which waited for: 19 -> 21; matrix products, arithmetic and copies ran while one was open for 3% -> 2% of each run, Pallas kernels for 12% -> 12%
where the time goes in v5:
time: 359 us; the launch traced here: 355 us
  waiting for transfers between devices  235 us (65%)
  starting transfers between devices  49.5 us (14%)
  Pallas kernels  44 us (12%)
  local copies, waits for them, and re-layouts  19.8 us (6%)
  other arithmetic  6.13 us (2%)
    ppermute x27, waiting for transfers between devices, swap(): return lax.ppermute(value, 'ep', [(i, i ^ 1 << bit) for i in range(size)])  198 us
    all_to_all x2, waiting for transfers between devices, move(): return lax.all_to_all(packed, 'ep', 0, 0, tiled=True)  33.9 us
    ppermute x27, starting transfers between devices, swap(): return lax.ppermute(value, 'ep', [(i, i ^ 1 << bit) for i in range(size)])  30.2 us
    pallas_call x1, Pallas kernels, hidden_units(): pl.pallas_call(hidden_kernel, grid=(8,), out_shape=jax.ShapeDtypeStruct((...  25.8 us
    all_to_all x2, starting transfers between devices, move(): return lax.all_to_all(packed, 'ep', 0, 0, tiled=True)  17.5 us
    unnamed x39, local copies, waits for them, and re-layouts  15 us
    pallas_call x4, Pallas kernels, down_product(): pl.pallas_call(functools.partial(down_kernel, rows, side, orders), out_sh...  9.88 us
  transfers between devices with their start and end apart: 36, of which 21 were waited for; matrix products, arithmetic and copies ran while one was open for 2% of the time, Pallas kernels for 12%

profile of v5, /device:TPU:14, one launch (start us, length us, event | category | flops | bytes accessed | tf_op | source)
XLA Modules:
  0.0 355.2 jit_solution(16342574341288398111)
XLA Ops:
  0.5 2.6 collective-permute-start.1
  3.0 0.9 select_reduce_fusion.4
  4.3 0.7 select_reduce_fusion.1
  5.0 18.4 %collective-permute-done.1 = bf16[128,1792]{1,0:T(8,128)(2,1)S(1)} collective-permute-done((bf16[128,1792]{1,0:T(8,128)(2,1)}, bf16[128,1792]{1,0:T(8,128)(2,1)S(1)}, u32[]{:S(2)}, u32[]{:S(2)}) %collective-permute-start.1) | collective-permute-done | bytes 458784 | tf_op jit(solution)/shard_map/ppermute | solution.py:335
  23.4 1.6 collective-permute-start.2
  25.1 0.8 broadcast_compare_fusion
  25.9 0.9 select_reduce_fusion.share_ref
  26.9 2.0 copy-done
  28.9 2.0 copy-done.2
  30.9 2.0 copy-done.3
  33.0 5.4 %pack_first.1 = bf16[16,2032,128]{2,1,0:T(8,128)(2,1)} custom-call(s32[14]{0:T(128)S(1)} %select_reduce_fusion.3.list_ref, bf16[16,224,512]{2,1,0:T(8,128)(2,1)S(1)} %copy-done.2, bf16[16,224,512]{2,1,0:T(8,128)(2,1)S(1)} %copy-done.3, bf16[16,224,512]{2,1,0:T(8,128)(2,1)S(1)} %copy-done, f32[16,16,128]{2,1,0:T(8,128)S(1)} %select_reduce_fusion.share_ref), custom_call_target="tpu_custom_call" | custom-call | tf_op jit(solution)/shard_map/pack_first/pallas_call | solution.py:113
  38.4 6.3 %all-to-all-start = ((bf16[16,2032,128]{2,1,0:T(8,128)(2,1)}), bf16[16,2032,128]{2,1,0:T(8,128)(2,1)}, u32[]{:S(2)}, u32[]{:S(2)}) async-start(bf16[16,2032,128]{2,1,0:T(8,128)(2,1)} %pack_first.1), calls=%async_computation | async-start | bytes 16646144 | tf_op jit(solution)/shard_map/all_to_all | solution.py:384
  45.0 0.6 collective-permute-start.3
  45.7 0.6 collective-permute-start.5
  46.2 61.3 %collective-permute-done.3 = bf16[512,896]{1,0:T(8,128)(2,1)S(1)} collective-permute-done((bf16[512,896]{1,0:T(8,128)(2,1)S(1)}, bf16[512,896]{1,0:T(8,128)(2,1)S(1)}, u32[]{:S(2)}, u32[]{:S(2)}) %collective-permute-start.3) | collective-permute-done | bytes 917536 | tf_op jit(solution)/shard_map/ppermute | solution.py:335
  107.7 0.6 collective-permute-start.4
  108.4 1.4 pad_maximum_fusion.1.refs_2_
  110.3 76.7 %collective-permute-done.4.refs_1_ = bf16[1024,896]{1,0:T(8,128)(2,1)} collective-permute-done((bf16[1024,896]{1,0:T(8,128)(2,1)S(1)}, bf16[1024,896]{1,0:T(8,128)(2,1)}, u32[]{:S(2)}, u32[]{:S(2)}) %collective-permute-start.4) | collective-permute-done | bytes 1835040 | tf_op jit(solution)/shard_map/ppermute | solution.py:335
  187.5 2.0 copy-done.1
  189.6 1.9 pack_rest.1
  191.5 0.6 pad_add_fusion.at_ref
  192.1 33.9 %all-to-all-done.refs_8_ = bf16[16,2032,128]{2,1,0:T(8,128)(2,1)} async-done(((bf16[16,2032,128]{2,1,0:T(8,128)(2,1)}), bf16[16,2032,128]{2,1,0:T(8,128)(2,1)}, u32[]{:S(2)}, u32[]{:S(2)}) %all-to-all-start) | async-done | bytes 8323104 | tf_op jit(solution)/shard_map/all_to_all | solution.py:384
  226.0 11.2 %all-to-all-start.1 = ((bf16[16,336,128]{2,1,0:T(8,128)(2,1)}), bf16[16,336,128]{2,1,0:T(8,128)(2,1)}, u32[]{:S(2)}, u32[]{:S(2)}) async-start(bf16[16,336,128]{2,1,0:T(8,128)(2,1)} %pack_rest.1), calls=%async_computation.1 | async-start | bytes 2752512 | tf_op jit(solution)/shard_map/all_to_all | solution.py:384
  237.2 25.8 %hidden.1.own_h = bf16[2048,512]{1,0:T(8,128)(2,1)} custom-call(s32[2]{0:T(128)} %pad_add_fusion.at_ref, bf16[1024,896]{1,0:T(8,128)(2,1)} %copy-done.16, bf16[1024,896]{1,0:T(8,128)(2,1)} %collective-permute-done.4.refs_1_, bf16[1024,896]{1,0:T(8,128)(2,1)} %pad_maximum_fusion.1.refs_2_, bf16[1024,896]{1,0:T(8,128)(2,1)} %collective-permute-done.6.refs_3_, ...), custom_call_target="tpu_custom_call" | custom-call | flops 15032385536 | bytes 25165824 | tf_op jit(solution)/shard_map/hidden/pallas_call | solution.py:211
  262.9 1.6 slice.11
  265.3 3.1 collective-permute-done.12.other_ref
  268.4 3.0 down_send.2
  271.5 0.9 copy-done.12
  272.4 0.9 copy-done.13
  273.3 0.8 copy-done.14
  274.1 1.6 copy-done.9
  275.7 3.0 down_keep.2
  278.7 1.0 copy-done.4
  279.7 1.5 constant_dynamic-slice_fusion
  281.5 0.6 collective-permute-start.14
  282.0 0.6 collective-permute-start.15
  282.7 0.7 collective-permute-done.13.other_ref
  283.5 1.6 copy-done.10
  285.1 1.9 down_send.3
  287.0 9.2 %collective-permute-done.16.refs_5_ = bf16[1024,256]{1,0:T(8,128)(2,1)S(1)} collective-permute-done((bf16[1024,256]{1,0:T(8,128)(2,1)S(1)}, bf16[1024,256]{1,0:T(8,128)(2,1)S(1)}, u32[]{:S(2)}, u32[]{:S(2)}) %collective-permute-start.16) | collective-permute-done | bytes 524320 | tf_op jit(solution)/shard_map/ppermute | solution.py:335
  296.2 5.3 %collective-permute-done.14.refs_1_ = bf16[1024,384]{1,0:T(8,128)(2,1)S(1)} collective-permute-done((bf16[1024,384]{1,0:T(8,128)(2,1)}, bf16[1024,384]{1,0:T(8,128)(2,1)S(1)}, u32[]{:S(2)}, u32[]{:S(2)}) %collective-permute-start.14) | collective-permute-done | bytes 786464 | tf_op jit(solution)/shard_map/ppermute | solution.py:335
  302.1 1.5 collective-permute-start.19
  303.7 0.6 collective-permute-start.24
  305.1 1.7 collective-permute-start.25
  306.8 4.6 %collective-permute-done.19.refs_5_ = bf16[512,256]{1,0:T(8,128)(2,1)S(1)} collective-permute-done((bf16[512,256]{1,0:T(8,128)(2,1)S(1)}, bf16[512,256]{1,0:T(8,128)(2,1)S(1)}, u32[]{:S(2)}, u32[]{:S(2)}) %collective-permute-start.19) | collective-permute-done | bytes 262176 | tf_op jit(solution)/shard_map/ppermute | solution.py:335
  312.0 4.3 %collective-permute-done.17.refs_1_ = bf16[512,384]{1,0:T(8,128)(2,1)S(1)} collective-permute-done((bf16[512,384]{1,0:T(8,128)(2,1)S(1)}, bf16[512,384]{1,0:T(8,128)(2,1)S(1)}, u32[]{:S(2)}, u32[]{:S(2)}) %collective-permute-start.17) | collective-permute-done | bytes 393248 | tf_op jit(solution)/shard_map/ppermute | solution.py:335
  317.0 1.5 collective-permute-start.22
  319.1 1.8 collective-permute-done.24.refs_1_
  320.9 1.4 collective-permute-start.21
  322.4 1.9 down_keep.3
  324.3 3.0 collective-permute-done.25.refs_3_
  327.2 0.8 collective-permute-done.26.refs_5_
  328.3 1.6 collective-permute-start.27
  330.4 1.5 collective-permute-start.29
  331.9 0.9 collective-permute-done.20.refs_1_
  332.8 4.0 %collective-permute-start.23 = (bf16[128,1024]{1,0:T(8,128)(2,1)S(1)}, bf16[128,1024]{1,0:T(8,128)(2,1)S(1)}, u32[]{:S(2)}, u32[]{:S(2)}) collective-permute-start(bf16[128,1024]{1,0:T(8,128)(2,1)S(1)} %get-tuple-element.117), channel_id=1, source_target_pairs={{0,16},{2,18},{4,20},{6,22},{8,24},{10,26},{12,28},{14,30},{16,0},... | collective-permute-start | bytes 786440 | tf_op jit(solution)/shard_map/ppermute | solution.py:335
  336.8 1.9 collective-permute-done.28.refs_3_
  338.9 1.8 collective-permute-start.31
  340.7 1.1 collective-permute-start.32
  341.8 2.1 collective-permute-done.30.refs_1_
  344.0 1.7 collective-permute-done.32.refs_5_
  345.7 3.2 collective-permute-start.33
  349.2 4.8 %collective-permute-done.33 = bf16[128,768]{1,0:T(8,128)(2,1)S(1)} collective-permute-done((bf16[128,768]{1,0:T(8,128)(2,1)S(1)}, bf16[128,768]{1,0:T(8,128)(2,1)S(1)}, u32[]{:S(2)}, u32[]{:S(2)}) %collective-permute-start.33) | collective-permute-done | bytes 196640 | tf_op jit(solution)/shard_map/ppermute | solution.py:335
  354.2 1.0 copy.15
  (82 shorter events, 8.5 us)
Async XLA Ops:
  0.0 38.3 %collective-permute-start = (bf16[128,1792]{1,0:T(8,128)(2,1)}, bf16[128,1792]{1,0:T(8,128)(2,1)S(1)}, u32[]{:S(2)}, u32[]{:S(2)}) collective-permute-start(bf16[128,1792]{1,0:T(8,128)(2,1)} %param.9), channel_id=1, source_target_pairs={{0,8},{2,10},{4,12},{6,14},{8,0},{10,2},{12,4},{14,6},{16,24},{18,... | collective-permute-start | bytes 1376264 | tf_op jit(solution)/shard_map/ppermute | solution.py:335
  0.5 23.0 %collective-permute-start.1 = (bf16[128,1792]{1,0:T(8,128)(2,1)}, bf16[128,1792]{1,0:T(8,128)(2,1)S(1)}, u32[]{:S(2)}, u32[]{:S(2)}) collective-permute-start(bf16[128,1792]{1,0:T(8,128)(2,1)} %param.9), channel_id=1, source_target_pairs={{0,16},{2,18},{4,20},{6,22},{8,24},{10,26},{12,28},{14,30},{16,0},... | collective-permute-start | bytes 1376264 | tf_op jit(solution)/shard_map/ppermute | solution.py:335
  23.4 14.9 %collective-permute-start.2 = (bf16[128,1792]{1,0:T(8,128)(2,1)S(1)}, bf16[128,1792]{1,0:T(8,128)(2,1)S(1)}, u32[]{:S(2)}, u32[]{:S(2)}) collective-permute-start(bf16[128,1792]{1,0:T(8,128)(2,1)S(1)} %collective-permute-done.1), channel_id=1, source_target_pairs={{0,8},{2,10},{4,12},{6,14},{8,0},{10,2},{12,4},{14,6},{16,24},{18,... | collective-permute-start | bytes 1376264 | tf_op jit(solution)/shard_map/ppermute | solution.py:335
  26.9 2.0 copy-start
  28.9 2.0 copy-start.2
  30.9 2.0 copy-start.3
  38.3 6.4 %copy-start.17 = (bf16[128,1792]{1,0:T(8,128)(2,1)S(1)}, bf16[128,1792]{1,0:T(8,128)(2,1)}, u32[]{:S(2)}) copy-start(bf16[128,1792]{1,0:T(8,128)(2,1)} %param.9) | copy-start | bytes 1376260
  38.4 187.6 %all-to-all-start = ((bf16[16,2032,128]{2,1,0:T(8,128)(2,1)}), bf16[16,2032,128]{2,1,0:T(8,128)(2,1)}, u32[]{:S(2)}, u32[]{:S(2)}) async-start(bf16[16,2032,128]{2,1,0:T(8,128)(2,1)} %pack_first.1), calls=%async_computation | async-start | bytes 16646144 | tf_op jit(solution)/shard_map/all_to_all | solution.py:384
  45.0 62.5 %collective-permute-start.3 = (bf16[512,896]{1,0:T(8,128)(2,1)S(1)}, bf16[512,896]{1,0:T(8,128)(2,1)S(1)}, u32[]{:S(2)}, u32[]{:S(2)}) collective-permute-start(bf16[512,896]{1,0:T(8,128)(2,1)S(1)} %get-tuple-element.142), channel_id=1, source_target_pairs={{0,4},{2,6},{4,0},{6,2},{8,12},{10,14},{12,8},{14,10},{16,20},{18,... | collective-permute-start | bytes 2752520 | tf_op jit(solution)/shard_map/ppermute | solution.py:335
  45.7 62.7 %collective-permute-start.5 = (bf16[512,896]{1,0:T(8,128)(2,1)S(1)}, bf16[512,896]{1,0:T(8,128)(2,1)S(1)}, u32[]{:S(2)}, u32[]{:S(2)}) collective-permute-start(bf16[512,896]{1,0:T(8,128)(2,1)S(1)} %get-tuple-element.141), channel_id=1, source_target_pairs={{0,2},{2,0},{4,6},{6,4},{8,10},{10,8},{12,14},{14,12},{16,18},{18,... | collective-permute-start | bytes 2752520 | tf_op jit(solution)/shard_map/ppermute | solution.py:335
  107.7 2.0 copy-start.16
  107.7 79.3 %collective-permute-start.4 = (bf16[1024,896]{1,0:T(8,128)(2,1)S(1)}, bf16[1024,896]{1,0:T(8,128)(2,1)}, u32[]{:S(2)}, u32[]{:S(2)}) collective-permute-start(bf16[1024,896]{1,0:T(8,128)(2,1)S(1)} %pad_maximum_fusion.refs_0_), channel_id=1, source_target_pairs={{0,2},{2,0},{4,6},{6,4},{8,10},{10,8},{12,14},{14,12},{16,18},{18,... | collective-permute-start | bytes 5505032 | tf_op jit(solution)/shard_map/ppermute | solution.py:335
  109.8 77.3 %collective-permute-start.6 = (bf16[1024,896]{1,0:T(8,128)(2,1)}, bf16[1024,896]{1,0:T(8,128)(2,1)}, u32[]{:S(2)}, u32[]{:S(2)}) collective-permute-start(bf16[1024,896]{1,0:T(8,128)(2,1)} %pad_maximum_fusion.1.refs_2_), channel_id=1, source_target_pairs={{0,4},{2,6},{4,0},{6,2},{8,12},{10,14},{12,8},{14,10},{16,20},{18,... | collective-permute-start | bytes 5505032 | tf_op jit(solution)/shard_map/ppermute | solution.py:335
  109.8 127.4 %collective-permute-start.7 = (bf16[1024,896]{1,0:T(8,128)(2,1)S(1)}, bf16[1024,896]{1,0:T(8,128)(2,1)}, u32[]{:S(2)}, u32[]{:S(2)}) collective-permute-start(bf16[1024,896]{1,0:T(8,128)(2,1)S(1)} %pad_maximum_fusion.refs_0_), channel_id=1, source_target_pairs={{0,1},{1,0},{2,3},{3,2},{4,5},{5,4},{6,7},{7,6},{8,9},{9,8},{10,11... | collective-permute-start | bytes 5505032 | tf_op jit(solution)/shard_map/ppermute | solution.py:381
  109.8 127.4 %collective-permute-start.9 = (bf16[1024,896]{1,0:T(8,128)(2,1)}, bf16[1024,896]{1,0:T(8,128)(2,1)}, u32[]{:S(2)}, u32[]{:S(2)}) collective-permute-start(bf16[1024,896]{1,0:T(8,128)(2,1)} %pad_maximum_fusion.1.refs_2_), channel_id=1, source_target_pairs={{0,1},{1,0},{2,3},{3,2},{4,5},{5,4},{6,7},{7,6},{8,9},{9,8},{10,11... | collective-permute-start | bytes 5505032 | tf_op jit(solution)/shard_map/ppermute | solution.py:381
  187.0 50.2 %collective-permute-start.8 = (bf16[1024,896]{1,0:T(8,128)(2,1)}, bf16[1024,896]{1,0:T(8,128)(2,1)}, u32[]{:S(2)}, u32[]{:S(2)}) collective-permute-start(bf16[1024,896]{1,0:T(8,128)(2,1)} %collective-permute-done.4.refs_1_), channel_id=1, source_target_pairs={{0,1},{1,0},{2,3},{3,2},{4,5},{5,4},{6,7},{7,6},{8,9},{9,8},{10,11... | collective-permute-start | bytes 5505032 | tf_op jit(solution)/shard_map/ppermute | solution.py:381
  187.0 50.2 %collective-permute-start.10 = (bf16[1024,896]{1,0:T(8,128)(2,1)}, bf16[1024,896]{1,0:T(8,128)(2,1)}, u32[]{:S(2)}, u32[]{:S(2)}) collective-permute-start(bf16[1024,896]{1,0:T(8,128)(2,1)} %collective-permute-done.6.refs_3_), channel_id=1, source_target_pairs={{0,1},{1,0},{2,3},{3,2},{4,5},{5,4},{6,7},{7,6},{8,9},{9,8},{10,11... | collective-permute-start | bytes 5505032 | tf_op jit(solution)/shard_map/ppermute | solution.py:381
  187.5 2.0 copy-start.1
  226.0 53.7 %all-to-all-start.1 = ((bf16[16,336,128]{2,1,0:T(8,128)(2,1)}), bf16[16,336,128]{2,1,0:T(8,128)(2,1)}, u32[]{:S(2)}, u32[]{:S(2)}) async-start(bf16[16,336,128]{2,1,0:T(8,128)(2,1)} %pack_rest.1), calls=%async_computation.1 | async-start | bytes 2752512 | tf_op jit(solution)/shard_map/all_to_all | solution.py:384
  262.9 5.5 %collective-permute-start.11 = (bf16[2048,512]{1,0:T(8,128)(2,1)}, bf16[2048,512]{1,0:T(8,128)(2,1)S(1)}, u32[]{:S(2)}, u32[]{:S(2)}) collective-permute-start(bf16[2048,512]{1,0:T(8,128)(2,1)} %hidden.1.own_h), channel_id=1, source_target_pairs={{0,1},{1,0},{2,3},{3,2},{4,5},{5,4},{6,7},{7,6},{8,9},{9,8},{10,11... | collective-permute-start | bytes 6291464 | tf_op jit(solution)/shard_map/ppermute | solution.py:381
  264.6 3.8 %copy-start.6 = (bf16[2048,512]{1,0:T(8,128)(2,1)S(1)}, bf16[2048,512]{1,0:T(8,128)(2,1)}, u32[]{:S(2)}) copy-start(bf16[2048,512]{1,0:T(8,128)(2,1)} %hidden.1.own_h) | copy-start | bytes 6291460
  264.7 3.7 %collective-permute-start.12 = (bf16[8,448,128]{2,1,0:T(8,128)(2,1)S(1)}, bf16[8,448,128]{2,1,0:T(8,128)(2,1)S(1)}, u32[]{:S(2)}, u32[]{:S(2)}) collective-permute-start(bf16[8,448,128]{2,1,0:T(8,128)(2,1)S(1)} %get-tuple-element.139), channel_id=1, source_target_pairs={{0,1},{1,0},{2,3},{3,2},{4,5},{5,4},{6,7},{7,6},{8,9},{9,8},{10,11... | collective-permute-start | bytes 2752520 | tf_op jit(solution)/shard_map/ppermute | solution.py:381
  268.4 3.0 copy-start.8
  271.5 0.9 copy-start.12
  272.4 0.9 copy-start.13
  273.3 0.8 copy-start.14
  274.1 1.6 copy-start.9
  278.7 1.0 copy-start.4
  279.7 2.9 copy-start.15
  279.7 3.8 %copy-start.7 = (bf16[2048,512]{1,0:T(8,128)(2,1)S(1)}, bf16[2048,512]{1,0:T(8,128)(2,1)}, u32[]{:S(2)}) copy-start(bf16[2048,512]{1,0:T(8,128)(2,1)} %hidden.1.own_h) | copy-start | bytes 6291460
  281.3 2.2 collective-permute-start.13
  281.5 20.0 %collective-permute-start.14 = (bf16[1024,384]{1,0:T(8,128)(2,1)}, bf16[1024,384]{1,0:T(8,128)(2,1)S(1)}, u32[]{:S(2)}, u32[]{:S(2)}) collective-permute-start(bf16[1024,384]{1,0:T(8,128)(2,1)} %copy-done.13), channel_id=1, source_target_pairs={{0,2},{2,0},{4,6},{6,4},{8,10},{10,8},{12,14},{14,12},{16,18},{18,... | collective-permute-start | bytes 2359304 | tf_op jit(solution)/shard_map/ppermute | solution.py:335
  282.0 19.7 %collective-permute-start.15 = (bf16[1024,384]{1,0:T(8,128)(2,1)}, bf16[1024,384]{1,0:T(8,128)(2,1)S(1)}, u32[]{:S(2)}, u32[]{:S(2)}) collective-permute-start(bf16[1024,384]{1,0:T(8,128)(2,1)} %copy-done.12), channel_id=1, source_target_pairs={{0,4},{2,6},{4,0},{6,2},{8,12},{10,14},{12,8},{14,10},{16,20},{18,... | collective-permute-start | bytes 2359304 | tf_op jit(solution)/shard_map/ppermute | solution.py:335
  282.6 13.6 %collective-permute-start.16 = (bf16[1024,256]{1,0:T(8,128)(2,1)S(1)}, bf16[1024,256]{1,0:T(8,128)(2,1)S(1)}, u32[]{:S(2)}, u32[]{:S(2)}) collective-permute-start(bf16[1024,256]{1,0:T(8,128)(2,1)S(1)} %copy-done.15), channel_id=1, source_target_pairs={{0,8},{2,10},{4,12},{6,14},{8,0},{10,2},{12,4},{14,6},{16,24},{18,... | collective-permute-start | bytes 1572872 | tf_op jit(solution)/shard_map/ppermute | solution.py:335
  283.5 1.6 copy-start.10
  285.1 16.7 %copy-start.5 = (f32[1024,256]{1,0:T(8,128)S(1)}, f32[1024,256]{1,0:T(8,128)}, u32[]{:S(2)}) copy-start(f32[1024,256]{1,0:T(8,128)} %copy-done.4) | copy-start | bytes 3145732
  302.1 20.2 %copy-start.11 = (bf16[2048,512]{1,0:T(8,128)(2,1)S(1)}, bf16[2048,512]{1,0:T(8,128)(2,1)}, u32[]{:S(2)}) copy-start(bf16[2048,512]{1,0:T(8,128)(2,1)} %copy-done.8) | copy-start | bytes 6291460
  302.1 9.3 %collective-permute-start.19 = (bf16[512,256]{1,0:T(8,128)(2,1)S(1)}, bf16[512,256]{1,0:T(8,128)(2,1)S(1)}, u32[]{:S(2)}, u32[]{:S(2)}) collective-permute-start(bf16[512,256]{1,0:T(8,128)(2,1)S(1)} %get-tuple-element.109), channel_id=1, source_target_pairs={{0,2},{2,0},{4,6},{6,4},{8,10},{10,8},{12,14},{14,12},{16,18},{18,... | collective-permute-start | bytes 786440 | tf_op jit(solution)/shard_map/ppermute | solution.py:335
  303.7 17.3 %collective-permute-start.24 = (bf16[1024,256]{1,0:T(8,128)(2,1)S(1)}, bf16[1024,256]{1,0:T(8,128)(2,1)S(1)}, u32[]{:S(2)}, u32[]{:S(2)}) collective-permute-start(bf16[1024,256]{1,0:T(8,128)(2,1)S(1)} %get-tuple-element.95), channel_id=1, source_target_pairs={{0,2},{2,0},{4,6},{6,4},{8,10},{10,8},{12,14},{14,12},{16,18},{18,... | collective-permute-start | bytes 1572872 | tf_op jit(solution)/shard_map/ppermute | solution.py:335
  304.2 12.1 %collective-permute-start.17 = (bf16[512,384]{1,0:T(8,128)(2,1)S(1)}, bf16[512,384]{1,0:T(8,128)(2,1)S(1)}, u32[]{:S(2)}, u32[]{:S(2)}) collective-permute-start(bf16[512,384]{1,0:T(8,128)(2,1)S(1)} %get-tuple-element.105), channel_id=1, source_target_pairs={{0,4},{2,6},{4,0},{6,2},{8,12},{10,14},{12,8},{14,10},{16,20},{18,... | collective-permute-start | bytes 1179656 | tf_op jit(solution)/shard_map/ppermute | solution.py:335
  304.8 12.1 %collective-permute-start.18 = (bf16[512,384]{1,0:T(8,128)(2,1)S(1)}, bf16[512,384]{1,0:T(8,128)(2,1)S(1)}, u32[]{:S(2)}, u32[]{:S(2)}) collective-permute-start(bf16[512,384]{1,0:T(8,128)(2,1)S(1)} %get-tuple-element.107), channel_id=1, source_target_pairs={{0,8},{2,10},{4,12},{6,14},{8,0},{10,2},{12,4},{14,6},{16,24},{18,... | collective-permute-start | bytes 1179656 | tf_op jit(solution)/shard_map/ppermute | solution.py:335
  305.1 22.2 %collective-permute-start.25 = (bf16[1024,256]{1,0:T(8,128)(2,1)S(1)}, bf16[1024,256]{1,0:T(8,128)(2,1)S(1)}, u32[]{:S(2)}, u32[]{:S(2)}) collective-permute-start(bf16[1024,256]{1,0:T(8,128)(2,1)S(1)} %get-tuple-element.96), channel_id=1, source_target_pairs={{0,4},{2,6},{4,0},{6,2},{8,12},{10,14},{12,8},{14,10},{16,20},{18,... | collective-permute-start | bytes 1572872 | tf_op jit(solution)/shard_map/ppermute | solution.py:335
  311.4 16.6 %collective-permute-start.26 = (bf16[1024,256]{1,0:T(8,128)(2,1)S(1)}, bf16[1024,256]{1,0:T(8,128)(2,1)S(1)}, u32[]{:S(2)}, u32[]{:S(2)}) collective-permute-start(bf16[1024,256]{1,0:T(8,128)(2,1)S(1)} %get-tuple-element.97), channel_id=1, source_target_pairs={{0,8},{2,10},{4,12},{6,14},{8,0},{10,2},{12,4},{14,6},{16,24},{18,... | collective-permute-start | bytes 1572872 | tf_op jit(solution)/shard_map/ppermute | solution.py:335
  317.0 13.4 %collective-permute-start.22 = (bf16[256,256]{1,0:T(8,128)(2,1)S(1)}, bf16[256,256]{1,0:T(8,128)(2,1)S(1)}, u32[]{:S(2)}, u32[]{:S(2)}) collective-permute-start(bf16[256,256]{1,0:T(8,128)(2,1)S(1)} %get-tuple-element.115), channel_id=1, source_target_pairs={{0,4},{2,6},{4,0},{6,2},{8,12},{10,14},{12,8},{14,10},{16,20},{18,... | collective-permute-start | bytes 393224 | tf_op jit(solution)/shard_map/ppermute | solution.py:335
  318.5 14.2 %collective-permute-start.20 = (bf16[256,384]{1,0:T(8,128)(2,1)S(1)}, bf16[256,384]{1,0:T(8,128)(2,1)S(1)}, u32[]{:S(2)}, u32[]{:S(2)}) collective-permute-start(bf16[256,384]{1,0:T(8,128)(2,1)S(1)} %get-tuple-element.111), channel_id=1, source_target_pairs={{0,8},{2,10},{4,12},{6,14},{8,0},{10,2},{12,4},{14,6},{16,24},{18,... | collective-permute-start | bytes 589832 | tf_op jit(solution)/shard_map/ppermute | solution.py:335
  320.9 11.8 %collective-permute-start.21 = (bf16[256,384]{1,0:T(8,128)(2,1)S(1)}, bf16[256,384]{1,0:T(8,128)(2,1)S(1)}, u32[]{:S(2)}, u32[]{:S(2)}) collective-permute-start(bf16[256,384]{1,0:T(8,128)(2,1)S(1)} %get-tuple-element.113), channel_id=1, source_target_pairs={{0,2},{2,0},{4,6},{6,4},{8,10},{10,8},{12,14},{14,12},{16,18},{18,... | collective-permute-start | bytes 589832 | tf_op jit(solution)/shard_map/ppermute | solution.py:335
  328.3 8.6 %collective-permute-start.27 = (bf16[512,256]{1,0:T(8,128)(2,1)S(1)}, bf16[512,256]{1,0:T(8,128)(2,1)S(1)}, u32[]{:S(2)}, u32[]{:S(2)}) collective-permute-start(bf16[512,256]{1,0:T(8,128)(2,1)S(1)} %get-tuple-element.126), channel_id=1, source_target_pairs={{0,4},{2,6},{4,0},{6,2},{8,12},{10,14},{12,8},{14,10},{16,20},{18,... | collective-permute-start | bytes 786440 | tf_op jit(solution)/shard_map/ppermute | solution.py:335
  329.9 8.9 %collective-permute-start.28 = (bf16[512,256]{1,0:T(8,128)(2,1)S(1)}, bf16[512,256]{1,0:T(8,128)(2,1)S(1)}, u32[]{:S(2)}, u32[]{:S(2)}) collective-permute-start(bf16[512,256]{1,0:T(8,128)(2,1)S(1)} %get-tuple-element.128), channel_id=1, source_target_pairs={{0,8},{2,10},{4,12},{6,14},{8,0},{10,2},{12,4},{14,6},{16,24},{18,... | collective-permute-start | bytes 786440 | tf_op jit(solution)/shard_map/ppermute | solution.py:335
  330.4 8.3 %collective-permute-start.29 = (bf16[512,256]{1,0:T(8,128)(2,1)S(1)}, bf16[512,256]{1,0:T(8,128)(2,1)S(1)}, u32[]{:S(2)}, u32[]{:S(2)}) collective-permute-start(bf16[512,256]{1,0:T(8,128)(2,1)S(1)} %get-tuple-element.130), channel_id=1, source_target_pairs={{0,2},{2,0},{4,6},{6,4},{8,10},{10,8},{12,14},{14,12},{16,18},{18,... | collective-permute-start | bytes 786440 | tf_op jit(solution)/shard_map/ppermute | solution.py:335
  332.8 16.1 %collective-permute-start.23 = (bf16[128,1024]{1,0:T(8,128)(2,1)S(1)}, bf16[128,1024]{1,0:T(8,128)(2,1)S(1)}, u32[]{:S(2)}, u32[]{:S(2)}) collective-permute-start(bf16[128,1024]{1,0:T(8,128)(2,1)S(1)} %get-tuple-element.117), channel_id=1, source_target_pairs={{0,16},{2,18},{4,20},{6,22},{8,24},{10,26},{12,28},{14,30},{16,0},... | collective-permute-start | bytes 786440 | tf_op jit(solution)/shard_map/ppermute | solution.py:335
  338.9 5.0 %collective-permute-start.30 = (bf16[256,256]{1,0:T(8,128)(2,1)S(1)}, bf16[256,256]{1,0:T(8,128)(2,1)S(1)}, u32[]{:S(2)}, u32[]{:S(2)}) collective-permute-start(bf16[256,256]{1,0:T(8,128)(2,1)S(1)} %get-tuple-element.132), channel_id=1, source_target_pairs={{0,8},{2,10},{4,12},{6,14},{8,0},{10,2},{12,4},{14,6},{16,24},{18,... | collective-permute-start | bytes 393224 | tf_op jit(solution)/shard_map/ppermute | solution.py:335
  338.9 5.0 %collective-permute-start.31 = (bf16[256,256]{1,0:T(8,128)(2,1)S(1)}, bf16[256,256]{1,0:T(8,128)(2,1)S(1)}, u32[]{:S(2)}, u32[]{:S(2)}) collective-permute-start(bf16[256,256]{1,0:T(8,128)(2,1)S(1)} %get-tuple-element.134), channel_id=1, source_target_pairs={{0,2},{2,0},{4,6},{6,4},{8,10},{10,8},{12,14},{14,12},{16,18},{18,... | collective-permute-start | bytes 393224 | tf_op jit(solution)/shard_map/ppermute | solution.py:335
  340.7 5.0 %collective-permute-start.32 = (bf16[256,256]{1,0:T(8,128)(2,1)S(1)}, bf16[256,256]{1,0:T(8,128)(2,1)S(1)}, u32[]{:S(2)}, u32[]{:S(2)}) collective-permute-start(bf16[256,256]{1,0:T(8,128)(2,1)S(1)} %get-tuple-element.136), channel_id=1, source_target_pairs={{0,4},{2,6},{4,0},{6,2},{8,12},{10,14},{12,8},{14,10},{16,20},{18,... | collective-permute-start | bytes 393224 | tf_op jit(solution)/shard_map/ppermute | solution.py:335
  345.7 8.3 %collective-permute-start.33 = (bf16[128,768]{1,0:T(8,128)(2,1)S(1)}, bf16[128,768]{1,0:T(8,128)(2,1)S(1)}, u32[]{:S(2)}, u32[]{:S(2)}) collective-permute-start(bf16[128,768]{1,0:T(8,128)(2,1)S(1)} %get-tuple-element.138), channel_id=1, source_target_pairs={{0,16},{2,18},{4,20},{6,22},{8,24},{10,26},{12,28},{14,30},{16,0},... | collective-permute-start | bytes 589832 | tf_op jit(solution)/shard_map/ppermute | solution.py:335

commit v6 on v5

--- a/solution.py
+++ b/solution.py
@@ -59,19 +59,14 @@
     out_ref[dest, base + 3 * rows : base + 3 * rows + mid, :] = both.astype(out_ref.dtype)
 
 
-def pack_first_kernel(rows, list_ref, gate_ref, up_ref, down_ref, share_ref, out_ref):
+def pack_gate_kernel(list_ref, gate_ref, share_ref, out_ref):
     slots, depth, width = gate_ref.shape
     size = depth * 7 // 2
     row = lax.broadcasted_iota(jnp.int32, share_ref.shape[1:], 0) // 4
     for dest in range(out_ref.shape[0]):
-        for number, in_ref in enumerate((gate_ref, up_ref)):
-            pack_rows(
-                lambda place, in_ref=in_ref: (in_ref, list_ref[place]),
-                out_ref, number * size, dest, 0, depth, width // LANES,
-            )
         pack_rows(
-            lambda place: (down_ref, list_ref[place]),
-            out_ref, 2 * size, dest, 0, rows, width // LANES,
+            lambda place: (gate_ref, list_ref[place]),
+            out_ref, 0, dest, 0, depth, width // LANES,
         )
         value = share_ref[dest]
         high = value.astype(out_ref.dtype)
@@ -87,7 +82,20 @@
                 jnp.where(row == 2, low.astype(jnp.float32), 0.0),
             ),
         )
-        out_ref[dest, 2 * size + rows * 7 // 2 :, :] = terms.astype(out_ref.dtype)
+        out_ref[dest, size:, :] = terms.astype(out_ref.dtype)
+
+
+def pack_up_kernel(rows, list_ref, up_ref, down_ref, out_ref):
+    slots, depth, width = up_ref.shape
+    for dest in range(out_ref.shape[0]):
+        pack_rows(
+            lambda place: (up_ref, list_ref[place]),
+            out_ref, 0, dest, 0, depth, width // LANES,
+        )
+        pack_rows(
+            lambda place: (down_ref, list_ref[place]),
+            out_ref, depth * 7 // 2, dest, 0, rows, width // LANES,
+        )
 
 
 def pack_rest_kernel(rows, list_ref, down_ref, out_ref):
@@ -107,17 +115,30 @@
     return pl.BlockSpec(memory_space=pltpu.SMEM)
 
 
-def pack_first(listing, gate_proj, up_proj, down_proj, rows, share, dests):
+def pack_gate(listing, gate_proj, share, dests):
     slots, depth, width = gate_proj.shape
-    shape = (dests, depth * 7 + rows * 7 // 2 + share.shape[1], LANES)
+    shape = (dests, depth * 7 // 2 + share.shape[1], LANES)
     return pl.pallas_call(
-        functools.partial(pack_first_kernel, rows),
+        pack_gate_kernel,
         out_shape=jax.ShapeDtypeStruct(shape, gate_proj.dtype),
-        in_specs=[smem(), vmem(), vmem(), vmem(), vmem()],
+        in_specs=[smem(), vmem(), vmem()],
+        out_specs=vmem(),
+        compiler_params=pltpu.CompilerParams(vmem_limit_bytes=32 * MIB),
+        name="pack_gate",
+    )(listing, gate_proj, share)
+
+
+def pack_up(listing, up_proj, down_proj, rows, dests):
+    slots, depth, width = up_proj.shape
+    shape = (dests, (depth + rows) * 7 // 2, LANES)
+    return pl.pallas_call(
+        functools.partial(pack_up_kernel, rows),
+        out_shape=jax.ShapeDtypeStruct(shape, up_proj.dtype),
+        in_specs=[smem(), vmem(), vmem()],
         out_specs=vmem(),
         compiler_params=pltpu.CompilerParams(vmem_limit_bytes=40 * MIB),
-        name="pack_first",
-    )(listing, gate_proj, up_proj, down_proj, share)
+        name="pack_up",
+    )(listing, up_proj, down_proj)
 
 
 def pack_rest(listing, down_proj, rows, dests):
@@ -147,22 +168,18 @@
     ).astype(out_ref.dtype)
 
 
-def hidden_kernel(at_ref, *refs):
-    pieces, (packed_ref, out_ref, gate_w, up_w, rows) = refs[:8], refs[8:]
+def input_product(at_ref, pieces, packed_ref, weights, rows):
     sources = packed_ref.shape[0]
-    depth = gate_w.shape[0] // sources
-    size = depth * 7 // 2
+    depth = weights.shape[0] // sources
     group = sources // 2
     tile = pl.program_id(0)
-    x, y, zl = tile // 4, tile // 2 % 2, tile % 2
-    me, core = at_ref[0], at_ref[1]
+    x, y = tile // 4, tile // 2 % 2
 
     @pl.when(tile == 0)
     def _():
         for at in range(sources):
-            place = (core + at // group) % 2 * group + at % group
-            unpack_rows(packed_ref, place, 0, depth, gate_w, at * depth, 0)
-            unpack_rows(packed_ref, place, size, depth, up_w, at * depth, 0)
+            place = (at_ref[1] + at // group) % 2 * group + at % group
+            unpack_rows(packed_ref, place, 0, depth, weights, at * depth, 0)
 
     mid = pieces[0].shape[1]
     for number in range(4):
@@ -174,10 +191,22 @@
             def _():
                 rows[:, lanes] = pieces[2 * number + value][...]
 
-    gate = jnp.dot(rows[...], gate_w[...], preferred_element_type=jnp.float32)
-    up = jnp.dot(rows[...], up_w[...], preferred_element_type=jnp.float32)
+    return jnp.dot(rows[...], weights[...], preferred_element_type=jnp.float32)
+
+
+def gate_kernel(at_ref, *refs):
+    pieces, (packed_ref, out_ref, weights, rows) = refs[:8], refs[8:]
+    out_ref[...] = input_product(at_ref, pieces, packed_ref, weights, rows)
+
+
+def hidden_kernel(at_ref, *refs):
+    pieces, (packed_ref, gate_ref, terms_ref, out_ref, weights, rows) = refs[:8], refs[8:]
+    up = input_product(at_ref, pieces, packed_ref, weights, rows)
+    gate = gate_ref[...]
     value = gate / (1.0 + jnp.exp(-gate)) * up
 
+    tile = pl.program_id(0)
+    x, y, zl = tile // 4, tile // 2 % 2, tile % 2
     wide = gate.shape[1]
     term = lax.broadcasted_iota(jnp.int32, (16, wide), 0)
     lane = lax.broadcasted_iota(jnp.int32, (16, wide), 1)
@@ -185,18 +214,15 @@
     chosen = jnp.where(chosen, 1.0, 0.0).astype(jnp.bfloat16)
     block = rows.shape[0] // 2
     for zh in range(2):
-        source = me ^ (x + 2 * y + 4 * zl + 8 * zh)
+        source = at_ref[0] ^ (x + 2 * y + 4 * zl + 8 * zh)
         weight = lax.dot_general(
-            packed_ref[source, packed_ref.shape[1] - 16 :, :],
-            chosen,
-            (((0,), (0,)), ((), ())),
-            preferred_element_type=jnp.float32,
+            terms_ref[source], chosen, (((0,), (0,)), ((), ())), preferred_element_type=jnp.float32
         )
         span = slice(zh * block, (zh + 1) * block)
         out_ref[span, :] = (value[span, :] * weight).astype(out_ref.dtype)
 
 
-def hidden_units(at, pieces, packed):
+def input_call(kernel, at, pieces, packed, more, dtype, name):
     total = 2 * pieces[0].shape[0]
     mid = pieces[0].shape[1]
     tile = total // 8
@@ -208,22 +234,28 @@
         lambda i: (i // 4 * 2 + jnp.where(i // 2 % 2 == 1, i % 2, 0), 0),
     ]
     maps = (by_x + by_y) * 2
+    tokens_spec = pl.BlockSpec((tile, wide), lambda i: (i, 0))
     return pl.pallas_call(
-        hidden_kernel,
+        kernel,
         grid=(8,),
-        out_shape=jax.ShapeDtypeStruct((total, wide), packed.dtype),
+        out_shape=jax.ShapeDtypeStruct((total, wide), dtype),
         in_specs=[smem()]
         + [pl.BlockSpec((tile, mid), where) for where in maps]
-        + [vmem()],
-        out_specs=pl.BlockSpec((tile, wide), lambda i: (i, 0)),
-        scratch_shapes=[pltpu.VMEM((model, wide), packed.dtype)] * 2
-        + [pltpu.VMEM((tile, model), packed.dtype)],
+        + [vmem()]
+        + [tokens_spec, vmem()][: len(more)],
+        out_specs=tokens_spec,
+        scratch_shapes=[
+            pltpu.VMEM((model, wide), packed.dtype),
+            pltpu.VMEM((tile, model), packed.dtype),
+        ],
         compiler_params=pltpu.CompilerParams(vmem_limit_bytes=56 * MIB),
         cost_estimate=pl.CostEstimate(
-            flops=4 * total * model * wide, bytes_accessed=24 * MIB, transcendentals=total * wide
+            flops=2 * total * model * wide,
+            bytes_accessed=20 * MIB,
+            transcendentals=total * wide * len(more) // 2,
         ),
-        name="hidden",
-    )(at, *pieces, packed)
+        name=name,
+    )(at, *pieces, packed, *more)
 
 
 THIRDS = ((0, 1, 2), (1, 2, 0), (2, 0, 1))
@@ -392,28 +424,46 @@
     belongs = slot_place[None, None, :, None] == places[:, :, None, None]
     share = jnp.sum(jnp.where(belongs, share[None, None], 0.0), axis=2)
 
+    parts = (128, 96)
+    at = jnp.stack([me, core]).astype(jnp.int32)
+    size = depth * 7 // 2
+
     near, far = swap(tokens, 2), swap(tokens, 3)
+    gate_packed = pack_gate(listing, gate_proj, share, devices)
+    moved = move(gate_packed)
     corner = swap(far, 2)
-    parts = (128, 96)
-    packed = pack_first(listing, gate_proj, up_proj, down_proj, parts[0], share, devices)
-    packed, near, far, corner = tie((packed, near, far, corner))
-
-    moved = move(packed)
     mid = tokens.shape[1] // 2
-    rows = jnp.concatenate([tokens, far, near, corner], axis=0)
-    first, second = rows[:, :mid], rows[:, mid:]
-    first = jnp.concatenate([first, swap(first, 1)], axis=0)
-    second = jnp.concatenate([second, swap(second, 0)], axis=0)
-    pieces = [first, swap(first, 0), second, swap(second, 1)]
-    others = [exchange(piece) for piece in pieces]
+    three = jnp.concatenate([tokens, far, near], axis=0)
+    first, second = three[:, :mid], three[:, mid:]
+    first_y, second_x = swap(first, 1), swap(second, 0)
+    up_packed = pack_up(listing, up_proj, down_proj, parts[0], devices)
+    moved, first, second, first_y, second_x, corner, up_packed = tie(
+        (moved, first, second, first_y, second_x, corner, up_packed)
+    )
+    gate_moved, terms = moved[:, :size], moved[:, size:]
+
+    moved = move(up_packed)
+    first_c, second_c = corner[:, :mid], corner[:, mid:]
+    first_most = jnp.concatenate([first, first_c, first_y], axis=0)
+    second_most = jnp.concatenate([second, second_c, second_x], axis=0)
+    cross = lax.ppermute(corner, "ep", [(i, i ^ 3) for i in range(devices)])
+    pieces = [
+        jnp.concatenate([first_most, swap(first_c, 1)], axis=0),
+        jnp.concatenate([swap(first_most, 0), cross[:, :mid]], axis=0),
+        jnp.concatenate([second_most, swap(second_c, 0)], axis=0),
+        jnp.concatenate([swap(second_most, 1), cross[:, mid:]], axis=0),
+    ]
+    pieces += [exchange(piece) for piece in pieces]
+    gate = input_call(gate_kernel, at, pieces, gate_moved, (), jnp.float32, "gate")
     rest = pack_rest(listing, down_proj, parts[0], devices)
-    moved, rest = tie((moved, rest))
+    moved, gate, rest = tie((moved, gate, rest))
+    up_moved, down0 = moved[:, :size], moved[:, size:]
 
     down1 = move(rest)
-    at = jnp.stack([me, core]).astype(jnp.int32)
-    hidden = hidden_units(at, pieces + others, moved)
+    hidden = input_call(
+        hidden_kernel, at, pieces, up_moved, (gate, terms), jnp.bfloat16, "hidden"
+    )
     hidden_other = exchange(hidden)
-    down0 = moved[:, depth * 7 : depth * 7 + parts[0] * 7 // 2]
 
     def products(down, rows_in, orders):
         own = lax.dynamic_slice_in_dim(down, core * group, group, 0)
@@ -422,8 +472,7 @@
         sent = down_product(*args, rows_in, 1, orders, jnp.bfloat16, "down_send")
         sent, args = tie((sent, args))
         come = [swap(value, order[0]) for value, order in zip(sent, orders)]
-        kept = down_product(*args, rows_in, 0, orders, jnp.float32, "down_keep")
-        return kept, come, sent
+        return down_product(*args, rows_in, 0, orders, jnp.float32, "down_keep"), come
 
     def stage(kept, come, number, orders):
         axes = tuple(stage_axis(order, number) for order in orders)
@@ -436,10 +485,9 @@
         come = swap(send, 3)
         return (keep + come.astype(jnp.float32)).astype(jnp.bfloat16)
 
-    kept0, come0, _ = products(down0, parts[0], THIRDS)
-    down1, kept0 = tie((down1, kept0))
-    kept1, come1, sent1 = products(down1, parts[1], THIRDS)
-    kept0, _ = tie((kept0, sent1))
+    kept0, come0 = products(down0, parts[0], THIRDS)
+    down1, kept0, come0 = tie((down1, kept0, come0))
+    kept1, come1 = products(down1, parts[1], THIRDS)
     kept0, come0 = stage(kept0, come0, 1, THIRDS)
     kept1, come1 = stage(kept1, come1, 1, THIRDS)
     kept0, come0 = stage(kept0, come0, 2, THIRDS)

time: 359 us -> 396 us (1.10)
  starting transfers between devices: 49.5 us -> 58.3 us
  Pallas kernels: 44 us -> 52.6 us
  waiting for transfers between devices: 235 us -> 242 us
  other arithmetic: 6.13 us -> 12.9 us
  local copies, waits for them, and re-layouts: 19.8 us -> 25.1 us
    ppermute x27 -> x29, waiting for transfers between devices: 198 us -> 221 us  [swap(): return lax.ppermute(value, 'ep', [(i, i ^ 1 << bit) for i in range(size)])]
    all_to_all x2 -> x3, waiting for transfers between devices: 33.9 us -> 18 us  [move(): return lax.all_to_all(packed, 'ep', 0, 0, tiled=True)]
    all_to_all x2 -> x3, starting transfers between devices: 17.5 us -> 29.6 us  [move(): return lax.all_to_all(packed, 'ep', 0, 0, tiled=True)]
    slice x2 -> x7, local copies, waits for them, and re-layouts: 1.78 us -> 9.21 us  [the longest x2 5.48 us: packed_layer(): up_moved, down0 = (moved[:, :size], moved[:, size:])]
    concatenate x2 -> x6, other arithmetic: 1.55 us -> 8.44 us  [the longest x1 2.5 us: packed_layer(): jnp.concatenate([first_most, swap(first_c, 1)], axis=0)]
    pallas_call x2 -> x4, Pallas kernels: 31.1 us -> 37.1 us  [the longest x2 32.8 us: input_call(): pl.pallas_call(kernel, grid=(8,), out_shape=jax.ShapeDtypeStruct((total,...]
    ppermute x27 -> x29, starting transfers between devices: 30.2 us -> 26.1 us  [swap(): return lax.ppermute(value, 'ep', [(i, i ^ 1 << bit) for i in range(size)])]
    unnamed x39 -> x42, local copies, waits for them, and re-layouts: 15 us -> 13 us
  transfers between devices with their start and end apart: 36 -> 40, of which waited for: 21 -> 21; matrix products, arithmetic and copies ran while one was open for 2% -> 4% of each run, Pallas kernels for 12% -> 8%
where the time goes in v6:
time: 396 us; the launch traced here: 391 us
  waiting for transfers between devices  242 us (61%)
  starting transfers between devices  58.3 us (15%)
  Pallas kernels  52.6 us (13%)
  local copies, waits for them, and re-layouts  25.1 us (6%)
  other arithmetic  12.9 us (3%)
    ppermute x29, waiting for transfers between devices, swap(): return lax.ppermute(value, 'ep', [(i, i ^ 1 << bit) for i in range(size)])  221 us
    pallas_call x2, Pallas kernels, input_call(): pl.pallas_call(kernel, grid=(8,), out_shape=jax.ShapeDtypeStruct((total,...  32.8 us
    all_to_all x3, starting transfers between devices, move(): return lax.all_to_all(packed, 'ep', 0, 0, tiled=True)  29.6 us
    ppermute x29, starting transfers between devices, swap(): return lax.ppermute(value, 'ep', [(i, i ^ 1 << bit) for i in range(size)])  26.1 us
    all_to_all x3, waiting for transfers between devices, move(): return lax.all_to_all(packed, 'ep', 0, 0, tiled=True)  18 us
    unnamed x42, local copies, waits for them, and re-layouts  13 us
    pallas_call x4, Pallas kernels, down_product(): pl.pallas_call(functools.partial(down_kernel, rows, side, orders), out_sh...  10.9 us
  transfers between devices with their start and end apart: 40, of which 21 were waited for; matrix products, arithmetic and copies ran while one was open for 4% of the time, Pallas kernels for 8%

profile of v6, /device:TPU:14, one launch (start us, length us, event | category | flops | bytes accessed | tf_op | source)
XLA Modules:
  0.0 391.1 jit_solution(16644713400487600139)
XLA Ops:
  3.8 2.0 copy-done.3
  5.9 2.8 pack_gate.1
  8.7 7.1 %all-to-all-start = ((bf16[16,800,128]{2,1,0:T(8,128)(2,1)}), bf16[16,800,128]{2,1,0:T(8,128)(2,1)S(1)}, u32[]{:S(2)}, u32[]{:S(2)}) async-start(bf16[16,800,128]{2,1,0:T(8,128)(2,1)} %pack_gate.1), calls=%async_computation | async-start | bytes 6553600 | tf_op jit(solution)/shard_map/all_to_all | solution.py:416
  15.8 2.4 collective-permute-start
  18.8 1.1 constant_dynamic-update-slice_fusion.2
  19.9 87.3 %collective-permute-done = bf16[128,1792]{1,0:T(8,128)(2,1)S(1)} collective-permute-done((bf16[128,1792]{1,0:T(8,128)(2,1)}, bf16[128,1792]{1,0:T(8,128)(2,1)S(1)}, u32[]{:S(2)}, u32[]{:S(2)}) %collective-permute-start) | collective-permute-done | bytes 458784 | tf_op jit(solution)/shard_map/ppermute | solution.py:367
  108.0 3.0 collective-permute-start.4
  111.0 2.0 copy-done.4
  113.0 1.5 pack_up.1
  114.6 2.3 copy-done
  116.9 3.6 collective-permute-done.4
  120.4 3.0 collective-permute-done.3
  124.3 7.8 %all-to-all-start.1 = ((bf16[16,1232,128]{2,1,0:T(8,128)(2,1)}), bf16[16,1232,128]{2,1,0:T(8,128)(2,1)}, u32[]{:S(2)}, u32[]{:S(2)}) async-start(bf16[16,1232,128]{2,1,0:T(8,128)(2,1)} %copy-done), calls=%async_computation.1 | async-start | bytes 10092544 | tf_op jit(solution)/shard_map/all_to_all | solution.py:416
  132.1 1.1 fusion.5
  133.3 1.5 pad_maximum_fusion.4
  136.2 1.5 collective-permute-start.8
  137.7 1.5 collective-permute-start.7
  139.7 74.7 %collective-permute-done.8 = bf16[128,896]{1,0:T(8,128)(2,1)S(1)} collective-permute-done((bf16[128,896]{1,0:T(8,128)(2,1)S(1)}, bf16[128,896]{1,0:T(8,128)(2,1)S(1)}, u32[]{:S(2)}, u32[]{:S(2)}) %collective-permute-start.8) | collective-permute-done | bytes 229408 | tf_op jit(solution)/shard_map/ppermute | solution.py:367
  214.4 1.4 pad_maximum_fusion.2.refs_2_
  215.8 11.7 %collective-permute-done.5 = bf16[128,896]{1,0:T(8,128)(2,1)S(1)} collective-permute-done((bf16[128,896]{1,0:T(8,128)(2,1)S(1)}, bf16[128,896]{1,0:T(8,128)(2,1)S(1)}, u32[]{:S(2)}, u32[]{:S(2)}) %collective-permute-start.5) | collective-permute-done | bytes 229408 | tf_op jit(solution)/shard_map/ppermute | solution.py:367
  227.5 2.5 pad_maximum_fusion.refs_0_
  230.1 1.5 pad_maximum_fusion.1.refs_1_
  232.0 1.4 pad_maximum_fusion.3.refs_3_
  233.5 2.0 copy-done.2
  235.5 1.9 pack_rest.1
  238.6 1.9 slice.36.refs_8_
  240.5 16.1 %gate.1.refs_9_ = f32[2048,512]{1,0:T(8,128)} custom-call(s32[2]{0:T(128)} %pad_add_fusion.at_ref, bf16[1024,896]{1,0:T(8,128)(2,1)} %pad_maximum_fusion.refs_0_, bf16[1024,896]{1,0:T(8,128)(2,1)} %pad_maximum_fusion.1.refs_1_, bf16[1024,896]{1,0:T(8,128)(2,1)} %pad_maximum_fusion.2.refs_2_, bf16[1024,896]{1,0:T(8,128)(2,1)} %pad_maximum_fusion.3.refs_3_, ...), custom_call_target="tpu_custom_call" | custom-call | flops 7516192768 | bytes 20971520 | tf_op jit(solution)/shard_map/gate/pallas_call | solution.py:238
  256.6 3.8 slice.37.refs_8_
  260.4 16.7 %hidden.1.own_h = bf16[2048,512]{1,0:T(8,128)(2,1)} custom-call(s32[2]{0:T(128)} %pad_add_fusion.at_ref, bf16[1024,896]{1,0:T(8,128)(2,1)} %pad_maximum_fusion.refs_0_, bf16[1024,896]{1,0:T(8,128)(2,1)} %pad_maximum_fusion.1.refs_1_, bf16[1024,896]{1,0:T(8,128)(2,1)} %pad_maximum_fusion.2.refs_2_, bf16[1024,896]{1,0:T(8,128)(2,1)} %pad_maximum_fusion.3.refs_3_, ...), custom_call_target="tpu_custom_call" | custom-call | flops 7516192768 | bytes 20971520 | tf_op jit(solution)/shard_map/hidden/pallas_call | solution.py:238
  277.6 14.6 %all-to-all-start.2 = ((bf16[16,336,128]{2,1,0:T(8,128)(2,1)}), bf16[16,336,128]{2,1,0:T(8,128)(2,1)}, u32[]{:S(2)}, u32[]{:S(2)}) async-start(bf16[16,336,128]{2,1,0:T(8,128)(2,1)} %pack_rest.1), calls=%async_computation.2 | async-start | bytes 2752512 | tf_op jit(solution)/shard_map/all_to_all | solution.py:416
  292.2 1.6 slice.39
  294.1 2.5 collective-permute-done.15.other_ref
  296.5 4.0 %down_send.2 = (bf16[1024,384]{1,0:T(8,128)(2,1)}, bf16[1024,384]{1,0:T(8,128)(2,1)}, bf16[1024,256]{1,0:T(8,128)(2,1)}) custom-call(bf16[2048,512]{1,0:T(8,128)(2,1)S(1)} %copy-done.7, bf16[2048,512]{1,0:T(8,128)(2,1)S(1)} %collective-permute-done.14.other_h, bf16[8,448,128]{2,1,0:T(8,128)(2,1)S(1)} %get-tuple-element.91.own_ref, ...), custom_call_target="tpu_custom_call" | custom-call | flops 2147483648 | bytes 8388608 | tf_op jit(solution)/shard_map/down_send/pallas_call | solution.py:307
  301.9 1.6 copy-done.10
  303.5 3.0 down_keep.2
  306.5 1.0 copy-done.5
  307.5 18.0 %all-to-all-done.2 = bf16[16,336,128]{2,1,0:T(8,128)(2,1)} async-done(((bf16[16,336,128]{2,1,0:T(8,128)(2,1)}), bf16[16,336,128]{2,1,0:T(8,128)(2,1)}, u32[]{:S(2)}, u32[]{:S(2)}) %all-to-all-start.2) | async-done | bytes 1376288 | tf_op jit(solution)/shard_map/all_to_all | solution.py:416
  325.5 1.9 collective-permute-done.18.refs_5_
  327.4 3.5 collective-permute-done.16.refs_1_
  331.0 1.4 constant_dynamic-slice_fusion
  332.5 2.0 sum_stage.6
  334.5 1.1 collective-permute-start.21
  335.6 1.9 down_send.3
  337.5 1.1 collective-permute-start.27
  338.6 1.2 collective-permute-start.19
  339.7 1.2 collective-permute-start.28
  341.0 2.8 collective-permute-done.21.refs_5_
  344.0 6.5 %collective-permute-done.19.refs_1_ = bf16[512,384]{1,0:T(8,128)(2,1)S(1)} collective-permute-done((bf16[512,384]{1,0:T(8,128)(2,1)S(1)}, bf16[512,384]{1,0:T(8,128)(2,1)S(1)}, u32[]{:S(2)}, u32[]{:S(2)}) %collective-permute-start.19) | collective-permute-done | bytes 393248 | tf_op jit(solution)/shard_map/ppermute | solution.py:367
  350.5 1.2 collective-permute-done.20.refs_3_
  353.2 1.5 collective-permute-done.27.refs_1_
  354.7 1.0 collective-permute-start.23
  355.7 1.9 down_keep.3
  357.6 4.1 %collective-permute-done.28.refs_3_ = bf16[1024,256]{1,0:T(8,128)(2,1)S(1)} collective-permute-done((bf16[1024,256]{1,0:T(8,128)(2,1)S(1)}, bf16[1024,256]{1,0:T(8,128)(2,1)S(1)}, u32[]{:S(2)}, u32[]{:S(2)}) %collective-permute-start.28) | collective-permute-done | bytes 524320 | tf_op jit(solution)/shard_map/ppermute | solution.py:367
  361.8 1.2 collective-permute-done.29.refs_5_
  365.3 1.7 collective-permute-done.22.refs_1_
  367.0 1.5 collective-permute-start.25
  368.5 1.2 collective-permute-done.30.refs_1_
  369.7 5.5 %collective-permute-done.31.refs_3_ = bf16[512,256]{1,0:T(8,128)(2,1)S(1)} collective-permute-done((bf16[512,256]{1,0:T(8,128)(2,1)S(1)}, bf16[512,256]{1,0:T(8,128)(2,1)S(1)}, u32[]{:S(2)}, u32[]{:S(2)}) %collective-permute-start.31) | collective-permute-done | bytes 262176 | tf_op jit(solution)/shard_map/ppermute | solution.py:367
  375.3 2.7 collective-permute-start.33
  378.7 2.9 collective-permute-done.33.refs_1_
  381.6 1.4 collective-permute-done.34.refs_3_
  383.1 1.0 collective-permute-start.36
  384.3 5.5 %collective-permute-done.36 = bf16[128,768]{1,0:T(8,128)(2,1)S(1)} collective-permute-done((bf16[128,768]{1,0:T(8,128)(2,1)S(1)}, bf16[128,768]{1,0:T(8,128)(2,1)S(1)}, u32[]{:S(2)}, u32[]{:S(2)}) %collective-permute-start.36) | collective-permute-done | bytes 196640 | tf_op jit(solution)/shard_map/ppermute | solution.py:367
  390.1 1.0 copy.15
  (104 shorter events, 17.2 us)
Async XLA Ops:
  3.8 2.0 copy-start.3
  8.7 115.6 %all-to-all-start = ((bf16[16,800,128]{2,1,0:T(8,128)(2,1)}), bf16[16,800,128]{2,1,0:T(8,128)(2,1)S(1)}, u32[]{:S(2)}, u32[]{:S(2)}) async-start(bf16[16,800,128]{2,1,0:T(8,128)(2,1)} %pack_gate.1), calls=%async_computation | async-start | bytes 6553600 | tf_op jit(solution)/shard_map/all_to_all | solution.py:416
  15.8 91.3 %collective-permute-start = (bf16[128,1792]{1,0:T(8,128)(2,1)}, bf16[128,1792]{1,0:T(8,128)(2,1)S(1)}, u32[]{:S(2)}, u32[]{:S(2)}) collective-permute-start(bf16[128,1792]{1,0:T(8,128)(2,1)} %param.9), channel_id=1, source_target_pairs={{0,16},{2,18},{4,20},{6,22},{8,24},{10,26},{12,28},{14,30},{16,0},... | collective-permute-start | bytes 1376264 | tf_op jit(solution)/shard_map/ppermute | solution.py:367
  18.2 89.0 %collective-permute-start.1 = (bf16[128,1792]{1,0:T(8,128)(2,1)}, bf16[128,1792]{1,0:T(8,128)(2,1)S(1)}, u32[]{:S(2)}, u32[]{:S(2)}) collective-permute-start(bf16[128,1792]{1,0:T(8,128)(2,1)} %param.9), channel_id=1, source_target_pairs={{0,8},{2,10},{4,12},{6,14},{8,0},{10,2},{12,4},{14,6},{16,24},{18,... | collective-permute-start | bytes 1376264 | tf_op jit(solution)/shard_map/ppermute | solution.py:367
  107.2 3.8 copy-start.1
  107.3 7.2 %copy-start.12 = (bf16[384,896]{1,0:T(8,128)(2,1)}, bf16[384,896]{1,0:T(8,128)(2,1)S(1)}, u32[]{:S(2)}) copy-start(bf16[384,896]{1,0:T(8,128)(2,1)S(1)} %get-tuple-element.77) | copy-start | bytes 2064388
  107.3 7.2 %copy-start.14 = (bf16[384,896]{1,0:T(8,128)(2,1)}, bf16[384,896]{1,0:T(8,128)(2,1)S(1)}, u32[]{:S(2)}) copy-start(bf16[384,896]{1,0:T(8,128)(2,1)S(1)} %get-tuple-element.80) | copy-start | bytes 2064388
  107.4 16.1 %collective-permute-start.3 = (bf16[384,896]{1,0:T(8,128)(2,1)S(1)}, bf16[384,896]{1,0:T(8,128)(2,1)S(1)}, u32[]{:S(2)}, u32[]{:S(2)}) collective-permute-start(bf16[384,896]{1,0:T(8,128)(2,1)S(1)} %get-tuple-element.80), channel_id=1, source_target_pairs={{0,2},{2,0},{4,6},{6,4},{8,10},{10,8},{12,14},{14,12},{16,18},{18,... | collective-permute-start | bytes 2064392 | tf_op jit(solution)/shard_map/ppermute | solution.py:367
  107.4 16.9 %collective-permute-start.2 = (bf16[384,896]{1,0:T(8,128)(2,1)S(1)}, bf16[384,896]{1,0:T(8,128)(2,1)}, u32[]{:S(2)}, u32[]{:S(2)}) collective-permute-start(bf16[384,896]{1,0:T(8,128)(2,1)S(1)} %get-tuple-element.77), channel_id=1, source_target_pairs={{0,4},{2,6},{4,0},{6,2},{8,12},{10,14},{12,8},{14,10},{16,20},{18,... | collective-permute-start | bytes 2064392 | tf_op jit(solution)/shard_map/ppermute | solution.py:367
  108.0 12.5 %collective-permute-start.4 = (bf16[128,1792]{1,0:T(8,128)(2,1)S(1)}, bf16[128,1792]{1,0:T(8,128)(2,1)S(1)}, u32[]{:S(2)}, u32[]{:S(2)}) collective-permute-start(bf16[128,1792]{1,0:T(8,128)(2,1)S(1)} %collective-permute-done), channel_id=1, source_target_pairs={{0,8},{2,10},{4,12},{6,14},{8,0},{10,2},{12,4},{14,6},{16,24},{18,... | collective-permute-start | bytes 1376264 | tf_op jit(solution)/shard_map/ppermute | solution.py:367
  111.0 2.0 copy-start.4
  114.6 2.3 copy-start
  120.4 3.0 copy-start.18
  123.4 0.9 copy-start.16
  124.3 132.2 %all-to-all-start.1 = ((bf16[16,1232,128]{2,1,0:T(8,128)(2,1)}), bf16[16,1232,128]{2,1,0:T(8,128)(2,1)}, u32[]{:S(2)}, u32[]{:S(2)}) async-start(bf16[16,1232,128]{2,1,0:T(8,128)(2,1)} %copy-done), calls=%async_computation.1 | async-start | bytes 10092544 | tf_op jit(solution)/shard_map/all_to_all | solution.py:416
  133.2 2.2 copy-start.15
  133.2 2.2 copy-start.17
  134.8 2.9 copy-start.19
  134.8 95.2 %collective-permute-start.6 = (bf16[896,896]{1,0:T(8,128)(2,1)S(1)}, bf16[896,896]{1,0:T(8,128)(2,1)S(1)}, u32[]{:S(2)}, u32[]{:S(2)}) collective-permute-start(bf16[896,896]{1,0:T(8,128)(2,1)S(1)} %pad_maximum_fusion.4), channel_id=1, source_target_pairs={{0,2},{2,0},{4,6},{6,4},{8,10},{10,8},{12,14},{14,12},{16,18},{18,... | collective-permute-start | bytes 4816904 | tf_op jit(solution)/shard_map/ppermute | solution.py:367
  135.6 91.9 %copy-start.13 = (bf16[384,896]{1,0:T(8,128)(2,1)S(1)}, bf16[384,896]{1,0:T(8,128)(2,1)}, u32[]{:S(2)}) copy-start(bf16[384,896]{1,0:T(8,128)(2,1)} %copy-done.12) | copy-start | bytes 2064388
  135.6 96.5 %collective-permute-start.9 = (bf16[896,896]{1,0:T(8,128)(2,1)S(1)}, bf16[896,896]{1,0:T(8,128)(2,1)S(1)}, u32[]{:S(2)}, u32[]{:S(2)}) collective-permute-start(bf16[896,896]{1,0:T(8,128)(2,1)S(1)} %pad_maximum_fusion.5), channel_id=1, source_target_pairs={{0,4},{2,6},{4,0},{6,2},{8,12},{10,14},{12,8},{14,10},{16,20},{18,... | collective-permute-start | bytes 4816904 | tf_op jit(solution)/shard_map/ppermute | solution.py:367
  136.2 78.2 %collective-permute-start.8 = (bf16[128,896]{1,0:T(8,128)(2,1)S(1)}, bf16[128,896]{1,0:T(8,128)(2,1)S(1)}, u32[]{:S(2)}, u32[]{:S(2)}) collective-permute-start(bf16[128,896]{1,0:T(8,128)(2,1)S(1)} %get-tuple-element.155), channel_id=1, source_target_pairs={{0,2},{2,0},{4,6},{6,4},{8,10},{10,8},{12,14},{14,12},{16,18},{18,... | collective-permute-start | bytes 688136 | tf_op jit(solution)/shard_map/ppermute | solution.py:367
  137.7 92.3 %collective-permute-start.7 = (bf16[128,1792]{1,0:T(8,128)(2,1)S(1)}, bf16[128,1792]{1,0:T(8,128)(2,1)S(1)}, u32[]{:S(2)}, u32[]{:S(2)}) collective-permute-start(bf16[128,1792]{1,0:T(8,128)(2,1)S(1)} %copy-done.19), channel_id=1, source_target_pairs={{0,6},{2,4},{4,2},{6,0},{8,14},{10,12},{12,10},{14,8},{16,22},{18,... | collective-permute-start | bytes 1376264 | tf_op jit(solution)/shard_map/ppermute | solution.py:449
  139.1 88.4 %collective-permute-start.5 = (bf16[128,896]{1,0:T(8,128)(2,1)S(1)}, bf16[128,896]{1,0:T(8,128)(2,1)S(1)}, u32[]{:S(2)}, u32[]{:S(2)}) collective-permute-start(bf16[128,896]{1,0:T(8,128)(2,1)S(1)} %get-tuple-element.156), channel_id=1, source_target_pairs={{0,4},{2,6},{4,0},{6,2},{8,12},{10,14},{12,8},{14,10},{16,20},{18,... | collective-permute-start | bytes 688136 | tf_op jit(solution)/shard_map/ppermute | solution.py:367
  215.8 24.7 %collective-permute-start.12 = (bf16[1024,896]{1,0:T(8,128)(2,1)}, bf16[1024,896]{1,0:T(8,128)(2,1)}, u32[]{:S(2)}, u32[]{:S(2)}) collective-permute-start(bf16[1024,896]{1,0:T(8,128)(2,1)} %pad_maximum_fusion.2.refs_2_), channel_id=1, source_target_pairs={{0,1},{1,0},{2,3},{3,2},{4,5},{5,4},{6,7},{7,6},{8,9},{9,8},{10,11... | collective-permute-start | bytes 5505032 | tf_op jit(solution)/shard_map/ppermute | solution.py:413
  230.0 10.5 %collective-permute-start.10 = (bf16[1024,896]{1,0:T(8,128)(2,1)}, bf16[1024,896]{1,0:T(8,128)(2,1)}, u32[]{:S(2)}, u32[]{:S(2)}) collective-permute-start(bf16[1024,896]{1,0:T(8,128)(2,1)} %pad_maximum_fusion.refs_0_), channel_id=1, source_target_pairs={{0,1},{1,0},{2,3},{3,2},{4,5},{5,4},{6,7},{7,6},{8,9},{9,8},{10,11... | collective-permute-start | bytes 5505032 | tf_op jit(solution)/shard_map/ppermute | solution.py:413
  231.5 8.9 %collective-permute-start.11 = (bf16[1024,896]{1,0:T(8,128)(2,1)}, bf16[1024,896]{1,0:T(8,128)(2,1)}, u32[]{:S(2)}, u32[]{:S(2)}) collective-permute-start(bf16[1024,896]{1,0:T(8,128)(2,1)} %pad_maximum_fusion.1.refs_1_), channel_id=1, source_target_pairs={{0,1},{1,0},{2,3},{3,2},{4,5},{5,4},{6,7},{7,6},{8,9},{9,8},{10,11... | collective-permute-start | bytes 5505032 | tf_op jit(solution)/shard_map/ppermute | solution.py:413
  233.5 7.0 %collective-permute-start.13 = (bf16[1024,896]{1,0:T(8,128)(2,1)}, bf16[1024,896]{1,0:T(8,128)(2,1)}, u32[]{:S(2)}, u32[]{:S(2)}) collective-permute-start(bf16[1024,896]{1,0:T(8,128)(2,1)} %pad_maximum_fusion.3.refs_3_), channel_id=1, source_target_pairs={{0,1},{1,0},{2,3},{3,2},{4,5},{5,4},{6,7},{7,6},{8,9},{9,8},{10,11... | collective-permute-start | bytes 5505032 | tf_op jit(solution)/shard_map/ppermute | solution.py:413
  233.5 2.0 copy-start.2
  277.1 19.4 %collective-permute-start.14 = (bf16[2048,512]{1,0:T(8,128)(2,1)}, bf16[2048,512]{1,0:T(8,128)(2,1)S(1)}, u32[]{:S(2)}, u32[]{:S(2)}) collective-permute-start(bf16[2048,512]{1,0:T(8,128)(2,1)} %hidden.1.own_h), channel_id=1, source_target_pairs={{0,1},{1,0},{2,3},{3,2},{4,5},{5,4},{6,7},{7,6},{8,9},{9,8},{10,11... | collective-permute-start | bytes 6291464 | tf_op jit(solution)/shard_map/ppermute | solution.py:413
  277.6 47.9 %all-to-all-start.2 = ((bf16[16,336,128]{2,1,0:T(8,128)(2,1)}), bf16[16,336,128]{2,1,0:T(8,128)(2,1)}, u32[]{:S(2)}, u32[]{:S(2)}) async-start(bf16[16,336,128]{2,1,0:T(8,128)(2,1)} %pack_rest.1), calls=%async_computation.2 | async-start | bytes 2752512 | tf_op jit(solution)/shard_map/all_to_all | solution.py:416
  293.8 2.7 copy-start.7
  294.0 2.5 collective-permute-start.15
  296.5 4.0 %copy-start.9 = (bf16[2048,512]{1,0:T(8,128)(2,1)}, bf16[2048,512]{1,0:T(8,128)(2,1)S(1)}, u32[]{:S(2)}) copy-start(bf16[2048,512]{1,0:T(8,128)(2,1)S(1)} %collective-permute-done.14.other_h) | copy-start | bytes 6291460
  300.6 30.4 %collective-permute-start.16 = (bf16[1024,384]{1,0:T(8,128)(2,1)}, bf16[1024,384]{1,0:T(8,128)(2,1)}, u32[]{:S(2)}, u32[]{:S(2)}) collective-permute-start(bf16[1024,384]{1,0:T(8,128)(2,1)} %get-tuple-element.96), channel_id=1, source_target_pairs={{0,2},{2,0},{4,6},{6,4},{8,10},{10,8},{12,14},{14,12},{16,18},{18,... | collective-permute-start | bytes 2359304 | tf_op jit(solution)/shard_map/ppermute | solution.py:367
  301.1 29.8 %collective-permute-start.17 = (bf16[1024,384]{1,0:T(8,128)(2,1)}, bf16[1024,384]{1,0:T(8,128)(2,1)}, u32[]{:S(2)}, u32[]{:S(2)}) collective-permute-start(bf16[1024,384]{1,0:T(8,128)(2,1)} %get-tuple-element.97), channel_id=1, source_target_pairs={{0,4},{2,6},{4,0},{6,2},{8,12},{10,14},{12,8},{14,10},{16,20},{18,... | collective-permute-start | bytes 2359304 | tf_op jit(solution)/shard_map/ppermute | solution.py:367
  301.7 25.7 %collective-permute-start.18 = (bf16[1024,256]{1,0:T(8,128)(2,1)}, bf16[1024,256]{1,0:T(8,128)(2,1)}, u32[]{:S(2)}, u32[]{:S(2)}) collective-permute-start(bf16[1024,256]{1,0:T(8,128)(2,1)} %get-tuple-element.98), channel_id=1, source_target_pairs={{0,8},{2,10},{4,12},{6,14},{8,0},{10,2},{12,4},{14,6},{16,24},{18,... | collective-permute-start | bytes 1572872 | tf_op jit(solution)/shard_map/ppermute | solution.py:367
  301.9 1.6 copy-start.10
  306.5 1.0 copy-start.5
  325.5 7.0 %copy-start.6 = (f32[1024,256]{1,0:T(8,128)S(1)}, f32[1024,256]{1,0:T(8,128)}, u32[]{:S(2)}) copy-start(f32[1024,256]{1,0:T(8,128)} %copy-done.5) | copy-start | bytes 3145732
  332.4 3.2 copy-start.8
  332.4 3.2 copy-start.11
  332.4 3.2 collective-permute-start.26
  334.5 9.2 %collective-permute-start.21 = (bf16[512,256]{1,0:T(8,128)(2,1)S(1)}, bf16[512,256]{1,0:T(8,128)(2,1)S(1)}, u32[]{:S(2)}, u32[]{:S(2)}) collective-permute-start(bf16[512,256]{1,0:T(8,128)(2,1)S(1)} %get-tuple-element.110), channel_id=1, source_target_pairs={{0,2},{2,0},{4,6},{6,4},{8,10},{10,8},{12,14},{14,12},{16,18},{18,... | collective-permute-start | bytes 786440 | tf_op jit(solution)/shard_map/ppermute | solution.py:367
  337.5 17.2 %collective-permute-start.27 = (bf16[1024,256]{1,0:T(8,128)(2,1)S(1)}, bf16[1024,256]{1,0:T(8,128)(2,1)S(1)}, u32[]{:S(2)}, u32[]{:S(2)}) collective-permute-start(bf16[1024,256]{1,0:T(8,128)(2,1)S(1)} %get-tuple-element.128), channel_id=1, source_target_pairs={{0,2},{2,0},{4,6},{6,4},{8,10},{10,8},{12,14},{14,12},{16,18},{18,... | collective-permute-start | bytes 1572872 | tf_op jit(solution)/shard_map/ppermute | solution.py:367
  338.6 12.0 %collective-permute-start.19 = (bf16[512,384]{1,0:T(8,128)(2,1)S(1)}, bf16[512,384]{1,0:T(8,128)(2,1)S(1)}, u32[]{:S(2)}, u32[]{:S(2)}) collective-permute-start(bf16[512,384]{1,0:T(8,128)(2,1)S(1)} %get-tuple-element.106), channel_id=1, source_target_pairs={{0,4},{2,6},{4,0},{6,2},{8,12},{10,14},{12,8},{14,10},{16,20},{18,... | collective-permute-start | bytes 1179656 | tf_op jit(solution)/shard_map/ppermute | solution.py:367
  339.7 12.1 %collective-permute-start.20 = (bf16[512,384]{1,0:T(8,128)(2,1)S(1)}, bf16[512,384]{1,0:T(8,128)(2,1)S(1)}, u32[]{:S(2)}, u32[]{:S(2)}) collective-permute-start(bf16[512,384]{1,0:T(8,128)(2,1)S(1)} %get-tuple-element.108), channel_id=1, source_target_pairs={{0,8},{2,10},{4,12},{6,14},{8,0},{10,2},{12,4},{14,6},{16,24},{18,... | collective-permute-start | bytes 1179656 | tf_op jit(solution)/shard_map/ppermute | solution.py:367
  339.7 22.0 %collective-permute-start.28 = (bf16[1024,256]{1,0:T(8,128)(2,1)S(1)}, bf16[1024,256]{1,0:T(8,128)(2,1)S(1)}, u32[]{:S(2)}, u32[]{:S(2)}) collective-permute-start(bf16[1024,256]{1,0:T(8,128)(2,1)S(1)} %get-tuple-element.130), channel_id=1, source_target_pairs={{0,4},{2,6},{4,0},{6,2},{8,12},{10,14},{12,8},{14,10},{16,20},{18,... | collective-permute-start | bytes 1572872 | tf_op jit(solution)/shard_map/ppermute | solution.py:367
  343.7 19.3 %collective-permute-start.29 = (bf16[1024,256]{1,0:T(8,128)(2,1)S(1)}, bf16[1024,256]{1,0:T(8,128)(2,1)S(1)}, u32[]{:S(2)}, u32[]{:S(2)}) collective-permute-start(bf16[1024,256]{1,0:T(8,128)(2,1)S(1)} %get-tuple-element.132), channel_id=1, source_target_pairs={{0,8},{2,10},{4,12},{6,14},{8,0},{10,2},{12,4},{14,6},{16,24},{18,... | collective-permute-start | bytes 1572872 | tf_op jit(solution)/shard_map/ppermute | solution.py:367
  351.9 12.6 %collective-permute-start.24 = (bf16[256,256]{1,0:T(8,128)(2,1)S(1)}, bf16[256,256]{1,0:T(8,128)(2,1)S(1)}, u32[]{:S(2)}, u32[]{:S(2)}) collective-permute-start(bf16[256,256]{1,0:T(8,128)(2,1)S(1)} %get-tuple-element.116), channel_id=1, source_target_pairs={{0,4},{2,6},{4,0},{6,2},{8,12},{10,14},{12,8},{14,10},{16,20},{18,... | collective-permute-start | bytes 393224 | tf_op jit(solution)/shard_map/ppermute | solution.py:367
  352.8 14.1 %collective-permute-start.22 = (bf16[256,384]{1,0:T(8,128)(2,1)S(1)}, bf16[256,384]{1,0:T(8,128)(2,1)S(1)}, u32[]{:S(2)}, u32[]{:S(2)}) collective-permute-start(bf16[256,384]{1,0:T(8,128)(2,1)S(1)} %get-tuple-element.112), channel_id=1, source_target_pairs={{0,8},{2,10},{4,12},{6,14},{8,0},{10,2},{12,4},{14,6},{16,24},{18,... | collective-permute-start | bytes 589832 | tf_op jit(solution)/shard_map/ppermute | solution.py:367
  354.7 12.3 %collective-permute-start.23 = (bf16[256,384]{1,0:T(8,128)(2,1)S(1)}, bf16[256,384]{1,0:T(8,128)(2,1)S(1)}, u32[]{:S(2)}, u32[]{:S(2)}) collective-permute-start(bf16[256,384]{1,0:T(8,128)(2,1)S(1)} %get-tuple-element.114), channel_id=1, source_target_pairs={{0,2},{2,0},{4,6},{6,4},{8,10},{10,8},{12,14},{14,12},{16,18},{18,... | collective-permute-start | bytes 589832 | tf_op jit(solution)/shard_map/ppermute | solution.py:367
  363.3 6.4 %collective-permute-start.30 = (bf16[512,256]{1,0:T(8,128)(2,1)S(1)}, bf16[512,256]{1,0:T(8,128)(2,1)S(1)}, u32[]{:S(2)}, u32[]{:S(2)}) collective-permute-start(bf16[512,256]{1,0:T(8,128)(2,1)S(1)} %get-tuple-element.134), channel_id=1, source_target_pairs={{0,4},{2,6},{4,0},{6,2},{8,12},{10,14},{12,8},{14,10},{16,20},{18,... | collective-permute-start | bytes 786440 | tf_op jit(solution)/shard_map/ppermute | solution.py:367
  364.1 11.1 %collective-permute-start.31 = (bf16[512,256]{1,0:T(8,128)(2,1)S(1)}, bf16[512,256]{1,0:T(8,128)(2,1)S(1)}, u32[]{:S(2)}, u32[]{:S(2)}) collective-permute-start(bf16[512,256]{1,0:T(8,128)(2,1)S(1)} %get-tuple-element.136), channel_id=1, source_target_pairs={{0,8},{2,10},{4,12},{6,14},{8,0},{10,2},{12,4},{14,6},{16,24},{18,... | collective-permute-start | bytes 786440 | tf_op jit(solution)/shard_map/ppermute | solution.py:367
  364.5 10.7 %collective-permute-start.32 = (bf16[512,256]{1,0:T(8,128)(2,1)S(1)}, bf16[512,256]{1,0:T(8,128)(2,1)S(1)}, u32[]{:S(2)}, u32[]{:S(2)}) collective-permute-start(bf16[512,256]{1,0:T(8,128)(2,1)S(1)} %get-tuple-element.138), channel_id=1, source_target_pairs={{0,2},{2,0},{4,6},{6,4},{8,10},{10,8},{12,14},{14,12},{16,18},{18,... | collective-permute-start | bytes 786440 | tf_op jit(solution)/shard_map/ppermute | solution.py:367
  367.0 17.0 %collective-permute-start.25 = (bf16[128,1024]{1,0:T(8,128)(2,1)S(1)}, bf16[128,1024]{1,0:T(8,128)(2,1)S(1)}, u32[]{:S(2)}, u32[]{:S(2)}) collective-permute-start(bf16[128,1024]{1,0:T(8,128)(2,1)S(1)} %get-tuple-element.118), channel_id=1, source_target_pairs={{0,16},{2,18},{4,20},{6,22},{8,24},{10,26},{12,28},{14,30},{16,0},... | collective-permute-start | bytes 786440 | tf_op jit(solution)/shard_map/ppermute | solution.py:367
  375.3 6.3 %collective-permute-start.33 = (bf16[256,256]{1,0:T(8,128)(2,1)S(1)}, bf16[256,256]{1,0:T(8,128)(2,1)S(1)}, u32[]{:S(2)}, u32[]{:S(2)}) collective-permute-start(bf16[256,256]{1,0:T(8,128)(2,1)S(1)} %get-tuple-element.140), channel_id=1, source_target_pairs={{0,8},{2,10},{4,12},{6,14},{8,0},{10,2},{12,4},{14,6},{16,24},{18,... | collective-permute-start | bytes 393224 | tf_op jit(solution)/shard_map/ppermute | solution.py:367
  378.1 5.0 %collective-permute-start.34 = (bf16[256,256]{1,0:T(8,128)(2,1)S(1)}, bf16[256,256]{1,0:T(8,128)(2,1)S(1)}, u32[]{:S(2)}, u32[]{:S(2)}) collective-permute-start(bf16[256,256]{1,0:T(8,128)(2,1)S(1)} %get-tuple-element.142), channel_id=1, source_target_pairs={{0,2},{2,0},{4,6},{6,4},{8,10},{10,8},{12,14},{14,12},{16,18},{18,... | collective-permute-start | bytes 393224 | tf_op jit(solution)/shard_map/ppermute | solution.py:367
  378.1 5.0 %collective-permute-start.35 = (bf16[256,256]{1,0:T(8,128)(2,1)S(1)}, bf16[256,256]{1,0:T(8,128)(2,1)S(1)}, u32[]{:S(2)}, u32[]{:S(2)}) collective-permute-start(bf16[256,256]{1,0:T(8,128)(2,1)S(1)} %get-tuple-element.144), channel_id=1, source_target_pairs={{0,4},{2,6},{4,0},{6,2},{8,12},{10,14},{12,8},{14,10},{16,20},{18,... | collective-permute-start | bytes 393224 | tf_op jit(solution)/shard_map/ppermute | solution.py:367
  383.1 6.7 %collective-permute-start.36 = (bf16[128,768]{1,0:T(8,128)(2,1)S(1)}, bf16[128,768]{1,0:T(8,128)(2,1)S(1)}, u32[]{:S(2)}, u32[]{:S(2)}) collective-permute-start(bf16[128,768]{1,0:T(8,128)(2,1)S(1)} %get-tuple-element.146), channel_id=1, source_target_pairs={{0,16},{2,18},{4,20},{6,22},{8,24},{10,26},{12,28},{14,30},{16,0},... | collective-permute-start | bytes 589832 | tf_op jit(solution)/shard_map/ppermute | solution.py:367

commit v7 on v5

--- a/solution.py
+++ b/solution.py
@@ -154,7 +154,7 @@
     size = depth * 7 // 2
     group = sources // 2
     tile = pl.program_id(0)
-    x, y, zl = tile // 4, tile // 2 % 2, tile % 2
+    x, y = tile // 2, tile % 2
     me, core = at_ref[0], at_ref[1]
 
     @pl.when(tile == 0)
@@ -183,34 +183,31 @@
     lane = lax.broadcasted_iota(jnp.int32, (16, wide), 1)
     chosen = (term % 4 == lane // LANES) & (term < 12) & (lane < wide - HALF)
     chosen = jnp.where(chosen, 1.0, 0.0).astype(jnp.bfloat16)
-    block = rows.shape[0] // 2
-    for zh in range(2):
-        source = me ^ (x + 2 * y + 4 * zl + 8 * zh)
+    block = rows.shape[0] // 4
+    for at in range(4):
+        source = me ^ (x + 2 * y + 4 * (at // 2) + 8 * (at % 2))
         weight = lax.dot_general(
             packed_ref[source, packed_ref.shape[1] - 16 :, :],
             chosen,
             (((0,), (0,)), ((), ())),
             preferred_element_type=jnp.float32,
         )
-        span = slice(zh * block, (zh + 1) * block)
+        span = slice(at * block, (at + 1) * block)
         out_ref[span, :] = (value[span, :] * weight).astype(out_ref.dtype)
 
 
 def hidden_units(at, pieces, packed):
     total = 2 * pieces[0].shape[0]
     mid = pieces[0].shape[1]
-    tile = total // 8
+    tile = total // 4
     wide = 4 * LANES
     model = 4 * mid
-    by_x = [lambda i: (jnp.minimum(i, 3), 0), lambda i: (jnp.maximum(i - 4, 0), 0)]
-    by_y = [
-        lambda i: (i // 4 * 2 + jnp.where(i // 2 % 2 == 0, i % 2, 1), 0),
-        lambda i: (i // 4 * 2 + jnp.where(i // 2 % 2 == 1, i % 2, 0), 0),
-    ]
+    by_x = [lambda i: (jnp.minimum(i, 1), 0), lambda i: (jnp.maximum(i - 2, 0), 0)]
+    by_y = [lambda i: (i // 2, 0)] * 2
     maps = (by_x + by_y) * 2
     return pl.pallas_call(
         hidden_kernel,
-        grid=(8,),
+        grid=(4,),
         out_shape=jax.ShapeDtypeStruct((total, wide), packed.dtype),
         in_specs=[smem()]
         + [pl.BlockSpec((tile, mid), where) for where in maps]
@@ -394,7 +391,7 @@
 
     near, far = swap(tokens, 2), swap(tokens, 3)
     corner = swap(far, 2)
-    parts = (128, 96)
+    parts = (96, 128)
     packed = pack_first(listing, gate_proj, up_proj, down_proj, parts[0], share, devices)
     packed, near, far, corner = tie((packed, near, far, corner))
 
@@ -422,8 +419,7 @@
         sent = down_product(*args, rows_in, 1, orders, jnp.bfloat16, "down_send")
         sent, args = tie((sent, args))
         come = [swap(value, order[0]) for value, order in zip(sent, orders)]
-        kept = down_product(*args, rows_in, 0, orders, jnp.float32, "down_keep")
-        return kept, come, sent
+        return down_product(*args, rows_in, 0, orders, jnp.float32, "down_keep"), come
 
     def stage(kept, come, number, orders):
         axes = tuple(stage_axis(order, number) for order in orders)
@@ -436,10 +432,9 @@
         come = swap(send, 3)
         return (keep + come.astype(jnp.float32)).astype(jnp.bfloat16)
 
-    kept0, come0, _ = products(down0, parts[0], THIRDS)
-    down1, kept0 = tie((down1, kept0))
-    kept1, come1, sent1 = products(down1, parts[1], THIRDS)
-    kept0, _ = tie((kept0, sent1))
+    kept0, come0 = products(down0, parts[0], THIRDS)
+    down1, kept0, come0[:2] = tie((down1, kept0, come0[:2]))
+    kept1, come1 = products(down1, parts[1], THIRDS)
     kept0, come0 = stage(kept0, come0, 1, THIRDS)
     kept1, come1 = stage(kept1, come1, 1, THIRDS)
     kept0, come0 = stage(kept0, come0, 2, THIRDS)

time: 359 us -> 367 us (1.022)
  waiting for transfers between devices: 235 us -> 243 us
    ppermute x27, waiting for transfers between devices: 198 us -> 208 us  [swap(): return lax.ppermute(value, 'ep', [(i, i ^ 1 << bit) for i in range(size)])]
    all_to_all x2, waiting for transfers between devices: 33.9 us -> 29.9 us  [move(): return lax.all_to_all(packed, 'ep', 0, 0, tiled=True)]
  transfers between devices with their start and end apart: 36 -> 36, of which waited for: 21 -> 16; matrix products, arithmetic and copies ran while one was open for 2% -> 2% of each run, Pallas kernels for 12% -> 11%
where the time goes in v7:
time: 367 us; the launch traced here: 361 us
  waiting for transfers between devices  243 us (66%)
  starting transfers between devices  49.9 us (14%)
  Pallas kernels  43.8 us (12%)
  local copies, waits for them, and re-layouts  17.9 us (5%)
  other arithmetic  6.09 us (2%)
    ppermute x27, waiting for transfers between devices, swap(): return lax.ppermute(value, 'ep', [(i, i ^ 1 << bit) for i in range(size)])  208 us
    all_to_all x2, waiting for transfers between devices, move(): return lax.all_to_all(packed, 'ep', 0, 0, tiled=True)  29.9 us
    ppermute x27, starting transfers between devices, swap(): return lax.ppermute(value, 'ep', [(i, i ^ 1 << bit) for i in range(size)])  27.5 us
    pallas_call x1, Pallas kernels, hidden_units(): pl.pallas_call(hidden_kernel, grid=(4,), out_shape=jax.ShapeDtypeStruct((...  25.6 us
    all_to_all x2, starting transfers between devices, move(): return lax.all_to_all(packed, 'ep', 0, 0, tiled=True)  20.8 us
    unnamed x39, local copies, waits for them, and re-layouts  13.1 us
    pallas_call x4, Pallas kernels, down_product(): pl.pallas_call(functools.partial(down_kernel, rows, side, orders), out_sh...  9.88 us
  transfers between devices with their start and end apart: 36, of which 16 were waited for; matrix products, arithmetic and copies ran while one was open for 2% of the time, Pallas kernels for 11%

profile of v7, /device:TPU:14, one launch (start us, length us, event | category | flops | bytes accessed | tf_op | source)
XLA Modules:
  0.0 361.2 jit_solution(996114620542118048)
XLA Ops:
  0.5 2.6 collective-permute-start.1
  3.0 0.9 select_reduce_fusion.4
  4.3 0.7 select_reduce_fusion.1
  5.0 18.4 %collective-permute-done.1 = bf16[128,1792]{1,0:T(8,128)(2,1)S(1)} collective-permute-done((bf16[128,1792]{1,0:T(8,128)(2,1)}, bf16[128,1792]{1,0:T(8,128)(2,1)S(1)}, u32[]{:S(2)}, u32[]{:S(2)}) %collective-permute-start.1) | collective-permute-done | bytes 458784 | tf_op jit(solution)/shard_map/ppermute | solution.py:332
  23.4 1.6 collective-permute-start.2
  25.1 0.8 broadcast_compare_fusion
  25.9 0.9 select_reduce_fusion.share_ref
  26.9 2.0 copy-done
  28.9 2.0 copy-done.2
  30.9 2.0 copy-done.3
  33.0 5.1 %pack_first.1 = bf16[16,1920,128]{2,1,0:T(8,128)(2,1)} custom-call(s32[14]{0:T(128)S(1)} %select_reduce_fusion.3.list_ref, bf16[16,224,512]{2,1,0:T(8,128)(2,1)S(1)} %copy-done.2, bf16[16,224,512]{2,1,0:T(8,128)(2,1)S(1)} %copy-done.3, bf16[16,224,512]{2,1,0:T(8,128)(2,1)S(1)} %copy-done, f32[16,16,128]{2,1,0:T(8,128)S(1)} %select_reduce_fusion.share_ref), custom_call_target="tpu_custom_call" | custom-call | tf_op jit(solution)/shard_map/pack_first/pallas_call | solution.py:113
  38.1 6.3 %all-to-all-start = ((bf16[16,1920,128]{2,1,0:T(8,128)(2,1)}), bf16[16,1920,128]{2,1,0:T(8,128)(2,1)}, u32[]{:S(2)}, u32[]{:S(2)}) async-start(bf16[16,1920,128]{2,1,0:T(8,128)(2,1)} %pack_first.1), calls=%async_computation | async-start | bytes 15728640 | tf_op jit(solution)/shard_map/all_to_all | solution.py:381
  44.8 0.6 collective-permute-start.3
  45.4 0.6 collective-permute-start.5
  46.0 58.9 %collective-permute-done.3 = bf16[512,896]{1,0:T(8,128)(2,1)S(1)} collective-permute-done((bf16[512,896]{1,0:T(8,128)(2,1)S(1)}, bf16[512,896]{1,0:T(8,128)(2,1)S(1)}, u32[]{:S(2)}, u32[]{:S(2)}) %collective-permute-start.3) | collective-permute-done | bytes 917536 | tf_op jit(solution)/shard_map/ppermute | solution.py:332
  105.0 0.6 collective-permute-start.4
  105.6 1.4 pad_maximum_fusion.1.refs_2_
  107.6 72.6 %collective-permute-done.4.refs_1_ = bf16[1024,896]{1,0:T(8,128)(2,1)} collective-permute-done((bf16[1024,896]{1,0:T(8,128)(2,1)S(1)}, bf16[1024,896]{1,0:T(8,128)(2,1)}, u32[]{:S(2)}, u32[]{:S(2)}) %collective-permute-start.4) | collective-permute-done | bytes 1835040 | tf_op jit(solution)/shard_map/ppermute | solution.py:332
  180.7 2.0 copy-done.1
  182.7 2.1 pack_rest.1
  184.9 0.6 pad_add_fusion.at_ref
  185.5 29.9 %all-to-all-done.refs_8_ = bf16[16,1920,128]{2,1,0:T(8,128)(2,1)} async-done(((bf16[16,1920,128]{2,1,0:T(8,128)(2,1)}), bf16[16,1920,128]{2,1,0:T(8,128)(2,1)}, u32[]{:S(2)}, u32[]{:S(2)}) %all-to-all-start) | async-done | bytes 7864352 | tf_op jit(solution)/shard_map/all_to_all | solution.py:381
  215.3 14.4 %all-to-all-start.1 = ((bf16[16,448,128]{2,1,0:T(8,128)(2,1)}), bf16[16,448,128]{2,1,0:T(8,128)(2,1)}, u32[]{:S(2)}, u32[]{:S(2)}) async-start(bf16[16,448,128]{2,1,0:T(8,128)(2,1)} %pack_rest.1), calls=%async_computation.1 | async-start | bytes 3670016 | tf_op jit(solution)/shard_map/all_to_all | solution.py:381
  229.8 25.6 %hidden.1.own_h = bf16[2048,512]{1,0:T(8,128)(2,1)} custom-call(s32[2]{0:T(128)} %pad_add_fusion.at_ref, bf16[1024,896]{1,0:T(8,128)(2,1)} %copy-done.16, bf16[1024,896]{1,0:T(8,128)(2,1)} %collective-permute-done.4.refs_1_, bf16[1024,896]{1,0:T(8,128)(2,1)} %pad_maximum_fusion.1.refs_2_, bf16[1024,896]{1,0:T(8,128)(2,1)} %collective-permute-done.6.refs_3_, ...), custom_call_target="tpu_custom_call" | custom-call | flops 15032385536 | bytes 25165824 | tf_op jit(solution)/shard_map/hidden/pallas_call | solution.py:208
  255.4 1.4 slice.11
  257.5 3.0 collective-permute-done.12.other_ref
  260.5 1.9 down_send.2
  262.5 0.6 collective-permute-start.13
  263.1 0.6 collective-permute-start.14
  263.7 1.6 copy-done.11
  265.3 1.9 down_keep.2
  267.2 14.2 %collective-permute-done.13.refs_1_ = bf16[1024,256]{1,0:T(8,128)(2,1)S(1)} collective-permute-done((bf16[1024,256]{1,0:T(8,128)(2,1)S(1)}, bf16[1024,256]{1,0:T(8,128)(2,1)S(1)}, u32[]{:S(2)}, u32[]{:S(2)}) %collective-permute-start.13) | collective-permute-done | bytes 524320 | tf_op jit(solution)/shard_map/ppermute | solution.py:332
  281.4 0.8 copy-done.4
  282.3 0.8 copy-done.6
  283.1 1.7 constant_dynamic-slice_fusion
  284.9 2.5 collective-permute-done.23.other_ref
  287.4 1.6 copy-done.12
  289.0 3.0 down_send.3
  292.0 0.6 collective-permute-start.24
  292.7 0.6 collective-permute-start.25
  293.2 2.0 collective-permute-start.26
  295.3 12.8 %collective-permute-done.15.refs_5_ = bf16[1024,256]{1,0:T(8,128)(2,1)S(1)} collective-permute-done((bf16[1024,256]{1,0:T(8,128)(2,1)S(1)}, bf16[1024,256]{1,0:T(8,128)(2,1)S(1)}, u32[]{:S(2)}, u32[]{:S(2)}) %collective-permute-start.15) | collective-permute-done | bytes 524320 | tf_op jit(solution)/shard_map/ppermute | solution.py:332
  308.3 1.5 collective-permute-start.16
  309.9 3.0 down_keep.3
  312.9 5.0 %collective-permute-done.26.refs_5_ = bf16[1024,256]{1,0:T(8,128)(2,1)S(1)} collective-permute-done((bf16[1024,256]{1,0:T(8,128)(2,1)S(1)}, bf16[1024,256]{1,0:T(8,128)(2,1)S(1)}, u32[]{:S(2)}, u32[]{:S(2)}) %collective-permute-start.26) | collective-permute-done | bytes 524320 | tf_op jit(solution)/shard_map/ppermute | solution.py:332
  318.2 1.5 collective-permute-start.27
  320.0 1.7 collective-permute-start.17
  321.8 1.5 collective-permute-start.18
  323.2 0.6 collective-permute-start.29
  323.8 11.0 %collective-permute-done.17.refs_3_ = bf16[512,256]{1,0:T(8,128)(2,1)S(1)} collective-permute-done((bf16[512,256]{1,0:T(8,128)(2,1)S(1)}, bf16[512,256]{1,0:T(8,128)(2,1)S(1)}, u32[]{:S(2)}, u32[]{:S(2)}) %collective-permute-start.17) | collective-permute-done | bytes 262176 | tf_op jit(solution)/shard_map/ppermute | solution.py:332
  334.9 0.7 collective-permute-start.19
  335.6 1.5 collective-permute-start.20
  337.7 1.5 collective-permute-start.30
  339.2 0.6 collective-permute-start.31
  339.8 1.0 collective-permute-done.19.refs_1_
  340.8 0.8 collective-permute-done.20.refs_3_
  341.7 0.7 collective-permute-done.21.refs_5_
  342.4 1.0 collective-permute-start.22
  343.4 1.7 collective-permute-start.32
  345.1 3.2 collective-permute-done.32.refs_5_
  348.4 2.1 collective-permute-start.33
  350.5 2.2 collective-permute-done.22
  352.9 7.0 %collective-permute-done.33 = bf16[128,1024]{1,0:T(8,128)(2,1)S(1)} collective-permute-done((bf16[128,1024]{1,0:T(8,128)(2,1)S(1)}, bf16[128,1024]{1,0:T(8,128)(2,1)S(1)}, u32[]{:S(2)}, u32[]{:S(2)}) %collective-permute-start.33) | collective-permute-done | bytes 262176 | tf_op jit(solution)/shard_map/ppermute | solution.py:332
  360.2 1.0 copy.15
  (82 shorter events, 5.5 us)
Async XLA Ops:
  0.0 38.1 %collective-permute-start = (bf16[128,1792]{1,0:T(8,128)(2,1)}, bf16[128,1792]{1,0:T(8,128)(2,1)S(1)}, u32[]{:S(2)}, u32[]{:S(2)}) collective-permute-start(bf16[128,1792]{1,0:T(8,128)(2,1)} %param.9), channel_id=1, source_target_pairs={{0,8},{2,10},{4,12},{6,14},{8,0},{10,2},{12,4},{14,6},{16,24},{18,... | collective-permute-start | bytes 1376264 | tf_op jit(solution)/shard_map/ppermute | solution.py:332
  0.5 23.0 %collective-permute-start.1 = (bf16[128,1792]{1,0:T(8,128)(2,1)}, bf16[128,1792]{1,0:T(8,128)(2,1)S(1)}, u32[]{:S(2)}, u32[]{:S(2)}) collective-permute-start(bf16[128,1792]{1,0:T(8,128)(2,1)} %param.9), channel_id=1, source_target_pairs={{0,16},{2,18},{4,20},{6,22},{8,24},{10,26},{12,28},{14,30},{16,0},... | collective-permute-start | bytes 1376264 | tf_op jit(solution)/shard_map/ppermute | solution.py:332
  23.4 14.7 %collective-permute-start.2 = (bf16[128,1792]{1,0:T(8,128)(2,1)S(1)}, bf16[128,1792]{1,0:T(8,128)(2,1)S(1)}, u32[]{:S(2)}, u32[]{:S(2)}) collective-permute-start(bf16[128,1792]{1,0:T(8,128)(2,1)S(1)} %collective-permute-done.1), channel_id=1, source_target_pairs={{0,8},{2,10},{4,12},{6,14},{8,0},{10,2},{12,4},{14,6},{16,24},{18,... | collective-permute-start | bytes 1376264 | tf_op jit(solution)/shard_map/ppermute | solution.py:332
  26.9 2.0 copy-start
  28.9 2.0 copy-start.2
  30.9 2.0 copy-start.3
  38.1 6.4 %copy-start.17 = (bf16[128,1792]{1,0:T(8,128)(2,1)S(1)}, bf16[128,1792]{1,0:T(8,128)(2,1)}, u32[]{:S(2)}) copy-start(bf16[128,1792]{1,0:T(8,128)(2,1)} %param.9) | copy-start | bytes 1376260
  38.1 177.2 %all-to-all-start = ((bf16[16,1920,128]{2,1,0:T(8,128)(2,1)}), bf16[16,1920,128]{2,1,0:T(8,128)(2,1)}, u32[]{:S(2)}, u32[]{:S(2)}) async-start(bf16[16,1920,128]{2,1,0:T(8,128)(2,1)} %pack_first.1), calls=%async_computation | async-start | bytes 15728640 | tf_op jit(solution)/shard_map/all_to_all | solution.py:381
  44.8 60.1 %collective-permute-start.3 = (bf16[512,896]{1,0:T(8,128)(2,1)S(1)}, bf16[512,896]{1,0:T(8,128)(2,1)S(1)}, u32[]{:S(2)}, u32[]{:S(2)}) collective-permute-start(bf16[512,896]{1,0:T(8,128)(2,1)S(1)} %get-tuple-element.140), channel_id=1, source_target_pairs={{0,4},{2,6},{4,0},{6,2},{8,12},{10,14},{12,8},{14,10},{16,20},{18,... | collective-permute-start | bytes 2752520 | tf_op jit(solution)/shard_map/ppermute | solution.py:332
  45.4 60.2 %collective-permute-start.5 = (bf16[512,896]{1,0:T(8,128)(2,1)S(1)}, bf16[512,896]{1,0:T(8,128)(2,1)S(1)}, u32[]{:S(2)}, u32[]{:S(2)}) collective-permute-start(bf16[512,896]{1,0:T(8,128)(2,1)S(1)} %get-tuple-element.139), channel_id=1, source_target_pairs={{0,2},{2,0},{4,6},{6,4},{8,10},{10,8},{12,14},{14,12},{16,18},{18,... | collective-permute-start | bytes 2752520 | tf_op jit(solution)/shard_map/ppermute | solution.py:332
  105.0 2.1 copy-start.16
  105.0 75.2 %collective-permute-start.4 = (bf16[1024,896]{1,0:T(8,128)(2,1)S(1)}, bf16[1024,896]{1,0:T(8,128)(2,1)}, u32[]{:S(2)}, u32[]{:S(2)}) collective-permute-start(bf16[1024,896]{1,0:T(8,128)(2,1)S(1)} %pad_maximum_fusion.refs_0_), channel_id=1, source_target_pairs={{0,2},{2,0},{4,6},{6,4},{8,10},{10,8},{12,14},{14,12},{16,18},{18,... | collective-permute-start | bytes 5505032 | tf_op jit(solution)/shard_map/ppermute | solution.py:332
  107.0 73.1 %collective-permute-start.6 = (bf16[1024,896]{1,0:T(8,128)(2,1)}, bf16[1024,896]{1,0:T(8,128)(2,1)}, u32[]{:S(2)}, u32[]{:S(2)}) collective-permute-start(bf16[1024,896]{1,0:T(8,128)(2,1)} %pad_maximum_fusion.1.refs_2_), channel_id=1, source_target_pairs={{0,4},{2,6},{4,0},{6,2},{8,12},{10,14},{12,8},{14,10},{16,20},{18,... | collective-permute-start | bytes 5505032 | tf_op jit(solution)/shard_map/ppermute | solution.py:332
  107.0 122.7 %collective-permute-start.7 = (bf16[1024,896]{1,0:T(8,128)(2,1)S(1)}, bf16[1024,896]{1,0:T(8,128)(2,1)}, u32[]{:S(2)}, u32[]{:S(2)}) collective-permute-start(bf16[1024,896]{1,0:T(8,128)(2,1)S(1)} %pad_maximum_fusion.refs_0_), channel_id=1, source_target_pairs={{0,1},{1,0},{2,3},{3,2},{4,5},{5,4},{6,7},{7,6},{8,9},{9,8},{10,11... | collective-permute-start | bytes 5505032 | tf_op jit(solution)/shard_map/ppermute | solution.py:378
  107.1 122.7 %collective-permute-start.9 = (bf16[1024,896]{1,0:T(8,128)(2,1)}, bf16[1024,896]{1,0:T(8,128)(2,1)}, u32[]{:S(2)}, u32[]{:S(2)}) collective-permute-start(bf16[1024,896]{1,0:T(8,128)(2,1)} %pad_maximum_fusion.1.refs_2_), channel_id=1, source_target_pairs={{0,1},{1,0},{2,3},{3,2},{4,5},{5,4},{6,7},{7,6},{8,9},{9,8},{10,11... | collective-permute-start | bytes 5505032 | tf_op jit(solution)/shard_map/ppermute | solution.py:378
  180.2 49.6 %collective-permute-start.8 = (bf16[1024,896]{1,0:T(8,128)(2,1)}, bf16[1024,896]{1,0:T(8,128)(2,1)}, u32[]{:S(2)}, u32[]{:S(2)}) collective-permute-start(bf16[1024,896]{1,0:T(8,128)(2,1)} %collective-permute-done.4.refs_1_), channel_id=1, source_target_pairs={{0,1},{1,0},{2,3},{3,2},{4,5},{5,4},{6,7},{7,6},{8,9},{9,8},{10,11... | collective-permute-start | bytes 5505032 | tf_op jit(solution)/shard_map/ppermute | solution.py:378
  180.2 49.6 %collective-permute-start.10 = (bf16[1024,896]{1,0:T(8,128)(2,1)}, bf16[1024,896]{1,0:T(8,128)(2,1)}, u32[]{:S(2)}, u32[]{:S(2)}) collective-permute-start(bf16[1024,896]{1,0:T(8,128)(2,1)} %collective-permute-done.6.refs_3_), channel_id=1, source_target_pairs={{0,1},{1,0},{2,3},{3,2},{4,5},{5,4},{6,7},{7,6},{8,9},{9,8},{10,11... | collective-permute-start | bytes 5505032 | tf_op jit(solution)/shard_map/ppermute | solution.py:378
  180.7 2.0 copy-start.1
  215.3 67.8 %all-to-all-start.1 = ((bf16[16,448,128]{2,1,0:T(8,128)(2,1)}), bf16[16,448,128]{2,1,0:T(8,128)(2,1)}, u32[]{:S(2)}, u32[]{:S(2)}) async-start(bf16[16,448,128]{2,1,0:T(8,128)(2,1)} %pack_rest.1), calls=%async_computation.1 | async-start | bytes 3670016 | tf_op jit(solution)/shard_map/all_to_all | solution.py:381
  255.4 5.1 %collective-permute-start.11 = (bf16[2048,512]{1,0:T(8,128)(2,1)}, bf16[2048,512]{1,0:T(8,128)(2,1)S(1)}, u32[]{:S(2)}, u32[]{:S(2)}) collective-permute-start(bf16[2048,512]{1,0:T(8,128)(2,1)} %hidden.1.own_h), channel_id=1, source_target_pairs={{0,1},{1,0},{2,3},{3,2},{4,5},{5,4},{6,7},{7,6},{8,9},{9,8},{10,11... | collective-permute-start | bytes 6291464 | tf_op jit(solution)/shard_map/ppermute | solution.py:378
  256.8 3.7 %copy-start.8 = (bf16[2048,512]{1,0:T(8,128)(2,1)S(1)}, bf16[2048,512]{1,0:T(8,128)(2,1)}, u32[]{:S(2)}) copy-start(bf16[2048,512]{1,0:T(8,128)(2,1)} %hidden.1.own_h) | copy-start | bytes 6291460
  257.0 3.6 collective-permute-start.12
  260.5 1.9 copy-start.10
  262.5 4.7 %copy-start.14 = (bf16[1024,256]{1,0:T(8,128)(2,1)}, bf16[1024,256]{1,0:T(8,128)(2,1)S(1)}, u32[]{:S(2)}) copy-start(bf16[1024,256]{1,0:T(8,128)(2,1)S(1)} %get-tuple-element.94) | copy-start | bytes 1572868
  262.5 18.9 %collective-permute-start.13 = (bf16[1024,256]{1,0:T(8,128)(2,1)S(1)}, bf16[1024,256]{1,0:T(8,128)(2,1)S(1)}, u32[]{:S(2)}, u32[]{:S(2)}) collective-permute-start(bf16[1024,256]{1,0:T(8,128)(2,1)S(1)} %get-tuple-element.87), channel_id=1, source_target_pairs={{0,2},{2,0},{4,6},{6,4},{8,10},{10,8},{12,14},{14,12},{16,18},{18,... | collective-permute-start | bytes 1572872 | tf_op jit(solution)/shard_map/ppermute | solution.py:332
  263.1 19.2 %collective-permute-start.14 = (bf16[1024,256]{1,0:T(8,128)(2,1)S(1)}, bf16[1024,256]{1,0:T(8,128)(2,1)S(1)}, u32[]{:S(2)}, u32[]{:S(2)}) collective-permute-start(bf16[1024,256]{1,0:T(8,128)(2,1)S(1)} %get-tuple-element.88), channel_id=1, source_target_pairs={{0,4},{2,6},{4,0},{6,2},{8,12},{10,14},{12,8},{14,10},{16,20},{18,... | collective-permute-start | bytes 1572872 | tf_op jit(solution)/shard_map/ppermute | solution.py:332
  263.7 1.6 copy-start.11
  281.4 0.8 copy-start.4
  282.3 0.8 copy-start.6
  283.1 4.3 %copy-start.9 = (bf16[2048,512]{1,0:T(8,128)(2,1)S(1)}, bf16[2048,512]{1,0:T(8,128)(2,1)}, u32[]{:S(2)}) copy-start(bf16[2048,512]{1,0:T(8,128)(2,1)} %hidden.1.own_h) | copy-start | bytes 6291460
  284.8 2.5 collective-permute-start.23
  287.4 1.6 copy-start.12
  289.0 4.3 %copy-start.15 = (bf16[1024,256]{1,0:T(8,128)(2,1)S(1)}, bf16[1024,256]{1,0:T(8,128)(2,1)}, u32[]{:S(2)}) copy-start(bf16[1024,256]{1,0:T(8,128)(2,1)} %copy-done.14) | copy-start | bytes 1572868
  289.0 19.1 %copy-start.5 = (bf16[1024,256]{1,0:T(8,128)(2,1)S(1)}, bf16[1024,256]{1,0:T(8,128)(2,1)}, u32[]{:S(2)}) copy-start(bf16[1024,256]{1,0:T(8,128)(2,1)} %copy-done.4) | copy-start | bytes 1572868
  289.0 19.1 %copy-start.7 = (bf16[1024,256]{1,0:T(8,128)(2,1)S(1)}, bf16[1024,256]{1,0:T(8,128)(2,1)}, u32[]{:S(2)}) copy-start(bf16[1024,256]{1,0:T(8,128)(2,1)} %copy-done.6) | copy-start | bytes 1572868
  292.0 17.8 %copy-start.13 = (bf16[2048,512]{1,0:T(8,128)(2,1)S(1)}, bf16[2048,512]{1,0:T(8,128)(2,1)}, u32[]{:S(2)}) copy-start(bf16[2048,512]{1,0:T(8,128)(2,1)} %copy-done.10) | copy-start | bytes 6291460
  292.0 25.8 %collective-permute-start.24 = (bf16[1024,384]{1,0:T(8,128)(2,1)S(1)}, bf16[1024,384]{1,0:T(8,128)(2,1)S(1)}, u32[]{:S(2)}, u32[]{:S(2)}) collective-permute-start(bf16[1024,384]{1,0:T(8,128)(2,1)S(1)} %get-tuple-element.118), channel_id=1, source_target_pairs={{0,2},{2,0},{4,6},{6,4},{8,10},{10,8},{12,14},{14,12},{16,18},{18,... | collective-permute-start | bytes 2359304 | tf_op jit(solution)/shard_map/ppermute | solution.py:332
  292.7 25.2 %collective-permute-start.25 = (bf16[1024,384]{1,0:T(8,128)(2,1)S(1)}, bf16[1024,384]{1,0:T(8,128)(2,1)S(1)}, u32[]{:S(2)}, u32[]{:S(2)}) collective-permute-start(bf16[1024,384]{1,0:T(8,128)(2,1)S(1)} %get-tuple-element.120), channel_id=1, source_target_pairs={{0,4},{2,6},{4,0},{6,2},{8,12},{10,14},{12,8},{14,10},{16,20},{18,... | collective-permute-start | bytes 2359304 | tf_op jit(solution)/shard_map/ppermute | solution.py:332
  293.2 14.8 %collective-permute-start.15 = (bf16[1024,256]{1,0:T(8,128)(2,1)S(1)}, bf16[1024,256]{1,0:T(8,128)(2,1)S(1)}, u32[]{:S(2)}, u32[]{:S(2)}) collective-permute-start(bf16[1024,256]{1,0:T(8,128)(2,1)S(1)} %copy-done.15), channel_id=1, source_target_pairs={{0,8},{2,10},{4,12},{6,14},{8,0},{10,2},{12,4},{14,6},{16,24},{18,... | collective-permute-start | bytes 1572872 | tf_op jit(solution)/shard_map/ppermute | solution.py:332
  293.2 24.6 %collective-permute-start.26 = (bf16[1024,256]{1,0:T(8,128)(2,1)S(1)}, bf16[1024,256]{1,0:T(8,128)(2,1)S(1)}, u32[]{:S(2)}, u32[]{:S(2)}) collective-permute-start(bf16[1024,256]{1,0:T(8,128)(2,1)S(1)} %get-tuple-element.122), channel_id=1, source_target_pairs={{0,8},{2,10},{4,12},{6,14},{8,0},{10,2},{12,4},{14,6},{16,24},{18,... | collective-permute-start | bytes 1572872 | tf_op jit(solution)/shard_map/ppermute | solution.py:332
  308.3 14.9 %collective-permute-start.16 = (bf16[512,256]{1,0:T(8,128)(2,1)S(1)}, bf16[512,256]{1,0:T(8,128)(2,1)S(1)}, u32[]{:S(2)}, u32[]{:S(2)}) collective-permute-start(bf16[512,256]{1,0:T(8,128)(2,1)S(1)} %get-tuple-element.96), channel_id=1, source_target_pairs={{0,4},{2,6},{4,0},{6,2},{8,12},{10,14},{12,8},{14,10},{16,20},{18,... | collective-permute-start | bytes 786440 | tf_op jit(solution)/shard_map/ppermute | solution.py:332
  318.2 19.3 %collective-permute-start.27 = (bf16[512,384]{1,0:T(8,128)(2,1)S(1)}, bf16[512,384]{1,0:T(8,128)(2,1)S(1)}, u32[]{:S(2)}, u32[]{:S(2)}) collective-permute-start(bf16[512,384]{1,0:T(8,128)(2,1)S(1)} %get-tuple-element.124), channel_id=1, source_target_pairs={{0,4},{2,6},{4,0},{6,2},{8,12},{10,14},{12,8},{14,10},{16,20},{18,... | collective-permute-start | bytes 1179656 | tf_op jit(solution)/shard_map/ppermute | solution.py:332
  319.7 17.8 %collective-permute-start.28 = (bf16[512,384]{1,0:T(8,128)(2,1)S(1)}, bf16[512,384]{1,0:T(8,128)(2,1)S(1)}, u32[]{:S(2)}, u32[]{:S(2)}) collective-permute-start(bf16[512,384]{1,0:T(8,128)(2,1)S(1)} %get-tuple-element.126), channel_id=1, source_target_pairs={{0,8},{2,10},{4,12},{6,14},{8,0},{10,2},{12,4},{14,6},{16,24},{18,... | collective-permute-start | bytes 1179656 | tf_op jit(solution)/shard_map/ppermute | solution.py:332
  320.0 14.7 %collective-permute-start.17 = (bf16[512,256]{1,0:T(8,128)(2,1)S(1)}, bf16[512,256]{1,0:T(8,128)(2,1)S(1)}, u32[]{:S(2)}, u32[]{:S(2)}) collective-permute-start(bf16[512,256]{1,0:T(8,128)(2,1)S(1)} %get-tuple-element.98), channel_id=1, source_target_pairs={{0,8},{2,10},{4,12},{6,14},{8,0},{10,2},{12,4},{14,6},{16,24},{18,... | collective-permute-start | bytes 786440 | tf_op jit(solution)/shard_map/ppermute | solution.py:332
  321.8 13.0 %collective-permute-start.18 = (bf16[512,256]{1,0:T(8,128)(2,1)S(1)}, bf16[512,256]{1,0:T(8,128)(2,1)S(1)}, u32[]{:S(2)}, u32[]{:S(2)}) collective-permute-start(bf16[512,256]{1,0:T(8,128)(2,1)S(1)} %get-tuple-element.100), channel_id=1, source_target_pairs={{0,2},{2,0},{4,6},{6,4},{8,10},{10,8},{12,14},{14,12},{16,18},{18,... | collective-permute-start | bytes 786440 | tf_op jit(solution)/shard_map/ppermute | solution.py:332
  323.2 13.8 %collective-permute-start.29 = (bf16[512,256]{1,0:T(8,128)(2,1)S(1)}, bf16[512,256]{1,0:T(8,128)(2,1)S(1)}, u32[]{:S(2)}, u32[]{:S(2)}) collective-permute-start(bf16[512,256]{1,0:T(8,128)(2,1)S(1)} %get-tuple-element.128), channel_id=1, source_target_pairs={{0,2},{2,0},{4,6},{6,4},{8,10},{10,8},{12,14},{14,12},{16,18},{18,... | collective-permute-start | bytes 786440 | tf_op jit(solution)/shard_map/ppermute | solution.py:332
  334.9 5.9 %collective-permute-start.19 = (bf16[256,256]{1,0:T(8,128)(2,1)S(1)}, bf16[256,256]{1,0:T(8,128)(2,1)S(1)}, u32[]{:S(2)}, u32[]{:S(2)}) collective-permute-start(bf16[256,256]{1,0:T(8,128)(2,1)S(1)} %get-tuple-element.102), channel_id=1, source_target_pairs={{0,8},{2,10},{4,12},{6,14},{8,0},{10,2},{12,4},{14,6},{16,24},{18,... | collective-permute-start | bytes 393224 | tf_op jit(solution)/shard_map/ppermute | solution.py:332
  335.6 6.1 %collective-permute-start.20 = (bf16[256,256]{1,0:T(8,128)(2,1)S(1)}, bf16[256,256]{1,0:T(8,128)(2,1)S(1)}, u32[]{:S(2)}, u32[]{:S(2)}) collective-permute-start(bf16[256,256]{1,0:T(8,128)(2,1)S(1)} %get-tuple-element.104), channel_id=1, source_target_pairs={{0,2},{2,0},{4,6},{6,4},{8,10},{10,8},{12,14},{14,12},{16,18},{18,... | collective-permute-start | bytes 393224 | tf_op jit(solution)/shard_map/ppermute | solution.py:332
  337.0 5.3 %collective-permute-start.21 = (bf16[256,256]{1,0:T(8,128)(2,1)S(1)}, bf16[256,256]{1,0:T(8,128)(2,1)S(1)}, u32[]{:S(2)}, u32[]{:S(2)}) collective-permute-start(bf16[256,256]{1,0:T(8,128)(2,1)S(1)} %get-tuple-element.106), channel_id=1, source_target_pairs={{0,4},{2,6},{4,0},{6,2},{8,12},{10,14},{12,8},{14,10},{16,20},{18,... | collective-permute-start | bytes 393224 | tf_op jit(solution)/shard_map/ppermute | solution.py:332
  337.7 10.6 %collective-permute-start.30 = (bf16[256,384]{1,0:T(8,128)(2,1)S(1)}, bf16[256,384]{1,0:T(8,128)(2,1)S(1)}, u32[]{:S(2)}, u32[]{:S(2)}) collective-permute-start(bf16[256,384]{1,0:T(8,128)(2,1)S(1)} %get-tuple-element.130), channel_id=1, source_target_pairs={{0,8},{2,10},{4,12},{6,14},{8,0},{10,2},{12,4},{14,6},{16,24},{18,... | collective-permute-start | bytes 589832 | tf_op jit(solution)/shard_map/ppermute | solution.py:332
  339.2 9.1 %collective-permute-start.31 = (bf16[256,384]{1,0:T(8,128)(2,1)S(1)}, bf16[256,384]{1,0:T(8,128)(2,1)S(1)}, u32[]{:S(2)}, u32[]{:S(2)}) collective-permute-start(bf16[256,384]{1,0:T(8,128)(2,1)S(1)} %get-tuple-element.132), channel_id=1, source_target_pairs={{0,2},{2,0},{4,6},{6,4},{8,10},{10,8},{12,14},{14,12},{16,18},{18,... | collective-permute-start | bytes 589832 | tf_op jit(solution)/shard_map/ppermute | solution.py:332
  342.4 10.3 %collective-permute-start.22 = (bf16[128,768]{1,0:T(8,128)(2,1)S(1)}, bf16[128,768]{1,0:T(8,128)(2,1)S(1)}, u32[]{:S(2)}, u32[]{:S(2)}) collective-permute-start(bf16[128,768]{1,0:T(8,128)(2,1)S(1)} %get-tuple-element.108), channel_id=1, source_target_pairs={{0,16},{2,18},{4,20},{6,22},{8,24},{10,26},{12,28},{14,30},{16,0},... | collective-permute-start | bytes 589832 | tf_op jit(solution)/shard_map/ppermute | solution.py:332
  343.4 5.0 %collective-permute-start.32 = (bf16[256,256]{1,0:T(8,128)(2,1)S(1)}, bf16[256,256]{1,0:T(8,128)(2,1)S(1)}, u32[]{:S(2)}, u32[]{:S(2)}) collective-permute-start(bf16[256,256]{1,0:T(8,128)(2,1)S(1)} %get-tuple-element.134), channel_id=1, source_target_pairs={{0,4},{2,6},{4,0},{6,2},{8,12},{10,14},{12,8},{14,10},{16,20},{18,... | collective-permute-start | bytes 393224 | tf_op jit(solution)/shard_map/ppermute | solution.py:332
  348.4 11.5 %collective-permute-start.33 = (bf16[128,1024]{1,0:T(8,128)(2,1)S(1)}, bf16[128,1024]{1,0:T(8,128)(2,1)S(1)}, u32[]{:S(2)}, u32[]{:S(2)}) collective-permute-start(bf16[128,1024]{1,0:T(8,128)(2,1)S(1)} %get-tuple-element.136), channel_id=1, source_target_pairs={{0,16},{2,18},{4,20},{6,22},{8,24},{10,26},{12,28},{14,30},{16,0},... | collective-permute-start | bytes 786440 | tf_op jit(solution)/shard_map/ppermute | solution.py:332

commit v8 on v5

--- a/solution.py
+++ b/solution.py
@@ -392,19 +392,47 @@
     belongs = slot_place[None, None, :, None] == places[:, :, None, None]
     share = jnp.sum(jnp.where(belongs, share[None, None], 0.0), axis=2)
 
+    def diagonal(value):
+        return lax.ppermute(value, "ep", [(i, i ^ 3) for i in range(devices)])
+
+    mid = tokens.shape[1] // 2
     near, far = swap(tokens, 2), swap(tokens, 3)
+    plane = [swap(tokens, 0), swap(tokens, 1), diagonal(tokens)]
+    pair = jnp.concatenate([far, near], axis=0)
     corner = swap(far, 2)
+    pair_y, pair_x = swap(pair[:, :mid], 1), swap(pair[:, mid:], 0)
     parts = (128, 96)
     packed = pack_first(listing, gate_proj, up_proj, down_proj, parts[0], share, devices)
-    packed, near, far, corner = tie((packed, near, far, corner))
+    packed, plane, pair, corner, pair_y, pair_x = tie(
+        (packed, plane, pair, corner, pair_y, pair_x)
+    )
 
     moved = move(packed)
-    mid = tokens.shape[1] // 2
-    rows = jnp.concatenate([tokens, far, near, corner], axis=0)
-    first, second = rows[:, :mid], rows[:, mid:]
-    first = jnp.concatenate([first, swap(first, 1)], axis=0)
-    second = jnp.concatenate([second, swap(second, 0)], axis=0)
-    pieces = [first, swap(first, 0), second, swap(second, 1)]
+    corner_a, corner_b = corner[:, :mid], corner[:, mid:]
+    cross = diagonal(corner)
+    most_a = swap(jnp.concatenate([pair[:, :mid], corner_a, pair_y], axis=0), 0)
+    most_b = swap(jnp.concatenate([pair[:, mid:], corner_b, pair_x], axis=0), 1)
+    corner_y, corner_x = swap(corner_a, 1), swap(corner_b, 0)
+    x_own, y_own, xy_own = plane
+
+    def lay(*values):
+        return jnp.concatenate(values, axis=0)
+
+    at_pair, at_corner = slice(0, 2 * block), slice(2 * block, 3 * block)
+    at_other = slice(3 * block, 5 * block)
+    first, second = slice(0, mid), slice(mid, 2 * mid)
+    pieces = [
+        lay(tokens[:, first], pair[:, first], corner_a, y_own[:, first], pair_y, corner_y),
+        lay(
+            x_own[:, first], most_a[at_pair], most_a[at_corner],
+            xy_own[:, first], most_a[at_other], cross[:, first],
+        ),
+        lay(tokens[:, second], pair[:, second], corner_b, x_own[:, second], pair_x, corner_x),
+        lay(
+            y_own[:, second], most_b[at_pair], most_b[at_corner],
+            xy_own[:, second], most_b[at_other], cross[:, second],
+        ),
+    ]
     others = [exchange(piece) for piece in pieces]
     rest = pack_rest(listing, down_proj, parts[0], devices)
     moved, rest = tie((moved, rest))
@@ -415,15 +443,16 @@
     hidden_other = exchange(hidden)
     down0 = moved[:, depth * 7 : depth * 7 + parts[0] * 7 // 2]
 
-    def products(down, rows_in, orders):
+    def products(down, rows_in, orders, before=None):
         own = lax.dynamic_slice_in_dim(down, core * group, group, 0)
         other = exchange(lax.dynamic_slice_in_dim(down, (1 - core) * group, group, 0))
         args = (hidden, hidden_other, own, other)
         sent = down_product(*args, rows_in, 1, orders, jnp.bfloat16, "down_send")
         sent, args = tie((sent, args))
         come = [swap(value, order[0]) for value, order in zip(sent, orders)]
+        args, _ = tie((args, before))
         kept = down_product(*args, rows_in, 0, orders, jnp.float32, "down_keep")
-        return kept, come, sent
+        return kept, come
 
     def stage(kept, come, number, orders):
         axes = tuple(stage_axis(order, number) for order in orders)
@@ -436,10 +465,9 @@
         come = swap(send, 3)
         return (keep + come.astype(jnp.float32)).astype(jnp.bfloat16)
 
-    kept0, come0, _ = products(down0, parts[0], THIRDS)
+    kept0, come0 = products(down0, parts[0], THIRDS)
     down1, kept0 = tie((down1, kept0))
-    kept1, come1, sent1 = products(down1, parts[1], THIRDS)
-    kept0, _ = tie((kept0, sent1))
+    kept1, come1 = products(down1, parts[1], THIRDS, before=come0)
     kept0, come0 = stage(kept0, come0, 1, THIRDS)
     kept1, come1 = stage(kept1, come1, 1, THIRDS)
     kept0, come0 = stage(kept0, come0, 2, THIRDS)

time: 359 us -> 357 us (level)
  waiting for transfers between devices: 235 us -> 222 us
  local copies, waits for them, and re-layouts: 19.8 us -> 28.5 us
    ppermute x27 -> x31, waiting for transfers between devices: 198 us -> 160 us  [swap(): return lax.ppermute(value, 'ep', [(i, i ^ 1 << bit) for i in range(size)])]
    all_to_all x2, waiting for transfers between devices: 33.9 us -> 58.9 us  [move(): return lax.all_to_all(packed, 'ep', 0, 0, tiled=True)]
    unnamed x39 -> x50, local copies, waits for them, and re-layouts: 15 us -> 19.6 us
    ppermute x27 -> x31, starting transfers between devices: 30.2 us -> 32.7 us  [swap(): return lax.ppermute(value, 'ep', [(i, i ^ 1 << bit) for i in range(size)])]
  transfers between devices with their start and end apart: 36 -> 42, of which waited for: 21 -> 19; matrix products, arithmetic and copies ran while one was open for 2% -> 6% of each run, Pallas kernels for 12% -> 13%
where the time goes in v8:
time: 357 us; the launch traced here: 352 us
  waiting for transfers between devices  222 us (62%)
  starting transfers between devices  51.5 us (14%)
  Pallas kernels  45.9 us (13%)
  local copies, waits for them, and re-layouts  28.5 us (8%)
  other arithmetic  4.09 us (1%)
    ppermute x31, waiting for transfers between devices, swap(): return lax.ppermute(value, 'ep', [(i, i ^ 1 << bit) for i in range(size)])  160 us
    all_to_all x2, waiting for transfers between devices, move(): return lax.all_to_all(packed, 'ep', 0, 0, tiled=True)  58.9 us
    ppermute x31, starting transfers between devices, swap(): return lax.ppermute(value, 'ep', [(i, i ^ 1 << bit) for i in range(size)])  32.7 us
    pallas_call x1, Pallas kernels, hidden_units(): pl.pallas_call(hidden_kernel, grid=(8,), out_shape=jax.ShapeDtypeStruct((...  25.7 us
    unnamed x50, local copies, waits for them, and re-layouts  19.6 us
    all_to_all x2, starting transfers between devices, move(): return lax.all_to_all(packed, 'ep', 0, 0, tiled=True)  15.2 us
    pallas_call x4, Pallas kernels, down_product(): pl.pallas_call(functools.partial(down_kernel, rows, side, orders), out_sh...  10.5 us
  transfers between devices with their start and end apart: 42, of which 19 were waited for; matrix products, arithmetic and copies ran while one was open for 6% of the time, Pallas kernels for 13%

profile of v8, /device:TPU:14, one launch (start us, length us, event | category | flops | bytes accessed | tf_op | source)
XLA Modules:
  0.0 351.9 jit_solution(11965731763423508267)
XLA Ops:
  0.0 2.6 collective-permute-start.3
  3.1 1.5 collective-permute-start.1
  4.6 1.5 collective-permute-start
  6.5 0.9 select_reduce_fusion.4
  8.5 13.9 %collective-permute-done.3 = bf16[128,1792]{1,0:T(8,128)(2,1)S(1)} collective-permute-done((bf16[128,1792]{1,0:T(8,128)(2,1)}, bf16[128,1792]{1,0:T(8,128)(2,1)S(1)}, u32[]{:S(2)}, u32[]{:S(2)}) %collective-permute-start.3) | collective-permute-done | bytes 458784 | tf_op jit(solution)/shard_map/ppermute | solution.py:335
  22.5 1.7 collective-permute-done.4
  25.4 2.4 collective-permute-start.5
  28.0 0.9 select_reduce_fusion.share_ref
  28.9 2.0 copy-done.2
  31.0 2.0 copy-done.3
  33.0 5.4 %pack_first.1 = bf16[16,2032,128]{2,1,0:T(8,128)(2,1)} custom-call(s32[14]{0:T(128)S(1)} %select_reduce_fusion.3.list_ref, bf16[16,224,512]{2,1,0:T(8,128)(2,1)S(1)} %copy-done.2, bf16[16,224,512]{2,1,0:T(8,128)(2,1)S(1)} %copy-done.3, bf16[16,224,512]{2,1,0:T(8,128)(2,1)S(1)} %copy-done, f32[16,16,128]{2,1,0:T(8,128)S(1)} %select_reduce_fusion.share_ref), custom_call_target="tpu_custom_call" | custom-call | tf_op jit(solution)/shard_map/pack_first/pallas_call | solution.py:113
  39.4 6.5 %all-to-all-start = ((bf16[16,2032,128]{2,1,0:T(8,128)(2,1)}), bf16[16,2032,128]{2,1,0:T(8,128)(2,1)}, u32[]{:S(2)}, u32[]{:S(2)}) async-start(bf16[16,2032,128]{2,1,0:T(8,128)(2,1)} %pack_first.1), calls=%async_computation | async-start | bytes 16646144 | tf_op jit(solution)/shard_map/all_to_all | solution.py:384
  45.8 0.8 slice_dynamic-update-slice_fusion.9
  46.6 1.1 fusion.3
  47.7 0.9 fusion.5
  49.3 1.5 collective-permute-start.10
  50.8 1.5 collective-permute-start.11
  53.7 0.8 slice_dynamic-update-slice_fusion.7
  54.5 0.9 slice_dynamic-update-slice_fusion.8
  55.3 0.9 constant_dynamic-update-slice_fusion.3
  57.0 85.3 %collective-permute-done.8 = bf16[128,896]{1,0:T(8,128)(2,1)S(1)} collective-permute-done((bf16[128,896]{1,0:T(8,128)(2,1)S(1)}, bf16[128,896]{1,0:T(8,128)(2,1)S(1)}, u32[]{:S(2)}, u32[]{:S(2)}) %collective-permute-start.8) | collective-permute-done | bytes 229408 | tf_op jit(solution)/shard_map/ppermute | solution.py:335
  144.3 0.9 slice_dynamic-update-slice_fusion
  145.2 13.9 %collective-permute-done.9 = bf16[640,896]{1,0:T(8,128)(2,1)S(1)} collective-permute-done((bf16[640,896]{1,0:T(8,128)(2,1)S(1)}, bf16[640,896]{1,0:T(8,128)(2,1)S(1)}, u32[]{:S(2)}, u32[]{:S(2)}) %collective-permute-start.9) | collective-permute-done | bytes 1146912 | tf_op jit(solution)/shard_map/ppermute | solution.py:335
  159.1 1.0 slice_dynamic-update-slice_fusion.1
  160.0 0.9 slice_dynamic-update-slice_fusion.6
  160.9 1.0 slice_dynamic-update-slice_fusion.2
  161.9 0.8 slice_dynamic-update-slice_fusion.4
  163.2 2.0 copy-done.1
  165.3 1.9 pack_rest.1
  167.8 58.9 %all-to-all-done.refs_8_ = bf16[16,2032,128]{2,1,0:T(8,128)(2,1)} async-done(((bf16[16,2032,128]{2,1,0:T(8,128)(2,1)}), bf16[16,2032,128]{2,1,0:T(8,128)(2,1)}, u32[]{:S(2)}, u32[]{:S(2)}) %all-to-all-start) | async-done | bytes 8323104 | tf_op jit(solution)/shard_map/all_to_all | solution.py:384
  226.7 8.7 %all-to-all-start.1 = ((bf16[16,336,128]{2,1,0:T(8,128)(2,1)}), bf16[16,336,128]{2,1,0:T(8,128)(2,1)}, u32[]{:S(2)}, u32[]{:S(2)}) async-start(bf16[16,336,128]{2,1,0:T(8,128)(2,1)} %pack_rest.1), calls=%async_computation.1 | async-start | bytes 2752512 | tf_op jit(solution)/shard_map/all_to_all | solution.py:384
  235.4 1.3 copy-done.19
  236.7 25.7 %hidden.1.own_h = bf16[2048,512]{1,0:T(8,128)(2,1)} custom-call(s32[2]{0:T(128)} %pad_add_fusion.at_ref, bf16[1024,896]{1,0:T(8,128)(2,1)} %constant_dynamic-update-slice_fusion.2.refs_0_, bf16[1024,896]{1,0:T(8,128)(2,1)} %get-tuple-element.168.refs_1_, bf16[1024,896]{1,0:T(8,128)(2,1)} %constant_dynamic-update-slice_fusion.6.refs_2_, ...), custom_call_target="tpu_custom_call" | custom-call | flops 15032385536 | bytes 25165824 | tf_op jit(solution)/shard_map/hidden/pallas_call | solution.py:211
  262.4 1.6 slice.89
  264.8 3.1 collective-permute-done.18.other_ref
  267.9 3.6 %down_send.2 = (bf16[1024,384]{1,0:T(8,128)(2,1)}, bf16[1024,384]{1,0:T(8,128)(2,1)}, bf16[1024,256]{1,0:T(8,128)(2,1)S(1)}) custom-call(bf16[2048,512]{1,0:T(8,128)(2,1)S(1)} %copy-done.6, bf16[2048,512]{1,0:T(8,128)(2,1)S(1)} %collective-permute-done.17.other_h, bf16[8,448,128]{2,1,0:T(8,128)(2,1)S(1)} %get-tuple-element.100.own_ref, ...), custom_call_target="tpu_custom_call" | custom-call | flops 2147483648 | bytes 8388608 | tf_op jit(solution)/shard_map/down_send/pallas_call | solution.py:275
  271.5 0.8 copy-done.11
  273.5 1.6 copy-done.9
  275.1 3.0 down_keep.2
  278.1 1.0 copy-done.4
  279.1 1.5 constant_dynamic-slice_fusion
  280.9 14.1 %collective-permute-done.21.refs_5_ = bf16[1024,256]{1,0:T(8,128)(2,1)S(1)} collective-permute-done((bf16[1024,256]{1,0:T(8,128)(2,1)S(1)}, bf16[1024,256]{1,0:T(8,128)(2,1)S(1)}, u32[]{:S(2)}, u32[]{:S(2)}) %collective-permute-start.21) | collective-permute-done | bytes 524320 | tf_op jit(solution)/shard_map/ppermute | solution.py:335
  295.1 1.7 sum_stage.6
  296.8 1.5 collective-permute-start.24
  298.3 1.9 down_send.3
  300.9 1.5 collective-permute-start.22
  303.2 2.9 collective-permute-done.24.refs_5_
  306.3 6.6 %collective-permute-done.22.refs_1_ = bf16[512,384]{1,0:T(8,128)(2,1)S(1)} collective-permute-done((bf16[512,384]{1,0:T(8,128)(2,1)S(1)}, bf16[512,384]{1,0:T(8,128)(2,1)S(1)}, u32[]{:S(2)}, u32[]{:S(2)}) %collective-permute-start.22) | collective-permute-done | bytes 393248 | tf_op jit(solution)/shard_map/ppermute | solution.py:335
  312.9 1.5 collective-permute-done.23.refs_3_
  316.0 1.5 collective-permute-start.26
  317.4 1.9 down_keep.3
  319.3 4.3 %collective-permute-done.31.refs_3_ = bf16[1024,256]{1,0:T(8,128)(2,1)S(1)} collective-permute-done((bf16[1024,256]{1,0:T(8,128)(2,1)S(1)}, bf16[1024,256]{1,0:T(8,128)(2,1)S(1)}, u32[]{:S(2)}, u32[]{:S(2)}) %collective-permute-start.31) | collective-permute-done | bytes 524320 | tf_op jit(solution)/shard_map/ppermute | solution.py:335
  323.6 2.0 collective-permute-done.32.refs_5_
  326.8 1.7 collective-permute-start.35
  328.5 2.1 collective-permute-done.25.refs_1_
  330.7 3.8 %collective-permute-start.28 = (bf16[128,1024]{1,0:T(8,128)(2,1)S(1)}, bf16[128,1024]{1,0:T(8,128)(2,1)S(1)}, u32[]{:S(2)}, u32[]{:S(2)}) collective-permute-start(bf16[128,1024]{1,0:T(8,128)(2,1)S(1)} %get-tuple-element.124), channel_id=1, source_target_pairs={{0,16},{2,18},{4,20},{6,22},{8,24},{10,26},{12,28},{14,30},{16,0},... | collective-permute-start | bytes 786440 | tf_op jit(solution)/shard_map/ppermute | solution.py:335
  334.5 1.2 collective-permute-done.34.refs_3_
  335.9 0.9 collective-permute-start.36
  336.8 1.5 collective-permute-start.37
  338.8 2.9 collective-permute-done.36.refs_1_
  341.8 1.5 collective-permute-done.38.refs_5_
  343.3 2.1 collective-permute-start.39
  345.6 5.1 %collective-permute-done.39 = bf16[128,768]{1,0:T(8,128)(2,1)S(1)} collective-permute-done((bf16[128,768]{1,0:T(8,128)(2,1)S(1)}, bf16[128,768]{1,0:T(8,128)(2,1)S(1)}, u32[]{:S(2)}, u32[]{:S(2)}) %collective-permute-start.39) | collective-permute-done | bytes 196640 | tf_op jit(solution)/shard_map/ppermute | solution.py:335
  350.9 1.0 copy.15
  (110 shorter events, 18.3 us)
Async XLA Ops:
  0.0 22.4 %collective-permute-start.3 = (bf16[128,1792]{1,0:T(8,128)(2,1)}, bf16[128,1792]{1,0:T(8,128)(2,1)S(1)}, u32[]{:S(2)}, u32[]{:S(2)}) collective-permute-start(bf16[128,1792]{1,0:T(8,128)(2,1)} %param.9), channel_id=1, source_target_pairs={{0,16},{2,18},{4,20},{6,22},{8,24},{10,26},{12,28},{14,30},{16,0},... | collective-permute-start | bytes 1376264 | tf_op jit(solution)/shard_map/ppermute | solution.py:335
  2.6 22.8 %collective-permute-start.2 = (bf16[128,1792]{1,0:T(8,128)(2,1)}, bf16[128,1792]{1,0:T(8,128)(2,1)S(1)}, u32[]{:S(2)}, u32[]{:S(2)}) collective-permute-start(bf16[128,1792]{1,0:T(8,128)(2,1)} %param.9), channel_id=1, source_target_pairs={{0,6},{2,4},{4,2},{6,0},{8,14},{10,12},{12,10},{14,8},{16,22},{18,... | collective-permute-start | bytes 1376264 | tf_op jit(solution)/shard_map/ppermute | solution.py:396
  3.1 35.4 %collective-permute-start.1 = (bf16[128,1792]{1,0:T(8,128)(2,1)}, bf16[128,1792]{1,0:T(8,128)(2,1)S(1)}, u32[]{:S(2)}, u32[]{:S(2)}) collective-permute-start(bf16[128,1792]{1,0:T(8,128)(2,1)} %param.9), channel_id=1, source_target_pairs={{0,4},{2,6},{4,0},{6,2},{8,12},{10,14},{12,8},{14,10},{16,20},{18,... | collective-permute-start | bytes 1376264 | tf_op jit(solution)/shard_map/ppermute | solution.py:335
  4.6 33.8 %collective-permute-start = (bf16[128,1792]{1,0:T(8,128)(2,1)}, bf16[128,1792]{1,0:T(8,128)(2,1)S(1)}, u32[]{:S(2)}, u32[]{:S(2)}) collective-permute-start(bf16[128,1792]{1,0:T(8,128)(2,1)} %param.9), channel_id=1, source_target_pairs={{0,2},{2,0},{4,6},{6,4},{8,10},{10,8},{12,14},{14,12},{16,18},{18,... | collective-permute-start | bytes 1376264 | tf_op jit(solution)/shard_map/ppermute | solution.py:335
  6.1 18.1 %collective-permute-start.4 = (bf16[128,1792]{1,0:T(8,128)(2,1)}, bf16[128,1792]{1,0:T(8,128)(2,1)S(1)}, u32[]{:S(2)}, u32[]{:S(2)}) collective-permute-start(bf16[128,1792]{1,0:T(8,128)(2,1)} %param.9), channel_id=1, source_target_pairs={{0,8},{2,10},{4,12},{6,14},{8,0},{10,2},{12,4},{14,6},{16,24},{18,... | collective-permute-start | bytes 1376264 | tf_op jit(solution)/shard_map/ppermute | solution.py:335
  7.8 20.1 %copy-start.18 = (s32[16,16]{1,0:T(8,128)S(1)}, s32[16,16]{1,0:T(8,128)}, u32[]{:S(2)}) copy-start(s32[16,16]{1,0:T(8,128)} %constant.24.clone) | copy-start | bytes 3076
  8.5 20.4 %copy-start = (bf16[16,224,512]{2,1,0:T(8,128)(2,1)S(1)}, bf16[16,224,512]{2,1,0:T(8,128)(2,1)}, u32[]{:S(2)}) copy-start(bf16[16,224,512]{2,1,0:T(8,128)(2,1)} %down_ref.3) | copy-start | bytes 11010052
  24.3 14.1 %collective-permute-start.7 = (bf16[256,896]{1,0:T(8,128)(2,1)S(1)}, bf16[256,896]{1,0:T(8,128)(2,1)S(1)}, u32[]{:S(2)}, u32[]{:S(2)}) collective-permute-start(bf16[256,896]{1,0:T(8,128)(2,1)S(1)} %get-tuple-element.165), channel_id=1, source_target_pairs={{0,2},{2,0},{4,6},{6,4},{8,10},{10,8},{12,14},{14,12},{16,18},{18,... | collective-permute-start | bytes 1376264 | tf_op jit(solution)/shard_map/ppermute | solution.py:335
  24.9 14.4 %collective-permute-start.6 = (bf16[256,896]{1,0:T(8,128)(2,1)S(1)}, bf16[256,896]{1,0:T(8,128)(2,1)S(1)}, u32[]{:S(2)}, u32[]{:S(2)}) collective-permute-start(bf16[256,896]{1,0:T(8,128)(2,1)S(1)} %get-tuple-element.166), channel_id=1, source_target_pairs={{0,4},{2,6},{4,0},{6,2},{8,12},{10,14},{12,8},{14,10},{16,20},{18,... | collective-permute-start | bytes 1376264 | tf_op jit(solution)/shard_map/ppermute | solution.py:335
  25.4 13.0 %collective-permute-start.5 = (bf16[128,1792]{1,0:T(8,128)(2,1)S(1)}, bf16[128,1792]{1,0:T(8,128)(2,1)S(1)}, u32[]{:S(2)}, u32[]{:S(2)}) collective-permute-start(bf16[128,1792]{1,0:T(8,128)(2,1)S(1)} %collective-permute-done.3), channel_id=1, source_target_pairs={{0,8},{2,10},{4,12},{6,14},{8,0},{10,2},{12,4},{14,6},{16,24},{18,... | collective-permute-start | bytes 1376264 | tf_op jit(solution)/shard_map/ppermute | solution.py:335
  28.9 2.0 copy-start.2
  31.0 2.0 copy-start.3
  38.4 7.4 %copy-start.13 = (bf16[128,1792]{1,0:T(8,128)(2,1)S(1)}, bf16[128,1792]{1,0:T(8,128)(2,1)}, u32[]{:S(2)}) copy-start(bf16[128,1792]{1,0:T(8,128)(2,1)} %param.9) | copy-start | bytes 1376260
  38.4 0.8 copy-start.14
  38.4 0.9 copy-start.16
  39.4 187.3 %all-to-all-start = ((bf16[16,2032,128]{2,1,0:T(8,128)(2,1)}), bf16[16,2032,128]{2,1,0:T(8,128)(2,1)}, u32[]{:S(2)}, u32[]{:S(2)}) async-start(bf16[16,2032,128]{2,1,0:T(8,128)(2,1)} %pack_first.1), calls=%async_computation | async-start | bytes 16646144 | tf_op jit(solution)/shard_map/all_to_all | solution.py:384
  45.8 1.9 copy-start.17
  48.6 5.0 %copy-start.15 = (bf16[128,1792]{1,0:T(8,128)(2,1)S(1)}, bf16[128,1792]{1,0:T(8,128)(2,1)}, u32[]{:S(2)}) copy-start(bf16[128,1792]{1,0:T(8,128)(2,1)} %copy-done.14) | copy-start | bytes 1376260
  48.7 95.6 %collective-permute-start.12 = (bf16[640,896]{1,0:T(8,128)(2,1)S(1)}, bf16[640,896]{1,0:T(8,128)(2,1)S(1)}, u32[]{:S(2)}, u32[]{:S(2)}) collective-permute-start(bf16[640,896]{1,0:T(8,128)(2,1)S(1)} %pad_maximum_fusion.1), channel_id=1, source_target_pairs={{0,4},{2,6},{4,0},{6,2},{8,12},{10,14},{12,8},{14,10},{16,20},{18,... | collective-permute-start | bytes 3440648 | tf_op jit(solution)/shard_map/ppermute | solution.py:335
  49.3 112.6 %collective-permute-start.10 = (bf16[128,1792]{1,0:T(8,128)(2,1)S(1)}, bf16[128,1792]{1,0:T(8,128)(2,1)S(1)}, u32[]{:S(2)}, u32[]{:S(2)}) collective-permute-start(bf16[128,1792]{1,0:T(8,128)(2,1)S(1)} %copy-done.17), channel_id=1, source_target_pairs={{0,6},{2,4},{4,2},{6,0},{8,14},{10,12},{12,10},{14,8},{16,22},{18,... | collective-permute-start | bytes 1376264 | tf_op jit(solution)/shard_map/ppermute | solution.py:396
  50.8 92.2 %collective-permute-start.11 = (bf16[128,896]{1,0:T(8,128)(2,1)S(1)}, bf16[128,896]{1,0:T(8,128)(2,1)S(1)}, u32[]{:S(2)}, u32[]{:S(2)}) collective-permute-start(bf16[128,896]{1,0:T(8,128)(2,1)S(1)} %get-tuple-element.173), channel_id=1, source_target_pairs={{0,2},{2,0},{4,6},{6,4},{8,10},{10,8},{12,14},{14,12},{16,18},{18,... | collective-permute-start | bytes 688136 | tf_op jit(solution)/shard_map/ppermute | solution.py:335
  52.3 90.0 %collective-permute-start.8 = (bf16[128,896]{1,0:T(8,128)(2,1)S(1)}, bf16[128,896]{1,0:T(8,128)(2,1)S(1)}, u32[]{:S(2)}, u32[]{:S(2)}) collective-permute-start(bf16[128,896]{1,0:T(8,128)(2,1)S(1)} %get-tuple-element.176), channel_id=1, source_target_pairs={{0,4},{2,6},{4,0},{6,2},{8,12},{10,14},{12,8},{14,10},{16,20},{18,... | collective-permute-start | bytes 688136 | tf_op jit(solution)/shard_map/ppermute | solution.py:335
  52.9 106.2 %collective-permute-start.9 = (bf16[640,896]{1,0:T(8,128)(2,1)S(1)}, bf16[640,896]{1,0:T(8,128)(2,1)S(1)}, u32[]{:S(2)}, u32[]{:S(2)}) collective-permute-start(bf16[640,896]{1,0:T(8,128)(2,1)S(1)} %pad_maximum_fusion), channel_id=1, source_target_pairs={{0,2},{2,0},{4,6},{6,4},{8,10},{10,8},{12,14},{14,12},{16,18},{18,... | collective-permute-start | bytes 3440648 | tf_op jit(solution)/shard_map/ppermute | solution.py:335
  143.0 92.4 %collective-permute-start.13 = (bf16[1024,896]{1,0:T(8,128)(2,1)}, bf16[1024,896]{1,0:T(8,128)(2,1)}, u32[]{:S(2)}, u32[]{:S(2)}) collective-permute-start(bf16[1024,896]{1,0:T(8,128)(2,1)} %constant_dynamic-update-slice_fusion.2.refs_0_), channel_id=1, source_target_pairs={{0,1},{1,0},{2,3},{3,2},{4,5},{5,4},{6,7},{7,6},{8,9},{9,8},{10,11... | collective-permute-start | bytes 5505032 | tf_op jit(solution)/shard_map/ppermute | solution.py:381
  143.8 91.6 %collective-permute-start.15 = (bf16[1024,896]{1,0:T(8,128)(2,1)}, bf16[1024,896]{1,0:T(8,128)(2,1)S(1)}, u32[]{:S(2)}, u32[]{:S(2)}) collective-permute-start(bf16[1024,896]{1,0:T(8,128)(2,1)} %constant_dynamic-update-slice_fusion.6.refs_2_), channel_id=1, source_target_pairs={{0,1},{1,0},{2,3},{3,2},{4,5},{5,4},{6,7},{7,6},{8,9},{9,8},{10,11... | collective-permute-start | bytes 5505032 | tf_op jit(solution)/shard_map/ppermute | solution.py:381
  162.7 72.7 %collective-permute-start.16 = (bf16[1024,896]{1,0:T(8,128)(2,1)}, bf16[1024,896]{1,0:T(8,128)(2,1)}, u32[]{:S(2)}, u32[]{:S(2)}) collective-permute-start(bf16[1024,896]{1,0:T(8,128)(2,1)} %get-tuple-element.167.refs_3_), channel_id=1, source_target_pairs={{0,1},{1,0},{2,3},{3,2},{4,5},{5,4},{6,7},{7,6},{8,9},{9,8},{10,11... | collective-permute-start | bytes 5505032 | tf_op jit(solution)/shard_map/ppermute | solution.py:381
  162.7 72.7 %collective-permute-start.14 = (bf16[1024,896]{1,0:T(8,128)(2,1)}, bf16[1024,896]{1,0:T(8,128)(2,1)}, u32[]{:S(2)}, u32[]{:S(2)}) collective-permute-start(bf16[1024,896]{1,0:T(8,128)(2,1)} %get-tuple-element.168.refs_1_), channel_id=1, source_target_pairs={{0,1},{1,0},{2,3},{3,2},{4,5},{5,4},{6,7},{7,6},{8,9},{9,8},{10,11... | collective-permute-start | bytes 5505032 | tf_op jit(solution)/shard_map/ppermute | solution.py:381
  163.2 2.0 copy-start.1
  226.7 52.4 %all-to-all-start.1 = ((bf16[16,336,128]{2,1,0:T(8,128)(2,1)}), bf16[16,336,128]{2,1,0:T(8,128)(2,1)}, u32[]{:S(2)}, u32[]{:S(2)}) async-start(bf16[16,336,128]{2,1,0:T(8,128)(2,1)} %pack_rest.1), calls=%async_computation.1 | async-start | bytes 2752512 | tf_op jit(solution)/shard_map/all_to_all | solution.py:384
  235.4 1.3 copy-start.19
  262.4 5.5 %collective-permute-start.17 = (bf16[2048,512]{1,0:T(8,128)(2,1)}, bf16[2048,512]{1,0:T(8,128)(2,1)S(1)}, u32[]{:S(2)}, u32[]{:S(2)}) collective-permute-start(bf16[2048,512]{1,0:T(8,128)(2,1)} %hidden.1.own_h), channel_id=1, source_target_pairs={{0,1},{1,0},{2,3},{3,2},{4,5},{5,4},{6,7},{7,6},{8,9},{9,8},{10,11... | collective-permute-start | bytes 6291464 | tf_op jit(solution)/shard_map/ppermute | solution.py:381
  264.1 3.8 %copy-start.6 = (bf16[2048,512]{1,0:T(8,128)(2,1)S(1)}, bf16[2048,512]{1,0:T(8,128)(2,1)}, u32[]{:S(2)}) copy-start(bf16[2048,512]{1,0:T(8,128)(2,1)} %hidden.1.own_h) | copy-start | bytes 6291460
  264.2 3.7 %collective-permute-start.18 = (bf16[8,448,128]{2,1,0:T(8,128)(2,1)S(1)}, bf16[8,448,128]{2,1,0:T(8,128)(2,1)S(1)}, u32[]{:S(2)}, u32[]{:S(2)}) collective-permute-start(bf16[8,448,128]{2,1,0:T(8,128)(2,1)S(1)} %get-tuple-element.157), channel_id=1, source_target_pairs={{0,1},{1,0},{2,3},{3,2},{4,5},{5,4},{6,7},{7,6},{8,9},{9,8},{10,11... | collective-permute-start | bytes 2752520 | tf_op jit(solution)/shard_map/ppermute | solution.py:381
  267.9 3.6 %copy-start.8 = (bf16[2048,512]{1,0:T(8,128)(2,1)}, bf16[2048,512]{1,0:T(8,128)(2,1)S(1)}, u32[]{:S(2)}) copy-start(bf16[2048,512]{1,0:T(8,128)(2,1)S(1)} %collective-permute-done.17.other_h) | copy-start | bytes 6291460
  271.5 0.8 copy-start.11
  272.4 22.7 %collective-permute-start.19 = (bf16[1024,384]{1,0:T(8,128)(2,1)}, bf16[1024,384]{1,0:T(8,128)(2,1)}, u32[]{:S(2)}, u32[]{:S(2)}) collective-permute-start(bf16[1024,384]{1,0:T(8,128)(2,1)} %get-tuple-element.106), channel_id=1, source_target_pairs={{0,2},{2,0},{4,6},{6,4},{8,10},{10,8},{12,14},{14,12},{16,18},{18,... | collective-permute-start | bytes 2359304 | tf_op jit(solution)/shard_map/ppermute | solution.py:335
  272.9 22.1 %collective-permute-start.20 = (bf16[1024,384]{1,0:T(8,128)(2,1)}, bf16[1024,384]{1,0:T(8,128)(2,1)}, u32[]{:S(2)}, u32[]{:S(2)}) collective-permute-start(bf16[1024,384]{1,0:T(8,128)(2,1)} %get-tuple-element.108), channel_id=1, source_target_pairs={{0,4},{2,6},{4,0},{6,2},{8,12},{10,14},{12,8},{14,10},{16,20},{18,... | collective-permute-start | bytes 2359304 | tf_op jit(solution)/shard_map/ppermute | solution.py:335
  273.5 1.6 copy-start.9
  278.1 1.0 copy-start.4
  279.1 1.6 copy-start.12
  279.1 16.0 %copy-start.5 = (f32[1024,256]{1,0:T(8,128)S(1)}, f32[1024,256]{1,0:T(8,128)}, u32[]{:S(2)}) copy-start(f32[1024,256]{1,0:T(8,128)} %copy-done.4) | copy-start | bytes 3145732
  280.6 17.7 %copy-start.7 = (bf16[2048,512]{1,0:T(8,128)(2,1)S(1)}, bf16[2048,512]{1,0:T(8,128)(2,1)}, u32[]{:S(2)}) copy-start(bf16[2048,512]{1,0:T(8,128)(2,1)} %hidden.1.own_h) | copy-start | bytes 6291460
  280.6 17.7 %copy-start.10 = (bf16[2048,512]{1,0:T(8,128)(2,1)S(1)}, bf16[2048,512]{1,0:T(8,128)(2,1)}, u32[]{:S(2)}) copy-start(bf16[2048,512]{1,0:T(8,128)(2,1)} %copy-done.8) | copy-start | bytes 6291460
  280.6 17.7 %collective-permute-start.29 = (bf16[8,336,128]{2,1,0:T(8,128)(2,1)S(1)}, bf16[8,336,128]{2,1,0:T(8,128)(2,1)S(1)}, u32[]{:S(2)}, u32[]{:S(2)}) collective-permute-start(bf16[8,336,128]{2,1,0:T(8,128)(2,1)S(1)} %get-tuple-element.159), channel_id=1, source_target_pairs={{0,1},{1,0},{2,3},{3,2},{4,5},{5,4},{6,7},{7,6},{8,9},{9,8},{10,11... | collective-permute-start | bytes 2064392 | tf_op jit(solution)/shard_map/ppermute | solution.py:381
  280.7 14.3 %collective-permute-start.21 = (bf16[1024,256]{1,0:T(8,128)(2,1)S(1)}, bf16[1024,256]{1,0:T(8,128)(2,1)S(1)}, u32[]{:S(2)}, u32[]{:S(2)}) collective-permute-start(bf16[1024,256]{1,0:T(8,128)(2,1)S(1)} %copy-done.12), channel_id=1, source_target_pairs={{0,8},{2,10},{4,12},{6,14},{8,0},{10,2},{12,4},{14,6},{16,24},{18,... | collective-permute-start | bytes 1572872 | tf_op jit(solution)/shard_map/ppermute | solution.py:335
  296.8 9.3 %collective-permute-start.24 = (bf16[512,256]{1,0:T(8,128)(2,1)S(1)}, bf16[512,256]{1,0:T(8,128)(2,1)S(1)}, u32[]{:S(2)}, u32[]{:S(2)}) collective-permute-start(bf16[512,256]{1,0:T(8,128)(2,1)S(1)} %get-tuple-element.116), channel_id=1, source_target_pairs={{0,2},{2,0},{4,6},{6,4},{8,10},{10,8},{12,14},{14,12},{16,18},{18,... | collective-permute-start | bytes 786440 | tf_op jit(solution)/shard_map/ppermute | solution.py:335
  300.3 15.7 %collective-permute-start.30 = (bf16[1024,256]{1,0:T(8,128)(2,1)S(1)}, bf16[1024,256]{1,0:T(8,128)(2,1)S(1)}, u32[]{:S(2)}, u32[]{:S(2)}) collective-permute-start(bf16[1024,256]{1,0:T(8,128)(2,1)S(1)} %get-tuple-element.138), channel_id=1, source_target_pairs={{0,2},{2,0},{4,6},{6,4},{8,10},{10,8},{12,14},{14,12},{16,18},{18,... | collective-permute-start | bytes 1572872 | tf_op jit(solution)/shard_map/ppermute | solution.py:335
  300.9 12.1 %collective-permute-start.22 = (bf16[512,384]{1,0:T(8,128)(2,1)S(1)}, bf16[512,384]{1,0:T(8,128)(2,1)S(1)}, u32[]{:S(2)}, u32[]{:S(2)}) collective-permute-start(bf16[512,384]{1,0:T(8,128)(2,1)S(1)} %get-tuple-element.112), channel_id=1, source_target_pairs={{0,4},{2,6},{4,0},{6,2},{8,12},{10,14},{12,8},{14,10},{16,20},{18,... | collective-permute-start | bytes 1179656 | tf_op jit(solution)/shard_map/ppermute | solution.py:335
  302.3 12.1 %collective-permute-start.23 = (bf16[512,384]{1,0:T(8,128)(2,1)S(1)}, bf16[512,384]{1,0:T(8,128)(2,1)S(1)}, u32[]{:S(2)}, u32[]{:S(2)}) collective-permute-start(bf16[512,384]{1,0:T(8,128)(2,1)S(1)} %get-tuple-element.114), channel_id=1, source_target_pairs={{0,8},{2,10},{4,12},{6,14},{8,0},{10,2},{12,4},{14,6},{16,24},{18,... | collective-permute-start | bytes 1179656 | tf_op jit(solution)/shard_map/ppermute | solution.py:335
  302.9 20.7 %collective-permute-start.31 = (bf16[1024,256]{1,0:T(8,128)(2,1)S(1)}, bf16[1024,256]{1,0:T(8,128)(2,1)S(1)}, u32[]{:S(2)}, u32[]{:S(2)}) collective-permute-start(bf16[1024,256]{1,0:T(8,128)(2,1)S(1)} %get-tuple-element.140), channel_id=1, source_target_pairs={{0,4},{2,6},{4,0},{6,2},{8,12},{10,14},{12,8},{14,10},{16,20},{18,... | collective-permute-start | bytes 1572872 | tf_op jit(solution)/shard_map/ppermute | solution.py:335
  306.1 19.6 %collective-permute-start.32 = (bf16[1024,256]{1,0:T(8,128)(2,1)S(1)}, bf16[1024,256]{1,0:T(8,128)(2,1)S(1)}, u32[]{:S(2)}, u32[]{:S(2)}) collective-permute-start(bf16[1024,256]{1,0:T(8,128)(2,1)S(1)} %get-tuple-element.142), channel_id=1, source_target_pairs={{0,8},{2,10},{4,12},{6,14},{8,0},{10,2},{12,4},{14,6},{16,24},{18,... | collective-permute-start | bytes 1572872 | tf_op jit(solution)/shard_map/ppermute | solution.py:335
  314.6 12.2 %collective-permute-start.27 = (bf16[256,256]{1,0:T(8,128)(2,1)S(1)}, bf16[256,256]{1,0:T(8,128)(2,1)S(1)}, u32[]{:S(2)}, u32[]{:S(2)}) collective-permute-start(bf16[256,256]{1,0:T(8,128)(2,1)S(1)} %get-tuple-element.122), channel_id=1, source_target_pairs={{0,4},{2,6},{4,0},{6,2},{8,12},{10,14},{12,8},{14,10},{16,20},{18,... | collective-permute-start | bytes 393224 | tf_op jit(solution)/shard_map/ppermute | solution.py:335
  315.2 15.4 %collective-permute-start.25 = (bf16[256,384]{1,0:T(8,128)(2,1)S(1)}, bf16[256,384]{1,0:T(8,128)(2,1)S(1)}, u32[]{:S(2)}, u32[]{:S(2)}) collective-permute-start(bf16[256,384]{1,0:T(8,128)(2,1)S(1)} %get-tuple-element.118), channel_id=1, source_target_pairs={{0,8},{2,10},{4,12},{6,14},{8,0},{10,2},{12,4},{14,6},{16,24},{18,... | collective-permute-start | bytes 589832 | tf_op jit(solution)/shard_map/ppermute | solution.py:335
  316.0 14.6 %collective-permute-start.26 = (bf16[256,384]{1,0:T(8,128)(2,1)S(1)}, bf16[256,384]{1,0:T(8,128)(2,1)S(1)}, u32[]{:S(2)}, u32[]{:S(2)}) collective-permute-start(bf16[256,384]{1,0:T(8,128)(2,1)S(1)} %get-tuple-element.120), channel_id=1, source_target_pairs={{0,2},{2,0},{4,6},{6,4},{8,10},{10,8},{12,14},{14,12},{16,18},{18,... | collective-permute-start | bytes 589832 | tf_op jit(solution)/shard_map/ppermute | solution.py:335
  325.9 8.6 %collective-permute-start.33 = (bf16[512,256]{1,0:T(8,128)(2,1)S(1)}, bf16[512,256]{1,0:T(8,128)(2,1)S(1)}, u32[]{:S(2)}, u32[]{:S(2)}) collective-permute-start(bf16[512,256]{1,0:T(8,128)(2,1)S(1)} %get-tuple-element.144), channel_id=1, source_target_pairs={{0,4},{2,6},{4,0},{6,2},{8,12},{10,14},{12,8},{14,10},{16,20},{18,... | collective-permute-start | bytes 786440 | tf_op jit(solution)/shard_map/ppermute | solution.py:335
  326.5 9.2 %collective-permute-start.34 = (bf16[512,256]{1,0:T(8,128)(2,1)S(1)}, bf16[512,256]{1,0:T(8,128)(2,1)S(1)}, u32[]{:S(2)}, u32[]{:S(2)}) collective-permute-start(bf16[512,256]{1,0:T(8,128)(2,1)S(1)} %get-tuple-element.146), channel_id=1, source_target_pairs={{0,8},{2,10},{4,12},{6,14},{8,0},{10,2},{12,4},{14,6},{16,24},{18,... | collective-permute-start | bytes 786440 | tf_op jit(solution)/shard_map/ppermute | solution.py:335
  326.8 9.0 %collective-permute-start.35 = (bf16[512,256]{1,0:T(8,128)(2,1)S(1)}, bf16[512,256]{1,0:T(8,128)(2,1)S(1)}, u32[]{:S(2)}, u32[]{:S(2)}) collective-permute-start(bf16[512,256]{1,0:T(8,128)(2,1)S(1)} %get-tuple-element.148), channel_id=1, source_target_pairs={{0,2},{2,0},{4,6},{6,4},{8,10},{10,8},{12,14},{14,12},{16,18},{18,... | collective-permute-start | bytes 786440 | tf_op jit(solution)/shard_map/ppermute | solution.py:335
  330.7 14.7 %collective-permute-start.28 = (bf16[128,1024]{1,0:T(8,128)(2,1)S(1)}, bf16[128,1024]{1,0:T(8,128)(2,1)S(1)}, u32[]{:S(2)}, u32[]{:S(2)}) collective-permute-start(bf16[128,1024]{1,0:T(8,128)(2,1)S(1)} %get-tuple-element.124), channel_id=1, source_target_pairs={{0,16},{2,18},{4,20},{6,22},{8,24},{10,26},{12,28},{14,30},{16,0},... | collective-permute-start | bytes 786440 | tf_op jit(solution)/shard_map/ppermute | solution.py:335
  335.9 5.8 %collective-permute-start.36 = (bf16[256,256]{1,0:T(8,128)(2,1)S(1)}, bf16[256,256]{1,0:T(8,128)(2,1)S(1)}, u32[]{:S(2)}, u32[]{:S(2)}) collective-permute-start(bf16[256,256]{1,0:T(8,128)(2,1)S(1)} %get-tuple-element.150), channel_id=1, source_target_pairs={{0,8},{2,10},{4,12},{6,14},{8,0},{10,2},{12,4},{14,6},{16,24},{18,... | collective-permute-start | bytes 393224 | tf_op jit(solution)/shard_map/ppermute | solution.py:335
  336.8 5.0 %collective-permute-start.37 = (bf16[256,256]{1,0:T(8,128)(2,1)S(1)}, bf16[256,256]{1,0:T(8,128)(2,1)S(1)}, u32[]{:S(2)}, u32[]{:S(2)}) collective-permute-start(bf16[256,256]{1,0:T(8,128)(2,1)S(1)} %get-tuple-element.152), channel_id=1, source_target_pairs={{0,2},{2,0},{4,6},{6,4},{8,10},{10,8},{12,14},{14,12},{16,18},{18,... | collective-permute-start | bytes 393224 | tf_op jit(solution)/shard_map/ppermute | solution.py:335
  338.3 5.0 %collective-permute-start.38 = (bf16[256,256]{1,0:T(8,128)(2,1)S(1)}, bf16[256,256]{1,0:T(8,128)(2,1)S(1)}, u32[]{:S(2)}, u32[]{:S(2)}) collective-permute-start(bf16[256,256]{1,0:T(8,128)(2,1)S(1)} %get-tuple-element.154), channel_id=1, source_target_pairs={{0,4},{2,6},{4,0},{6,2},{8,12},{10,14},{12,8},{14,10},{16,20},{18,... | collective-permute-start | bytes 393224 | tf_op jit(solution)/shard_map/ppermute | solution.py:335
  343.3 7.4 %collective-permute-start.39 = (bf16[128,768]{1,0:T(8,128)(2,1)S(1)}, bf16[128,768]{1,0:T(8,128)(2,1)S(1)}, u32[]{:S(2)}, u32[]{:S(2)}) collective-permute-start(bf16[128,768]{1,0:T(8,128)(2,1)S(1)} %get-tuple-element.156), channel_id=1, source_target_pairs={{0,16},{2,18},{4,20},{6,22},{8,24},{10,26},{12,28},{14,30},{16,0},... | collective-permute-start | bytes 589832 | tf_op jit(solution)/shard_map/ppermute | solution.py:335

commit v9 on v5

--- a/solution.py
+++ b/solution.py
@@ -392,19 +392,32 @@
     belongs = slot_place[None, None, :, None] == places[:, :, None, None]
     share = jnp.sum(jnp.where(belongs, share[None, None], 0.0), axis=2)
 
+    mid = tokens.shape[1] // 2
+    first, second = slice(0, mid), slice(mid, 2 * mid)
+
+    def lay(*values):
+        return jnp.concatenate(values, axis=0)
+
     near, far = swap(tokens, 2), swap(tokens, 3)
     corner = swap(far, 2)
+    pair = lay(far, near)
+    pair_y, pair_x = swap(pair[:, first], 1), swap(pair[:, second], 0)
     parts = (128, 96)
     packed = pack_first(listing, gate_proj, up_proj, down_proj, parts[0], share, devices)
-    packed, near, far, corner = tie((packed, near, far, corner))
+    packed, pair, corner, pair_y, pair_x = tie((packed, pair, corner, pair_y, pair_x))
 
     moved = move(packed)
-    mid = tokens.shape[1] // 2
-    rows = jnp.concatenate([tokens, far, near, corner], axis=0)
-    first, second = rows[:, :mid], rows[:, mid:]
-    first = jnp.concatenate([first, swap(first, 1)], axis=0)
-    second = jnp.concatenate([second, swap(second, 0)], axis=0)
-    pieces = [first, swap(first, 0), second, swap(second, 1)]
+    column, ends = lay(tokens, pair, corner), lay(tokens, corner)
+    most_a = swap(lay(column[:, first], pair_y), 0)
+    most_b = swap(lay(column[:, second], pair_x), 1)
+    ends_y, ends_x = swap(ends[:, first], 1), swap(ends[:, second], 0)
+    cross = lax.ppermute(ends, "ep", [(i, i ^ 3) for i in range(devices)])
+    pieces = [
+        lay(column[:, first], ends_y[:block], pair_y, ends_y[block:]),
+        lay(most_a[: 4 * block], cross[:block, first], most_a[4 * block :], cross[block:, first]),
+        lay(column[:, second], ends_x[:block], pair_x, ends_x[block:]),
+        lay(most_b[: 4 * block], cross[:block, second], most_b[4 * block :], cross[block:, second]),
+    ]
     others = [exchange(piece) for piece in pieces]
     rest = pack_rest(listing, down_proj, parts[0], devices)
     moved, rest = tie((moved, rest))
@@ -415,13 +428,14 @@
     hidden_other = exchange(hidden)
     down0 = moved[:, depth * 7 : depth * 7 + parts[0] * 7 // 2]
 
-    def products(down, rows_in, orders):
+    def products(down, rows_in, orders, before=None):
         own = lax.dynamic_slice_in_dim(down, core * group, group, 0)
         other = exchange(lax.dynamic_slice_in_dim(down, (1 - core) * group, group, 0))
         args = (hidden, hidden_other, own, other)
         sent = down_product(*args, rows_in, 1, orders, jnp.bfloat16, "down_send")
         sent, args = tie((sent, args))
         come = [swap(value, order[0]) for value, order in zip(sent, orders)]
+        args, _ = tie((args, before))
         kept = down_product(*args, rows_in, 0, orders, jnp.float32, "down_keep")
         return kept, come, sent
 
@@ -438,7 +452,7 @@
 
     kept0, come0, _ = products(down0, parts[0], THIRDS)
     down1, kept0 = tie((down1, kept0))
-    kept1, come1, sent1 = products(down1, parts[1], THIRDS)
+    kept1, come1, sent1 = products(down1, parts[1], THIRDS, before=come0)
     kept0, _ = tie((kept0, sent1))
     kept0, come0 = stage(kept0, come0, 1, THIRDS)
     kept1, come1 = stage(kept1, come1, 1, THIRDS)

time: 359 us -> 361 us (level)
    ppermute x27 -> x29, waiting for transfers between devices: 198 us -> 155 us  [swap(): return lax.ppermute(value, 'ep', [(i, i ^ 1 << bit) for i in range(size)])]
    ppermute x0 -> x1, waiting for transfers between devices: none -> 29.4 us  [packed_layer(): cross = lax.ppermute(ends, 'ep', [(i, i ^ 3) for i in range(devices)])]
    all_to_all x2, waiting for transfers between devices: 33.9 us -> 48 us  [move(): return lax.all_to_all(packed, 'ep', 0, 0, tiled=True)]
    all_to_all x2, starting transfers between devices: 17.5 us -> 13 us  [move(): return lax.all_to_all(packed, 'ep', 0, 0, tiled=True)]
    ppermute x27 -> x29, starting transfers between devices: 30.2 us -> 31.6 us  [swap(): return lax.ppermute(value, 'ep', [(i, i ^ 1 << bit) for i in range(size)])]
    unnamed x39 -> x45, local copies, waits for them, and re-layouts: 15 us -> 14.7 us
  transfers between devices with their start and end apart: 36 -> 39, of which waited for: 21 -> 23; matrix products, arithmetic and copies ran while one was open for 2% -> 3% of each run, Pallas kernels for 12% -> 12%
where the time goes in v9:
time: 361 us; the launch traced here: 357 us
  waiting for transfers between devices  237 us (66%)
  starting transfers between devices  47.4 us (13%)
  Pallas kernels  43.9 us (12%)
  local copies, waits for them, and re-layouts  20.1 us (6%)
  other arithmetic  8.35 us (2%)
    ppermute x29, waiting for transfers between devices, swap(): return lax.ppermute(value, 'ep', [(i, i ^ 1 << bit) for i in range(size)])  155 us
    all_to_all x2, waiting for transfers between devices, move(): return lax.all_to_all(packed, 'ep', 0, 0, tiled=True)  48 us
    ppermute x29, starting transfers between devices, swap(): return lax.ppermute(value, 'ep', [(i, i ^ 1 << bit) for i in range(size)])  31.6 us
    ppermute x1, waiting for transfers between devices, packed_layer(): cross = lax.ppermute(ends, 'ep', [(i, i ^ 3) for i in range(devices)])  29.4 us
    pallas_call x1, Pallas kernels, hidden_units(): pl.pallas_call(hidden_kernel, grid=(8,), out_shape=jax.ShapeDtypeStruct((...  25.8 us
    unnamed x45, local copies, waits for them, and re-layouts  14.7 us
    all_to_all x2, starting transfers between devices, move(): return lax.all_to_all(packed, 'ep', 0, 0, tiled=True)  13 us
    pallas_call x4, Pallas kernels, down_product(): pl.pallas_call(functools.partial(down_kernel, rows, side, orders), out_sh...  9.89 us
  transfers between devices with their start and end apart: 39, of which 23 were waited for; matrix products, arithmetic and copies ran while one was open for 3% of the time, Pallas kernels for 12%

profile of v9, /device:TPU:14, one launch (start us, length us, event | category | flops | bytes accessed | tf_op | source)
XLA Modules:
  0.0 356.9 jit_solution(3240565311670133663)
XLA Ops:
  0.0 2.6 collective-permute-start
  3.0 0.9 select_reduce_fusion.4
  4.3 0.7 select_reduce_fusion.1
  5.1 17.3 %collective-permute-done = bf16[128,1792]{1,0:T(8,128)(2,1)S(1)} collective-permute-done((bf16[128,1792]{1,0:T(8,128)(2,1)}, bf16[128,1792]{1,0:T(8,128)(2,1)S(1)}, u32[]{:S(2)}, u32[]{:S(2)}) %collective-permute-start) | collective-permute-done | bytes 458784 | tf_op jit(solution)/shard_map/ppermute | solution.py:335
  22.4 0.9 collective-permute-done.1
  25.3 0.9 select_reduce_fusion.share_ref
  26.3 2.0 copy-done.2
  28.3 2.0 copy-done.3
  30.4 5.4 %pack_first.1 = bf16[16,2032,128]{2,1,0:T(8,128)(2,1)} custom-call(s32[14]{0:T(128)S(1)} %select_reduce_fusion.3.list_ref, bf16[16,224,512]{2,1,0:T(8,128)(2,1)S(1)} %copy-done.2, bf16[16,224,512]{2,1,0:T(8,128)(2,1)S(1)} %copy-done.3, bf16[16,224,512]{2,1,0:T(8,128)(2,1)S(1)} %copy-done, f32[16,16,128]{2,1,0:T(8,128)S(1)} %select_reduce_fusion.share_ref), custom_call_target="tpu_custom_call" | custom-call | tf_op jit(solution)/shard_map/pack_first/pallas_call | solution.py:113
  35.8 0.8 copy-done.18
  36.5 7.9 %all-to-all-start = ((bf16[16,2032,128]{2,1,0:T(8,128)(2,1)}), bf16[16,2032,128]{2,1,0:T(8,128)(2,1)}, u32[]{:S(2)}, u32[]{:S(2)}) async-start(bf16[16,2032,128]{2,1,0:T(8,128)(2,1)} %pack_first.1), calls=%async_computation | async-start | bytes 16646144 | tf_op jit(solution)/shard_map/all_to_all | solution.py:384
  44.6 0.9 copy-done.19
  45.6 0.6 collective-permute-start.8
  46.5 1.5 collective-permute-start.6
  48.1 0.6 collective-permute-start.9
  48.8 1.5 collective-permute-start.7
  50.8 33.5 %collective-permute-done.8 = bf16[256,896]{1,0:T(8,128)(2,1)S(1)} collective-permute-done((bf16[256,896]{1,0:T(8,128)(2,1)S(1)}, bf16[256,896]{1,0:T(8,128)(2,1)S(1)}, u32[]{:S(2)}, u32[]{:S(2)}) %collective-permute-start.8) | collective-permute-done | bytes 458784 | tf_op jit(solution)/shard_map/ppermute | solution.py:335
  84.5 62.2 %collective-permute-done.5 = bf16[256,896]{1,0:T(8,128)(2,1)S(1)} collective-permute-done((bf16[256,896]{1,0:T(8,128)(2,1)S(1)}, bf16[256,896]{1,0:T(8,128)(2,1)S(1)}, u32[]{:S(2)}, u32[]{:S(2)}) %collective-permute-start.5) | collective-permute-done | bytes 458784 | tf_op jit(solution)/shard_map/ppermute | solution.py:335
  146.8 1.4 pad_maximum_fusion.refs_0_
  148.2 29.4 %collective-permute-done.7 = bf16[256,1792]{1,0:T(8,128)(2,1)S(1)} collective-permute-done((bf16[256,1792]{1,0:T(8,128)(2,1)S(1)}, bf16[256,1792]{1,0:T(8,128)(2,1)S(1)}, u32[]{:S(2)}, u32[]{:S(2)}) %collective-permute-start.7) | collective-permute-done | bytes 917536 | tf_op jit(solution)/shard_map/ppermute | solution.py:414
  177.9 1.4 pad_maximum_fusion.1.refs_1_
  179.4 1.4 pad_maximum_fusion.3.refs_3_
  181.3 2.0 copy-done.1
  183.3 1.9 pack_rest.1
  185.7 48.0 %all-to-all-done.refs_8_ = bf16[16,2032,128]{2,1,0:T(8,128)(2,1)} async-done(((bf16[16,2032,128]{2,1,0:T(8,128)(2,1)}), bf16[16,2032,128]{2,1,0:T(8,128)(2,1)}, u32[]{:S(2)}, u32[]{:S(2)}) %all-to-all-start) | async-done | bytes 8323104 | tf_op jit(solution)/shard_map/all_to_all | solution.py:384
  233.8 5.1 %all-to-all-start.1 = ((bf16[16,336,128]{2,1,0:T(8,128)(2,1)}), bf16[16,336,128]{2,1,0:T(8,128)(2,1)}, u32[]{:S(2)}, u32[]{:S(2)}) async-start(bf16[16,336,128]{2,1,0:T(8,128)(2,1)} %pack_rest.1), calls=%async_computation.1 | async-start | bytes 2752512 | tf_op jit(solution)/shard_map/all_to_all | solution.py:384
  238.9 25.8 %hidden.1.own_h = bf16[2048,512]{1,0:T(8,128)(2,1)} custom-call(s32[2]{0:T(128)} %pad_add_fusion.at_ref, bf16[1024,896]{1,0:T(8,128)(2,1)} %pad_maximum_fusion.refs_0_, bf16[1024,896]{1,0:T(8,128)(2,1)} %pad_maximum_fusion.1.refs_1_, bf16[1024,896]{1,0:T(8,128)(2,1)} %copy-done.16, bf16[1024,896]{1,0:T(8,128)(2,1)} %pad_maximum_fusion.3.refs_3_, ...), custom_call_target="tpu_custom_call" | custom-call | flops 15032385536 | bytes 25165824 | tf_op jit(solution)/shard_map/hidden/pallas_call | solution.py:211
  264.7 1.6 slice.77
  267.0 3.1 collective-permute-done.15.other_ref
  270.1 3.0 down_send.2
  273.2 0.9 copy-done.12
  274.1 0.9 copy-done.13
  275.0 0.8 copy-done.14
  275.8 1.6 copy-done.9
  277.4 3.0 down_keep.2
  280.4 1.0 copy-done.4
  281.4 1.5 constant_dynamic-slice_fusion
  284.4 0.7 collective-permute-done.16.other_ref
  285.2 1.6 copy-done.10
  286.7 1.9 down_send.3
  288.7 9.2 %collective-permute-done.19.refs_5_ = bf16[1024,256]{1,0:T(8,128)(2,1)S(1)} collective-permute-done((bf16[1024,256]{1,0:T(8,128)(2,1)S(1)}, bf16[1024,256]{1,0:T(8,128)(2,1)S(1)}, u32[]{:S(2)}, u32[]{:S(2)}) %collective-permute-start.19) | collective-permute-done | bytes 524320 | tf_op jit(solution)/shard_map/ppermute | solution.py:335
  297.9 5.3 %collective-permute-done.17.refs_1_ = bf16[1024,384]{1,0:T(8,128)(2,1)S(1)} collective-permute-done((bf16[1024,384]{1,0:T(8,128)(2,1)}, bf16[1024,384]{1,0:T(8,128)(2,1)S(1)}, u32[]{:S(2)}, u32[]{:S(2)}) %collective-permute-start.17) | collective-permute-done | bytes 786464 | tf_op jit(solution)/shard_map/ppermute | solution.py:335
  303.8 1.5 collective-permute-start.22
  306.8 1.7 collective-permute-start.28
  308.5 4.6 %collective-permute-done.22.refs_5_ = bf16[512,256]{1,0:T(8,128)(2,1)S(1)} collective-permute-done((bf16[512,256]{1,0:T(8,128)(2,1)S(1)}, bf16[512,256]{1,0:T(8,128)(2,1)S(1)}, u32[]{:S(2)}, u32[]{:S(2)}) %collective-permute-start.22) | collective-permute-done | bytes 262176 | tf_op jit(solution)/shard_map/ppermute | solution.py:335
  313.7 4.3 %collective-permute-done.20.refs_1_ = bf16[512,384]{1,0:T(8,128)(2,1)S(1)} collective-permute-done((bf16[512,384]{1,0:T(8,128)(2,1)S(1)}, bf16[512,384]{1,0:T(8,128)(2,1)S(1)}, u32[]{:S(2)}, u32[]{:S(2)}) %collective-permute-start.20) | collective-permute-done | bytes 393248 | tf_op jit(solution)/shard_map/ppermute | solution.py:335
  318.7 1.5 collective-permute-start.25
  320.8 1.8 collective-permute-done.27.refs_1_
  322.6 1.4 collective-permute-start.24
  324.0 1.9 down_keep.3
  325.9 3.0 collective-permute-done.28.refs_3_
  328.9 0.9 collective-permute-done.29.refs_5_
  330.0 1.5 collective-permute-start.30
  332.1 1.5 collective-permute-start.32
  333.6 0.9 collective-permute-done.23.refs_1_
  334.5 3.9 %collective-permute-start.26 = (bf16[128,1024]{1,0:T(8,128)(2,1)S(1)}, bf16[128,1024]{1,0:T(8,128)(2,1)S(1)}, u32[]{:S(2)}, u32[]{:S(2)}) collective-permute-start(bf16[128,1024]{1,0:T(8,128)(2,1)S(1)} %get-tuple-element.131), channel_id=1, source_target_pairs={{0,16},{2,18},{4,20},{6,22},{8,24},{10,26},{12,28},{14,30},{16,0},... | collective-permute-start | bytes 786440 | tf_op jit(solution)/shard_map/ppermute | solution.py:335
  338.4 2.0 collective-permute-done.31.refs_3_
  340.6 1.7 collective-permute-start.34
  342.4 1.1 collective-permute-start.35
  343.5 2.1 collective-permute-done.33.refs_1_
  345.7 1.7 collective-permute-done.35.refs_5_
  347.4 3.2 collective-permute-start.36
  350.8 4.8 %collective-permute-done.36 = bf16[128,768]{1,0:T(8,128)(2,1)S(1)} collective-permute-done((bf16[128,768]{1,0:T(8,128)(2,1)S(1)}, bf16[128,768]{1,0:T(8,128)(2,1)S(1)}, u32[]{:S(2)}, u32[]{:S(2)}) %collective-permute-start.36) | collective-permute-done | bytes 196640 | tf_op jit(solution)/shard_map/ppermute | solution.py:335
  355.9 1.0 copy.15
  (108 shorter events, 13.6 us)
Async XLA Ops:
  0.0 22.4 %collective-permute-start = (bf16[128,1792]{1,0:T(8,128)(2,1)}, bf16[128,1792]{1,0:T(8,128)(2,1)S(1)}, u32[]{:S(2)}, u32[]{:S(2)}) collective-permute-start(bf16[128,1792]{1,0:T(8,128)(2,1)} %param.9), channel_id=1, source_target_pairs={{0,16},{2,18},{4,20},{6,22},{8,24},{10,26},{12,28},{14,30},{16,0},... | collective-permute-start | bytes 1376264 | tf_op jit(solution)/shard_map/ppermute | solution.py:335
  2.6 20.8 %collective-permute-start.1 = (bf16[128,1792]{1,0:T(8,128)(2,1)}, bf16[128,1792]{1,0:T(8,128)(2,1)S(1)}, u32[]{:S(2)}, u32[]{:S(2)}) collective-permute-start(bf16[128,1792]{1,0:T(8,128)(2,1)} %param.9), channel_id=1, source_target_pairs={{0,8},{2,10},{4,12},{6,14},{8,0},{10,2},{12,4},{14,6},{16,24},{18,... | collective-permute-start | bytes 1376264 | tf_op jit(solution)/shard_map/ppermute | solution.py:335
  4.3 20.9 %copy-start.20 = (s32[16,16]{1,0:T(8,128)S(1)}, s32[16,16]{1,0:T(8,128)}, u32[]{:S(2)}) copy-start(s32[16,16]{1,0:T(8,128)} %constant.24.clone) | copy-start | bytes 3076
  5.0 21.2 %copy-start = (bf16[16,224,512]{2,1,0:T(8,128)(2,1)S(1)}, bf16[16,224,512]{2,1,0:T(8,128)(2,1)}, u32[]{:S(2)}) copy-start(bf16[16,224,512]{2,1,0:T(8,128)(2,1)} %down_ref.3) | copy-start | bytes 11010052
  23.5 12.3 %collective-permute-start.4 = (bf16[256,896]{1,0:T(8,128)(2,1)S(1)}, bf16[256,896]{1,0:T(8,128)(2,1)S(1)}, u32[]{:S(2)}, u32[]{:S(2)}) collective-permute-start(bf16[256,896]{1,0:T(8,128)(2,1)S(1)} %get-tuple-element.169), channel_id=1, source_target_pairs={{0,2},{2,0},{4,6},{6,4},{8,10},{10,8},{12,14},{14,12},{16,18},{18,... | collective-permute-start | bytes 1376264 | tf_op jit(solution)/shard_map/ppermute | solution.py:335
  24.1 12.4 %collective-permute-start.3 = (bf16[256,896]{1,0:T(8,128)(2,1)S(1)}, bf16[256,896]{1,0:T(8,128)(2,1)S(1)}, u32[]{:S(2)}, u32[]{:S(2)}) collective-permute-start(bf16[256,896]{1,0:T(8,128)(2,1)S(1)} %get-tuple-element.170), channel_id=1, source_target_pairs={{0,4},{2,6},{4,0},{6,2},{8,12},{10,14},{12,8},{14,10},{16,20},{18,... | collective-permute-start | bytes 1376264 | tf_op jit(solution)/shard_map/ppermute | solution.py:335
  24.6 11.2 %collective-permute-start.2 = (bf16[128,1792]{1,0:T(8,128)(2,1)S(1)}, bf16[128,1792]{1,0:T(8,128)(2,1)S(1)}, u32[]{:S(2)}, u32[]{:S(2)}) collective-permute-start(bf16[128,1792]{1,0:T(8,128)(2,1)S(1)} %collective-permute-done), channel_id=1, source_target_pairs={{0,8},{2,10},{4,12},{6,14},{8,0},{10,2},{12,4},{14,6},{16,24},{18,... | collective-permute-start | bytes 1376264 | tf_op jit(solution)/shard_map/ppermute | solution.py:335
  26.3 2.0 copy-start.2
  28.3 2.0 copy-start.3
  35.7 8.7 %copy-start.17 = (bf16[128,1792]{1,0:T(8,128)(2,1)S(1)}, bf16[128,1792]{1,0:T(8,128)(2,1)}, u32[]{:S(2)}) copy-start(bf16[128,1792]{1,0:T(8,128)(2,1)} %param.9) | copy-start | bytes 1376260
  35.7 0.8 copy-start.18
  36.5 197.2 %all-to-all-start = ((bf16[16,2032,128]{2,1,0:T(8,128)(2,1)}), bf16[16,2032,128]{2,1,0:T(8,128)(2,1)}, u32[]{:S(2)}, u32[]{:S(2)}) async-start(bf16[16,2032,128]{2,1,0:T(8,128)(2,1)} %pack_first.1), calls=%async_computation | async-start | bytes 16646144 | tf_op jit(solution)/shard_map/all_to_all | solution.py:384
  44.4 1.0 copy-start.19
  45.6 38.6 %collective-permute-start.8 = (bf16[256,896]{1,0:T(8,128)(2,1)S(1)}, bf16[256,896]{1,0:T(8,128)(2,1)S(1)}, u32[]{:S(2)}, u32[]{:S(2)}) collective-permute-start(bf16[256,896]{1,0:T(8,128)(2,1)S(1)} %get-tuple-element.167), channel_id=1, source_target_pairs={{0,2},{2,0},{4,6},{6,4},{8,10},{10,8},{12,14},{14,12},{16,18},{18,... | collective-permute-start | bytes 1376264 | tf_op jit(solution)/shard_map/ppermute | solution.py:335
  46.5 131.2 %collective-permute-start.6 = (bf16[768,896]{1,0:T(8,128)(2,1)S(1)}, bf16[768,896]{1,0:T(8,128)(2,1)S(1)}, u32[]{:S(2)}, u32[]{:S(2)}) collective-permute-start(bf16[768,896]{1,0:T(8,128)(2,1)S(1)} %pad_maximum_fusion.4), channel_id=1, source_target_pairs={{0,2},{2,0},{4,6},{6,4},{8,10},{10,8},{12,14},{14,12},{16,18},{18,... | collective-permute-start | bytes 4128776 | tf_op jit(solution)/shard_map/ppermute | solution.py:335
  48.1 131.1 %collective-permute-start.9 = (bf16[768,896]{1,0:T(8,128)(2,1)S(1)}, bf16[768,896]{1,0:T(8,128)(2,1)S(1)}, u32[]{:S(2)}, u32[]{:S(2)}) collective-permute-start(bf16[768,896]{1,0:T(8,128)(2,1)S(1)} %pad_maximum_fusion.5), channel_id=1, source_target_pairs={{0,4},{2,6},{4,0},{6,2},{8,12},{10,14},{12,8},{14,10},{16,20},{18,... | collective-permute-start | bytes 4128776 | tf_op jit(solution)/shard_map/ppermute | solution.py:335
  48.8 128.9 %collective-permute-start.7 = (bf16[256,1792]{1,0:T(8,128)(2,1)S(1)}, bf16[256,1792]{1,0:T(8,128)(2,1)S(1)}, u32[]{:S(2)}, u32[]{:S(2)}) collective-permute-start(bf16[256,1792]{1,0:T(8,128)(2,1)S(1)} %get-tuple-element.174), channel_id=1, source_target_pairs={{0,6},{2,4},{4,2},{6,0},{8,14},{10,12},{12,10},{14,8},{16,22},{18,... | collective-permute-start | bytes 2752520 | tf_op jit(solution)/shard_map/ppermute | solution.py:414
  50.2 96.5 %collective-permute-start.5 = (bf16[256,896]{1,0:T(8,128)(2,1)S(1)}, bf16[256,896]{1,0:T(8,128)(2,1)S(1)}, u32[]{:S(2)}, u32[]{:S(2)}) collective-permute-start(bf16[256,896]{1,0:T(8,128)(2,1)S(1)} %get-tuple-element.168), channel_id=1, source_target_pairs={{0,4},{2,6},{4,0},{6,2},{8,12},{10,14},{12,8},{14,10},{16,20},{18,... | collective-permute-start | bytes 1376264 | tf_op jit(solution)/shard_map/ppermute | solution.py:335
  84.4 63.8 %copy-start.16 = (bf16[1024,896]{1,0:T(8,128)(2,1)}, bf16[1024,896]{1,0:T(8,128)(2,1)S(1)}, u32[]{:S(2)}) copy-start(bf16[1024,896]{1,0:T(8,128)(2,1)S(1)} %pad_maximum_fusion.2.refs_2_) | copy-start | bytes 5505028
  84.4 154.4 %collective-permute-start.12 = (bf16[1024,896]{1,0:T(8,128)(2,1)S(1)}, bf16[1024,896]{1,0:T(8,128)(2,1)}, u32[]{:S(2)}, u32[]{:S(2)}) collective-permute-start(bf16[1024,896]{1,0:T(8,128)(2,1)S(1)} %pad_maximum_fusion.2.refs_2_), channel_id=1, source_target_pairs={{0,1},{1,0},{2,3},{3,2},{4,5},{5,4},{6,7},{7,6},{8,9},{9,8},{10,11... | collective-permute-start | bytes 5505032 | tf_op jit(solution)/shard_map/ppermute | solution.py:381
  148.2 90.7 %collective-permute-start.10 = (bf16[1024,896]{1,0:T(8,128)(2,1)}, bf16[1024,896]{1,0:T(8,128)(2,1)}, u32[]{:S(2)}, u32[]{:S(2)}) collective-permute-start(bf16[1024,896]{1,0:T(8,128)(2,1)} %pad_maximum_fusion.refs_0_), channel_id=1, source_target_pairs={{0,1},{1,0},{2,3},{3,2},{4,5},{5,4},{6,7},{7,6},{8,9},{9,8},{10,11... | collective-permute-start | bytes 5505032 | tf_op jit(solution)/shard_map/ppermute | solution.py:381
  179.2 59.6 %collective-permute-start.11 = (bf16[1024,896]{1,0:T(8,128)(2,1)}, bf16[1024,896]{1,0:T(8,128)(2,1)}, u32[]{:S(2)}, u32[]{:S(2)}) collective-permute-start(bf16[1024,896]{1,0:T(8,128)(2,1)} %pad_maximum_fusion.1.refs_1_), channel_id=1, source_target_pairs={{0,1},{1,0},{2,3},{3,2},{4,5},{5,4},{6,7},{7,6},{8,9},{9,8},{10,11... | collective-permute-start | bytes 5505032 | tf_op jit(solution)/shard_map/ppermute | solution.py:381
  180.8 58.1 %collective-permute-start.13 = (bf16[1024,896]{1,0:T(8,128)(2,1)}, bf16[1024,896]{1,0:T(8,128)(2,1)}, u32[]{:S(2)}, u32[]{:S(2)}) collective-permute-start(bf16[1024,896]{1,0:T(8,128)(2,1)} %pad_maximum_fusion.3.refs_3_), channel_id=1, source_target_pairs={{0,1},{1,0},{2,3},{3,2},{4,5},{5,4},{6,7},{7,6},{8,9},{9,8},{10,11... | collective-permute-start | bytes 5505032 | tf_op jit(solution)/shard_map/ppermute | solution.py:381
  181.3 2.0 copy-start.1
  233.8 47.6 %all-to-all-start.1 = ((bf16[16,336,128]{2,1,0:T(8,128)(2,1)}), bf16[16,336,128]{2,1,0:T(8,128)(2,1)}, u32[]{:S(2)}, u32[]{:S(2)}) async-start(bf16[16,336,128]{2,1,0:T(8,128)(2,1)} %pack_rest.1), calls=%async_computation.1 | async-start | bytes 2752512 | tf_op jit(solution)/shard_map/all_to_all | solution.py:384
  264.7 5.5 %collective-permute-start.14 = (bf16[2048,512]{1,0:T(8,128)(2,1)}, bf16[2048,512]{1,0:T(8,128)(2,1)S(1)}, u32[]{:S(2)}, u32[]{:S(2)}) collective-permute-start(bf16[2048,512]{1,0:T(8,128)(2,1)} %hidden.1.own_h), channel_id=1, source_target_pairs={{0,1},{1,0},{2,3},{3,2},{4,5},{5,4},{6,7},{7,6},{8,9},{9,8},{10,11... | collective-permute-start | bytes 6291464 | tf_op jit(solution)/shard_map/ppermute | solution.py:381
  266.3 3.8 %copy-start.6 = (bf16[2048,512]{1,0:T(8,128)(2,1)S(1)}, bf16[2048,512]{1,0:T(8,128)(2,1)}, u32[]{:S(2)}) copy-start(bf16[2048,512]{1,0:T(8,128)(2,1)} %hidden.1.own_h) | copy-start | bytes 6291460
  266.5 3.7 %collective-permute-start.15 = (bf16[8,448,128]{2,1,0:T(8,128)(2,1)S(1)}, bf16[8,448,128]{2,1,0:T(8,128)(2,1)S(1)}, u32[]{:S(2)}, u32[]{:S(2)}) collective-permute-start(bf16[8,448,128]{2,1,0:T(8,128)(2,1)S(1)} %get-tuple-element.157), channel_id=1, source_target_pairs={{0,1},{1,0},{2,3},{3,2},{4,5},{5,4},{6,7},{7,6},{8,9},{9,8},{10,11... | collective-permute-start | bytes 2752520 | tf_op jit(solution)/shard_map/ppermute | solution.py:381
  270.1 3.0 copy-start.8
  273.2 0.9 copy-start.12
  274.1 0.9 copy-start.13
  275.0 0.8 copy-start.14
  275.8 1.6 copy-start.9
  280.4 1.0 copy-start.4
  281.4 2.9 copy-start.15
  281.4 3.8 %copy-start.7 = (bf16[2048,512]{1,0:T(8,128)(2,1)S(1)}, bf16[2048,512]{1,0:T(8,128)(2,1)}, u32[]{:S(2)}) copy-start(bf16[2048,512]{1,0:T(8,128)(2,1)} %hidden.1.own_h) | copy-start | bytes 6291460
  282.9 2.2 collective-permute-start.16
  283.1 20.0 %collective-permute-start.17 = (bf16[1024,384]{1,0:T(8,128)(2,1)}, bf16[1024,384]{1,0:T(8,128)(2,1)S(1)}, u32[]{:S(2)}, u32[]{:S(2)}) collective-permute-start(bf16[1024,384]{1,0:T(8,128)(2,1)} %copy-done.13), channel_id=1, source_target_pairs={{0,2},{2,0},{4,6},{6,4},{8,10},{10,8},{12,14},{14,12},{16,18},{18,... | collective-permute-start | bytes 2359304 | tf_op jit(solution)/shard_map/ppermute | solution.py:335
  283.7 19.7 %collective-permute-start.18 = (bf16[1024,384]{1,0:T(8,128)(2,1)}, bf16[1024,384]{1,0:T(8,128)(2,1)S(1)}, u32[]{:S(2)}, u32[]{:S(2)}) collective-permute-start(bf16[1024,384]{1,0:T(8,128)(2,1)} %copy-done.12), channel_id=1, source_target_pairs={{0,4},{2,6},{4,0},{6,2},{8,12},{10,14},{12,8},{14,10},{16,20},{18,... | collective-permute-start | bytes 2359304 | tf_op jit(solution)/shard_map/ppermute | solution.py:335
  284.3 13.6 %collective-permute-start.19 = (bf16[1024,256]{1,0:T(8,128)(2,1)S(1)}, bf16[1024,256]{1,0:T(8,128)(2,1)S(1)}, u32[]{:S(2)}, u32[]{:S(2)}) collective-permute-start(bf16[1024,256]{1,0:T(8,128)(2,1)S(1)} %copy-done.15), channel_id=1, source_target_pairs={{0,8},{2,10},{4,12},{6,14},{8,0},{10,2},{12,4},{14,6},{16,24},{18,... | collective-permute-start | bytes 1572872 | tf_op jit(solution)/shard_map/ppermute | solution.py:335
  285.1 1.6 copy-start.10
  286.7 16.7 %copy-start.5 = (f32[1024,256]{1,0:T(8,128)S(1)}, f32[1024,256]{1,0:T(8,128)}, u32[]{:S(2)}) copy-start(f32[1024,256]{1,0:T(8,128)} %copy-done.4) | copy-start | bytes 3145732
  303.8 20.2 %copy-start.11 = (bf16[2048,512]{1,0:T(8,128)(2,1)S(1)}, bf16[2048,512]{1,0:T(8,128)(2,1)}, u32[]{:S(2)}) copy-start(bf16[2048,512]{1,0:T(8,128)(2,1)} %copy-done.8) | copy-start | bytes 6291460
  303.8 9.3 %collective-permute-start.22 = (bf16[512,256]{1,0:T(8,128)(2,1)S(1)}, bf16[512,256]{1,0:T(8,128)(2,1)S(1)}, u32[]{:S(2)}, u32[]{:S(2)}) collective-permute-start(bf16[512,256]{1,0:T(8,128)(2,1)S(1)} %get-tuple-element.123), channel_id=1, source_target_pairs={{0,2},{2,0},{4,6},{6,4},{8,10},{10,8},{12,14},{14,12},{16,18},{18,... | collective-permute-start | bytes 786440 | tf_op jit(solution)/shard_map/ppermute | solution.py:335
  305.3 17.3 %collective-permute-start.27 = (bf16[1024,256]{1,0:T(8,128)(2,1)S(1)}, bf16[1024,256]{1,0:T(8,128)(2,1)S(1)}, u32[]{:S(2)}, u32[]{:S(2)}) collective-permute-start(bf16[1024,256]{1,0:T(8,128)(2,1)S(1)} %get-tuple-element.109), channel_id=1, source_target_pairs={{0,2},{2,0},{4,6},{6,4},{8,10},{10,8},{12,14},{14,12},{16,18},{18,... | collective-permute-start | bytes 1572872 | tf_op jit(solution)/shard_map/ppermute | solution.py:335
  305.9 12.1 %collective-permute-start.20 = (bf16[512,384]{1,0:T(8,128)(2,1)S(1)}, bf16[512,384]{1,0:T(8,128)(2,1)S(1)}, u32[]{:S(2)}, u32[]{:S(2)}) collective-permute-start(bf16[512,384]{1,0:T(8,128)(2,1)S(1)} %get-tuple-element.119), channel_id=1, source_target_pairs={{0,4},{2,6},{4,0},{6,2},{8,12},{10,14},{12,8},{14,10},{16,20},{18,... | collective-permute-start | bytes 1179656 | tf_op jit(solution)/shard_map/ppermute | solution.py:335
  306.5 12.1 %collective-permute-start.21 = (bf16[512,384]{1,0:T(8,128)(2,1)S(1)}, bf16[512,384]{1,0:T(8,128)(2,1)S(1)}, u32[]{:S(2)}, u32[]{:S(2)}) collective-permute-start(bf16[512,384]{1,0:T(8,128)(2,1)S(1)} %get-tuple-element.121), channel_id=1, source_target_pairs={{0,8},{2,10},{4,12},{6,14},{8,0},{10,2},{12,4},{14,6},{16,24},{18,... | collective-permute-start | bytes 1179656 | tf_op jit(solution)/shard_map/ppermute | solution.py:335
  306.8 22.1 %collective-permute-start.28 = (bf16[1024,256]{1,0:T(8,128)(2,1)S(1)}, bf16[1024,256]{1,0:T(8,128)(2,1)S(1)}, u32[]{:S(2)}, u32[]{:S(2)}) collective-permute-start(bf16[1024,256]{1,0:T(8,128)(2,1)S(1)} %get-tuple-element.110), channel_id=1, source_target_pairs={{0,4},{2,6},{4,0},{6,2},{8,12},{10,14},{12,8},{14,10},{16,20},{18,... | collective-permute-start | bytes 1572872 | tf_op jit(solution)/shard_map/ppermute | solution.py:335
  313.1 16.6 %collective-permute-start.29 = (bf16[1024,256]{1,0:T(8,128)(2,1)S(1)}, bf16[1024,256]{1,0:T(8,128)(2,1)S(1)}, u32[]{:S(2)}, u32[]{:S(2)}) collective-permute-start(bf16[1024,256]{1,0:T(8,128)(2,1)S(1)} %get-tuple-element.111), channel_id=1, source_target_pairs={{0,8},{2,10},{4,12},{6,14},{8,0},{10,2},{12,4},{14,6},{16,24},{18,... | collective-permute-start | bytes 1572872 | tf_op jit(solution)/shard_map/ppermute | solution.py:335
  318.7 13.4 %collective-permute-start.25 = (bf16[256,256]{1,0:T(8,128)(2,1)S(1)}, bf16[256,256]{1,0:T(8,128)(2,1)S(1)}, u32[]{:S(2)}, u32[]{:S(2)}) collective-permute-start(bf16[256,256]{1,0:T(8,128)(2,1)S(1)} %get-tuple-element.129), channel_id=1, source_target_pairs={{0,4},{2,6},{4,0},{6,2},{8,12},{10,14},{12,8},{14,10},{16,20},{18,... | collective-permute-start | bytes 393224 | tf_op jit(solution)/shard_map/ppermute | solution.py:335
  320.2 14.2 %collective-permute-start.23 = (bf16[256,384]{1,0:T(8,128)(2,1)S(1)}, bf16[256,384]{1,0:T(8,128)(2,1)S(1)}, u32[]{:S(2)}, u32[]{:S(2)}) collective-permute-start(bf16[256,384]{1,0:T(8,128)(2,1)S(1)} %get-tuple-element.125), channel_id=1, source_target_pairs={{0,8},{2,10},{4,12},{6,14},{8,0},{10,2},{12,4},{14,6},{16,24},{18,... | collective-permute-start | bytes 589832 | tf_op jit(solution)/shard_map/ppermute | solution.py:335
  322.6 11.8 %collective-permute-start.24 = (bf16[256,384]{1,0:T(8,128)(2,1)S(1)}, bf16[256,384]{1,0:T(8,128)(2,1)S(1)}, u32[]{:S(2)}, u32[]{:S(2)}) collective-permute-start(bf16[256,384]{1,0:T(8,128)(2,1)S(1)} %get-tuple-element.127), channel_id=1, source_target_pairs={{0,2},{2,0},{4,6},{6,4},{8,10},{10,8},{12,14},{14,12},{16,18},{18,... | collective-permute-start | bytes 589832 | tf_op jit(solution)/shard_map/ppermute | solution.py:335
  330.0 8.4 %collective-permute-start.30 = (bf16[512,256]{1,0:T(8,128)(2,1)S(1)}, bf16[512,256]{1,0:T(8,128)(2,1)S(1)}, u32[]{:S(2)}, u32[]{:S(2)}) collective-permute-start(bf16[512,256]{1,0:T(8,128)(2,1)S(1)} %get-tuple-element.144), channel_id=1, source_target_pairs={{0,4},{2,6},{4,0},{6,2},{8,12},{10,14},{12,8},{14,10},{16,20},{18,... | collective-permute-start | bytes 786440 | tf_op jit(solution)/shard_map/ppermute | solution.py:335
  331.5 8.9 %collective-permute-start.31 = (bf16[512,256]{1,0:T(8,128)(2,1)S(1)}, bf16[512,256]{1,0:T(8,128)(2,1)S(1)}, u32[]{:S(2)}, u32[]{:S(2)}) collective-permute-start(bf16[512,256]{1,0:T(8,128)(2,1)S(1)} %get-tuple-element.146), channel_id=1, source_target_pairs={{0,8},{2,10},{4,12},{6,14},{8,0},{10,2},{12,4},{14,6},{16,24},{18,... | collective-permute-start | bytes 786440 | tf_op jit(solution)/shard_map/ppermute | solution.py:335
  332.1 8.3 %collective-permute-start.32 = (bf16[512,256]{1,0:T(8,128)(2,1)S(1)}, bf16[512,256]{1,0:T(8,128)(2,1)S(1)}, u32[]{:S(2)}, u32[]{:S(2)}) collective-permute-start(bf16[512,256]{1,0:T(8,128)(2,1)S(1)} %get-tuple-element.148), channel_id=1, source_target_pairs={{0,2},{2,0},{4,6},{6,4},{8,10},{10,8},{12,14},{14,12},{16,18},{18,... | collective-permute-start | bytes 786440 | tf_op jit(solution)/shard_map/ppermute | solution.py:335
  334.5 16.1 %collective-permute-start.26 = (bf16[128,1024]{1,0:T(8,128)(2,1)S(1)}, bf16[128,1024]{1,0:T(8,128)(2,1)S(1)}, u32[]{:S(2)}, u32[]{:S(2)}) collective-permute-start(bf16[128,1024]{1,0:T(8,128)(2,1)S(1)} %get-tuple-element.131), channel_id=1, source_target_pairs={{0,16},{2,18},{4,20},{6,22},{8,24},{10,26},{12,28},{14,30},{16,0},... | collective-permute-start | bytes 786440 | tf_op jit(solution)/shard_map/ppermute | solution.py:335
  340.6 5.0 %collective-permute-start.33 = (bf16[256,256]{1,0:T(8,128)(2,1)S(1)}, bf16[256,256]{1,0:T(8,128)(2,1)S(1)}, u32[]{:S(2)}, u32[]{:S(2)}) collective-permute-start(bf16[256,256]{1,0:T(8,128)(2,1)S(1)} %get-tuple-element.150), channel_id=1, source_target_pairs={{0,8},{2,10},{4,12},{6,14},{8,0},{10,2},{12,4},{14,6},{16,24},{18,... | collective-permute-start | bytes 393224 | tf_op jit(solution)/shard_map/ppermute | solution.py:335
  340.6 5.0 %collective-permute-start.34 = (bf16[256,256]{1,0:T(8,128)(2,1)S(1)}, bf16[256,256]{1,0:T(8,128)(2,1)S(1)}, u32[]{:S(2)}, u32[]{:S(2)}) collective-permute-start(bf16[256,256]{1,0:T(8,128)(2,1)S(1)} %get-tuple-element.152), channel_id=1, source_target_pairs={{0,2},{2,0},{4,6},{6,4},{8,10},{10,8},{12,14},{14,12},{16,18},{18,... | collective-permute-start | bytes 393224 | tf_op jit(solution)/shard_map/ppermute | solution.py:335
  342.4 5.0 %collective-permute-start.35 = (bf16[256,256]{1,0:T(8,128)(2,1)S(1)}, bf16[256,256]{1,0:T(8,128)(2,1)S(1)}, u32[]{:S(2)}, u32[]{:S(2)}) collective-permute-start(bf16[256,256]{1,0:T(8,128)(2,1)S(1)} %get-tuple-element.154), channel_id=1, source_target_pairs={{0,4},{2,6},{4,0},{6,2},{8,12},{10,14},{12,8},{14,10},{16,20},{18,... | collective-permute-start | bytes 393224 | tf_op jit(solution)/shard_map/ppermute | solution.py:335
  347.4 8.3 %collective-permute-start.36 = (bf16[128,768]{1,0:T(8,128)(2,1)S(1)}, bf16[128,768]{1,0:T(8,128)(2,1)S(1)}, u32[]{:S(2)}, u32[]{:S(2)}) collective-permute-start(bf16[128,768]{1,0:T(8,128)(2,1)S(1)} %get-tuple-element.156), channel_id=1, source_target_pairs={{0,16},{2,18},{4,20},{6,22},{8,24},{10,26},{12,28},{14,30},{16,0},... | collective-permute-start | bytes 589832 | tf_op jit(solution)/shard_map/ppermute | solution.py:335

commit v10 on v5

--- a/solution.py
+++ b/solution.py
@@ -30,73 +30,55 @@
 
 
 def units_of(dest):
-    if dest % 2 == 0:
-        start = 7 * dest // 2
-        return start, start + 3, 0
-    start = (7 * dest + 1) // 2
-    return start, start - 1, 1
-
-
-def pack_rows(slab_of, out_ref, base, dest, lo, rows, per_slab):
+    side = dest % 2
+    first = (7 * dest + side) // 2
+    return first, first + 3 - 4 * side, side
+
+
+def pack_rows(dest, list_ref, in_ref, lo, rows, out_ref, at, base):
+    slabs, depth, width = in_ref.shape
+    per_slab = width // LANES
     first, half, side = units_of(dest)
+
+    def unit_rows(unit, start, size):
+        lane = pl.multiple_of(unit % per_slab * LANES, LANES)
+        return in_ref[list_ref[unit // per_slab], start : start + size, pl.ds(lane, LANES)]
+
     for number in range(3):
-        unit = first + number
-        ref, slab = slab_of(unit // per_slab)
-        lane = (unit % per_slab) * LANES
-        out_ref[dest, base + number * rows : base + (number + 1) * rows, :] = ref[
-            slab, lo : lo + rows, lane : lane + LANES
-        ]
-    ref, slab = slab_of(half // per_slab)
-    lane = (half % per_slab) * LANES
+        out_ref[at, base + number * rows : base + (number + 1) * rows, :] = unit_rows(
+            first + number, lo, rows
+        )
     mid = rows // 2
-    top = ref[slab, lo : lo + mid, lane : lane + LANES].astype(jnp.float32)
-    low = ref[slab, lo + mid : lo + rows, lane : lane + LANES].astype(jnp.float32)
+    top = unit_rows(half, lo, mid).astype(jnp.float32)
+    low = unit_rows(half, lo + mid, mid).astype(jnp.float32)
     left = lax.broadcasted_iota(jnp.int32, (mid, LANES), 1) < HALF
-    if side == 0:
-        both = jnp.where(left, top, pltpu.roll(low, HALF, 1))
-    else:
-        both = jnp.where(left, pltpu.roll(top, HALF, 1), low)
-    out_ref[dest, base + 3 * rows : base + 3 * rows + mid, :] = both.astype(out_ref.dtype)
-
-
-def pack_first_kernel(rows, list_ref, gate_ref, up_ref, down_ref, share_ref, out_ref):
-    slots, depth, width = gate_ref.shape
-    size = depth * 7 // 2
-    row = lax.broadcasted_iota(jnp.int32, share_ref.shape[1:], 0) // 4
-    for dest in range(out_ref.shape[0]):
-        for number, in_ref in enumerate((gate_ref, up_ref)):
-            pack_rows(
-                lambda place, in_ref=in_ref: (in_ref, list_ref[place]),
-                out_ref, number * size, dest, 0, depth, width // LANES,
-            )
-        pack_rows(
-            lambda place: (down_ref, list_ref[place]),
-            out_ref, 2 * size, dest, 0, rows, width // LANES,
-        )
-        value = share_ref[dest]
-        high = value.astype(out_ref.dtype)
-        rest = value - high.astype(jnp.float32)
-        middle = rest.astype(out_ref.dtype)
-        low = (rest - middle.astype(jnp.float32)).astype(out_ref.dtype)
-        terms = jnp.where(
-            row == 0,
-            high.astype(jnp.float32),
-            jnp.where(
-                row == 1,
-                middle.astype(jnp.float32),
-                jnp.where(row == 2, low.astype(jnp.float32), 0.0),
-            ),
-        )
-        out_ref[dest, 2 * size + rows * 7 // 2 :, :] = terms.astype(out_ref.dtype)
-
-
-def pack_rest_kernel(rows, list_ref, down_ref, out_ref):
-    slots, depth, width = down_ref.shape
-    for dest in range(out_ref.shape[0]):
-        pack_rows(
-            lambda place: (down_ref, list_ref[place]),
-            out_ref, 0, dest, rows, depth - rows, width // LANES,
-        )
+    odd = jnp.full((mid, LANES), side, jnp.int32) == 1
+    both = jnp.where(
+        left,
+        jnp.where(odd, pltpu.roll(top, HALF, 1), top),
+        jnp.where(odd, low, pltpu.roll(low, HALF, 1)),
+    )
+    out_ref[at, base + 3 * rows : base + 3 * rows + mid, :] = both.astype(out_ref.dtype)
+
+
+def pack_kernel(segments, with_terms, list_ref, *refs):
+    out_refs = refs[-4:]
+    me = list_ref[list_ref.shape[0] - 1]
+    for j in range(16):
+        dest = me ^ j
+        base = 0
+        for in_ref, (lo, rows) in zip(refs, segments):
+            pack_rows(dest, list_ref, in_ref, lo, rows, out_refs[j // 4], j % 4, base)
+            base += rows * 7 // 2
+        if with_terms:
+            value = refs[len(segments)][dest]
+            row = lax.broadcasted_iota(jnp.int32, value.shape, 0) // 4
+            high = value.astype(jnp.bfloat16).astype(jnp.float32)
+            middle = (value - high).astype(jnp.bfloat16).astype(jnp.float32)
+            low = value - high - middle
+            terms = jnp.where(row == 0, high, jnp.where(row == 1, middle, low))
+            terms = jnp.where(row == 3, 0.0, terms)
+            out_refs[j // 4][j % 4, base:, :] = terms.astype(jnp.bfloat16)
 
 
 def vmem():
@@ -107,62 +89,50 @@
     return pl.BlockSpec(memory_space=pltpu.SMEM)
 
 
-def pack_first(listing, gate_proj, up_proj, down_proj, rows, share, dests):
-    slots, depth, width = gate_proj.shape
-    shape = (dests, depth * 7 + rows * 7 // 2 + share.shape[1], LANES)
+def pack(info, weights, segments, share, name):
+    size = sum(rows * 7 // 2 for _, rows in segments)
+    more = () if share is None else (share,)
+    if more:
+        size += share.shape[1]
     return pl.pallas_call(
-        functools.partial(pack_first_kernel, rows),
-        out_shape=jax.ShapeDtypeStruct(shape, gate_proj.dtype),
-        in_specs=[smem(), vmem(), vmem(), vmem(), vmem()],
-        out_specs=vmem(),
-        compiler_params=pltpu.CompilerParams(vmem_limit_bytes=40 * MIB),
-        name="pack_first",
-    )(listing, gate_proj, up_proj, down_proj, share)
-
-
-def pack_rest(listing, down_proj, rows, dests):
-    slots, depth, width = down_proj.shape
-    shape = (dests, (depth - rows) * 7 // 2, LANES)
-    return pl.pallas_call(
-        functools.partial(pack_rest_kernel, rows),
-        out_shape=jax.ShapeDtypeStruct(shape, down_proj.dtype),
-        in_specs=[smem(), vmem()],
-        out_specs=vmem(),
+        functools.partial(pack_kernel, segments, bool(more)),
+        out_shape=[jax.ShapeDtypeStruct((4, size, LANES), weights[0].dtype)] * 4,
+        in_specs=[smem()] + [vmem()] * (len(weights) + len(more)),
+        out_specs=[vmem()] * 4,
         compiler_params=pltpu.CompilerParams(vmem_limit_bytes=32 * MIB),
-        name="pack_rest",
-    )(listing, down_proj)
-
-
-def unpack_rows(in_ref, at, base, rows, out_ref, out_row, out_lane):
+        name=name,
+    )(info, *weights, *more)
+
+
+def unpack_rows(in_ref, at, rows, out_ref, row):
+    row = pl.multiple_of(row, 16)
     for number in range(3):
-        out_ref[out_row : out_row + rows, out_lane + number * LANES : out_lane + (number + 1) * LANES] = (
-            in_ref[at, base + number * rows : base + (number + 1) * rows, :]
-        )
+        out_ref[pl.ds(row, rows), number * LANES : (number + 1) * LANES] = in_ref[
+            (*at, slice(number * rows, (number + 1) * rows))
+        ]
     mid = rows // 2
-    both = in_ref[at, base + 3 * rows : base + 3 * rows + mid, :]
-    lanes = slice(out_lane + 3 * LANES, out_lane + 4 * LANES)
-    out_ref[out_row : out_row + mid, lanes] = both
-    out_ref[out_row + mid : out_row + rows, lanes] = pltpu.roll(
-        both.astype(jnp.float32), HALF, 1
-    ).astype(out_ref.dtype)
+    both = in_ref[(*at, slice(3 * rows, 3 * rows + mid))]
+    lanes = slice(3 * LANES, 4 * LANES)
+    out_ref[pl.ds(row, mid), lanes] = both
+    other = pltpu.roll(both.astype(jnp.float32), HALF, 1).astype(out_ref.dtype)
+    out_ref[pl.ds(pl.multiple_of(row + mid, 16), mid), lanes] = other
 
 
 def hidden_kernel(at_ref, *refs):
-    pieces, (packed_ref, out_ref, gate_w, up_w, rows) = refs[:8], refs[8:]
-    sources = packed_ref.shape[0]
-    depth = gate_w.shape[0] // sources
-    size = depth * 7 // 2
-    group = sources // 2
+    pieces, gates, ups = refs[:8], refs[8:12], refs[12:16]
+    terms_ref, out_ref, gate_w, up_w, rows = refs[16:]
+    depth = gate_w.shape[0] // 16
     tile = pl.program_id(0)
     x, y, zl = tile // 4, tile // 2 % 2, tile % 2
     me, core = at_ref[0], at_ref[1]
 
     @pl.when(tile == 0)
     def _():
-        for at in range(sources):
-            place = (core + at // group) % 2 * group + at % group
-            unpack_rows(packed_ref, place, 0, depth, gate_w, at * depth, 0)
-            unpack_rows(packed_ref, place, size, depth, up_w, at * depth, 0)
+        for plane in range(4):
+            for column in range(4):
+                place = (me ^ (plane + 4 * column)) ^ (8 * core)
+                unpack_rows(gates[plane], (column,), depth, gate_w, place * depth)
+                unpack_rows(ups[plane], (column,), depth, up_w, place * depth)
 
     mid = pieces[0].shape[1]
     for number in range(4):
@@ -185,9 +155,8 @@
     chosen = jnp.where(chosen, 1.0, 0.0).astype(jnp.bfloat16)
     block = rows.shape[0] // 2
     for zh in range(2):
-        source = me ^ (x + 2 * y + 4 * zl + 8 * zh)
         weight = lax.dot_general(
-            packed_ref[source, packed_ref.shape[1] - 16 :, :],
+            terms_ref[x + 2 * y, zl + 2 * zh],
             chosen,
             (((0,), (0,)), ((), ())),
             preferred_element_type=jnp.float32,
@@ -196,7 +165,7 @@
         out_ref[span, :] = (value[span, :] * weight).astype(out_ref.dtype)
 
 
-def hidden_units(at, pieces, packed):
+def hidden_units(at, pieces, gates, ups, terms):
     total = 2 * pieces[0].shape[0]
     mid = pieces[0].shape[1]
     tile = total // 8
@@ -208,22 +177,23 @@
         lambda i: (i // 4 * 2 + jnp.where(i // 2 % 2 == 1, i % 2, 0), 0),
     ]
     maps = (by_x + by_y) * 2
+    dtype = pieces[0].dtype
     return pl.pallas_call(
         hidden_kernel,
         grid=(8,),
-        out_shape=jax.ShapeDtypeStruct((total, wide), packed.dtype),
+        out_shape=jax.ShapeDtypeStruct((total, wide), dtype),
         in_specs=[smem()]
         + [pl.BlockSpec((tile, mid), where) for where in maps]
-        + [vmem()],
+        + [vmem()] * 9,
         out_specs=pl.BlockSpec((tile, wide), lambda i: (i, 0)),
-        scratch_shapes=[pltpu.VMEM((model, wide), packed.dtype)] * 2
-        + [pltpu.VMEM((tile, model), packed.dtype)],
+        scratch_shapes=[pltpu.VMEM((model, wide), dtype)] * 2
+        + [pltpu.VMEM((tile, model), dtype)],
         compiler_params=pltpu.CompilerParams(vmem_limit_bytes=56 * MIB),
         cost_estimate=pl.CostEstimate(
             flops=4 * total * model * wide, bytes_accessed=24 * MIB, transcendentals=total * wide
         ),
         name="hidden",
-    )(at, *pieces, packed)
+    )(at, *pieces, *gates, *ups, terms)
 
 
 THIRDS = ((0, 1, 2), (1, 2, 0), (2, 0, 1))
@@ -244,11 +214,13 @@
     return [slice((2 * at + side) * size, (2 * at + side + 1) * size) for at in range(1 << axis)]
 
 
-def down_kernel(rows, side, orders, own_h, other_h, own_ref, other_ref, *refs):
+def down_kernel(rows, side, orders, at_ref, own_h, other_h, own_ref, other_ref, *refs):
     out_refs, (own_w, other_w) = refs[:-2], refs[-2:]
     for in_ref, w_ref in ((own_ref, own_w), (other_ref, other_w)):
-        for at in range(in_ref.shape[0]):
-            unpack_rows(in_ref, at, 0, rows, w_ref, at * rows, 0)
+        for plane in range(4):
+            for column in range(2):
+                place = (at_ref[0] ^ (plane + 4 * column)) % 8
+                unpack_rows(in_ref, (plane, column), rows, w_ref, place * rows)
     dims = (((1,), (1,)), ((), ()))
     for number, span in enumerate(group_spans(own_w.shape[0], len(orders))):
         done = 0
@@ -263,8 +235,8 @@
             done += size
 
 
-def down_product(own_h, other_h, own, other, rows, side, orders, dtype, name):
-    sources = own.shape[0]
+def down_product(at, own_h, other_h, own, other, rows, side, orders, dtype, name):
+    sources = own.shape[0] * own.shape[1]
     total, wide = own_h.shape
     tokens = total // 2
     features = sources * rows
@@ -275,7 +247,7 @@
     return pl.pallas_call(
         functools.partial(down_kernel, rows, side, orders),
         out_shape=shapes,
-        in_specs=[vmem()] * 4,
+        in_specs=[smem()] + [vmem()] * 4,
         out_specs=[vmem()] * len(shapes),
         scratch_shapes=[pltpu.VMEM((features, wide), own.dtype)] * 2,
         compiler_params=pltpu.CompilerParams(vmem_limit_bytes=40 * MIB),
@@ -283,7 +255,7 @@
             flops=4 * tokens * wide * features, bytes_accessed=8 * MIB, transcendentals=0
         ),
         name=name,
-    )(own_h, other_h, own, other)
+    )(at, own_h, other_h, own, other)
 
 
 def halve_kernel(axes, *refs):
@@ -380,8 +352,15 @@
     def exchange(value):
         return lax.ppermute(value, "et", [(0, 1), (1, 0)])
 
-    def move(packed):
-        return lax.all_to_all(packed, "ep", 0, 0, tiled=True)
+    def across(value, number):
+        return lax.ppermute(value, "ep", [(i, i ^ number) for i in range(devices)])
+
+    def along_z(packed):
+        return [packed[0]] + [across(packed[k], 4 * k) for k in (1, 2, 3)]
+
+    def in_plane(blocks):
+        parts = [jnp.stack([block[q] for block in blocks]) for q in range(4)]
+        return [parts[0]] + [across(parts[q], q) for q in (1, 2, 3)]
 
     places = []
     for dest in range(devices):
@@ -392,38 +371,55 @@
     belongs = slot_place[None, None, :, None] == places[:, :, None, None]
     share = jnp.sum(jnp.where(belongs, share[None, None], 0.0), axis=2)
 
+    parts = (128, 96)
+    size = depth * 7 // 2
+    at = jnp.stack([me, core]).astype(jnp.int32)
+    info = jnp.concatenate([listing, at[:1]])
+
     near, far = swap(tokens, 2), swap(tokens, 3)
+    gate_z = along_z(pack(info, (gate_proj,), ((0, depth),), share, "pack_gate"))
     corner = swap(far, 2)
-    parts = (128, 96)
-    packed = pack_first(listing, gate_proj, up_proj, down_proj, parts[0], share, devices)
-    packed, near, far, corner = tie((packed, near, far, corner))
-
-    moved = move(packed)
+    up_packed = pack(info, (up_proj,), ((0, depth),), None, "pack_up")
+    gate_z, corner, near, far, up_packed = tie((gate_z, corner, near, far, up_packed))
+
+    up_z = along_z(up_packed)
+    gates = in_plane(gate_z)
     mid = tokens.shape[1] // 2
     rows = jnp.concatenate([tokens, far, near, corner], axis=0)
     first, second = rows[:, :mid], rows[:, mid:]
     first = jnp.concatenate([first, swap(first, 1)], axis=0)
     second = jnp.concatenate([second, swap(second, 0)], axis=0)
+    down_packed = [
+        pack(info, (down_proj,), ((0, parts[0]),), None, "pack_down"),
+        pack(info, (down_proj,), ((parts[0], parts[1]),), None, "pack_down"),
+    ]
+    up_z, gates, first, second, packed0 = tie((up_z, gates, first, second, down_packed[0]))
+
+    down0_z = along_z(packed0)
+    ups = in_plane(up_z)
     pieces = [first, swap(first, 0), second, swap(second, 1)]
     others = [exchange(piece) for piece in pieces]
-    rest = pack_rest(listing, down_proj, parts[0], devices)
-    moved, rest = tie((moved, rest))
-
-    down1 = move(rest)
-    at = jnp.stack([me, core]).astype(jnp.int32)
-    hidden = hidden_units(at, pieces + others, moved)
+    down0_z, ups, packed1 = tie((down0_z, ups, down_packed[1]))
+
+    down1_z = along_z(packed1)
+    downs0 = in_plane(down0_z)
+    terms = jnp.stack([gate[:, size:] for gate in gates])
+    hidden = hidden_units(at, pieces + others, [gate[:, :size] for gate in gates], ups, terms)
     hidden_other = exchange(hidden)
-    down0 = moved[:, depth * 7 : depth * 7 + parts[0] * 7 // 2]
+    downs0, down1_z, hidden = tie((downs0, down1_z, hidden))
+    downs1 = in_plane(down1_z)
+
+    def core_half(downs, which):
+        start = 2 * (which ^ (me >> 3))
+        return jnp.stack([lax.dynamic_slice_in_dim(down, start, 2, 0) for down in downs])
 
     def products(down, rows_in, orders):
-        own = lax.dynamic_slice_in_dim(down, core * group, group, 0)
-        other = exchange(lax.dynamic_slice_in_dim(down, (1 - core) * group, group, 0))
-        args = (hidden, hidden_other, own, other)
+        own, other = core_half(down, core), exchange(core_half(down, 1 - core))
+        args = (at, hidden, hidden_other, own, other)
         sent = down_product(*args, rows_in, 1, orders, jnp.bfloat16, "down_send")
         sent, args = tie((sent, args))
         come = [swap(value, order[0]) for value, order in zip(sent, orders)]
-        kept = down_product(*args, rows_in, 0, orders, jnp.float32, "down_keep")
-        return kept, come, sent
+        return down_product(*args, rows_in, 0, orders, jnp.float32, "down_keep"), come
 
     def stage(kept, come, number, orders):
         axes = tuple(stage_axis(order, number) for order in orders)
@@ -436,10 +432,9 @@
         come = swap(send, 3)
         return (keep + come.astype(jnp.float32)).astype(jnp.bfloat16)
 
-    kept0, come0, _ = products(down0, parts[0], THIRDS)
-    down1, kept0 = tie((down1, kept0))
-    kept1, come1, sent1 = products(down1, parts[1], THIRDS)
-    kept0, _ = tie((kept0, sent1))
+    kept0, come0 = products(downs0, parts[0], THIRDS)
+    downs1, kept0 = tie((downs1, kept0))
+    kept1, come1 = products(downs1, parts[1], THIRDS)
     kept0, come0 = stage(kept0, come0, 1, THIRDS)
     kept1, come1 = stage(kept1, come1, 1, THIRDS)
     kept0, come0 = stage(kept0, come0, 2, THIRDS)

time: 359 us -> 413 us (1.15)
  waiting for transfers between devices: 235 us -> 258 us
  starting transfers between devices: 49.5 us -> 63.2 us
  local copies, waits for them, and re-layouts: 19.8 us -> 28.7 us
  other arithmetic: 6.13 us -> 13.3 us
    ppermute x0 -> x24, waiting for transfers between devices: none -> 147 us  [across(): return lax.ppermute(value, 'ep', [(i, i ^ number) for i in range(devices)])]
    ppermute x27, waiting for transfers between devices: 198 us -> 111 us  [swap(): return lax.ppermute(value, 'ep', [(i, i ^ 1 << bit) for i in range(size)])]
    all_to_all x2 -> x0, waiting for transfers between devices: 33.9 us -> none  [move(): return lax.all_to_all(packed, 'ep', 0, 0, tiled=True)]
    ppermute x0 -> x24, starting transfers between devices: none -> 27.6 us  [across(): return lax.ppermute(value, 'ep', [(i, i ^ number) for i in range(devices)])]
    all_to_all x2 -> x0, starting transfers between devices: 17.5 us -> none  [move(): return lax.all_to_all(packed, 'ep', 0, 0, tiled=True)]
    slice x1 -> x18, local copies, waits for them, and re-layouts: 1.63 us -> 11.8 us  [the longest x4 7.25 us: packed_layer(): gate[:, :size]]
    another operation x0 -> x21, other arithmetic: none -> 7.05 us  [the longest x16 6 us: in_plane(): parts = [jnp.stack([block[q] for block in blocks]) for q in range(4)]]
    unnamed x39 -> x77, local copies, waits for them, and re-layouts: 15 us -> 12.9 us
  transfers between devices with their start and end apart: 36 -> 58, of which waited for: 21 -> 29; matrix products, arithmetic and copies ran while one was open for 2% -> 7% of each run, Pallas kernels for 12% -> 11%
where the time goes in v10:
time: 413 us; the launch traced here: 409 us
  waiting for transfers between devices  258 us (62%)
  starting transfers between devices  63.2 us (15%)
  Pallas kernels  45.6 us (11%)
  local copies, waits for them, and re-layouts  28.7 us (7%)
  other arithmetic  13.3 us (3%)
    ppermute x24, waiting for transfers between devices, across(): return lax.ppermute(value, 'ep', [(i, i ^ number) for i in range(devices)])  147 us
    ppermute x27, waiting for transfers between devices, swap(): return lax.ppermute(value, 'ep', [(i, i ^ 1 << bit) for i in range(size)])  111 us
    ppermute x27, starting transfers between devices, swap(): return lax.ppermute(value, 'ep', [(i, i ^ 1 << bit) for i in range(size)])  34.3 us
    ppermute x24, starting transfers between devices, across(): return lax.ppermute(value, 'ep', [(i, i ^ number) for i in range(devices)])  27.6 us
    pallas_call x1, Pallas kernels, hidden_units(): pl.pallas_call(hidden_kernel, grid=(8,), out_shape=jax.ShapeDtypeStruct((...  25.8 us
    unnamed x77, local copies, waits for them, and re-layouts  12.9 us
    pallas_call x4, Pallas kernels, down_product(): pl.pallas_call(functools.partial(down_kernel, rows, side, orders), out_sh...  12.8 us
  transfers between devices with their start and end apart: 58, of which 29 were waited for; matrix products, arithmetic and copies ran while one was open for 7% of the time, Pallas kernels for 11%

profile of v10, /device:TPU:14, one launch (start us, length us, event | category | flops | bytes accessed | tf_op | source)
XLA Modules:
  0.0 409.3 jit_solution(13229391379645304012)
XLA Ops:
  0.0 2.6 collective-permute-start.3
  6.5 2.0 copy-done.1
  8.5 1.7 pack_gate.1
  11.1 2.7 collective-permute-start.2
  13.8 1.3 collective-permute-start.5
  15.1 7.4 %collective-permute-done.3 = bf16[128,1792]{1,0:T(8,128)(2,1)} collective-permute-done((bf16[128,1792]{1,0:T(8,128)(2,1)}, bf16[128,1792]{1,0:T(8,128)(2,1)}, u32[]{:S(2)}, u32[]{:S(2)}) %collective-permute-start.3) | collective-permute-done | bytes 458784 | tf_op jit(solution)/shard_map/ppermute | solution.py:307
  22.5 2.4 collective-permute-start.4
  25.0 1.6 pack_up.1
  26.7 56.3 %collective-permute-done.5 = bf16[128,1792]{1,0:T(8,128)(2,1)S(1)} collective-permute-done((bf16[128,1792]{1,0:T(8,128)(2,1)}, bf16[128,1792]{1,0:T(8,128)(2,1)S(1)}, u32[]{:S(2)}, u32[]{:S(2)}) %collective-permute-start.5) | collective-permute-done | bytes 458784 | tf_op jit(solution)/shard_map/ppermute | solution.py:307
  83.0 9.6 %collective-permute-done.2 = bf16[4,800,128]{2,1,0:T(8,128)(2,1)S(1)} collective-permute-done((bf16[4,800,128]{2,1,0:T(8,128)(2,1)S(1)}, bf16[4,800,128]{2,1,0:T(8,128)(2,1)S(1)}, u32[]{:S(2)}, u32[]{:S(2)}) %collective-permute-start.2) | collective-permute-done | bytes 819232 | tf_op jit(solution)/shard_map/ppermute | solution.py:356
  93.9 1.4 collective-permute-start.6
  98.9 1.5 collective-permute-start.9
  101.5 1.5 collective-permute-start.10
  104.0 9.8 %collective-permute-done.6 = bf16[4,784,128]{2,1,0:T(8,128)(2,1)S(1)} collective-permute-done((bf16[4,784,128]{2,1,0:T(8,128)(2,1)S(1)}, bf16[4,784,128]{2,1,0:T(8,128)(2,1)S(1)}, u32[]{:S(2)}, u32[]{:S(2)}) %collective-permute-start.6) | collective-permute-done | bytes 802848 | tf_op jit(solution)/shard_map/ppermute | solution.py:356
  114.3 4.3 %collective-permute-done.13 = bf16[512,896]{1,0:T(8,128)(2,1)S(1)} collective-permute-done((bf16[512,896]{1,0:T(8,128)(2,1)S(1)}, bf16[512,896]{1,0:T(8,128)(2,1)S(1)}, u32[]{:S(2)}, u32[]{:S(2)}) %collective-permute-start.13) | collective-permute-done | bytes 917536 | tf_op jit(solution)/shard_map/ppermute | solution.py:307
  118.6 2.6 collective-permute-start.7
  122.1 2.0 copy-done
  124.2 1.3 pack_down.3
  127.7 1.4 pack_down.2
  133.4 1.5 pad_maximum_fusion.1.refs_2_
  135.3 35.2 %collective-permute-done.7 = bf16[4,784,128]{2,1,0:T(8,128)(2,1)} collective-permute-done((bf16[4,784,128]{2,1,0:T(8,128)(2,1)S(1)}, bf16[4,784,128]{2,1,0:T(8,128)(2,1)}, u32[]{:S(2)}, u32[]{:S(2)}) %collective-permute-start.7) | collective-permute-done | bytes 802848 | tf_op jit(solution)/shard_map/ppermute | solution.py:356
  170.5 17.3 %collective-permute-done.8 = bf16[4,784,128]{2,1,0:T(8,128)(2,1)} collective-permute-done((bf16[4,784,128]{2,1,0:T(8,128)(2,1)S(1)}, bf16[4,784,128]{2,1,0:T(8,128)(2,1)}, u32[]{:S(2)}, u32[]{:S(2)}) %collective-permute-start.8) | collective-permute-done | bytes 802848 | tf_op jit(solution)/shard_map/ppermute | solution.py:356
  187.9 3.8 collective-permute-start.15
  192.9 1.3 fusion.10
  194.2 1.3 fusion.11
  195.7 11.8 %collective-permute-done.14 = bf16[4,448,128]{2,1,0:T(8,128)(2,1)S(1)} collective-permute-done((bf16[4,448,128]{2,1,0:T(8,128)(2,1)S(1)}, bf16[4,448,128]{2,1,0:T(8,128)(2,1)S(1)}, u32[]{:S(2)}, u32[]{:S(2)}) %collective-permute-start.14) | collective-permute-done | bytes 458784 | tf_op jit(solution)/shard_map/ppermute | solution.py:356
  208.0 14.3 %collective-permute-done.15 = bf16[4,448,128]{2,1,0:T(8,128)(2,1)S(1)} collective-permute-done((bf16[4,448,128]{2,1,0:T(8,128)(2,1)S(1)}, bf16[4,448,128]{2,1,0:T(8,128)(2,1)S(1)}, u32[]{:S(2)}, u32[]{:S(2)}) %collective-permute-start.15) | collective-permute-done | bytes 458784 | tf_op jit(solution)/shard_map/ppermute | solution.py:356
  222.9 8.0 %collective-permute-done.16 = bf16[4,448,128]{2,1,0:T(8,128)(2,1)S(1)} collective-permute-done((bf16[4,448,128]{2,1,0:T(8,128)(2,1)S(1)}, bf16[4,448,128]{2,1,0:T(8,128)(2,1)S(1)}, u32[]{:S(2)}, u32[]{:S(2)}) %collective-permute-start.16) | collective-permute-done | bytes 458784 | tf_op jit(solution)/shard_map/ppermute | solution.py:356
  233.1 2.1 slice.273.refs_9_
  235.2 2.1 slice.274.refs_10_
  237.2 2.1 slice.275.refs_11_
  240.1 11.8 %collective-permute-done.17.refs_13_ = bf16[4,784,128]{2,1,0:T(8,128)(2,1)S(1)} collective-permute-done((bf16[4,784,128]{2,1,0:T(8,128)(2,1)S(1)}, bf16[4,784,128]{2,1,0:T(8,128)(2,1)S(1)}, u32[]{:S(2)}, u32[]{:S(2)}) %collective-permute-start.17) | collective-permute-done | bytes 802848 | tf_op jit(solution)/shard_map/ppermute | solution.py:356
  251.9 16.0 %collective-permute-done.18.refs_14_ = bf16[4,784,128]{2,1,0:T(8,128)(2,1)} collective-permute-done((bf16[4,784,128]{2,1,0:T(8,128)(2,1)S(1)}, bf16[4,784,128]{2,1,0:T(8,128)(2,1)}, u32[]{:S(2)}, u32[]{:S(2)}) %collective-permute-start.18) | collective-permute-done | bytes 802848 | tf_op jit(solution)/shard_map/ppermute | solution.py:356
  271.0 1.6 collective-permute-start.23
  273.0 8.4 %collective-permute-done.23 = bf16[4,336,128]{2,1,0:T(8,128)(2,1)S(1)} collective-permute-done((bf16[4,336,128]{2,1,0:T(8,128)(2,1)S(1)}, bf16[4,336,128]{2,1,0:T(8,128)(2,1)S(1)}, u32[]{:S(2)}, u32[]{:S(2)}) %collective-permute-start.23) | collective-permute-done | bytes 344096 | tf_op jit(solution)/shard_map/ppermute | solution.py:356
  281.4 2.4 collective-permute-start.24
  284.5 1.5 collective-permute-start.20
  287.2 1.3 copy-done.34
  289.3 25.8 %hidden.1.own_h = bf16[2048,512]{1,0:T(8,128)(2,1)} custom-call(s32[2]{0:T(128)} %pad_add_fusion.1.at_ref, bf16[1024,896]{1,0:T(8,128)(2,1)} %copy-done.22, bf16[1024,896]{1,0:T(8,128)(2,1)} %copy-done.29, bf16[1024,896]{1,0:T(8,128)(2,1)} %copy-done.21, bf16[1024,896]{1,0:T(8,128)(2,1)} %copy-done.30, bf16[1024,896]{1,0:T(8,128)(2,1)} %copy-done.31, ...), custom_call_target="tpu_custom_call" | custom-call | flops 15032385536 | bytes 25165824 | tf_op jit(solution)/shard_map/hidden/pallas_call | solution.py:181
  316.2 1.6 collective-permute-start.32
  317.8 1.3 collective-permute-start.33
  320.6 3.7 down_send.2
  324.3 1.6 collective-permute-start.37
  327.1 3.7 down_keep.2
  330.9 4.6 %collective-permute-done.33 = bf16[4,336,128]{2,1,0:T(8,128)(2,1)S(1)} collective-permute-done((bf16[4,336,128]{2,1,0:T(8,128)(2,1)S(1)}, bf16[4,336,128]{2,1,0:T(8,128)(2,1)S(1)}, u32[]{:S(2)}, u32[]{:S(2)}) %collective-permute-start.33) | collective-permute-done | bytes 344096 | tf_op jit(solution)/shard_map/ppermute | solution.py:356
  335.8 1.5 collective-permute-start.39
  337.3 12.8 %collective-permute-done.39.refs_5_ = bf16[1024,256]{1,0:T(8,128)(2,1)S(1)} collective-permute-done((bf16[1024,256]{1,0:T(8,128)(2,1)S(1)}, bf16[1024,256]{1,0:T(8,128)(2,1)S(1)}, u32[]{:S(2)}, u32[]{:S(2)}) %collective-permute-start.39) | collective-permute-done | bytes 524320 | tf_op jit(solution)/shard_map/ppermute | solution.py:307
  350.5 1.3 collective-permute-done.38.refs_3_
  352.8 2.7 down_send.3
  355.5 1.5 collective-permute-start.48
  358.2 1.4 collective-permute-start.41
  361.5 1.4 collective-permute-start.50
  362.9 6.2 %collective-permute-done.40.refs_1_ = bf16[512,384]{1,0:T(8,128)(2,1)S(1)} collective-permute-done((bf16[512,384]{1,0:T(8,128)(2,1)S(1)}, bf16[512,384]{1,0:T(8,128)(2,1)S(1)}, u32[]{:S(2)}, u32[]{:S(2)}) %collective-permute-start.40) | collective-permute-done | bytes 393248 | tf_op jit(solution)/shard_map/ppermute | solution.py:307
  371.3 1.4 collective-permute-start.43
  373.3 2.6 down_keep.3
  375.9 4.1 collective-permute-done.49.refs_3_
  382.6 1.4 collective-permute-start.52
  384.6 2.4 collective-permute-done.43.refs_1_
  387.1 3.4 collective-permute-start.46
  391.6 1.5 collective-permute-start.54
  393.1 3.3 collective-permute-start.55
  397.1 2.2 collective-permute-done.55.refs_3_
  399.3 2.0 collective-permute-done.56.refs_5_
  402.2 5.9 %collective-permute-done.57 = bf16[128,768]{1,0:T(8,128)(2,1)S(1)} collective-permute-done((bf16[128,768]{1,0:T(8,128)(2,1)S(1)}, bf16[128,768]{1,0:T(8,128)(2,1)S(1)}, u32[]{:S(2)}, u32[]{:S(2)}) %collective-permute-start.57) | collective-permute-done | bytes 196640 | tf_op jit(solution)/shard_map/ppermute | solution.py:307
  (215 shorter events, 50.3 us)
Async XLA Ops:
  0.0 22.5 %collective-permute-start.3 = (bf16[128,1792]{1,0:T(8,128)(2,1)}, bf16[128,1792]{1,0:T(8,128)(2,1)}, u32[]{:S(2)}, u32[]{:S(2)}) collective-permute-start(bf16[128,1792]{1,0:T(8,128)(2,1)} %param.9), channel_id=1, source_target_pairs={{0,16},{2,18},{4,20},{6,22},{8,24},{10,26},{12,28},{14,30},{16,0},... | collective-permute-start | bytes 1376264 | tf_op jit(solution)/shard_map/ppermute | solution.py:307
  10.2 72.8 %collective-permute-start = (bf16[4,800,128]{2,1,0:T(8,128)(2,1)S(1)}, bf16[4,800,128]{2,1,0:T(8,128)(2,1)S(1)}, u32[]{:S(2)}, u32[]{:S(2)}) collective-permute-start(bf16[4,800,128]{2,1,0:T(8,128)(2,1)S(1)} %get-tuple-element.131), channel_id=1, source_target_pairs={{0,8},{2,10},{4,12},{6,14},{8,0},{10,2},{12,4},{14,6},{16,24},{18,... | collective-permute-start | bytes 2457608 | tf_op jit(solution)/shard_map/ppermute | solution.py:356
  10.7 72.3 %collective-permute-start.1 = (bf16[4,800,128]{2,1,0:T(8,128)(2,1)S(1)}, bf16[4,800,128]{2,1,0:T(8,128)(2,1)S(1)}, u32[]{:S(2)}, u32[]{:S(2)}) collective-permute-start(bf16[4,800,128]{2,1,0:T(8,128)(2,1)S(1)} %get-tuple-element.132), channel_id=1, source_target_pairs={{0,16},{2,18},{4,20},{6,22},{8,24},{10,26},{12,28},{14,30},{16,0},... | collective-permute-start | bytes 2457608 | tf_op jit(solution)/shard_map/ppermute | solution.py:356
  11.1 81.6 %collective-permute-start.2 = (bf16[4,800,128]{2,1,0:T(8,128)(2,1)S(1)}, bf16[4,800,128]{2,1,0:T(8,128)(2,1)S(1)}, u32[]{:S(2)}, u32[]{:S(2)}) collective-permute-start(bf16[4,800,128]{2,1,0:T(8,128)(2,1)S(1)} %get-tuple-element.133), channel_id=1, source_target_pairs={{0,24},{2,26},{4,28},{6,30},{8,16},{10,18},{12,20},{14,22},{16,8},... | collective-permute-start | bytes 2457608 | tf_op jit(solution)/shard_map/ppermute | solution.py:356
  13.8 69.2 %collective-permute-start.5 = (bf16[128,1792]{1,0:T(8,128)(2,1)}, bf16[128,1792]{1,0:T(8,128)(2,1)S(1)}, u32[]{:S(2)}, u32[]{:S(2)}) collective-permute-start(bf16[128,1792]{1,0:T(8,128)(2,1)} %param.9), channel_id=1, source_target_pairs={{0,8},{2,10},{4,12},{6,14},{8,0},{10,2},{12,4},{14,6},{16,24},{18,... | collective-permute-start | bytes 1376264 | tf_op jit(solution)/shard_map/ppermute | solution.py:307
  22.5 70.1 %collective-permute-start.4 = (bf16[128,1792]{1,0:T(8,128)(2,1)}, bf16[128,1792]{1,0:T(8,128)(2,1)S(1)}, u32[]{:S(2)}, u32[]{:S(2)}) collective-permute-start(bf16[128,1792]{1,0:T(8,128)(2,1)} %collective-permute-done.3), channel_id=1, source_target_pairs={{0,8},{2,10},{4,12},{6,14},{8,0},{10,2},{12,4},{14,6},{16,24},{18,... | collective-permute-start | bytes 1376264 | tf_op jit(solution)/shard_map/ppermute | solution.py:307
  93.9 19.9 %collective-permute-start.6 = (bf16[4,784,128]{2,1,0:T(8,128)(2,1)S(1)}, bf16[4,784,128]{2,1,0:T(8,128)(2,1)S(1)}, u32[]{:S(2)}, u32[]{:S(2)}) collective-permute-start(bf16[4,784,128]{2,1,0:T(8,128)(2,1)S(1)} %get-tuple-element.139), channel_id=1, source_target_pairs={{0,8},{2,10},{4,12},{6,14},{8,0},{10,2},{12,4},{14,6},{16,24},{18,... | collective-permute-start | bytes 2408456 | tf_op jit(solution)/shard_map/ppermute | solution.py:356
  95.3 23.3 %collective-permute-start.13 = (bf16[512,896]{1,0:T(8,128)(2,1)S(1)}, bf16[512,896]{1,0:T(8,128)(2,1)S(1)}, u32[]{:S(2)}, u32[]{:S(2)}) collective-permute-start(bf16[512,896]{1,0:T(8,128)(2,1)S(1)} %get-tuple-element.255), channel_id=1, source_target_pairs={{0,2},{2,0},{4,6},{6,4},{8,10},{10,8},{12,14},{14,12},{16,18},{18,... | collective-permute-start | bytes 2752520 | tf_op jit(solution)/shard_map/ppermute | solution.py:307
  95.8 25.4 %collective-permute-start.12 = (bf16[512,896]{1,0:T(8,128)(2,1)S(1)}, bf16[512,896]{1,0:T(8,128)(2,1)S(1)}, u32[]{:S(2)}, u32[]{:S(2)}) collective-permute-start(bf16[512,896]{1,0:T(8,128)(2,1)S(1)} %get-tuple-element.256), channel_id=1, source_target_pairs={{0,4},{2,6},{4,0},{6,2},{8,12},{10,14},{12,8},{14,10},{16,20},{18,... | collective-permute-start | bytes 2752520 | tf_op jit(solution)/shard_map/ppermute | solution.py:307
  98.9 88.9 %collective-permute-start.9 = (bf16[4,800,128]{2,1,0:T(8,128)(2,1)}, bf16[4,800,128]{2,1,0:T(8,128)(2,1)}, u32[]{:S(2)}, u32[]{:S(2)}) collective-permute-start(bf16[4,800,128]{2,1,0:T(8,128)(2,1)} %pad_maximum_fusion.5), channel_id=1, source_target_pairs={{0,2},{2,0},{4,6},{6,4},{8,10},{10,8},{12,14},{14,12},{16,18},{18,... | collective-permute-start | bytes 2457608 | tf_op jit(solution)/shard_map/ppermute | solution.py:356
  101.5 86.3 %collective-permute-start.10 = (bf16[4,800,128]{2,1,0:T(8,128)(2,1)}, bf16[4,800,128]{2,1,0:T(8,128)(2,1)}, u32[]{:S(2)}, u32[]{:S(2)}) collective-permute-start(bf16[4,800,128]{2,1,0:T(8,128)(2,1)} %pad_maximum_fusion.6), channel_id=1, source_target_pairs={{0,4},{2,6},{4,0},{6,2},{8,12},{10,14},{12,8},{14,10},{16,20},{18,... | collective-permute-start | bytes 2457608 | tf_op jit(solution)/shard_map/ppermute | solution.py:356
  113.8 74.0 %collective-permute-start.11 = (bf16[4,800,128]{2,1,0:T(8,128)(2,1)}, bf16[4,800,128]{2,1,0:T(8,128)(2,1)}, u32[]{:S(2)}, u32[]{:S(2)}) collective-permute-start(bf16[4,800,128]{2,1,0:T(8,128)(2,1)} %pad_maximum_fusion.7), channel_id=1, source_target_pairs={{0,6},{2,4},{4,2},{6,0},{8,14},{10,12},{12,10},{14,8},{16,22},{18,... | collective-permute-start | bytes 2457608 | tf_op jit(solution)/shard_map/ppermute | solution.py:356
  118.6 51.9 %collective-permute-start.7 = (bf16[4,784,128]{2,1,0:T(8,128)(2,1)S(1)}, bf16[4,784,128]{2,1,0:T(8,128)(2,1)}, u32[]{:S(2)}, u32[]{:S(2)}) collective-permute-start(bf16[4,784,128]{2,1,0:T(8,128)(2,1)S(1)} %get-tuple-element.140), channel_id=1, source_target_pairs={{0,16},{2,18},{4,20},{6,22},{8,24},{10,26},{12,28},{14,30},{16,0},... | collective-permute-start | bytes 2408456 | tf_op jit(solution)/shard_map/ppermute | solution.py:356
  122.1 65.7 %collective-permute-start.8 = (bf16[4,784,128]{2,1,0:T(8,128)(2,1)S(1)}, bf16[4,784,128]{2,1,0:T(8,128)(2,1)}, u32[]{:S(2)}, u32[]{:S(2)}) collective-permute-start(bf16[4,784,128]{2,1,0:T(8,128)(2,1)S(1)} %get-tuple-element.141), channel_id=1, source_target_pairs={{0,24},{2,26},{4,28},{6,30},{8,16},{10,18},{12,20},{14,22},{16,8},... | collective-permute-start | bytes 2408456 | tf_op jit(solution)/shard_map/ppermute | solution.py:356
  135.1 132.7 %copy-start.21 = (bf16[1024,896]{1,0:T(8,128)(2,1)}, bf16[1024,896]{1,0:T(8,128)(2,1)S(1)}, u32[]{:S(2)}) copy-start(bf16[1024,896]{1,0:T(8,128)(2,1)S(1)} %pad_maximum_fusion.1.refs_2_) | copy-start | bytes 5505028
  135.1 52.7 %copy-start.9 = (bf16[4,448,128]{2,1,0:T(8,128)(2,1)S(1)}, bf16[4,448,128]{2,1,0:T(8,128)(2,1)}, u32[]{:S(2)}) copy-start(bf16[4,448,128]{2,1,0:T(8,128)(2,1)} %copy-done.8) | copy-start | bytes 1376260
  135.1 52.8 %copy-start.7 = (bf16[4,448,128]{2,1,0:T(8,128)(2,1)S(1)}, bf16[4,448,128]{2,1,0:T(8,128)(2,1)}, u32[]{:S(2)}) copy-start(bf16[4,448,128]{2,1,0:T(8,128)(2,1)} %copy-done.6) | copy-start | bytes 1376260
  135.1 56.6 %copy-start.5 = (bf16[4,448,128]{2,1,0:T(8,128)(2,1)S(1)}, bf16[4,448,128]{2,1,0:T(8,128)(2,1)}, u32[]{:S(2)}) copy-start(bf16[4,448,128]{2,1,0:T(8,128)(2,1)} %copy-done.4) | copy-start | bytes 1376260
  135.1 57.7 %copy-start.27 = (bf16[4,784,128]{2,1,0:T(8,128)(2,1)S(1)}, bf16[4,784,128]{2,1,0:T(8,128)(2,1)}, u32[]{:S(2)}) copy-start(bf16[4,784,128]{2,1,0:T(8,128)(2,1)} %copy-done.26) | copy-start | bytes 2408452
  135.3 116.6 %copy-start.22 = (bf16[1024,896]{1,0:T(8,128)(2,1)}, bf16[1024,896]{1,0:T(8,128)(2,1)S(1)}, u32[]{:S(2)}) copy-start(bf16[1024,896]{1,0:T(8,128)(2,1)S(1)} %pad_maximum_fusion.refs_0_) | copy-start | bytes 5505028
  187.8 19.6 %collective-permute-start.14 = (bf16[4,448,128]{2,1,0:T(8,128)(2,1)S(1)}, bf16[4,448,128]{2,1,0:T(8,128)(2,1)S(1)}, u32[]{:S(2)}, u32[]{:S(2)}) collective-permute-start(bf16[4,448,128]{2,1,0:T(8,128)(2,1)S(1)} %copy-done.9), channel_id=1, source_target_pairs={{0,8},{2,10},{4,12},{6,14},{8,0},{10,2},{12,4},{14,6},{16,24},{18,... | collective-permute-start | bytes 1376264 | tf_op jit(solution)/shard_map/ppermute | solution.py:356
  187.9 34.4 %collective-permute-start.15 = (bf16[4,448,128]{2,1,0:T(8,128)(2,1)S(1)}, bf16[4,448,128]{2,1,0:T(8,128)(2,1)S(1)}, u32[]{:S(2)}, u32[]{:S(2)}) collective-permute-start(bf16[4,448,128]{2,1,0:T(8,128)(2,1)S(1)} %copy-done.7), channel_id=1, source_target_pairs={{0,16},{2,18},{4,20},{6,22},{8,24},{10,26},{12,28},{14,30},{16,0},... | collective-permute-start | bytes 1376264 | tf_op jit(solution)/shard_map/ppermute | solution.py:356
  191.7 39.2 %collective-permute-start.16 = (bf16[4,448,128]{2,1,0:T(8,128)(2,1)S(1)}, bf16[4,448,128]{2,1,0:T(8,128)(2,1)S(1)}, u32[]{:S(2)}, u32[]{:S(2)}) collective-permute-start(bf16[4,448,128]{2,1,0:T(8,128)(2,1)S(1)} %copy-done.5), channel_id=1, source_target_pairs={{0,24},{2,26},{4,28},{6,30},{8,16},{10,18},{12,20},{14,22},{16,8},... | collective-permute-start | bytes 1376264 | tf_op jit(solution)/shard_map/ppermute | solution.py:356
  191.7 76.2 %collective-permute-start.26 = (bf16[1024,896]{1,0:T(8,128)(2,1)S(1)}, bf16[1024,896]{1,0:T(8,128)(2,1)S(1)}, u32[]{:S(2)}, u32[]{:S(2)}) collective-permute-start(bf16[1024,896]{1,0:T(8,128)(2,1)S(1)} %pad_maximum_fusion.refs_0_), channel_id=1, source_target_pairs={{0,2},{2,0},{4,6},{6,4},{8,10},{10,8},{12,14},{14,12},{16,18},{18,... | collective-permute-start | bytes 5505032 | tf_op jit(solution)/shard_map/ppermute | solution.py:307
  192.3 76.2 %collective-permute-start.27 = (bf16[1024,896]{1,0:T(8,128)(2,1)S(1)}, bf16[1024,896]{1,0:T(8,128)(2,1)S(1)}, u32[]{:S(2)}, u32[]{:S(2)}) collective-permute-start(bf16[1024,896]{1,0:T(8,128)(2,1)S(1)} %pad_maximum_fusion.1.refs_2_), channel_id=1, source_target_pairs={{0,4},{2,6},{4,0},{6,2},{8,12},{10,14},{12,8},{14,10},{16,20},{18,... | collective-permute-start | bytes 5505032 | tf_op jit(solution)/shard_map/ppermute | solution.py:307
  207.5 44.4 %collective-permute-start.17 = (bf16[4,784,128]{2,1,0:T(8,128)(2,1)S(1)}, bf16[4,784,128]{2,1,0:T(8,128)(2,1)S(1)}, u32[]{:S(2)}, u32[]{:S(2)}) collective-permute-start(bf16[4,784,128]{2,1,0:T(8,128)(2,1)S(1)} %pad_maximum_fusion.9), channel_id=1, source_target_pairs={{0,2},{2,0},{4,6},{6,4},{8,10},{10,8},{12,14},{14,12},{16,18},{18,... | collective-permute-start | bytes 2408456 | tf_op jit(solution)/shard_map/ppermute | solution.py:356
  222.3 45.5 %collective-permute-start.18 = (bf16[4,784,128]{2,1,0:T(8,128)(2,1)S(1)}, bf16[4,784,128]{2,1,0:T(8,128)(2,1)}, u32[]{:S(2)}, u32[]{:S(2)}) collective-permute-start(bf16[4,784,128]{2,1,0:T(8,128)(2,1)S(1)} %pad_maximum_fusion.10), channel_id=1, source_target_pairs={{0,4},{2,6},{4,0},{6,2},{8,12},{10,14},{12,8},{14,10},{16,20},{18,... | collective-permute-start | bytes 2408456 | tf_op jit(solution)/shard_map/ppermute | solution.py:356
  230.9 40.0 %collective-permute-start.19 = (bf16[4,784,128]{2,1,0:T(8,128)(2,1)S(1)}, bf16[4,784,128]{2,1,0:T(8,128)(2,1)S(1)}, u32[]{:S(2)}, u32[]{:S(2)}) collective-permute-start(bf16[4,784,128]{2,1,0:T(8,128)(2,1)S(1)} %pad_maximum_fusion.11), channel_id=1, source_target_pairs={{0,6},{2,4},{4,2},{6,0},{8,14},{10,12},{12,10},{14,8},{16,22},{18,... | collective-permute-start | bytes 2408456 | tf_op jit(solution)/shard_map/ppermute | solution.py:356
  251.9 32.0 %collective-permute-start.28 = (bf16[1024,896]{1,0:T(8,128)(2,1)S(1)}, bf16[1024,896]{1,0:T(8,128)(2,1)S(1)}, u32[]{:S(2)}, u32[]{:S(2)}) collective-permute-start(bf16[1024,896]{1,0:T(8,128)(2,1)S(1)} %pad_maximum_fusion.refs_0_), channel_id=1, source_target_pairs={{0,1},{1,0},{2,3},{3,2},{4,5},{5,4},{6,7},{7,6},{8,9},{9,8},{10,11... | collective-permute-start | bytes 5505032 | tf_op jit(solution)/shard_map/ppermute | solution.py:353
  267.9 16.6 %collective-permute-start.30 = (bf16[1024,896]{1,0:T(8,128)(2,1)S(1)}, bf16[1024,896]{1,0:T(8,128)(2,1)S(1)}, u32[]{:S(2)}, u32[]{:S(2)}) collective-permute-start(bf16[1024,896]{1,0:T(8,128)(2,1)S(1)} %pad_maximum_fusion.1.refs_2_), channel_id=1, source_target_pairs={{0,1},{1,0},{2,3},{3,2},{4,5},{5,4},{6,7},{7,6},{8,9},{9,8},{10,11... | collective-permute-start | bytes 5505032 | tf_op jit(solution)/shard_map/ppermute | solution.py:353
  267.9 18.1 %collective-permute-start.29 = (bf16[1024,896]{1,0:T(8,128)(2,1)S(1)}, bf16[1024,896]{1,0:T(8,128)(2,1)S(1)}, u32[]{:S(2)}, u32[]{:S(2)}) collective-permute-start(bf16[1024,896]{1,0:T(8,128)(2,1)S(1)} %collective-permute-done.26.refs_1_), channel_id=1, source_target_pairs={{0,1},{1,0},{2,3},{3,2},{4,5},{5,4},{6,7},{7,6},{8,9},{9,8},{10,11... | collective-permute-start | bytes 5505032 | tf_op jit(solution)/shard_map/ppermute | solution.py:353
  268.5 18.0 %collective-permute-start.31 = (bf16[1024,896]{1,0:T(8,128)(2,1)S(1)}, bf16[1024,896]{1,0:T(8,128)(2,1)S(1)}, u32[]{:S(2)}, u32[]{:S(2)}) collective-permute-start(bf16[1024,896]{1,0:T(8,128)(2,1)S(1)} %collective-permute-done.27.refs_3_), channel_id=1, source_target_pairs={{0,1},{1,0},{2,3},{3,2},{4,5},{5,4},{6,7},{7,6},{8,9},{9,8},{10,11... | collective-permute-start | bytes 5505032 | tf_op jit(solution)/shard_map/ppermute | solution.py:353
  271.0 10.5 %collective-permute-start.23 = (bf16[4,336,128]{2,1,0:T(8,128)(2,1)S(1)}, bf16[4,336,128]{2,1,0:T(8,128)(2,1)S(1)}, u32[]{:S(2)}, u32[]{:S(2)}) collective-permute-start(bf16[4,336,128]{2,1,0:T(8,128)(2,1)S(1)} %copy-done.15), channel_id=1, source_target_pairs={{0,8},{2,10},{4,12},{6,14},{8,0},{10,2},{12,4},{14,6},{16,24},{18,... | collective-permute-start | bytes 1032200 | tf_op jit(solution)/shard_map/ppermute | solution.py:356
  281.4 33.6 %collective-permute-start.24 = (bf16[4,336,128]{2,1,0:T(8,128)(2,1)S(1)}, bf16[4,336,128]{2,1,0:T(8,128)(2,1)S(1)}, u32[]{:S(2)}, u32[]{:S(2)}) collective-permute-start(bf16[4,336,128]{2,1,0:T(8,128)(2,1)S(1)} %copy-done.13), channel_id=1, source_target_pairs={{0,16},{2,18},{4,20},{6,22},{8,24},{10,26},{12,28},{14,30},{16,0},... | collective-permute-start | bytes 1032200 | tf_op jit(solution)/shard_map/ppermute | solution.py:356
  283.9 31.3 %collective-permute-start.25 = (bf16[4,336,128]{2,1,0:T(8,128)(2,1)S(1)}, bf16[4,336,128]{2,1,0:T(8,128)(2,1)S(1)}, u32[]{:S(2)}, u32[]{:S(2)}) collective-permute-start(bf16[4,336,128]{2,1,0:T(8,128)(2,1)S(1)} %copy-done.11), channel_id=1, source_target_pairs={{0,24},{2,26},{4,28},{6,30},{8,16},{10,18},{12,20},{14,22},{16,8},... | collective-permute-start | bytes 1032200 | tf_op jit(solution)/shard_map/ppermute | solution.py:356
  284.5 30.7 %collective-permute-start.20 = (bf16[4,448,128]{2,1,0:T(8,128)(2,1)S(1)}, bf16[4,448,128]{2,1,0:T(8,128)(2,1)S(1)}, u32[]{:S(2)}, u32[]{:S(2)}) collective-permute-start(bf16[4,448,128]{2,1,0:T(8,128)(2,1)S(1)} %pad_maximum_fusion.15), channel_id=1, source_target_pairs={{0,2},{2,0},{4,6},{6,4},{8,10},{10,8},{12,14},{14,12},{16,18},{18,... | collective-permute-start | bytes 1376264 | tf_op jit(solution)/shard_map/ppermute | solution.py:356
  286.0 29.2 %collective-permute-start.21 = (bf16[4,448,128]{2,1,0:T(8,128)(2,1)S(1)}, bf16[4,448,128]{2,1,0:T(8,128)(2,1)S(1)}, u32[]{:S(2)}, u32[]{:S(2)}) collective-permute-start(bf16[4,448,128]{2,1,0:T(8,128)(2,1)S(1)} %pad_maximum_fusion.16), channel_id=1, source_target_pairs={{0,4},{2,6},{4,0},{6,2},{8,12},{10,14},{12,8},{14,10},{16,20},{18,... | collective-permute-start | bytes 1376264 | tf_op jit(solution)/shard_map/ppermute | solution.py:356
  288.5 26.7 %collective-permute-start.22 = (bf16[4,448,128]{2,1,0:T(8,128)(2,1)S(1)}, bf16[4,448,128]{2,1,0:T(8,128)(2,1)S(1)}, u32[]{:S(2)}, u32[]{:S(2)}) collective-permute-start(bf16[4,448,128]{2,1,0:T(8,128)(2,1)S(1)} %pad_maximum_fusion.17), channel_id=1, source_target_pairs={{0,6},{2,4},{4,2},{6,0},{8,14},{10,12},{12,10},{14,8},{16,22},{18,... | collective-permute-start | bytes 1376264 | tf_op jit(solution)/shard_map/ppermute | solution.py:356
  315.0 5.5 %collective-permute-start.35 = (bf16[2048,512]{1,0:T(8,128)(2,1)}, bf16[2048,512]{1,0:T(8,128)(2,1)S(1)}, u32[]{:S(2)}, u32[]{:S(2)}) collective-permute-start(bf16[2048,512]{1,0:T(8,128)(2,1)} %hidden.1.own_h), channel_id=1, source_target_pairs={{0,1},{1,0},{2,3},{3,2},{4,5},{5,4},{6,7},{7,6},{8,9},{9,8},{10,11... | collective-permute-start | bytes 6291464 | tf_op jit(solution)/shard_map/ppermute | solution.py:353
  315.5 5.1 %collective-permute-start.36 = (bf16[4,2,448,128]{3,2,1,0:T(8,128)(2,1)S(1)}, bf16[4,2,448,128]{3,2,1,0:T(8,128)(2,1)S(1)}, u32[]{:S(2)}, u32[]{:S(2)}) collective-permute-start(bf16[4,2,448,128]{3,2,1,0:T(8,128)(2,1)S(1)} %pad_maximum_fusion.3), channel_id=1, source_target_pairs={{0,1},{1,0},{2,3},{3,2},{4,5},{5,4},{6,7},{7,6},{8,9},{9,8},{10,11... | collective-permute-start | bytes 2752520 | tf_op jit(solution)/shard_map/ppermute | solution.py:353
  316.2 14.7 %collective-permute-start.32 = (bf16[4,336,128]{2,1,0:T(8,128)(2,1)S(1)}, bf16[4,336,128]{2,1,0:T(8,128)(2,1)S(1)}, u32[]{:S(2)}, u32[]{:S(2)}) collective-permute-start(bf16[4,336,128]{2,1,0:T(8,128)(2,1)S(1)} %pad_maximum_fusion.20), channel_id=1, source_target_pairs={{0,2},{2,0},{4,6},{6,4},{8,10},{10,8},{12,14},{14,12},{16,18},{18,... | collective-permute-start | bytes 1032200 | tf_op jit(solution)/shard_map/ppermute | solution.py:356
  317.8 17.6 %collective-permute-start.33 = (bf16[4,336,128]{2,1,0:T(8,128)(2,1)S(1)}, bf16[4,336,128]{2,1,0:T(8,128)(2,1)S(1)}, u32[]{:S(2)}, u32[]{:S(2)}) collective-permute-start(bf16[4,336,128]{2,1,0:T(8,128)(2,1)S(1)} %pad_maximum_fusion.21), channel_id=1, source_target_pairs={{0,4},{2,6},{4,0},{6,2},{8,12},{10,14},{12,8},{14,10},{16,20},{18,... | collective-permute-start | bytes 1032200 | tf_op jit(solution)/shard_map/ppermute | solution.py:356
  319.2 16.3 %collective-permute-start.34 = (bf16[4,336,128]{2,1,0:T(8,128)(2,1)S(1)}, bf16[4,336,128]{2,1,0:T(8,128)(2,1)S(1)}, u32[]{:S(2)}, u32[]{:S(2)}) collective-permute-start(bf16[4,336,128]{2,1,0:T(8,128)(2,1)S(1)} %pad_maximum_fusion.22), channel_id=1, source_target_pairs={{0,6},{2,4},{4,2},{6,0},{8,14},{10,12},{12,10},{14,8},{16,22},{18,... | collective-permute-start | bytes 1032200 | tf_op jit(solution)/shard_map/ppermute | solution.py:356
  324.3 26.2 %collective-permute-start.37 = (bf16[1024,384]{1,0:T(8,128)(2,1)S(1)}, bf16[1024,384]{1,0:T(8,128)(2,1)S(1)}, u32[]{:S(2)}, u32[]{:S(2)}) collective-permute-start(bf16[1024,384]{1,0:T(8,128)(2,1)S(1)} %get-tuple-element.204), channel_id=1, source_target_pairs={{0,2},{2,0},{4,6},{6,4},{8,10},{10,8},{12,14},{14,12},{16,18},{18,... | collective-permute-start | bytes 2359304 | tf_op jit(solution)/shard_map/ppermute | solution.py:307
  325.9 25.9 %collective-permute-start.38 = (bf16[1024,384]{1,0:T(8,128)(2,1)S(1)}, bf16[1024,384]{1,0:T(8,128)(2,1)S(1)}, u32[]{:S(2)}, u32[]{:S(2)}) collective-permute-start(bf16[1024,384]{1,0:T(8,128)(2,1)S(1)} %get-tuple-element.206), channel_id=1, source_target_pairs={{0,4},{2,6},{4,0},{6,2},{8,12},{10,14},{12,8},{14,10},{16,20},{18,... | collective-permute-start | bytes 2359304 | tf_op jit(solution)/shard_map/ppermute | solution.py:307
  335.7 17.1 %collective-permute-start.47 = (bf16[4,2,336,128]{3,2,1,0:T(8,128)(2,1)S(1)}, bf16[4,2,336,128]{3,2,1,0:T(8,128)(2,1)S(1)}, u32[]{:S(2)}, u32[]{:S(2)}) collective-permute-start(bf16[4,2,336,128]{3,2,1,0:T(8,128)(2,1)S(1)} %pad_maximum_fusion.13), channel_id=1, source_target_pairs={{0,1},{1,0},{2,3},{3,2},{4,5},{5,4},{6,7},{7,6},{8,9},{9,8},{10,11... | collective-permute-start | bytes 2064392 | tf_op jit(solution)/shard_map/ppermute | solution.py:353
  335.8 14.3 %collective-permute-start.39 = (bf16[1024,256]{1,0:T(8,128)(2,1)S(1)}, bf16[1024,256]{1,0:T(8,128)(2,1)S(1)}, u32[]{:S(2)}, u32[]{:S(2)}) collective-permute-start(bf16[1024,256]{1,0:T(8,128)(2,1)S(1)} %get-tuple-element.208), channel_id=1, source_target_pairs={{0,8},{2,10},{4,12},{6,14},{8,0},{10,2},{12,4},{14,6},{16,24},{18,... | collective-permute-start | bytes 1572872 | tf_op jit(solution)/shard_map/ppermute | solution.py:307
  352.2 9.3 %collective-permute-start.42 = (bf16[512,256]{1,0:T(8,128)(2,1)S(1)}, bf16[512,256]{1,0:T(8,128)(2,1)S(1)}, u32[]{:S(2)}, u32[]{:S(2)}) collective-permute-start(bf16[512,256]{1,0:T(8,128)(2,1)S(1)} %get-tuple-element.214), channel_id=1, source_target_pairs={{0,2},{2,0},{4,6},{6,4},{8,10},{10,8},{12,14},{14,12},{16,18},{18,... | collective-permute-start | bytes 786440 | tf_op jit(solution)/shard_map/ppermute | solution.py:307
  355.5 17.2 %collective-permute-start.48 = (bf16[1024,256]{1,0:T(8,128)(2,1)S(1)}, bf16[1024,256]{1,0:T(8,128)(2,1)S(1)}, u32[]{:S(2)}, u32[]{:S(2)}) collective-permute-start(bf16[1024,256]{1,0:T(8,128)(2,1)S(1)} %get-tuple-element.236), channel_id=1, source_target_pairs={{0,2},{2,0},{4,6},{6,4},{8,10},{10,8},{12,14},{14,12},{16,18},{18,... | collective-permute-start | bytes 1572872 | tf_op jit(solution)/shard_map/ppermute | solution.py:307
  357.0 12.1 %collective-permute-start.40 = (bf16[512,384]{1,0:T(8,128)(2,1)S(1)}, bf16[512,384]{1,0:T(8,128)(2,1)S(1)}, u32[]{:S(2)}, u32[]{:S(2)}) collective-permute-start(bf16[512,384]{1,0:T(8,128)(2,1)S(1)} %get-tuple-element.210), channel_id=1, source_target_pairs={{0,4},{2,6},{4,0},{6,2},{8,12},{10,14},{12,8},{14,10},{16,20},{18,... | collective-permute-start | bytes 1179656 | tf_op jit(solution)/shard_map/ppermute | solution.py:307
  358.2 12.1 %collective-permute-start.41 = (bf16[512,384]{1,0:T(8,128)(2,1)S(1)}, bf16[512,384]{1,0:T(8,128)(2,1)S(1)}, u32[]{:S(2)}, u32[]{:S(2)}) collective-permute-start(bf16[512,384]{1,0:T(8,128)(2,1)S(1)} %get-tuple-element.212), channel_id=1, source_target_pairs={{0,8},{2,10},{4,12},{6,14},{8,0},{10,2},{12,4},{14,6},{16,24},{18,... | collective-permute-start | bytes 1179656 | tf_op jit(solution)/shard_map/ppermute | solution.py:307
  359.6 20.4 %collective-permute-start.49 = (bf16[1024,256]{1,0:T(8,128)(2,1)S(1)}, bf16[1024,256]{1,0:T(8,128)(2,1)S(1)}, u32[]{:S(2)}, u32[]{:S(2)}) collective-permute-start(bf16[1024,256]{1,0:T(8,128)(2,1)S(1)} %get-tuple-element.238), channel_id=1, source_target_pairs={{0,4},{2,6},{4,0},{6,2},{8,12},{10,14},{12,8},{14,10},{16,20},{18,... | collective-permute-start | bytes 1572872 | tf_op jit(solution)/shard_map/ppermute | solution.py:307
  361.5 19.7 %collective-permute-start.50 = (bf16[1024,256]{1,0:T(8,128)(2,1)S(1)}, bf16[1024,256]{1,0:T(8,128)(2,1)S(1)}, u32[]{:S(2)}, u32[]{:S(2)}) collective-permute-start(bf16[1024,256]{1,0:T(8,128)(2,1)S(1)} %get-tuple-element.240), channel_id=1, source_target_pairs={{0,8},{2,10},{4,12},{6,14},{8,0},{10,2},{12,4},{14,6},{16,24},{18,... | collective-permute-start | bytes 1572872 | tf_op jit(solution)/shard_map/ppermute | solution.py:307
  370.4 13.6 %collective-permute-start.45 = (bf16[256,256]{1,0:T(8,128)(2,1)S(1)}, bf16[256,256]{1,0:T(8,128)(2,1)S(1)}, u32[]{:S(2)}, u32[]{:S(2)}) collective-permute-start(bf16[256,256]{1,0:T(8,128)(2,1)S(1)} %get-tuple-element.220), channel_id=1, source_target_pairs={{0,4},{2,6},{4,0},{6,2},{8,12},{10,14},{12,8},{14,10},{16,20},{18,... | collective-permute-start | bytes 393224 | tf_op jit(solution)/shard_map/ppermute | solution.py:307
  371.3 15.7 %collective-permute-start.43 = (bf16[256,384]{1,0:T(8,128)(2,1)S(1)}, bf16[256,384]{1,0:T(8,128)(2,1)S(1)}, u32[]{:S(2)}, u32[]{:S(2)}) collective-permute-start(bf16[256,384]{1,0:T(8,128)(2,1)S(1)} %get-tuple-element.216), channel_id=1, source_target_pairs={{0,8},{2,10},{4,12},{6,14},{8,0},{10,2},{12,4},{14,6},{16,24},{18,... | collective-permute-start | bytes 589832 | tf_op jit(solution)/shard_map/ppermute | solution.py:307
  372.7 14.3 %collective-permute-start.44 = (bf16[256,384]{1,0:T(8,128)(2,1)S(1)}, bf16[256,384]{1,0:T(8,128)(2,1)S(1)}, u32[]{:S(2)}, u32[]{:S(2)}) collective-permute-start(bf16[256,384]{1,0:T(8,128)(2,1)S(1)} %get-tuple-element.218), channel_id=1, source_target_pairs={{0,2},{2,0},{4,6},{6,4},{8,10},{10,8},{12,14},{14,12},{16,18},{18,... | collective-permute-start | bytes 589832 | tf_op jit(solution)/shard_map/ppermute | solution.py:307
  381.5 9.0 %collective-permute-start.51 = (bf16[512,256]{1,0:T(8,128)(2,1)S(1)}, bf16[512,256]{1,0:T(8,128)(2,1)S(1)}, u32[]{:S(2)}, u32[]{:S(2)}) collective-permute-start(bf16[512,256]{1,0:T(8,128)(2,1)S(1)} %get-tuple-element.242), channel_id=1, source_target_pairs={{0,4},{2,6},{4,0},{6,2},{8,12},{10,14},{12,8},{14,10},{16,20},{18,... | collective-permute-start | bytes 786440 | tf_op jit(solution)/shard_map/ppermute | solution.py:307
  382.6 8.8 %collective-permute-start.52 = (bf16[512,256]{1,0:T(8,128)(2,1)S(1)}, bf16[512,256]{1,0:T(8,128)(2,1)S(1)}, u32[]{:S(2)}, u32[]{:S(2)}) collective-permute-start(bf16[512,256]{1,0:T(8,128)(2,1)S(1)} %get-tuple-element.244), channel_id=1, source_target_pairs={{0,8},{2,10},{4,12},{6,14},{8,0},{10,2},{12,4},{14,6},{16,24},{18,... | collective-permute-start | bytes 786440 | tf_op jit(solution)/shard_map/ppermute | solution.py:307
  384.0 7.4 %collective-permute-start.53 = (bf16[512,256]{1,0:T(8,128)(2,1)S(1)}, bf16[512,256]{1,0:T(8,128)(2,1)S(1)}, u32[]{:S(2)}, u32[]{:S(2)}) collective-permute-start(bf16[512,256]{1,0:T(8,128)(2,1)S(1)} %get-tuple-element.246), channel_id=1, source_target_pairs={{0,2},{2,0},{4,6},{6,4},{8,10},{10,8},{12,14},{14,12},{16,18},{18,... | collective-permute-start | bytes 786440 | tf_op jit(solution)/shard_map/ppermute | solution.py:307
  387.1 14.9 %collective-permute-start.46 = (bf16[128,1024]{1,0:T(8,128)(2,1)S(1)}, bf16[128,1024]{1,0:T(8,128)(2,1)S(1)}, u32[]{:S(2)}, u32[]{:S(2)}) collective-permute-start(bf16[128,1024]{1,0:T(8,128)(2,1)S(1)} %get-tuple-element.222), channel_id=1, source_target_pairs={{0,16},{2,18},{4,20},{6,22},{8,24},{10,26},{12,28},{14,30},{16,0},... | collective-permute-start | bytes 786440 | tf_op jit(solution)/shard_map/ppermute | solution.py:307
  391.6 5.5 %collective-permute-start.54 = (bf16[256,256]{1,0:T(8,128)(2,1)S(1)}, bf16[256,256]{1,0:T(8,128)(2,1)S(1)}, u32[]{:S(2)}, u32[]{:S(2)}) collective-permute-start(bf16[256,256]{1,0:T(8,128)(2,1)S(1)} %get-tuple-element.248), channel_id=1, source_target_pairs={{0,8},{2,10},{4,12},{6,14},{8,0},{10,2},{12,4},{14,6},{16,24},{18,... | collective-permute-start | bytes 393224 | tf_op jit(solution)/shard_map/ppermute | solution.py:307
  393.1 6.2 %collective-permute-start.55 = (bf16[256,256]{1,0:T(8,128)(2,1)S(1)}, bf16[256,256]{1,0:T(8,128)(2,1)S(1)}, u32[]{:S(2)}, u32[]{:S(2)}) collective-permute-start(bf16[256,256]{1,0:T(8,128)(2,1)S(1)} %get-tuple-element.250), channel_id=1, source_target_pairs={{0,2},{2,0},{4,6},{6,4},{8,10},{10,8},{12,14},{14,12},{16,18},{18,... | collective-permute-start | bytes 393224 | tf_op jit(solution)/shard_map/ppermute | solution.py:307
  396.3 5.0 %collective-permute-start.56 = (bf16[256,256]{1,0:T(8,128)(2,1)S(1)}, bf16[256,256]{1,0:T(8,128)(2,1)S(1)}, u32[]{:S(2)}, u32[]{:S(2)}) collective-permute-start(bf16[256,256]{1,0:T(8,128)(2,1)S(1)} %get-tuple-element.252), channel_id=1, source_target_pairs={{0,4},{2,6},{4,0},{6,2},{8,12},{10,14},{12,8},{14,10},{16,20},{18,... | collective-permute-start | bytes 393224 | tf_op jit(solution)/shard_map/ppermute | solution.py:307
  401.4 6.7 %collective-permute-start.57 = (bf16[128,768]{1,0:T(8,128)(2,1)S(1)}, bf16[128,768]{1,0:T(8,128)(2,1)S(1)}, u32[]{:S(2)}, u32[]{:S(2)}) collective-permute-start(bf16[128,768]{1,0:T(8,128)(2,1)S(1)} %get-tuple-element.254), channel_id=1, source_target_pairs={{0,16},{2,18},{4,20},{6,22},{8,24},{10,26},{12,28},{14,30},{16,0},... | collective-permute-start | bytes 589832 | tf_op jit(solution)/shard_map/ppermute | solution.py:307
  (31 other events, 157.9 us)

commit v11 on v10

--- a/solution.py
+++ b/solution.py
@@ -65,7 +65,7 @@
     out_refs = refs[-4:]
     me = list_ref[list_ref.shape[0] - 1]
     for j in range(16):
-        dest = me ^ j
+        dest = (me // 4 ^ j // 4) * 4 + j % 4
         base = 0
         for in_ref, (lo, rows) in zip(refs, segments):
             pack_rows(dest, list_ref, in_ref, lo, rows, out_refs[j // 4], j % 4, base)
@@ -118,45 +118,42 @@
     out_ref[pl.ds(pl.multiple_of(row + mid, 16), mid), lanes] = other
 
 
-def hidden_kernel(at_ref, *refs):
-    pieces, gates, ups = refs[:8], refs[8:12], refs[12:16]
-    terms_ref, out_ref, gate_w, up_w, rows = refs[16:]
+def hidden_kernel(at_ref, x_ref, gate_ref, up_ref, out_ref, gate_w, up_w):
+    cores, rows, mid = x_ref.shape
     depth = gate_w.shape[0] // 16
     tile = pl.program_id(0)
     x, y, zl = tile // 4, tile // 2 % 2, tile % 2
-    me, core = at_ref[0], at_ref[1]
+    me = at_ref[0]
 
     @pl.when(tile == 0)
     def _():
-        for plane in range(4):
-            for column in range(4):
-                place = (me ^ (plane + 4 * column)) ^ (8 * core)
-                unpack_rows(gates[plane], (column,), depth, gate_w, place * depth)
-                unpack_rows(ups[plane], (column,), depth, up_w, place * depth)
-
-    mid = pieces[0].shape[1]
-    for number in range(4):
-        lanes = slice(number * mid, (number + 1) * mid)
-        coordinate = (x, y)[number % 2]
-        for value in range(2):
-
-            @pl.when(coordinate == value)
-            def _():
-                rows[:, lanes] = pieces[2 * number + value][...]
-
-    gate = jnp.dot(rows[...], gate_w[...], preferred_element_type=jnp.float32)
-    up = jnp.dot(rows[...], up_w[...], preferred_element_type=jnp.float32)
-    value = gate / (1.0 + jnp.exp(-gate)) * up
+        for place in range(4):
+            for plane in range(4):
+                row = ((me // 4 ^ plane) * 4 + place) * depth
+                unpack_rows(gate_ref, (place, plane), depth, gate_w, row)
+                unpack_rows(up_ref, (place, plane), depth, up_w, row)
+
+    def product(w_ref):
+        return sum(
+            jnp.dot(
+                x_ref[at], w_ref[at * mid : (at + 1) * mid, :], preferred_element_type=jnp.float32
+            )
+            for at in range(cores)
+        )
+
+    gate = product(gate_w)
+    value = gate / (1.0 + jnp.exp(-gate)) * product(up_w)
 
     wide = gate.shape[1]
     term = lax.broadcasted_iota(jnp.int32, (16, wide), 0)
     lane = lax.broadcasted_iota(jnp.int32, (16, wide), 1)
     chosen = (term % 4 == lane // LANES) & (term < 12) & (lane < wide - HALF)
     chosen = jnp.where(chosen, 1.0, 0.0).astype(jnp.bfloat16)
-    block = rows.shape[0] // 2
+    block = rows // 2
+    terms_at = up_ref.shape[2]
     for zh in range(2):
         weight = lax.dot_general(
-            terms_ref[x + 2 * y, zl + 2 * zh],
+            gate_ref[me % 4 ^ (x + 2 * y), zl + 2 * zh, terms_at:, :],
             chosen,
             (((0,), (0,)), ((), ())),
             preferred_element_type=jnp.float32,
@@ -165,35 +162,24 @@
         out_ref[span, :] = (value[span, :] * weight).astype(out_ref.dtype)
 
 
-def hidden_units(at, pieces, gates, ups, terms):
-    total = 2 * pieces[0].shape[0]
-    mid = pieces[0].shape[1]
+def hidden_units(at, rows, gates, ups):
+    cores, total, mid = rows.shape
     tile = total // 8
     wide = 4 * LANES
-    model = 4 * mid
-    by_x = [lambda i: (jnp.minimum(i, 3), 0), lambda i: (jnp.maximum(i - 4, 0), 0)]
-    by_y = [
-        lambda i: (i // 4 * 2 + jnp.where(i // 2 % 2 == 0, i % 2, 1), 0),
-        lambda i: (i // 4 * 2 + jnp.where(i // 2 % 2 == 1, i % 2, 0), 0),
-    ]
-    maps = (by_x + by_y) * 2
-    dtype = pieces[0].dtype
+    model = cores * mid
     return pl.pallas_call(
         hidden_kernel,
         grid=(8,),
-        out_shape=jax.ShapeDtypeStruct((total, wide), dtype),
-        in_specs=[smem()]
-        + [pl.BlockSpec((tile, mid), where) for where in maps]
-        + [vmem()] * 9,
+        out_shape=jax.ShapeDtypeStruct((total, wide), rows.dtype),
+        in_specs=[smem(), pl.BlockSpec((cores, tile, mid), lambda i: (0, i, 0)), vmem(), vmem()],
         out_specs=pl.BlockSpec((tile, wide), lambda i: (i, 0)),
-        scratch_shapes=[pltpu.VMEM((model, wide), dtype)] * 2
-        + [pltpu.VMEM((tile, model), dtype)],
+        scratch_shapes=[pltpu.VMEM((model, wide), rows.dtype)] * 2,
         compiler_params=pltpu.CompilerParams(vmem_limit_bytes=56 * MIB),
         cost_estimate=pl.CostEstimate(
             flops=4 * total * model * wide, bytes_accessed=24 * MIB, transcendentals=total * wide
         ),
         name="hidden",
-    )(at, *pieces, *gates, *ups, terms)
+    )(at, rows, gates, ups)
 
 
 THIRDS = ((0, 1, 2), (1, 2, 0), (2, 0, 1))
@@ -217,10 +203,10 @@
 def down_kernel(rows, side, orders, at_ref, own_h, other_h, own_ref, other_ref, *refs):
     out_refs, (own_w, other_w) = refs[:-2], refs[-2:]
     for in_ref, w_ref in ((own_ref, own_w), (other_ref, other_w)):
-        for plane in range(4):
-            for column in range(2):
-                place = (at_ref[0] ^ (plane + 4 * column)) % 8
-                unpack_rows(in_ref, (plane, column), rows, w_ref, place * rows)
+        for place in range(4):
+            for plane in range(2):
+                row = ((at_ref[0] // 4 % 2 ^ plane) * 4 + place) * rows
+                unpack_rows(in_ref, (place, plane), rows, w_ref, row)
     dims = (((1,), (1,)), ((), ()))
     for number, span in enumerate(group_spans(own_w.shape[0], len(orders))):
         done = 0
@@ -358,9 +344,11 @@
     def along_z(packed):
         return [packed[0]] + [across(packed[k], 4 * k) for k in (1, 2, 3)]
 
+    planes = [[4 * z + at for at in range(4)] for z in range(devices // 4)]
+
     def in_plane(blocks):
-        parts = [jnp.stack([block[q] for block in blocks]) for q in range(4)]
-        return [parts[0]] + [across(parts[q], q) for q in (1, 2, 3)]
+        blocks = jnp.stack(blocks, axis=1)
+        return lax.all_to_all(blocks, "ep", 0, 0, axis_index_groups=planes, tiled=True)
 
     places = []
     for dest in range(devices):
@@ -377,41 +365,41 @@
     info = jnp.concatenate([listing, at[:1]])
 
     near, far = swap(tokens, 2), swap(tokens, 3)
-    gate_z = along_z(pack(info, (gate_proj,), ((0, depth),), share, "pack_gate"))
     corner = swap(far, 2)
-    up_packed = pack(info, (up_proj,), ((0, depth),), None, "pack_up")
-    gate_z, corner, near, far, up_packed = tie((gate_z, corner, near, far, up_packed))
-
-    up_z = along_z(up_packed)
-    gates = in_plane(gate_z)
+    packed = pack(info, (gate_proj,), ((0, depth),), share, "pack_gate")
+    packed, near, far, corner = tie((packed, near, far, corner))
+
+    gate_z = along_z(packed)
     mid = tokens.shape[1] // 2
     rows = jnp.concatenate([tokens, far, near, corner], axis=0)
-    first, second = rows[:, :mid], rows[:, mid:]
-    first = jnp.concatenate([first, swap(first, 1)], axis=0)
-    second = jnp.concatenate([second, swap(second, 0)], axis=0)
-    down_packed = [
-        pack(info, (down_proj,), ((0, parts[0]),), None, "pack_down"),
-        pack(info, (down_proj,), ((parts[0], parts[1]),), None, "pack_down"),
-    ]
-    up_z, gates, first, second, packed0 = tie((up_z, gates, first, second, down_packed[0]))
-
-    down0_z = along_z(packed0)
+    rows_a = gather_bits(rows[:, :mid].reshape(2, 2, block, mid), 4, (1,), (2, 3))
+    rows_b = gather_bits(rows[:, mid:].reshape(2, 2, block, mid), 4, (0,), (2, 3))
+    packed = pack(info, (up_proj,), ((0, depth),), None, "pack_up")
+    gate_z, rows_a, rows_b, packed = tie((gate_z, rows_a, rows_b, packed))
+
+    up_z = along_z(packed)
+    gates = in_plane(gate_z)
+    rows_a = gather_bits(rows_a, 4, (0,), (1, 2, 3)).reshape(-1, mid)
+    rows_b = gather_bits(rows_b, 4, (1,), (0, 2, 3)).reshape(-1, mid)
+    rows = lax.all_gather(jnp.concatenate([rows_a, rows_b], axis=1), "et")
+    packed = pack(info, (down_proj,), ((0, parts[0]),), None, "pack_down")
+    up_z, packed = tie((up_z, packed))
+
+    down0_z = along_z(packed)
     ups = in_plane(up_z)
-    pieces = [first, swap(first, 0), second, swap(second, 1)]
-    others = [exchange(piece) for piece in pieces]
-    down0_z, ups, packed1 = tie((down0_z, ups, down_packed[1]))
-
-    down1_z = along_z(packed1)
+    packed = pack(info, (down_proj,), ((parts[0], parts[1]),), None, "pack_down")
+    down0_z, packed = tie((down0_z, packed))
+
+    down1_z = along_z(packed)
     downs0 = in_plane(down0_z)
-    terms = jnp.stack([gate[:, size:] for gate in gates])
-    hidden = hidden_units(at, pieces + others, [gate[:, :size] for gate in gates], ups, terms)
+    hidden = hidden_units(at, rows, gates, ups)
     hidden_other = exchange(hidden)
     downs0, down1_z, hidden = tie((downs0, down1_z, hidden))
     downs1 = in_plane(down1_z)
 
     def core_half(downs, which):
         start = 2 * (which ^ (me >> 3))
-        return jnp.stack([lax.dynamic_slice_in_dim(down, start, 2, 0) for down in downs])
+        return lax.dynamic_slice_in_dim(downs, start, 2, 1)
 
     def products(down, rows_in, orders):
         own, other = core_half(down, core), exchange(core_half(down, 1 - core))

time: 413 us -> 453 us (1.097)
  waiting for transfers between devices: 258 us -> 273 us
  between operations: 0.76 us -> 13.8 us
  other arithmetic: 13.3 us -> 23.4 us
  local copies, waits for them, and re-layouts: 28.7 us -> 22.6 us
    all_to_all x0 -> x4, starting transfers between devices: none -> 21.9 us  [in_plane(): lax.all_to_all(blocks, 'ep', 0, 0, axis_index_groups=planes, tiled=True)]
    ppermute x24 -> x12, starting transfers between devices: 27.6 us -> 14.8 us  [across(): return lax.ppermute(value, 'ep', [(i, i ^ number) for i in range(devices)])]
    slice x19 -> x1, local copies, waits for them, and re-layouts: 12 us -> 0.15 us  [packed_layer(): rows[:, mid:].reshape(2, 2, block, mid)]
    ppermute x24 -> x12, waiting for transfers between devices: 147 us -> 154 us  [across(): return lax.ppermute(value, 'ep', [(i, i ^ number) for i in range(devices)])]
    ppermute x27, waiting for transfers between devices: 111 us -> 117 us  [swap(): return lax.ppermute(value, 'ep', [(i, i ^ 1 << bit) for i in range(size)])]
    another operation x21 -> x8, other arithmetic: 7.05 us -> 12.1 us  [the longest x4 9.2 us: in_plane(): blocks = jnp.stack(blocks, axis=1)]
    concatenate x2 -> x1, other arithmetic: 1.61 us -> 6.63 us  [packed_layer(): rows = lax.all_gather(jnp.concatenate([rows_a, rows_b], axis=1), 'et')]
    pallas_call x4, Pallas kernels: 12.8 us -> 17.6 us  [down_product(): pl.pallas_call(functools.partial(down_kernel, rows, side, orders), out_sh...]
  transfers between devices with their start and end apart: 58 -> 47, of which waited for: 29 -> 30; matrix products, arithmetic and copies ran while one was open for 7% -> 5% of each run, Pallas kernels for 11% -> 11%
where the time goes in v11:
time: 453 us; the launch traced here: 448 us
  waiting for transfers between devices  273 us (60%)
  starting transfers between devices  66.6 us (15%)
  Pallas kernels  48.6 us (11%)
  other arithmetic  23.4 us (5%)
  local copies, waits for them, and re-layouts  22.6 us (5%)
  between operations  13.8 us (3%)
    ppermute x12, waiting for transfers between devices, across(): return lax.ppermute(value, 'ep', [(i, i ^ number) for i in range(devices)])  154 us
    ppermute x27, waiting for transfers between devices, swap(): return lax.ppermute(value, 'ep', [(i, i ^ 1 << bit) for i in range(size)])  117 us
    ppermute x27, starting transfers between devices, swap(): return lax.ppermute(value, 'ep', [(i, i ^ 1 << bit) for i in range(size)])  29.7 us
    pallas_call x1, Pallas kernels, hidden_units(): pl.pallas_call(hidden_kernel, grid=(8,), out_shape=jax.ShapeDtypeStruct((...  22.9 us
    all_to_all x4, starting transfers between devices, in_plane(): lax.all_to_all(blocks, 'ep', 0, 0, axis_index_groups=planes, tiled=True)  21.9 us
    pallas_call x4, Pallas kernels, down_product(): pl.pallas_call(functools.partial(down_kernel, rows, side, orders), out_sh...  17.6 us
    unnamed x59, local copies, waits for them, and re-layouts  14.9 us
    ppermute x12, starting transfers between devices, across(): return lax.ppermute(value, 'ep', [(i, i ^ number) for i in range(devices)])  14.8 us
  transfers between devices with their start and end apart: 47, of which 30 were waited for; matrix products, arithmetic and copies ran while one was open for 5% of the time, Pallas kernels for 11%

profile of v11, /device:TPU:14, one launch (start us, length us, event | category | flops | bytes accessed | tf_op | source)
XLA Modules:
  0.0 448.1 jit_solution(17342267401099121616)
XLA Ops:
  6.5 2.6 collective-permute-start.1
  12.5 16.4 %collective-permute-done.1 = bf16[128,1792]{1,0:T(8,128)(2,1)S(1)} collective-permute-done((bf16[128,1792]{1,0:T(8,128)(2,1)}, bf16[128,1792]{1,0:T(8,128)(2,1)S(1)}, u32[]{:S(2)}, u32[]{:S(2)}) %collective-permute-start.1) | collective-permute-done | bytes 458784 | tf_op jit(solution)/shard_map/ppermute | solution.py:293
  31.3 2.0 copy-done.2
  33.3 1.7 pack_gate.1
  35.0 6.3 %collective-permute-done.2 = bf16[128,1792]{1,0:T(8,128)(2,1)S(1)} collective-permute-done((bf16[128,1792]{1,0:T(8,128)(2,1)S(1)}, bf16[128,1792]{1,0:T(8,128)(2,1)S(1)}, u32[]{:S(2)}, u32[]{:S(2)}) %collective-permute-start.2) | collective-permute-done | bytes 458784 | tf_op jit(solution)/shard_map/ppermute | solution.py:293
  43.3 3.0 collective-permute-start.4
  46.6 2.6 pack_up.1
  49.2 13.9 %collective-permute-done.7 = bf16[2,2,128,896]{3,2,1,0:T(8,128)(2,1)S(1)} collective-permute-done((bf16[2,2,128,896]{3,2,1,0:T(8,128)(2,1)S(1)}, bf16[2,2,128,896]{3,2,1,0:T(8,128)(2,1)S(1)}, u32[]{:S(2)}, u32[]{:S(2)}) %collective-permute-start.7) | collective-permute-done | bytes 917536 | tf_op jit(solution)/shard_map/ppermute | solution.py:293
  63.6 12.1 %collective-permute-done.3 = bf16[4,800,128]{2,1,0:T(8,128)(2,1)S(1)} collective-permute-done((bf16[4,800,128]{2,1,0:T(8,128)(2,1)S(1)}, bf16[4,800,128]{2,1,0:T(8,128)(2,1)S(1)}, u32[]{:S(2)}, u32[]{:S(2)}) %collective-permute-start.3) | collective-permute-done | bytes 819232 | tf_op jit(solution)/shard_map/ppermute | solution.py:342
  75.7 24.4 %collective-permute-done.4 = bf16[4,800,128]{2,1,0:T(8,128)(2,1)S(1)} collective-permute-done((bf16[4,800,128]{2,1,0:T(8,128)(2,1)S(1)}, bf16[4,800,128]{2,1,0:T(8,128)(2,1)S(1)}, u32[]{:S(2)}, u32[]{:S(2)}) %collective-permute-start.4) | collective-permute-done | bytes 819232 | tf_op jit(solution)/shard_map/ppermute | solution.py:342
  100.1 15.9 %collective-permute-done.5 = bf16[4,800,128]{2,1,0:T(8,128)(2,1)S(1)} collective-permute-done((bf16[4,800,128]{2,1,0:T(8,128)(2,1)S(1)}, bf16[4,800,128]{2,1,0:T(8,128)(2,1)S(1)}, u32[]{:S(2)}, u32[]{:S(2)}) %collective-permute-start.5) | collective-permute-done | bytes 819232 | tf_op jit(solution)/shard_map/ppermute | solution.py:342
  116.1 1.5 collective-permute-start.18
  117.6 1.5 collective-permute-start.17
  119.1 36.6 %collective-permute-done.18 = bf16[2,2,2,128,896]{4,3,2,1,0:T(8,128)(2,1)S(1)} collective-permute-done((bf16[2,2,2,128,896]{4,3,2,1,0:T(8,128)(2,1)S(1)}, bf16[2,2,2,128,896]{4,3,2,1,0:T(8,128)(2,1)S(1)}, u32[]{:S(2)}, u32[]{:S(2)}) %collective-permute-start.18) | collective-permute-done | bytes 1835040 | tf_op jit(solution)/shard_map/ppermute | solution.py:293
  156.1 2.2 copy.15
  158.3 2.2 pad_maximum_fusion.1
  160.5 6.6 %pad_maximum_fusion = bf16[2048,1792]{1,0:T(8,128)(2,1)} fusion(bf16[2048,896]{1,0:T(8,128)(2,1)} %bitcast.40, bf16[2048,896]{1,0:T(8,128)(2,1)} %bitcast.41), kind=kLoop, calls=%fused_computation | loop fusion | flops 14680064 | bytes 14680064 | tf_op jit(solution)/shard_map/concatenate | solution.py:384
  167.1 3.2 pad_maximum_fusion.3
  170.3 7.3 %all-to-all-start.1 = ((bf16[4,4,800,128]{3,2,1,0:T(8,128)(2,1)}), bf16[4,4,800,128]{3,2,1,0:T(8,128)(2,1)}, u32[]{:S(2)}, u32[]{:S(2)}) async-start(bf16[4,4,800,128]{3,2,1,0:T(8,128)(2,1)} %pad_maximum_fusion.3), calls=%async_computation.1 | async-start | bytes 6553600 | tf_op jit(solution)/shard_map/all_to_all | solution.py:351
  177.6 1.8 collective-permute-start.10
  179.4 1.7 collective-permute-start.9
  181.1 2.7 copy-done
  183.8 1.4 pack_down.2
  187.6 28.3 %collective-permute-done.10 = bf16[4,784,128]{2,1,0:T(8,128)(2,1)S(1)} collective-permute-done((bf16[4,784,128]{2,1,0:T(8,128)(2,1)}, bf16[4,784,128]{2,1,0:T(8,128)(2,1)S(1)}, u32[]{:S(2)}, u32[]{:S(2)}) %collective-permute-start.10) | collective-permute-done | bytes 802848 | tf_op jit(solution)/shard_map/ppermute | solution.py:342
  215.8 11.9 %collective-permute-done.9 = bf16[4,784,128]{2,1,0:T(8,128)(2,1)S(1)} collective-permute-done((bf16[4,784,128]{2,1,0:T(8,128)(2,1)S(1)}, bf16[4,784,128]{2,1,0:T(8,128)(2,1)S(1)}, u32[]{:S(2)}, u32[]{:S(2)}) %collective-permute-start.9) | collective-permute-done | bytes 802848 | tf_op jit(solution)/shard_map/ppermute | solution.py:342
  227.7 1.9 pad_maximum_fusion.4
  229.6 5.2 %all-to-all-start.2 = ((bf16[4,4,784,128]{3,2,1,0:T(8,128)(2,1)}), bf16[4,4,784,128]{3,2,1,0:T(8,128)(2,1)}, u32[]{:S(2)}, u32[]{:S(2)}) async-start(bf16[4,4,784,128]{3,2,1,0:T(8,128)(2,1)} %pad_maximum_fusion.4), calls=%async_computation.2 | async-start | bytes 6422528 | tf_op jit(solution)/shard_map/all_to_all | solution.py:351
  234.8 2.2 collective-permute-start.11
  238.8 2.0 copy-done.1
  240.8 1.4 pack_down.3
  242.8 8.6 %collective-permute-done.11 = bf16[4,448,128]{2,1,0:T(8,128)(2,1)} collective-permute-done((bf16[4,448,128]{2,1,0:T(8,128)(2,1)S(1)}, bf16[4,448,128]{2,1,0:T(8,128)(2,1)}, u32[]{:S(2)}, u32[]{:S(2)}) %collective-permute-start.11) | collective-permute-done | bytes 458784 | tf_op jit(solution)/shard_map/ppermute | solution.py:342
  251.4 16.3 %collective-permute-done.12 = bf16[4,448,128]{2,1,0:T(8,128)(2,1)} collective-permute-done((bf16[4,448,128]{2,1,0:T(8,128)(2,1)S(1)}, bf16[4,448,128]{2,1,0:T(8,128)(2,1)}, u32[]{:S(2)}, u32[]{:S(2)}) %collective-permute-start.12) | collective-permute-done | bytes 458784 | tf_op jit(solution)/shard_map/ppermute | solution.py:342
  267.7 6.5 %collective-permute-done.13 = bf16[4,448,128]{2,1,0:T(8,128)(2,1)} collective-permute-done((bf16[4,448,128]{2,1,0:T(8,128)(2,1)S(1)}, bf16[4,448,128]{2,1,0:T(8,128)(2,1)}, u32[]{:S(2)}, u32[]{:S(2)}) %collective-permute-start.13) | collective-permute-done | bytes 458784 | tf_op jit(solution)/shard_map/ppermute | solution.py:342
  274.2 2.7 pad_maximum_fusion.7
  277.0 4.8 %all-to-all-start = ((bf16[4,4,448,128]{3,2,1,0:T(8,128)(2,1)}), bf16[4,4,448,128]{3,2,1,0:T(8,128)(2,1)}, u32[]{:S(2)}, u32[]{:S(2)}) async-start(bf16[4,4,448,128]{3,2,1,0:T(8,128)(2,1)} %pad_maximum_fusion.7), calls=%async_computation | async-start | bytes 3670016 | tf_op jit(solution)/shard_map/all_to_all | solution.py:351
  281.8 22.9 %hidden.1.own_h = bf16[2048,512]{1,0:T(8,128)(2,1)} custom-call(s32[2]{0:T(128)} %pad_add_fusion.1.at_ref, bf16[2,2048,1792]{2,1,0:T(8,128)(2,1)} %bitcast.66, bf16[4,4,800,128]{3,2,1,0:T(8,128)(2,1)} %all-to-all-done.1.gate_ref, bf16[4,4,784,128]{3,2,1,0:T(8,128)(2,1)} %all-to-all-done.2.up_ref), custom_call_target="tpu_custom_call" | custom-call | flops 15032385536 | bytes 25165824 | tf_op jit(solution)/shard_map/hidden/pallas_call | solution.py:170
  304.7 3.0 collective-permute-start.15
  308.1 11.7 %collective-permute-done.14 = bf16[4,336,128]{2,1,0:T(8,128)(2,1)S(1)} collective-permute-done((bf16[4,336,128]{2,1,0:T(8,128)(2,1)S(1)}, bf16[4,336,128]{2,1,0:T(8,128)(2,1)S(1)}, u32[]{:S(2)}, u32[]{:S(2)}) %collective-permute-start.14) | collective-permute-done | bytes 344096 | tf_op jit(solution)/shard_map/ppermute | solution.py:342
  319.9 11.0 %collective-permute-done.15 = bf16[4,336,128]{2,1,0:T(8,128)(2,1)S(1)} collective-permute-done((bf16[4,336,128]{2,1,0:T(8,128)(2,1)S(1)}, bf16[4,336,128]{2,1,0:T(8,128)(2,1)S(1)}, u32[]{:S(2)}, u32[]{:S(2)}) %collective-permute-start.15) | collective-permute-done | bytes 344096 | tf_op jit(solution)/shard_map/ppermute | solution.py:342
  330.9 7.6 %collective-permute-done.16 = bf16[4,336,128]{2,1,0:T(8,128)(2,1)S(1)} collective-permute-done((bf16[4,336,128]{2,1,0:T(8,128)(2,1)S(1)}, bf16[4,336,128]{2,1,0:T(8,128)(2,1)S(1)}, u32[]{:S(2)}, u32[]{:S(2)}) %collective-permute-start.16) | collective-permute-done | bytes 344096 | tf_op jit(solution)/shard_map/ppermute | solution.py:342
  339.2 2.7 constant_dynamic-slice_fusion.2
  341.9 1.4 pad_maximum_fusion.8
  343.3 4.7 %all-to-all-start.3 = ((bf16[4,4,336,128]{3,2,1,0:T(8,128)(2,1)}), bf16[4,4,336,128]{3,2,1,0:T(8,128)(2,1)}, u32[]{:S(2)}, u32[]{:S(2)}) async-start(bf16[4,4,336,128]{3,2,1,0:T(8,128)(2,1)} %pad_maximum_fusion.8), calls=%async_computation.3 | async-start | bytes 2752512 | tf_op jit(solution)/shard_map/all_to_all | solution.py:351
  348.1 5.2 %down_send.2 = (bf16[1024,384]{1,0:T(8,128)(2,1)S(1)}, bf16[1024,384]{1,0:T(8,128)(2,1)S(1)}, bf16[1024,256]{1,0:T(8,128)(2,1)S(1)}) custom-call(s32[2]{0:T(128)S(1)} %copy-done.21, bf16[2048,512]{1,0:T(8,128)(2,1)S(1)} %copy-done.8, bf16[2048,512]{1,0:T(8,128)(2,1)} %collective-permute-done.19.other_h, ...), custom_call_target="tpu_custom_call" | custom-call | flops 2147483648 | bytes 8388608 | tf_op jit(solution)/shard_map/down_send/pallas_call | solution.py:233
  357.2 5.0 %down_keep.2 = (f32[1024,384]{1,0:T(8,128)S(1)}, f32[1024,384]{1,0:T(8,128)S(1)}, f32[1024,256]{1,0:T(8,128)S(1)}) custom-call(s32[2]{0:T(128)S(1)} %copy-done.21, bf16[2048,512]{1,0:T(8,128)(2,1)S(1)} %copy-done.9, bf16[2048,512]{1,0:T(8,128)(2,1)} %collective-permute-done.19.other_h, bf16[4,2,448,128]{3,2,1,0:T(8,128)(2,1)S(1)} %copy-done.7, ...), custom_call_target="tpu_custom_call" | custom-call | flops 2147483648 | bytes 8388608 | tf_op jit(solution)/shard_map/down_keep/pallas_call | solution.py:233
  363.2 1.4 all-to-all-done.3
  364.6 1.5 collective-permute-start.21
  366.7 1.4 constant_dynamic-slice_fusion
  368.3 14.3 %collective-permute-done.23.refs_5_ = bf16[1024,256]{1,0:T(8,128)(2,1)S(1)} collective-permute-done((bf16[1024,256]{1,0:T(8,128)(2,1)S(1)}, bf16[1024,256]{1,0:T(8,128)(2,1)S(1)}, u32[]{:S(2)}, u32[]{:S(2)}) %collective-permute-start.23) | collective-permute-done | bytes 524320 | tf_op jit(solution)/shard_map/ppermute | solution.py:293
  386.0 3.7 down_send.3
  389.7 1.6 collective-permute-start.32
  391.8 1.5 collective-permute-start.33
  393.5 1.8 collective-permute-start.34
  395.3 8.0 %collective-permute-done.24.refs_1_ = bf16[512,384]{1,0:T(8,128)(2,1)S(1)} collective-permute-done((bf16[512,384]{1,0:T(8,128)(2,1)S(1)}, bf16[512,384]{1,0:T(8,128)(2,1)S(1)}, u32[]{:S(2)}, u32[]{:S(2)}) %collective-permute-start.24) | collective-permute-done | bytes 393248 | tf_op jit(solution)/shard_map/ppermute | solution.py:293
  404.1 1.5 collective-permute-start.28
  406.2 3.7 down_keep.3
  409.9 4.4 collective-permute-done.33.refs_3_
  415.4 1.5 collective-permute-start.35
  417.5 1.9 collective-permute-done.27.refs_1_
  419.4 3.4 collective-permute-start.30
  422.9 2.8 collective-permute-done.36.refs_3_
  428.2 3.2 collective-permute-done.38.refs_1_
  432.0 3.0 collective-permute-start.41
  435.3 4.8 %collective-permute-done.41 = bf16[128,768]{1,0:T(8,128)(2,1)S(1)} collective-permute-done((bf16[128,768]{1,0:T(8,128)(2,1)S(1)}, bf16[128,768]{1,0:T(8,128)(2,1)S(1)}, u32[]{:S(2)}, u32[]{:S(2)}) %collective-permute-start.41) | collective-permute-done | bytes 196640 | tf_op jit(solution)/shard_map/ppermute | solution.py:293
  (135 shorter events, 32.2 us)
Async XLA Ops:
  6.5 275.2 %all-gather.3.cloned.1.call-start = ((), (), s32[]{:S(2)}) async-start(), calls=%async_computation.4 | async-start | bytes 22020096 | tf_op jit(solution)/shard_map/all_gather | solution.py:384
  6.5 22.4 %collective-permute-start.1 = (bf16[128,1792]{1,0:T(8,128)(2,1)}, bf16[128,1792]{1,0:T(8,128)(2,1)S(1)}, u32[]{:S(2)}, u32[]{:S(2)}) collective-permute-start(bf16[128,1792]{1,0:T(8,128)(2,1)} %param.9), channel_id=1, source_target_pairs={{0,16},{2,18},{4,20},{6,22},{8,24},{10,26},{12,28},{14,30},{16,0},... | collective-permute-start | bytes 1376264 | tf_op jit(solution)/shard_map/ppermute | solution.py:293
  9.1 25.9 %collective-permute-start = (bf16[128,1792]{1,0:T(8,128)(2,1)}, bf16[128,1792]{1,0:T(8,128)(2,1)S(1)}, u32[]{:S(2)}, u32[]{:S(2)}) collective-permute-start(bf16[128,1792]{1,0:T(8,128)(2,1)} %param.9), channel_id=1, source_target_pairs={{0,8},{2,10},{4,12},{6,14},{8,0},{10,2},{12,4},{14,6},{16,24},{18,... | collective-permute-start | bytes 1376264 | tf_op jit(solution)/shard_map/ppermute | solution.py:293
  28.9 12.4 %collective-permute-start.2 = (bf16[128,1792]{1,0:T(8,128)(2,1)S(1)}, bf16[128,1792]{1,0:T(8,128)(2,1)S(1)}, u32[]{:S(2)}, u32[]{:S(2)}) collective-permute-start(bf16[128,1792]{1,0:T(8,128)(2,1)S(1)} %collective-permute-done.1), channel_id=1, source_target_pairs={{0,8},{2,10},{4,12},{6,14},{8,0},{10,2},{12,4},{14,6},{16,24},{18,... | collective-permute-start | bytes 1376264 | tf_op jit(solution)/shard_map/ppermute | solution.py:293
  31.3 2.0 copy-start.2
  41.5 5.1 %copy-start.3 = (bf16[16,224,512]{2,1,0:T(8,128)(2,1)S(1)}, bf16[16,224,512]{2,1,0:T(8,128)(2,1)}, u32[]{:S(2)}) copy-start(bf16[16,224,512]{2,1,0:T(8,128)(2,1)} %refs_0_.5) | copy-start | bytes 11010052
  41.7 21.5 %collective-permute-start.7 = (bf16[2,2,128,896]{3,2,1,0:T(8,128)(2,1)S(1)}, bf16[2,2,128,896]{3,2,1,0:T(8,128)(2,1)S(1)}, u32[]{:S(2)}, u32[]{:S(2)}) collective-permute-start(bf16[2,2,128,896]{3,2,1,0:T(8,128)(2,1)S(1)} %bitcast.46), channel_id=1, source_target_pairs={{0,2},{2,0},{4,6},{6,4},{8,10},{10,8},{12,14},{14,12},{16,18},{18,... | collective-permute-start | bytes 2752520 | tf_op jit(solution)/shard_map/ppermute | solution.py:293
  42.3 21.1 %collective-permute-start.6 = (bf16[2,2,128,896]{3,2,1,0:T(8,128)(2,1)S(1)}, bf16[2,2,128,896]{3,2,1,0:T(8,128)(2,1)S(1)}, u32[]{:S(2)}, u32[]{:S(2)}) collective-permute-start(bf16[2,2,128,896]{3,2,1,0:T(8,128)(2,1)S(1)} %bitcast.44), channel_id=1, source_target_pairs={{0,4},{2,6},{4,0},{6,2},{8,12},{10,14},{12,8},{14,10},{16,20},{18,... | collective-permute-start | bytes 2752520 | tf_op jit(solution)/shard_map/ppermute | solution.py:293
  42.8 33.0 %collective-permute-start.3 = (bf16[4,800,128]{2,1,0:T(8,128)(2,1)S(1)}, bf16[4,800,128]{2,1,0:T(8,128)(2,1)S(1)}, u32[]{:S(2)}, u32[]{:S(2)}) collective-permute-start(bf16[4,800,128]{2,1,0:T(8,128)(2,1)S(1)} %get-tuple-element.125), channel_id=1, source_target_pairs={{0,8},{2,10},{4,12},{6,14},{8,0},{10,2},{12,4},{14,6},{16,24},{18,... | collective-permute-start | bytes 2457608 | tf_op jit(solution)/shard_map/ppermute | solution.py:342
  43.3 56.9 %collective-permute-start.4 = (bf16[4,800,128]{2,1,0:T(8,128)(2,1)S(1)}, bf16[4,800,128]{2,1,0:T(8,128)(2,1)S(1)}, u32[]{:S(2)}, u32[]{:S(2)}) collective-permute-start(bf16[4,800,128]{2,1,0:T(8,128)(2,1)S(1)} %get-tuple-element.126), channel_id=1, source_target_pairs={{0,16},{2,18},{4,20},{6,22},{8,24},{10,26},{12,28},{14,30},{16,0},... | collective-permute-start | bytes 2457608 | tf_op jit(solution)/shard_map/ppermute | solution.py:342
  46.3 69.7 %collective-permute-start.5 = (bf16[4,800,128]{2,1,0:T(8,128)(2,1)S(1)}, bf16[4,800,128]{2,1,0:T(8,128)(2,1)S(1)}, u32[]{:S(2)}, u32[]{:S(2)}) collective-permute-start(bf16[4,800,128]{2,1,0:T(8,128)(2,1)S(1)} %get-tuple-element.127), channel_id=1, source_target_pairs={{0,24},{2,26},{4,28},{6,30},{8,16},{10,18},{12,20},{14,22},{16,8},... | collective-permute-start | bytes 2457608 | tf_op jit(solution)/shard_map/ppermute | solution.py:342
  75.7 80.3 %copy-start.22 = (bf16[4,800,128]{2,1,0:T(8,128)(2,1)}, bf16[4,800,128]{2,1,0:T(8,128)(2,1)S(1)}, u32[]{:S(2)}) copy-start(bf16[4,800,128]{2,1,0:T(8,128)(2,1)S(1)} %collective-permute-done.3) | copy-start | bytes 2457604
  100.1 56.0 %copy-start.23 = (bf16[4,800,128]{2,1,0:T(8,128)(2,1)}, bf16[4,800,128]{2,1,0:T(8,128)(2,1)S(1)}, u32[]{:S(2)}) copy-start(bf16[4,800,128]{2,1,0:T(8,128)(2,1)S(1)} %collective-permute-done.4) | copy-start | bytes 2457604
  116.1 40.0 %copy-start.24 = (bf16[4,800,128]{2,1,0:T(8,128)(2,1)}, bf16[4,800,128]{2,1,0:T(8,128)(2,1)S(1)}, u32[]{:S(2)}) copy-start(bf16[4,800,128]{2,1,0:T(8,128)(2,1)S(1)} %collective-permute-done.5) | copy-start | bytes 2457604
  116.1 39.7 %collective-permute-start.18 = (bf16[2,2,2,128,896]{4,3,2,1,0:T(8,128)(2,1)S(1)}, bf16[2,2,2,128,896]{4,3,2,1,0:T(8,128)(2,1)S(1)}, u32[]{:S(2)}, u32[]{:S(2)}) collective-permute-start(bf16[2,2,2,128,896]{4,3,2,1,0:T(8,128)(2,1)S(1)} %pad_maximum_fusion.6), channel_id=1, source_target_pairs={{0,4},{2,6},{4,0},{6,2},{8,12},{10,14},{12,8},{14,10},{16,20},{18,... | collective-permute-start | bytes 5505032 | tf_op jit(solution)/shard_map/ppermute | solution.py:293
  117.6 40.7 %collective-permute-start.17 = (bf16[2,2,2,128,896]{4,3,2,1,0:T(8,128)(2,1)S(1)}, bf16[2,2,2,128,896]{4,3,2,1,0:T(8,128)(2,1)S(1)}, u32[]{:S(2)}, u32[]{:S(2)}) collective-permute-start(bf16[2,2,2,128,896]{4,3,2,1,0:T(8,128)(2,1)S(1)} %pad_maximum_fusion.5), channel_id=1, source_target_pairs={{0,2},{2,0},{4,6},{6,4},{8,10},{10,8},{12,14},{14,12},{16,18},{18,... | collective-permute-start | bytes 5505032 | tf_op jit(solution)/shard_map/ppermute | solution.py:293
  170.3 59.3 %all-to-all-start.1 = ((bf16[4,4,800,128]{3,2,1,0:T(8,128)(2,1)}), bf16[4,4,800,128]{3,2,1,0:T(8,128)(2,1)}, u32[]{:S(2)}, u32[]{:S(2)}) async-start(bf16[4,4,800,128]{3,2,1,0:T(8,128)(2,1)} %pad_maximum_fusion.3), calls=%async_computation.1 | async-start | bytes 6553600 | tf_op jit(solution)/shard_map/all_to_all | solution.py:351
  177.6 38.2 %collective-permute-start.10 = (bf16[4,784,128]{2,1,0:T(8,128)(2,1)}, bf16[4,784,128]{2,1,0:T(8,128)(2,1)S(1)}, u32[]{:S(2)}, u32[]{:S(2)}) collective-permute-start(bf16[4,784,128]{2,1,0:T(8,128)(2,1)} %get-tuple-element.138), channel_id=1, source_target_pairs={{0,24},{2,26},{4,28},{6,30},{8,16},{10,18},{12,20},{14,22},{16,8},... | collective-permute-start | bytes 2408456 | tf_op jit(solution)/shard_map/ppermute | solution.py:342
  179.4 36.4 %collective-permute-start.8 = (bf16[4,784,128]{2,1,0:T(8,128)(2,1)S(1)}, bf16[4,784,128]{2,1,0:T(8,128)(2,1)S(1)}, u32[]{:S(2)}, u32[]{:S(2)}) collective-permute-start(bf16[4,784,128]{2,1,0:T(8,128)(2,1)S(1)} %get-tuple-element.136), channel_id=1, source_target_pairs={{0,8},{2,10},{4,12},{6,14},{8,0},{10,2},{12,4},{14,6},{16,24},{18,... | collective-permute-start | bytes 2408456 | tf_op jit(solution)/shard_map/ppermute | solution.py:342
  179.4 48.3 %collective-permute-start.9 = (bf16[4,784,128]{2,1,0:T(8,128)(2,1)S(1)}, bf16[4,784,128]{2,1,0:T(8,128)(2,1)S(1)}, u32[]{:S(2)}, u32[]{:S(2)}) collective-permute-start(bf16[4,784,128]{2,1,0:T(8,128)(2,1)S(1)} %get-tuple-element.137), channel_id=1, source_target_pairs={{0,16},{2,18},{4,20},{6,22},{8,24},{10,26},{12,28},{14,30},{16,0},... | collective-permute-start | bytes 2408456 | tf_op jit(solution)/shard_map/ppermute | solution.py:342
  181.1 2.7 copy-start
  229.6 5.2 %copy-start.20 = (bf16[4,448,128]{2,1,0:T(8,128)(2,1)S(1)}, bf16[4,448,128]{2,1,0:T(8,128)(2,1)}, u32[]{:S(2)}) copy-start(bf16[4,448,128]{2,1,0:T(8,128)(2,1)} %copy-done.19) | copy-start | bytes 1376260
  229.6 7.4 %copy-start.18 = (bf16[4,448,128]{2,1,0:T(8,128)(2,1)S(1)}, bf16[4,448,128]{2,1,0:T(8,128)(2,1)}, u32[]{:S(2)}) copy-start(bf16[4,448,128]{2,1,0:T(8,128)(2,1)} %copy-done.17) | copy-start | bytes 1376260
  229.6 8.6 %copy-start.16 = (bf16[4,448,128]{2,1,0:T(8,128)(2,1)S(1)}, bf16[4,448,128]{2,1,0:T(8,128)(2,1)}, u32[]{:S(2)}) copy-start(bf16[4,448,128]{2,1,0:T(8,128)(2,1)} %copy-done.15) | copy-start | bytes 1376260
  229.6 47.4 %all-to-all-start.2 = ((bf16[4,4,784,128]{3,2,1,0:T(8,128)(2,1)}), bf16[4,4,784,128]{3,2,1,0:T(8,128)(2,1)}, u32[]{:S(2)}, u32[]{:S(2)}) async-start(bf16[4,4,784,128]{3,2,1,0:T(8,128)(2,1)} %pad_maximum_fusion.4), calls=%async_computation.2 | async-start | bytes 6422528 | tf_op jit(solution)/shard_map/all_to_all | solution.py:351
  234.8 16.6 %collective-permute-start.11 = (bf16[4,448,128]{2,1,0:T(8,128)(2,1)S(1)}, bf16[4,448,128]{2,1,0:T(8,128)(2,1)}, u32[]{:S(2)}, u32[]{:S(2)}) collective-permute-start(bf16[4,448,128]{2,1,0:T(8,128)(2,1)S(1)} %copy-done.20), channel_id=1, source_target_pairs={{0,8},{2,10},{4,12},{6,14},{8,0},{10,2},{12,4},{14,6},{16,24},{18,... | collective-permute-start | bytes 1376264 | tf_op jit(solution)/shard_map/ppermute | solution.py:342
  237.0 30.7 %collective-permute-start.12 = (bf16[4,448,128]{2,1,0:T(8,128)(2,1)S(1)}, bf16[4,448,128]{2,1,0:T(8,128)(2,1)}, u32[]{:S(2)}, u32[]{:S(2)}) collective-permute-start(bf16[4,448,128]{2,1,0:T(8,128)(2,1)S(1)} %copy-done.18), channel_id=1, source_target_pairs={{0,16},{2,18},{4,20},{6,22},{8,24},{10,26},{12,28},{14,30},{16,0},... | collective-permute-start | bytes 1376264 | tf_op jit(solution)/shard_map/ppermute | solution.py:342
  238.2 36.0 %collective-permute-start.13 = (bf16[4,448,128]{2,1,0:T(8,128)(2,1)S(1)}, bf16[4,448,128]{2,1,0:T(8,128)(2,1)}, u32[]{:S(2)}, u32[]{:S(2)}) collective-permute-start(bf16[4,448,128]{2,1,0:T(8,128)(2,1)S(1)} %copy-done.16), channel_id=1, source_target_pairs={{0,24},{2,26},{4,28},{6,30},{8,16},{10,18},{12,20},{14,22},{16,8},... | collective-permute-start | bytes 1376264 | tf_op jit(solution)/shard_map/ppermute | solution.py:342
  277.0 62.2 %all-to-all-start = ((bf16[4,4,448,128]{3,2,1,0:T(8,128)(2,1)}), bf16[4,4,448,128]{3,2,1,0:T(8,128)(2,1)}, u32[]{:S(2)}, u32[]{:S(2)}) async-start(bf16[4,4,448,128]{3,2,1,0:T(8,128)(2,1)} %pad_maximum_fusion.7), calls=%async_computation | async-start | bytes 3670016 | tf_op jit(solution)/shard_map/all_to_all | solution.py:351
  304.7 43.4 %collective-permute-start.19 = (bf16[2048,512]{1,0:T(8,128)(2,1)}, bf16[2048,512]{1,0:T(8,128)(2,1)}, u32[]{:S(2)}, u32[]{:S(2)}) collective-permute-start(bf16[2048,512]{1,0:T(8,128)(2,1)} %hidden.1.own_h), channel_id=1, source_target_pairs={{0,1},{1,0},{2,3},{3,2},{4,5},{5,4},{6,7},{7,6},{8,9},{9,8},{10,11... | collective-permute-start | bytes 6291464 | tf_op jit(solution)/shard_map/ppermute | solution.py:339
  304.7 15.2 %collective-permute-start.14 = (bf16[4,336,128]{2,1,0:T(8,128)(2,1)S(1)}, bf16[4,336,128]{2,1,0:T(8,128)(2,1)S(1)}, u32[]{:S(2)}, u32[]{:S(2)}) collective-permute-start(bf16[4,336,128]{2,1,0:T(8,128)(2,1)S(1)} %get-tuple-element.156), channel_id=1, source_target_pairs={{0,8},{2,10},{4,12},{6,14},{8,0},{10,2},{12,4},{14,6},{16,24},{18,... | collective-permute-start | bytes 1032200 | tf_op jit(solution)/shard_map/ppermute | solution.py:342
  304.7 26.2 %collective-permute-start.15 = (bf16[4,336,128]{2,1,0:T(8,128)(2,1)S(1)}, bf16[4,336,128]{2,1,0:T(8,128)(2,1)S(1)}, u32[]{:S(2)}, u32[]{:S(2)}) collective-permute-start(bf16[4,336,128]{2,1,0:T(8,128)(2,1)S(1)} %get-tuple-element.157), channel_id=1, source_target_pairs={{0,16},{2,18},{4,20},{6,22},{8,24},{10,26},{12,28},{14,30},{16,0},... | collective-permute-start | bytes 1032200 | tf_op jit(solution)/shard_map/ppermute | solution.py:342
  307.7 30.8 %collective-permute-start.16 = (bf16[4,336,128]{2,1,0:T(8,128)(2,1)S(1)}, bf16[4,336,128]{2,1,0:T(8,128)(2,1)S(1)}, u32[]{:S(2)}, u32[]{:S(2)}) collective-permute-start(bf16[4,336,128]{2,1,0:T(8,128)(2,1)S(1)} %get-tuple-element.158), channel_id=1, source_target_pairs={{0,24},{2,26},{4,28},{6,30},{8,16},{10,18},{12,20},{14,22},{16,8},... | collective-permute-start | bytes 1032200 | tf_op jit(solution)/shard_map/ppermute | solution.py:342
  339.2 2.7 copy-start.27
  341.9 6.2 %copy-start.6 = (bf16[4,2,448,128]{3,2,1,0:T(8,128)(2,1)}, bf16[4,2,448,128]{3,2,1,0:T(8,128)(2,1)S(1)}, u32[]{:S(2)}) copy-start(bf16[4,2,448,128]{3,2,1,0:T(8,128)(2,1)S(1)} %get-tuple-element.181.own_ref) | copy-start | bytes 2752516
  341.9 6.2 %collective-permute-start.20 = (bf16[4,2,448,128]{3,2,1,0:T(8,128)(2,1)}, bf16[4,2,448,128]{3,2,1,0:T(8,128)(2,1)}, u32[]{:S(2)}, u32[]{:S(2)}) collective-permute-start(bf16[4,2,448,128]{3,2,1,0:T(8,128)(2,1)} %get-tuple-element.235), channel_id=1, source_target_pairs={{0,1},{1,0},{2,3},{3,2},{4,5},{5,4},{6,7},{7,6},{8,9},{9,8},{10,11... | collective-permute-start | bytes 2752520 | tf_op jit(solution)/shard_map/ppermute | solution.py:339
  343.3 4.7 %copy-start.8 = (bf16[2048,512]{1,0:T(8,128)(2,1)S(1)}, bf16[2048,512]{1,0:T(8,128)(2,1)}, u32[]{:S(2)}) copy-start(bf16[2048,512]{1,0:T(8,128)(2,1)} %hidden.1.own_h) | copy-start | bytes 6291460
  343.3 4.7 %copy-start.21 = (s32[2]{0:T(128)S(1)}, s32[2]{0:T(128)}, u32[]{:S(2)}) copy-start(s32[2]{0:T(128)} %pad_add_fusion.1.at_ref) | copy-start | bytes 28
  343.3 21.3 %all-to-all-start.3 = ((bf16[4,4,336,128]{3,2,1,0:T(8,128)(2,1)}), bf16[4,4,336,128]{3,2,1,0:T(8,128)(2,1)}, u32[]{:S(2)}, u32[]{:S(2)}) async-start(bf16[4,4,336,128]{3,2,1,0:T(8,128)(2,1)} %pad_maximum_fusion.8), calls=%async_computation.3 | async-start | bytes 2752512 | tf_op jit(solution)/shard_map/all_to_all | solution.py:351
  348.1 7.9 %copy-start.9 = (bf16[2048,512]{1,0:T(8,128)(2,1)S(1)}, bf16[2048,512]{1,0:T(8,128)(2,1)}, u32[]{:S(2)}) copy-start(bf16[2048,512]{1,0:T(8,128)(2,1)} %hidden.1.own_h) | copy-start | bytes 6291460
  364.6 3.6 copy-start.14
  364.6 20.4 %copy-start.5 = (f32[1024,256]{1,0:T(8,128)S(1)}, f32[1024,256]{1,0:T(8,128)}, u32[]{:S(2)}) copy-start(f32[1024,256]{1,0:T(8,128)} %copy-done.4) | copy-start | bytes 3145732
  364.6 19.2 %collective-permute-start.21 = (bf16[1024,384]{1,0:T(8,128)(2,1)}, bf16[1024,384]{1,0:T(8,128)(2,1)S(1)}, u32[]{:S(2)}, u32[]{:S(2)}) collective-permute-start(bf16[1024,384]{1,0:T(8,128)(2,1)} %copy-done.12), channel_id=1, source_target_pairs={{0,2},{2,0},{4,6},{6,4},{8,10},{10,8},{12,14},{14,12},{16,18},{18,... | collective-permute-start | bytes 2359304 | tf_op jit(solution)/shard_map/ppermute | solution.py:293
  366.1 18.9 %collective-permute-start.22 = (bf16[1024,384]{1,0:T(8,128)(2,1)}, bf16[1024,384]{1,0:T(8,128)(2,1)S(1)}, u32[]{:S(2)}, u32[]{:S(2)}) collective-permute-start(bf16[1024,384]{1,0:T(8,128)(2,1)} %copy-done.11), channel_id=1, source_target_pairs={{0,4},{2,6},{4,0},{6,2},{8,12},{10,14},{12,8},{14,10},{16,20},{18,... | collective-permute-start | bytes 2359304 | tf_op jit(solution)/shard_map/ppermute | solution.py:293
  368.1 17.9 %copy-start.10 = (bf16[2048,512]{1,0:T(8,128)(2,1)S(1)}, bf16[2048,512]{1,0:T(8,128)(2,1)}, u32[]{:S(2)}) copy-start(bf16[2048,512]{1,0:T(8,128)(2,1)} %hidden.1.own_h) | copy-start | bytes 6291460
  368.1 17.9 %collective-permute-start.31 = (bf16[4,2,336,128]{3,2,1,0:T(8,128)(2,1)S(1)}, bf16[4,2,336,128]{3,2,1,0:T(8,128)(2,1)S(1)}, u32[]{:S(2)}, u32[]{:S(2)}) collective-permute-start(bf16[4,2,336,128]{3,2,1,0:T(8,128)(2,1)S(1)} %get-tuple-element.239), channel_id=1, source_target_pairs={{0,1},{1,0},{2,3},{3,2},{4,5},{5,4},{6,7},{7,6},{8,9},{9,8},{10,11... | collective-permute-start | bytes 2064392 | tf_op jit(solution)/shard_map/ppermute | solution.py:339
  368.2 14.3 %collective-permute-start.23 = (bf16[1024,256]{1,0:T(8,128)(2,1)S(1)}, bf16[1024,256]{1,0:T(8,128)(2,1)S(1)}, u32[]{:S(2)}, u32[]{:S(2)}) collective-permute-start(bf16[1024,256]{1,0:T(8,128)(2,1)S(1)} %copy-done.14), channel_id=1, source_target_pairs={{0,8},{2,10},{4,12},{6,14},{8,0},{10,2},{12,4},{14,6},{16,24},{18,... | collective-permute-start | bytes 1572872 | tf_op jit(solution)/shard_map/ppermute | solution.py:293
  385.4 8.1 %collective-permute-start.26 = (bf16[512,256]{1,0:T(8,128)(2,1)S(1)}, bf16[512,256]{1,0:T(8,128)(2,1)S(1)}, u32[]{:S(2)}, u32[]{:S(2)}) collective-permute-start(bf16[512,256]{1,0:T(8,128)(2,1)S(1)} %get-tuple-element.197), channel_id=1, source_target_pairs={{0,2},{2,0},{4,6},{6,4},{8,10},{10,8},{12,14},{14,12},{16,18},{18,... | collective-permute-start | bytes 786440 | tf_op jit(solution)/shard_map/ppermute | solution.py:293
  389.7 15.9 %collective-permute-start.32 = (bf16[1024,256]{1,0:T(8,128)(2,1)S(1)}, bf16[1024,256]{1,0:T(8,128)(2,1)S(1)}, u32[]{:S(2)}, u32[]{:S(2)}) collective-permute-start(bf16[1024,256]{1,0:T(8,128)(2,1)S(1)} %get-tuple-element.216), channel_id=1, source_target_pairs={{0,2},{2,0},{4,6},{6,4},{8,10},{10,8},{12,14},{14,12},{16,18},{18,... | collective-permute-start | bytes 1572872 | tf_op jit(solution)/shard_map/ppermute | solution.py:293
  391.3 12.1 %collective-permute-start.24 = (bf16[512,384]{1,0:T(8,128)(2,1)S(1)}, bf16[512,384]{1,0:T(8,128)(2,1)S(1)}, u32[]{:S(2)}, u32[]{:S(2)}) collective-permute-start(bf16[512,384]{1,0:T(8,128)(2,1)S(1)} %get-tuple-element.193), channel_id=1, source_target_pairs={{0,4},{2,6},{4,0},{6,2},{8,12},{10,14},{12,8},{14,10},{16,20},{18,... | collective-permute-start | bytes 1179656 | tf_op jit(solution)/shard_map/ppermute | solution.py:293
  391.8 12.1 %collective-permute-start.25 = (bf16[512,384]{1,0:T(8,128)(2,1)S(1)}, bf16[512,384]{1,0:T(8,128)(2,1)S(1)}, u32[]{:S(2)}, u32[]{:S(2)}) collective-permute-start(bf16[512,384]{1,0:T(8,128)(2,1)S(1)} %get-tuple-element.195), channel_id=1, source_target_pairs={{0,8},{2,10},{4,12},{6,14},{8,0},{10,2},{12,4},{14,6},{16,24},{18,... | collective-permute-start | bytes 1179656 | tf_op jit(solution)/shard_map/ppermute | solution.py:293
  391.8 22.4 %collective-permute-start.33 = (bf16[1024,256]{1,0:T(8,128)(2,1)S(1)}, bf16[1024,256]{1,0:T(8,128)(2,1)S(1)}, u32[]{:S(2)}, u32[]{:S(2)}) collective-permute-start(bf16[1024,256]{1,0:T(8,128)(2,1)S(1)} %get-tuple-element.218), channel_id=1, source_target_pairs={{0,4},{2,6},{4,0},{6,2},{8,12},{10,14},{12,8},{14,10},{16,20},{18,... | collective-permute-start | bytes 1572872 | tf_op jit(solution)/shard_map/ppermute | solution.py:293
  393.5 21.6 %collective-permute-start.34 = (bf16[1024,256]{1,0:T(8,128)(2,1)S(1)}, bf16[1024,256]{1,0:T(8,128)(2,1)S(1)}, u32[]{:S(2)}, u32[]{:S(2)}) collective-permute-start(bf16[1024,256]{1,0:T(8,128)(2,1)S(1)} %get-tuple-element.220), channel_id=1, source_target_pairs={{0,8},{2,10},{4,12},{6,14},{8,0},{10,2},{12,4},{14,6},{16,24},{18,... | collective-permute-start | bytes 1572872 | tf_op jit(solution)/shard_map/ppermute | solution.py:293
  404.1 15.3 %collective-permute-start.27 = (bf16[256,384]{1,0:T(8,128)(2,1)S(1)}, bf16[256,384]{1,0:T(8,128)(2,1)S(1)}, u32[]{:S(2)}, u32[]{:S(2)}) collective-permute-start(bf16[256,384]{1,0:T(8,128)(2,1)S(1)} %get-tuple-element.199), channel_id=1, source_target_pairs={{0,8},{2,10},{4,12},{6,14},{8,0},{10,2},{12,4},{14,6},{16,24},{18,... | collective-permute-start | bytes 589832 | tf_op jit(solution)/shard_map/ppermute | solution.py:293
  404.1 15.2 %collective-permute-start.28 = (bf16[256,384]{1,0:T(8,128)(2,1)S(1)}, bf16[256,384]{1,0:T(8,128)(2,1)S(1)}, u32[]{:S(2)}, u32[]{:S(2)}) collective-permute-start(bf16[256,384]{1,0:T(8,128)(2,1)S(1)} %get-tuple-element.201), channel_id=1, source_target_pairs={{0,2},{2,0},{4,6},{6,4},{8,10},{10,8},{12,14},{14,12},{16,18},{18,... | collective-permute-start | bytes 589832 | tf_op jit(solution)/shard_map/ppermute | solution.py:293
  405.6 11.3 %collective-permute-start.29 = (bf16[256,256]{1,0:T(8,128)(2,1)S(1)}, bf16[256,256]{1,0:T(8,128)(2,1)S(1)}, u32[]{:S(2)}, u32[]{:S(2)}) collective-permute-start(bf16[256,256]{1,0:T(8,128)(2,1)S(1)} %get-tuple-element.203), channel_id=1, source_target_pairs={{0,4},{2,6},{4,0},{6,2},{8,12},{10,14},{12,8},{14,10},{16,20},{18,... | collective-permute-start | bytes 393224 | tf_op jit(solution)/shard_map/ppermute | solution.py:293
  415.4 7.5 %collective-permute-start.35 = (bf16[512,256]{1,0:T(8,128)(2,1)S(1)}, bf16[512,256]{1,0:T(8,128)(2,1)S(1)}, u32[]{:S(2)}, u32[]{:S(2)}) collective-permute-start(bf16[512,256]{1,0:T(8,128)(2,1)S(1)} %get-tuple-element.222), channel_id=1, source_target_pairs={{0,4},{2,6},{4,0},{6,2},{8,12},{10,14},{12,8},{14,10},{16,20},{18,... | collective-permute-start | bytes 786440 | tf_op jit(solution)/shard_map/ppermute | solution.py:293
  416.9 8.7 %collective-permute-start.36 = (bf16[512,256]{1,0:T(8,128)(2,1)S(1)}, bf16[512,256]{1,0:T(8,128)(2,1)S(1)}, u32[]{:S(2)}, u32[]{:S(2)}) collective-permute-start(bf16[512,256]{1,0:T(8,128)(2,1)S(1)} %get-tuple-element.224), channel_id=1, source_target_pairs={{0,8},{2,10},{4,12},{6,14},{8,0},{10,2},{12,4},{14,6},{16,24},{18,... | collective-permute-start | bytes 786440 | tf_op jit(solution)/shard_map/ppermute | solution.py:293
  417.0 8.7 %collective-permute-start.37 = (bf16[512,256]{1,0:T(8,128)(2,1)S(1)}, bf16[512,256]{1,0:T(8,128)(2,1)S(1)}, u32[]{:S(2)}, u32[]{:S(2)}) collective-permute-start(bf16[512,256]{1,0:T(8,128)(2,1)S(1)} %get-tuple-element.226), channel_id=1, source_target_pairs={{0,2},{2,0},{4,6},{6,4},{8,10},{10,8},{12,14},{14,12},{16,18},{18,... | collective-permute-start | bytes 786440 | tf_op jit(solution)/shard_map/ppermute | solution.py:293
  419.4 15.6 %collective-permute-start.30 = (bf16[128,1024]{1,0:T(8,128)(2,1)S(1)}, bf16[128,1024]{1,0:T(8,128)(2,1)S(1)}, u32[]{:S(2)}, u32[]{:S(2)}) collective-permute-start(bf16[128,1024]{1,0:T(8,128)(2,1)S(1)} %get-tuple-element.205), channel_id=1, source_target_pairs={{0,16},{2,18},{4,20},{6,22},{8,24},{10,26},{12,28},{14,30},{16,0},... | collective-permute-start | bytes 786440 | tf_op jit(solution)/shard_map/ppermute | solution.py:293
  425.8 5.6 %collective-permute-start.38 = (bf16[256,256]{1,0:T(8,128)(2,1)S(1)}, bf16[256,256]{1,0:T(8,128)(2,1)S(1)}, u32[]{:S(2)}, u32[]{:S(2)}) collective-permute-start(bf16[256,256]{1,0:T(8,128)(2,1)S(1)} %get-tuple-element.228), channel_id=1, source_target_pairs={{0,8},{2,10},{4,12},{6,14},{8,0},{10,2},{12,4},{14,6},{16,24},{18,... | collective-permute-start | bytes 393224 | tf_op jit(solution)/shard_map/ppermute | solution.py:293
  426.3 5.2 %collective-permute-start.39 = (bf16[256,256]{1,0:T(8,128)(2,1)S(1)}, bf16[256,256]{1,0:T(8,128)(2,1)S(1)}, u32[]{:S(2)}, u32[]{:S(2)}) collective-permute-start(bf16[256,256]{1,0:T(8,128)(2,1)S(1)} %get-tuple-element.230), channel_id=1, source_target_pairs={{0,2},{2,0},{4,6},{6,4},{8,10},{10,8},{12,14},{14,12},{16,18},{18,... | collective-permute-start | bytes 393224 | tf_op jit(solution)/shard_map/ppermute | solution.py:293
  427.0 5.0 %collective-permute-start.40 = (bf16[256,256]{1,0:T(8,128)(2,1)S(1)}, bf16[256,256]{1,0:T(8,128)(2,1)S(1)}, u32[]{:S(2)}, u32[]{:S(2)}) collective-permute-start(bf16[256,256]{1,0:T(8,128)(2,1)S(1)} %get-tuple-element.232), channel_id=1, source_target_pairs={{0,4},{2,6},{4,0},{6,2},{8,12},{10,14},{12,8},{14,10},{16,20},{18,... | collective-permute-start | bytes 393224 | tf_op jit(solution)/shard_map/ppermute | solution.py:293
  432.0 8.0 %collective-permute-start.41 = (bf16[128,768]{1,0:T(8,128)(2,1)S(1)}, bf16[128,768]{1,0:T(8,128)(2,1)S(1)}, u32[]{:S(2)}, u32[]{:S(2)}) collective-permute-start(bf16[128,768]{1,0:T(8,128)(2,1)S(1)} %get-tuple-element.234), channel_id=1, source_target_pairs={{0,16},{2,18},{4,20},{6,22},{8,24},{10,26},{12,28},{14,30},{16,0},... | collective-permute-start | bytes 589832 | tf_op jit(solution)/shard_map/ppermute | solution.py:293
  (11 other events, 11.6 us)
Sparse Core Ops, SparseCore 0:
  167.3 27.6 all-gather.2

commit v12 on v5

--- a/solution.py
+++ b/solution.py
@@ -147,45 +147,39 @@
     ).astype(out_ref.dtype)
 
 
-def hidden_kernel(at_ref, *refs):
-    pieces, (packed_ref, out_ref, gate_w, up_w, rows) = refs[:8], refs[8:]
+def hidden_kernel(at_ref, x_ref, packed_ref, out_ref, gate_w, up_w):
+    cores, rows, mid = x_ref.shape
     sources = packed_ref.shape[0]
     depth = gate_w.shape[0] // sources
     size = depth * 7 // 2
-    group = sources // 2
     tile = pl.program_id(0)
     x, y, zl = tile // 4, tile // 2 % 2, tile % 2
-    me, core = at_ref[0], at_ref[1]
 
     @pl.when(tile == 0)
     def _():
         for at in range(sources):
-            place = (core + at // group) % 2 * group + at % group
-            unpack_rows(packed_ref, place, 0, depth, gate_w, at * depth, 0)
-            unpack_rows(packed_ref, place, size, depth, up_w, at * depth, 0)
-
-    mid = pieces[0].shape[1]
-    for number in range(4):
-        lanes = slice(number * mid, (number + 1) * mid)
-        coordinate = (x, y)[number % 2]
-        for value in range(2):
-
-            @pl.when(coordinate == value)
-            def _():
-                rows[:, lanes] = pieces[2 * number + value][...]
-
-    gate = jnp.dot(rows[...], gate_w[...], preferred_element_type=jnp.float32)
-    up = jnp.dot(rows[...], up_w[...], preferred_element_type=jnp.float32)
-    value = gate / (1.0 + jnp.exp(-gate)) * up
+            unpack_rows(packed_ref, at, 0, depth, gate_w, at * depth, 0)
+            unpack_rows(packed_ref, at, size, depth, up_w, at * depth, 0)
+
+    def product(w_ref):
+        return sum(
+            jnp.dot(
+                x_ref[at], w_ref[at * mid : (at + 1) * mid, :], preferred_element_type=jnp.float32
+            )
+            for at in range(cores)
+        )
+
+    gate = product(gate_w)
+    value = gate / (1.0 + jnp.exp(-gate)) * product(up_w)
 
     wide = gate.shape[1]
     term = lax.broadcasted_iota(jnp.int32, (16, wide), 0)
     lane = lax.broadcasted_iota(jnp.int32, (16, wide), 1)
     chosen = (term % 4 == lane // LANES) & (term < 12) & (lane < wide - HALF)
     chosen = jnp.where(chosen, 1.0, 0.0).astype(jnp.bfloat16)
-    block = rows.shape[0] // 2
+    block = rows // 2
     for zh in range(2):
-        source = me ^ (x + 2 * y + 4 * zl + 8 * zh)
+        source = at_ref[0] ^ (x + 2 * y + 4 * zl + 8 * zh)
         weight = lax.dot_general(
             packed_ref[source, packed_ref.shape[1] - 16 :, :],
             chosen,
@@ -196,36 +190,27 @@
         out_ref[span, :] = (value[span, :] * weight).astype(out_ref.dtype)
 
 
-def hidden_units(at, pieces, packed):
-    total = 2 * pieces[0].shape[0]
-    mid = pieces[0].shape[1]
+def hidden_units(at, rows, packed):
+    cores, total, mid = rows.shape
     tile = total // 8
     wide = 4 * LANES
-    model = 4 * mid
-    by_x = [lambda i: (jnp.minimum(i, 3), 0), lambda i: (jnp.maximum(i - 4, 0), 0)]
-    by_y = [
-        lambda i: (i // 4 * 2 + jnp.where(i // 2 % 2 == 0, i % 2, 1), 0),
-        lambda i: (i // 4 * 2 + jnp.where(i // 2 % 2 == 1, i % 2, 0), 0),
-    ]
-    maps = (by_x + by_y) * 2
+    model = cores * mid
     return pl.pallas_call(
         hidden_kernel,
         grid=(8,),
-        out_shape=jax.ShapeDtypeStruct((total, wide), packed.dtype),
-        in_specs=[smem()]
-        + [pl.BlockSpec((tile, mid), where) for where in maps]
-        + [vmem()],
+        out_shape=jax.ShapeDtypeStruct((total, wide), rows.dtype),
+        in_specs=[smem(), pl.BlockSpec((cores, tile, mid), lambda i: (0, i, 0)), vmem()],
         out_specs=pl.BlockSpec((tile, wide), lambda i: (i, 0)),
-        scratch_shapes=[pltpu.VMEM((model, wide), packed.dtype)] * 2
-        + [pltpu.VMEM((tile, model), packed.dtype)],
+        scratch_shapes=[pltpu.VMEM((model, wide), rows.dtype)] * 2,
         compiler_params=pltpu.CompilerParams(vmem_limit_bytes=56 * MIB),
         cost_estimate=pl.CostEstimate(
             flops=4 * total * model * wide, bytes_accessed=24 * MIB, transcendentals=total * wide
         ),
         name="hidden",
-    )(at, *pieces, packed)
-
-
+    )(at, rows, packed)
+
+
+HALVES = ((0, 1, 2), (1, 0, 2))
 THIRDS = ((0, 1, 2), (1, 2, 0), (2, 0, 1))
 
 
@@ -392,38 +377,66 @@
     belongs = slot_place[None, None, :, None] == places[:, :, None, None]
     share = jnp.sum(jnp.where(belongs, share[None, None], 0.0), axis=2)
 
-    near, far = swap(tokens, 2), swap(tokens, 3)
-    corner = swap(far, 2)
+    mid = tokens.shape[1] // 2
+    first, second = slice(0, mid), slice(mid, 2 * mid)
+
+    def lay(*values):
+        return jnp.concatenate(values, axis=0)
+
     parts = (128, 96)
     packed = pack_first(listing, gate_proj, up_proj, down_proj, parts[0], share, devices)
-    packed, near, far, corner = tie((packed, near, far, corner))
+    far_a, far_b = swap(tokens[:, first], 3), swap(tokens[:, second], 3)
+    near = swap(tokens, 2)
+    far_a, packed = tie((far_a, packed))
+    corner_a, corner_b = swap(far_a, 2), swap(far_b, 2)
+    pair_a, pair_b = lay(far_a, near[:, first]), lay(far_b, near[:, second])
+    pair_y, pair_x = swap(pair_a, 1), swap(pair_b, 0)
+    packed, pair_a, pair_b, corner_a, corner_b, pair_y, pair_x = tie(
+        (packed, pair_a, pair_b, corner_a, corner_b, pair_y, pair_x)
+    )
 
     moved = move(packed)
-    mid = tokens.shape[1] // 2
-    rows = jnp.concatenate([tokens, far, near, corner], axis=0)
-    first, second = rows[:, :mid], rows[:, mid:]
-    first = jnp.concatenate([first, swap(first, 1)], axis=0)
-    second = jnp.concatenate([second, swap(second, 0)], axis=0)
-    pieces = [first, swap(first, 0), second, swap(second, 1)]
-    others = [exchange(piece) for piece in pieces]
+    column_a = lay(tokens[:, first], pair_a, corner_a)
+    column_b = lay(tokens[:, second], pair_b, corner_b)
+    ends_a, ends_b = lay(tokens[:, first], corner_a), lay(tokens[:, second], corner_b)
+    most_a, most_b = swap(lay(column_a, pair_y), 0), swap(lay(column_b, pair_x), 1)
+    ends_y, ends_x = swap(ends_a, 1), swap(ends_b, 0)
+    cross = jnp.concatenate([ends_a, ends_b], axis=1)
+    cross = lax.ppermute(cross, "ep", [(i, i ^ 3) for i in range(devices)])
+    top, low = slice(0, block), slice(block, 2 * block)
+    four, rest_two = slice(0, 4 * block), slice(4 * block, 6 * block)
+    y_side = lay(ends_y[top], pair_y, ends_y[low])
+    x_side = lay(ends_x[top], pair_x, ends_x[low])
+    cross_a = lay(cross[top, first], most_a[rest_two], cross[low, first])
+    cross_b = lay(cross[top, second], most_b[rest_two], cross[low, second])
+    rows = jnp.concatenate(
+        [
+            lay(column_a, y_side, most_a[four], cross_a),
+            lay(column_b, most_b[four], x_side, cross_b),
+        ],
+        axis=1,
+    )
+    rows = lax.all_gather(rows, "et")
     rest = pack_rest(listing, down_proj, parts[0], devices)
-    moved, rest = tie((moved, rest))
+    moved, rest, rows = tie((moved, rest, rows))
 
     down1 = move(rest)
     at = jnp.stack([me, core]).astype(jnp.int32)
-    hidden = hidden_units(at, pieces + others, moved)
+    hidden = hidden_units(at, rows, moved)
     hidden_other = exchange(hidden)
     down0 = moved[:, depth * 7 : depth * 7 + parts[0] * 7 // 2]
 
-    def products(down, rows_in, orders):
+    def slivers(down):
         own = lax.dynamic_slice_in_dim(down, core * group, group, 0)
-        other = exchange(lax.dynamic_slice_in_dim(down, (1 - core) * group, group, 0))
-        args = (hidden, hidden_other, own, other)
-        sent = down_product(*args, rows_in, 1, orders, jnp.bfloat16, "down_send")
-        sent, args = tie((sent, args))
-        come = [swap(value, order[0]) for value, order in zip(sent, orders)]
-        kept = down_product(*args, rows_in, 0, orders, jnp.float32, "down_keep")
-        return kept, come, sent
+        return own, exchange(lax.dynamic_slice_in_dim(down, (1 - core) * group, group, 0))
+
+    def product(weights, rows_in, side, orders, after=None):
+        args, _ = tie(((hidden, hidden_other, *weights), after))
+        kind = ((jnp.float32, "down_keep"), (jnp.bfloat16, "down_send"))[side]
+        return down_product(*args, rows_in, side, orders, *kind)
+
+    def send(values, orders):
+        return [swap(value, order[0]) for value, order in zip(values, orders)]
 
     def stage(kept, come, number, orders):
         axes = tuple(stage_axis(order, number) for order in orders)
@@ -436,13 +449,17 @@
         come = swap(send, 3)
         return (keep + come.astype(jnp.float32)).astype(jnp.bfloat16)
 
-    kept0, come0, _ = products(down0, parts[0], THIRDS)
-    down1, kept0 = tie((down1, kept0))
-    kept1, come1, sent1 = products(down1, parts[1], THIRDS)
-    kept0, _ = tie((kept0, sent1))
-    kept0, come0 = stage(kept0, come0, 1, THIRDS)
+    weights0 = slivers(down0)
+    sent0 = product(weights0, parts[0], 1, HALVES)
+    come0 = send(sent0, HALVES)
+    weights1 = slivers(tie((down1, sent0))[0])
+    sent1 = product(weights1, parts[1], 1, THIRDS)
+    come1 = send(sent1, THIRDS)
+    kept0 = product(weights0, parts[0], 0, HALVES, after=sent1)
+    kept1 = product(weights1, parts[1], 0, THIRDS, after=sent1)
+    kept0, come0 = stage(kept0, come0, 1, HALVES)
     kept1, come1 = stage(kept1, come1, 1, THIRDS)
-    kept0, come0 = stage(kept0, come0, 2, THIRDS)
+    kept0, come0 = stage(kept0, come0, 2, HALVES)
     kept1, come1 = stage(kept1, come1, 2, THIRDS)
     out = []
     for rows_in, total in zip(parts, (last_stage(kept0, come0), last_stage(kept1, come1))):

time: 359 us -> 375 us (1.045)
  waiting for transfers between devices: 235 us -> 210 us
  local copies, waits for them, and re-layouts: 19.8 us -> 38.4 us
  between operations: 0.33 us -> 13.6 us
  other arithmetic: 6.13 us -> 16.4 us
    ppermute x27 -> x28, waiting for transfers between devices: 198 us -> 124 us  [swap(): return lax.ppermute(value, 'ep', [(i, i ^ 1 << bit) for i in range(size)])]
    all_to_all x2, waiting for transfers between devices: 33.9 us -> 80.4 us  [move(): return lax.all_to_all(packed, 'ep', 0, 0, tiled=True)]
    unnamed x39, local copies, waits for them, and re-layouts: 15 us -> 32.8 us
    concatenate x2 -> x8, other arithmetic: 1.55 us -> 11.8 us  [the longest x1 6.66 us: packed_layer(): jnp.concatenate([lay(column_a, y_side, most_a[four], cross_a), lay(column...]
    ppermute x27 -> x28, starting transfers between devices: 30.2 us -> 31.1 us  [swap(): return lax.ppermute(value, 'ep', [(i, i ^ 1 << bit) for i in range(size)])]
  transfers between devices with their start and end apart: 36 -> 35, of which waited for: 21 -> 18; matrix products, arithmetic and copies ran while one was open for 2% -> 11% of each run, Pallas kernels for 12% -> 11%
where the time goes in v12:
time: 375 us; the launch traced here: 371 us
  waiting for transfers between devices  210 us (56%)
  starting transfers between devices  50.7 us (14%)
  Pallas kernels  41.6 us (11%)
  local copies, waits for them, and re-layouts  38.4 us (10%)
  other arithmetic  16.4 us (4%)
  between operations  13.6 us (4%)
    ppermute x28, waiting for transfers between devices, swap(): return lax.ppermute(value, 'ep', [(i, i ^ 1 << bit) for i in range(size)])  124 us
    all_to_all x2, waiting for transfers between devices, move(): return lax.all_to_all(packed, 'ep', 0, 0, tiled=True)  80.4 us
    unnamed x39, local copies, waits for them, and re-layouts  32.8 us
    ppermute x28, starting transfers between devices, swap(): return lax.ppermute(value, 'ep', [(i, i ^ 1 << bit) for i in range(size)])  31.1 us
    pallas_call x1, Pallas kernels, hidden_units(): pl.pallas_call(hidden_kernel, grid=(8,), out_shape=jax.ShapeDtypeStruct((...  23.3 us
    all_to_all x2, starting transfers between devices, move(): return lax.all_to_all(packed, 'ep', 0, 0, tiled=True)  17.5 us
    pallas_call x4, Pallas kernels, down_product(): pl.pallas_call(functools.partial(down_kernel, rows, side, orders), out_sh...  10 us
  transfers between devices with their start and end apart: 35, of which 18 were waited for; matrix products, arithmetic and copies ran while one was open for 11% of the time, Pallas kernels for 11%

profile of v12, /device:TPU:14, one launch (start us, length us, event | category | flops | bytes accessed | tf_op | source)
XLA Modules:
  0.0 370.6 jit_solution(13401158824848512671)
XLA Ops:
  7.0 1.9 constant_dynamic-update-slice_fusion.3
  8.9 2.6 collective-permute-start
  11.8 0.9 select_reduce_fusion.4
  14.7 0.9 select_reduce_fusion.share_ref
  15.6 2.0 copy-done
  17.7 2.0 copy-done.2
  19.7 2.0 copy-done.3
  21.7 5.4 %pack_first.1 = bf16[16,2032,128]{2,1,0:T(8,128)(2,1)} custom-call(s32[14]{0:T(128)S(1)} %select_reduce_fusion.3.list_ref, bf16[16,224,512]{2,1,0:T(8,128)(2,1)S(1)} %copy-done.2, bf16[16,224,512]{2,1,0:T(8,128)(2,1)S(1)} %copy-done.3, bf16[16,224,512]{2,1,0:T(8,128)(2,1)S(1)} %copy-done, f32[16,16,128]{2,1,0:T(8,128)S(1)} %select_reduce_fusion.share_ref), custom_call_target="tpu_custom_call" | custom-call | tf_op jit(solution)/shard_map/pack_first/pallas_call | solution.py:113
  27.8 3.0 collective-permute-done.2
  31.5 2.4 collective-permute-start.3
  33.9 6.5 %collective-permute-done.3 = bf16[128,896]{1,0:T(8,128)(2,1)S(1)} collective-permute-done((bf16[128,896]{1,0:T(8,128)(2,1)S(1)}, bf16[128,896]{1,0:T(8,128)(2,1)S(1)}, u32[]{:S(2)}, u32[]{:S(2)}) %collective-permute-start.3) | collective-permute-done | bytes 229408 | tf_op jit(solution)/shard_map/ppermute | solution.py:320
  40.4 2.6 collective-permute-done.4
  43.8 1.3 pad_maximum_fusion.2
  45.5 1.5 collective-permute-start.11
  47.8 1.5 collective-permute-start.7
  49.4 1.0 maximum_maximum_fusion
  50.4 1.2 pad_maximum_fusion.1
  52.1 1.4 collective-permute-start.9
  53.5 7.4 %all-to-all-start = ((bf16[16,2032,128]{2,1,0:T(8,128)(2,1)}), bf16[16,2032,128]{2,1,0:T(8,128)(2,1)}, u32[]{:S(2)}, u32[]{:S(2)}) async-start(bf16[16,2032,128]{2,1,0:T(8,128)(2,1)} %pack_first.1), calls=%async_computation | async-start | bytes 16646144 | tf_op jit(solution)/shard_map/all_to_all | solution.py:369
  60.9 1.0 constant_dynamic-update-slice_fusion.2
  63.4 68.1 %collective-permute-done.7 = bf16[256,896]{1,0:T(8,128)(2,1)} collective-permute-done((bf16[256,896]{1,0:T(8,128)(2,1)}, bf16[256,896]{1,0:T(8,128)(2,1)}, u32[]{:S(2)}, u32[]{:S(2)}) %collective-permute-start.7) | collective-permute-done | bytes 458784 | tf_op jit(solution)/shard_map/ppermute | solution.py:320
  131.5 1.6 slice_dynamic-update-slice_fusion.11
  133.1 0.8 constant_dynamic-update-slice_fusion
  133.9 1.6 slice_dynamic-update-slice_fusion.10
  135.6 2.2 slice_dynamic-update-slice_fusion
  137.8 1.6 slice_dynamic-update-slice_fusion.7
  140.3 1.6 slice_dynamic-update-slice_fusion.6
  142.0 2.2 slice_dynamic-update-slice_fusion.1
  145.0 1.8 slice_dynamic-update-slice_fusion.2
  146.8 1.8 slice_dynamic-update-slice_fusion.3
  149.4 6.7 %pad_maximum_fusion = bf16[2048,1792]{1,0:T(8,128)(2,1)} fusion(bf16[2048,896]{1,0:T(8,128)(2,1)} %get-tuple-element.136, bf16[2048,896]{1,0:T(8,128)(2,1)} %get-tuple-element.135), kind=kLoop, calls=%fused_computation | loop fusion | flops 14680064 | bytes 14680064 | tf_op jit(solution)/shard_map/concatenate | solution.py:412
  156.1 2.0 copy-done.1
  158.2 1.9 pack_rest.1
  160.7 80.4 %all-to-all-done.packed_ref = bf16[16,2032,128]{2,1,0:T(8,128)(2,1)} async-done(((bf16[16,2032,128]{2,1,0:T(8,128)(2,1)}), bf16[16,2032,128]{2,1,0:T(8,128)(2,1)}, u32[]{:S(2)}, u32[]{:S(2)}) %all-to-all-start) | async-done | bytes 8323104 | tf_op jit(solution)/shard_map/all_to_all | solution.py:369
  241.2 10.1 %all-to-all-start.1 = ((bf16[16,336,128]{2,1,0:T(8,128)(2,1)}), bf16[16,336,128]{2,1,0:T(8,128)(2,1)}, u32[]{:S(2)}, u32[]{:S(2)}) async-start(bf16[16,336,128]{2,1,0:T(8,128)(2,1)} %pack_rest.1), calls=%async_computation.1 | async-start | bytes 2752512 | tf_op jit(solution)/shard_map/all_to_all | solution.py:369
  251.3 23.3 %hidden.1.own_h = bf16[2048,512]{1,0:T(8,128)(2,1)} custom-call(s32[2]{0:T(128)} %pad_add_fusion.at_ref, bf16[2,2048,1792]{2,1,0:T(8,128)(2,1)} %bitcast.13, bf16[16,2032,128]{2,1,0:T(8,128)(2,1)} %all-to-all-done.packed_ref), custom_call_target="tpu_custom_call" | custom-call | flops 15032385536 | bytes 25165824 | tf_op jit(solution)/shard_map/hidden/pallas_call | solution.py:198
  274.6 1.8 slice.71
  277.1 3.0 collective-permute-done.13.other_ref
  280.0 3.7 %down_send.2 = (bf16[1024,512]{1,0:T(8,128)(2,1)}, bf16[1024,512]{1,0:T(8,128)(2,1)}) custom-call(bf16[2048,512]{1,0:T(8,128)(2,1)S(1)} %copy-done.4, bf16[2048,512]{1,0:T(8,128)(2,1)S(1)} %collective-permute-done.12.other_h, bf16[8,448,128]{2,1,0:T(8,128)(2,1)S(1)} %get-tuple-element.96.own_ref, bf16[8,448,128]{2,1,0:T(8,128)(2,1)S(1)} %collective-permute-done.13.other_ref), custom_call_target="tpu_custom_call" | custom-call | flops 2147483648 | bytes 8388608 | tf_op jit(solution)/shard_map/down_send/pallas_call | solution.py:260
  284.9 1.5 constant_dynamic-slice_fusion
  286.5 2.1 collective-permute-done.14.other_ref
  288.6 1.6 copy-done.5
  290.2 1.6 copy-done.8
  291.8 1.9 down_send.3
  293.8 2.5 down_keep.2
  296.3 12.9 %collective-permute-done.15.refs_1_ = bf16[1024,512]{1,0:T(8,128)(2,1)S(1)} collective-permute-done((bf16[1024,512]{1,0:T(8,128)(2,1)}, bf16[1024,512]{1,0:T(8,128)(2,1)S(1)}, u32[]{:S(2)}, u32[]{:S(2)}) %collective-permute-start.15) | collective-permute-done | bytes 1048608 | tf_op jit(solution)/shard_map/ppermute | solution.py:320
  310.4 1.5 collective-permute-start.18
  312.4 1.6 collective-permute-start.23
  314.5 10.3 %collective-permute-done.17.refs_1_ = bf16[512,512]{1,0:T(8,128)(2,1)S(1)} collective-permute-done((bf16[512,512]{1,0:T(8,128)(2,1)S(1)}, bf16[512,512]{1,0:T(8,128)(2,1)S(1)}, u32[]{:S(2)}, u32[]{:S(2)}) %collective-permute-start.17) | collective-permute-done | bytes 524320 | tf_op jit(solution)/shard_map/ppermute | solution.py:320
  325.9 1.7 collective-permute-start.20
  327.5 1.9 down_keep.3
  329.5 4.8 %collective-permute-done.22.refs_1_ = bf16[1024,256]{1,0:T(8,128)(2,1)S(1)} collective-permute-done((bf16[1024,256]{1,0:T(8,128)(2,1)S(1)}, bf16[1024,256]{1,0:T(8,128)(2,1)S(1)}, u32[]{:S(2)}, u32[]{:S(2)}) %collective-permute-start.22) | collective-permute-done | bytes 524320 | tf_op jit(solution)/shard_map/ppermute | solution.py:320
  334.5 1.6 collective-permute-start.25
  336.6 1.4 collective-permute-start.27
  338.1 2.4 collective-permute-start.21
  340.9 5.4 %collective-permute-done.26.refs_3_ = bf16[512,256]{1,0:T(8,128)(2,1)S(1)} collective-permute-done((bf16[512,256]{1,0:T(8,128)(2,1)S(1)}, bf16[512,256]{1,0:T(8,128)(2,1)S(1)}, u32[]{:S(2)}, u32[]{:S(2)}) %collective-permute-start.26) | collective-permute-done | bytes 262176 | tf_op jit(solution)/shard_map/ppermute | solution.py:320
  346.4 2.5 collective-permute-start.28
  349.0 1.2 collective-permute-start.29
  350.8 1.1 collective-permute-done.28.refs_1_
  351.9 2.0 collective-permute-done.29.refs_3_
  354.0 1.2 collective-permute-done.30.refs_5_
  355.3 2.0 collective-permute-start.31
  357.5 5.1 %collective-permute-done.31 = bf16[128,768]{1,0:T(8,128)(2,1)S(1)} collective-permute-done((bf16[128,768]{1,0:T(8,128)(2,1)S(1)}, bf16[128,768]{1,0:T(8,128)(2,1)S(1)}, u32[]{:S(2)}, u32[]{:S(2)}) %collective-permute-start.31) | collective-permute-done | bytes 196640 | tf_op jit(solution)/shard_map/ppermute | solution.py:320
  362.8 1.0 copy.15
  (87 shorter events, 19.2 us)
Async XLA Ops:
  6.5 20.6 %collective-permute-start.1 = (bf16[128,1792]{1,0:T(8,128)(2,1)}, bf16[128,1792]{1,0:T(8,128)(2,1)S(1)}, u32[]{:S(2)}, u32[]{:S(2)}) collective-permute-start(bf16[128,1792]{1,0:T(8,128)(2,1)} %param.9), channel_id=1, source_target_pairs={{0,8},{2,10},{4,12},{6,14},{8,0},{10,2},{12,4},{14,6},{16,24},{18,... | collective-permute-start | bytes 1376264 | tf_op jit(solution)/shard_map/ppermute | solution.py:320
  8.9 18.3 %collective-permute-start = (bf16[128,896]{1,0:T(8,128)(2,1)S(1)}, bf16[128,896]{1,0:T(8,128)(2,1)S(1)}, u32[]{:S(2)}, u32[]{:S(2)}) collective-permute-start(bf16[128,896]{1,0:T(8,128)(2,1)S(1)} %get-tuple-element.141), channel_id=1, source_target_pairs={{0,16},{2,18},{4,20},{6,22},{8,24},{10,26},{12,28},{14,30},{16,0},... | collective-permute-start | bytes 688136 | tf_op jit(solution)/shard_map/ppermute | solution.py:320
  11.5 19.4 %collective-permute-start.2 = (bf16[128,896]{1,0:T(8,128)(2,1)S(1)}, bf16[128,896]{1,0:T(8,128)(2,1)S(1)}, u32[]{:S(2)}, u32[]{:S(2)}) collective-permute-start(bf16[128,896]{1,0:T(8,128)(2,1)S(1)} %get-tuple-element.142), channel_id=1, source_target_pairs={{0,16},{2,18},{4,20},{6,22},{8,24},{10,26},{12,28},{14,30},{16,0},... | collective-permute-start | bytes 688136 | tf_op jit(solution)/shard_map/ppermute | solution.py:320
  15.6 2.0 copy-start
  17.7 2.0 copy-start.2
  19.7 2.0 copy-start.3
  27.2 15.7 %collective-permute-start.5 = (bf16[256,896]{1,0:T(8,128)(2,1)S(1)}, bf16[256,896]{1,0:T(8,128)(2,1)S(1)}, u32[]{:S(2)}, u32[]{:S(2)}) collective-permute-start(bf16[256,896]{1,0:T(8,128)(2,1)S(1)} %pad_maximum_fusion.3), channel_id=1, source_target_pairs={{0,4},{2,6},{4,0},{6,2},{8,12},{10,14},{12,8},{14,10},{16,20},{18,... | collective-permute-start | bytes 1376264 | tf_op jit(solution)/shard_map/ppermute | solution.py:320
  30.9 12.1 %collective-permute-start.6 = (bf16[256,896]{1,0:T(8,128)(2,1)S(1)}, bf16[256,896]{1,0:T(8,128)(2,1)S(1)}, u32[]{:S(2)}, u32[]{:S(2)}) collective-permute-start(bf16[256,896]{1,0:T(8,128)(2,1)S(1)} %pad_maximum_fusion.4), channel_id=1, source_target_pairs={{0,2},{2,0},{4,6},{6,4},{8,10},{10,8},{12,14},{14,12},{16,18},{18,... | collective-permute-start | bytes 1376264 | tf_op jit(solution)/shard_map/ppermute | solution.py:320
  31.5 8.9 %collective-permute-start.3 = (bf16[128,896]{1,0:T(8,128)(2,1)S(1)}, bf16[128,896]{1,0:T(8,128)(2,1)S(1)}, u32[]{:S(2)}, u32[]{:S(2)}) collective-permute-start(bf16[128,896]{1,0:T(8,128)(2,1)S(1)} %collective-permute-done), channel_id=1, source_target_pairs={{0,8},{2,10},{4,12},{6,14},{8,0},{10,2},{12,4},{14,6},{16,24},{18,... | collective-permute-start | bytes 688136 | tf_op jit(solution)/shard_map/ppermute | solution.py:320
  33.9 9.1 %collective-permute-start.4 = (bf16[128,896]{1,0:T(8,128)(2,1)S(1)}, bf16[128,896]{1,0:T(8,128)(2,1)S(1)}, u32[]{:S(2)}, u32[]{:S(2)}) collective-permute-start(bf16[128,896]{1,0:T(8,128)(2,1)S(1)} %collective-permute-done.2), channel_id=1, source_target_pairs={{0,8},{2,10},{4,12},{6,14},{8,0},{10,2},{12,4},{14,6},{16,24},{18,... | collective-permute-start | bytes 688136 | tf_op jit(solution)/shard_map/ppermute | solution.py:320
  45.0 90.6 %collective-permute-start.10 = (bf16[768,896]{1,0:T(8,128)(2,1)}, bf16[768,896]{1,0:T(8,128)(2,1)}, u32[]{:S(2)}, u32[]{:S(2)}) collective-permute-start(bf16[768,896]{1,0:T(8,128)(2,1)} %pad_maximum_fusion.2), channel_id=1, source_target_pairs={{0,4},{2,6},{4,0},{6,2},{8,12},{10,14},{12,8},{14,10},{16,20},{18,... | collective-permute-start | bytes 4128776 | tf_op jit(solution)/shard_map/ppermute | solution.py:320
  45.5 92.3 %collective-permute-start.11 = (bf16[256,896]{1,0:T(8,128)(2,1)}, bf16[256,896]{1,0:T(8,128)(2,1)}, u32[]{:S(2)}, u32[]{:S(2)}) collective-permute-start(bf16[256,896]{1,0:T(8,128)(2,1)} %pad_maximum_fusion.6), channel_id=1, source_target_pairs={{0,2},{2,0},{4,6},{6,4},{8,10},{10,8},{12,14},{14,12},{16,18},{18,... | collective-permute-start | bytes 1376264 | tf_op jit(solution)/shard_map/ppermute | solution.py:320
  47.8 83.6 %collective-permute-start.7 = (bf16[256,896]{1,0:T(8,128)(2,1)}, bf16[256,896]{1,0:T(8,128)(2,1)}, u32[]{:S(2)}, u32[]{:S(2)}) collective-permute-start(bf16[256,896]{1,0:T(8,128)(2,1)} %pad_maximum_fusion.5), channel_id=1, source_target_pairs={{0,4},{2,6},{4,0},{6,2},{8,12},{10,14},{12,8},{14,10},{16,20},{18,... | collective-permute-start | bytes 1376264 | tf_op jit(solution)/shard_map/ppermute | solution.py:320
  51.6 90.4 %collective-permute-start.8 = (bf16[768,896]{1,0:T(8,128)(2,1)}, bf16[768,896]{1,0:T(8,128)(2,1)}, u32[]{:S(2)}, u32[]{:S(2)}) collective-permute-start(bf16[768,896]{1,0:T(8,128)(2,1)} %pad_maximum_fusion.1), channel_id=1, source_target_pairs={{0,2},{2,0},{4,6},{6,4},{8,10},{10,8},{12,14},{14,12},{16,18},{18,... | collective-permute-start | bytes 4128776 | tf_op jit(solution)/shard_map/ppermute | solution.py:320
  52.1 92.1 %collective-permute-start.9 = (bf16[256,1792]{1,0:T(8,128)(2,1)}, bf16[256,1792]{1,0:T(8,128)(2,1)S(1)}, u32[]{:S(2)}, u32[]{:S(2)}) collective-permute-start(bf16[256,1792]{1,0:T(8,128)(2,1)} %maximum_maximum_fusion), channel_id=1, source_target_pairs={{0,6},{2,4},{4,2},{6,0},{8,14},{10,12},{12,10},{14,8},{16,22},{18,... | collective-permute-start | bytes 2752520 | tf_op jit(solution)/shard_map/ppermute | solution.py:405
  53.5 187.6 %all-to-all-start = ((bf16[16,2032,128]{2,1,0:T(8,128)(2,1)}), bf16[16,2032,128]{2,1,0:T(8,128)(2,1)}, u32[]{:S(2)}, u32[]{:S(2)}) async-start(bf16[16,2032,128]{2,1,0:T(8,128)(2,1)} %pack_first.1), calls=%async_computation | async-start | bytes 16646144 | tf_op jit(solution)/shard_map/all_to_all | solution.py:369
  60.9 180.3 %all-gather.3.cloned.1.call-start = ((), (), s32[]{:S(2)}) async-start(), calls=%async_computation.2 | async-start | bytes 22020096 | tf_op jit(solution)/shard_map/all_gather | solution.py:419
  156.1 2.0 copy-start.1
  241.2 43.7 %all-to-all-start.1 = ((bf16[16,336,128]{2,1,0:T(8,128)(2,1)}), bf16[16,336,128]{2,1,0:T(8,128)(2,1)}, u32[]{:S(2)}, u32[]{:S(2)}) async-start(bf16[16,336,128]{2,1,0:T(8,128)(2,1)} %pack_rest.1), calls=%async_computation.1 | async-start | bytes 2752512 | tf_op jit(solution)/shard_map/all_to_all | solution.py:369
  274.6 5.5 %collective-permute-start.12 = (bf16[2048,512]{1,0:T(8,128)(2,1)}, bf16[2048,512]{1,0:T(8,128)(2,1)S(1)}, u32[]{:S(2)}, u32[]{:S(2)}) collective-permute-start(bf16[2048,512]{1,0:T(8,128)(2,1)} %hidden.1.own_h), channel_id=1, source_target_pairs={{0,1},{1,0},{2,3},{3,2},{4,5},{5,4},{6,7},{7,6},{8,9},{9,8},{10,11... | collective-permute-start | bytes 6291464 | tf_op jit(solution)/shard_map/ppermute | solution.py:366
  274.6 5.5 %copy-start.4 = (bf16[2048,512]{1,0:T(8,128)(2,1)S(1)}, bf16[2048,512]{1,0:T(8,128)(2,1)}, u32[]{:S(2)}) copy-start(bf16[2048,512]{1,0:T(8,128)(2,1)} %hidden.1.own_h) | copy-start | bytes 6291460
  276.5 3.5 collective-permute-start.13
  280.0 3.7 %copy-start.10 = (bf16[8,448,128]{2,1,0:T(8,128)(2,1)}, bf16[8,448,128]{2,1,0:T(8,128)(2,1)S(1)}, u32[]{:S(2)}) copy-start(bf16[8,448,128]{2,1,0:T(8,128)(2,1)S(1)} %collective-permute-done.13.other_ref) | copy-start | bytes 2752516
  280.0 3.7 %copy-start.7 = (bf16[2048,512]{1,0:T(8,128)(2,1)}, bf16[2048,512]{1,0:T(8,128)(2,1)S(1)}, u32[]{:S(2)}) copy-start(bf16[2048,512]{1,0:T(8,128)(2,1)S(1)} %collective-permute-done.12.other_h) | copy-start | bytes 6291460
  283.8 25.4 %collective-permute-start.15 = (bf16[1024,512]{1,0:T(8,128)(2,1)}, bf16[1024,512]{1,0:T(8,128)(2,1)S(1)}, u32[]{:S(2)}, u32[]{:S(2)}) collective-permute-start(bf16[1024,512]{1,0:T(8,128)(2,1)} %get-tuple-element.84), channel_id=1, source_target_pairs={{0,2},{2,0},{4,6},{6,4},{8,10},{10,8},{12,14},{14,12},{16,18},{18,... | collective-permute-start | bytes 3145736 | tf_op jit(solution)/shard_map/ppermute | solution.py:320
  284.4 25.1 %collective-permute-start.16 = (bf16[1024,512]{1,0:T(8,128)(2,1)}, bf16[1024,512]{1,0:T(8,128)(2,1)S(1)}, u32[]{:S(2)}, u32[]{:S(2)}) collective-permute-start(bf16[1024,512]{1,0:T(8,128)(2,1)} %get-tuple-element.85), channel_id=1, source_target_pairs={{0,4},{2,6},{4,0},{6,2},{8,12},{10,14},{12,8},{14,10},{16,20},{18,... | collective-permute-start | bytes 3145736 | tf_op jit(solution)/shard_map/ppermute | solution.py:320
  284.9 8.9 %copy-start.6 = (bf16[2048,512]{1,0:T(8,128)(2,1)S(1)}, bf16[2048,512]{1,0:T(8,128)(2,1)}, u32[]{:S(2)}) copy-start(bf16[2048,512]{1,0:T(8,128)(2,1)} %hidden.1.own_h) | copy-start | bytes 6291460
  286.4 2.2 collective-permute-start.14
  288.6 1.6 copy-start.5
  290.2 1.6 copy-start.8
  291.8 1.9 copy-start.11
  309.5 18.0 %copy-start.9 = (bf16[2048,512]{1,0:T(8,128)(2,1)S(1)}, bf16[2048,512]{1,0:T(8,128)(2,1)}, u32[]{:S(2)}) copy-start(bf16[2048,512]{1,0:T(8,128)(2,1)} %copy-done.7) | copy-start | bytes 6291460
  309.9 14.9 %collective-permute-start.17 = (bf16[512,512]{1,0:T(8,128)(2,1)S(1)}, bf16[512,512]{1,0:T(8,128)(2,1)S(1)}, u32[]{:S(2)}, u32[]{:S(2)}) collective-permute-start(bf16[512,512]{1,0:T(8,128)(2,1)S(1)} %get-tuple-element.101), channel_id=1, source_target_pairs={{0,4},{2,6},{4,0},{6,2},{8,12},{10,14},{12,8},{14,10},{16,20},{18,... | collective-permute-start | bytes 1572872 | tf_op jit(solution)/shard_map/ppermute | solution.py:320
  310.4 14.9 %collective-permute-start.18 = (bf16[512,512]{1,0:T(8,128)(2,1)S(1)}, bf16[512,512]{1,0:T(8,128)(2,1)S(1)}, u32[]{:S(2)}, u32[]{:S(2)}) collective-permute-start(bf16[512,512]{1,0:T(8,128)(2,1)S(1)} %get-tuple-element.103), channel_id=1, source_target_pairs={{0,2},{2,0},{4,6},{6,4},{8,10},{10,8},{12,14},{14,12},{16,18},{18,... | collective-permute-start | bytes 1572872 | tf_op jit(solution)/shard_map/ppermute | solution.py:320
  311.9 22.3 %collective-permute-start.22 = (bf16[1024,256]{1,0:T(8,128)(2,1)S(1)}, bf16[1024,256]{1,0:T(8,128)(2,1)S(1)}, u32[]{:S(2)}, u32[]{:S(2)}) collective-permute-start(bf16[1024,256]{1,0:T(8,128)(2,1)S(1)} %get-tuple-element.91), channel_id=1, source_target_pairs={{0,2},{2,0},{4,6},{6,4},{8,10},{10,8},{12,14},{14,12},{16,18},{18,... | collective-permute-start | bytes 1572872 | tf_op jit(solution)/shard_map/ppermute | solution.py:320
  312.4 21.8 %collective-permute-start.23 = (bf16[1024,256]{1,0:T(8,128)(2,1)S(1)}, bf16[1024,256]{1,0:T(8,128)(2,1)S(1)}, u32[]{:S(2)}, u32[]{:S(2)}) collective-permute-start(bf16[1024,256]{1,0:T(8,128)(2,1)S(1)} %get-tuple-element.92), channel_id=1, source_target_pairs={{0,4},{2,6},{4,0},{6,2},{8,12},{10,14},{12,8},{14,10},{16,20},{18,... | collective-permute-start | bytes 1572872 | tf_op jit(solution)/shard_map/ppermute | solution.py:320
  314.0 20.2 %collective-permute-start.24 = (bf16[1024,256]{1,0:T(8,128)(2,1)S(1)}, bf16[1024,256]{1,0:T(8,128)(2,1)S(1)}, u32[]{:S(2)}, u32[]{:S(2)}) collective-permute-start(bf16[1024,256]{1,0:T(8,128)(2,1)S(1)} %get-tuple-element.93), channel_id=1, source_target_pairs={{0,8},{2,10},{4,12},{6,14},{8,0},{10,2},{12,4},{14,6},{16,24},{18,... | collective-permute-start | bytes 1572872 | tf_op jit(solution)/shard_map/ppermute | solution.py:320
  325.5 12.6 %collective-permute-start.19 = (bf16[256,512]{1,0:T(8,128)(2,1)S(1)}, bf16[256,512]{1,0:T(8,128)(2,1)S(1)}, u32[]{:S(2)}, u32[]{:S(2)}) collective-permute-start(bf16[256,512]{1,0:T(8,128)(2,1)S(1)} %get-tuple-element.105), channel_id=1, source_target_pairs={{0,8},{2,10},{4,12},{6,14},{8,0},{10,2},{12,4},{14,6},{16,24},{18,... | collective-permute-start | bytes 786440 | tf_op jit(solution)/shard_map/ppermute | solution.py:320
  325.9 12.1 %collective-permute-start.20 = (bf16[256,512]{1,0:T(8,128)(2,1)S(1)}, bf16[256,512]{1,0:T(8,128)(2,1)S(1)}, u32[]{:S(2)}, u32[]{:S(2)}) collective-permute-start(bf16[256,512]{1,0:T(8,128)(2,1)S(1)} %get-tuple-element.107), channel_id=1, source_target_pairs={{0,8},{2,10},{4,12},{6,14},{8,0},{10,2},{12,4},{14,6},{16,24},{18,... | collective-permute-start | bytes 786440 | tf_op jit(solution)/shard_map/ppermute | solution.py:320
  334.5 6.4 %collective-permute-start.25 = (bf16[512,256]{1,0:T(8,128)(2,1)S(1)}, bf16[512,256]{1,0:T(8,128)(2,1)S(1)}, u32[]{:S(2)}, u32[]{:S(2)}) collective-permute-start(bf16[512,256]{1,0:T(8,128)(2,1)S(1)} %get-tuple-element.118), channel_id=1, source_target_pairs={{0,4},{2,6},{4,0},{6,2},{8,12},{10,14},{12,8},{14,10},{16,20},{18,... | collective-permute-start | bytes 786440 | tf_op jit(solution)/shard_map/ppermute | solution.py:320
  336.1 10.2 %collective-permute-start.26 = (bf16[512,256]{1,0:T(8,128)(2,1)S(1)}, bf16[512,256]{1,0:T(8,128)(2,1)S(1)}, u32[]{:S(2)}, u32[]{:S(2)}) collective-permute-start(bf16[512,256]{1,0:T(8,128)(2,1)S(1)} %get-tuple-element.120), channel_id=1, source_target_pairs={{0,8},{2,10},{4,12},{6,14},{8,0},{10,2},{12,4},{14,6},{16,24},{18,... | collective-permute-start | bytes 786440 | tf_op jit(solution)/shard_map/ppermute | solution.py:320
  336.6 9.7 %collective-permute-start.27 = (bf16[512,256]{1,0:T(8,128)(2,1)S(1)}, bf16[512,256]{1,0:T(8,128)(2,1)S(1)}, u32[]{:S(2)}, u32[]{:S(2)}) collective-permute-start(bf16[512,256]{1,0:T(8,128)(2,1)S(1)} %get-tuple-element.122), channel_id=1, source_target_pairs={{0,2},{2,0},{4,6},{6,4},{8,10},{10,8},{12,14},{14,12},{16,18},{18,... | collective-permute-start | bytes 786440 | tf_op jit(solution)/shard_map/ppermute | solution.py:320
  338.1 19.1 %collective-permute-start.21 = (bf16[128,1024]{1,0:T(8,128)(2,1)S(1)}, bf16[128,1024]{1,0:T(8,128)(2,1)S(1)}, u32[]{:S(2)}, u32[]{:S(2)}) collective-permute-start(bf16[128,1024]{1,0:T(8,128)(2,1)S(1)} %get-tuple-element.109), channel_id=1, source_target_pairs={{0,16},{2,18},{4,20},{6,22},{8,24},{10,26},{12,28},{14,30},{16,0},... | collective-permute-start | bytes 786440 | tf_op jit(solution)/shard_map/ppermute | solution.py:320
  346.4 5.5 %collective-permute-start.28 = (bf16[256,256]{1,0:T(8,128)(2,1)S(1)}, bf16[256,256]{1,0:T(8,128)(2,1)S(1)}, u32[]{:S(2)}, u32[]{:S(2)}) collective-permute-start(bf16[256,256]{1,0:T(8,128)(2,1)S(1)} %get-tuple-element.124), channel_id=1, source_target_pairs={{0,8},{2,10},{4,12},{6,14},{8,0},{10,2},{12,4},{14,6},{16,24},{18,... | collective-permute-start | bytes 393224 | tf_op jit(solution)/shard_map/ppermute | solution.py:320
  349.0 5.0 %collective-permute-start.29 = (bf16[256,256]{1,0:T(8,128)(2,1)S(1)}, bf16[256,256]{1,0:T(8,128)(2,1)S(1)}, u32[]{:S(2)}, u32[]{:S(2)}) collective-permute-start(bf16[256,256]{1,0:T(8,128)(2,1)S(1)} %get-tuple-element.126), channel_id=1, source_target_pairs={{0,2},{2,0},{4,6},{6,4},{8,10},{10,8},{12,14},{14,12},{16,18},{18,... | collective-permute-start | bytes 393224 | tf_op jit(solution)/shard_map/ppermute | solution.py:320
  350.2 5.0 %collective-permute-start.30 = (bf16[256,256]{1,0:T(8,128)(2,1)S(1)}, bf16[256,256]{1,0:T(8,128)(2,1)S(1)}, u32[]{:S(2)}, u32[]{:S(2)}) collective-permute-start(bf16[256,256]{1,0:T(8,128)(2,1)S(1)} %get-tuple-element.128), channel_id=1, source_target_pairs={{0,4},{2,6},{4,0},{6,2},{8,12},{10,14},{12,8},{14,10},{16,20},{18,... | collective-permute-start | bytes 393224 | tf_op jit(solution)/shard_map/ppermute | solution.py:320
  355.3 7.3 %collective-permute-start.31 = (bf16[128,768]{1,0:T(8,128)(2,1)S(1)}, bf16[128,768]{1,0:T(8,128)(2,1)S(1)}, u32[]{:S(2)}, u32[]{:S(2)}) collective-permute-start(bf16[128,768]{1,0:T(8,128)(2,1)S(1)} %get-tuple-element.130), channel_id=1, source_target_pairs={{0,16},{2,18},{4,20},{6,22},{8,24},{10,26},{12,28},{14,30},{16,0},... | collective-permute-start | bytes 589832 | tf_op jit(solution)/shard_map/ppermute | solution.py:320
Sparse Core Ops, SparseCore 0:
  156.2 70.1 all-gather.2

commit v13 on v5

--- a/solution.py
+++ b/solution.py
@@ -147,45 +147,37 @@
     ).astype(out_ref.dtype)
 
 
-def hidden_kernel(at_ref, *refs):
-    pieces, (packed_ref, out_ref, gate_w, up_w, rows) = refs[:8], refs[8:]
+def hidden_kernel(at_ref, own_ref, other_ref, packed_ref, out_ref, gate_w, up_w):
+    rows, mid = own_ref.shape
     sources = packed_ref.shape[0]
     depth = gate_w.shape[0] // sources
     size = depth * 7 // 2
-    group = sources // 2
     tile = pl.program_id(0)
     x, y, zl = tile // 4, tile // 2 % 2, tile % 2
-    me, core = at_ref[0], at_ref[1]
 
     @pl.when(tile == 0)
     def _():
         for at in range(sources):
-            place = (core + at // group) % 2 * group + at % group
+            place = at_ref[1] * (sources // 2) ^ at
             unpack_rows(packed_ref, place, 0, depth, gate_w, at * depth, 0)
             unpack_rows(packed_ref, place, size, depth, up_w, at * depth, 0)
 
-    mid = pieces[0].shape[1]
-    for number in range(4):
-        lanes = slice(number * mid, (number + 1) * mid)
-        coordinate = (x, y)[number % 2]
-        for value in range(2):
-
-            @pl.when(coordinate == value)
-            def _():
-                rows[:, lanes] = pieces[2 * number + value][...]
-
-    gate = jnp.dot(rows[...], gate_w[...], preferred_element_type=jnp.float32)
-    up = jnp.dot(rows[...], up_w[...], preferred_element_type=jnp.float32)
-    value = gate / (1.0 + jnp.exp(-gate)) * up
+    def product(w_ref):
+        return jnp.dot(
+            own_ref[...], w_ref[:mid, :], preferred_element_type=jnp.float32
+        ) + jnp.dot(other_ref[...], w_ref[mid:, :], preferred_element_type=jnp.float32)
+
+    gate = product(gate_w)
+    value = gate / (1.0 + jnp.exp(-gate)) * product(up_w)
 
     wide = gate.shape[1]
     term = lax.broadcasted_iota(jnp.int32, (16, wide), 0)
     lane = lax.broadcasted_iota(jnp.int32, (16, wide), 1)
     chosen = (term % 4 == lane // LANES) & (term < 12) & (lane < wide - HALF)
     chosen = jnp.where(chosen, 1.0, 0.0).astype(jnp.bfloat16)
-    block = rows.shape[0] // 2
+    block = rows // 2
     for zh in range(2):
-        source = me ^ (x + 2 * y + 4 * zl + 8 * zh)
+        source = at_ref[0] ^ (x + 2 * y + 4 * zl + 8 * zh)
         weight = lax.dot_general(
             packed_ref[source, packed_ref.shape[1] - 16 :, :],
             chosen,
@@ -196,36 +188,27 @@
         out_ref[span, :] = (value[span, :] * weight).astype(out_ref.dtype)
 
 
-def hidden_units(at, pieces, packed):
-    total = 2 * pieces[0].shape[0]
-    mid = pieces[0].shape[1]
+def hidden_units(at, own, other, packed):
+    total, mid = own.shape
     tile = total // 8
     wide = 4 * LANES
-    model = 4 * mid
-    by_x = [lambda i: (jnp.minimum(i, 3), 0), lambda i: (jnp.maximum(i - 4, 0), 0)]
-    by_y = [
-        lambda i: (i // 4 * 2 + jnp.where(i // 2 % 2 == 0, i % 2, 1), 0),
-        lambda i: (i // 4 * 2 + jnp.where(i // 2 % 2 == 1, i % 2, 0), 0),
-    ]
-    maps = (by_x + by_y) * 2
+    model = 2 * mid
     return pl.pallas_call(
         hidden_kernel,
         grid=(8,),
-        out_shape=jax.ShapeDtypeStruct((total, wide), packed.dtype),
-        in_specs=[smem()]
-        + [pl.BlockSpec((tile, mid), where) for where in maps]
-        + [vmem()],
+        out_shape=jax.ShapeDtypeStruct((total, wide), own.dtype),
+        in_specs=[smem()] + [pl.BlockSpec((tile, mid), lambda i: (i, 0))] * 2 + [vmem()],
         out_specs=pl.BlockSpec((tile, wide), lambda i: (i, 0)),
-        scratch_shapes=[pltpu.VMEM((model, wide), packed.dtype)] * 2
-        + [pltpu.VMEM((tile, model), packed.dtype)],
+        scratch_shapes=[pltpu.VMEM((model, wide), own.dtype)] * 2,
         compiler_params=pltpu.CompilerParams(vmem_limit_bytes=56 * MIB),
         cost_estimate=pl.CostEstimate(
             flops=4 * total * model * wide, bytes_accessed=24 * MIB, transcendentals=total * wide
         ),
         name="hidden",
-    )(at, *pieces, packed)
-
-
+    )(at, own, other, packed)
+
+
+HALVES = ((0, 1, 2), (1, 0, 2))
 THIRDS = ((0, 1, 2), (1, 2, 0), (2, 0, 1))
 
 
@@ -392,26 +375,59 @@
     belongs = slot_place[None, None, :, None] == places[:, :, None, None]
     share = jnp.sum(jnp.where(belongs, share[None, None], 0.0), axis=2)
 
+    def diagonal(value):
+        return lax.ppermute(value, "ep", [(i, i ^ 3) for i in range(devices)])
+
+    mid = tokens.shape[1] // 2
     near, far = swap(tokens, 2), swap(tokens, 3)
-    corner = swap(far, 2)
+    x_own, y_own = swap(tokens, 0), swap(tokens, 1)
     parts = (128, 96)
     packed = pack_first(listing, gate_proj, up_proj, down_proj, parts[0], share, devices)
-    packed, near, far, corner = tie((packed, near, far, corner))
+    far, packed = tie((far, packed))
+    corner = swap(far, 2)
+    pair = jnp.concatenate([far, near], axis=0)
+    pair_y, pair_x = swap(pair[:, :mid], 1), swap(pair[:, mid:], 0)
+    packed, x_own, y_own, pair, corner, pair_y, pair_x = tie(
+        (packed, x_own, y_own, pair, corner, pair_y, pair_x)
+    )
 
     moved = move(packed)
-    mid = tokens.shape[1] // 2
-    rows = jnp.concatenate([tokens, far, near, corner], axis=0)
-    first, second = rows[:, :mid], rows[:, mid:]
-    first = jnp.concatenate([first, swap(first, 1)], axis=0)
-    second = jnp.concatenate([second, swap(second, 0)], axis=0)
-    pieces = [first, swap(first, 0), second, swap(second, 1)]
-    others = [exchange(piece) for piece in pieces]
+    corner_a, corner_b = corner[:, :mid], corner[:, mid:]
+    cross = diagonal(jnp.concatenate([tokens, corner], axis=0))
+    most_a = swap(jnp.concatenate([pair[:, :mid], corner_a, pair_y], axis=0), 0)
+    most_b = swap(jnp.concatenate([pair[:, mid:], corner_b, pair_x], axis=0), 1)
+    corner_y, corner_x = swap(corner_a, 1), swap(corner_b, 0)
+
+    def lay(*values):
+        return jnp.concatenate(values, axis=0)
+
+    three, two = slice(0, 3 * block), slice(3 * block, 5 * block)
+    top, low = slice(0, block), slice(block, 2 * block)
+    first, second = slice(0, mid), slice(mid, 2 * mid)
+    rows = jnp.concatenate(
+        [
+            lay(
+                tokens[:, first], pair[:, first], corner_a,
+                y_own[:, first], pair_y, corner_y,
+                x_own[:, first], most_a[three],
+                cross[top, first], most_a[two], cross[low, first],
+            ),
+            lay(
+                tokens[:, second], pair[:, second], corner_b,
+                y_own[:, second], most_b[three],
+                x_own[:, second], pair_x, corner_x,
+                cross[top, second], most_b[two], cross[low, second],
+            ),
+        ],
+        axis=1,
+    )
+    rows_other = exchange(rows)
     rest = pack_rest(listing, down_proj, parts[0], devices)
-    moved, rest = tie((moved, rest))
+    moved, rest, rows, rows_other = tie((moved, rest, rows, rows_other))
 
     down1 = move(rest)
     at = jnp.stack([me, core]).astype(jnp.int32)
-    hidden = hidden_units(at, pieces + others, moved)
+    hidden = hidden_units(at, rows, rows_other, moved)
     hidden_other = exchange(hidden)
     down0 = moved[:, depth * 7 : depth * 7 + parts[0] * 7 // 2]
 
@@ -423,7 +439,7 @@
         sent, args = tie((sent, args))
         come = [swap(value, order[0]) for value, order in zip(sent, orders)]
         kept = down_product(*args, rows_in, 0, orders, jnp.float32, "down_keep")
-        return kept, come, sent
+        return kept, come
 
     def stage(kept, come, number, orders):
         axes = tuple(stage_axis(order, number) for order in orders)
@@ -436,13 +452,12 @@
         come = swap(send, 3)
         return (keep + come.astype(jnp.float32)).astype(jnp.bfloat16)
 
-    kept0, come0, _ = products(down0, parts[0], THIRDS)
+    kept0, come0 = products(down0, parts[0], HALVES)
     down1, kept0 = tie((down1, kept0))
-    kept1, come1, sent1 = products(down1, parts[1], THIRDS)
-    kept0, _ = tie((kept0, sent1))
-    kept0, come0 = stage(kept0, come0, 1, THIRDS)
+    kept1, come1 = products(down1, parts[1], THIRDS)
+    kept0, come0 = stage(kept0, come0, 1, HALVES)
     kept1, come1 = stage(kept1, come1, 1, THIRDS)
-    kept0, come0 = stage(kept0, come0, 2, THIRDS)
+    kept0, come0 = stage(kept0, come0, 2, HALVES)
     kept1, come1 = stage(kept1, come1, 2, THIRDS)
     out = []
     for rows_in, total in zip(parts, (last_stage(kept0, come0), last_stage(kept1, come1))):

time: 359 us -> 357 us (level)
  waiting for transfers between devices: 235 us -> 218 us
  local copies, waits for them, and re-layouts: 19.8 us -> 28 us
  other arithmetic: 6.13 us -> 11.4 us
  starting transfers between devices: 49.5 us -> 54 us
    ppermute x27 -> x28, waiting for transfers between devices: 198 us -> 153 us  [swap(): return lax.ppermute(value, 'ep', [(i, i ^ 1 << bit) for i in range(size)])]
    all_to_all x2, waiting for transfers between devices: 33.9 us -> 44.9 us  [move(): return lax.all_to_all(packed, 'ep', 0, 0, tiled=True)]
    ppermute x0 -> x1, waiting for transfers between devices: none -> 9.18 us  [diagonal(): return lax.ppermute(value, 'ep', [(i, i ^ 3) for i in range(devices)])]
    ppermute x7 -> x4, waiting for transfers between devices: 3.84 us -> 10.4 us  [exchange(): return lax.ppermute(value, 'et', [(0, 1), (1, 0)])]
    unnamed x39 -> x40, local copies, waits for them, and re-layouts: 15 us -> 20.4 us
    concatenate x2 -> x4, other arithmetic: 1.55 us -> 6.81 us  [the longest x1 6.57 us: packed_layer(): jnp.concatenate([lay(tokens[:, first], pair[:, first], corner_a, y_own[:,...]
    ppermute x27 -> x28, starting transfers between devices: 30.2 us -> 34.1 us  [swap(): return lax.ppermute(value, 'ep', [(i, i ^ 1 << bit) for i in range(size)])]
  transfers between devices with their start and end apart: 36 -> 35, of which waited for: 21 -> 20; matrix products, arithmetic and copies ran while one was open for 2% -> 8% of each run, Pallas kernels for 12% -> 12%
where the time goes in v13:
time: 357 us; the launch traced here: 354 us
  waiting for transfers between devices  218 us (61%)
  starting transfers between devices  54 us (15%)
  Pallas kernels  42.8 us (12%)
  local copies, waits for them, and re-layouts  28 us (8%)
  other arithmetic  11.4 us (3%)
    ppermute x28, waiting for transfers between devices, swap(): return lax.ppermute(value, 'ep', [(i, i ^ 1 << bit) for i in range(size)])  153 us
    all_to_all x2, waiting for transfers between devices, move(): return lax.all_to_all(packed, 'ep', 0, 0, tiled=True)  44.9 us
    ppermute x28, starting transfers between devices, swap(): return lax.ppermute(value, 'ep', [(i, i ^ 1 << bit) for i in range(size)])  34.1 us
    pallas_call x1, Pallas kernels, hidden_units(): pl.pallas_call(hidden_kernel, grid=(8,), out_shape=jax.ShapeDtypeStruct((...  23.3 us
    unnamed x40, local copies, waits for them, and re-layouts  20.4 us
    all_to_all x2, starting transfers between devices, move(): return lax.all_to_all(packed, 'ep', 0, 0, tiled=True)  18.6 us
    ppermute x4, waiting for transfers between devices, exchange(): return lax.ppermute(value, 'et', [(0, 1), (1, 0)])  10.4 us
    pallas_call x4, Pallas kernels, down_product(): pl.pallas_call(functools.partial(down_kernel, rows, side, orders), out_sh...  10 us
  transfers between devices with their start and end apart: 35, of which 20 were waited for; matrix products, arithmetic and copies ran while one was open for 8% of the time, Pallas kernels for 12%

profile of v13, /device:TPU:14, one launch (start us, length us, event | category | flops | bytes accessed | tf_op | source)
XLA Modules:
  0.0 354.3 jit_solution(12017816498423344727)
XLA Ops:
  0.0 2.6 collective-permute-start
  4.1 0.9 select_reduce_fusion.4
  6.1 0.8 broadcast_compare_fusion
  7.0 0.9 select_reduce_fusion.share_ref
  7.9 2.0 copy-done
  10.0 2.0 copy-done.2
  12.0 2.0 copy-done.3
  14.0 5.4 %pack_first.1 = bf16[16,2032,128]{2,1,0:T(8,128)(2,1)} custom-call(s32[14]{0:T(128)S(1)} %select_reduce_fusion.3.list_ref, bf16[16,224,512]{2,1,0:T(8,128)(2,1)S(1)} %copy-done.2, bf16[16,224,512]{2,1,0:T(8,128)(2,1)S(1)} %copy-done.3, bf16[16,224,512]{2,1,0:T(8,128)(2,1)S(1)} %copy-done, f32[16,16,128]{2,1,0:T(8,128)S(1)} %select_reduce_fusion.share_ref), custom_call_target="tpu_custom_call" | custom-call | tf_op jit(solution)/shard_map/pack_first/pallas_call | solution.py:113
  19.4 3.0 collective-permute-done
  22.4 1.4 collective-permute-start.4
  24.5 1.5 collective-permute-start.6
  26.0 8.9 %collective-permute-done.4 = bf16[128,1792]{1,0:T(8,128)(2,1)S(1)} collective-permute-done((bf16[128,1792]{1,0:T(8,128)(2,1)S(1)}, bf16[128,1792]{1,0:T(8,128)(2,1)S(1)}, u32[]{:S(2)}, u32[]{:S(2)}) %collective-permute-start.4) | collective-permute-done | bytes 458784 | tf_op jit(solution)/shard_map/ppermute | solution.py:318
  35.4 8.1 %all-to-all-start = ((bf16[16,2032,128]{2,1,0:T(8,128)(2,1)}), bf16[16,2032,128]{2,1,0:T(8,128)(2,1)}, u32[]{:S(2)}, u32[]{:S(2)}) async-start(bf16[16,2032,128]{2,1,0:T(8,128)(2,1)} %pack_first.1), calls=%async_computation | async-start | bytes 16646144 | tf_op jit(solution)/shard_map/all_to_all | solution.py:367
  43.5 0.8 slice_dynamic-update-slice_fusion.13
  44.3 1.1 fusion.3
  45.4 0.9 fusion.5
  47.6 1.5 collective-permute-start.7
  49.1 1.5 collective-permute-start.8
  51.4 0.8 slice_dynamic-update-slice_fusion.12
  52.2 0.8 constant_dynamic-update-slice_fusion.3
  53.0 94.7 %collective-permute-done.7 = bf16[128,896]{1,0:T(8,128)(2,1)S(1)} collective-permute-done((bf16[128,896]{1,0:T(8,128)(2,1)S(1)}, bf16[128,896]{1,0:T(8,128)(2,1)S(1)}, u32[]{:S(2)}, u32[]{:S(2)}) %collective-permute-start.7) | collective-permute-done | bytes 229408 | tf_op jit(solution)/shard_map/ppermute | solution.py:318
  148.5 1.0 slice_dynamic-update-slice_fusion
  149.4 0.8 slice_dynamic-update-slice_fusion.11
  150.2 0.8 constant_dynamic-update-slice_fusion.7
  151.7 1.4 collective-permute-done.8
  153.1 0.9 slice_dynamic-update-slice_fusion.1
  154.0 9.2 %collective-permute-done.9 = bf16[256,1792]{1,0:T(8,128)(2,1)S(1)} collective-permute-done((bf16[256,1792]{1,0:T(8,128)(2,1)S(1)}, bf16[256,1792]{1,0:T(8,128)(2,1)S(1)}, u32[]{:S(2)}, u32[]{:S(2)}) %collective-permute-start.9) | collective-permute-done | bytes 917536 | tf_op jit(solution)/shard_map/ppermute | solution.py:379
  163.2 0.8 slice_dynamic-update-slice_fusion.7
  164.0 1.1 slice_dynamic-update-slice_fusion.2
  165.1 0.8 slice_dynamic-update-slice_fusion.6
  165.9 6.6 %pad_maximum_fusion.own_ref = bf16[2048,1792]{1,0:T(8,128)(2,1)} fusion(bf16[2048,896]{1,0:T(8,128)(2,1)} %get-tuple-element.136, bf16[2048,896]{1,0:T(8,128)(2,1)} %get-tuple-element.135), kind=kLoop, calls=%fused_computation | loop fusion | flops 14680064 | bytes 14680064 | tf_op jit(solution)/shard_map/concatenate | solution.py:407
  172.4 2.0 copy-done.1
  174.5 1.9 pack_rest.1
  177.0 7.4 %collective-permute-done.12.other_ref = bf16[2048,1792]{1,0:T(8,128)(2,1)} collective-permute-done((bf16[2048,1792]{1,0:T(8,128)(2,1)}, bf16[2048,1792]{1,0:T(8,128)(2,1)}, u32[]{:S(2)}, u32[]{:S(2)}) %collective-permute-start.12) | collective-permute-done | bytes 7340064 | tf_op jit(solution)/shard_map/ppermute | solution.py:364
  184.4 44.9 %all-to-all-done.packed_ref = bf16[16,2032,128]{2,1,0:T(8,128)(2,1)} async-done(((bf16[16,2032,128]{2,1,0:T(8,128)(2,1)}), bf16[16,2032,128]{2,1,0:T(8,128)(2,1)}, u32[]{:S(2)}, u32[]{:S(2)}) %all-to-all-start) | async-done | bytes 8323104 | tf_op jit(solution)/shard_map/all_to_all | solution.py:367
  229.4 10.5 %all-to-all-start.1 = ((bf16[16,336,128]{2,1,0:T(8,128)(2,1)}), bf16[16,336,128]{2,1,0:T(8,128)(2,1)}, u32[]{:S(2)}, u32[]{:S(2)}) async-start(bf16[16,336,128]{2,1,0:T(8,128)(2,1)} %pack_rest.1), calls=%async_computation.1 | async-start | bytes 2752512 | tf_op jit(solution)/shard_map/all_to_all | solution.py:367
  239.9 23.3 %hidden.1.own_h = bf16[2048,512]{1,0:T(8,128)(2,1)} custom-call(s32[2]{0:T(128)} %pad_add_fusion.at_ref, bf16[2048,1792]{1,0:T(8,128)(2,1)} %pad_maximum_fusion.own_ref, bf16[2048,1792]{1,0:T(8,128)(2,1)} %collective-permute-done.12.other_ref, bf16[16,2032,128]{2,1,0:T(8,128)(2,1)} %all-to-all-done.packed_ref), custom_call_target="tpu_custom_call" | custom-call | flops 15032385536 | bytes 25165824 | tf_op jit(solution)/shard_map/hidden/pallas_call | solution.py:196
  263.2 1.8 slice.85
  265.7 3.0 collective-permute-done.14.other_ref
  268.7 3.7 %down_send.2 = (bf16[1024,512]{1,0:T(8,128)(2,1)}, bf16[1024,512]{1,0:T(8,128)(2,1)}) custom-call(bf16[2048,512]{1,0:T(8,128)(2,1)S(1)} %copy-done.6, bf16[2048,512]{1,0:T(8,128)(2,1)S(1)} %collective-permute-done.13.other_h, bf16[8,448,128]{2,1,0:T(8,128)(2,1)S(1)} %get-tuple-element.85.own_ref, bf16[8,448,128]{2,1,0:T(8,128)(2,1)S(1)} %collective-permute-done.14.other_ref), custom_call_target="tpu_custom_call" | custom-call | flops 2147483648 | bytes 8388608 | tf_op jit(solution)/shard_map/down_send/pallas_call | solution.py:258
  273.5 1.6 copy-done.9
  275.1 2.5 down_keep.2
  277.6 1.3 copy-done.4
  278.9 1.5 constant_dynamic-slice_fusion
  280.6 17.2 %collective-permute-done.15.refs_1_ = bf16[1024,512]{1,0:T(8,128)(2,1)S(1)} collective-permute-done((bf16[1024,512]{1,0:T(8,128)(2,1)}, bf16[1024,512]{1,0:T(8,128)(2,1)S(1)}, u32[]{:S(2)}, u32[]{:S(2)}) %collective-permute-start.15) | collective-permute-done | bytes 1048608 | tf_op jit(solution)/shard_map/ppermute | solution.py:318
  298.2 1.6 sum_stage.6
  300.3 1.5 collective-permute-start.18
  301.8 1.9 down_send.3
  304.4 1.5 collective-permute-start.24
  306.4 8.2 %collective-permute-done.17.refs_1_ = bf16[512,512]{1,0:T(8,128)(2,1)S(1)} collective-permute-done((bf16[512,512]{1,0:T(8,128)(2,1)S(1)}, bf16[512,512]{1,0:T(8,128)(2,1)S(1)}, u32[]{:S(2)}, u32[]{:S(2)}) %collective-permute-start.17) | collective-permute-done | bytes 524320 | tf_op jit(solution)/shard_map/ppermute | solution.py:318
  315.7 1.7 collective-permute-start.20
  317.5 1.9 down_keep.3
  319.4 4.8 %collective-permute-done.23.refs_1_ = bf16[1024,256]{1,0:T(8,128)(2,1)S(1)} collective-permute-done((bf16[1024,256]{1,0:T(8,128)(2,1)S(1)}, bf16[1024,256]{1,0:T(8,128)(2,1)S(1)}, u32[]{:S(2)}, u32[]{:S(2)}) %collective-permute-start.23) | collective-permute-done | bytes 524320 | tf_op jit(solution)/shard_map/ppermute | solution.py:318
  324.4 1.5 collective-permute-start.26
  326.5 1.4 collective-permute-start.28
  327.9 4.4 %collective-permute-done.20.refs_3_ = bf16[256,512]{1,0:T(8,128)(2,1)S(1)} collective-permute-done((bf16[256,512]{1,0:T(8,128)(2,1)S(1)}, bf16[256,512]{1,0:T(8,128)(2,1)S(1)}, u32[]{:S(2)}, u32[]{:S(2)}) %collective-permute-start.20) | collective-permute-done | bytes 262176 | tf_op jit(solution)/shard_map/ppermute | solution.py:318
  332.4 4.4 %collective-permute-start.21 = (bf16[128,1024]{1,0:T(8,128)(2,1)S(1)}, bf16[128,1024]{1,0:T(8,128)(2,1)S(1)}, u32[]{:S(2)}, u32[]{:S(2)}) collective-permute-start(bf16[128,1024]{1,0:T(8,128)(2,1)S(1)} %get-tuple-element.102), channel_id=1, source_target_pairs={{0,16},{2,18},{4,20},{6,22},{8,24},{10,26},{12,28},{14,30},{16,0},... | collective-permute-start | bytes 786440 | tf_op jit(solution)/shard_map/ppermute | solution.py:318
  337.2 0.8 collective-permute-start.29
  338.0 1.4 collective-permute-start.30
  340.0 2.9 collective-permute-done.29.refs_1_
  342.9 1.4 collective-permute-done.31.refs_5_
  344.4 3.9 %collective-permute-start.32 = (bf16[128,768]{1,0:T(8,128)(2,1)S(1)}, bf16[128,768]{1,0:T(8,128)(2,1)S(1)}, u32[]{:S(2)}, u32[]{:S(2)}) collective-permute-start(bf16[128,768]{1,0:T(8,128)(2,1)S(1)} %get-tuple-element.130), channel_id=1, source_target_pairs={{0,16},{2,18},{4,20},{6,22},{8,24},{10,26},{12,28},{14,30},{16,0},... | collective-permute-start | bytes 589832 | tf_op jit(solution)/shard_map/ppermute | solution.py:318
  348.6 4.5 %collective-permute-done.32 = bf16[128,768]{1,0:T(8,128)(2,1)S(1)} collective-permute-done((bf16[128,768]{1,0:T(8,128)(2,1)S(1)}, bf16[128,768]{1,0:T(8,128)(2,1)S(1)}, u32[]{:S(2)}, u32[]{:S(2)}) %collective-permute-start.32) | collective-permute-done | bytes 196640 | tf_op jit(solution)/shard_map/ppermute | solution.py:318
  353.3 1.0 copy.15
  (86 shorter events, 15.7 us)
Async XLA Ops:
  0.0 22.4 %collective-permute-start = (bf16[128,1792]{1,0:T(8,128)(2,1)}, bf16[128,1792]{1,0:T(8,128)(2,1)S(1)}, u32[]{:S(2)}, u32[]{:S(2)}) collective-permute-start(bf16[128,1792]{1,0:T(8,128)(2,1)} %param.9), channel_id=1, source_target_pairs={{0,16},{2,18},{4,20},{6,22},{8,24},{10,26},{12,28},{14,30},{16,0},... | collective-permute-start | bytes 1376264 | tf_op jit(solution)/shard_map/ppermute | solution.py:318
  2.6 23.4 %collective-permute-start.1 = (bf16[128,1792]{1,0:T(8,128)(2,1)}, bf16[128,1792]{1,0:T(8,128)(2,1)S(1)}, u32[]{:S(2)}, u32[]{:S(2)}) collective-permute-start(bf16[128,1792]{1,0:T(8,128)(2,1)} %param.9), channel_id=1, source_target_pairs={{0,2},{2,0},{4,6},{6,4},{8,10},{10,8},{12,14},{14,12},{16,18},{18,... | collective-permute-start | bytes 1376264 | tf_op jit(solution)/shard_map/ppermute | solution.py:318
  3.1 22.8 %collective-permute-start.2 = (bf16[128,1792]{1,0:T(8,128)(2,1)}, bf16[128,1792]{1,0:T(8,128)(2,1)S(1)}, u32[]{:S(2)}, u32[]{:S(2)}) collective-permute-start(bf16[128,1792]{1,0:T(8,128)(2,1)} %param.9), channel_id=1, source_target_pairs={{0,4},{2,6},{4,0},{6,2},{8,12},{10,14},{12,8},{14,10},{16,20},{18,... | collective-permute-start | bytes 1376264 | tf_op jit(solution)/shard_map/ppermute | solution.py:318
  3.6 20.2 %collective-permute-start.3 = (bf16[128,1792]{1,0:T(8,128)(2,1)}, bf16[128,1792]{1,0:T(8,128)(2,1)S(1)}, u32[]{:S(2)}, u32[]{:S(2)}) collective-permute-start(bf16[128,1792]{1,0:T(8,128)(2,1)} %param.9), channel_id=1, source_target_pairs={{0,8},{2,10},{4,12},{6,14},{8,0},{10,2},{12,4},{14,6},{16,24},{18,... | collective-permute-start | bytes 1376264 | tf_op jit(solution)/shard_map/ppermute | solution.py:318
  7.9 2.0 copy-start
  10.0 2.0 copy-start.2
  12.0 2.0 copy-start.3
  22.4 12.4 %collective-permute-start.4 = (bf16[128,1792]{1,0:T(8,128)(2,1)S(1)}, bf16[128,1792]{1,0:T(8,128)(2,1)S(1)}, u32[]{:S(2)}, u32[]{:S(2)}) collective-permute-start(bf16[128,1792]{1,0:T(8,128)(2,1)S(1)} %collective-permute-done), channel_id=1, source_target_pairs={{0,8},{2,10},{4,12},{6,14},{8,0},{10,2},{12,4},{14,6},{16,24},{18,... | collective-permute-start | bytes 1376264 | tf_op jit(solution)/shard_map/ppermute | solution.py:318
  23.9 11.2 %collective-permute-start.5 = (bf16[256,896]{1,0:T(8,128)(2,1)S(1)}, bf16[256,896]{1,0:T(8,128)(2,1)S(1)}, u32[]{:S(2)}, u32[]{:S(2)}) collective-permute-start(bf16[256,896]{1,0:T(8,128)(2,1)S(1)} %get-tuple-element.144), channel_id=1, source_target_pairs={{0,4},{2,6},{4,0},{6,2},{8,12},{10,14},{12,8},{14,10},{16,20},{18,... | collective-permute-start | bytes 1376264 | tf_op jit(solution)/shard_map/ppermute | solution.py:318
  24.5 19.0 %copy-start.11 = (bf16[128,1792]{1,0:T(8,128)(2,1)S(1)}, bf16[128,1792]{1,0:T(8,128)(2,1)}, u32[]{:S(2)}) copy-start(bf16[128,1792]{1,0:T(8,128)(2,1)} %param.9) | copy-start | bytes 1376260
  24.5 10.9 %collective-permute-start.6 = (bf16[256,896]{1,0:T(8,128)(2,1)S(1)}, bf16[256,896]{1,0:T(8,128)(2,1)S(1)}, u32[]{:S(2)}, u32[]{:S(2)}) collective-permute-start(bf16[256,896]{1,0:T(8,128)(2,1)S(1)} %get-tuple-element.143), channel_id=1, source_target_pairs={{0,2},{2,0},{4,6},{6,4},{8,10},{10,8},{12,14},{14,12},{16,18},{18,... | collective-permute-start | bytes 1376264 | tf_op jit(solution)/shard_map/ppermute | solution.py:318
  26.0 9.1 %copy-start.12 = (bf16[128,1792]{1,0:T(8,128)(2,1)}, bf16[128,1792]{1,0:T(8,128)(2,1)S(1)}, u32[]{:S(2)}) copy-start(bf16[128,1792]{1,0:T(8,128)(2,1)S(1)} %collective-permute-done.2) | copy-start | bytes 1376260
  35.4 194.0 %all-to-all-start = ((bf16[16,2032,128]{2,1,0:T(8,128)(2,1)}), bf16[16,2032,128]{2,1,0:T(8,128)(2,1)}, u32[]{:S(2)}, u32[]{:S(2)}) async-start(bf16[16,2032,128]{2,1,0:T(8,128)(2,1)} %pack_first.1), calls=%async_computation | async-start | bytes 16646144 | tf_op jit(solution)/shard_map/all_to_all | solution.py:367
  45.4 5.9 %copy-start.13 = (bf16[128,1792]{1,0:T(8,128)(2,1)S(1)}, bf16[128,1792]{1,0:T(8,128)(2,1)}, u32[]{:S(2)}) copy-start(bf16[128,1792]{1,0:T(8,128)(2,1)} %copy-done.12) | copy-start | bytes 1376260
  46.4 102.1 %collective-permute-start.10 = (bf16[640,896]{1,0:T(8,128)(2,1)S(1)}, bf16[640,896]{1,0:T(8,128)(2,1)S(1)}, u32[]{:S(2)}, u32[]{:S(2)}) collective-permute-start(bf16[640,896]{1,0:T(8,128)(2,1)S(1)} %pad_maximum_fusion.2), channel_id=1, source_target_pairs={{0,4},{2,6},{4,0},{6,2},{8,12},{10,14},{12,8},{14,10},{16,20},{18,... | collective-permute-start | bytes 3440648 | tf_op jit(solution)/shard_map/ppermute | solution.py:318
  47.0 104.0 %collective-permute-start.11 = (bf16[128,896]{1,0:T(8,128)(2,1)S(1)}, bf16[128,896]{1,0:T(8,128)(2,1)S(1)}, u32[]{:S(2)}, u32[]{:S(2)}) collective-permute-start(bf16[128,896]{1,0:T(8,128)(2,1)S(1)} %get-tuple-element.150), channel_id=1, source_target_pairs={{0,2},{2,0},{4,6},{6,4},{8,10},{10,8},{12,14},{14,12},{16,18},{18,... | collective-permute-start | bytes 688136 | tf_op jit(solution)/shard_map/ppermute | solution.py:318
  47.6 100.2 %collective-permute-start.7 = (bf16[128,896]{1,0:T(8,128)(2,1)S(1)}, bf16[128,896]{1,0:T(8,128)(2,1)S(1)}, u32[]{:S(2)}, u32[]{:S(2)}) collective-permute-start(bf16[128,896]{1,0:T(8,128)(2,1)S(1)} %get-tuple-element.147), channel_id=1, source_target_pairs={{0,4},{2,6},{4,0},{6,2},{8,12},{10,14},{12,8},{14,10},{16,20},{18,... | collective-permute-start | bytes 688136 | tf_op jit(solution)/shard_map/ppermute | solution.py:318
  49.1 104.0 %collective-permute-start.8 = (bf16[640,896]{1,0:T(8,128)(2,1)S(1)}, bf16[640,896]{1,0:T(8,128)(2,1)S(1)}, u32[]{:S(2)}, u32[]{:S(2)}) collective-permute-start(bf16[640,896]{1,0:T(8,128)(2,1)S(1)} %pad_maximum_fusion.1), channel_id=1, source_target_pairs={{0,2},{2,0},{4,6},{6,4},{8,10},{10,8},{12,14},{14,12},{16,18},{18,... | collective-permute-start | bytes 3440648 | tf_op jit(solution)/shard_map/ppermute | solution.py:318
  50.7 112.5 %collective-permute-start.9 = (bf16[256,1792]{1,0:T(8,128)(2,1)S(1)}, bf16[256,1792]{1,0:T(8,128)(2,1)S(1)}, u32[]{:S(2)}, u32[]{:S(2)}) collective-permute-start(bf16[256,1792]{1,0:T(8,128)(2,1)S(1)} %pad_maximum_fusion.3), channel_id=1, source_target_pairs={{0,6},{2,4},{4,2},{6,0},{8,14},{10,12},{12,10},{14,8},{16,22},{18,... | collective-permute-start | bytes 2752520 | tf_op jit(solution)/shard_map/ppermute | solution.py:379
  172.4 12.0 %collective-permute-start.12 = (bf16[2048,1792]{1,0:T(8,128)(2,1)}, bf16[2048,1792]{1,0:T(8,128)(2,1)}, u32[]{:S(2)}, u32[]{:S(2)}) collective-permute-start(bf16[2048,1792]{1,0:T(8,128)(2,1)} %pad_maximum_fusion.own_ref), channel_id=1, source_target_pairs={{0,1},{1,0},{2,3},{3,2},{4,5},{5,4},{6,7},{7,6},{8,9},{9,8},{10,11... | collective-permute-start | bytes 22020104 | tf_op jit(solution)/shard_map/ppermute | solution.py:364
  172.4 2.0 copy-start.1
  229.4 49.6 %all-to-all-start.1 = ((bf16[16,336,128]{2,1,0:T(8,128)(2,1)}), bf16[16,336,128]{2,1,0:T(8,128)(2,1)}, u32[]{:S(2)}, u32[]{:S(2)}) async-start(bf16[16,336,128]{2,1,0:T(8,128)(2,1)} %pack_rest.1), calls=%async_computation.1 | async-start | bytes 2752512 | tf_op jit(solution)/shard_map/all_to_all | solution.py:367
  263.2 5.5 %collective-permute-start.13 = (bf16[2048,512]{1,0:T(8,128)(2,1)}, bf16[2048,512]{1,0:T(8,128)(2,1)S(1)}, u32[]{:S(2)}, u32[]{:S(2)}) collective-permute-start(bf16[2048,512]{1,0:T(8,128)(2,1)} %hidden.1.own_h), channel_id=1, source_target_pairs={{0,1},{1,0},{2,3},{3,2},{4,5},{5,4},{6,7},{7,6},{8,9},{9,8},{10,11... | collective-permute-start | bytes 6291464 | tf_op jit(solution)/shard_map/ppermute | solution.py:364
  263.2 5.5 %copy-start.6 = (bf16[2048,512]{1,0:T(8,128)(2,1)S(1)}, bf16[2048,512]{1,0:T(8,128)(2,1)}, u32[]{:S(2)}) copy-start(bf16[2048,512]{1,0:T(8,128)(2,1)} %hidden.1.own_h) | copy-start | bytes 6291460
  265.1 3.5 collective-permute-start.14
  268.7 3.7 %copy-start.8 = (bf16[2048,512]{1,0:T(8,128)(2,1)}, bf16[2048,512]{1,0:T(8,128)(2,1)S(1)}, u32[]{:S(2)}) copy-start(bf16[2048,512]{1,0:T(8,128)(2,1)S(1)} %collective-permute-done.13.other_h) | copy-start | bytes 6291460
  272.4 25.4 %collective-permute-start.15 = (bf16[1024,512]{1,0:T(8,128)(2,1)}, bf16[1024,512]{1,0:T(8,128)(2,1)S(1)}, u32[]{:S(2)}, u32[]{:S(2)}) collective-permute-start(bf16[1024,512]{1,0:T(8,128)(2,1)} %get-tuple-element.90), channel_id=1, source_target_pairs={{0,2},{2,0},{4,6},{6,4},{8,10},{10,8},{12,14},{14,12},{16,18},{18,... | collective-permute-start | bytes 3145736 | tf_op jit(solution)/shard_map/ppermute | solution.py:318
  272.9 25.2 %collective-permute-start.16 = (bf16[1024,512]{1,0:T(8,128)(2,1)}, bf16[1024,512]{1,0:T(8,128)(2,1)}, u32[]{:S(2)}, u32[]{:S(2)}) collective-permute-start(bf16[1024,512]{1,0:T(8,128)(2,1)} %get-tuple-element.92), channel_id=1, source_target_pairs={{0,4},{2,6},{4,0},{6,2},{8,12},{10,14},{12,8},{14,10},{16,20},{18,... | collective-permute-start | bytes 3145736 | tf_op jit(solution)/shard_map/ppermute | solution.py:318
  273.5 1.6 copy-start.9
  277.6 1.3 copy-start.4
  278.9 19.2 %copy-start.5 = (f32[1024,512]{1,0:T(8,128)S(1)}, f32[1024,512]{1,0:T(8,128)}, u32[]{:S(2)}) copy-start(f32[1024,512]{1,0:T(8,128)} %copy-done.4) | copy-start | bytes 6291460
  280.5 21.3 %copy-start.7 = (bf16[2048,512]{1,0:T(8,128)(2,1)S(1)}, bf16[2048,512]{1,0:T(8,128)(2,1)}, u32[]{:S(2)}) copy-start(bf16[2048,512]{1,0:T(8,128)(2,1)} %hidden.1.own_h) | copy-start | bytes 6291460
  280.5 21.3 %copy-start.10 = (bf16[2048,512]{1,0:T(8,128)(2,1)S(1)}, bf16[2048,512]{1,0:T(8,128)(2,1)}, u32[]{:S(2)}) copy-start(bf16[2048,512]{1,0:T(8,128)(2,1)} %copy-done.8) | copy-start | bytes 6291460
  280.5 21.3 %collective-permute-start.22 = (bf16[8,336,128]{2,1,0:T(8,128)(2,1)S(1)}, bf16[8,336,128]{2,1,0:T(8,128)(2,1)S(1)}, u32[]{:S(2)}, u32[]{:S(2)}) collective-permute-start(bf16[8,336,128]{2,1,0:T(8,128)(2,1)S(1)} %get-tuple-element.133), channel_id=1, source_target_pairs={{0,1},{1,0},{2,3},{3,2},{4,5},{5,4},{6,7},{7,6},{8,9},{9,8},{10,11... | collective-permute-start | bytes 2064392 | tf_op jit(solution)/shard_map/ppermute | solution.py:364
  299.7 14.9 %collective-permute-start.17 = (bf16[512,512]{1,0:T(8,128)(2,1)S(1)}, bf16[512,512]{1,0:T(8,128)(2,1)S(1)}, u32[]{:S(2)}, u32[]{:S(2)}) collective-permute-start(bf16[512,512]{1,0:T(8,128)(2,1)S(1)} %get-tuple-element.94), channel_id=1, source_target_pairs={{0,4},{2,6},{4,0},{6,2},{8,12},{10,14},{12,8},{14,10},{16,20},{18,... | collective-permute-start | bytes 1572872 | tf_op jit(solution)/shard_map/ppermute | solution.py:318
  300.3 14.9 %collective-permute-start.18 = (bf16[512,512]{1,0:T(8,128)(2,1)S(1)}, bf16[512,512]{1,0:T(8,128)(2,1)S(1)}, u32[]{:S(2)}, u32[]{:S(2)}) collective-permute-start(bf16[512,512]{1,0:T(8,128)(2,1)S(1)} %get-tuple-element.96), channel_id=1, source_target_pairs={{0,2},{2,0},{4,6},{6,4},{8,10},{10,8},{12,14},{14,12},{16,18},{18,... | collective-permute-start | bytes 1572872 | tf_op jit(solution)/shard_map/ppermute | solution.py:318
  303.7 20.4 %collective-permute-start.23 = (bf16[1024,256]{1,0:T(8,128)(2,1)S(1)}, bf16[1024,256]{1,0:T(8,128)(2,1)S(1)}, u32[]{:S(2)}, u32[]{:S(2)}) collective-permute-start(bf16[1024,256]{1,0:T(8,128)(2,1)S(1)} %get-tuple-element.112), channel_id=1, source_target_pairs={{0,2},{2,0},{4,6},{6,4},{8,10},{10,8},{12,14},{14,12},{16,18},{18,... | collective-permute-start | bytes 1572872 | tf_op jit(solution)/shard_map/ppermute | solution.py:318
  304.4 19.8 %collective-permute-start.24 = (bf16[1024,256]{1,0:T(8,128)(2,1)S(1)}, bf16[1024,256]{1,0:T(8,128)(2,1)S(1)}, u32[]{:S(2)}, u32[]{:S(2)}) collective-permute-start(bf16[1024,256]{1,0:T(8,128)(2,1)S(1)} %get-tuple-element.114), channel_id=1, source_target_pairs={{0,4},{2,6},{4,0},{6,2},{8,12},{10,14},{12,8},{14,10},{16,20},{18,... | collective-permute-start | bytes 1572872 | tf_op jit(solution)/shard_map/ppermute | solution.py:318
  305.8 18.3 %collective-permute-start.25 = (bf16[1024,256]{1,0:T(8,128)(2,1)S(1)}, bf16[1024,256]{1,0:T(8,128)(2,1)S(1)}, u32[]{:S(2)}, u32[]{:S(2)}) collective-permute-start(bf16[1024,256]{1,0:T(8,128)(2,1)S(1)} %get-tuple-element.116), channel_id=1, source_target_pairs={{0,8},{2,10},{4,12},{6,14},{8,0},{10,2},{12,4},{14,6},{16,24},{18,... | collective-permute-start | bytes 1572872 | tf_op jit(solution)/shard_map/ppermute | solution.py:318
  315.4 12.5 %collective-permute-start.19 = (bf16[256,512]{1,0:T(8,128)(2,1)S(1)}, bf16[256,512]{1,0:T(8,128)(2,1)S(1)}, u32[]{:S(2)}, u32[]{:S(2)}) collective-permute-start(bf16[256,512]{1,0:T(8,128)(2,1)S(1)} %get-tuple-element.98), channel_id=1, source_target_pairs={{0,8},{2,10},{4,12},{6,14},{8,0},{10,2},{12,4},{14,6},{16,24},{18,... | collective-permute-start | bytes 786440 | tf_op jit(solution)/shard_map/ppermute | solution.py:318
  315.7 16.6 %collective-permute-start.20 = (bf16[256,512]{1,0:T(8,128)(2,1)S(1)}, bf16[256,512]{1,0:T(8,128)(2,1)S(1)}, u32[]{:S(2)}, u32[]{:S(2)}) collective-permute-start(bf16[256,512]{1,0:T(8,128)(2,1)S(1)} %get-tuple-element.100), channel_id=1, source_target_pairs={{0,8},{2,10},{4,12},{6,14},{8,0},{10,2},{12,4},{14,6},{16,24},{18,... | collective-permute-start | bytes 786440 | tf_op jit(solution)/shard_map/ppermute | solution.py:318
  324.4 12.4 %collective-permute-start.26 = (bf16[512,256]{1,0:T(8,128)(2,1)S(1)}, bf16[512,256]{1,0:T(8,128)(2,1)S(1)}, u32[]{:S(2)}, u32[]{:S(2)}) collective-permute-start(bf16[512,256]{1,0:T(8,128)(2,1)S(1)} %get-tuple-element.118), channel_id=1, source_target_pairs={{0,4},{2,6},{4,0},{6,2},{8,12},{10,14},{12,8},{14,10},{16,20},{18,... | collective-permute-start | bytes 786440 | tf_op jit(solution)/shard_map/ppermute | solution.py:318
  326.0 11.1 %collective-permute-start.27 = (bf16[512,256]{1,0:T(8,128)(2,1)S(1)}, bf16[512,256]{1,0:T(8,128)(2,1)S(1)}, u32[]{:S(2)}, u32[]{:S(2)}) collective-permute-start(bf16[512,256]{1,0:T(8,128)(2,1)S(1)} %get-tuple-element.120), channel_id=1, source_target_pairs={{0,8},{2,10},{4,12},{6,14},{8,0},{10,2},{12,4},{14,6},{16,24},{18,... | collective-permute-start | bytes 786440 | tf_op jit(solution)/shard_map/ppermute | solution.py:318
  326.5 10.6 %collective-permute-start.28 = (bf16[512,256]{1,0:T(8,128)(2,1)S(1)}, bf16[512,256]{1,0:T(8,128)(2,1)S(1)}, u32[]{:S(2)}, u32[]{:S(2)}) collective-permute-start(bf16[512,256]{1,0:T(8,128)(2,1)S(1)} %get-tuple-element.122), channel_id=1, source_target_pairs={{0,2},{2,0},{4,6},{6,4},{8,10},{10,8},{12,14},{14,12},{16,18},{18,... | collective-permute-start | bytes 786440 | tf_op jit(solution)/shard_map/ppermute | solution.py:318
  332.4 15.9 %collective-permute-start.21 = (bf16[128,1024]{1,0:T(8,128)(2,1)S(1)}, bf16[128,1024]{1,0:T(8,128)(2,1)S(1)}, u32[]{:S(2)}, u32[]{:S(2)}) collective-permute-start(bf16[128,1024]{1,0:T(8,128)(2,1)S(1)} %get-tuple-element.102), channel_id=1, source_target_pairs={{0,16},{2,18},{4,20},{6,22},{8,24},{10,26},{12,28},{14,30},{16,0},... | collective-permute-start | bytes 786440 | tf_op jit(solution)/shard_map/ppermute | solution.py:318
  337.2 5.7 %collective-permute-start.29 = (bf16[256,256]{1,0:T(8,128)(2,1)S(1)}, bf16[256,256]{1,0:T(8,128)(2,1)S(1)}, u32[]{:S(2)}, u32[]{:S(2)}) collective-permute-start(bf16[256,256]{1,0:T(8,128)(2,1)S(1)} %get-tuple-element.124), channel_id=1, source_target_pairs={{0,8},{2,10},{4,12},{6,14},{8,0},{10,2},{12,4},{14,6},{16,24},{18,... | collective-permute-start | bytes 393224 | tf_op jit(solution)/shard_map/ppermute | solution.py:318
  338.0 5.0 %collective-permute-start.30 = (bf16[256,256]{1,0:T(8,128)(2,1)S(1)}, bf16[256,256]{1,0:T(8,128)(2,1)S(1)}, u32[]{:S(2)}, u32[]{:S(2)}) collective-permute-start(bf16[256,256]{1,0:T(8,128)(2,1)S(1)} %get-tuple-element.126), channel_id=1, source_target_pairs={{0,2},{2,0},{4,6},{6,4},{8,10},{10,8},{12,14},{14,12},{16,18},{18,... | collective-permute-start | bytes 393224 | tf_op jit(solution)/shard_map/ppermute | solution.py:318
  339.4 5.0 %collective-permute-start.31 = (bf16[256,256]{1,0:T(8,128)(2,1)S(1)}, bf16[256,256]{1,0:T(8,128)(2,1)S(1)}, u32[]{:S(2)}, u32[]{:S(2)}) collective-permute-start(bf16[256,256]{1,0:T(8,128)(2,1)S(1)} %get-tuple-element.128), channel_id=1, source_target_pairs={{0,4},{2,6},{4,0},{6,2},{8,12},{10,14},{12,8},{14,10},{16,20},{18,... | collective-permute-start | bytes 393224 | tf_op jit(solution)/shard_map/ppermute | solution.py:318
  344.4 8.6 %collective-permute-start.32 = (bf16[128,768]{1,0:T(8,128)(2,1)S(1)}, bf16[128,768]{1,0:T(8,128)(2,1)S(1)}, u32[]{:S(2)}, u32[]{:S(2)}) collective-permute-start(bf16[128,768]{1,0:T(8,128)(2,1)S(1)} %get-tuple-element.130), channel_id=1, source_target_pairs={{0,16},{2,18},{4,20},{6,22},{8,24},{10,26},{12,28},{14,30},{16,0},... | collective-permute-start | bytes 589832 | tf_op jit(solution)/shard_map/ppermute | solution.py:318

commit v14 on v13

--- a/solution.py
+++ b/solution.py
@@ -208,7 +208,6 @@
     )(at, own, other, packed)
 
 
-HALVES = ((0, 1, 2), (1, 0, 2))
 THIRDS = ((0, 1, 2), (1, 2, 0), (2, 0, 1))
 
 
@@ -380,20 +379,20 @@
 
     mid = tokens.shape[1] // 2
     near, far = swap(tokens, 2), swap(tokens, 3)
-    x_own, y_own = swap(tokens, 0), swap(tokens, 1)
+    x_own, y_own, xy_own = swap(tokens, 0), swap(tokens, 1), diagonal(tokens)
     parts = (128, 96)
     packed = pack_first(listing, gate_proj, up_proj, down_proj, parts[0], share, devices)
     far, packed = tie((far, packed))
     corner = swap(far, 2)
     pair = jnp.concatenate([far, near], axis=0)
     pair_y, pair_x = swap(pair[:, :mid], 1), swap(pair[:, mid:], 0)
-    packed, x_own, y_own, pair, corner, pair_y, pair_x = tie(
-        (packed, x_own, y_own, pair, corner, pair_y, pair_x)
+    packed, x_own, y_own, xy_own, pair, corner, pair_y, pair_x = tie(
+        (packed, x_own, y_own, xy_own, pair, corner, pair_y, pair_x)
     )
 
     moved = move(packed)
     corner_a, corner_b = corner[:, :mid], corner[:, mid:]
-    cross = diagonal(jnp.concatenate([tokens, corner], axis=0))
+    cross = diagonal(corner)
     most_a = swap(jnp.concatenate([pair[:, :mid], corner_a, pair_y], axis=0), 0)
     most_b = swap(jnp.concatenate([pair[:, mid:], corner_b, pair_x], axis=0), 1)
     corner_y, corner_x = swap(corner_a, 1), swap(corner_b, 0)
@@ -402,7 +401,6 @@
         return jnp.concatenate(values, axis=0)
 
     three, two = slice(0, 3 * block), slice(3 * block, 5 * block)
-    top, low = slice(0, block), slice(block, 2 * block)
     first, second = slice(0, mid), slice(mid, 2 * mid)
     rows = jnp.concatenate(
         [
@@ -410,13 +408,13 @@
                 tokens[:, first], pair[:, first], corner_a,
                 y_own[:, first], pair_y, corner_y,
                 x_own[:, first], most_a[three],
-                cross[top, first], most_a[two], cross[low, first],
+                xy_own[:, first], most_a[two], cross[:, first],
             ),
             lay(
                 tokens[:, second], pair[:, second], corner_b,
                 y_own[:, second], most_b[three],
                 x_own[:, second], pair_x, corner_x,
-                cross[top, second], most_b[two], cross[low, second],
+                xy_own[:, second], most_b[two], cross[:, second],
             ),
         ],
         axis=1,
@@ -431,13 +429,14 @@
     hidden_other = exchange(hidden)
     down0 = moved[:, depth * 7 : depth * 7 + parts[0] * 7 // 2]
 
-    def products(down, rows_in, orders):
+    def products(down, rows_in, orders, before=None):
         own = lax.dynamic_slice_in_dim(down, core * group, group, 0)
         other = exchange(lax.dynamic_slice_in_dim(down, (1 - core) * group, group, 0))
         args = (hidden, hidden_other, own, other)
         sent = down_product(*args, rows_in, 1, orders, jnp.bfloat16, "down_send")
         sent, args = tie((sent, args))
         come = [swap(value, order[0]) for value, order in zip(sent, orders)]
+        args, _ = tie((args, before))
         kept = down_product(*args, rows_in, 0, orders, jnp.float32, "down_keep")
         return kept, come
 
@@ -452,12 +451,12 @@
         come = swap(send, 3)
         return (keep + come.astype(jnp.float32)).astype(jnp.bfloat16)
 
-    kept0, come0 = products(down0, parts[0], HALVES)
+    kept0, come0 = products(down0, parts[0], THIRDS)
     down1, kept0 = tie((down1, kept0))
-    kept1, come1 = products(down1, parts[1], THIRDS)
-    kept0, come0 = stage(kept0, come0, 1, HALVES)
+    kept1, come1 = products(down1, parts[1], THIRDS, before=come0)
+    kept0, come0 = stage(kept0, come0, 1, THIRDS)
     kept1, come1 = stage(kept1, come1, 1, THIRDS)
-    kept0, come0 = stage(kept0, come0, 2, HALVES)
+    kept0, come0 = stage(kept0, come0, 2, THIRDS)
     kept1, come1 = stage(kept1, come1, 2, THIRDS)
     out = []
     for rows_in, total in zip(parts, (last_stage(kept0, come0), last_stage(kept1, come1))):

time: 357 us -> 358 us (level)
    ppermute x1 -> x2, waiting for transfers between devices: 9.18 us -> 0.01 us  [diagonal(): return lax.ppermute(value, 'ep', [(i, i ^ 3) for i in range(devices)])]
    all_to_all x2, waiting for transfers between devices: 44.9 us -> 52.7 us  [move(): return lax.all_to_all(packed, 'ep', 0, 0, tiled=True)]
    ppermute x28 -> x31, starting transfers between devices: 34.1 us -> 29.8 us  [swap(): return lax.ppermute(value, 'ep', [(i, i ^ 1 << bit) for i in range(size)])]
    ppermute x1 -> x2, starting transfers between devices: 0.63 us -> 4.81 us  [diagonal(): return lax.ppermute(value, 'ep', [(i, i ^ 3) for i in range(devices)])]
    unnamed x40 -> x46, local copies, waits for them, and re-layouts: 20.4 us -> 22.7 us
    ppermute x28 -> x31, waiting for transfers between devices: 153 us -> 154 us  [swap(): return lax.ppermute(value, 'ep', [(i, i ^ 1 << bit) for i in range(size)])]
  transfers between devices with their start and end apart: 35 -> 39, of which waited for: 20 -> 22; matrix products, arithmetic and copies ran while one was open for 8% -> 8% of each run, Pallas kernels for 12% -> 12%
where the time goes in v14:
time: 358 us; the launch traced here: 354 us
  waiting for transfers between devices  217 us (61%)
  starting transfers between devices  50.9 us (14%)
  Pallas kernels  43.6 us (12%)
  local copies, waits for them, and re-layouts  30.4 us (8%)
  other arithmetic  11.3 us (3%)
    ppermute x31, waiting for transfers between devices, swap(): return lax.ppermute(value, 'ep', [(i, i ^ 1 << bit) for i in range(size)])  154 us
    all_to_all x2, waiting for transfers between devices, move(): return lax.all_to_all(packed, 'ep', 0, 0, tiled=True)  52.7 us
    ppermute x31, starting transfers between devices, swap(): return lax.ppermute(value, 'ep', [(i, i ^ 1 << bit) for i in range(size)])  29.8 us
    pallas_call x1, Pallas kernels, hidden_units(): pl.pallas_call(hidden_kernel, grid=(8,), out_shape=jax.ShapeDtypeStruct((...  23.3 us
    unnamed x46, local copies, waits for them, and re-layouts  22.7 us
    all_to_all x2, starting transfers between devices, move(): return lax.all_to_all(packed, 'ep', 0, 0, tiled=True)  15.7 us
    pallas_call x4, Pallas kernels, down_product(): pl.pallas_call(functools.partial(down_kernel, rows, side, orders), out_sh...  10.5 us
    ppermute x4, waiting for transfers between devices, exchange(): return lax.ppermute(value, 'et', [(0, 1), (1, 0)])  10.5 us
  transfers between devices with their start and end apart: 39, of which 22 were waited for; matrix products, arithmetic and copies ran while one was open for 8% of the time, Pallas kernels for 12%

profile of v14, /device:TPU:14, one launch (start us, length us, event | category | flops | bytes accessed | tf_op | source)
XLA Modules:
  0.0 353.5 jit_solution(12830339521091359176)
XLA Ops:
  0.0 2.6 collective-permute-start
  3.6 2.4 collective-permute-start.3
  6.5 0.9 select_reduce_fusion.4
  9.4 0.9 select_reduce_fusion.share_ref
  10.4 2.0 copy-done
  12.4 2.0 copy-done.2
  14.4 2.0 copy-done.3
  16.5 5.4 %pack_first.1 = bf16[16,2032,128]{2,1,0:T(8,128)(2,1)} custom-call(s32[14]{0:T(128)S(1)} %select_reduce_fusion.3.list_ref, bf16[16,224,512]{2,1,0:T(8,128)(2,1)S(1)} %copy-done.2, bf16[16,224,512]{2,1,0:T(8,128)(2,1)S(1)} %copy-done.3, bf16[16,224,512]{2,1,0:T(8,128)(2,1)S(1)} %copy-done, f32[16,16,128]{2,1,0:T(8,128)S(1)} %select_reduce_fusion.share_ref), custom_call_target="tpu_custom_call" | custom-call | tf_op jit(solution)/shard_map/pack_first/pallas_call | solution.py:113
  22.4 1.3 collective-permute-start.5
  23.8 1.6 collective-permute-done.4
  26.4 8.5 %collective-permute-done.5 = bf16[128,1792]{1,0:T(8,128)(2,1)S(1)} collective-permute-done((bf16[128,1792]{1,0:T(8,128)(2,1)S(1)}, bf16[128,1792]{1,0:T(8,128)(2,1)S(1)}, u32[]{:S(2)}, u32[]{:S(2)}) %collective-permute-start.5) | collective-permute-done | bytes 458784 | tf_op jit(solution)/shard_map/ppermute | solution.py:317
  35.7 7.9 %all-to-all-start = ((bf16[16,2032,128]{2,1,0:T(8,128)(2,1)}), bf16[16,2032,128]{2,1,0:T(8,128)(2,1)}, u32[]{:S(2)}, u32[]{:S(2)}) async-start(bf16[16,2032,128]{2,1,0:T(8,128)(2,1)} %pack_first.1), calls=%async_computation | async-start | bytes 16646144 | tf_op jit(solution)/shard_map/all_to_all | solution.py:366
  43.5 0.8 slice_dynamic-update-slice_fusion.13
  44.4 1.2 fusion.3
  45.5 0.9 fusion.5
  47.7 2.4 collective-permute-start.10
  51.3 0.8 slice_dynamic-update-slice_fusion.12
  53.0 90.7 %collective-permute-done.8 = bf16[128,896]{1,0:T(8,128)(2,1)S(1)} collective-permute-done((bf16[128,896]{1,0:T(8,128)(2,1)S(1)}, bf16[128,896]{1,0:T(8,128)(2,1)S(1)}, u32[]{:S(2)}, u32[]{:S(2)}) %collective-permute-start.8) | collective-permute-done | bytes 229408 | tf_op jit(solution)/shard_map/ppermute | solution.py:317
  144.4 1.0 slice_dynamic-update-slice_fusion
  145.4 0.8 slice_dynamic-update-slice_fusion.11
  146.2 0.8 constant_dynamic-update-slice_fusion.7
  147.7 8.6 %collective-permute-done.9 = bf16[640,896]{1,0:T(8,128)(2,1)S(1)} collective-permute-done((bf16[640,896]{1,0:T(8,128)(2,1)S(1)}, bf16[640,896]{1,0:T(8,128)(2,1)S(1)}, u32[]{:S(2)}, u32[]{:S(2)}) %collective-permute-start.9) | collective-permute-done | bytes 1146912 | tf_op jit(solution)/shard_map/ppermute | solution.py:317
  156.4 0.9 slice_dynamic-update-slice_fusion.1
  157.3 0.8 slice_dynamic-update-slice_fusion.10
  158.1 1.0 slice_dynamic-update-slice_fusion.2
  160.0 6.6 %pad_maximum_fusion.own_ref = bf16[2048,1792]{1,0:T(8,128)(2,1)} fusion(bf16[2048,896]{1,0:T(8,128)(2,1)} %get-tuple-element.176, bf16[2048,896]{1,0:T(8,128)(2,1)} %get-tuple-element.175), kind=kLoop, calls=%fused_computation | loop fusion | flops 14680064 | bytes 14680064 | tf_op jit(solution)/shard_map/concatenate | solution.py:405
  166.6 2.0 copy-done.1
  168.6 1.9 pack_rest.1
  171.1 7.5 %collective-permute-done.13.other_ref = bf16[2048,1792]{1,0:T(8,128)(2,1)} collective-permute-done((bf16[2048,1792]{1,0:T(8,128)(2,1)}, bf16[2048,1792]{1,0:T(8,128)(2,1)}, u32[]{:S(2)}, u32[]{:S(2)}) %collective-permute-start.13) | collective-permute-done | bytes 7340064 | tf_op jit(solution)/shard_map/ppermute | solution.py:363
  178.6 52.7 %all-to-all-done.packed_ref = bf16[16,2032,128]{2,1,0:T(8,128)(2,1)} async-done(((bf16[16,2032,128]{2,1,0:T(8,128)(2,1)}), bf16[16,2032,128]{2,1,0:T(8,128)(2,1)}, u32[]{:S(2)}, u32[]{:S(2)}) %all-to-all-start) | async-done | bytes 8323104 | tf_op jit(solution)/shard_map/all_to_all | solution.py:366
  231.3 7.8 %all-to-all-start.1 = ((bf16[16,336,128]{2,1,0:T(8,128)(2,1)}), bf16[16,336,128]{2,1,0:T(8,128)(2,1)}, u32[]{:S(2)}, u32[]{:S(2)}) async-start(bf16[16,336,128]{2,1,0:T(8,128)(2,1)} %pack_rest.1), calls=%async_computation.1 | async-start | bytes 2752512 | tf_op jit(solution)/shard_map/all_to_all | solution.py:366
  239.1 23.3 %hidden.1.own_h = bf16[2048,512]{1,0:T(8,128)(2,1)} custom-call(s32[2]{0:T(128)} %pad_add_fusion.at_ref, bf16[2048,1792]{1,0:T(8,128)(2,1)} %pad_maximum_fusion.own_ref, bf16[2048,1792]{1,0:T(8,128)(2,1)} %collective-permute-done.13.other_ref, bf16[16,2032,128]{2,1,0:T(8,128)(2,1)} %all-to-all-done.packed_ref), custom_call_target="tpu_custom_call" | custom-call | flops 15032385536 | bytes 25165824 | tf_op jit(solution)/shard_map/hidden/pallas_call | solution.py:196
  262.4 1.8 slice.85
  264.9 3.0 collective-permute-done.15.other_ref
  267.9 3.6 %down_send.2 = (bf16[1024,384]{1,0:T(8,128)(2,1)}, bf16[1024,384]{1,0:T(8,128)(2,1)}, bf16[1024,256]{1,0:T(8,128)(2,1)S(1)}) custom-call(bf16[2048,512]{1,0:T(8,128)(2,1)S(1)} %copy-done.6, bf16[2048,512]{1,0:T(8,128)(2,1)S(1)} %collective-permute-done.14.other_h, bf16[8,448,128]{2,1,0:T(8,128)(2,1)S(1)} %get-tuple-element.108.own_ref, ...), custom_call_target="tpu_custom_call" | custom-call | flops 2147483648 | bytes 8388608 | tf_op jit(solution)/shard_map/down_send/pallas_call | solution.py:257
  273.5 1.6 copy-done.9
  275.1 3.0 down_keep.2
  278.1 1.0 copy-done.4
  279.1 1.5 constant_dynamic-slice_fusion
  280.9 14.3 %collective-permute-done.18.refs_5_ = bf16[1024,256]{1,0:T(8,128)(2,1)S(1)} collective-permute-done((bf16[1024,256]{1,0:T(8,128)(2,1)}, bf16[1024,256]{1,0:T(8,128)(2,1)S(1)}, u32[]{:S(2)}, u32[]{:S(2)}) %collective-permute-start.18) | collective-permute-done | bytes 524320 | tf_op jit(solution)/shard_map/ppermute | solution.py:317
  295.3 1.2 copy-done.5
  296.5 1.9 sum_stage.6
  298.4 1.5 collective-permute-start.21
  299.9 1.9 down_send.3
  302.5 1.5 collective-permute-start.19
  304.7 2.9 collective-permute-done.21.refs_5_
  307.9 6.6 %collective-permute-done.19.refs_1_ = bf16[512,384]{1,0:T(8,128)(2,1)S(1)} collective-permute-done((bf16[512,384]{1,0:T(8,128)(2,1)S(1)}, bf16[512,384]{1,0:T(8,128)(2,1)S(1)}, u32[]{:S(2)}, u32[]{:S(2)}) %collective-permute-start.19) | collective-permute-done | bytes 393248 | tf_op jit(solution)/shard_map/ppermute | solution.py:317
  314.5 1.5 collective-permute-done.20.refs_3_
  316.8 1.5 collective-permute-start.23
  318.9 1.5 collective-permute-start.24
  320.3 1.9 down_keep.3
  322.3 3.0 collective-permute-done.28.refs_3_
  325.2 2.0 collective-permute-done.29.refs_5_
  328.4 1.7 collective-permute-start.32
  330.0 2.1 collective-permute-done.22.refs_1_
  332.3 3.9 %collective-permute-start.25 = (bf16[128,1024]{1,0:T(8,128)(2,1)S(1)}, bf16[128,1024]{1,0:T(8,128)(2,1)S(1)}, u32[]{:S(2)}, u32[]{:S(2)}) collective-permute-start(bf16[128,1024]{1,0:T(8,128)(2,1)S(1)} %get-tuple-element.132), channel_id=1, source_target_pairs={{0,16},{2,18},{4,20},{6,22},{8,24},{10,26},{12,28},{14,30},{16,0},... | collective-permute-start | bytes 786440 | tf_op jit(solution)/shard_map/ppermute | solution.py:317
  336.1 1.1 collective-permute-done.31.refs_3_
  337.4 1.0 collective-permute-start.33
  338.4 1.5 collective-permute-start.34
  340.4 2.9 collective-permute-done.33.refs_1_
  343.4 1.5 collective-permute-done.35.refs_5_
  344.9 2.1 collective-permute-start.36
  347.3 5.1 %collective-permute-done.36 = bf16[128,768]{1,0:T(8,128)(2,1)S(1)} collective-permute-done((bf16[128,768]{1,0:T(8,128)(2,1)S(1)}, bf16[128,768]{1,0:T(8,128)(2,1)S(1)}, u32[]{:S(2)}, u32[]{:S(2)}) %collective-permute-start.36) | collective-permute-done | bytes 196640 | tf_op jit(solution)/shard_map/ppermute | solution.py:317
  352.6 1.0 copy.15
  (99 shorter events, 20.7 us)
Async XLA Ops:
  0.0 22.4 %collective-permute-start = (bf16[128,1792]{1,0:T(8,128)(2,1)}, bf16[128,1792]{1,0:T(8,128)(2,1)S(1)}, u32[]{:S(2)}, u32[]{:S(2)}) collective-permute-start(bf16[128,1792]{1,0:T(8,128)(2,1)} %param.9), channel_id=1, source_target_pairs={{0,16},{2,18},{4,20},{6,22},{8,24},{10,26},{12,28},{14,30},{16,0},... | collective-permute-start | bytes 1376264 | tf_op jit(solution)/shard_map/ppermute | solution.py:317
  2.6 23.5 %collective-permute-start.1 = (bf16[128,1792]{1,0:T(8,128)(2,1)}, bf16[128,1792]{1,0:T(8,128)(2,1)S(1)}, u32[]{:S(2)}, u32[]{:S(2)}) collective-permute-start(bf16[128,1792]{1,0:T(8,128)(2,1)} %param.9), channel_id=1, source_target_pairs={{0,2},{2,0},{4,6},{6,4},{8,10},{10,8},{12,14},{14,12},{16,18},{18,... | collective-permute-start | bytes 1376264 | tf_op jit(solution)/shard_map/ppermute | solution.py:317
  3.1 23.2 %collective-permute-start.2 = (bf16[128,1792]{1,0:T(8,128)(2,1)}, bf16[128,1792]{1,0:T(8,128)(2,1)S(1)}, u32[]{:S(2)}, u32[]{:S(2)}) collective-permute-start(bf16[128,1792]{1,0:T(8,128)(2,1)} %param.9), channel_id=1, source_target_pairs={{0,4},{2,6},{4,0},{6,2},{8,12},{10,14},{12,8},{14,10},{16,20},{18,... | collective-permute-start | bytes 1376264 | tf_op jit(solution)/shard_map/ppermute | solution.py:317
  3.6 22.7 %collective-permute-start.3 = (bf16[128,1792]{1,0:T(8,128)(2,1)}, bf16[128,1792]{1,0:T(8,128)(2,1)S(1)}, u32[]{:S(2)}, u32[]{:S(2)}) collective-permute-start(bf16[128,1792]{1,0:T(8,128)(2,1)} %param.9), channel_id=1, source_target_pairs={{0,6},{2,4},{4,2},{6,0},{8,14},{10,12},{12,10},{14,8},{16,22},{18,... | collective-permute-start | bytes 1376264 | tf_op jit(solution)/shard_map/ppermute | solution.py:378
  6.1 19.3 %collective-permute-start.4 = (bf16[128,1792]{1,0:T(8,128)(2,1)}, bf16[128,1792]{1,0:T(8,128)(2,1)S(1)}, u32[]{:S(2)}, u32[]{:S(2)}) collective-permute-start(bf16[128,1792]{1,0:T(8,128)(2,1)} %param.9), channel_id=1, source_target_pairs={{0,8},{2,10},{4,12},{6,14},{8,0},{10,2},{12,4},{14,6},{16,24},{18,... | collective-permute-start | bytes 1376264 | tf_op jit(solution)/shard_map/ppermute | solution.py:317
  10.4 2.0 copy-start
  12.4 2.0 copy-start.2
  14.4 2.0 copy-start.3
  22.4 12.4 %collective-permute-start.5 = (bf16[128,1792]{1,0:T(8,128)(2,1)S(1)}, bf16[128,1792]{1,0:T(8,128)(2,1)S(1)}, u32[]{:S(2)}, u32[]{:S(2)}) collective-permute-start(bf16[128,1792]{1,0:T(8,128)(2,1)S(1)} %collective-permute-done), channel_id=1, source_target_pairs={{0,8},{2,10},{4,12},{6,14},{8,0},{10,2},{12,4},{14,6},{16,24},{18,... | collective-permute-start | bytes 1376264 | tf_op jit(solution)/shard_map/ppermute | solution.py:317
  25.5 9.6 %collective-permute-start.6 = (bf16[256,896]{1,0:T(8,128)(2,1)S(1)}, bf16[256,896]{1,0:T(8,128)(2,1)S(1)}, u32[]{:S(2)}, u32[]{:S(2)}) collective-permute-start(bf16[256,896]{1,0:T(8,128)(2,1)S(1)} %get-tuple-element.174), channel_id=1, source_target_pairs={{0,4},{2,6},{4,0},{6,2},{8,12},{10,14},{12,8},{14,10},{16,20},{18,... | collective-permute-start | bytes 1376264 | tf_op jit(solution)/shard_map/ppermute | solution.py:317
  26.1 17.4 %copy-start.12 = (bf16[128,1792]{1,0:T(8,128)(2,1)S(1)}, bf16[128,1792]{1,0:T(8,128)(2,1)}, u32[]{:S(2)}) copy-start(bf16[128,1792]{1,0:T(8,128)(2,1)} %param.9) | copy-start | bytes 1376260
  26.1 9.6 %collective-permute-start.7 = (bf16[256,896]{1,0:T(8,128)(2,1)S(1)}, bf16[256,896]{1,0:T(8,128)(2,1)S(1)}, u32[]{:S(2)}, u32[]{:S(2)}) collective-permute-start(bf16[256,896]{1,0:T(8,128)(2,1)S(1)} %get-tuple-element.173), channel_id=1, source_target_pairs={{0,2},{2,0},{4,6},{6,4},{8,10},{10,8},{12,14},{14,12},{16,18},{18,... | collective-permute-start | bytes 1376264 | tf_op jit(solution)/shard_map/ppermute | solution.py:317
  26.4 8.8 %copy-start.13 = (bf16[128,1792]{1,0:T(8,128)(2,1)}, bf16[128,1792]{1,0:T(8,128)(2,1)S(1)}, u32[]{:S(2)}) copy-start(bf16[128,1792]{1,0:T(8,128)(2,1)S(1)} %collective-permute-done.2) | copy-start | bytes 1376260
  34.9 0.8 copy-start.15
  35.7 195.6 %all-to-all-start = ((bf16[16,2032,128]{2,1,0:T(8,128)(2,1)}), bf16[16,2032,128]{2,1,0:T(8,128)(2,1)}, u32[]{:S(2)}, u32[]{:S(2)}) async-start(bf16[16,2032,128]{2,1,0:T(8,128)(2,1)} %pack_first.1), calls=%async_computation | async-start | bytes 16646144 | tf_op jit(solution)/shard_map/all_to_all | solution.py:366
  43.5 2.0 copy-start.16
  45.5 5.8 %copy-start.14 = (bf16[128,1792]{1,0:T(8,128)(2,1)S(1)}, bf16[128,1792]{1,0:T(8,128)(2,1)}, u32[]{:S(2)}) copy-start(bf16[128,1792]{1,0:T(8,128)(2,1)} %copy-done.13) | copy-start | bytes 1376260
  46.5 97.9 %collective-permute-start.11 = (bf16[640,896]{1,0:T(8,128)(2,1)S(1)}, bf16[640,896]{1,0:T(8,128)(2,1)S(1)}, u32[]{:S(2)}, u32[]{:S(2)}) collective-permute-start(bf16[640,896]{1,0:T(8,128)(2,1)S(1)} %pad_maximum_fusion.2), channel_id=1, source_target_pairs={{0,4},{2,6},{4,0},{6,2},{8,12},{10,14},{12,8},{14,10},{16,20},{18,... | collective-permute-start | bytes 3440648 | tf_op jit(solution)/shard_map/ppermute | solution.py:317
  47.1 99.9 %collective-permute-start.12 = (bf16[128,896]{1,0:T(8,128)(2,1)S(1)}, bf16[128,896]{1,0:T(8,128)(2,1)S(1)}, u32[]{:S(2)}, u32[]{:S(2)}) collective-permute-start(bf16[128,896]{1,0:T(8,128)(2,1)S(1)} %get-tuple-element.184), channel_id=1, source_target_pairs={{0,2},{2,0},{4,6},{6,4},{8,10},{10,8},{12,14},{14,12},{16,18},{18,... | collective-permute-start | bytes 688136 | tf_op jit(solution)/shard_map/ppermute | solution.py:317
  47.7 111.5 %collective-permute-start.10 = (bf16[128,1792]{1,0:T(8,128)(2,1)S(1)}, bf16[128,1792]{1,0:T(8,128)(2,1)S(1)}, u32[]{:S(2)}, u32[]{:S(2)}) collective-permute-start(bf16[128,1792]{1,0:T(8,128)(2,1)S(1)} %copy-done.16), channel_id=1, source_target_pairs={{0,6},{2,4},{4,2},{6,0},{8,14},{10,12},{12,10},{14,8},{16,22},{18,... | collective-permute-start | bytes 1376264 | tf_op jit(solution)/shard_map/ppermute | solution.py:378
  50.0 93.6 %collective-permute-start.8 = (bf16[128,896]{1,0:T(8,128)(2,1)S(1)}, bf16[128,896]{1,0:T(8,128)(2,1)S(1)}, u32[]{:S(2)}, u32[]{:S(2)}) collective-permute-start(bf16[128,896]{1,0:T(8,128)(2,1)S(1)} %get-tuple-element.181), channel_id=1, source_target_pairs={{0,4},{2,6},{4,0},{6,2},{8,12},{10,14},{12,8},{14,10},{16,20},{18,... | collective-permute-start | bytes 688136 | tf_op jit(solution)/shard_map/ppermute | solution.py:317
  50.7 105.7 %collective-permute-start.9 = (bf16[640,896]{1,0:T(8,128)(2,1)S(1)}, bf16[640,896]{1,0:T(8,128)(2,1)S(1)}, u32[]{:S(2)}, u32[]{:S(2)}) collective-permute-start(bf16[640,896]{1,0:T(8,128)(2,1)S(1)} %pad_maximum_fusion.1), channel_id=1, source_target_pairs={{0,2},{2,0},{4,6},{6,4},{8,10},{10,8},{12,14},{14,12},{16,18},{18,... | collective-permute-start | bytes 3440648 | tf_op jit(solution)/shard_map/ppermute | solution.py:317
  166.6 12.0 %collective-permute-start.13 = (bf16[2048,1792]{1,0:T(8,128)(2,1)}, bf16[2048,1792]{1,0:T(8,128)(2,1)}, u32[]{:S(2)}, u32[]{:S(2)}) collective-permute-start(bf16[2048,1792]{1,0:T(8,128)(2,1)} %pad_maximum_fusion.own_ref), channel_id=1, source_target_pairs={{0,1},{1,0},{2,3},{3,2},{4,5},{5,4},{6,7},{7,6},{8,9},{9,8},{10,11... | collective-permute-start | bytes 22020104 | tf_op jit(solution)/shard_map/ppermute | solution.py:363
  166.6 2.0 copy-start.1
  231.3 47.8 %all-to-all-start.1 = ((bf16[16,336,128]{2,1,0:T(8,128)(2,1)}), bf16[16,336,128]{2,1,0:T(8,128)(2,1)}, u32[]{:S(2)}, u32[]{:S(2)}) async-start(bf16[16,336,128]{2,1,0:T(8,128)(2,1)} %pack_rest.1), calls=%async_computation.1 | async-start | bytes 2752512 | tf_op jit(solution)/shard_map/all_to_all | solution.py:366
  262.4 5.5 %collective-permute-start.14 = (bf16[2048,512]{1,0:T(8,128)(2,1)}, bf16[2048,512]{1,0:T(8,128)(2,1)S(1)}, u32[]{:S(2)}, u32[]{:S(2)}) collective-permute-start(bf16[2048,512]{1,0:T(8,128)(2,1)} %hidden.1.own_h), channel_id=1, source_target_pairs={{0,1},{1,0},{2,3},{3,2},{4,5},{5,4},{6,7},{7,6},{8,9},{9,8},{10,11... | collective-permute-start | bytes 6291464 | tf_op jit(solution)/shard_map/ppermute | solution.py:363
  262.4 5.5 %copy-start.6 = (bf16[2048,512]{1,0:T(8,128)(2,1)S(1)}, bf16[2048,512]{1,0:T(8,128)(2,1)}, u32[]{:S(2)}) copy-start(bf16[2048,512]{1,0:T(8,128)(2,1)} %hidden.1.own_h) | copy-start | bytes 6291460
  264.4 3.5 %collective-permute-start.15 = (bf16[8,448,128]{2,1,0:T(8,128)(2,1)S(1)}, bf16[8,448,128]{2,1,0:T(8,128)(2,1)S(1)}, u32[]{:S(2)}, u32[]{:S(2)}) collective-permute-start(bf16[8,448,128]{2,1,0:T(8,128)(2,1)S(1)} %get-tuple-element.165), channel_id=1, source_target_pairs={{0,1},{1,0},{2,3},{3,2},{4,5},{5,4},{6,7},{7,6},{8,9},{9,8},{10,11... | collective-permute-start | bytes 2752520 | tf_op jit(solution)/shard_map/ppermute | solution.py:363
  267.9 3.6 %copy-start.8 = (bf16[2048,512]{1,0:T(8,128)(2,1)}, bf16[2048,512]{1,0:T(8,128)(2,1)S(1)}, u32[]{:S(2)}) copy-start(bf16[2048,512]{1,0:T(8,128)(2,1)S(1)} %collective-permute-done.14.other_h) | copy-start | bytes 6291460
  271.5 0.8 copy-start.11
  272.3 22.9 %collective-permute-start.16 = (bf16[1024,384]{1,0:T(8,128)(2,1)}, bf16[1024,384]{1,0:T(8,128)(2,1)}, u32[]{:S(2)}, u32[]{:S(2)}) collective-permute-start(bf16[1024,384]{1,0:T(8,128)(2,1)} %get-tuple-element.114), channel_id=1, source_target_pairs={{0,2},{2,0},{4,6},{6,4},{8,10},{10,8},{12,14},{14,12},{16,18},{18,... | collective-permute-start | bytes 2359304 | tf_op jit(solution)/shard_map/ppermute | solution.py:317
  272.9 22.4 %collective-permute-start.17 = (bf16[1024,384]{1,0:T(8,128)(2,1)}, bf16[1024,384]{1,0:T(8,128)(2,1)}, u32[]{:S(2)}, u32[]{:S(2)}) collective-permute-start(bf16[1024,384]{1,0:T(8,128)(2,1)} %get-tuple-element.116), channel_id=1, source_target_pairs={{0,4},{2,6},{4,0},{6,2},{8,12},{10,14},{12,8},{14,10},{16,20},{18,... | collective-permute-start | bytes 2359304 | tf_op jit(solution)/shard_map/ppermute | solution.py:317
  273.5 1.6 copy-start.9
  278.1 1.0 copy-start.4
  279.1 20.8 %copy-start.7 = (bf16[2048,512]{1,0:T(8,128)(2,1)S(1)}, bf16[2048,512]{1,0:T(8,128)(2,1)}, u32[]{:S(2)}) copy-start(bf16[2048,512]{1,0:T(8,128)(2,1)} %hidden.1.own_h) | copy-start | bytes 6291460
  280.6 19.3 %collective-permute-start.26 = (bf16[8,336,128]{2,1,0:T(8,128)(2,1)S(1)}, bf16[8,336,128]{2,1,0:T(8,128)(2,1)S(1)}, u32[]{:S(2)}, u32[]{:S(2)}) collective-permute-start(bf16[8,336,128]{2,1,0:T(8,128)(2,1)S(1)} %get-tuple-element.167), channel_id=1, source_target_pairs={{0,1},{1,0},{2,3},{3,2},{4,5},{5,4},{6,7},{7,6},{8,9},{9,8},{10,11... | collective-permute-start | bytes 2064392 | tf_op jit(solution)/shard_map/ppermute | solution.py:363
  280.7 14.6 %collective-permute-start.18 = (bf16[1024,256]{1,0:T(8,128)(2,1)}, bf16[1024,256]{1,0:T(8,128)(2,1)S(1)}, u32[]{:S(2)}, u32[]{:S(2)}) collective-permute-start(bf16[1024,256]{1,0:T(8,128)(2,1)} %copy-done.11), channel_id=1, source_target_pairs={{0,8},{2,10},{4,12},{6,14},{8,0},{10,2},{12,4},{14,6},{16,24},{18,... | collective-permute-start | bytes 1572872 | tf_op jit(solution)/shard_map/ppermute | solution.py:317
  295.3 1.2 copy-start.5
  296.5 3.4 copy-start.10
  298.4 9.3 %collective-permute-start.21 = (bf16[512,256]{1,0:T(8,128)(2,1)S(1)}, bf16[512,256]{1,0:T(8,128)(2,1)S(1)}, u32[]{:S(2)}, u32[]{:S(2)}) collective-permute-start(bf16[512,256]{1,0:T(8,128)(2,1)S(1)} %get-tuple-element.124), channel_id=1, source_target_pairs={{0,2},{2,0},{4,6},{6,4},{8,10},{10,8},{12,14},{14,12},{16,18},{18,... | collective-permute-start | bytes 786440 | tf_op jit(solution)/shard_map/ppermute | solution.py:317
  301.8 17.0 %collective-permute-start.27 = (bf16[1024,256]{1,0:T(8,128)(2,1)S(1)}, bf16[1024,256]{1,0:T(8,128)(2,1)S(1)}, u32[]{:S(2)}, u32[]{:S(2)}) collective-permute-start(bf16[1024,256]{1,0:T(8,128)(2,1)S(1)} %get-tuple-element.146), channel_id=1, source_target_pairs={{0,2},{2,0},{4,6},{6,4},{8,10},{10,8},{12,14},{14,12},{16,18},{18,... | collective-permute-start | bytes 1572872 | tf_op jit(solution)/shard_map/ppermute | solution.py:317
  302.5 12.1 %collective-permute-start.19 = (bf16[512,384]{1,0:T(8,128)(2,1)S(1)}, bf16[512,384]{1,0:T(8,128)(2,1)S(1)}, u32[]{:S(2)}, u32[]{:S(2)}) collective-permute-start(bf16[512,384]{1,0:T(8,128)(2,1)S(1)} %get-tuple-element.120), channel_id=1, source_target_pairs={{0,4},{2,6},{4,0},{6,2},{8,12},{10,14},{12,8},{14,10},{16,20},{18,... | collective-permute-start | bytes 1179656 | tf_op jit(solution)/shard_map/ppermute | solution.py:317
  303.9 12.1 %collective-permute-start.20 = (bf16[512,384]{1,0:T(8,128)(2,1)S(1)}, bf16[512,384]{1,0:T(8,128)(2,1)S(1)}, u32[]{:S(2)}, u32[]{:S(2)}) collective-permute-start(bf16[512,384]{1,0:T(8,128)(2,1)S(1)} %get-tuple-element.122), channel_id=1, source_target_pairs={{0,8},{2,10},{4,12},{6,14},{8,0},{10,2},{12,4},{14,6},{16,24},{18,... | collective-permute-start | bytes 1179656 | tf_op jit(solution)/shard_map/ppermute | solution.py:317
  304.5 20.7 %collective-permute-start.28 = (bf16[1024,256]{1,0:T(8,128)(2,1)S(1)}, bf16[1024,256]{1,0:T(8,128)(2,1)S(1)}, u32[]{:S(2)}, u32[]{:S(2)}) collective-permute-start(bf16[1024,256]{1,0:T(8,128)(2,1)S(1)} %get-tuple-element.148), channel_id=1, source_target_pairs={{0,4},{2,6},{4,0},{6,2},{8,12},{10,14},{12,8},{14,10},{16,20},{18,... | collective-permute-start | bytes 1572872 | tf_op jit(solution)/shard_map/ppermute | solution.py:317
  307.6 19.6 %collective-permute-start.29 = (bf16[1024,256]{1,0:T(8,128)(2,1)S(1)}, bf16[1024,256]{1,0:T(8,128)(2,1)S(1)}, u32[]{:S(2)}, u32[]{:S(2)}) collective-permute-start(bf16[1024,256]{1,0:T(8,128)(2,1)S(1)} %get-tuple-element.150), channel_id=1, source_target_pairs={{0,8},{2,10},{4,12},{6,14},{8,0},{10,2},{12,4},{14,6},{16,24},{18,... | collective-permute-start | bytes 1572872 | tf_op jit(solution)/shard_map/ppermute | solution.py:317
  316.1 16.0 %collective-permute-start.22 = (bf16[256,384]{1,0:T(8,128)(2,1)S(1)}, bf16[256,384]{1,0:T(8,128)(2,1)S(1)}, u32[]{:S(2)}, u32[]{:S(2)}) collective-permute-start(bf16[256,384]{1,0:T(8,128)(2,1)S(1)} %get-tuple-element.126), channel_id=1, source_target_pairs={{0,8},{2,10},{4,12},{6,14},{8,0},{10,2},{12,4},{14,6},{16,24},{18,... | collective-permute-start | bytes 589832 | tf_op jit(solution)/shard_map/ppermute | solution.py:317
  316.8 15.4 %collective-permute-start.23 = (bf16[256,384]{1,0:T(8,128)(2,1)S(1)}, bf16[256,384]{1,0:T(8,128)(2,1)S(1)}, u32[]{:S(2)}, u32[]{:S(2)}) collective-permute-start(bf16[256,384]{1,0:T(8,128)(2,1)S(1)} %get-tuple-element.128), channel_id=1, source_target_pairs={{0,2},{2,0},{4,6},{6,4},{8,10},{10,8},{12,14},{14,12},{16,18},{18,... | collective-permute-start | bytes 589832 | tf_op jit(solution)/shard_map/ppermute | solution.py:317
  318.9 9.5 %collective-permute-start.24 = (bf16[256,256]{1,0:T(8,128)(2,1)S(1)}, bf16[256,256]{1,0:T(8,128)(2,1)S(1)}, u32[]{:S(2)}, u32[]{:S(2)}) collective-permute-start(bf16[256,256]{1,0:T(8,128)(2,1)S(1)} %get-tuple-element.130), channel_id=1, source_target_pairs={{0,4},{2,6},{4,0},{6,2},{8,12},{10,14},{12,8},{14,10},{16,20},{18,... | collective-permute-start | bytes 393224 | tf_op jit(solution)/shard_map/ppermute | solution.py:317
  327.5 8.7 %collective-permute-start.30 = (bf16[512,256]{1,0:T(8,128)(2,1)S(1)}, bf16[512,256]{1,0:T(8,128)(2,1)S(1)}, u32[]{:S(2)}, u32[]{:S(2)}) collective-permute-start(bf16[512,256]{1,0:T(8,128)(2,1)S(1)} %get-tuple-element.152), channel_id=1, source_target_pairs={{0,4},{2,6},{4,0},{6,2},{8,12},{10,14},{12,8},{14,10},{16,20},{18,... | collective-permute-start | bytes 786440 | tf_op jit(solution)/shard_map/ppermute | solution.py:317
  328.0 9.2 %collective-permute-start.31 = (bf16[512,256]{1,0:T(8,128)(2,1)S(1)}, bf16[512,256]{1,0:T(8,128)(2,1)S(1)}, u32[]{:S(2)}, u32[]{:S(2)}) collective-permute-start(bf16[512,256]{1,0:T(8,128)(2,1)S(1)} %get-tuple-element.154), channel_id=1, source_target_pairs={{0,8},{2,10},{4,12},{6,14},{8,0},{10,2},{12,4},{14,6},{16,24},{18,... | collective-permute-start | bytes 786440 | tf_op jit(solution)/shard_map/ppermute | solution.py:317
  328.4 8.9 %collective-permute-start.32 = (bf16[512,256]{1,0:T(8,128)(2,1)S(1)}, bf16[512,256]{1,0:T(8,128)(2,1)S(1)}, u32[]{:S(2)}, u32[]{:S(2)}) collective-permute-start(bf16[512,256]{1,0:T(8,128)(2,1)S(1)} %get-tuple-element.156), channel_id=1, source_target_pairs={{0,2},{2,0},{4,6},{6,4},{8,10},{10,8},{12,14},{14,12},{16,18},{18,... | collective-permute-start | bytes 786440 | tf_op jit(solution)/shard_map/ppermute | solution.py:317
  332.3 14.8 %collective-permute-start.25 = (bf16[128,1024]{1,0:T(8,128)(2,1)S(1)}, bf16[128,1024]{1,0:T(8,128)(2,1)S(1)}, u32[]{:S(2)}, u32[]{:S(2)}) collective-permute-start(bf16[128,1024]{1,0:T(8,128)(2,1)S(1)} %get-tuple-element.132), channel_id=1, source_target_pairs={{0,16},{2,18},{4,20},{6,22},{8,24},{10,26},{12,28},{14,30},{16,0},... | collective-permute-start | bytes 786440 | tf_op jit(solution)/shard_map/ppermute | solution.py:317
  337.4 5.9 %collective-permute-start.33 = (bf16[256,256]{1,0:T(8,128)(2,1)S(1)}, bf16[256,256]{1,0:T(8,128)(2,1)S(1)}, u32[]{:S(2)}, u32[]{:S(2)}) collective-permute-start(bf16[256,256]{1,0:T(8,128)(2,1)S(1)} %get-tuple-element.158), channel_id=1, source_target_pairs={{0,8},{2,10},{4,12},{6,14},{8,0},{10,2},{12,4},{14,6},{16,24},{18,... | collective-permute-start | bytes 393224 | tf_op jit(solution)/shard_map/ppermute | solution.py:317
  338.4 5.0 %collective-permute-start.34 = (bf16[256,256]{1,0:T(8,128)(2,1)S(1)}, bf16[256,256]{1,0:T(8,128)(2,1)S(1)}, u32[]{:S(2)}, u32[]{:S(2)}) collective-permute-start(bf16[256,256]{1,0:T(8,128)(2,1)S(1)} %get-tuple-element.160), channel_id=1, source_target_pairs={{0,2},{2,0},{4,6},{6,4},{8,10},{10,8},{12,14},{14,12},{16,18},{18,... | collective-permute-start | bytes 393224 | tf_op jit(solution)/shard_map/ppermute | solution.py:317
  339.9 5.0 %collective-permute-start.35 = (bf16[256,256]{1,0:T(8,128)(2,1)S(1)}, bf16[256,256]{1,0:T(8,128)(2,1)S(1)}, u32[]{:S(2)}, u32[]{:S(2)}) collective-permute-start(bf16[256,256]{1,0:T(8,128)(2,1)S(1)} %get-tuple-element.162), channel_id=1, source_target_pairs={{0,4},{2,6},{4,0},{6,2},{8,12},{10,14},{12,8},{14,10},{16,20},{18,... | collective-permute-start | bytes 393224 | tf_op jit(solution)/shard_map/ppermute | solution.py:317
  344.9 7.4 %collective-permute-start.36 = (bf16[128,768]{1,0:T(8,128)(2,1)S(1)}, bf16[128,768]{1,0:T(8,128)(2,1)S(1)}, u32[]{:S(2)}, u32[]{:S(2)}) collective-permute-start(bf16[128,768]{1,0:T(8,128)(2,1)S(1)} %get-tuple-element.164), channel_id=1, source_target_pairs={{0,16},{2,18},{4,20},{6,22},{8,24},{10,26},{12,28},{14,30},{16,0},... | collective-permute-start | bytes 589832 | tf_op jit(solution)/shard_map/ppermute | solution.py:317

commit v15 on v14

--- a/solution.py
+++ b/solution.py
@@ -380,7 +380,7 @@
     mid = tokens.shape[1] // 2
     near, far = swap(tokens, 2), swap(tokens, 3)
     x_own, y_own, xy_own = swap(tokens, 0), swap(tokens, 1), diagonal(tokens)
-    parts = (128, 96)
+    parts = (96, 128)
     packed = pack_first(listing, gate_proj, up_proj, down_proj, parts[0], share, devices)
     far, packed = tie((far, packed))
     corner = swap(far, 2)

time: 358 us -> 364 us (1.017)
  waiting for transfers between devices: 217 us -> 222 us
  Pallas kernels: 43.6 us -> 47.8 us
    pallas_call x4, Pallas kernels: 10.5 us -> 16.3 us  [down_product(): pl.pallas_call(functools.partial(down_kernel, rows, side, orders), out_sh...]
    ppermute x31, waiting for transfers between devices: 154 us -> 160 us  [swap(): return lax.ppermute(value, 'ep', [(i, i ^ 1 << bit) for i in range(size)])]
    unnamed x46 -> x48, local copies, waits for them, and re-layouts: 22.7 us -> 20.4 us
  transfers between devices with their start and end apart: 39 -> 39, of which waited for: 22 -> 19; matrix products, arithmetic and copies ran while one was open for 8% -> 7% of each run, Pallas kernels for 12% -> 13%
where the time goes in v15:
time: 364 us; the launch traced here: 359 us
  waiting for transfers between devices  222 us (61%)
  starting transfers between devices  49.4 us (14%)
  Pallas kernels  47.8 us (13%)
  local copies, waits for them, and re-layouts  27.9 us (8%)
  other arithmetic  11.4 us (3%)
    ppermute x31, waiting for transfers between devices, swap(): return lax.ppermute(value, 'ep', [(i, i ^ 1 << bit) for i in range(size)])  160 us
    all_to_all x2, waiting for transfers between devices, move(): return lax.all_to_all(packed, 'ep', 0, 0, tiled=True)  50.7 us
    ppermute x31, starting transfers between devices, swap(): return lax.ppermute(value, 'ep', [(i, i ^ 1 << bit) for i in range(size)])  29.3 us
    pallas_call x1, Pallas kernels, hidden_units(): pl.pallas_call(hidden_kernel, grid=(8,), out_shape=jax.ShapeDtypeStruct((...  23.2 us
    unnamed x48, local copies, waits for them, and re-layouts  20.4 us
    pallas_call x4, Pallas kernels, down_product(): pl.pallas_call(functools.partial(down_kernel, rows, side, orders), out_sh...  16.3 us
    all_to_all x2, starting transfers between devices, move(): return lax.all_to_all(packed, 'ep', 0, 0, tiled=True)  14.9 us
    ppermute x4, waiting for transfers between devices, exchange(): return lax.ppermute(value, 'et', [(0, 1), (1, 0)])  11.3 us
  transfers between devices with their start and end apart: 39, of which 19 were waited for; matrix products, arithmetic and copies ran while one was open for 7% of the time, Pallas kernels for 13%

profile of v15, /device:TPU:14, one launch (start us, length us, event | category | flops | bytes accessed | tf_op | source)
XLA Modules:
  0.0 358.6 jit_solution(10293524595414680318)
XLA Ops:
  0.0 2.6 collective-permute-start
  3.6 2.4 collective-permute-start.3
  6.5 0.9 select_reduce_fusion.4
  8.5 0.8 broadcast_compare_fusion
  9.4 0.9 select_reduce_fusion.share_ref
  10.4 2.0 copy-done
  12.4 2.0 copy-done.2
  14.4 2.0 copy-done.3
  16.5 5.1 %pack_first.1 = bf16[16,1920,128]{2,1,0:T(8,128)(2,1)} custom-call(s32[14]{0:T(128)S(1)} %select_reduce_fusion.3.list_ref, bf16[16,224,512]{2,1,0:T(8,128)(2,1)S(1)} %copy-done.2, bf16[16,224,512]{2,1,0:T(8,128)(2,1)S(1)} %copy-done.3, bf16[16,224,512]{2,1,0:T(8,128)(2,1)S(1)} %copy-done, f32[16,16,128]{2,1,0:T(8,128)S(1)} %select_reduce_fusion.share_ref), custom_call_target="tpu_custom_call" | custom-call | tf_op jit(solution)/shard_map/pack_first/pallas_call | solution.py:113
  21.6 0.9 collective-permute-done
  22.4 1.3 collective-permute-start.5
  23.8 1.6 collective-permute-done.4
  26.4 8.5 %collective-permute-done.5 = bf16[128,1792]{1,0:T(8,128)(2,1)S(1)} collective-permute-done((bf16[128,1792]{1,0:T(8,128)(2,1)S(1)}, bf16[128,1792]{1,0:T(8,128)(2,1)S(1)}, u32[]{:S(2)}, u32[]{:S(2)}) %collective-permute-start.5) | collective-permute-done | bytes 458784 | tf_op jit(solution)/shard_map/ppermute | solution.py:317
  35.7 7.9 %all-to-all-start = ((bf16[16,1920,128]{2,1,0:T(8,128)(2,1)}), bf16[16,1920,128]{2,1,0:T(8,128)(2,1)}, u32[]{:S(2)}, u32[]{:S(2)}) async-start(bf16[16,1920,128]{2,1,0:T(8,128)(2,1)} %pack_first.1), calls=%async_computation | async-start | bytes 15728640 | tf_op jit(solution)/shard_map/all_to_all | solution.py:366
  43.5 0.8 slice_dynamic-update-slice_fusion.13
  44.3 1.1 fusion.3
  45.4 0.9 fusion.5
  47.5 2.4 collective-permute-start.10
  51.2 0.8 slice_dynamic-update-slice_fusion.12
  52.0 0.9 constant_dynamic-update-slice_fusion.3
  52.9 87.8 %collective-permute-done.8 = bf16[128,896]{1,0:T(8,128)(2,1)S(1)} collective-permute-done((bf16[128,896]{1,0:T(8,128)(2,1)S(1)}, bf16[128,896]{1,0:T(8,128)(2,1)S(1)}, u32[]{:S(2)}, u32[]{:S(2)}) %collective-permute-start.8) | collective-permute-done | bytes 229408 | tf_op jit(solution)/shard_map/ppermute | solution.py:317
  141.4 0.9 slice_dynamic-update-slice_fusion
  142.3 0.8 slice_dynamic-update-slice_fusion.11
  143.1 0.9 constant_dynamic-update-slice_fusion.7
  144.7 7.3 %collective-permute-done.9 = bf16[640,896]{1,0:T(8,128)(2,1)S(1)} collective-permute-done((bf16[640,896]{1,0:T(8,128)(2,1)S(1)}, bf16[640,896]{1,0:T(8,128)(2,1)S(1)}, u32[]{:S(2)}, u32[]{:S(2)}) %collective-permute-start.9) | collective-permute-done | bytes 1146912 | tf_op jit(solution)/shard_map/ppermute | solution.py:317
  152.0 0.9 slice_dynamic-update-slice_fusion.1
  152.9 0.8 slice_dynamic-update-slice_fusion.10
  153.7 1.0 slice_dynamic-update-slice_fusion.2
  154.7 0.8 slice_dynamic-update-slice_fusion.5
  155.5 6.7 %pad_maximum_fusion.own_ref = bf16[2048,1792]{1,0:T(8,128)(2,1)} fusion(bf16[2048,896]{1,0:T(8,128)(2,1)} %get-tuple-element.176, bf16[2048,896]{1,0:T(8,128)(2,1)} %get-tuple-element.175), kind=kLoop, calls=%fused_computation | loop fusion | flops 14680064 | bytes 14680064 | tf_op jit(solution)/shard_map/concatenate | solution.py:405
  162.2 2.0 copy-done.1
  164.2 2.1 pack_rest.1
  167.0 7.2 %collective-permute-done.13.other_ref = bf16[2048,1792]{1,0:T(8,128)(2,1)} collective-permute-done((bf16[2048,1792]{1,0:T(8,128)(2,1)}, bf16[2048,1792]{1,0:T(8,128)(2,1)}, u32[]{:S(2)}, u32[]{:S(2)}) %collective-permute-start.13) | collective-permute-done | bytes 7340064 | tf_op jit(solution)/shard_map/ppermute | solution.py:363
  174.2 48.1 %all-to-all-done.packed_ref = bf16[16,1920,128]{2,1,0:T(8,128)(2,1)} async-done(((bf16[16,1920,128]{2,1,0:T(8,128)(2,1)}), bf16[16,1920,128]{2,1,0:T(8,128)(2,1)}, u32[]{:S(2)}, u32[]{:S(2)}) %all-to-all-start) | async-done | bytes 7864352 | tf_op jit(solution)/shard_map/all_to_all | solution.py:366
  222.3 7.0 %all-to-all-start.1 = ((bf16[16,448,128]{2,1,0:T(8,128)(2,1)}), bf16[16,448,128]{2,1,0:T(8,128)(2,1)}, u32[]{:S(2)}, u32[]{:S(2)}) async-start(bf16[16,448,128]{2,1,0:T(8,128)(2,1)} %pack_rest.1), calls=%async_computation.1 | async-start | bytes 3670016 | tf_op jit(solution)/shard_map/all_to_all | solution.py:366
  229.3 23.2 %hidden.1.own_h = bf16[2048,512]{1,0:T(8,128)(2,1)} custom-call(s32[2]{0:T(128)} %pad_add_fusion.at_ref, bf16[2048,1792]{1,0:T(8,128)(2,1)} %pad_maximum_fusion.own_ref, bf16[2048,1792]{1,0:T(8,128)(2,1)} %collective-permute-done.13.other_ref, bf16[16,1920,128]{2,1,0:T(8,128)(2,1)} %all-to-all-done.packed_ref), custom_call_target="tpu_custom_call" | custom-call | flops 15032385536 | bytes 25165824 | tf_op jit(solution)/shard_map/hidden/pallas_call | solution.py:196
  252.5 1.6 slice.85
  254.6 3.0 collective-permute-done.15.other_ref
  257.6 3.5 down_send.2
  263.5 3.5 down_keep.2
  267.0 2.6 all-to-all-done.1
  269.6 1.7 constant_dynamic-slice_fusion
  271.5 1.3 collective-permute-start.16
  272.8 1.1 collective-permute-done.26.other_ref
  273.9 4.7 %down_send.3 = (bf16[1024,384]{1,0:T(8,128)(2,1)S(1)}, bf16[1024,384]{1,0:T(8,128)(2,1)S(1)}, bf16[1024,256]{1,0:T(8,128)(2,1)S(1)}) custom-call(bf16[2048,512]{1,0:T(8,128)(2,1)S(1)} %copy-done.6, bf16[2048,512]{1,0:T(8,128)(2,1)} %collective-permute-done.14.other_h, bf16[8,448,128]{2,1,0:T(8,128)(2,1)S(1)} %get-tuple-element.143.own_ref, ...), custom_call_target="tpu_custom_call" | custom-call | flops 2147483648 | bytes 8388608 | tf_op jit(solution)/shard_map/down_send/pallas_call | solution.py:257
  278.7 1.3 collective-permute-start.27
  280.0 2.0 collective-permute-start.17
  282.0 4.3 %collective-permute-done.16.refs_1_ = bf16[1024,256]{1,0:T(8,128)(2,1)S(1)} collective-permute-done((bf16[1024,256]{1,0:T(8,128)(2,1)S(1)}, bf16[1024,256]{1,0:T(8,128)(2,1)S(1)}, u32[]{:S(2)}, u32[]{:S(2)}) %collective-permute-start.16) | collective-permute-done | bytes 524320 | tf_op jit(solution)/shard_map/ppermute | solution.py:317
  286.3 24.2 %collective-permute-done.17.refs_3_ = bf16[1024,256]{1,0:T(8,128)(2,1)S(1)} collective-permute-done((bf16[1024,256]{1,0:T(8,128)(2,1)S(1)}, bf16[1024,256]{1,0:T(8,128)(2,1)S(1)}, u32[]{:S(2)}, u32[]{:S(2)}) %collective-permute-start.17) | collective-permute-done | bytes 524320 | tf_op jit(solution)/shard_map/ppermute | solution.py:317
  311.1 4.6 %down_keep.3 = (f32[1024,384]{1,0:T(8,128)S(1)}, f32[1024,384]{1,0:T(8,128)S(1)}, f32[1024,256]{1,0:T(8,128)S(1)}) custom-call(bf16[2048,512]{1,0:T(8,128)(2,1)S(1)} %copy-done.6, bf16[2048,512]{1,0:T(8,128)(2,1)} %collective-permute-done.14.other_h, bf16[8,448,128]{2,1,0:T(8,128)(2,1)S(1)} %get-tuple-element.143.own_ref, ...), custom_call_target="tpu_custom_call" | custom-call | flops 2147483648 | bytes 8388608 | tf_op jit(solution)/shard_map/down_keep/pallas_call | solution.py:257
  316.1 1.8 collective-permute-start.30
  318.0 2.0 collective-permute-start.20
  320.7 1.3 collective-permute-start.32
  322.0 11.0 %collective-permute-done.20.refs_3_ = bf16[512,256]{1,0:T(8,128)(2,1)S(1)} collective-permute-done((bf16[512,256]{1,0:T(8,128)(2,1)S(1)}, bf16[512,256]{1,0:T(8,128)(2,1)S(1)}, u32[]{:S(2)}, u32[]{:S(2)}) %collective-permute-start.20) | collective-permute-done | bytes 262176 | tf_op jit(solution)/shard_map/ppermute | solution.py:317
  335.0 1.8 collective-permute-start.33
  336.8 1.3 collective-permute-start.34
  338.6 0.9 collective-permute-done.23.refs_3_
  339.6 1.2 collective-permute-start.25
  340.8 2.1 collective-permute-start.35
  342.9 2.9 collective-permute-done.35.refs_5_
  345.9 1.8 collective-permute-start.36
  347.7 2.7 collective-permute-done.25
  350.7 6.7 %collective-permute-done.36 = bf16[128,1024]{1,0:T(8,128)(2,1)S(1)} collective-permute-done((bf16[128,1024]{1,0:T(8,128)(2,1)S(1)}, bf16[128,1024]{1,0:T(8,128)(2,1)S(1)}, u32[]{:S(2)}, u32[]{:S(2)}) %collective-permute-start.36) | collective-permute-done | bytes 262176 | tf_op jit(solution)/shard_map/ppermute | solution.py:317
  357.6 1.0 copy.15
  (101 shorter events, 17.0 us)
Async XLA Ops:
  0.0 22.4 %collective-permute-start = (bf16[128,1792]{1,0:T(8,128)(2,1)}, bf16[128,1792]{1,0:T(8,128)(2,1)S(1)}, u32[]{:S(2)}, u32[]{:S(2)}) collective-permute-start(bf16[128,1792]{1,0:T(8,128)(2,1)} %param.9), channel_id=1, source_target_pairs={{0,16},{2,18},{4,20},{6,22},{8,24},{10,26},{12,28},{14,30},{16,0},... | collective-permute-start | bytes 1376264 | tf_op jit(solution)/shard_map/ppermute | solution.py:317
  2.6 23.5 %collective-permute-start.1 = (bf16[128,1792]{1,0:T(8,128)(2,1)}, bf16[128,1792]{1,0:T(8,128)(2,1)S(1)}, u32[]{:S(2)}, u32[]{:S(2)}) collective-permute-start(bf16[128,1792]{1,0:T(8,128)(2,1)} %param.9), channel_id=1, source_target_pairs={{0,2},{2,0},{4,6},{6,4},{8,10},{10,8},{12,14},{14,12},{16,18},{18,... | collective-permute-start | bytes 1376264 | tf_op jit(solution)/shard_map/ppermute | solution.py:317
  3.1 23.2 %collective-permute-start.2 = (bf16[128,1792]{1,0:T(8,128)(2,1)}, bf16[128,1792]{1,0:T(8,128)(2,1)S(1)}, u32[]{:S(2)}, u32[]{:S(2)}) collective-permute-start(bf16[128,1792]{1,0:T(8,128)(2,1)} %param.9), channel_id=1, source_target_pairs={{0,4},{2,6},{4,0},{6,2},{8,12},{10,14},{12,8},{14,10},{16,20},{18,... | collective-permute-start | bytes 1376264 | tf_op jit(solution)/shard_map/ppermute | solution.py:317
  3.6 22.7 %collective-permute-start.3 = (bf16[128,1792]{1,0:T(8,128)(2,1)}, bf16[128,1792]{1,0:T(8,128)(2,1)S(1)}, u32[]{:S(2)}, u32[]{:S(2)}) collective-permute-start(bf16[128,1792]{1,0:T(8,128)(2,1)} %param.9), channel_id=1, source_target_pairs={{0,6},{2,4},{4,2},{6,0},{8,14},{10,12},{12,10},{14,8},{16,22},{18,... | collective-permute-start | bytes 1376264 | tf_op jit(solution)/shard_map/ppermute | solution.py:378
  6.1 19.3 %collective-permute-start.4 = (bf16[128,1792]{1,0:T(8,128)(2,1)}, bf16[128,1792]{1,0:T(8,128)(2,1)S(1)}, u32[]{:S(2)}, u32[]{:S(2)}) collective-permute-start(bf16[128,1792]{1,0:T(8,128)(2,1)} %param.9), channel_id=1, source_target_pairs={{0,8},{2,10},{4,12},{6,14},{8,0},{10,2},{12,4},{14,6},{16,24},{18,... | collective-permute-start | bytes 1376264 | tf_op jit(solution)/shard_map/ppermute | solution.py:317
  10.4 2.0 copy-start
  12.4 2.0 copy-start.2
  14.4 2.0 copy-start.3
  22.4 12.4 %collective-permute-start.5 = (bf16[128,1792]{1,0:T(8,128)(2,1)S(1)}, bf16[128,1792]{1,0:T(8,128)(2,1)S(1)}, u32[]{:S(2)}, u32[]{:S(2)}) collective-permute-start(bf16[128,1792]{1,0:T(8,128)(2,1)S(1)} %collective-permute-done), channel_id=1, source_target_pairs={{0,8},{2,10},{4,12},{6,14},{8,0},{10,2},{12,4},{14,6},{16,24},{18,... | collective-permute-start | bytes 1376264 | tf_op jit(solution)/shard_map/ppermute | solution.py:317
  25.5 9.6 %collective-permute-start.6 = (bf16[256,896]{1,0:T(8,128)(2,1)S(1)}, bf16[256,896]{1,0:T(8,128)(2,1)S(1)}, u32[]{:S(2)}, u32[]{:S(2)}) collective-permute-start(bf16[256,896]{1,0:T(8,128)(2,1)S(1)} %get-tuple-element.174), channel_id=1, source_target_pairs={{0,4},{2,6},{4,0},{6,2},{8,12},{10,14},{12,8},{14,10},{16,20},{18,... | collective-permute-start | bytes 1376264 | tf_op jit(solution)/shard_map/ppermute | solution.py:317
  26.1 17.4 %copy-start.13 = (bf16[128,1792]{1,0:T(8,128)(2,1)S(1)}, bf16[128,1792]{1,0:T(8,128)(2,1)}, u32[]{:S(2)}) copy-start(bf16[128,1792]{1,0:T(8,128)(2,1)} %param.9) | copy-start | bytes 1376260
  26.1 9.6 %collective-permute-start.7 = (bf16[256,896]{1,0:T(8,128)(2,1)S(1)}, bf16[256,896]{1,0:T(8,128)(2,1)S(1)}, u32[]{:S(2)}, u32[]{:S(2)}) collective-permute-start(bf16[256,896]{1,0:T(8,128)(2,1)S(1)} %get-tuple-element.173), channel_id=1, source_target_pairs={{0,2},{2,0},{4,6},{6,4},{8,10},{10,8},{12,14},{14,12},{16,18},{18,... | collective-permute-start | bytes 1376264 | tf_op jit(solution)/shard_map/ppermute | solution.py:317
  26.4 8.8 %copy-start.14 = (bf16[128,1792]{1,0:T(8,128)(2,1)}, bf16[128,1792]{1,0:T(8,128)(2,1)S(1)}, u32[]{:S(2)}) copy-start(bf16[128,1792]{1,0:T(8,128)(2,1)S(1)} %collective-permute-done.2) | copy-start | bytes 1376260
  34.9 0.8 copy-start.16
  35.7 186.6 %all-to-all-start = ((bf16[16,1920,128]{2,1,0:T(8,128)(2,1)}), bf16[16,1920,128]{2,1,0:T(8,128)(2,1)}, u32[]{:S(2)}, u32[]{:S(2)}) async-start(bf16[16,1920,128]{2,1,0:T(8,128)(2,1)} %pack_first.1), calls=%async_computation | async-start | bytes 15728640 | tf_op jit(solution)/shard_map/all_to_all | solution.py:366
  43.5 1.9 copy-start.17
  45.4 5.8 %copy-start.15 = (bf16[128,1792]{1,0:T(8,128)(2,1)S(1)}, bf16[128,1792]{1,0:T(8,128)(2,1)}, u32[]{:S(2)}) copy-start(bf16[128,1792]{1,0:T(8,128)(2,1)} %copy-done.14) | copy-start | bytes 1376260
  46.3 95.0 %collective-permute-start.11 = (bf16[640,896]{1,0:T(8,128)(2,1)S(1)}, bf16[640,896]{1,0:T(8,128)(2,1)S(1)}, u32[]{:S(2)}, u32[]{:S(2)}) collective-permute-start(bf16[640,896]{1,0:T(8,128)(2,1)S(1)} %pad_maximum_fusion.2), channel_id=1, source_target_pairs={{0,4},{2,6},{4,0},{6,2},{8,12},{10,14},{12,8},{14,10},{16,20},{18,... | collective-permute-start | bytes 3440648 | tf_op jit(solution)/shard_map/ppermute | solution.py:317
  47.0 97.0 %collective-permute-start.12 = (bf16[128,896]{1,0:T(8,128)(2,1)S(1)}, bf16[128,896]{1,0:T(8,128)(2,1)S(1)}, u32[]{:S(2)}, u32[]{:S(2)}) collective-permute-start(bf16[128,896]{1,0:T(8,128)(2,1)S(1)} %get-tuple-element.184), channel_id=1, source_target_pairs={{0,2},{2,0},{4,6},{6,4},{8,10},{10,8},{12,14},{14,12},{16,18},{18,... | collective-permute-start | bytes 688136 | tf_op jit(solution)/shard_map/ppermute | solution.py:317
  47.5 107.2 %collective-permute-start.10 = (bf16[128,1792]{1,0:T(8,128)(2,1)S(1)}, bf16[128,1792]{1,0:T(8,128)(2,1)S(1)}, u32[]{:S(2)}, u32[]{:S(2)}) collective-permute-start(bf16[128,1792]{1,0:T(8,128)(2,1)S(1)} %copy-done.17), channel_id=1, source_target_pairs={{0,6},{2,4},{4,2},{6,0},{8,14},{10,12},{12,10},{14,8},{16,22},{18,... | collective-permute-start | bytes 1376264 | tf_op jit(solution)/shard_map/ppermute | solution.py:378
  49.9 90.7 %collective-permute-start.8 = (bf16[128,896]{1,0:T(8,128)(2,1)S(1)}, bf16[128,896]{1,0:T(8,128)(2,1)S(1)}, u32[]{:S(2)}, u32[]{:S(2)}) collective-permute-start(bf16[128,896]{1,0:T(8,128)(2,1)S(1)} %get-tuple-element.181), channel_id=1, source_target_pairs={{0,4},{2,6},{4,0},{6,2},{8,12},{10,14},{12,8},{14,10},{16,20},{18,... | collective-permute-start | bytes 688136 | tf_op jit(solution)/shard_map/ppermute | solution.py:317
  50.6 101.4 %collective-permute-start.9 = (bf16[640,896]{1,0:T(8,128)(2,1)S(1)}, bf16[640,896]{1,0:T(8,128)(2,1)S(1)}, u32[]{:S(2)}, u32[]{:S(2)}) collective-permute-start(bf16[640,896]{1,0:T(8,128)(2,1)S(1)} %pad_maximum_fusion.1), channel_id=1, source_target_pairs={{0,2},{2,0},{4,6},{6,4},{8,10},{10,8},{12,14},{14,12},{16,18},{18,... | collective-permute-start | bytes 3440648 | tf_op jit(solution)/shard_map/ppermute | solution.py:317
  162.2 12.0 %collective-permute-start.13 = (bf16[2048,1792]{1,0:T(8,128)(2,1)}, bf16[2048,1792]{1,0:T(8,128)(2,1)}, u32[]{:S(2)}, u32[]{:S(2)}) collective-permute-start(bf16[2048,1792]{1,0:T(8,128)(2,1)} %pad_maximum_fusion.own_ref), channel_id=1, source_target_pairs={{0,1},{1,0},{2,3},{3,2},{4,5},{5,4},{6,7},{7,6},{8,9},{9,8},{10,11... | collective-permute-start | bytes 22020104 | tf_op jit(solution)/shard_map/ppermute | solution.py:363
  162.2 2.0 copy-start.1
  222.3 47.4 %all-to-all-start.1 = ((bf16[16,448,128]{2,1,0:T(8,128)(2,1)}), bf16[16,448,128]{2,1,0:T(8,128)(2,1)}, u32[]{:S(2)}, u32[]{:S(2)}) async-start(bf16[16,448,128]{2,1,0:T(8,128)(2,1)} %pack_rest.1), calls=%async_computation.1 | async-start | bytes 3670016 | tf_op jit(solution)/shard_map/all_to_all | solution.py:366
  252.5 5.2 %copy-start.4 = (bf16[2048,512]{1,0:T(8,128)(2,1)S(1)}, bf16[2048,512]{1,0:T(8,128)(2,1)}, u32[]{:S(2)}) copy-start(bf16[2048,512]{1,0:T(8,128)(2,1)} %hidden.1.own_h) | copy-start | bytes 6291460
  252.5 5.1 %collective-permute-start.14 = (bf16[2048,512]{1,0:T(8,128)(2,1)}, bf16[2048,512]{1,0:T(8,128)(2,1)}, u32[]{:S(2)}, u32[]{:S(2)}) collective-permute-start(bf16[2048,512]{1,0:T(8,128)(2,1)} %hidden.1.own_h), channel_id=1, source_target_pairs={{0,1},{1,0},{2,3},{3,2},{4,5},{5,4},{6,7},{7,6},{8,9},{9,8},{10,11... | collective-permute-start | bytes 6291464 | tf_op jit(solution)/shard_map/ppermute | solution.py:363
  254.2 9.4 %copy-start.5 = (bf16[2048,512]{1,0:T(8,128)(2,1)S(1)}, bf16[2048,512]{1,0:T(8,128)(2,1)}, u32[]{:S(2)}) copy-start(bf16[2048,512]{1,0:T(8,128)(2,1)} %hidden.1.own_h) | copy-start | bytes 6291460
  254.2 3.4 collective-permute-start.15
  261.1 0.8 copy-start.7
  261.9 0.8 copy-start.9
  262.7 0.8 copy-start.11
  269.6 1.8 copy-start.12
  269.6 4.3 %copy-start.6 = (bf16[2048,512]{1,0:T(8,128)(2,1)S(1)}, bf16[2048,512]{1,0:T(8,128)(2,1)}, u32[]{:S(2)}) copy-start(bf16[2048,512]{1,0:T(8,128)(2,1)} %hidden.1.own_h) | copy-start | bytes 6291460
  271.4 2.5 collective-permute-start.26
  271.5 14.8 %collective-permute-start.16 = (bf16[1024,256]{1,0:T(8,128)(2,1)S(1)}, bf16[1024,256]{1,0:T(8,128)(2,1)S(1)}, u32[]{:S(2)}, u32[]{:S(2)}) collective-permute-start(bf16[1024,256]{1,0:T(8,128)(2,1)S(1)} %copy-done.12), channel_id=1, source_target_pairs={{0,2},{2,0},{4,6},{6,4},{8,10},{10,8},{12,14},{14,12},{16,18},{18,... | collective-permute-start | bytes 1572872 | tf_op jit(solution)/shard_map/ppermute | solution.py:317
  273.9 6.1 %copy-start.10 = (bf16[1024,256]{1,0:T(8,128)(2,1)S(1)}, bf16[1024,256]{1,0:T(8,128)(2,1)}, u32[]{:S(2)}) copy-start(bf16[1024,256]{1,0:T(8,128)(2,1)} %copy-done.9) | copy-start | bytes 1572868
  273.9 8.1 %copy-start.8 = (bf16[1024,256]{1,0:T(8,128)(2,1)S(1)}, bf16[1024,256]{1,0:T(8,128)(2,1)}, u32[]{:S(2)}) copy-start(bf16[1024,256]{1,0:T(8,128)(2,1)} %copy-done.7) | copy-start | bytes 1572868
  278.7 37.1 %collective-permute-start.27 = (bf16[1024,384]{1,0:T(8,128)(2,1)S(1)}, bf16[1024,384]{1,0:T(8,128)(2,1)S(1)}, u32[]{:S(2)}, u32[]{:S(2)}) collective-permute-start(bf16[1024,384]{1,0:T(8,128)(2,1)S(1)} %get-tuple-element.146), channel_id=1, source_target_pairs={{0,2},{2,0},{4,6},{6,4},{8,10},{10,8},{12,14},{14,12},{16,18},{18,... | collective-permute-start | bytes 2359304 | tf_op jit(solution)/shard_map/ppermute | solution.py:317
  280.0 35.8 %collective-permute-start.28 = (bf16[1024,384]{1,0:T(8,128)(2,1)S(1)}, bf16[1024,384]{1,0:T(8,128)(2,1)S(1)}, u32[]{:S(2)}, u32[]{:S(2)}) collective-permute-start(bf16[1024,384]{1,0:T(8,128)(2,1)S(1)} %get-tuple-element.148), channel_id=1, source_target_pairs={{0,4},{2,6},{4,0},{6,2},{8,12},{10,14},{12,8},{14,10},{16,20},{18,... | collective-permute-start | bytes 2359304 | tf_op jit(solution)/shard_map/ppermute | solution.py:317
  280.0 30.5 %collective-permute-start.17 = (bf16[1024,256]{1,0:T(8,128)(2,1)S(1)}, bf16[1024,256]{1,0:T(8,128)(2,1)S(1)}, u32[]{:S(2)}, u32[]{:S(2)}) collective-permute-start(bf16[1024,256]{1,0:T(8,128)(2,1)S(1)} %copy-done.10), channel_id=1, source_target_pairs={{0,4},{2,6},{4,0},{6,2},{8,12},{10,14},{12,8},{14,10},{16,20},{18,... | collective-permute-start | bytes 1572872 | tf_op jit(solution)/shard_map/ppermute | solution.py:317
  282.0 28.5 %collective-permute-start.18 = (bf16[1024,256]{1,0:T(8,128)(2,1)S(1)}, bf16[1024,256]{1,0:T(8,128)(2,1)S(1)}, u32[]{:S(2)}, u32[]{:S(2)}) collective-permute-start(bf16[1024,256]{1,0:T(8,128)(2,1)S(1)} %copy-done.8), channel_id=1, source_target_pairs={{0,8},{2,10},{4,12},{6,14},{8,0},{10,2},{12,4},{14,6},{16,24},{18,... | collective-permute-start | bytes 1572872 | tf_op jit(solution)/shard_map/ppermute | solution.py:317
  286.3 29.5 %collective-permute-start.29 = (bf16[1024,256]{1,0:T(8,128)(2,1)S(1)}, bf16[1024,256]{1,0:T(8,128)(2,1)S(1)}, u32[]{:S(2)}, u32[]{:S(2)}) collective-permute-start(bf16[1024,256]{1,0:T(8,128)(2,1)S(1)} %get-tuple-element.150), channel_id=1, source_target_pairs={{0,8},{2,10},{4,12},{6,14},{8,0},{10,2},{12,4},{14,6},{16,24},{18,... | collective-permute-start | bytes 1572872 | tf_op jit(solution)/shard_map/ppermute | solution.py:317
  310.8 10.0 %collective-permute-start.19 = (bf16[512,256]{1,0:T(8,128)(2,1)S(1)}, bf16[512,256]{1,0:T(8,128)(2,1)S(1)}, u32[]{:S(2)}, u32[]{:S(2)}) collective-permute-start(bf16[512,256]{1,0:T(8,128)(2,1)S(1)} %get-tuple-element.120), channel_id=1, source_target_pairs={{0,4},{2,6},{4,0},{6,2},{8,12},{10,14},{12,8},{14,10},{16,20},{18,... | collective-permute-start | bytes 786440 | tf_op jit(solution)/shard_map/ppermute | solution.py:317
  316.1 18.7 %collective-permute-start.30 = (bf16[512,384]{1,0:T(8,128)(2,1)S(1)}, bf16[512,384]{1,0:T(8,128)(2,1)S(1)}, u32[]{:S(2)}, u32[]{:S(2)}) collective-permute-start(bf16[512,384]{1,0:T(8,128)(2,1)S(1)} %get-tuple-element.152), channel_id=1, source_target_pairs={{0,4},{2,6},{4,0},{6,2},{8,12},{10,14},{12,8},{14,10},{16,20},{18,... | collective-permute-start | bytes 1179656 | tf_op jit(solution)/shard_map/ppermute | solution.py:317
  317.9 16.8 %collective-permute-start.31 = (bf16[512,384]{1,0:T(8,128)(2,1)S(1)}, bf16[512,384]{1,0:T(8,128)(2,1)S(1)}, u32[]{:S(2)}, u32[]{:S(2)}) collective-permute-start(bf16[512,384]{1,0:T(8,128)(2,1)S(1)} %get-tuple-element.154), channel_id=1, source_target_pairs={{0,8},{2,10},{4,12},{6,14},{8,0},{10,2},{12,4},{14,6},{16,24},{18,... | collective-permute-start | bytes 1179656 | tf_op jit(solution)/shard_map/ppermute | solution.py:317
  318.0 15.1 %collective-permute-start.20 = (bf16[512,256]{1,0:T(8,128)(2,1)S(1)}, bf16[512,256]{1,0:T(8,128)(2,1)S(1)}, u32[]{:S(2)}, u32[]{:S(2)}) collective-permute-start(bf16[512,256]{1,0:T(8,128)(2,1)S(1)} %get-tuple-element.122), channel_id=1, source_target_pairs={{0,8},{2,10},{4,12},{6,14},{8,0},{10,2},{12,4},{14,6},{16,24},{18,... | collective-permute-start | bytes 786440 | tf_op jit(solution)/shard_map/ppermute | solution.py:317
  320.0 13.0 %collective-permute-start.21 = (bf16[512,256]{1,0:T(8,128)(2,1)S(1)}, bf16[512,256]{1,0:T(8,128)(2,1)S(1)}, u32[]{:S(2)}, u32[]{:S(2)}) collective-permute-start(bf16[512,256]{1,0:T(8,128)(2,1)S(1)} %get-tuple-element.124), channel_id=1, source_target_pairs={{0,2},{2,0},{4,6},{6,4},{8,10},{10,8},{12,14},{14,12},{16,18},{18,... | collective-permute-start | bytes 786440 | tf_op jit(solution)/shard_map/ppermute | solution.py:317
  320.7 13.5 %collective-permute-start.32 = (bf16[512,256]{1,0:T(8,128)(2,1)S(1)}, bf16[512,256]{1,0:T(8,128)(2,1)S(1)}, u32[]{:S(2)}, u32[]{:S(2)}) collective-permute-start(bf16[512,256]{1,0:T(8,128)(2,1)S(1)} %get-tuple-element.156), channel_id=1, source_target_pairs={{0,2},{2,0},{4,6},{6,4},{8,10},{10,8},{12,14},{14,12},{16,18},{18,... | collective-permute-start | bytes 786440 | tf_op jit(solution)/shard_map/ppermute | solution.py:317
  333.1 5.5 %collective-permute-start.22 = (bf16[256,256]{1,0:T(8,128)(2,1)S(1)}, bf16[256,256]{1,0:T(8,128)(2,1)S(1)}, u32[]{:S(2)}, u32[]{:S(2)}) collective-permute-start(bf16[256,256]{1,0:T(8,128)(2,1)S(1)} %get-tuple-element.126), channel_id=1, source_target_pairs={{0,8},{2,10},{4,12},{6,14},{8,0},{10,2},{12,4},{14,6},{16,24},{18,... | collective-permute-start | bytes 393224 | tf_op jit(solution)/shard_map/ppermute | solution.py:317
  333.5 6.0 %collective-permute-start.23 = (bf16[256,256]{1,0:T(8,128)(2,1)S(1)}, bf16[256,256]{1,0:T(8,128)(2,1)S(1)}, u32[]{:S(2)}, u32[]{:S(2)}) collective-permute-start(bf16[256,256]{1,0:T(8,128)(2,1)S(1)} %get-tuple-element.128), channel_id=1, source_target_pairs={{0,2},{2,0},{4,6},{6,4},{8,10},{10,8},{12,14},{14,12},{16,18},{18,... | collective-permute-start | bytes 393224 | tf_op jit(solution)/shard_map/ppermute | solution.py:317
  334.3 5.3 %collective-permute-start.24 = (bf16[256,256]{1,0:T(8,128)(2,1)S(1)}, bf16[256,256]{1,0:T(8,128)(2,1)S(1)}, u32[]{:S(2)}, u32[]{:S(2)}) collective-permute-start(bf16[256,256]{1,0:T(8,128)(2,1)S(1)} %get-tuple-element.130), channel_id=1, source_target_pairs={{0,4},{2,6},{4,0},{6,2},{8,12},{10,14},{12,8},{14,10},{16,20},{18,... | collective-permute-start | bytes 393224 | tf_op jit(solution)/shard_map/ppermute | solution.py:317
  335.0 10.8 %collective-permute-start.33 = (bf16[256,384]{1,0:T(8,128)(2,1)S(1)}, bf16[256,384]{1,0:T(8,128)(2,1)S(1)}, u32[]{:S(2)}, u32[]{:S(2)}) collective-permute-start(bf16[256,384]{1,0:T(8,128)(2,1)S(1)} %get-tuple-element.158), channel_id=1, source_target_pairs={{0,8},{2,10},{4,12},{6,14},{8,0},{10,2},{12,4},{14,6},{16,24},{18,... | collective-permute-start | bytes 589832 | tf_op jit(solution)/shard_map/ppermute | solution.py:317
  336.8 9.0 %collective-permute-start.34 = (bf16[256,384]{1,0:T(8,128)(2,1)S(1)}, bf16[256,384]{1,0:T(8,128)(2,1)S(1)}, u32[]{:S(2)}, u32[]{:S(2)}) collective-permute-start(bf16[256,384]{1,0:T(8,128)(2,1)S(1)} %get-tuple-element.160), channel_id=1, source_target_pairs={{0,2},{2,0},{4,6},{6,4},{8,10},{10,8},{12,14},{14,12},{16,18},{18,... | collective-permute-start | bytes 589832 | tf_op jit(solution)/shard_map/ppermute | solution.py:317
  339.6 10.9 %collective-permute-start.25 = (bf16[128,768]{1,0:T(8,128)(2,1)S(1)}, bf16[128,768]{1,0:T(8,128)(2,1)S(1)}, u32[]{:S(2)}, u32[]{:S(2)}) collective-permute-start(bf16[128,768]{1,0:T(8,128)(2,1)S(1)} %get-tuple-element.132), channel_id=1, source_target_pairs={{0,16},{2,18},{4,20},{6,22},{8,24},{10,26},{12,28},{14,30},{16,0},... | collective-permute-start | bytes 589832 | tf_op jit(solution)/shard_map/ppermute | solution.py:317
  340.8 5.0 %collective-permute-start.35 = (bf16[256,256]{1,0:T(8,128)(2,1)S(1)}, bf16[256,256]{1,0:T(8,128)(2,1)S(1)}, u32[]{:S(2)}, u32[]{:S(2)}) collective-permute-start(bf16[256,256]{1,0:T(8,128)(2,1)S(1)} %get-tuple-element.162), channel_id=1, source_target_pairs={{0,4},{2,6},{4,0},{6,2},{8,12},{10,14},{12,8},{14,10},{16,20},{18,... | collective-permute-start | bytes 393224 | tf_op jit(solution)/shard_map/ppermute | solution.py:317
  345.9 11.4 %collective-permute-start.36 = (bf16[128,1024]{1,0:T(8,128)(2,1)S(1)}, bf16[128,1024]{1,0:T(8,128)(2,1)S(1)}, u32[]{:S(2)}, u32[]{:S(2)}) collective-permute-start(bf16[128,1024]{1,0:T(8,128)(2,1)S(1)} %get-tuple-element.164), channel_id=1, source_target_pairs={{0,16},{2,18},{4,20},{6,22},{8,24},{10,26},{12,28},{14,30},{16,0},... | collective-permute-start | bytes 786440 | tf_op jit(solution)/shard_map/ppermute | solution.py:317

commit v16 on v15

--- a/solution.py
+++ b/solution.py
@@ -432,11 +432,10 @@
     def products(down, rows_in, orders, before=None):
         own = lax.dynamic_slice_in_dim(down, core * group, group, 0)
         other = exchange(lax.dynamic_slice_in_dim(down, (1 - core) * group, group, 0))
-        args = (hidden, hidden_other, own, other)
+        args, _ = tie(((hidden, hidden_other, own, other), before))
         sent = down_product(*args, rows_in, 1, orders, jnp.bfloat16, "down_send")
         sent, args = tie((sent, args))
         come = [swap(value, order[0]) for value, order in zip(sent, orders)]
-        args, _ = tie((args, before))
         kept = down_product(*args, rows_in, 0, orders, jnp.float32, "down_keep")
         return kept, come
 
@@ -452,7 +451,6 @@
         return (keep + come.astype(jnp.float32)).astype(jnp.bfloat16)
 
     kept0, come0 = products(down0, parts[0], THIRDS)
-    down1, kept0 = tie((down1, kept0))
     kept1, come1 = products(down1, parts[1], THIRDS, before=come0)
     kept0, come0 = stage(kept0, come0, 1, THIRDS)
     kept1, come1 = stage(kept1, come1, 1, THIRDS)

time: 364 us -> 361 us (level)
  local copies, waits for them, and re-layouts: 27.9 us -> 18.1 us
  waiting for transfers between devices: 222 us -> 230 us
    all_to_all x2, waiting for transfers between devices: 50.7 us -> 61.8 us  [move(): return lax.all_to_all(packed, 'ep', 0, 0, tiled=True)]
    unnamed x48 -> x38, local copies, waits for them, and re-layouts: 20.4 us -> 12.3 us
  transfers between devices with their start and end apart: 39 -> 39, of which waited for: 19 -> 21; matrix products, arithmetic and copies ran while one was open for 7% -> 5% of each run, Pallas kernels for 13% -> 12%
where the time goes in v16:
time: 361 us; the launch traced here: 356 us
  waiting for transfers between devices  230 us (64%)
  starting transfers between devices  49.2 us (14%)
  Pallas kernels  46.4 us (13%)
  local copies, waits for them, and re-layouts  18.1 us (5%)
  other arithmetic  11.5 us (3%)
    ppermute x31, waiting for transfers between devices, swap(): return lax.ppermute(value, 'ep', [(i, i ^ 1 << bit) for i in range(size)])  159 us
    all_to_all x2, waiting for transfers between devices, move(): return lax.all_to_all(packed, 'ep', 0, 0, tiled=True)  61.8 us
    ppermute x31, starting transfers between devices, swap(): return lax.ppermute(value, 'ep', [(i, i ^ 1 << bit) for i in range(size)])  28.9 us
    pallas_call x1, Pallas kernels, hidden_units(): pl.pallas_call(hidden_kernel, grid=(8,), out_shape=jax.ShapeDtypeStruct((...  23.1 us
    pallas_call x4, Pallas kernels, down_product(): pl.pallas_call(functools.partial(down_kernel, rows, side, orders), out_sh...  16.3 us
    all_to_all x2, starting transfers between devices, move(): return lax.all_to_all(packed, 'ep', 0, 0, tiled=True)  14.9 us
    unnamed x38, local copies, waits for them, and re-layouts  12.3 us
    ppermute x4, waiting for transfers between devices, exchange(): return lax.ppermute(value, 'et', [(0, 1), (1, 0)])  9.86 us
  transfers between devices with their start and end apart: 39, of which 21 were waited for; matrix products, arithmetic and copies ran while one was open for 5% of the time, Pallas kernels for 12%

profile of v16, /device:TPU:14, one launch (start us, length us, event | category | flops | bytes accessed | tf_op | source)
XLA Modules:
  0.0 355.9 jit_solution(13315571483649318531)
XLA Ops:
  0.0 2.6 collective-permute-start
  3.6 2.4 collective-permute-start.3
  6.5 0.9 select_reduce_fusion.4
  7.8 0.7 select_reduce_fusion.1
  8.5 0.8 broadcast_compare_fusion
  9.4 0.9 select_reduce_fusion.share_ref
  10.4 2.0 copy-done
  12.4 2.0 copy-done.3
  14.4 2.0 copy-done.4
  16.5 5.1 %pack_first.1 = bf16[16,1920,128]{2,1,0:T(8,128)(2,1)} custom-call(s32[14]{0:T(128)S(1)} %select_reduce_fusion.3.list_ref, bf16[16,224,512]{2,1,0:T(8,128)(2,1)S(1)} %copy-done.3, bf16[16,224,512]{2,1,0:T(8,128)(2,1)S(1)} %copy-done.4, bf16[16,224,512]{2,1,0:T(8,128)(2,1)S(1)} %copy-done, f32[16,16,128]{2,1,0:T(8,128)S(1)} %select_reduce_fusion.share_ref), custom_call_target="tpu_custom_call" | custom-call | tf_op jit(solution)/shard_map/pack_first/pallas_call | solution.py:113
  21.6 0.8 collective-permute-done
  22.4 1.3 collective-permute-start.5
  23.8 1.6 collective-permute-done.4
  26.4 8.5 %collective-permute-done.5 = bf16[128,1792]{1,0:T(8,128)(2,1)S(1)} collective-permute-done((bf16[128,1792]{1,0:T(8,128)(2,1)S(1)}, bf16[128,1792]{1,0:T(8,128)(2,1)S(1)}, u32[]{:S(2)}, u32[]{:S(2)}) %collective-permute-start.5) | collective-permute-done | bytes 458784 | tf_op jit(solution)/shard_map/ppermute | solution.py:317
  35.7 7.9 %all-to-all-start = ((bf16[16,1920,128]{2,1,0:T(8,128)(2,1)}), bf16[16,1920,128]{2,1,0:T(8,128)(2,1)}, u32[]{:S(2)}, u32[]{:S(2)}) async-start(bf16[16,1920,128]{2,1,0:T(8,128)(2,1)} %pack_first.1), calls=%async_computation | async-start | bytes 15728640 | tf_op jit(solution)/shard_map/all_to_all | solution.py:366
  43.8 0.7 copy-done.12
  44.7 0.6 collective-permute-start.11
  45.9 2.4 collective-permute-start.10
  49.0 0.6 collective-permute-start.9
  49.7 90.9 %collective-permute-done.8 = bf16[128,896]{1,0:T(8,128)(2,1)S(1)} collective-permute-done((bf16[128,896]{1,0:T(8,128)(2,1)S(1)}, bf16[128,896]{1,0:T(8,128)(2,1)S(1)}, u32[]{:S(2)}, u32[]{:S(2)}) %collective-permute-start.8) | collective-permute-done | bytes 229408 | tf_op jit(solution)/shard_map/ppermute | solution.py:317
  140.9 11.0 %collective-permute-done.9 = bf16[640,896]{1,0:T(8,128)(2,1)S(1)} collective-permute-done((bf16[640,896]{1,0:T(8,128)(2,1)S(1)}, bf16[640,896]{1,0:T(8,128)(2,1)S(1)}, u32[]{:S(2)}, u32[]{:S(2)}) %collective-permute-start.9) | collective-permute-done | bytes 1146912 | tf_op jit(solution)/shard_map/ppermute | solution.py:317
  152.4 1.9 copy-done.6
  154.3 1.1 copy-done.7
  155.3 6.8 %pad_maximum_fusion.own_ref = bf16[2048,1792]{1,0:T(8,128)(2,1)} fusion(bf16[2048,896]{1,0:T(8,128)(2,1)} %copy-done.7, bf16[2048,896]{1,0:T(8,128)(2,1)} %copy-done.6), kind=kLoop, calls=%fused_computation | loop fusion | flops 14680064 | bytes 14680064 | tf_op jit(solution)/shard_map/concatenate | solution.py:405
  162.1 0.9 pack_rest.1
  163.0 1.2 copy-done.2
  164.3 9.9 %collective-permute-done.13.other_ref = bf16[2048,1792]{1,0:T(8,128)(2,1)} collective-permute-done((bf16[2048,1792]{1,0:T(8,128)(2,1)}, bf16[2048,1792]{1,0:T(8,128)(2,1)}, u32[]{:S(2)}, u32[]{:S(2)}) %collective-permute-start.13) | collective-permute-done | bytes 7340064 | tf_op jit(solution)/shard_map/ppermute | solution.py:363
  174.1 48.1 %all-to-all-done.packed_ref = bf16[16,1920,128]{2,1,0:T(8,128)(2,1)} async-done(((bf16[16,1920,128]{2,1,0:T(8,128)(2,1)}), bf16[16,1920,128]{2,1,0:T(8,128)(2,1)}, u32[]{:S(2)}, u32[]{:S(2)}) %all-to-all-start) | async-done | bytes 7864352 | tf_op jit(solution)/shard_map/all_to_all | solution.py:366
  222.3 7.0 %all-to-all-start.1 = ((bf16[16,448,128]{2,1,0:T(8,128)(2,1)}), bf16[16,448,128]{2,1,0:T(8,128)(2,1)}, u32[]{:S(2)}, u32[]{:S(2)}) async-start(bf16[16,448,128]{2,1,0:T(8,128)(2,1)} %copy-done.2), calls=%async_computation.1 | async-start | bytes 3670016 | tf_op jit(solution)/shard_map/all_to_all | solution.py:366
  229.3 0.6 pad_add_fusion.at_ref
  229.9 23.1 %hidden.1.own_h = bf16[2048,512]{1,0:T(8,128)(2,1)} custom-call(s32[2]{0:T(128)} %pad_add_fusion.at_ref, bf16[2048,1792]{1,0:T(8,128)(2,1)} %pad_maximum_fusion.own_ref, bf16[2048,1792]{1,0:T(8,128)(2,1)} %collective-permute-done.13.other_ref, bf16[16,1920,128]{2,1,0:T(8,128)(2,1)} %all-to-all-done.packed_ref), custom_call_target="tpu_custom_call" | custom-call | flops 15032385536 | bytes 25165824 | tf_op jit(solution)/shard_map/hidden/pallas_call | solution.py:196
  253.1 1.4 slice.85
  254.5 1.0 constant_dynamic-slice_fusion.2
  256.0 13.6 %all-to-all-done.1 = bf16[16,448,128]{2,1,0:T(8,128)(2,1)} async-done(((bf16[16,448,128]{2,1,0:T(8,128)(2,1)}), bf16[16,448,128]{2,1,0:T(8,128)(2,1)}, u32[]{:S(2)}, u32[]{:S(2)}) %all-to-all-start.1) | async-done | bytes 1835040 | tf_op jit(solution)/shard_map/all_to_all | solution.py:366
  269.6 1.6 constant_dynamic-slice_fusion
  271.3 3.5 down_send.2
  274.9 1.3 collective-permute-start.16
  276.2 13.0 %collective-permute-done.16.refs_1_ = bf16[1024,256]{1,0:T(8,128)(2,1)S(1)} collective-permute-done((bf16[1024,256]{1,0:T(8,128)(2,1)S(1)}, bf16[1024,256]{1,0:T(8,128)(2,1)S(1)}, u32[]{:S(2)}, u32[]{:S(2)}) %collective-permute-start.16) | collective-permute-done | bytes 524320 | tf_op jit(solution)/shard_map/ppermute | solution.py:317
  289.2 1.0 collective-permute-done.17.refs_3_
  290.2 4.6 %down_send.3 = (bf16[1024,384]{1,0:T(8,128)(2,1)S(1)}, bf16[1024,384]{1,0:T(8,128)(2,1)S(1)}, bf16[1024,256]{1,0:T(8,128)(2,1)S(1)}) custom-call(bf16[2048,512]{1,0:T(8,128)(2,1)S(1)} %copy-done.5, bf16[2048,512]{1,0:T(8,128)(2,1)} %collective-permute-done.14.other_h, bf16[8,448,128]{2,1,0:T(8,128)(2,1)S(1)} %get-tuple-element.135.own_ref, ...), custom_call_target="tpu_custom_call" | custom-call | flops 2147483648 | bytes 8388608 | tf_op jit(solution)/shard_map/down_send/pallas_call | solution.py:257
  294.8 0.8 collective-permute-start.27
  295.7 1.7 collective-permute-start.28
  297.7 3.5 down_keep.2
  301.8 4.6 %down_keep.3 = (f32[1024,384]{1,0:T(8,128)S(1)}, f32[1024,384]{1,0:T(8,128)S(1)}, f32[1024,256]{1,0:T(8,128)S(1)}) custom-call(bf16[2048,512]{1,0:T(8,128)(2,1)S(1)} %copy-done.5, bf16[2048,512]{1,0:T(8,128)(2,1)} %collective-permute-done.14.other_h, bf16[8,448,128]{2,1,0:T(8,128)(2,1)S(1)} %get-tuple-element.135.own_ref, ...), custom_call_target="tpu_custom_call" | custom-call | flops 2147483648 | bytes 8388608 | tf_op jit(solution)/shard_map/down_keep/pallas_call | solution.py:257
  306.4 3.3 collective-permute-done.29.refs_5_
  309.7 4.0 %collective-permute-done.27.refs_1_ = bf16[1024,384]{1,0:T(8,128)(2,1)S(1)} collective-permute-done((bf16[1024,384]{1,0:T(8,128)(2,1)S(1)}, bf16[1024,384]{1,0:T(8,128)(2,1)S(1)}, u32[]{:S(2)}, u32[]{:S(2)}) %collective-permute-start.27) | collective-permute-done | bytes 786464 | tf_op jit(solution)/shard_map/ppermute | solution.py:317
  313.7 2.4 collective-permute-done.28.refs_3_
  316.5 1.8 collective-permute-start.30
  318.6 1.7 collective-permute-start.20
  320.3 1.3 collective-permute-start.21
  321.8 1.2 collective-permute-start.32
  323.0 9.3 %collective-permute-done.20.refs_3_ = bf16[512,256]{1,0:T(8,128)(2,1)S(1)} collective-permute-done((bf16[512,256]{1,0:T(8,128)(2,1)S(1)}, bf16[512,256]{1,0:T(8,128)(2,1)S(1)}, u32[]{:S(2)}, u32[]{:S(2)}) %collective-permute-start.20) | collective-permute-done | bytes 262176 | tf_op jit(solution)/shard_map/ppermute | solution.py:317
  332.5 1.0 collective-permute-start.22
  333.5 1.3 collective-permute-start.23
  335.2 1.8 collective-permute-start.33
  337.0 0.8 collective-permute-start.34
  337.8 0.7 collective-permute-done.23.refs_3_
  338.5 1.3 collective-permute-done.24.refs_5_
  339.8 0.9 collective-permute-start.25
  340.6 1.2 collective-permute-start.35
  341.8 3.8 %collective-permute-done.35.refs_5_ = bf16[256,256]{1,0:T(8,128)(2,1)S(1)} collective-permute-done((bf16[256,256]{1,0:T(8,128)(2,1)S(1)}, bf16[256,256]{1,0:T(8,128)(2,1)S(1)}, u32[]{:S(2)}, u32[]{:S(2)}) %collective-permute-start.35) | collective-permute-done | bytes 131104 | tf_op jit(solution)/shard_map/ppermute | solution.py:317
  345.7 2.2 collective-permute-start.36
  348.4 6.2 %collective-permute-done.36 = bf16[128,1024]{1,0:T(8,128)(2,1)S(1)} collective-permute-done((bf16[128,1024]{1,0:T(8,128)(2,1)S(1)}, bf16[128,1024]{1,0:T(8,128)(2,1)S(1)}, u32[]{:S(2)}, u32[]{:S(2)}) %collective-permute-start.36) | collective-permute-done | bytes 262176 | tf_op jit(solution)/shard_map/ppermute | solution.py:317
  354.9 1.0 copy.15
  (91 shorter events, 10.0 us)
Async XLA Ops:
  0.0 22.4 %collective-permute-start = (bf16[128,1792]{1,0:T(8,128)(2,1)}, bf16[128,1792]{1,0:T(8,128)(2,1)S(1)}, u32[]{:S(2)}, u32[]{:S(2)}) collective-permute-start(bf16[128,1792]{1,0:T(8,128)(2,1)} %param.9), channel_id=1, source_target_pairs={{0,16},{2,18},{4,20},{6,22},{8,24},{10,26},{12,28},{14,30},{16,0},... | collective-permute-start | bytes 1376264 | tf_op jit(solution)/shard_map/ppermute | solution.py:317
  2.6 23.5 %collective-permute-start.1 = (bf16[128,1792]{1,0:T(8,128)(2,1)}, bf16[128,1792]{1,0:T(8,128)(2,1)S(1)}, u32[]{:S(2)}, u32[]{:S(2)}) collective-permute-start(bf16[128,1792]{1,0:T(8,128)(2,1)} %param.9), channel_id=1, source_target_pairs={{0,2},{2,0},{4,6},{6,4},{8,10},{10,8},{12,14},{14,12},{16,18},{18,... | collective-permute-start | bytes 1376264 | tf_op jit(solution)/shard_map/ppermute | solution.py:317
  3.1 23.2 %collective-permute-start.2 = (bf16[128,1792]{1,0:T(8,128)(2,1)}, bf16[128,1792]{1,0:T(8,128)(2,1)S(1)}, u32[]{:S(2)}, u32[]{:S(2)}) collective-permute-start(bf16[128,1792]{1,0:T(8,128)(2,1)} %param.9), channel_id=1, source_target_pairs={{0,4},{2,6},{4,0},{6,2},{8,12},{10,14},{12,8},{14,10},{16,20},{18,... | collective-permute-start | bytes 1376264 | tf_op jit(solution)/shard_map/ppermute | solution.py:317
  3.6 22.7 %collective-permute-start.3 = (bf16[128,1792]{1,0:T(8,128)(2,1)}, bf16[128,1792]{1,0:T(8,128)(2,1)S(1)}, u32[]{:S(2)}, u32[]{:S(2)}) collective-permute-start(bf16[128,1792]{1,0:T(8,128)(2,1)} %param.9), channel_id=1, source_target_pairs={{0,6},{2,4},{4,2},{6,0},{8,14},{10,12},{12,10},{14,8},{16,22},{18,... | collective-permute-start | bytes 1376264 | tf_op jit(solution)/shard_map/ppermute | solution.py:378
  6.1 19.3 %collective-permute-start.4 = (bf16[128,1792]{1,0:T(8,128)(2,1)}, bf16[128,1792]{1,0:T(8,128)(2,1)S(1)}, u32[]{:S(2)}, u32[]{:S(2)}) collective-permute-start(bf16[128,1792]{1,0:T(8,128)(2,1)} %param.9), channel_id=1, source_target_pairs={{0,8},{2,10},{4,12},{6,14},{8,0},{10,2},{12,4},{14,6},{16,24},{18,... | collective-permute-start | bytes 1376264 | tf_op jit(solution)/shard_map/ppermute | solution.py:317
  10.4 2.0 copy-start
  12.4 2.0 copy-start.3
  14.4 2.0 copy-start.4
  22.4 12.4 %collective-permute-start.5 = (bf16[128,1792]{1,0:T(8,128)(2,1)S(1)}, bf16[128,1792]{1,0:T(8,128)(2,1)S(1)}, u32[]{:S(2)}, u32[]{:S(2)}) collective-permute-start(bf16[128,1792]{1,0:T(8,128)(2,1)S(1)} %collective-permute-done), channel_id=1, source_target_pairs={{0,8},{2,10},{4,12},{6,14},{8,0},{10,2},{12,4},{14,6},{16,24},{18,... | collective-permute-start | bytes 1376264 | tf_op jit(solution)/shard_map/ppermute | solution.py:317
  25.5 9.6 %collective-permute-start.6 = (bf16[256,896]{1,0:T(8,128)(2,1)S(1)}, bf16[256,896]{1,0:T(8,128)(2,1)S(1)}, u32[]{:S(2)}, u32[]{:S(2)}) collective-permute-start(bf16[256,896]{1,0:T(8,128)(2,1)S(1)} %get-tuple-element.166), channel_id=1, source_target_pairs={{0,4},{2,6},{4,0},{6,2},{8,12},{10,14},{12,8},{14,10},{16,20},{18,... | collective-permute-start | bytes 1376264 | tf_op jit(solution)/shard_map/ppermute | solution.py:317
  26.1 17.4 %copy-start.8 = (bf16[128,1792]{1,0:T(8,128)(2,1)S(1)}, bf16[128,1792]{1,0:T(8,128)(2,1)}, u32[]{:S(2)}) copy-start(bf16[128,1792]{1,0:T(8,128)(2,1)} %param.9) | copy-start | bytes 1376260
  26.1 9.6 %collective-permute-start.7 = (bf16[256,896]{1,0:T(8,128)(2,1)S(1)}, bf16[256,896]{1,0:T(8,128)(2,1)S(1)}, u32[]{:S(2)}, u32[]{:S(2)}) collective-permute-start(bf16[256,896]{1,0:T(8,128)(2,1)S(1)} %get-tuple-element.165), channel_id=1, source_target_pairs={{0,2},{2,0},{4,6},{6,4},{8,10},{10,8},{12,14},{14,12},{16,18},{18,... | collective-permute-start | bytes 1376264 | tf_op jit(solution)/shard_map/ppermute | solution.py:317
  26.4 8.8 %copy-start.9 = (bf16[128,1792]{1,0:T(8,128)(2,1)}, bf16[128,1792]{1,0:T(8,128)(2,1)S(1)}, u32[]{:S(2)}) copy-start(bf16[128,1792]{1,0:T(8,128)(2,1)S(1)} %collective-permute-done.2) | copy-start | bytes 1376260
  34.9 0.8 copy-start.11
  35.7 186.6 %all-to-all-start = ((bf16[16,1920,128]{2,1,0:T(8,128)(2,1)}), bf16[16,1920,128]{2,1,0:T(8,128)(2,1)}, u32[]{:S(2)}, u32[]{:S(2)}) async-start(bf16[16,1920,128]{2,1,0:T(8,128)(2,1)} %pack_first.1), calls=%async_computation | async-start | bytes 15728640 | tf_op jit(solution)/shard_map/all_to_all | solution.py:366
  43.5 1.0 copy-start.12
  43.8 5.8 %copy-start.10 = (bf16[128,1792]{1,0:T(8,128)(2,1)S(1)}, bf16[128,1792]{1,0:T(8,128)(2,1)}, u32[]{:S(2)}) copy-start(bf16[128,1792]{1,0:T(8,128)(2,1)} %copy-done.9) | copy-start | bytes 1376260
  44.7 95.9 %collective-permute-start.11 = (bf16[640,896]{1,0:T(8,128)(2,1)S(1)}, bf16[640,896]{1,0:T(8,128)(2,1)S(1)}, u32[]{:S(2)}, u32[]{:S(2)}) collective-permute-start(bf16[640,896]{1,0:T(8,128)(2,1)S(1)} %pad_maximum_fusion.2), channel_id=1, source_target_pairs={{0,4},{2,6},{4,0},{6,2},{8,12},{10,14},{12,8},{14,10},{16,20},{18,... | collective-permute-start | bytes 3440648 | tf_op jit(solution)/shard_map/ppermute | solution.py:317
  45.4 95.5 %collective-permute-start.12 = (bf16[128,896]{1,0:T(8,128)(2,1)S(1)}, bf16[128,896]{1,0:T(8,128)(2,1)S(1)}, u32[]{:S(2)}, u32[]{:S(2)}) collective-permute-start(bf16[128,896]{1,0:T(8,128)(2,1)S(1)} %get-tuple-element.176), channel_id=1, source_target_pairs={{0,2},{2,0},{4,6},{6,4},{8,10},{10,8},{12,14},{14,12},{16,18},{18,... | collective-permute-start | bytes 688136 | tf_op jit(solution)/shard_map/ppermute | solution.py:317
  45.9 106.3 %collective-permute-start.10 = (bf16[128,1792]{1,0:T(8,128)(2,1)S(1)}, bf16[128,1792]{1,0:T(8,128)(2,1)S(1)}, u32[]{:S(2)}, u32[]{:S(2)}) collective-permute-start(bf16[128,1792]{1,0:T(8,128)(2,1)S(1)} %copy-done.12), channel_id=1, source_target_pairs={{0,6},{2,4},{4,2},{6,0},{8,14},{10,12},{12,10},{14,8},{16,22},{18,... | collective-permute-start | bytes 1376264 | tf_op jit(solution)/shard_map/ppermute | solution.py:378
  48.3 92.3 %collective-permute-start.8 = (bf16[128,896]{1,0:T(8,128)(2,1)S(1)}, bf16[128,896]{1,0:T(8,128)(2,1)S(1)}, u32[]{:S(2)}, u32[]{:S(2)}) collective-permute-start(bf16[128,896]{1,0:T(8,128)(2,1)S(1)} %get-tuple-element.173), channel_id=1, source_target_pairs={{0,4},{2,6},{4,0},{6,2},{8,12},{10,14},{12,8},{14,10},{16,20},{18,... | collective-permute-start | bytes 688136 | tf_op jit(solution)/shard_map/ppermute | solution.py:317
  49.0 103.0 %collective-permute-start.9 = (bf16[640,896]{1,0:T(8,128)(2,1)S(1)}, bf16[640,896]{1,0:T(8,128)(2,1)S(1)}, u32[]{:S(2)}, u32[]{:S(2)}) collective-permute-start(bf16[640,896]{1,0:T(8,128)(2,1)S(1)} %pad_maximum_fusion.1), channel_id=1, source_target_pairs={{0,2},{2,0},{4,6},{6,4},{8,10},{10,8},{12,14},{14,12},{16,18},{18,... | collective-permute-start | bytes 3440648 | tf_op jit(solution)/shard_map/ppermute | solution.py:317
  152.3 1.9 copy-start.6
  152.3 3.0 copy-start.7
  155.3 6.8 %copy-start.1 = (bf16[16,224,512]{2,1,0:T(8,128)(2,1)S(1)}, bf16[16,224,512]{2,1,0:T(8,128)(2,1)}, u32[]{:S(2)}) copy-start(bf16[16,224,512]{2,1,0:T(8,128)(2,1)} %down_ref.3) | copy-start | bytes 11010052
  162.1 12.0 %collective-permute-start.13 = (bf16[2048,1792]{1,0:T(8,128)(2,1)}, bf16[2048,1792]{1,0:T(8,128)(2,1)}, u32[]{:S(2)}, u32[]{:S(2)}) collective-permute-start(bf16[2048,1792]{1,0:T(8,128)(2,1)} %pad_maximum_fusion.own_ref), channel_id=1, source_target_pairs={{0,1},{1,0},{2,3},{3,2},{4,5},{5,4},{6,7},{7,6},{8,9},{9,8},{10,11... | collective-permute-start | bytes 22020104 | tf_op jit(solution)/shard_map/ppermute | solution.py:363
  163.0 1.2 copy-start.2
  222.3 47.4 %all-to-all-start.1 = ((bf16[16,448,128]{2,1,0:T(8,128)(2,1)}), bf16[16,448,128]{2,1,0:T(8,128)(2,1)}, u32[]{:S(2)}, u32[]{:S(2)}) async-start(bf16[16,448,128]{2,1,0:T(8,128)(2,1)} %copy-done.2), calls=%async_computation.1 | async-start | bytes 3670016 | tf_op jit(solution)/shard_map/all_to_all | solution.py:366
  253.1 18.2 %collective-permute-start.14 = (bf16[2048,512]{1,0:T(8,128)(2,1)}, bf16[2048,512]{1,0:T(8,128)(2,1)}, u32[]{:S(2)}, u32[]{:S(2)}) collective-permute-start(bf16[2048,512]{1,0:T(8,128)(2,1)} %hidden.1.own_h), channel_id=1, source_target_pairs={{0,1},{1,0},{2,3},{3,2},{4,5},{5,4},{6,7},{7,6},{8,9},{9,8},{10,11... | collective-permute-start | bytes 6291464 | tf_op jit(solution)/shard_map/ppermute | solution.py:363
  254.5 16.8 %copy-start.5 = (bf16[2048,512]{1,0:T(8,128)(2,1)S(1)}, bf16[2048,512]{1,0:T(8,128)(2,1)}, u32[]{:S(2)}) copy-start(bf16[2048,512]{1,0:T(8,128)(2,1)} %hidden.1.own_h) | copy-start | bytes 6291460
  255.5 15.8 %collective-permute-start.15 = (bf16[8,336,128]{2,1,0:T(8,128)(2,1)}, bf16[8,336,128]{2,1,0:T(8,128)(2,1)S(1)}, u32[]{:S(2)}, u32[]{:S(2)}) collective-permute-start(bf16[8,336,128]{2,1,0:T(8,128)(2,1)} %get-tuple-element.159), channel_id=1, source_target_pairs={{0,1},{1,0},{2,3},{3,2},{4,5},{5,4},{6,7},{7,6},{8,9},{9,8},{10,11... | collective-permute-start | bytes 2064392 | tf_op jit(solution)/shard_map/ppermute | solution.py:363
  271.2 19.0 %collective-permute-start.26 = (bf16[8,448,128]{2,1,0:T(8,128)(2,1)S(1)}, bf16[8,448,128]{2,1,0:T(8,128)(2,1)S(1)}, u32[]{:S(2)}, u32[]{:S(2)}) collective-permute-start(bf16[8,448,128]{2,1,0:T(8,128)(2,1)S(1)} %get-tuple-element.157), channel_id=1, source_target_pairs={{0,1},{1,0},{2,3},{3,2},{4,5},{5,4},{6,7},{7,6},{8,9},{9,8},{10,11... | collective-permute-start | bytes 2752520 | tf_op jit(solution)/shard_map/ppermute | solution.py:363
  274.9 14.4 %collective-permute-start.16 = (bf16[1024,256]{1,0:T(8,128)(2,1)S(1)}, bf16[1024,256]{1,0:T(8,128)(2,1)S(1)}, u32[]{:S(2)}, u32[]{:S(2)}) collective-permute-start(bf16[1024,256]{1,0:T(8,128)(2,1)S(1)} %get-tuple-element.106), channel_id=1, source_target_pairs={{0,2},{2,0},{4,6},{6,4},{8,10},{10,8},{12,14},{14,12},{16,18},{18,... | collective-permute-start | bytes 1572872 | tf_op jit(solution)/shard_map/ppermute | solution.py:317
  276.2 14.0 %collective-permute-start.17 = (bf16[1024,256]{1,0:T(8,128)(2,1)S(1)}, bf16[1024,256]{1,0:T(8,128)(2,1)S(1)}, u32[]{:S(2)}, u32[]{:S(2)}) collective-permute-start(bf16[1024,256]{1,0:T(8,128)(2,1)S(1)} %get-tuple-element.108), channel_id=1, source_target_pairs={{0,4},{2,6},{4,0},{6,2},{8,12},{10,14},{12,8},{14,10},{16,20},{18,... | collective-permute-start | bytes 1572872 | tf_op jit(solution)/shard_map/ppermute | solution.py:317
  276.2 14.0 %collective-permute-start.18 = (bf16[1024,256]{1,0:T(8,128)(2,1)S(1)}, bf16[1024,256]{1,0:T(8,128)(2,1)S(1)}, u32[]{:S(2)}, u32[]{:S(2)}) collective-permute-start(bf16[1024,256]{1,0:T(8,128)(2,1)S(1)} %get-tuple-element.110), channel_id=1, source_target_pairs={{0,8},{2,10},{4,12},{6,14},{8,0},{10,2},{12,4},{14,6},{16,24},{18,... | collective-permute-start | bytes 1572872 | tf_op jit(solution)/shard_map/ppermute | solution.py:317
  294.8 18.9 %collective-permute-start.27 = (bf16[1024,384]{1,0:T(8,128)(2,1)S(1)}, bf16[1024,384]{1,0:T(8,128)(2,1)S(1)}, u32[]{:S(2)}, u32[]{:S(2)}) collective-permute-start(bf16[1024,384]{1,0:T(8,128)(2,1)S(1)} %get-tuple-element.138), channel_id=1, source_target_pairs={{0,2},{2,0},{4,6},{6,4},{8,10},{10,8},{12,14},{14,12},{16,18},{18,... | collective-permute-start | bytes 2359304 | tf_op jit(solution)/shard_map/ppermute | solution.py:317
  295.7 20.5 %collective-permute-start.28 = (bf16[1024,384]{1,0:T(8,128)(2,1)S(1)}, bf16[1024,384]{1,0:T(8,128)(2,1)S(1)}, u32[]{:S(2)}, u32[]{:S(2)}) collective-permute-start(bf16[1024,384]{1,0:T(8,128)(2,1)S(1)} %get-tuple-element.140), channel_id=1, source_target_pairs={{0,4},{2,6},{4,0},{6,2},{8,12},{10,14},{12,8},{14,10},{16,20},{18,... | collective-permute-start | bytes 2359304 | tf_op jit(solution)/shard_map/ppermute | solution.py:317
  297.4 12.3 %collective-permute-start.29 = (bf16[1024,256]{1,0:T(8,128)(2,1)S(1)}, bf16[1024,256]{1,0:T(8,128)(2,1)S(1)}, u32[]{:S(2)}, u32[]{:S(2)}) collective-permute-start(bf16[1024,256]{1,0:T(8,128)(2,1)S(1)} %get-tuple-element.142), channel_id=1, source_target_pairs={{0,8},{2,10},{4,12},{6,14},{8,0},{10,2},{12,4},{14,6},{16,24},{18,... | collective-permute-start | bytes 1572872 | tf_op jit(solution)/shard_map/ppermute | solution.py:317
  301.5 20.3 %collective-permute-start.19 = (bf16[512,256]{1,0:T(8,128)(2,1)S(1)}, bf16[512,256]{1,0:T(8,128)(2,1)S(1)}, u32[]{:S(2)}, u32[]{:S(2)}) collective-permute-start(bf16[512,256]{1,0:T(8,128)(2,1)S(1)} %get-tuple-element.112), channel_id=1, source_target_pairs={{0,4},{2,6},{4,0},{6,2},{8,12},{10,14},{12,8},{14,10},{16,20},{18,... | collective-permute-start | bytes 786440 | tf_op jit(solution)/shard_map/ppermute | solution.py:317
  316.5 18.5 %collective-permute-start.30 = (bf16[512,384]{1,0:T(8,128)(2,1)S(1)}, bf16[512,384]{1,0:T(8,128)(2,1)S(1)}, u32[]{:S(2)}, u32[]{:S(2)}) collective-permute-start(bf16[512,384]{1,0:T(8,128)(2,1)S(1)} %get-tuple-element.144), channel_id=1, source_target_pairs={{0,4},{2,6},{4,0},{6,2},{8,12},{10,14},{12,8},{14,10},{16,20},{18,... | collective-permute-start | bytes 1179656 | tf_op jit(solution)/shard_map/ppermute | solution.py:317
  318.3 16.7 %collective-permute-start.31 = (bf16[512,384]{1,0:T(8,128)(2,1)S(1)}, bf16[512,384]{1,0:T(8,128)(2,1)S(1)}, u32[]{:S(2)}, u32[]{:S(2)}) collective-permute-start(bf16[512,384]{1,0:T(8,128)(2,1)S(1)} %get-tuple-element.146), channel_id=1, source_target_pairs={{0,8},{2,10},{4,12},{6,14},{8,0},{10,2},{12,4},{14,6},{16,24},{18,... | collective-permute-start | bytes 1179656 | tf_op jit(solution)/shard_map/ppermute | solution.py:317
  318.6 13.7 %collective-permute-start.20 = (bf16[512,256]{1,0:T(8,128)(2,1)S(1)}, bf16[512,256]{1,0:T(8,128)(2,1)S(1)}, u32[]{:S(2)}, u32[]{:S(2)}) collective-permute-start(bf16[512,256]{1,0:T(8,128)(2,1)S(1)} %get-tuple-element.114), channel_id=1, source_target_pairs={{0,8},{2,10},{4,12},{6,14},{8,0},{10,2},{12,4},{14,6},{16,24},{18,... | collective-permute-start | bytes 786440 | tf_op jit(solution)/shard_map/ppermute | solution.py:317
  320.3 12.0 %collective-permute-start.21 = (bf16[512,256]{1,0:T(8,128)(2,1)S(1)}, bf16[512,256]{1,0:T(8,128)(2,1)S(1)}, u32[]{:S(2)}, u32[]{:S(2)}) collective-permute-start(bf16[512,256]{1,0:T(8,128)(2,1)S(1)} %get-tuple-element.116), channel_id=1, source_target_pairs={{0,2},{2,0},{4,6},{6,4},{8,10},{10,8},{12,14},{14,12},{16,18},{18,... | collective-permute-start | bytes 786440 | tf_op jit(solution)/shard_map/ppermute | solution.py:317
  321.8 13.0 %collective-permute-start.32 = (bf16[512,256]{1,0:T(8,128)(2,1)S(1)}, bf16[512,256]{1,0:T(8,128)(2,1)S(1)}, u32[]{:S(2)}, u32[]{:S(2)}) collective-permute-start(bf16[512,256]{1,0:T(8,128)(2,1)S(1)} %get-tuple-element.148), channel_id=1, source_target_pairs={{0,2},{2,0},{4,6},{6,4},{8,10},{10,8},{12,14},{14,12},{16,18},{18,... | collective-permute-start | bytes 786440 | tf_op jit(solution)/shard_map/ppermute | solution.py:317
  332.5 5.3 %collective-permute-start.22 = (bf16[256,256]{1,0:T(8,128)(2,1)S(1)}, bf16[256,256]{1,0:T(8,128)(2,1)S(1)}, u32[]{:S(2)}, u32[]{:S(2)}) collective-permute-start(bf16[256,256]{1,0:T(8,128)(2,1)S(1)} %get-tuple-element.118), channel_id=1, source_target_pairs={{0,8},{2,10},{4,12},{6,14},{8,0},{10,2},{12,4},{14,6},{16,24},{18,... | collective-permute-start | bytes 393224 | tf_op jit(solution)/shard_map/ppermute | solution.py:317
  333.5 5.0 %collective-permute-start.23 = (bf16[256,256]{1,0:T(8,128)(2,1)S(1)}, bf16[256,256]{1,0:T(8,128)(2,1)S(1)}, u32[]{:S(2)}, u32[]{:S(2)}) collective-permute-start(bf16[256,256]{1,0:T(8,128)(2,1)S(1)} %get-tuple-element.120), channel_id=1, source_target_pairs={{0,2},{2,0},{4,6},{6,4},{8,10},{10,8},{12,14},{14,12},{16,18},{18,... | collective-permute-start | bytes 393224 | tf_op jit(solution)/shard_map/ppermute | solution.py:317
  334.8 5.0 %collective-permute-start.24 = (bf16[256,256]{1,0:T(8,128)(2,1)S(1)}, bf16[256,256]{1,0:T(8,128)(2,1)S(1)}, u32[]{:S(2)}, u32[]{:S(2)}) collective-permute-start(bf16[256,256]{1,0:T(8,128)(2,1)S(1)} %get-tuple-element.122), channel_id=1, source_target_pairs={{0,4},{2,6},{4,0},{6,2},{8,12},{10,14},{12,8},{14,10},{16,20},{18,... | collective-permute-start | bytes 393224 | tf_op jit(solution)/shard_map/ppermute | solution.py:317
  335.2 10.4 %collective-permute-start.33 = (bf16[256,384]{1,0:T(8,128)(2,1)S(1)}, bf16[256,384]{1,0:T(8,128)(2,1)S(1)}, u32[]{:S(2)}, u32[]{:S(2)}) collective-permute-start(bf16[256,384]{1,0:T(8,128)(2,1)S(1)} %get-tuple-element.150), channel_id=1, source_target_pairs={{0,8},{2,10},{4,12},{6,14},{8,0},{10,2},{12,4},{14,6},{16,24},{18,... | collective-permute-start | bytes 589832 | tf_op jit(solution)/shard_map/ppermute | solution.py:317
  337.0 8.6 %collective-permute-start.34 = (bf16[256,384]{1,0:T(8,128)(2,1)S(1)}, bf16[256,384]{1,0:T(8,128)(2,1)S(1)}, u32[]{:S(2)}, u32[]{:S(2)}) collective-permute-start(bf16[256,384]{1,0:T(8,128)(2,1)S(1)} %get-tuple-element.152), channel_id=1, source_target_pairs={{0,2},{2,0},{4,6},{6,4},{8,10},{10,8},{12,14},{14,12},{16,18},{18,... | collective-permute-start | bytes 589832 | tf_op jit(solution)/shard_map/ppermute | solution.py:317
  339.8 8.4 %collective-permute-start.25 = (bf16[128,768]{1,0:T(8,128)(2,1)S(1)}, bf16[128,768]{1,0:T(8,128)(2,1)S(1)}, u32[]{:S(2)}, u32[]{:S(2)}) collective-permute-start(bf16[128,768]{1,0:T(8,128)(2,1)S(1)} %get-tuple-element.124), channel_id=1, source_target_pairs={{0,16},{2,18},{4,20},{6,22},{8,24},{10,26},{12,28},{14,30},{16,0},... | collective-permute-start | bytes 589832 | tf_op jit(solution)/shard_map/ppermute | solution.py:317
  340.6 5.0 %collective-permute-start.35 = (bf16[256,256]{1,0:T(8,128)(2,1)S(1)}, bf16[256,256]{1,0:T(8,128)(2,1)S(1)}, u32[]{:S(2)}, u32[]{:S(2)}) collective-permute-start(bf16[256,256]{1,0:T(8,128)(2,1)S(1)} %get-tuple-element.154), channel_id=1, source_target_pairs={{0,4},{2,6},{4,0},{6,2},{8,12},{10,14},{12,8},{14,10},{16,20},{18,... | collective-permute-start | bytes 393224 | tf_op jit(solution)/shard_map/ppermute | solution.py:317
  345.7 8.9 %collective-permute-start.36 = (bf16[128,1024]{1,0:T(8,128)(2,1)S(1)}, bf16[128,1024]{1,0:T(8,128)(2,1)S(1)}, u32[]{:S(2)}, u32[]{:S(2)}) collective-permute-start(bf16[128,1024]{1,0:T(8,128)(2,1)S(1)} %get-tuple-element.156), channel_id=1, source_target_pairs={{0,16},{2,18},{4,20},{6,22},{8,24},{10,26},{12,28},{14,30},{16,0},... | collective-permute-start | bytes 786440 | tf_op jit(solution)/shard_map/ppermute | solution.py:317

commit v17 on v16

--- a/solution.py
+++ b/solution.py
@@ -437,7 +437,7 @@
         sent, args = tie((sent, args))
         come = [swap(value, order[0]) for value, order in zip(sent, orders)]
         kept = down_product(*args, rows_in, 0, orders, jnp.float32, "down_keep")
-        return kept, come
+        return kept, come, sent
 
     def stage(kept, come, number, orders):
         axes = tuple(stage_axis(order, number) for order in orders)
@@ -450,8 +450,9 @@
         come = swap(send, 3)
         return (keep + come.astype(jnp.float32)).astype(jnp.bfloat16)
 
-    kept0, come0 = products(down0, parts[0], THIRDS)
-    kept1, come1 = products(down1, parts[1], THIRDS, before=come0)
+    kept0, come0, sent0 = products(down0, parts[0], THIRDS)
+    down1, _ = tie((down1, sent0))
+    kept1, come1, _ = products(down1, parts[1], THIRDS, before=come0)
     kept0, come0 = stage(kept0, come0, 1, THIRDS)
     kept1, come1 = stage(kept1, come1, 1, THIRDS)
     kept0, come0 = stage(kept0, come0, 2, THIRDS)

time: 361 us -> 357 us (0.989)
  waiting for transfers between devices: 230 us -> 216 us
  local copies, waits for them, and re-layouts: 18.1 us -> 27.9 us
    unnamed x38 -> x44, local copies, waits for them, and re-layouts: 12.3 us -> 20.4 us
    all_to_all x2, waiting for transfers between devices: 61.8 us -> 54.2 us  [move(): return lax.all_to_all(packed, 'ep', 0, 0, tiled=True)]
    ppermute x31, waiting for transfers between devices: 159 us -> 151 us  [swap(): return lax.ppermute(value, 'ep', [(i, i ^ 1 << bit) for i in range(size)])]
  transfers between devices with their start and end apart: 39 -> 39, of which waited for: 21 -> 23; matrix products, arithmetic and copies ran while one was open for 5% -> 7% of each run, Pallas kernels for 12% -> 12%
where the time goes in v17:
time: 357 us; the launch traced here: 352 us
  waiting for transfers between devices  216 us (61%)
  starting transfers between devices  49.4 us (14%)
  Pallas kernels  47.7 us (13%)
  local copies, waits for them, and re-layouts  27.9 us (8%)
  other arithmetic  11.4 us (3%)
    ppermute x31, waiting for transfers between devices, swap(): return lax.ppermute(value, 'ep', [(i, i ^ 1 << bit) for i in range(size)])  151 us
    all_to_all x2, waiting for transfers between devices, move(): return lax.all_to_all(packed, 'ep', 0, 0, tiled=True)  54.2 us
    ppermute x31, starting transfers between devices, swap(): return lax.ppermute(value, 'ep', [(i, i ^ 1 << bit) for i in range(size)])  29.2 us
    pallas_call x1, Pallas kernels, hidden_units(): pl.pallas_call(hidden_kernel, grid=(8,), out_shape=jax.ShapeDtypeStruct((...  23.2 us
    unnamed x44, local copies, waits for them, and re-layouts  20.4 us
    pallas_call x4, Pallas kernels, down_product(): pl.pallas_call(functools.partial(down_kernel, rows, side, orders), out_sh...  16.2 us
    all_to_all x2, starting transfers between devices, move(): return lax.all_to_all(packed, 'ep', 0, 0, tiled=True)  14.9 us
    ppermute x4, waiting for transfers between devices, exchange(): return lax.ppermute(value, 'et', [(0, 1), (1, 0)])  10.3 us
  transfers between devices with their start and end apart: 39, of which 23 were waited for; matrix products, arithmetic and copies ran while one was open for 7% of the time, Pallas kernels for 12%

profile of v17, /device:TPU:14, one launch (start us, length us, event | category | flops | bytes accessed | tf_op | source)
XLA Modules:
  0.0 352.4 jit_solution(2099654767377716022)
XLA Ops:
  0.0 2.6 collective-permute-start
  3.6 2.4 collective-permute-start.3
  6.5 0.9 select_reduce_fusion.4
  9.4 0.9 select_reduce_fusion.share_ref
  10.4 2.0 copy-done
  12.4 2.0 copy-done.2
  14.4 2.0 copy-done.3
  16.5 5.1 %pack_first.1 = bf16[16,1920,128]{2,1,0:T(8,128)(2,1)} custom-call(s32[14]{0:T(128)S(1)} %select_reduce_fusion.3.list_ref, bf16[16,224,512]{2,1,0:T(8,128)(2,1)S(1)} %copy-done.2, bf16[16,224,512]{2,1,0:T(8,128)(2,1)S(1)} %copy-done.3, bf16[16,224,512]{2,1,0:T(8,128)(2,1)S(1)} %copy-done, f32[16,16,128]{2,1,0:T(8,128)S(1)} %select_reduce_fusion.share_ref), custom_call_target="tpu_custom_call" | custom-call | tf_op jit(solution)/shard_map/pack_first/pallas_call | solution.py:113
  21.6 0.9 collective-permute-done
  22.4 1.3 collective-permute-start.5
  23.8 1.6 collective-permute-done.4
  26.4 8.5 %collective-permute-done.5 = bf16[128,1792]{1,0:T(8,128)(2,1)S(1)} collective-permute-done((bf16[128,1792]{1,0:T(8,128)(2,1)S(1)}, bf16[128,1792]{1,0:T(8,128)(2,1)S(1)}, u32[]{:S(2)}, u32[]{:S(2)}) %collective-permute-start.5) | collective-permute-done | bytes 458784 | tf_op jit(solution)/shard_map/ppermute | solution.py:317
  35.7 7.9 %all-to-all-start = ((bf16[16,1920,128]{2,1,0:T(8,128)(2,1)}), bf16[16,1920,128]{2,1,0:T(8,128)(2,1)}, u32[]{:S(2)}, u32[]{:S(2)}) async-start(bf16[16,1920,128]{2,1,0:T(8,128)(2,1)} %pack_first.1), calls=%async_computation | async-start | bytes 15728640 | tf_op jit(solution)/shard_map/all_to_all | solution.py:366
  44.3 1.1 fusion.3
  45.4 0.8 fusion.5
  47.5 2.4 collective-permute-start.10
  51.2 0.8 slice_dynamic-update-slice_fusion.12
  52.0 0.9 constant_dynamic-update-slice_fusion.3
  52.9 87.8 %collective-permute-done.8 = bf16[128,896]{1,0:T(8,128)(2,1)S(1)} collective-permute-done((bf16[128,896]{1,0:T(8,128)(2,1)S(1)}, bf16[128,896]{1,0:T(8,128)(2,1)S(1)}, u32[]{:S(2)}, u32[]{:S(2)}) %collective-permute-start.8) | collective-permute-done | bytes 229408 | tf_op jit(solution)/shard_map/ppermute | solution.py:317
  141.4 0.9 slice_dynamic-update-slice_fusion
  142.3 0.8 slice_dynamic-update-slice_fusion.11
  143.1 0.8 constant_dynamic-update-slice_fusion.7
  144.7 7.3 %collective-permute-done.9 = bf16[640,896]{1,0:T(8,128)(2,1)S(1)} collective-permute-done((bf16[640,896]{1,0:T(8,128)(2,1)S(1)}, bf16[640,896]{1,0:T(8,128)(2,1)S(1)}, u32[]{:S(2)}, u32[]{:S(2)}) %collective-permute-start.9) | collective-permute-done | bytes 1146912 | tf_op jit(solution)/shard_map/ppermute | solution.py:317
  152.0 0.9 slice_dynamic-update-slice_fusion.1
  152.9 0.9 slice_dynamic-update-slice_fusion.10
  153.7 1.0 slice_dynamic-update-slice_fusion.2
  155.5 6.7 %pad_maximum_fusion.own_ref = bf16[2048,1792]{1,0:T(8,128)(2,1)} fusion(bf16[2048,896]{1,0:T(8,128)(2,1)} %get-tuple-element.170, bf16[2048,896]{1,0:T(8,128)(2,1)} %get-tuple-element.169), kind=kLoop, calls=%fused_computation | loop fusion | flops 14680064 | bytes 14680064 | tf_op jit(solution)/shard_map/concatenate | solution.py:405
  162.2 2.0 copy-done.1
  164.2 2.1 pack_rest.1
  167.0 7.2 %collective-permute-done.13.other_ref = bf16[2048,1792]{1,0:T(8,128)(2,1)} collective-permute-done((bf16[2048,1792]{1,0:T(8,128)(2,1)}, bf16[2048,1792]{1,0:T(8,128)(2,1)}, u32[]{:S(2)}, u32[]{:S(2)}) %collective-permute-start.13) | collective-permute-done | bytes 7340064 | tf_op jit(solution)/shard_map/ppermute | solution.py:363
  174.2 48.1 %all-to-all-done.packed_ref = bf16[16,1920,128]{2,1,0:T(8,128)(2,1)} async-done(((bf16[16,1920,128]{2,1,0:T(8,128)(2,1)}), bf16[16,1920,128]{2,1,0:T(8,128)(2,1)}, u32[]{:S(2)}, u32[]{:S(2)}) %all-to-all-start) | async-done | bytes 7864352 | tf_op jit(solution)/shard_map/all_to_all | solution.py:366
  222.3 7.0 %all-to-all-start.1 = ((bf16[16,448,128]{2,1,0:T(8,128)(2,1)}), bf16[16,448,128]{2,1,0:T(8,128)(2,1)}, u32[]{:S(2)}, u32[]{:S(2)}) async-start(bf16[16,448,128]{2,1,0:T(8,128)(2,1)} %pack_rest.1), calls=%async_computation.1 | async-start | bytes 3670016 | tf_op jit(solution)/shard_map/all_to_all | solution.py:366
  229.3 23.2 %hidden.1.own_h = bf16[2048,512]{1,0:T(8,128)(2,1)} custom-call(s32[2]{0:T(128)} %pad_add_fusion.at_ref, bf16[2048,1792]{1,0:T(8,128)(2,1)} %pad_maximum_fusion.own_ref, bf16[2048,1792]{1,0:T(8,128)(2,1)} %collective-permute-done.13.other_ref, bf16[16,1920,128]{2,1,0:T(8,128)(2,1)} %all-to-all-done.packed_ref), custom_call_target="tpu_custom_call" | custom-call | flops 15032385536 | bytes 25165824 | tf_op jit(solution)/shard_map/hidden/pallas_call | solution.py:196
  252.5 1.6 slice.85
  254.6 3.0 collective-permute-done.15.other_ref
  257.6 3.5 down_send.2
  263.5 6.1 %all-to-all-done.1 = bf16[16,448,128]{2,1,0:T(8,128)(2,1)} async-done(((bf16[16,448,128]{2,1,0:T(8,128)(2,1)}), bf16[16,448,128]{2,1,0:T(8,128)(2,1)}, u32[]{:S(2)}, u32[]{:S(2)}) %all-to-all-start.1) | async-done | bytes 1835040 | tf_op jit(solution)/shard_map/all_to_all | solution.py:366
  269.6 1.7 constant_dynamic-slice_fusion
  271.4 1.3 collective-permute-start.16
  272.9 12.9 %collective-permute-done.16.refs_1_ = bf16[1024,256]{1,0:T(8,128)(2,1)S(1)} collective-permute-done((bf16[1024,256]{1,0:T(8,128)(2,1)S(1)}, bf16[1024,256]{1,0:T(8,128)(2,1)S(1)}, u32[]{:S(2)}, u32[]{:S(2)}) %collective-permute-start.16) | collective-permute-done | bytes 524320 | tf_op jit(solution)/shard_map/ppermute | solution.py:317
  285.8 1.0 collective-permute-done.17.refs_3_
  286.8 4.6 %down_send.3 = (bf16[1024,384]{1,0:T(8,128)(2,1)S(1)}, bf16[1024,384]{1,0:T(8,128)(2,1)S(1)}, bf16[1024,256]{1,0:T(8,128)(2,1)S(1)}) custom-call(bf16[2048,512]{1,0:T(8,128)(2,1)S(1)} %copy-done.4, bf16[2048,512]{1,0:T(8,128)(2,1)} %collective-permute-done.14.other_h, bf16[8,448,128]{2,1,0:T(8,128)(2,1)S(1)} %get-tuple-element.137.own_ref, ...), custom_call_target="tpu_custom_call" | custom-call | flops 2147483648 | bytes 8388608 | tf_op jit(solution)/shard_map/down_send/pallas_call | solution.py:257
  291.5 0.8 collective-permute-start.27
  292.3 1.7 collective-permute-start.28
  294.3 3.5 down_keep.2
  298.4 4.6 %down_keep.3 = (f32[1024,384]{1,0:T(8,128)S(1)}, f32[1024,384]{1,0:T(8,128)S(1)}, f32[1024,256]{1,0:T(8,128)S(1)}) custom-call(bf16[2048,512]{1,0:T(8,128)(2,1)S(1)} %copy-done.4, bf16[2048,512]{1,0:T(8,128)(2,1)} %collective-permute-done.14.other_h, bf16[8,448,128]{2,1,0:T(8,128)(2,1)S(1)} %get-tuple-element.137.own_ref, ...), custom_call_target="tpu_custom_call" | custom-call | flops 2147483648 | bytes 8388608 | tf_op jit(solution)/shard_map/down_keep/pallas_call | solution.py:257
  303.1 3.2 collective-permute-done.29.refs_5_
  306.3 4.0 %collective-permute-done.27.refs_1_ = bf16[1024,384]{1,0:T(8,128)(2,1)S(1)} collective-permute-done((bf16[1024,384]{1,0:T(8,128)(2,1)S(1)}, bf16[1024,384]{1,0:T(8,128)(2,1)S(1)}, u32[]{:S(2)}, u32[]{:S(2)}) %collective-permute-start.27) | collective-permute-done | bytes 786464 | tf_op jit(solution)/shard_map/ppermute | solution.py:317
  310.3 2.5 collective-permute-done.28.refs_3_
  313.1 1.7 collective-permute-start.30
  315.1 1.7 collective-permute-start.20
  316.9 1.3 collective-permute-start.21
  318.4 1.3 collective-permute-start.32
  319.7 8.9 %collective-permute-done.20.refs_3_ = bf16[512,256]{1,0:T(8,128)(2,1)S(1)} collective-permute-done((bf16[512,256]{1,0:T(8,128)(2,1)S(1)}, bf16[512,256]{1,0:T(8,128)(2,1)S(1)}, u32[]{:S(2)}, u32[]{:S(2)}) %collective-permute-start.20) | collective-permute-done | bytes 262176 | tf_op jit(solution)/shard_map/ppermute | solution.py:317
  328.7 1.4 collective-permute-start.22
  330.0 1.3 collective-permute-start.23
  331.8 1.8 collective-permute-start.33
  335.0 1.3 collective-permute-done.24.refs_5_
  336.3 0.9 collective-permute-start.25
  337.2 1.1 collective-permute-start.35
  338.3 3.9 %collective-permute-done.35.refs_5_ = bf16[256,256]{1,0:T(8,128)(2,1)S(1)} collective-permute-done((bf16[256,256]{1,0:T(8,128)(2,1)S(1)}, bf16[256,256]{1,0:T(8,128)(2,1)S(1)}, u32[]{:S(2)}, u32[]{:S(2)}) %collective-permute-start.35) | collective-permute-done | bytes 131104 | tf_op jit(solution)/shard_map/ppermute | solution.py:317
  342.3 2.2 collective-permute-start.36
  344.8 6.4 %collective-permute-done.36 = bf16[128,1024]{1,0:T(8,128)(2,1)S(1)} collective-permute-done((bf16[128,1024]{1,0:T(8,128)(2,1)S(1)}, bf16[128,1024]{1,0:T(8,128)(2,1)S(1)}, u32[]{:S(2)}, u32[]{:S(2)}) %collective-permute-start.36) | collective-permute-done | bytes 262176 | tf_op jit(solution)/shard_map/ppermute | solution.py:317
  351.4 1.0 copy.15
  (97 shorter events, 19.2 us)
Async XLA Ops:
  0.0 22.4 %collective-permute-start = (bf16[128,1792]{1,0:T(8,128)(2,1)}, bf16[128,1792]{1,0:T(8,128)(2,1)S(1)}, u32[]{:S(2)}, u32[]{:S(2)}) collective-permute-start(bf16[128,1792]{1,0:T(8,128)(2,1)} %param.9), channel_id=1, source_target_pairs={{0,16},{2,18},{4,20},{6,22},{8,24},{10,26},{12,28},{14,30},{16,0},... | collective-permute-start | bytes 1376264 | tf_op jit(solution)/shard_map/ppermute | solution.py:317
  2.6 23.5 %collective-permute-start.1 = (bf16[128,1792]{1,0:T(8,128)(2,1)}, bf16[128,1792]{1,0:T(8,128)(2,1)S(1)}, u32[]{:S(2)}, u32[]{:S(2)}) collective-permute-start(bf16[128,1792]{1,0:T(8,128)(2,1)} %param.9), channel_id=1, source_target_pairs={{0,2},{2,0},{4,6},{6,4},{8,10},{10,8},{12,14},{14,12},{16,18},{18,... | collective-permute-start | bytes 1376264 | tf_op jit(solution)/shard_map/ppermute | solution.py:317
  3.1 23.2 %collective-permute-start.2 = (bf16[128,1792]{1,0:T(8,128)(2,1)}, bf16[128,1792]{1,0:T(8,128)(2,1)S(1)}, u32[]{:S(2)}, u32[]{:S(2)}) collective-permute-start(bf16[128,1792]{1,0:T(8,128)(2,1)} %param.9), channel_id=1, source_target_pairs={{0,4},{2,6},{4,0},{6,2},{8,12},{10,14},{12,8},{14,10},{16,20},{18,... | collective-permute-start | bytes 1376264 | tf_op jit(solution)/shard_map/ppermute | solution.py:317
  3.6 22.7 %collective-permute-start.3 = (bf16[128,1792]{1,0:T(8,128)(2,1)}, bf16[128,1792]{1,0:T(8,128)(2,1)S(1)}, u32[]{:S(2)}, u32[]{:S(2)}) collective-permute-start(bf16[128,1792]{1,0:T(8,128)(2,1)} %param.9), channel_id=1, source_target_pairs={{0,6},{2,4},{4,2},{6,0},{8,14},{10,12},{12,10},{14,8},{16,22},{18,... | collective-permute-start | bytes 1376264 | tf_op jit(solution)/shard_map/ppermute | solution.py:378
  6.1 19.3 %collective-permute-start.4 = (bf16[128,1792]{1,0:T(8,128)(2,1)}, bf16[128,1792]{1,0:T(8,128)(2,1)S(1)}, u32[]{:S(2)}, u32[]{:S(2)}) collective-permute-start(bf16[128,1792]{1,0:T(8,128)(2,1)} %param.9), channel_id=1, source_target_pairs={{0,8},{2,10},{4,12},{6,14},{8,0},{10,2},{12,4},{14,6},{16,24},{18,... | collective-permute-start | bytes 1376264 | tf_op jit(solution)/shard_map/ppermute | solution.py:317
  10.4 2.0 copy-start
  12.4 2.0 copy-start.2
  14.4 2.0 copy-start.3
  22.4 12.4 %collective-permute-start.5 = (bf16[128,1792]{1,0:T(8,128)(2,1)S(1)}, bf16[128,1792]{1,0:T(8,128)(2,1)S(1)}, u32[]{:S(2)}, u32[]{:S(2)}) collective-permute-start(bf16[128,1792]{1,0:T(8,128)(2,1)S(1)} %collective-permute-done), channel_id=1, source_target_pairs={{0,8},{2,10},{4,12},{6,14},{8,0},{10,2},{12,4},{14,6},{16,24},{18,... | collective-permute-start | bytes 1376264 | tf_op jit(solution)/shard_map/ppermute | solution.py:317
  25.5 9.6 %collective-permute-start.6 = (bf16[256,896]{1,0:T(8,128)(2,1)S(1)}, bf16[256,896]{1,0:T(8,128)(2,1)S(1)}, u32[]{:S(2)}, u32[]{:S(2)}) collective-permute-start(bf16[256,896]{1,0:T(8,128)(2,1)S(1)} %get-tuple-element.168), channel_id=1, source_target_pairs={{0,4},{2,6},{4,0},{6,2},{8,12},{10,14},{12,8},{14,10},{16,20},{18,... | collective-permute-start | bytes 1376264 | tf_op jit(solution)/shard_map/ppermute | solution.py:317
  26.1 17.4 %copy-start.11 = (bf16[128,1792]{1,0:T(8,128)(2,1)S(1)}, bf16[128,1792]{1,0:T(8,128)(2,1)}, u32[]{:S(2)}) copy-start(bf16[128,1792]{1,0:T(8,128)(2,1)} %param.9) | copy-start | bytes 1376260
  26.1 9.6 %collective-permute-start.7 = (bf16[256,896]{1,0:T(8,128)(2,1)S(1)}, bf16[256,896]{1,0:T(8,128)(2,1)S(1)}, u32[]{:S(2)}, u32[]{:S(2)}) collective-permute-start(bf16[256,896]{1,0:T(8,128)(2,1)S(1)} %get-tuple-element.167), channel_id=1, source_target_pairs={{0,2},{2,0},{4,6},{6,4},{8,10},{10,8},{12,14},{14,12},{16,18},{18,... | collective-permute-start | bytes 1376264 | tf_op jit(solution)/shard_map/ppermute | solution.py:317
  26.4 8.8 %copy-start.12 = (bf16[128,1792]{1,0:T(8,128)(2,1)}, bf16[128,1792]{1,0:T(8,128)(2,1)S(1)}, u32[]{:S(2)}) copy-start(bf16[128,1792]{1,0:T(8,128)(2,1)S(1)} %collective-permute-done.2) | copy-start | bytes 1376260
  34.9 0.8 copy-start.14
  35.7 186.6 %all-to-all-start = ((bf16[16,1920,128]{2,1,0:T(8,128)(2,1)}), bf16[16,1920,128]{2,1,0:T(8,128)(2,1)}, u32[]{:S(2)}, u32[]{:S(2)}) async-start(bf16[16,1920,128]{2,1,0:T(8,128)(2,1)} %pack_first.1), calls=%async_computation | async-start | bytes 15728640 | tf_op jit(solution)/shard_map/all_to_all | solution.py:366
  43.5 1.9 copy-start.15
  45.4 5.8 %copy-start.13 = (bf16[128,1792]{1,0:T(8,128)(2,1)S(1)}, bf16[128,1792]{1,0:T(8,128)(2,1)}, u32[]{:S(2)}) copy-start(bf16[128,1792]{1,0:T(8,128)(2,1)} %copy-done.12) | copy-start | bytes 1376260
  46.3 95.0 %collective-permute-start.11 = (bf16[640,896]{1,0:T(8,128)(2,1)S(1)}, bf16[640,896]{1,0:T(8,128)(2,1)S(1)}, u32[]{:S(2)}, u32[]{:S(2)}) collective-permute-start(bf16[640,896]{1,0:T(8,128)(2,1)S(1)} %pad_maximum_fusion.2), channel_id=1, source_target_pairs={{0,4},{2,6},{4,0},{6,2},{8,12},{10,14},{12,8},{14,10},{16,20},{18,... | collective-permute-start | bytes 3440648 | tf_op jit(solution)/shard_map/ppermute | solution.py:317
  47.0 97.0 %collective-permute-start.12 = (bf16[128,896]{1,0:T(8,128)(2,1)S(1)}, bf16[128,896]{1,0:T(8,128)(2,1)S(1)}, u32[]{:S(2)}, u32[]{:S(2)}) collective-permute-start(bf16[128,896]{1,0:T(8,128)(2,1)S(1)} %get-tuple-element.178), channel_id=1, source_target_pairs={{0,2},{2,0},{4,6},{6,4},{8,10},{10,8},{12,14},{14,12},{16,18},{18,... | collective-permute-start | bytes 688136 | tf_op jit(solution)/shard_map/ppermute | solution.py:317
  47.5 107.2 %collective-permute-start.10 = (bf16[128,1792]{1,0:T(8,128)(2,1)S(1)}, bf16[128,1792]{1,0:T(8,128)(2,1)S(1)}, u32[]{:S(2)}, u32[]{:S(2)}) collective-permute-start(bf16[128,1792]{1,0:T(8,128)(2,1)S(1)} %copy-done.15), channel_id=1, source_target_pairs={{0,6},{2,4},{4,2},{6,0},{8,14},{10,12},{12,10},{14,8},{16,22},{18,... | collective-permute-start | bytes 1376264 | tf_op jit(solution)/shard_map/ppermute | solution.py:378
  49.9 90.7 %collective-permute-start.8 = (bf16[128,896]{1,0:T(8,128)(2,1)S(1)}, bf16[128,896]{1,0:T(8,128)(2,1)S(1)}, u32[]{:S(2)}, u32[]{:S(2)}) collective-permute-start(bf16[128,896]{1,0:T(8,128)(2,1)S(1)} %get-tuple-element.175), channel_id=1, source_target_pairs={{0,4},{2,6},{4,0},{6,2},{8,12},{10,14},{12,8},{14,10},{16,20},{18,... | collective-permute-start | bytes 688136 | tf_op jit(solution)/shard_map/ppermute | solution.py:317
  50.5 101.4 %collective-permute-start.9 = (bf16[640,896]{1,0:T(8,128)(2,1)S(1)}, bf16[640,896]{1,0:T(8,128)(2,1)S(1)}, u32[]{:S(2)}, u32[]{:S(2)}) collective-permute-start(bf16[640,896]{1,0:T(8,128)(2,1)S(1)} %pad_maximum_fusion.1), channel_id=1, source_target_pairs={{0,2},{2,0},{4,6},{6,4},{8,10},{10,8},{12,14},{14,12},{16,18},{18,... | collective-permute-start | bytes 3440648 | tf_op jit(solution)/shard_map/ppermute | solution.py:317
  162.2 12.0 %collective-permute-start.13 = (bf16[2048,1792]{1,0:T(8,128)(2,1)}, bf16[2048,1792]{1,0:T(8,128)(2,1)}, u32[]{:S(2)}, u32[]{:S(2)}) collective-permute-start(bf16[2048,1792]{1,0:T(8,128)(2,1)} %pad_maximum_fusion.own_ref), channel_id=1, source_target_pairs={{0,1},{1,0},{2,3},{3,2},{4,5},{5,4},{6,7},{7,6},{8,9},{9,8},{10,11... | collective-permute-start | bytes 22020104 | tf_op jit(solution)/shard_map/ppermute | solution.py:363
  162.2 2.0 copy-start.1
  222.3 47.4 %all-to-all-start.1 = ((bf16[16,448,128]{2,1,0:T(8,128)(2,1)}), bf16[16,448,128]{2,1,0:T(8,128)(2,1)}, u32[]{:S(2)}, u32[]{:S(2)}) async-start(bf16[16,448,128]{2,1,0:T(8,128)(2,1)} %pack_rest.1), calls=%async_computation.1 | async-start | bytes 3670016 | tf_op jit(solution)/shard_map/all_to_all | solution.py:366
  252.5 5.2 %copy-start.4 = (bf16[2048,512]{1,0:T(8,128)(2,1)S(1)}, bf16[2048,512]{1,0:T(8,128)(2,1)}, u32[]{:S(2)}) copy-start(bf16[2048,512]{1,0:T(8,128)(2,1)} %hidden.1.own_h) | copy-start | bytes 6291460
  252.5 5.1 %collective-permute-start.14 = (bf16[2048,512]{1,0:T(8,128)(2,1)}, bf16[2048,512]{1,0:T(8,128)(2,1)}, u32[]{:S(2)}, u32[]{:S(2)}) collective-permute-start(bf16[2048,512]{1,0:T(8,128)(2,1)} %hidden.1.own_h), channel_id=1, source_target_pairs={{0,1},{1,0},{2,3},{3,2},{4,5},{5,4},{6,7},{7,6},{8,9},{9,8},{10,11... | collective-permute-start | bytes 6291464 | tf_op jit(solution)/shard_map/ppermute | solution.py:363
  254.2 3.4 collective-permute-start.15
  261.1 0.8 copy-start.5
  261.9 0.8 copy-start.7
  262.7 0.8 copy-start.9
  269.6 1.8 copy-start.10
  269.6 3.1 copy-start.8
  269.6 3.2 copy-start.6
  271.4 15.5 %collective-permute-start.26 = (bf16[8,448,128]{2,1,0:T(8,128)(2,1)S(1)}, bf16[8,448,128]{2,1,0:T(8,128)(2,1)S(1)}, u32[]{:S(2)}, u32[]{:S(2)}) collective-permute-start(bf16[8,448,128]{2,1,0:T(8,128)(2,1)S(1)} %get-tuple-element.159), channel_id=1, source_target_pairs={{0,1},{1,0},{2,3},{3,2},{4,5},{5,4},{6,7},{7,6},{8,9},{9,8},{10,11... | collective-permute-start | bytes 2752520 | tf_op jit(solution)/shard_map/ppermute | solution.py:363
  271.4 14.3 %collective-permute-start.16 = (bf16[1024,256]{1,0:T(8,128)(2,1)S(1)}, bf16[1024,256]{1,0:T(8,128)(2,1)S(1)}, u32[]{:S(2)}, u32[]{:S(2)}) collective-permute-start(bf16[1024,256]{1,0:T(8,128)(2,1)S(1)} %copy-done.10), channel_id=1, source_target_pairs={{0,2},{2,0},{4,6},{6,4},{8,10},{10,8},{12,14},{14,12},{16,18},{18,... | collective-permute-start | bytes 1572872 | tf_op jit(solution)/shard_map/ppermute | solution.py:317
  272.8 14.0 %collective-permute-start.17 = (bf16[1024,256]{1,0:T(8,128)(2,1)S(1)}, bf16[1024,256]{1,0:T(8,128)(2,1)S(1)}, u32[]{:S(2)}, u32[]{:S(2)}) collective-permute-start(bf16[1024,256]{1,0:T(8,128)(2,1)S(1)} %copy-done.8), channel_id=1, source_target_pairs={{0,4},{2,6},{4,0},{6,2},{8,12},{10,14},{12,8},{14,10},{16,20},{18,... | collective-permute-start | bytes 1572872 | tf_op jit(solution)/shard_map/ppermute | solution.py:317
  272.8 14.0 %collective-permute-start.18 = (bf16[1024,256]{1,0:T(8,128)(2,1)S(1)}, bf16[1024,256]{1,0:T(8,128)(2,1)S(1)}, u32[]{:S(2)}, u32[]{:S(2)}) collective-permute-start(bf16[1024,256]{1,0:T(8,128)(2,1)S(1)} %copy-done.6), channel_id=1, source_target_pairs={{0,8},{2,10},{4,12},{6,14},{8,0},{10,2},{12,4},{14,6},{16,24},{18,... | collective-permute-start | bytes 1572872 | tf_op jit(solution)/shard_map/ppermute | solution.py:317
  291.5 18.8 %collective-permute-start.27 = (bf16[1024,384]{1,0:T(8,128)(2,1)S(1)}, bf16[1024,384]{1,0:T(8,128)(2,1)S(1)}, u32[]{:S(2)}, u32[]{:S(2)}) collective-permute-start(bf16[1024,384]{1,0:T(8,128)(2,1)S(1)} %get-tuple-element.140), channel_id=1, source_target_pairs={{0,2},{2,0},{4,6},{6,4},{8,10},{10,8},{12,14},{14,12},{16,18},{18,... | collective-permute-start | bytes 2359304 | tf_op jit(solution)/shard_map/ppermute | solution.py:317
  292.3 20.5 %collective-permute-start.28 = (bf16[1024,384]{1,0:T(8,128)(2,1)S(1)}, bf16[1024,384]{1,0:T(8,128)(2,1)S(1)}, u32[]{:S(2)}, u32[]{:S(2)}) collective-permute-start(bf16[1024,384]{1,0:T(8,128)(2,1)S(1)} %get-tuple-element.142), channel_id=1, source_target_pairs={{0,4},{2,6},{4,0},{6,2},{8,12},{10,14},{12,8},{14,10},{16,20},{18,... | collective-permute-start | bytes 2359304 | tf_op jit(solution)/shard_map/ppermute | solution.py:317
  294.0 12.3 %collective-permute-start.29 = (bf16[1024,256]{1,0:T(8,128)(2,1)S(1)}, bf16[1024,256]{1,0:T(8,128)(2,1)S(1)}, u32[]{:S(2)}, u32[]{:S(2)}) collective-permute-start(bf16[1024,256]{1,0:T(8,128)(2,1)S(1)} %get-tuple-element.144), channel_id=1, source_target_pairs={{0,8},{2,10},{4,12},{6,14},{8,0},{10,2},{12,4},{14,6},{16,24},{18,... | collective-permute-start | bytes 1572872 | tf_op jit(solution)/shard_map/ppermute | solution.py:317
  298.0 20.4 %collective-permute-start.19 = (bf16[512,256]{1,0:T(8,128)(2,1)S(1)}, bf16[512,256]{1,0:T(8,128)(2,1)S(1)}, u32[]{:S(2)}, u32[]{:S(2)}) collective-permute-start(bf16[512,256]{1,0:T(8,128)(2,1)S(1)} %get-tuple-element.113), channel_id=1, source_target_pairs={{0,4},{2,6},{4,0},{6,2},{8,12},{10,14},{12,8},{14,10},{16,20},{18,... | collective-permute-start | bytes 786440 | tf_op jit(solution)/shard_map/ppermute | solution.py:317
  313.1 18.5 %collective-permute-start.30 = (bf16[512,384]{1,0:T(8,128)(2,1)S(1)}, bf16[512,384]{1,0:T(8,128)(2,1)S(1)}, u32[]{:S(2)}, u32[]{:S(2)}) collective-permute-start(bf16[512,384]{1,0:T(8,128)(2,1)S(1)} %get-tuple-element.146), channel_id=1, source_target_pairs={{0,4},{2,6},{4,0},{6,2},{8,12},{10,14},{12,8},{14,10},{16,20},{18,... | collective-permute-start | bytes 1179656 | tf_op jit(solution)/shard_map/ppermute | solution.py:317
  314.9 16.8 %collective-permute-start.31 = (bf16[512,384]{1,0:T(8,128)(2,1)S(1)}, bf16[512,384]{1,0:T(8,128)(2,1)S(1)}, u32[]{:S(2)}, u32[]{:S(2)}) collective-permute-start(bf16[512,384]{1,0:T(8,128)(2,1)S(1)} %get-tuple-element.148), channel_id=1, source_target_pairs={{0,8},{2,10},{4,12},{6,14},{8,0},{10,2},{12,4},{14,6},{16,24},{18,... | collective-permute-start | bytes 1179656 | tf_op jit(solution)/shard_map/ppermute | solution.py:317
  315.1 13.4 %collective-permute-start.20 = (bf16[512,256]{1,0:T(8,128)(2,1)S(1)}, bf16[512,256]{1,0:T(8,128)(2,1)S(1)}, u32[]{:S(2)}, u32[]{:S(2)}) collective-permute-start(bf16[512,256]{1,0:T(8,128)(2,1)S(1)} %get-tuple-element.115), channel_id=1, source_target_pairs={{0,8},{2,10},{4,12},{6,14},{8,0},{10,2},{12,4},{14,6},{16,24},{18,... | collective-permute-start | bytes 786440 | tf_op jit(solution)/shard_map/ppermute | solution.py:317
  316.9 11.6 %collective-permute-start.21 = (bf16[512,256]{1,0:T(8,128)(2,1)S(1)}, bf16[512,256]{1,0:T(8,128)(2,1)S(1)}, u32[]{:S(2)}, u32[]{:S(2)}) collective-permute-start(bf16[512,256]{1,0:T(8,128)(2,1)S(1)} %get-tuple-element.117), channel_id=1, source_target_pairs={{0,2},{2,0},{4,6},{6,4},{8,10},{10,8},{12,14},{14,12},{16,18},{18,... | collective-permute-start | bytes 786440 | tf_op jit(solution)/shard_map/ppermute | solution.py:317
  318.4 12.9 %collective-permute-start.32 = (bf16[512,256]{1,0:T(8,128)(2,1)S(1)}, bf16[512,256]{1,0:T(8,128)(2,1)S(1)}, u32[]{:S(2)}, u32[]{:S(2)}) collective-permute-start(bf16[512,256]{1,0:T(8,128)(2,1)S(1)} %get-tuple-element.150), channel_id=1, source_target_pairs={{0,2},{2,0},{4,6},{6,4},{8,10},{10,8},{12,14},{14,12},{16,18},{18,... | collective-permute-start | bytes 786440 | tf_op jit(solution)/shard_map/ppermute | solution.py:317
  328.7 5.8 %collective-permute-start.22 = (bf16[256,256]{1,0:T(8,128)(2,1)S(1)}, bf16[256,256]{1,0:T(8,128)(2,1)S(1)}, u32[]{:S(2)}, u32[]{:S(2)}) collective-permute-start(bf16[256,256]{1,0:T(8,128)(2,1)S(1)} %get-tuple-element.119), channel_id=1, source_target_pairs={{0,8},{2,10},{4,12},{6,14},{8,0},{10,2},{12,4},{14,6},{16,24},{18,... | collective-permute-start | bytes 393224 | tf_op jit(solution)/shard_map/ppermute | solution.py:317
  330.0 5.0 %collective-permute-start.23 = (bf16[256,256]{1,0:T(8,128)(2,1)S(1)}, bf16[256,256]{1,0:T(8,128)(2,1)S(1)}, u32[]{:S(2)}, u32[]{:S(2)}) collective-permute-start(bf16[256,256]{1,0:T(8,128)(2,1)S(1)} %get-tuple-element.121), channel_id=1, source_target_pairs={{0,2},{2,0},{4,6},{6,4},{8,10},{10,8},{12,14},{14,12},{16,18},{18,... | collective-permute-start | bytes 393224 | tf_op jit(solution)/shard_map/ppermute | solution.py:317
  331.3 5.0 %collective-permute-start.24 = (bf16[256,256]{1,0:T(8,128)(2,1)S(1)}, bf16[256,256]{1,0:T(8,128)(2,1)S(1)}, u32[]{:S(2)}, u32[]{:S(2)}) collective-permute-start(bf16[256,256]{1,0:T(8,128)(2,1)S(1)} %get-tuple-element.123), channel_id=1, source_target_pairs={{0,4},{2,6},{4,0},{6,2},{8,12},{10,14},{12,8},{14,10},{16,20},{18,... | collective-permute-start | bytes 393224 | tf_op jit(solution)/shard_map/ppermute | solution.py:317
  331.8 10.3 %collective-permute-start.33 = (bf16[256,384]{1,0:T(8,128)(2,1)S(1)}, bf16[256,384]{1,0:T(8,128)(2,1)S(1)}, u32[]{:S(2)}, u32[]{:S(2)}) collective-permute-start(bf16[256,384]{1,0:T(8,128)(2,1)S(1)} %get-tuple-element.152), channel_id=1, source_target_pairs={{0,8},{2,10},{4,12},{6,14},{8,0},{10,2},{12,4},{14,6},{16,24},{18,... | collective-permute-start | bytes 589832 | tf_op jit(solution)/shard_map/ppermute | solution.py:317
  333.7 8.5 %collective-permute-start.34 = (bf16[256,384]{1,0:T(8,128)(2,1)S(1)}, bf16[256,384]{1,0:T(8,128)(2,1)S(1)}, u32[]{:S(2)}, u32[]{:S(2)}) collective-permute-start(bf16[256,384]{1,0:T(8,128)(2,1)S(1)} %get-tuple-element.154), channel_id=1, source_target_pairs={{0,2},{2,0},{4,6},{6,4},{8,10},{10,8},{12,14},{14,12},{16,18},{18,... | collective-permute-start | bytes 589832 | tf_op jit(solution)/shard_map/ppermute | solution.py:317
  336.3 8.3 %collective-permute-start.25 = (bf16[128,768]{1,0:T(8,128)(2,1)S(1)}, bf16[128,768]{1,0:T(8,128)(2,1)S(1)}, u32[]{:S(2)}, u32[]{:S(2)}) collective-permute-start(bf16[128,768]{1,0:T(8,128)(2,1)S(1)} %get-tuple-element.125), channel_id=1, source_target_pairs={{0,16},{2,18},{4,20},{6,22},{8,24},{10,26},{12,28},{14,30},{16,0},... | collective-permute-start | bytes 589832 | tf_op jit(solution)/shard_map/ppermute | solution.py:317
  337.2 5.0 %collective-permute-start.35 = (bf16[256,256]{1,0:T(8,128)(2,1)S(1)}, bf16[256,256]{1,0:T(8,128)(2,1)S(1)}, u32[]{:S(2)}, u32[]{:S(2)}) collective-permute-start(bf16[256,256]{1,0:T(8,128)(2,1)S(1)} %get-tuple-element.156), channel_id=1, source_target_pairs={{0,4},{2,6},{4,0},{6,2},{8,12},{10,14},{12,8},{14,10},{16,20},{18,... | collective-permute-start | bytes 393224 | tf_op jit(solution)/shard_map/ppermute | solution.py:317
  342.3 8.9 %collective-permute-start.36 = (bf16[128,1024]{1,0:T(8,128)(2,1)S(1)}, bf16[128,1024]{1,0:T(8,128)(2,1)S(1)}, u32[]{:S(2)}, u32[]{:S(2)}) collective-permute-start(bf16[128,1024]{1,0:T(8,128)(2,1)S(1)} %get-tuple-element.158), channel_id=1, source_target_pairs={{0,16},{2,18},{4,20},{6,22},{8,24},{10,26},{12,28},{14,30},{16,0},... | collective-permute-start | bytes 786440 | tf_op jit(solution)/shard_map/ppermute | solution.py:317

commit v18 on v17

--- a/solution.py
+++ b/solution.py
@@ -380,7 +380,7 @@
     mid = tokens.shape[1] // 2
     near, far = swap(tokens, 2), swap(tokens, 3)
     x_own, y_own, xy_own = swap(tokens, 0), swap(tokens, 1), diagonal(tokens)
-    parts = (96, 128)
+    parts = (128, 96)
     packed = pack_first(listing, gate_proj, up_proj, down_proj, parts[0], share, devices)
     far, packed = tie((far, packed))
     corner = swap(far, 2)

time: 357 us -> 351 us (0.983)
  Pallas kernels: 47.7 us -> 42 us
  waiting for transfers between devices: 216 us -> 211 us
    pallas_call x4, Pallas kernels: 16.2 us -> 10.5 us  [down_product(): pl.pallas_call(functools.partial(down_kernel, rows, side, orders), out_sh...]
    ppermute x31, waiting for transfers between devices: 151 us -> 148 us  [swap(): return lax.ppermute(value, 'ep', [(i, i ^ 1 << bit) for i in range(size)])]
    unnamed x44 -> x46, local copies, waits for them, and re-layouts: 20.4 us -> 22.4 us
  transfers between devices with their start and end apart: 39 -> 39, of which waited for: 23 -> 24; matrix products, arithmetic and copies ran while one was open for 7% -> 8% of each run, Pallas kernels for 12% -> 12%
where the time goes in v18:
time: 351 us; the launch traced here: 347 us
  waiting for transfers between devices  211 us (60%)
  starting transfers between devices  52.3 us (15%)
  Pallas kernels  42 us (12%)
  local copies, waits for them, and re-layouts  30 us (9%)
  other arithmetic  11.3 us (3%)
    ppermute x31, waiting for transfers between devices, swap(): return lax.ppermute(value, 'ep', [(i, i ^ 1 << bit) for i in range(size)])  148 us
    all_to_all x2, waiting for transfers between devices, move(): return lax.all_to_all(packed, 'ep', 0, 0, tiled=True)  52.7 us
    ppermute x31, starting transfers between devices, swap(): return lax.ppermute(value, 'ep', [(i, i ^ 1 << bit) for i in range(size)])  31.1 us
    pallas_call x1, Pallas kernels, hidden_units(): pl.pallas_call(hidden_kernel, grid=(8,), out_shape=jax.ShapeDtypeStruct((...  23.3 us
    unnamed x46, local copies, waits for them, and re-layouts  22.4 us
    all_to_all x2, starting transfers between devices, move(): return lax.all_to_all(packed, 'ep', 0, 0, tiled=True)  15.7 us
    pallas_call x4, Pallas kernels, down_product(): pl.pallas_call(functools.partial(down_kernel, rows, side, orders), out_sh...  10.5 us
    ppermute x4, waiting for transfers between devices, exchange(): return lax.ppermute(value, 'et', [(0, 1), (1, 0)])  10.5 us
  transfers between devices with their start and end apart: 39, of which 24 were waited for; matrix products, arithmetic and copies ran while one was open for 8% of the time, Pallas kernels for 12%

profile of v18, /device:TPU:14, one launch (start us, length us, event | category | flops | bytes accessed | tf_op | source)
XLA Modules:
  0.0 346.8 jit_solution(12901967932816172496)
XLA Ops:
  0.0 2.6 collective-permute-start
  3.6 2.4 collective-permute-start.3
  6.5 0.9 select_reduce_fusion.4
  9.4 0.9 select_reduce_fusion.share_ref
  10.4 2.0 copy-done
  12.4 2.0 copy-done.2
  14.4 2.0 copy-done.3
  16.5 5.4 %pack_first.1 = bf16[16,2032,128]{2,1,0:T(8,128)(2,1)} custom-call(s32[14]{0:T(128)S(1)} %select_reduce_fusion.3.list_ref, bf16[16,224,512]{2,1,0:T(8,128)(2,1)S(1)} %copy-done.2, bf16[16,224,512]{2,1,0:T(8,128)(2,1)S(1)} %copy-done.3, bf16[16,224,512]{2,1,0:T(8,128)(2,1)S(1)} %copy-done, f32[16,16,128]{2,1,0:T(8,128)S(1)} %select_reduce_fusion.share_ref), custom_call_target="tpu_custom_call" | custom-call | tf_op jit(solution)/shard_map/pack_first/pallas_call | solution.py:113
  22.4 1.3 collective-permute-start.5
  23.8 1.6 collective-permute-done.4
  26.4 8.5 %collective-permute-done.5 = bf16[128,1792]{1,0:T(8,128)(2,1)S(1)} collective-permute-done((bf16[128,1792]{1,0:T(8,128)(2,1)S(1)}, bf16[128,1792]{1,0:T(8,128)(2,1)S(1)}, u32[]{:S(2)}, u32[]{:S(2)}) %collective-permute-start.5) | collective-permute-done | bytes 458784 | tf_op jit(solution)/shard_map/ppermute | solution.py:317
  35.7 7.9 %all-to-all-start = ((bf16[16,2032,128]{2,1,0:T(8,128)(2,1)}), bf16[16,2032,128]{2,1,0:T(8,128)(2,1)}, u32[]{:S(2)}, u32[]{:S(2)}) async-start(bf16[16,2032,128]{2,1,0:T(8,128)(2,1)} %pack_first.1), calls=%async_computation | async-start | bytes 16646144 | tf_op jit(solution)/shard_map/all_to_all | solution.py:366
  43.5 0.8 slice_dynamic-update-slice_fusion.13
  44.4 1.2 fusion.3
  45.5 0.9 fusion.5
  47.7 2.4 collective-permute-start.10
  51.3 0.8 slice_dynamic-update-slice_fusion.12
  53.0 90.7 %collective-permute-done.8 = bf16[128,896]{1,0:T(8,128)(2,1)S(1)} collective-permute-done((bf16[128,896]{1,0:T(8,128)(2,1)S(1)}, bf16[128,896]{1,0:T(8,128)(2,1)S(1)}, u32[]{:S(2)}, u32[]{:S(2)}) %collective-permute-start.8) | collective-permute-done | bytes 229408 | tf_op jit(solution)/shard_map/ppermute | solution.py:317
  144.4 1.0 slice_dynamic-update-slice_fusion
  145.4 0.8 slice_dynamic-update-slice_fusion.11
  146.2 0.8 constant_dynamic-update-slice_fusion.7
  147.7 8.6 %collective-permute-done.9 = bf16[640,896]{1,0:T(8,128)(2,1)S(1)} collective-permute-done((bf16[640,896]{1,0:T(8,128)(2,1)S(1)}, bf16[640,896]{1,0:T(8,128)(2,1)S(1)}, u32[]{:S(2)}, u32[]{:S(2)}) %collective-permute-start.9) | collective-permute-done | bytes 1146912 | tf_op jit(solution)/shard_map/ppermute | solution.py:317
  156.4 0.9 slice_dynamic-update-slice_fusion.1
  157.3 0.8 slice_dynamic-update-slice_fusion.10
  158.1 1.0 slice_dynamic-update-slice_fusion.2
  160.0 6.6 %pad_maximum_fusion.own_ref = bf16[2048,1792]{1,0:T(8,128)(2,1)} fusion(bf16[2048,896]{1,0:T(8,128)(2,1)} %get-tuple-element.170, bf16[2048,896]{1,0:T(8,128)(2,1)} %get-tuple-element.169), kind=kLoop, calls=%fused_computation | loop fusion | flops 14680064 | bytes 14680064 | tf_op jit(solution)/shard_map/concatenate | solution.py:405
  166.6 2.0 copy-done.1
  168.6 1.9 pack_rest.1
  171.1 7.5 %collective-permute-done.13.other_ref = bf16[2048,1792]{1,0:T(8,128)(2,1)} collective-permute-done((bf16[2048,1792]{1,0:T(8,128)(2,1)}, bf16[2048,1792]{1,0:T(8,128)(2,1)}, u32[]{:S(2)}, u32[]{:S(2)}) %collective-permute-start.13) | collective-permute-done | bytes 7340064 | tf_op jit(solution)/shard_map/ppermute | solution.py:363
  178.6 52.7 %all-to-all-done.packed_ref = bf16[16,2032,128]{2,1,0:T(8,128)(2,1)} async-done(((bf16[16,2032,128]{2,1,0:T(8,128)(2,1)}), bf16[16,2032,128]{2,1,0:T(8,128)(2,1)}, u32[]{:S(2)}, u32[]{:S(2)}) %all-to-all-start) | async-done | bytes 8323104 | tf_op jit(solution)/shard_map/all_to_all | solution.py:366
  231.3 7.8 %all-to-all-start.1 = ((bf16[16,336,128]{2,1,0:T(8,128)(2,1)}), bf16[16,336,128]{2,1,0:T(8,128)(2,1)}, u32[]{:S(2)}, u32[]{:S(2)}) async-start(bf16[16,336,128]{2,1,0:T(8,128)(2,1)} %pack_rest.1), calls=%async_computation.1 | async-start | bytes 2752512 | tf_op jit(solution)/shard_map/all_to_all | solution.py:366
  239.1 23.3 %hidden.1.own_h = bf16[2048,512]{1,0:T(8,128)(2,1)} custom-call(s32[2]{0:T(128)} %pad_add_fusion.at_ref, bf16[2048,1792]{1,0:T(8,128)(2,1)} %pad_maximum_fusion.own_ref, bf16[2048,1792]{1,0:T(8,128)(2,1)} %collective-permute-done.13.other_ref, bf16[16,2032,128]{2,1,0:T(8,128)(2,1)} %all-to-all-done.packed_ref), custom_call_target="tpu_custom_call" | custom-call | flops 15032385536 | bytes 25165824 | tf_op jit(solution)/shard_map/hidden/pallas_call | solution.py:196
  262.4 1.8 slice.85
  264.9 3.0 collective-permute-done.15.other_ref
  267.9 3.6 %down_send.2 = (bf16[1024,384]{1,0:T(8,128)(2,1)}, bf16[1024,384]{1,0:T(8,128)(2,1)}, bf16[1024,256]{1,0:T(8,128)(2,1)S(1)}) custom-call(bf16[2048,512]{1,0:T(8,128)(2,1)S(1)} %copy-done.4, bf16[2048,512]{1,0:T(8,128)(2,1)S(1)} %collective-permute-done.14.other_h, bf16[8,448,128]{2,1,0:T(8,128)(2,1)S(1)} %get-tuple-element.104.own_ref, ...), custom_call_target="tpu_custom_call" | custom-call | flops 2147483648 | bytes 8388608 | tf_op jit(solution)/shard_map/down_send/pallas_call | solution.py:257
  272.7 1.4 constant_dynamic-slice_fusion
  274.4 1.6 copy-done.5
  276.0 1.6 copy-done.8
  277.5 1.2 copy-done.11
  278.7 3.0 down_keep.2
  281.8 6.7 %collective-permute-done.18.refs_5_ = bf16[1024,256]{1,0:T(8,128)(2,1)S(1)} collective-permute-done((bf16[1024,256]{1,0:T(8,128)(2,1)S(1)}, bf16[1024,256]{1,0:T(8,128)(2,1)S(1)}, u32[]{:S(2)}, u32[]{:S(2)}) %collective-permute-start.18) | collective-permute-done | bytes 524320 | tf_op jit(solution)/shard_map/ppermute | solution.py:317
  288.5 2.8 collective-permute-done.16.refs_1_
  292.0 1.5 collective-permute-start.21
  293.5 1.9 down_send.3
  297.0 1.7 collective-permute-start.28
  298.6 2.6 collective-permute-done.21.refs_5_
  301.8 6.3 %collective-permute-done.19.refs_1_ = bf16[512,384]{1,0:T(8,128)(2,1)S(1)} collective-permute-done((bf16[512,384]{1,0:T(8,128)(2,1)S(1)}, bf16[512,384]{1,0:T(8,128)(2,1)S(1)}, u32[]{:S(2)}, u32[]{:S(2)}) %collective-permute-start.19) | collective-permute-done | bytes 393248 | tf_op jit(solution)/shard_map/ppermute | solution.py:317
  309.2 1.7 collective-permute-start.23
  310.9 1.6 collective-permute-done.27.refs_1_
  313.1 1.9 down_keep.3
  315.0 4.0 %collective-permute-done.28.refs_3_ = bf16[1024,256]{1,0:T(8,128)(2,1)S(1)} collective-permute-done((bf16[1024,256]{1,0:T(8,128)(2,1)S(1)}, bf16[1024,256]{1,0:T(8,128)(2,1)S(1)}, u32[]{:S(2)}, u32[]{:S(2)}) %collective-permute-start.28) | collective-permute-done | bytes 524320 | tf_op jit(solution)/shard_map/ppermute | solution.py:317
  319.0 0.9 collective-permute-done.29.refs_5_
  320.2 1.5 collective-permute-start.30
  322.2 1.5 collective-permute-start.32
  323.7 1.1 collective-permute-done.22.refs_1_
  324.9 4.2 %collective-permute-start.25 = (bf16[128,1024]{1,0:T(8,128)(2,1)S(1)}, bf16[128,1024]{1,0:T(8,128)(2,1)S(1)}, u32[]{:S(2)}, u32[]{:S(2)}) collective-permute-start(bf16[128,1024]{1,0:T(8,128)(2,1)S(1)} %get-tuple-element.125), channel_id=1, source_target_pairs={{0,16},{2,18},{4,20},{6,22},{8,24},{10,26},{12,28},{14,30},{16,0},... | collective-permute-start | bytes 786440 | tf_op jit(solution)/shard_map/ppermute | solution.py:317
  329.1 1.5 collective-permute-done.31.refs_3_
  330.9 1.7 collective-permute-start.34
  332.5 0.8 collective-permute-start.35
  333.3 2.5 collective-permute-done.33.refs_1_
  335.9 1.6 collective-permute-done.35.refs_5_
  337.6 2.9 collective-permute-start.36
  340.7 4.8 %collective-permute-done.36 = bf16[128,768]{1,0:T(8,128)(2,1)S(1)} collective-permute-done((bf16[128,768]{1,0:T(8,128)(2,1)S(1)}, bf16[128,768]{1,0:T(8,128)(2,1)S(1)}, u32[]{:S(2)}, u32[]{:S(2)}) %collective-permute-start.36) | collective-permute-done | bytes 196640 | tf_op jit(solution)/shard_map/ppermute | solution.py:317
  345.8 1.0 copy.15
  (99 shorter events, 20.4 us)
Async XLA Ops:
  0.0 22.4 %collective-permute-start = (bf16[128,1792]{1,0:T(8,128)(2,1)}, bf16[128,1792]{1,0:T(8,128)(2,1)S(1)}, u32[]{:S(2)}, u32[]{:S(2)}) collective-permute-start(bf16[128,1792]{1,0:T(8,128)(2,1)} %param.9), channel_id=1, source_target_pairs={{0,16},{2,18},{4,20},{6,22},{8,24},{10,26},{12,28},{14,30},{16,0},... | collective-permute-start | bytes 1376264 | tf_op jit(solution)/shard_map/ppermute | solution.py:317
  2.6 23.5 %collective-permute-start.1 = (bf16[128,1792]{1,0:T(8,128)(2,1)}, bf16[128,1792]{1,0:T(8,128)(2,1)S(1)}, u32[]{:S(2)}, u32[]{:S(2)}) collective-permute-start(bf16[128,1792]{1,0:T(8,128)(2,1)} %param.9), channel_id=1, source_target_pairs={{0,2},{2,0},{4,6},{6,4},{8,10},{10,8},{12,14},{14,12},{16,18},{18,... | collective-permute-start | bytes 1376264 | tf_op jit(solution)/shard_map/ppermute | solution.py:317
  3.1 23.2 %collective-permute-start.2 = (bf16[128,1792]{1,0:T(8,128)(2,1)}, bf16[128,1792]{1,0:T(8,128)(2,1)S(1)}, u32[]{:S(2)}, u32[]{:S(2)}) collective-permute-start(bf16[128,1792]{1,0:T(8,128)(2,1)} %param.9), channel_id=1, source_target_pairs={{0,4},{2,6},{4,0},{6,2},{8,12},{10,14},{12,8},{14,10},{16,20},{18,... | collective-permute-start | bytes 1376264 | tf_op jit(solution)/shard_map/ppermute | solution.py:317
  3.6 22.7 %collective-permute-start.3 = (bf16[128,1792]{1,0:T(8,128)(2,1)}, bf16[128,1792]{1,0:T(8,128)(2,1)S(1)}, u32[]{:S(2)}, u32[]{:S(2)}) collective-permute-start(bf16[128,1792]{1,0:T(8,128)(2,1)} %param.9), channel_id=1, source_target_pairs={{0,6},{2,4},{4,2},{6,0},{8,14},{10,12},{12,10},{14,8},{16,22},{18,... | collective-permute-start | bytes 1376264 | tf_op jit(solution)/shard_map/ppermute | solution.py:378
  6.1 19.3 %collective-permute-start.4 = (bf16[128,1792]{1,0:T(8,128)(2,1)}, bf16[128,1792]{1,0:T(8,128)(2,1)S(1)}, u32[]{:S(2)}, u32[]{:S(2)}) collective-permute-start(bf16[128,1792]{1,0:T(8,128)(2,1)} %param.9), channel_id=1, source_target_pairs={{0,8},{2,10},{4,12},{6,14},{8,0},{10,2},{12,4},{14,6},{16,24},{18,... | collective-permute-start | bytes 1376264 | tf_op jit(solution)/shard_map/ppermute | solution.py:317
  10.4 2.0 copy-start
  12.4 2.0 copy-start.2
  14.4 2.0 copy-start.3
  22.4 12.4 %collective-permute-start.5 = (bf16[128,1792]{1,0:T(8,128)(2,1)S(1)}, bf16[128,1792]{1,0:T(8,128)(2,1)S(1)}, u32[]{:S(2)}, u32[]{:S(2)}) collective-permute-start(bf16[128,1792]{1,0:T(8,128)(2,1)S(1)} %collective-permute-done), channel_id=1, source_target_pairs={{0,8},{2,10},{4,12},{6,14},{8,0},{10,2},{12,4},{14,6},{16,24},{18,... | collective-permute-start | bytes 1376264 | tf_op jit(solution)/shard_map/ppermute | solution.py:317
  25.5 9.6 %collective-permute-start.6 = (bf16[256,896]{1,0:T(8,128)(2,1)S(1)}, bf16[256,896]{1,0:T(8,128)(2,1)S(1)}, u32[]{:S(2)}, u32[]{:S(2)}) collective-permute-start(bf16[256,896]{1,0:T(8,128)(2,1)S(1)} %get-tuple-element.168), channel_id=1, source_target_pairs={{0,4},{2,6},{4,0},{6,2},{8,12},{10,14},{12,8},{14,10},{16,20},{18,... | collective-permute-start | bytes 1376264 | tf_op jit(solution)/shard_map/ppermute | solution.py:317
  26.1 17.4 %copy-start.12 = (bf16[128,1792]{1,0:T(8,128)(2,1)S(1)}, bf16[128,1792]{1,0:T(8,128)(2,1)}, u32[]{:S(2)}) copy-start(bf16[128,1792]{1,0:T(8,128)(2,1)} %param.9) | copy-start | bytes 1376260
  26.1 9.6 %collective-permute-start.7 = (bf16[256,896]{1,0:T(8,128)(2,1)S(1)}, bf16[256,896]{1,0:T(8,128)(2,1)S(1)}, u32[]{:S(2)}, u32[]{:S(2)}) collective-permute-start(bf16[256,896]{1,0:T(8,128)(2,1)S(1)} %get-tuple-element.167), channel_id=1, source_target_pairs={{0,2},{2,0},{4,6},{6,4},{8,10},{10,8},{12,14},{14,12},{16,18},{18,... | collective-permute-start | bytes 1376264 | tf_op jit(solution)/shard_map/ppermute | solution.py:317
  26.4 8.8 %copy-start.13 = (bf16[128,1792]{1,0:T(8,128)(2,1)}, bf16[128,1792]{1,0:T(8,128)(2,1)S(1)}, u32[]{:S(2)}) copy-start(bf16[128,1792]{1,0:T(8,128)(2,1)S(1)} %collective-permute-done.2) | copy-start | bytes 1376260
  34.9 0.8 copy-start.15
  35.7 195.6 %all-to-all-start = ((bf16[16,2032,128]{2,1,0:T(8,128)(2,1)}), bf16[16,2032,128]{2,1,0:T(8,128)(2,1)}, u32[]{:S(2)}, u32[]{:S(2)}) async-start(bf16[16,2032,128]{2,1,0:T(8,128)(2,1)} %pack_first.1), calls=%async_computation | async-start | bytes 16646144 | tf_op jit(solution)/shard_map/all_to_all | solution.py:366
  43.5 2.0 copy-start.16
  45.5 5.8 %copy-start.14 = (bf16[128,1792]{1,0:T(8,128)(2,1)S(1)}, bf16[128,1792]{1,0:T(8,128)(2,1)}, u32[]{:S(2)}) copy-start(bf16[128,1792]{1,0:T(8,128)(2,1)} %copy-done.13) | copy-start | bytes 1376260
  46.5 97.9 %collective-permute-start.11 = (bf16[640,896]{1,0:T(8,128)(2,1)S(1)}, bf16[640,896]{1,0:T(8,128)(2,1)S(1)}, u32[]{:S(2)}, u32[]{:S(2)}) collective-permute-start(bf16[640,896]{1,0:T(8,128)(2,1)S(1)} %pad_maximum_fusion.2), channel_id=1, source_target_pairs={{0,4},{2,6},{4,0},{6,2},{8,12},{10,14},{12,8},{14,10},{16,20},{18,... | collective-permute-start | bytes 3440648 | tf_op jit(solution)/shard_map/ppermute | solution.py:317
  47.1 99.9 %collective-permute-start.12 = (bf16[128,896]{1,0:T(8,128)(2,1)S(1)}, bf16[128,896]{1,0:T(8,128)(2,1)S(1)}, u32[]{:S(2)}, u32[]{:S(2)}) collective-permute-start(bf16[128,896]{1,0:T(8,128)(2,1)S(1)} %get-tuple-element.178), channel_id=1, source_target_pairs={{0,2},{2,0},{4,6},{6,4},{8,10},{10,8},{12,14},{14,12},{16,18},{18,... | collective-permute-start | bytes 688136 | tf_op jit(solution)/shard_map/ppermute | solution.py:317
  47.7 111.5 %collective-permute-start.10 = (bf16[128,1792]{1,0:T(8,128)(2,1)S(1)}, bf16[128,1792]{1,0:T(8,128)(2,1)S(1)}, u32[]{:S(2)}, u32[]{:S(2)}) collective-permute-start(bf16[128,1792]{1,0:T(8,128)(2,1)S(1)} %copy-done.16), channel_id=1, source_target_pairs={{0,6},{2,4},{4,2},{6,0},{8,14},{10,12},{12,10},{14,8},{16,22},{18,... | collective-permute-start | bytes 1376264 | tf_op jit(solution)/shard_map/ppermute | solution.py:378
  50.0 93.6 %collective-permute-start.8 = (bf16[128,896]{1,0:T(8,128)(2,1)S(1)}, bf16[128,896]{1,0:T(8,128)(2,1)S(1)}, u32[]{:S(2)}, u32[]{:S(2)}) collective-permute-start(bf16[128,896]{1,0:T(8,128)(2,1)S(1)} %get-tuple-element.175), channel_id=1, source_target_pairs={{0,4},{2,6},{4,0},{6,2},{8,12},{10,14},{12,8},{14,10},{16,20},{18,... | collective-permute-start | bytes 688136 | tf_op jit(solution)/shard_map/ppermute | solution.py:317
  50.7 105.7 %collective-permute-start.9 = (bf16[640,896]{1,0:T(8,128)(2,1)S(1)}, bf16[640,896]{1,0:T(8,128)(2,1)S(1)}, u32[]{:S(2)}, u32[]{:S(2)}) collective-permute-start(bf16[640,896]{1,0:T(8,128)(2,1)S(1)} %pad_maximum_fusion.1), channel_id=1, source_target_pairs={{0,2},{2,0},{4,6},{6,4},{8,10},{10,8},{12,14},{14,12},{16,18},{18,... | collective-permute-start | bytes 3440648 | tf_op jit(solution)/shard_map/ppermute | solution.py:317
  166.6 12.0 %collective-permute-start.13 = (bf16[2048,1792]{1,0:T(8,128)(2,1)}, bf16[2048,1792]{1,0:T(8,128)(2,1)}, u32[]{:S(2)}, u32[]{:S(2)}) collective-permute-start(bf16[2048,1792]{1,0:T(8,128)(2,1)} %pad_maximum_fusion.own_ref), channel_id=1, source_target_pairs={{0,1},{1,0},{2,3},{3,2},{4,5},{5,4},{6,7},{7,6},{8,9},{9,8},{10,11... | collective-permute-start | bytes 22020104 | tf_op jit(solution)/shard_map/ppermute | solution.py:363
  166.6 2.0 copy-start.1
  231.3 41.4 %all-to-all-start.1 = ((bf16[16,336,128]{2,1,0:T(8,128)(2,1)}), bf16[16,336,128]{2,1,0:T(8,128)(2,1)}, u32[]{:S(2)}, u32[]{:S(2)}) async-start(bf16[16,336,128]{2,1,0:T(8,128)(2,1)} %pack_rest.1), calls=%async_computation.1 | async-start | bytes 2752512 | tf_op jit(solution)/shard_map/all_to_all | solution.py:366
  262.4 5.5 %collective-permute-start.14 = (bf16[2048,512]{1,0:T(8,128)(2,1)}, bf16[2048,512]{1,0:T(8,128)(2,1)S(1)}, u32[]{:S(2)}, u32[]{:S(2)}) collective-permute-start(bf16[2048,512]{1,0:T(8,128)(2,1)} %hidden.1.own_h), channel_id=1, source_target_pairs={{0,1},{1,0},{2,3},{3,2},{4,5},{5,4},{6,7},{7,6},{8,9},{9,8},{10,11... | collective-permute-start | bytes 6291464 | tf_op jit(solution)/shard_map/ppermute | solution.py:363
  262.4 5.5 %copy-start.4 = (bf16[2048,512]{1,0:T(8,128)(2,1)S(1)}, bf16[2048,512]{1,0:T(8,128)(2,1)}, u32[]{:S(2)}) copy-start(bf16[2048,512]{1,0:T(8,128)(2,1)} %hidden.1.own_h) | copy-start | bytes 6291460
  264.4 3.5 %collective-permute-start.15 = (bf16[8,448,128]{2,1,0:T(8,128)(2,1)S(1)}, bf16[8,448,128]{2,1,0:T(8,128)(2,1)S(1)}, u32[]{:S(2)}, u32[]{:S(2)}) collective-permute-start(bf16[8,448,128]{2,1,0:T(8,128)(2,1)S(1)} %get-tuple-element.159), channel_id=1, source_target_pairs={{0,1},{1,0},{2,3},{3,2},{4,5},{5,4},{6,7},{7,6},{8,9},{9,8},{10,11... | collective-permute-start | bytes 2752520 | tf_op jit(solution)/shard_map/ppermute | solution.py:363
  267.9 3.6 %copy-start.10 = (bf16[8,448,128]{2,1,0:T(8,128)(2,1)}, bf16[8,448,128]{2,1,0:T(8,128)(2,1)S(1)}, u32[]{:S(2)}) copy-start(bf16[8,448,128]{2,1,0:T(8,128)(2,1)S(1)} %collective-permute-done.15.other_ref) | copy-start | bytes 2752516
  267.9 3.6 %copy-start.7 = (bf16[2048,512]{1,0:T(8,128)(2,1)}, bf16[2048,512]{1,0:T(8,128)(2,1)S(1)}, u32[]{:S(2)}) copy-start(bf16[2048,512]{1,0:T(8,128)(2,1)S(1)} %collective-permute-done.14.other_h) | copy-start | bytes 6291460
  271.5 19.8 %collective-permute-start.16 = (bf16[1024,384]{1,0:T(8,128)(2,1)}, bf16[1024,384]{1,0:T(8,128)(2,1)S(1)}, u32[]{:S(2)}, u32[]{:S(2)}) collective-permute-start(bf16[1024,384]{1,0:T(8,128)(2,1)} %get-tuple-element.107), channel_id=1, source_target_pairs={{0,2},{2,0},{4,6},{6,4},{8,10},{10,8},{12,14},{14,12},{16,18},{18,... | collective-permute-start | bytes 2359304 | tf_op jit(solution)/shard_map/ppermute | solution.py:317
  272.1 19.5 %collective-permute-start.17 = (bf16[1024,384]{1,0:T(8,128)(2,1)}, bf16[1024,384]{1,0:T(8,128)(2,1)S(1)}, u32[]{:S(2)}, u32[]{:S(2)}) collective-permute-start(bf16[1024,384]{1,0:T(8,128)(2,1)} %get-tuple-element.109), channel_id=1, source_target_pairs={{0,4},{2,6},{4,0},{6,2},{8,12},{10,14},{12,8},{14,10},{16,20},{18,... | collective-permute-start | bytes 2359304 | tf_op jit(solution)/shard_map/ppermute | solution.py:317
  274.1 19.4 %collective-permute-start.26 = (bf16[8,336,128]{2,1,0:T(8,128)(2,1)S(1)}, bf16[8,336,128]{2,1,0:T(8,128)(2,1)S(1)}, u32[]{:S(2)}, u32[]{:S(2)}) collective-permute-start(bf16[8,336,128]{2,1,0:T(8,128)(2,1)S(1)} %get-tuple-element.161), channel_id=1, source_target_pairs={{0,1},{1,0},{2,3},{3,2},{4,5},{5,4},{6,7},{7,6},{8,9},{9,8},{10,11... | collective-permute-start | bytes 2064392 | tf_op jit(solution)/shard_map/ppermute | solution.py:363
  274.1 14.3 %collective-permute-start.18 = (bf16[1024,256]{1,0:T(8,128)(2,1)S(1)}, bf16[1024,256]{1,0:T(8,128)(2,1)S(1)}, u32[]{:S(2)}, u32[]{:S(2)}) collective-permute-start(bf16[1024,256]{1,0:T(8,128)(2,1)S(1)} %get-tuple-element.111), channel_id=1, source_target_pairs={{0,8},{2,10},{4,12},{6,14},{8,0},{10,2},{12,4},{14,6},{16,24},{18,... | collective-permute-start | bytes 1572872 | tf_op jit(solution)/shard_map/ppermute | solution.py:317
  274.4 1.6 copy-start.5
  276.0 1.6 copy-start.8
  277.5 1.2 copy-start.11
  281.8 11.7 %copy-start.9 = (bf16[2048,512]{1,0:T(8,128)(2,1)S(1)}, bf16[2048,512]{1,0:T(8,128)(2,1)}, u32[]{:S(2)}) copy-start(bf16[2048,512]{1,0:T(8,128)(2,1)} %copy-done.7) | copy-start | bytes 6291460
  292.0 9.3 %collective-permute-start.21 = (bf16[512,256]{1,0:T(8,128)(2,1)S(1)}, bf16[512,256]{1,0:T(8,128)(2,1)S(1)}, u32[]{:S(2)}, u32[]{:S(2)}) collective-permute-start(bf16[512,256]{1,0:T(8,128)(2,1)S(1)} %get-tuple-element.117), channel_id=1, source_target_pairs={{0,2},{2,0},{4,6},{6,4},{8,10},{10,8},{12,14},{14,12},{16,18},{18,... | collective-permute-start | bytes 786440 | tf_op jit(solution)/shard_map/ppermute | solution.py:317
  293.5 19.6 %copy-start.6 = (bf16[2048,512]{1,0:T(8,128)(2,1)S(1)}, bf16[2048,512]{1,0:T(8,128)(2,1)}, u32[]{:S(2)}) copy-start(bf16[2048,512]{1,0:T(8,128)(2,1)} %hidden.1.own_h) | copy-start | bytes 6291460
  295.4 17.1 %collective-permute-start.27 = (bf16[1024,256]{1,0:T(8,128)(2,1)S(1)}, bf16[1024,256]{1,0:T(8,128)(2,1)S(1)}, u32[]{:S(2)}, u32[]{:S(2)}) collective-permute-start(bf16[1024,256]{1,0:T(8,128)(2,1)S(1)} %get-tuple-element.140), channel_id=1, source_target_pairs={{0,2},{2,0},{4,6},{6,4},{8,10},{10,8},{12,14},{14,12},{16,18},{18,... | collective-permute-start | bytes 1572872 | tf_op jit(solution)/shard_map/ppermute | solution.py:317
  296.0 12.1 %collective-permute-start.19 = (bf16[512,384]{1,0:T(8,128)(2,1)S(1)}, bf16[512,384]{1,0:T(8,128)(2,1)S(1)}, u32[]{:S(2)}, u32[]{:S(2)}) collective-permute-start(bf16[512,384]{1,0:T(8,128)(2,1)S(1)} %get-tuple-element.113), channel_id=1, source_target_pairs={{0,4},{2,6},{4,0},{6,2},{8,12},{10,14},{12,8},{14,10},{16,20},{18,... | collective-permute-start | bytes 1179656 | tf_op jit(solution)/shard_map/ppermute | solution.py:317
  296.6 12.1 %collective-permute-start.20 = (bf16[512,384]{1,0:T(8,128)(2,1)S(1)}, bf16[512,384]{1,0:T(8,128)(2,1)S(1)}, u32[]{:S(2)}, u32[]{:S(2)}) collective-permute-start(bf16[512,384]{1,0:T(8,128)(2,1)S(1)} %get-tuple-element.115), channel_id=1, source_target_pairs={{0,8},{2,10},{4,12},{6,14},{8,0},{10,2},{12,4},{14,6},{16,24},{18,... | collective-permute-start | bytes 1179656 | tf_op jit(solution)/shard_map/ppermute | solution.py:317
  297.0 22.1 %collective-permute-start.28 = (bf16[1024,256]{1,0:T(8,128)(2,1)S(1)}, bf16[1024,256]{1,0:T(8,128)(2,1)S(1)}, u32[]{:S(2)}, u32[]{:S(2)}) collective-permute-start(bf16[1024,256]{1,0:T(8,128)(2,1)S(1)} %get-tuple-element.142), channel_id=1, source_target_pairs={{0,4},{2,6},{4,0},{6,2},{8,12},{10,14},{12,8},{14,10},{16,20},{18,... | collective-permute-start | bytes 1572872 | tf_op jit(solution)/shard_map/ppermute | solution.py:317
  301.3 18.6 %collective-permute-start.29 = (bf16[1024,256]{1,0:T(8,128)(2,1)S(1)}, bf16[1024,256]{1,0:T(8,128)(2,1)S(1)}, u32[]{:S(2)}, u32[]{:S(2)}) collective-permute-start(bf16[1024,256]{1,0:T(8,128)(2,1)S(1)} %get-tuple-element.144), channel_id=1, source_target_pairs={{0,8},{2,10},{4,12},{6,14},{8,0},{10,2},{12,4},{14,6},{16,24},{18,... | collective-permute-start | bytes 1572872 | tf_op jit(solution)/shard_map/ppermute | solution.py:317
  308.8 15.9 %collective-permute-start.22 = (bf16[256,384]{1,0:T(8,128)(2,1)S(1)}, bf16[256,384]{1,0:T(8,128)(2,1)S(1)}, u32[]{:S(2)}, u32[]{:S(2)}) collective-permute-start(bf16[256,384]{1,0:T(8,128)(2,1)S(1)} %get-tuple-element.119), channel_id=1, source_target_pairs={{0,8},{2,10},{4,12},{6,14},{8,0},{10,2},{12,4},{14,6},{16,24},{18,... | collective-permute-start | bytes 589832 | tf_op jit(solution)/shard_map/ppermute | solution.py:317
  309.2 15.5 %collective-permute-start.23 = (bf16[256,384]{1,0:T(8,128)(2,1)S(1)}, bf16[256,384]{1,0:T(8,128)(2,1)S(1)}, u32[]{:S(2)}, u32[]{:S(2)}) collective-permute-start(bf16[256,384]{1,0:T(8,128)(2,1)S(1)} %get-tuple-element.121), channel_id=1, source_target_pairs={{0,2},{2,0},{4,6},{6,4},{8,10},{10,8},{12,14},{14,12},{16,18},{18,... | collective-permute-start | bytes 589832 | tf_op jit(solution)/shard_map/ppermute | solution.py:317
  312.5 9.7 %collective-permute-start.24 = (bf16[256,256]{1,0:T(8,128)(2,1)S(1)}, bf16[256,256]{1,0:T(8,128)(2,1)S(1)}, u32[]{:S(2)}, u32[]{:S(2)}) collective-permute-start(bf16[256,256]{1,0:T(8,128)(2,1)S(1)} %get-tuple-element.123), channel_id=1, source_target_pairs={{0,4},{2,6},{4,0},{6,2},{8,12},{10,14},{12,8},{14,10},{16,20},{18,... | collective-permute-start | bytes 393224 | tf_op jit(solution)/shard_map/ppermute | solution.py:317
  320.2 9.0 %collective-permute-start.30 = (bf16[512,256]{1,0:T(8,128)(2,1)S(1)}, bf16[512,256]{1,0:T(8,128)(2,1)S(1)}, u32[]{:S(2)}, u32[]{:S(2)}) collective-permute-start(bf16[512,256]{1,0:T(8,128)(2,1)S(1)} %get-tuple-element.146), channel_id=1, source_target_pairs={{0,4},{2,6},{4,0},{6,2},{8,12},{10,14},{12,8},{14,10},{16,20},{18,... | collective-permute-start | bytes 786440 | tf_op jit(solution)/shard_map/ppermute | solution.py:317
  321.7 9.0 %collective-permute-start.31 = (bf16[512,256]{1,0:T(8,128)(2,1)S(1)}, bf16[512,256]{1,0:T(8,128)(2,1)S(1)}, u32[]{:S(2)}, u32[]{:S(2)}) collective-permute-start(bf16[512,256]{1,0:T(8,128)(2,1)S(1)} %get-tuple-element.148), channel_id=1, source_target_pairs={{0,8},{2,10},{4,12},{6,14},{8,0},{10,2},{12,4},{14,6},{16,24},{18,... | collective-permute-start | bytes 786440 | tf_op jit(solution)/shard_map/ppermute | solution.py:317
  322.2 8.4 %collective-permute-start.32 = (bf16[512,256]{1,0:T(8,128)(2,1)S(1)}, bf16[512,256]{1,0:T(8,128)(2,1)S(1)}, u32[]{:S(2)}, u32[]{:S(2)}) collective-permute-start(bf16[512,256]{1,0:T(8,128)(2,1)S(1)} %get-tuple-element.150), channel_id=1, source_target_pairs={{0,2},{2,0},{4,6},{6,4},{8,10},{10,8},{12,14},{14,12},{16,18},{18,... | collective-permute-start | bytes 786440 | tf_op jit(solution)/shard_map/ppermute | solution.py:317
  324.9 15.6 %collective-permute-start.25 = (bf16[128,1024]{1,0:T(8,128)(2,1)S(1)}, bf16[128,1024]{1,0:T(8,128)(2,1)S(1)}, u32[]{:S(2)}, u32[]{:S(2)}) collective-permute-start(bf16[128,1024]{1,0:T(8,128)(2,1)S(1)} %get-tuple-element.125), channel_id=1, source_target_pairs={{0,16},{2,18},{4,20},{6,22},{8,24},{10,26},{12,28},{14,30},{16,0},... | collective-permute-start | bytes 786440 | tf_op jit(solution)/shard_map/ppermute | solution.py:317
  330.8 5.0 %collective-permute-start.33 = (bf16[256,256]{1,0:T(8,128)(2,1)S(1)}, bf16[256,256]{1,0:T(8,128)(2,1)S(1)}, u32[]{:S(2)}, u32[]{:S(2)}) collective-permute-start(bf16[256,256]{1,0:T(8,128)(2,1)S(1)} %get-tuple-element.152), channel_id=1, source_target_pairs={{0,8},{2,10},{4,12},{6,14},{8,0},{10,2},{12,4},{14,6},{16,24},{18,... | collective-permute-start | bytes 393224 | tf_op jit(solution)/shard_map/ppermute | solution.py:317
  330.9 5.0 %collective-permute-start.34 = (bf16[256,256]{1,0:T(8,128)(2,1)S(1)}, bf16[256,256]{1,0:T(8,128)(2,1)S(1)}, u32[]{:S(2)}, u32[]{:S(2)}) collective-permute-start(bf16[256,256]{1,0:T(8,128)(2,1)S(1)} %get-tuple-element.154), channel_id=1, source_target_pairs={{0,2},{2,0},{4,6},{6,4},{8,10},{10,8},{12,14},{14,12},{16,18},{18,... | collective-permute-start | bytes 393224 | tf_op jit(solution)/shard_map/ppermute | solution.py:317
  332.5 5.0 %collective-permute-start.35 = (bf16[256,256]{1,0:T(8,128)(2,1)S(1)}, bf16[256,256]{1,0:T(8,128)(2,1)S(1)}, u32[]{:S(2)}, u32[]{:S(2)}) collective-permute-start(bf16[256,256]{1,0:T(8,128)(2,1)S(1)} %get-tuple-element.156), channel_id=1, source_target_pairs={{0,4},{2,6},{4,0},{6,2},{8,12},{10,14},{12,8},{14,10},{16,20},{18,... | collective-permute-start | bytes 393224 | tf_op jit(solution)/shard_map/ppermute | solution.py:317
  337.6 8.0 %collective-permute-start.36 = (bf16[128,768]{1,0:T(8,128)(2,1)S(1)}, bf16[128,768]{1,0:T(8,128)(2,1)S(1)}, u32[]{:S(2)}, u32[]{:S(2)}) collective-permute-start(bf16[128,768]{1,0:T(8,128)(2,1)S(1)} %get-tuple-element.158), channel_id=1, source_target_pairs={{0,16},{2,18},{4,20},{6,22},{8,24},{10,26},{12,28},{14,30},{16,0},... | collective-permute-start | bytes 589832 | tf_op jit(solution)/shard_map/ppermute | solution.py:317
